TPU v7x, 32 devices: a whole 2x2x4 slice. The times are simulated.
32 devices in a mesh: dp: 4 (over z), fsdp: 8 (over y, x, core).
Axes of the slice: x: 2, y: 2, z: 4, core: 2. Of those that a mesh axis runs over, the one named last changes fastest.
Arguments:
- layer_input: bfloat16 [8192, 8192], P('dp', 'fsdp'), may hold values from -6 to 6
- cotangent: bfloat16 [2, 8192, 1024], P(None, ('dp', 'fsdp')), may hold values from -6 to 6
- candidates: bfloat16 [2, 4, 1024, 512], P(None, 'dp', None, 'fsdp'), may hold values from -0.1875 to 0.1875
- moment_first: float32 [2, 512, 8192], P(None, 'dp', 'fsdp'), may hold values from -0.6 to 0.6
- moment_second: float32 [2, 512, 8192], P(None, 'dp', 'fsdp'), may hold values from 0.0001 to 0.01
- owners: int32 [2], replicated, may hold values from 0 to 3
Outputs:
- update: bfloat16 [2, 1024, 8192], P(None, 'dp', 'fsdp')
- first_next: float32 [2, 512, 8192], P(None, 'dp', 'fsdp')
- second_next: float32 [2, 512, 8192], P(None, 'dp', 'fsdp')
Inputs may be any that keep to these rules, and one draw needn't show every extreme that they name: owners[m] names a data-parallel replica.
All inputs are finite; a program needn't handle non-finite values.
Results may differ from a plain program's by a relative error of at most 0.0056.
Values may be sent and summed in bfloat16 or wider, within the bound.
No kernel may reach another device: no remote copies, remote signals or barrier semaphores. Data moves between devices by JAX's collectives and lax.ppermute only.
A program may use at most 64 MiB of HBM per device.

v0:
```python
import math

import jax
import jax.numpy as jnp
from jax import lax
from jax.sharding import PartitionSpec as P

MATS = 2
STEP = 10


beta_first = 0.9
beta_second = 0.999
epsilon = 1e-08


def from_root(value, axis, source):
    kept = jnp.where(lax.axis_index(axis) == source, value, 0).astype(value.dtype)
    return lax.psum(kept, axis)


def on_device(layer_input, cotangent, candidates, moment_first, moment_second, owners):
    replicas = lax.axis_size("dp")
    replica_index = lax.axis_index("dp")
    inverse_root = 1.0 / math.sqrt(layer_input.shape[0] * replicas)
    kv_share = candidates.shape[2] // replicas
    updates = []
    firsts = []
    seconds = []
    for matrix in range(MATS):
        candidate_own = candidates[matrix, 0]
        owner_index = owners[matrix]
        assembled = lax.all_gather(candidate_own, "fsdp", axis=1, tiled=True)
        projector = from_root(assembled, "dp", owner_index)
        head_rows = jnp.dot(
            cotangent[matrix], projector, preferred_element_type=jnp.float32
        ).astype(jnp.bfloat16)
        partial_value = lax.dot_general(
            lax.all_gather(head_rows, "fsdp", axis=0, tiled=True),
            layer_input,
            (((0,), (0,)), ((), ())),
            preferred_element_type=jnp.float32,
        )
        projected = (
            lax.psum_scatter(partial_value, "dp", scatter_dimension=0, tiled=True) * inverse_root
        )
        first = beta_first * moment_first[matrix] + (1.0 - beta_first) * projected
        second = beta_second * moment_second[matrix] + (1.0 - beta_second) * projected * projected
        direction = (
            first
            / (1.0 - beta_first**STEP)
            / (jnp.sqrt(second / (1.0 - beta_second**STEP)) + epsilon)
        )
        direction = direction.astype(jnp.bfloat16)
        own_rows = lax.dynamic_slice_in_dim(projector, replica_index * kv_share, kv_share, 0)
        update = jnp.dot(
            own_rows,
            lax.all_gather(direction, "dp", axis=0, tiled=True),
            preferred_element_type=jnp.float32,
        )
        updates.append(update.astype(jnp.bfloat16))
        firsts.append(first)
        seconds.append(second)
    return (jnp.stack(updates), jnp.stack(firsts), jnp.stack(seconds))


def solution(mesh):
    placed = (
        P("dp", "fsdp"),
        P(None, ("dp", "fsdp"), None),
        P(None, "dp", None, "fsdp"),
        P(None, "dp", "fsdp"),
        P(None, "dp", "fsdp"),
        P(),
    )
    return jax.shard_map(
        on_device,
        mesh=mesh,
        in_specs=placed,
        out_specs=(P(None, "dp", "fsdp"), P(None, "dp", "fsdp"), P(None, "dp", "fsdp")),
        check_vma=False,
    )
```

profile of v0, /device:TPU:0, one launch (start us, length us, event | category | flops | bytes accessed | tf_op | source)
XLA Modules:
  0.0 373.9 jit_solution(13099983221002184518)
XLA Ops:
  7.2 0.0 all-gather.17.cloned.1.call-start
  7.2 1.7 fusion.16
  8.9 0.0 all-gather.17.cloned.1.call-update
  8.9 0.0 all-gather.19.cloned.1.call-start
  9.0 0.7 all-gather.19.cloned.1.call-update
  9.7 0.0 all-reduce.3.cloned.1.call-start
  9.7 1.3 fusion.17
  12.3 24.3 %all-gather.17.cloned.1.call-done = bf16[1,1,1024,512]{2,3,1,0:T(8,128)(2,1)} async-done(((bf16[1,1,1024,64]{2,3,1,0:T(8,128)(2,1)}), bf16[1,1,1024,512]{2,3,1,0:T(8,128)(2,1)}) %all-gather.17.cloned.1.call-update) | async-done | bytes 1048592 | tf_op jit(solution)/shard_map/all_gather | solution.py:33
  36.7 1.0 select_bitcast_fusion.1
  37.7 0.0 copy-start.2
  37.7 24.9 %all-gather.19.cloned.1.call-done = bf16[1,1,1024,512]{2,3,1,0:T(8,128)(2,1)} async-done(((bf16[1,1,1024,64]{2,3,1,0:T(8,128)(2,1)}), bf16[1,1,1024,512]{2,3,1,0:T(8,128)(2,1)}) %all-gather.19.cloned.1.call-update) | async-done | bytes 1048592 | tf_op jit(solution)/shard_map/all_gather | solution.py:33
  62.7 1.0 select_bitcast_fusion
  63.7 0.0 all-reduce.3.cloned.1.call-update
  63.7 0.0 all-gather.13.cloned.1.call-start
  63.8 89.0 %all-reduce.3.cloned.1.call-done = (bf16[1024,512]{0,1:T(8,128)(2,1)}, bf16[1024,512]{0,1:T(8,128)(2,1)}) async-done(((bf16[1024,512]{0,1:T(8,128)(2,1)}, bf16[1024,512]{0,1:T(8,128)(2,1)}), (bf16[1024,512]{0,1:T(8,128)(2,1)}, bf16[1024,512]{0,1:T(8,128)(2,1)})) %all-reduce.3.cloned.1.call-update) | async-done | bytes 2097168 | tf_op jit(solution)/shard_map/psum | solution.py:19
  152.7 0.0 copy-start.1
  152.7 0.0 copy-done.2
  152.7 2.5 fusion.3
  155.2 0.0 all-gather.13.cloned.1.call-update
  155.3 0.0 all-gather.9.cloned.1.call-start
  155.3 0.0 copy-done.1
  155.3 1.2 fusion.2
  156.5 0.0 all-gather.9.cloned.1.call-update
  156.5 0.0 reduce-scatter.5.cloned.1.call-start
  156.6 26.0 %all-gather.13.cloned.1.call-done = bf16[2048,512]{0,1:T(8,128)(2,1)} async-done(((bf16[256,512]{0,1:T(8,128)(2,1)}), bf16[2048,512]{0,1:T(8,128)(2,1)}) %all-gather.13.cloned.1.call-update) | async-done | bytes 2097168 | tf_op jit(solution)/shard_map/all_gather | solution.py:39
  182.6 6.5 %fusion.19 = f32[512,1024]{1,0:T(8,128)} fusion(bf16[2048,512]{0,1:T(8,128)(2,1)} %all-gather.13.cloned.1.call-done, bf16[2048,1024]{1,0:T(8,128)(2,1)} %param.6), kind=kOutput, calls=%fused_computation.34 | convolution fusion | flops 2147483648 | bytes 8388608 | tf_op jit(solution)/shard_map/dot_general | solution.py:38
  189.1 0.0 reduce-scatter.5.cloned.1.call-update
  189.1 0.0 reduce-scatter.3.cloned.1.call-start
  189.1 24.1 %all-gather.9.cloned.1.call-done = bf16[2048,512]{0,1:T(8,128)(2,1)} async-done(((bf16[256,512]{0,1:T(8,128)(2,1)}), bf16[2048,512]{0,1:T(8,128)(2,1)}) %all-gather.9.cloned.1.call-update) | async-done | bytes 2097168 | tf_op jit(solution)/shard_map/all_gather | solution.py:39
  213.3 6.5 %fusion.18 = f32[512,1024]{1,0:T(8,128)} fusion(bf16[2048,512]{0,1:T(8,128)(2,1)} %all-gather.9.cloned.1.call-done, bf16[2048,1024]{1,0:T(8,128)(2,1)} %param.6), kind=kOutput, calls=%fused_computation.33 | convolution fusion | flops 2147483648 | bytes 8388608 | tf_op jit(solution)/shard_map/dot_general | solution.py:38
  219.8 0.0 copy-start
  219.8 0.0 reduce-scatter.3.cloned.1.call-update
  219.8 0.0 all-gather.11.cloned.1.call-start
  219.9 39.6 %reduce-scatter.5.cloned.1.call-done = f32[128,1024]{1,0:T(8,128)} async-done(((f32[512,1024]{1,0:T(8,128)}), f32[128,1024]{1,0:T(8,128)}) %reduce-scatter.5.cloned.1.call-update) | async-done | bytes 524304 | tf_op jit(solution)/shard_map/reduce_scatter | solution.py:45
  259.4 45.5 %reduce-scatter.3.cloned.1.call-done = f32[128,1024]{1,0:T(8,128)} async-done(((f32[512,1024]{1,0:T(8,128)}), f32[128,1024]{1,0:T(8,128)}) %reduce-scatter.3.cloned.1.call-update) | async-done | bytes 524304 | tf_op jit(solution)/shard_map/reduce_scatter | solution.py:45
  304.9 0.0 copy-done
  304.9 3.0 divide_convert_fusion.1
  308.0 0.0 all-gather.11.cloned.1.call-update
  308.0 0.0 all-gather.15.cloned.1.call-start
  308.0 0.7 all-gather.15.cloned.1.call-update
  308.7 1.5 pad_maximum_fusion.1
  310.2 25.2 %all-gather.11.cloned.1.call-done = bf16[512,1024]{1,0:T(8,128)(2,1)} async-done(((bf16[128,1024]{1,0:T(8,128)(2,1)}), bf16[512,1024]{1,0:T(8,128)(2,1)}) %all-gather.11.cloned.1.call-update) | async-done | bytes 1048592 | tf_op jit(solution)/shard_map/all_gather | solution.py:58
  335.4 1.8 fusion
  337.2 27.3 %all-gather.15.cloned.1.call-done = bf16[512,1024]{1,0:T(8,128)(2,1)} async-done(((bf16[128,1024]{1,0:T(8,128)(2,1)}), bf16[512,1024]{1,0:T(8,128)(2,1)}) %all-gather.15.cloned.1.call-update) | async-done | bytes 1048592 | tf_op jit(solution)/shard_map/all_gather | solution.py:58
  364.5 1.8 fusion.1
  366.3 1.1 pad_maximum_fusion
Async XLA Ops:
  7.2 29.5 %all-gather.17.cloned.1.call-start = ((), (), s32[]{:S(2)}) async-start(), calls=%async_computation.8 | async-start | bytes 1179648 | tf_op jit(solution)/shard_map/all_gather | solution.py:33
  8.9 53.7 %all-gather.19.cloned.1.call-start = ((), (), s32[]{:S(2)}) async-start(), calls=%async_computation.9 | async-start | bytes 1179648 | tf_op jit(solution)/shard_map/all_gather | solution.py:33
  9.7 143.1 %all-reduce.3.cloned.1.call-start = ((), (), s32[]{:S(2)}) async-start(), calls=%async_computation.10 | async-start | bytes 4194304 | tf_op jit(solution)/shard_map/psum | solution.py:19
  37.7 115.0 %copy-start.2 = (bf16[2,256,1024]{2,1,0:T(8,128)(2,1)S(1)}, bf16[2,256,1024]{2,1,0:T(8,128)(2,1)}, u32[]{:S(2)}) copy-start(bf16[2,256,1024]{2,1,0:T(8,128)(2,1)} %param.7) | copy-start | bytes 3145732
  63.7 118.9 %all-gather.13.cloned.1.call-start = ((), (), s32[]{:S(2)}) async-start(), calls=%async_computation.5 | async-start | bytes 2359296 | tf_op jit(solution)/shard_map/all_gather | solution.py:39
  152.7 2.6 copy-start.1
  155.3 58.0 %all-gather.9.cloned.1.call-start = ((), (), s32[]{:S(2)}) async-start(), calls=%async_computation.2 | async-start | bytes 2359296 | tf_op jit(solution)/shard_map/all_gather | solution.py:39
  156.5 102.9 %reduce-scatter.5.cloned.1.call-start = ((), (), s32[]{:S(2)}) async-start(), calls=%async_computation.6 | async-start | bytes 2621440 | tf_op jit(solution)/shard_map/reduce_scatter | solution.py:45
  189.1 115.8 %reduce-scatter.3.cloned.1.call-start = ((), (), s32[]{:S(2)}) async-start(), calls=%async_computation.3 | async-start | bytes 2621440 | tf_op jit(solution)/shard_map/reduce_scatter | solution.py:45
  219.8 85.2 %copy-start = (f32[2,128,1024]{2,1,0:T(8,128)S(1)}, f32[2,128,1024]{2,1,0:T(8,128)}, u32[]{:S(2)}) copy-start(f32[2,128,1024]{2,1,0:T(8,128)} %param.9) | copy-start | bytes 3145732
  219.8 115.6 %all-gather.11.cloned.1.call-start = ((), (), s32[]{:S(2)}) async-start(), calls=%async_computation.4 | async-start | bytes 1310720 | tf_op jit(solution)/shard_map/all_gather | solution.py:58
  308.0 56.5 %all-gather.15.cloned.1.call-start = ((), (), s32[]{:S(2)}) async-start(), calls=%async_computation.7 | async-start | bytes 1310720 | tf_op jit(solution)/shard_map/all_gather | solution.py:58
Sparse Core Ops, SparseCore 0:
  10.5 26.1 all-gather.16
  39.1 23.4 all-gather.18
  65.7 87.0 all-reduce.2
  155.4 27.1 all-gather.12
  185.0 28.1 all-gather.8
  215.5 43.8 reduce-scatter.4
  261.7 43.1 reduce-scatter.2
  308.1 27.2 all-gather.10
  337.1 27.4 all-gather.14
where the time goes:
time: 374 us
  waiting for transfers between devices  327 us (87%)
  matrix products  20.2 us (5%)
  between operations  15.1 us (4%)
  other arithmetic  7.63 us (2%)
    psum x1, waiting for transfers between devices, from_root(): return lax.psum(kept, axis)  89 us
    reduce_scatter x2, waiting for transfers between devices, on_device(): lax.psum_scatter(partial_value, 'dp', scatter_dimension=0, tiled=True)  85.1 us
    all_gather x2, waiting for transfers between devices, on_device(): lax.all_gather(direction, 'dp', axis=0, tiled=True)  52.5 us
    all_gather x2, waiting for transfers between devices, on_device(): lax.all_gather(head_rows, 'fsdp', axis=0, tiled=True)  50.1 us
    all_gather x2, waiting for transfers between devices, on_device(): assembled = lax.all_gather(candidate_own, 'fsdp', axis=1, tiled=True)  49.3 us
    dot_general x2, matrix products, on_device(): lax.dot_general(lax.all_gather(head_rows, 'fsdp', axis=0, tiled=True), la...  13 us
  transfers between devices with their start and end apart: 9, of which 9 were waited for; matrix products, arithmetic and copies ran while one was open for 5% of the time, Pallas kernels for 0%

commit v1 on v0

v1 whole, which is shorter than its diff:
```python
import functools
import math

import jax
import jax.numpy as jnp
from jax import lax
from jax.experimental import pallas as pl
from jax.experimental.pallas import tpu as pltpu
from jax.sharding import PartitionSpec as P

MATS = 2
STEP = 10

beta_first = 0.9
beta_second = 0.999
epsilon = 1e-08

TRANSPOSED = (((0,), (0,)), ((), ()))
MIB = 1 << 20


def swap(value, axis, mask):
    size = lax.axis_size(axis)
    return lax.ppermute(value, axis, [(i, i ^ mask) for i in range(size)])


def bits_of(size):
    return [1 << k for k in range(size.bit_length() - 1)]


def spread(block, bits):
    if len(bits) == 2:
        low, high = bits
        half = block.shape[0] // 2
        by_low = swap(block, "fsdp", low)
        by_high = swap(block, "fsdp", high)
        upper = swap(by_low[:half], "fsdp", high)
        lower = swap(by_high[half:], "fsdp", low)
        return {
            0: block,
            low: by_low,
            high: by_high,
            low | high: jnp.concatenate([upper, lower], axis=0),
        }
    blocks = {0: block}
    for bit in bits:
        blocks.update({mask ^ bit: swap(held, "fsdp", bit) for mask, held in list(blocks.items())})
    return blocks


def tile_of(size):
    return min(size, 256)


def product_body(count, first, places, *refs):
    blocks, inputs = refs[:count], refs[count : 2 * count]
    total = None if first else refs[2 * count][...]
    for block, rows in zip(blocks, inputs):
        term = lax.dot_general(
            block[...], rows[...], TRANSPOSED, preferred_element_type=jnp.float32
        )
        total = term if total is None else total + term
    refs[-1][...] = total


def add_products(blocks, places, layer_input, total=None):
    count = len(blocks)
    rows, kv = blocks[0].shape
    width = layer_input.shape[1]
    tile = tile_of(kv)
    in_specs = [pl.BlockSpec((rows, tile), lambda i, places: (0, i))] * count
    in_specs += [
        pl.BlockSpec((rows, width), functools.partial(lambda k, i, places: (places[k], 0), k))
        for k in range(count)
    ]
    operands = list(blocks) + [layer_input] * count
    if total is not None:
        in_specs.append(pl.BlockSpec((tile, width), lambda i, places: (i, 0)))
        operands.append(total)
    return pl.pallas_call(
        functools.partial(product_body, count, total is None),
        grid_spec=pltpu.PrefetchScalarGridSpec(
            num_scalar_prefetch=1,
            grid=(kv // tile,),
            in_specs=in_specs,
            out_specs=pl.BlockSpec((tile, width), lambda i, places: (i, 0)),
        ),
        out_shape=jax.ShapeDtypeStruct((kv, width), jnp.float32),
        compiler_params=pltpu.CompilerParams(vmem_limit_bytes=32 * MIB),
        cost_estimate=pl.CostEstimate(
            flops=2 * count * rows * kv * width,
            bytes_accessed=2 * count * rows * (kv + width) + 8 * kv * width,
            transcendentals=0,
        ),
    )(places, *operands)


def project_body(count, scale, places, *refs):
    blocks, inputs = refs[:count], refs[count : 2 * count]
    partial, projector, send, keep, held = refs[2 * count :]
    step = pl.program_id(0)
    total = partial[...]
    for block, rows in zip(blocks, inputs):
        total += lax.dot_general(
            block[...], rows[...], TRANSPOSED, preferred_element_type=jnp.float32
        )
    term = jnp.dot(
        projector[...], total.astype(jnp.bfloat16), preferred_element_type=jnp.float32
    )

    @pl.when(step == 0)
    def _():
        held[...] = term

    @pl.when(step > 0)
    def _():
        held[...] += term

    @pl.when(step == pl.num_programs(0) - 1)
    def _():
        half = send.shape[0]
        send[...] = (held[:half] * scale).astype(send.dtype)
        keep[...] = held[half:] * scale


def project(blocks, places, layer_input, partial, projector, scale):
    count = len(blocks)
    rows, kv = blocks[0].shape
    width = layer_input.shape[1]
    rank = projector.shape[0]
    tile = tile_of(kv)
    in_specs = [pl.BlockSpec((rows, tile), lambda i, places: (0, i))] * count
    in_specs += [
        pl.BlockSpec((rows, width), functools.partial(lambda k, i, places: (places[k], 0), k))
        for k in range(count)
    ]
    in_specs += [
        pl.BlockSpec((tile, width), lambda i, places: (i, 0)),
        pl.BlockSpec((rank, tile), lambda i, places: (0, i)),
    ]
    half = pl.BlockSpec((rank // 2, width), lambda i, places: (0, 0))
    return pl.pallas_call(
        functools.partial(project_body, count, scale),
        grid_spec=pltpu.PrefetchScalarGridSpec(
            num_scalar_prefetch=1,
            grid=(kv // tile,),
            in_specs=in_specs,
            out_specs=[half, half],
            scratch_shapes=[pltpu.VMEM((rank, width), jnp.float32)],
        ),
        out_shape=[
            jax.ShapeDtypeStruct((rank // 2, width), jnp.bfloat16),
            jax.ShapeDtypeStruct((rank // 2, width), jnp.float32),
        ],
        compiler_params=pltpu.CompilerParams(vmem_limit_bytes=32 * MIB),
        cost_estimate=pl.CostEstimate(
            flops=2 * count * rows * kv * width + 2 * rank * kv * width,
            bytes_accessed=2 * count * rows * (kv + width) + 4 * kv * width,
            transcendentals=0,
        ),
    )(places, *blocks, *([layer_input] * count), partial, projector)


def on_device(layer_input, cotangent, candidates, moment_first, moment_second, owners):
    replicas = lax.axis_size("dp")
    members = lax.axis_size("fsdp")
    me_dp = lax.axis_index("dp")
    me_fsdp = lax.axis_index("fsdp")
    dp_bits = bits_of(replicas)
    far_bits = bits_of(members)[1:]
    scale = 1.0 / math.sqrt(layer_input.shape[0] * replicas)
    kv = candidates.shape[2]
    kv_share = kv // replicas
    rank_share = moment_first.shape[1]

    order = [0]
    for bit in reversed(dp_bits):
        order = [mask ^ bit for mask in order] + order

    def owned(matrix):
        value = candidates[matrix, 0].T
        for bit in reversed(dp_bits):
            other = swap(value, "dp", bit)
            mine = (me_dp & bit) == (owners[matrix] & bit)
            value = jnp.where(mine, value, other)
        return value

    def assembled(value):
        blocks = spread(value, far_bits)
        masks = sorted(blocks)
        same = jnp.concatenate([blocks[mask] for mask in masks], axis=0)
        other = swap(same, "fsdp", 1)
        count = value.shape[0]
        both = jnp.concatenate([same, other], axis=0)
        rows = []
        per = members // replicas
        for mask in order:
            for sub in range(per):
                member = (me_dp ^ mask) * per + sub
                away = member ^ me_fsdp
                slot = (away >> 1) + (away & 1) * len(masks)
                rows.append(lax.dynamic_slice_in_dim(both, slot * count, count, 0))
        return jnp.concatenate(rows, axis=0)

    sends, keeps, projectors = [], [], []
    for matrix in range(MATS):
        own = cotangent[matrix]
        blocks = spread(own, far_bits)
        last = max(blocks)
        early = {mask: held for mask, held in blocks.items() if mask != last}
        early.update({mask ^ 1: swap(held, "fsdp", 1) for mask, held in early.items()})
        late = {last: blocks[last], last ^ 1: swap(blocks[last], "fsdp", 1)}
        projector = assembled(owned(matrix))
        partial = add_products(
            list(early.values()), jnp.stack([me_fsdp ^ mask for mask in early]), layer_input
        )
        send, keep = project(
            list(late.values()),
            jnp.stack([me_fsdp ^ mask for mask in late]),
            layer_input,
            partial,
            projector,
            scale,
        )
        sends.append(send)
        keeps.append(keep)
        projectors.append(projector)

    updates, firsts, seconds = [], [], []
    for matrix in range(MATS):
        send, keep = sends[matrix], keeps[matrix]
        for bit in dp_bits:
            total = keep + swap(send, "dp", bit).astype(jnp.float32)
            half = total.shape[0] // 2
            if half >= rank_share:
                send, keep = total[:half].astype(jnp.bfloat16), total[half:]
        projected = total
        first = beta_first * moment_first[matrix] + (1.0 - beta_first) * projected
        second = beta_second * moment_second[matrix] + (1.0 - beta_second) * projected * projected
        direction = (
            first
            / (1.0 - beta_first**STEP)
            / (jnp.sqrt(second / (1.0 - beta_second**STEP)) + epsilon)
        )
        direction = direction.astype(jnp.bfloat16)
        for bit in reversed(dp_bits):
            direction = jnp.concatenate([swap(direction, "dp", bit), direction], axis=0)
        own = lax.dynamic_slice_in_dim(projectors[matrix], me_dp * kv_share, kv_share, 1)
        update = lax.dot_general(own, direction, TRANSPOSED, preferred_element_type=jnp.float32)
        updates.append(update.astype(jnp.bfloat16))
        firsts.append(first)
        seconds.append(second)
    return (jnp.stack(updates), jnp.stack(firsts), jnp.stack(seconds))


def solution(mesh):
    placed = (
        P("dp", "fsdp"),
        P(None, ("dp", "fsdp"), None),
        P(None, "dp", None, "fsdp"),
        P(None, "dp", "fsdp"),
        P(None, "dp", "fsdp"),
        P(),
    )
    return jax.shard_map(
        on_device,
        mesh=mesh,
        in_specs=placed,
        out_specs=(P(None, "dp", "fsdp"), P(None, "dp", "fsdp"), P(None, "dp", "fsdp")),
        check_vma=False,
    )
```

time: 374 us -> 203 us (0.54)
  waiting for transfers between devices: 327 us -> 123 us
  starting transfers between devices: 0.37 us -> 35.9 us
  Pallas kernels: 0 us -> 20.8 us
  matrix products: 20.2 us -> 3.03 us
  between operations: 15.1 us -> 3.87 us
  local copies, waits for them, and re-layouts: 3.04 us -> 6.9 us
    all_gather x6 -> x0, waiting for transfers between devices: 152 us -> none  [the longest x2 52.5 us: on_device(): lax.all_gather(direction, 'dp', axis=0, tiled=True)]
    ppermute x0 -> x38, waiting for transfers between devices: none -> 123 us  [swap(): return lax.ppermute(value, axis, [(i, i ^ mask) for i in range(size)])]
    psum x1 -> x0, waiting for transfers between devices: 89 us -> none  [from_root(): return lax.psum(kept, axis)]
    reduce_scatter x2 -> x0, waiting for transfers between devices: 85.1 us -> none  [on_device(): lax.psum_scatter(partial_value, 'dp', scatter_dimension=0, tiled=True)]
    ppermute x0 -> x38, starting transfers between devices: none -> 35.9 us  [swap(): return lax.ppermute(value, axis, [(i, i ^ mask) for i in range(size)])]
    pallas_call x0 -> x4, Pallas kernels: none -> 20.8 us  [the longest x2 10.8 us: add_products(): pl.pallas_call(functools.partial(product_body, count, total is None), gri...]
    dot_general x6 -> x2, matrix products: 20.2 us -> 3.03 us  [on_device(): lax.dot_general(own, direction, TRANSPOSED, preferred_element_type=jnp.fl...]
  transfers between devices with their start and end apart: 9 -> 38, of which waited for: 9 -> 21; matrix products, arithmetic and copies ran while one was open for 5% -> 6% of each run, Pallas kernels for 0% -> 10%
where the time goes in v1:
time: 203 us
  waiting for transfers between devices  123 us (61%)
  starting transfers between devices  35.9 us (18%)
  Pallas kernels  20.8 us (10%)
  other arithmetic  9.4 us (5%)
  local copies, waits for them, and re-layouts  6.9 us (3%)
  between operations  3.87 us (2%)
  matrix products  3.03 us (1%)
    ppermute x38, waiting for transfers between devices, swap(): return lax.ppermute(value, axis, [(i, i ^ mask) for i in range(size)])  123 us
    ppermute x38, starting transfers between devices, swap(): return lax.ppermute(value, axis, [(i, i ^ mask) for i in range(size)])  35.9 us
    pallas_call x2, Pallas kernels, add_products(): pl.pallas_call(functools.partial(product_body, count, total is None), gri...  10.8 us
    pallas_call x2, Pallas kernels, project(): pl.pallas_call(functools.partial(project_body, count, scale), grid_spec=p...  9.99 us
    another operation x4, other arithmetic, on_device(): return (jnp.stack(updates), jnp.stack(firsts), jnp.stack(seconds))  6.14 us
  transfers between devices with their start and end apart: 38, of which 21 were waited for; matrix products, arithmetic and copies ran while one was open for 6% of the time, Pallas kernels for 10%

profile of v1, /device:TPU:0, one launch (start us, length us, event | category | flops | bytes accessed | tf_op | source)
XLA Modules:
  0.0 202.6 jit_solution(15928841824094133473)
XLA Ops:
  0.6 1.0 slice_bitcast_fusion.3
  1.6 4.1 %collective-permute-start = (bf16[64,1024]{1,0:T(8,128)(2,1)S(1)}, bf16[64,1024]{1,0:T(8,128)(2,1)S(1)}, u32[]{:S(2)}, u32[]{:S(2)}) collective-permute-start(bf16[64,1024]{1,0:T(8,128)(2,1)S(1)} %get-tuple-element.28), channel_id=1, source_target_pairs={{0,16},{8,24},{16,0},{24,8},{1,17},{9,25},{17,1},{25,9},{2,18},{10... | collective-permute-start | bytes 393224 | tf_op jit(solution)/shard_map/ppermute | solution.py:24
  5.8 1.3 fusion.24
  8.4 7.2 %collective-permute-done = bf16[64,1024]{1,0:T(8,128)(2,1)S(1)} collective-permute-done((bf16[64,1024]{1,0:T(8,128)(2,1)S(1)}, bf16[64,1024]{1,0:T(8,128)(2,1)S(1)}, u32[]{:S(2)}, u32[]{:S(2)}) %collective-permute-start) | collective-permute-done | bytes 131104 | tf_op jit(solution)/shard_map/ppermute | solution.py:24
  15.7 2.0 collective-permute-done.19
  17.6 1.0 broadcast_select_fusion.2
  18.6 0.8 collective-permute-start.1
  19.4 1.3 slice_bitcast_fusion.1
  20.7 1.6 collective-permute-start.7
  22.3 1.5 collective-permute-start.9
  23.8 0.5 collective-permute-start.26
  25.9 1.4 collective-permute-start.20
  27.3 1.6 collective-permute-start.2
  28.8 2.0 collective-permute-done.20
  30.8 0.5 collective-permute-start.3
  31.4 17.0 %collective-permute-done.2 = bf16[64,1024]{1,0:T(8,128)(2,1)S(1)} collective-permute-done((bf16[64,1024]{1,0:T(8,128)(2,1)S(1)}, bf16[64,1024]{1,0:T(8,128)(2,1)S(1)}, u32[]{:S(2)}, u32[]{:S(2)}) %collective-permute-start.2) | collective-permute-done | bytes 131104 | tf_op jit(solution)/shard_map/ppermute | solution.py:24
  48.4 1.5 collective-permute-start.21
  49.9 1.6 collective-permute-start.22
  51.5 1.8 collective-permute-done.21
  53.4 1.5 collective-permute-start.28
  54.9 1.3 collective-permute-done.22
  56.2 1.5 collective-permute-start.4
  57.8 9.8 %collective-permute-done.4 = bf16[32,1024]{1,0:T(8,128)(2,1)S(1)} collective-permute-done((bf16[32,1024]{1,0:T(8,128)(2,1)S(1)}, bf16[32,1024]{1,0:T(8,128)(2,1)S(1)}, u32[]{:S(2)}, u32[]{:S(2)}) %collective-permute-start.4) | collective-permute-done | bytes 65568 | tf_op jit(solution)/shard_map/ppermute | solution.py:24
  67.6 0.5 collective-permute-start.5
  68.1 1.6 collective-permute-start.23
  69.7 1.0 slice.94
  70.7 1.2 collective-permute-done.5
  71.8 1.7 collective-permute-start.8
  74.0 0.6 collective-permute-start.27
  74.7 1.0 slice.95
  75.7 2.3 %collective-permute-done.24 = bf16[32,1024]{1,0:T(8,128)(2,1)S(1)} collective-permute-done((bf16[32,1024]{1,0:T(8,128)(2,1)S(1)}, bf16[32,1024]{1,0:T(8,128)(2,1)S(1)}, u32[]{:S(2)}, u32[]{:S(2)}) %collective-permute-start.24) | collective-permute-done | bytes 65568 | tf_op jit(solution)/shard_map/ppermute | solution.py:24
  78.4 2.1 %collective-permute-done.8 = bf16[128,1024]{1,0:T(8,128)(2,1)S(1)} collective-permute-done((bf16[128,1024]{1,0:T(8,128)(2,1)S(1)}, bf16[128,1024]{1,0:T(8,128)(2,1)S(1)}, u32[]{:S(2)}, u32[]{:S(2)}) %collective-permute-start.8) | collective-permute-done | bytes 262176 | tf_op jit(solution)/shard_map/ppermute | solution.py:24
  80.5 1.0 collective-permute-start.29
  81.5 1.8 collective-permute-done.27
  83.3 3.9 %collective-permute-done.10 = bf16[128,1024]{1,0:T(8,128)(2,1)S(1)} collective-permute-done((bf16[128,1024]{1,0:T(8,128)(2,1)S(1)}, bf16[128,1024]{1,0:T(8,128)(2,1)S(1)}, u32[]{:S(2)}, u32[]{:S(2)}) %collective-permute-start.10) | collective-permute-done | bytes 262176 | tf_op jit(solution)/shard_map/ppermute | solution.py:24
  87.2 2.9 %collective-permute-done.29 = bf16[128,1024]{1,0:T(8,128)(2,1)S(1)} collective-permute-done((bf16[128,1024]{1,0:T(8,128)(2,1)S(1)}, bf16[128,1024]{1,0:T(8,128)(2,1)S(1)}, u32[]{:S(2)}, u32[]{:S(2)}) %collective-permute-start.29) | collective-permute-done | bytes 262176 | tf_op jit(solution)/shard_map/ppermute | solution.py:24
  90.1 0.6 collective-permute-start.14
  91.3 0.6 copy-done.2
  91.9 0.5 collective-permute-start.32
  92.4 1.3 collective-permute-done.14.refs_5_
  93.8 5.8 %shard_map.85.refs_4_ = f32[1024,1024]{1,0:T(8,128)S(1)} custom-call(s32[6]{0:T(128)S(1)} %stack.76.places, bf16[256,1024]{1,0:T(8,128)(2,1)S(1)} %get-tuple-element.24.refs_0_, bf16[256,1024]{1,0:T(8,128)(2,1)} %collective-permute-done.7.refs_1_, bf16[256,1024]{1,0:T(8,128)(2,1)} %collective-permute-done.9.refs_2_, ...), custom_call_target="tpu_custom_call" | custom-call | flops 3221225472 | bytes 14680064 | tf_op jit(solution)/shard_map/pallas_call | solution.py:80
  99.6 5.0 %shard_map.86 = (bf16[256,1024]{1,0:T(8,128)(2,1)S(1)}, f32[256,1024]{1,0:T(8,128)S(1)}) custom-call(s32[2]{0:T(128)S(1)} %pad_add_fusion.places, bf16[256,1024]{1,0:T(8,128)(2,1)S(1)} %constant_dynamic-update-slice_fusion.11.refs_0_, bf16[256,1024]{1,0:T(8,128)(2,1)S(1)} %collective-permute-done.11.refs_1_, bf16[2048,1024]{1,0:T(8,128)(2,1)S(1)} %copy-done, ...), custom_call_target="tpu_custom_call" | custom-call | flops 2147483648 | bytes 6291456 | tf_op jit(solution)/shard_map/pallas_call | solution.py:142
  104.6 0.6 collective-permute-start.15
  105.2 5.0 %shard_map.87.refs_4_ = f32[1024,1024]{1,0:T(8,128)S(1)} custom-call(s32[6]{0:T(128)S(1)} %stack.76.places, bf16[256,1024]{1,0:T(8,128)(2,1)S(1)} %get-tuple-element.25.refs_0_, bf16[256,1024]{1,0:T(8,128)(2,1)S(1)} %copy-done.2, bf16[256,1024]{1,0:T(8,128)(2,1)S(1)} %collective-permute-done.28.refs_2_, ...), custom_call_target="tpu_custom_call" | custom-call | flops 3221225472 | bytes 14680064 | tf_op jit(solution)/shard_map/pallas_call | solution.py:80
  110.3 5.0 %shard_map.88 = (bf16[256,1024]{1,0:T(8,128)(2,1)S(1)}, f32[256,1024]{1,0:T(8,128)S(1)}) custom-call(s32[2]{0:T(128)S(1)} %pad_add_fusion.places, bf16[256,1024]{1,0:T(8,128)(2,1)S(1)} %constant_dynamic-update-slice_fusion.24.refs_0_, bf16[256,1024]{1,0:T(8,128)(2,1)S(1)} %collective-permute-done.30.refs_1_, bf16[2048,1024]{1,0:T(8,128)(2,1)S(1)} %copy-done, ...), custom_call_target="tpu_custom_call" | custom-call | flops 2147483648 | bytes 6291456 | tf_op jit(solution)/shard_map/pallas_call | solution.py:142
  115.3 1.6 collective-permute-start.34
  116.9 2.6 %collective-permute-done.15 = bf16[256,1024]{1,0:T(8,128)(2,1)S(1)} collective-permute-done((bf16[256,1024]{1,0:T(8,128)(2,1)S(1)}, bf16[256,1024]{1,0:T(8,128)(2,1)S(1)}, u32[]{:S(2)}, u32[]{:S(2)}) %collective-permute-start.15) | collective-permute-done | bytes 524320 | tf_op jit(solution)/shard_map/ppermute | solution.py:24
  119.7 3.4 %collective-permute-start.16 = (bf16[128,1024]{1,0:T(8,128)(2,1)S(1)}, bf16[128,1024]{1,0:T(8,128)(2,1)S(1)}, u32[]{:S(2)}, u32[]{:S(2)}) collective-permute-start(bf16[128,1024]{1,0:T(8,128)(2,1)S(1)} %slice.161), channel_id=1, source_target_pairs={{0,16},{8,24},{16,0},{24,8},{1,17},{9,25},{17,1},{25,9},{2,18},{10... | collective-permute-start | bytes 786440 | tf_op jit(solution)/shard_map/ppermute | solution.py:24
  123.1 12.6 %collective-permute-done.34 = bf16[256,1024]{1,0:T(8,128)(2,1)S(1)} collective-permute-done((bf16[256,1024]{1,0:T(8,128)(2,1)S(1)}, bf16[256,1024]{1,0:T(8,128)(2,1)S(1)}, u32[]{:S(2)}, u32[]{:S(2)}) %collective-permute-start.34) | collective-permute-done | bytes 524320 | tf_op jit(solution)/shard_map/ppermute | solution.py:24
  136.0 1.6 collective-permute-start.35
  137.6 12.7 %collective-permute-done.35 = bf16[128,1024]{1,0:T(8,128)(2,1)S(1)} collective-permute-done((bf16[128,1024]{1,0:T(8,128)(2,1)S(1)}, bf16[128,1024]{1,0:T(8,128)(2,1)S(1)}, u32[]{:S(2)}, u32[]{:S(2)}) %collective-permute-start.35) | collective-permute-done | bytes 262176 | tf_op jit(solution)/shard_map/ppermute | solution.py:24
  150.3 1.7 fusion.22
  152.0 2.9 %collective-permute-start.36 = (bf16[128,1024]{1,0:T(8,128)(2,1)S(1)}, bf16[128,1024]{1,0:T(8,128)(2,1)S(1)}, u32[]{:S(2)}, u32[]{:S(2)}) collective-permute-start(bf16[128,1024]{1,0:T(8,128)(2,1)S(1)} %get-tuple-element.19), channel_id=1, source_target_pairs={{0,16},{8,24},{16,0},{24,8},{1,17},{9,25},{17,1},{25,9},{2,18},{10... | collective-permute-start | bytes 786440 | tf_op jit(solution)/shard_map/ppermute | solution.py:24
  155.0 17.0 %collective-permute-done.17 = bf16[128,1024]{1,0:T(8,128)(2,1)S(1)} collective-permute-done((bf16[128,1024]{1,0:T(8,128)(2,1)S(1)}, bf16[128,1024]{1,0:T(8,128)(2,1)S(1)}, u32[]{:S(2)}, u32[]{:S(2)}) %collective-permute-start.17) | collective-permute-done | bytes 262176 | tf_op jit(solution)/shard_map/ppermute | solution.py:24
  172.0 0.9 pad_maximum_fusion.3
  172.9 4.7 %collective-permute-done.36 = bf16[128,1024]{1,0:T(8,128)(2,1)S(1)} collective-permute-done((bf16[128,1024]{1,0:T(8,128)(2,1)S(1)}, bf16[128,1024]{1,0:T(8,128)(2,1)S(1)}, u32[]{:S(2)}, u32[]{:S(2)}) %collective-permute-start.36) | collective-permute-done | bytes 262176 | tf_op jit(solution)/shard_map/ppermute | solution.py:24
  177.5 0.9 pad_maximum_fusion.4
  178.5 2.3 %pad_maximum_fusion.2 = f32[2,128,1024]{2,1,0:T(8,128)} fusion(f32[1,128,1024]{2,1,0:T(8,128)} %get-tuple-element.18, f32[1,128,1024]{2,1,0:T(8,128)} %get-tuple-element.23), kind=kLoop, calls=%fused_computation.16 | loop fusion | flops 262144 | bytes 2097152 | tf_op jit(solution)/shard_map/stack | solution.py:253
  180.8 1.0 pad_maximum_fusion.1
  181.8 7.0 %collective-permute-done.18 = bf16[256,1024]{1,0:T(8,128)(2,1)} collective-permute-done((bf16[256,1024]{1,0:T(8,128)(2,1)}, bf16[256,1024]{1,0:T(8,128)(2,1)}, u32[]{:S(2)}, u32[]{:S(2)}) %collective-permute-start.18) | collective-permute-done | bytes 524320 | tf_op jit(solution)/shard_map/ppermute | solution.py:24
  188.9 1.5 fusion
  190.4 9.6 %collective-permute-done.37 = bf16[256,1024]{1,0:T(8,128)(2,1)} collective-permute-done((bf16[256,1024]{1,0:T(8,128)(2,1)}, bf16[256,1024]{1,0:T(8,128)(2,1)}, u32[]{:S(2)}, u32[]{:S(2)}) %collective-permute-start.37) | collective-permute-done | bytes 524320 | tf_op jit(solution)/shard_map/ppermute | solution.py:24
  200.0 1.5 fusion.1
  201.5 1.1 pad_maximum_fusion
  (97 shorter events, 2.5 us)
Async XLA Ops:
  1.6 14.0 %collective-permute-start = (bf16[64,1024]{1,0:T(8,128)(2,1)S(1)}, bf16[64,1024]{1,0:T(8,128)(2,1)S(1)}, u32[]{:S(2)}, u32[]{:S(2)}) collective-permute-start(bf16[64,1024]{1,0:T(8,128)(2,1)S(1)} %get-tuple-element.28), channel_id=1, source_target_pairs={{0,16},{8,24},{16,0},{24,8},{1,17},{9,25},{17,1},{25,9},{2,18},{10... | collective-permute-start | bytes 393224 | tf_op jit(solution)/shard_map/ppermute | solution.py:24
  5.7 11.9 %collective-permute-start.19 = (bf16[64,1024]{1,0:T(8,128)(2,1)S(1)}, bf16[64,1024]{1,0:T(8,128)(2,1)S(1)}, u32[]{:S(2)}, u32[]{:S(2)}) collective-permute-start(bf16[64,1024]{1,0:T(8,128)(2,1)S(1)} %get-tuple-element.29), channel_id=1, source_target_pairs={{0,16},{8,24},{16,0},{24,8},{1,17},{9,25},{17,1},{25,9},{2,18},{10... | collective-permute-start | bytes 393224 | tf_op jit(solution)/shard_map/ppermute | solution.py:24
  18.6 8.6 %collective-permute-start.1 = (bf16[64,1024]{1,0:T(8,128)(2,1)S(1)}, bf16[64,1024]{1,0:T(8,128)(2,1)S(1)}, u32[]{:S(2)}, u32[]{:S(2)}) collective-permute-start(bf16[64,1024]{1,0:T(8,128)(2,1)S(1)} %get-tuple-element.26), channel_id=1, source_target_pairs={{0,8},{8,0},{16,24},{24,16},{1,9},{9,1},{17,25},{25,17},{2,10},{10... | collective-permute-start | bytes 393224 | tf_op jit(solution)/shard_map/ppermute | solution.py:24
  20.7 47.4 %collective-permute-start.7 = (bf16[256,1024]{1,0:T(8,128)(2,1)S(1)}, bf16[256,1024]{1,0:T(8,128)(2,1)}, u32[]{:S(2)}, u32[]{:S(2)}) collective-permute-start(bf16[256,1024]{1,0:T(8,128)(2,1)S(1)} %get-tuple-element.24.refs_0_), channel_id=1, source_target_pairs={{0,2},{1,3},{2,0},{3,1},{4,6},{5,7},{6,4},{7,5},{8,10},{9,11},{10,... | collective-permute-start | bytes 1572872 | tf_op jit(solution)/shard_map/ppermute | solution.py:24
  22.3 52.4 %collective-permute-start.9 = (bf16[256,1024]{1,0:T(8,128)(2,1)S(1)}, bf16[256,1024]{1,0:T(8,128)(2,1)}, u32[]{:S(2)}, u32[]{:S(2)}) collective-permute-start(bf16[256,1024]{1,0:T(8,128)(2,1)S(1)} %get-tuple-element.24.refs_0_), channel_id=1, source_target_pairs={{0,4},{1,5},{2,6},{3,7},{4,0},{5,1},{6,2},{7,3},{8,12},{9,13},{10,... | collective-permute-start | bytes 1572872 | tf_op jit(solution)/shard_map/ppermute | solution.py:24
  23.8 49.8 %collective-permute-start.26 = (bf16[256,1024]{1,0:T(8,128)(2,1)S(1)}, bf16[256,1024]{1,0:T(8,128)(2,1)S(1)}, u32[]{:S(2)}, u32[]{:S(2)}) collective-permute-start(bf16[256,1024]{1,0:T(8,128)(2,1)S(1)} %get-tuple-element.25.refs_0_), channel_id=1, source_target_pairs={{0,2},{1,3},{2,0},{3,1},{4,6},{5,7},{6,4},{7,5},{8,10},{9,11},{10,... | collective-permute-start | bytes 1572872 | tf_op jit(solution)/shard_map/ppermute | solution.py:24
  25.9 5.0 %collective-permute-start.20 = (bf16[64,1024]{1,0:T(8,128)(2,1)S(1)}, bf16[64,1024]{1,0:T(8,128)(2,1)S(1)}, u32[]{:S(2)}, u32[]{:S(2)}) collective-permute-start(bf16[64,1024]{1,0:T(8,128)(2,1)S(1)} %get-tuple-element.27), channel_id=1, source_target_pairs={{0,8},{8,0},{16,24},{24,16},{1,9},{9,1},{17,25},{25,17},{2,10},{10... | collective-permute-start | bytes 393224 | tf_op jit(solution)/shard_map/ppermute | solution.py:24
  27.3 21.1 %collective-permute-start.2 = (bf16[64,1024]{1,0:T(8,128)(2,1)S(1)}, bf16[64,1024]{1,0:T(8,128)(2,1)S(1)}, u32[]{:S(2)}, u32[]{:S(2)}) collective-permute-start(bf16[64,1024]{1,0:T(8,128)(2,1)S(1)} %get-tuple-element.12), channel_id=1, source_target_pairs={{0,2},{1,3},{2,0},{3,1},{4,6},{5,7},{6,4},{7,5},{8,10},{9,11},{10,... | collective-permute-start | bytes 393224 | tf_op jit(solution)/shard_map/ppermute | solution.py:24
  30.8 19.1 %collective-permute-start.3 = (bf16[64,1024]{1,0:T(8,128)(2,1)S(1)}, bf16[64,1024]{1,0:T(8,128)(2,1)S(1)}, u32[]{:S(2)}, u32[]{:S(2)}) collective-permute-start(bf16[64,1024]{1,0:T(8,128)(2,1)S(1)} %get-tuple-element.12), channel_id=1, source_target_pairs={{0,4},{1,5},{2,6},{3,7},{4,0},{5,1},{6,2},{7,3},{8,12},{9,13},{10,... | collective-permute-start | bytes 393224 | tf_op jit(solution)/shard_map/ppermute | solution.py:24
  48.4 5.0 %collective-permute-start.21 = (bf16[64,1024]{1,0:T(8,128)(2,1)S(1)}, bf16[64,1024]{1,0:T(8,128)(2,1)S(1)}, u32[]{:S(2)}, u32[]{:S(2)}) collective-permute-start(bf16[64,1024]{1,0:T(8,128)(2,1)S(1)} %get-tuple-element.14), channel_id=1, source_target_pairs={{0,2},{1,3},{2,0},{3,1},{4,6},{5,7},{6,4},{7,5},{8,10},{9,11},{10,... | collective-permute-start | bytes 393224 | tf_op jit(solution)/shard_map/ppermute | solution.py:24
  49.9 6.3 %collective-permute-start.22 = (bf16[64,1024]{1,0:T(8,128)(2,1)S(1)}, bf16[64,1024]{1,0:T(8,128)(2,1)S(1)}, u32[]{:S(2)}, u32[]{:S(2)}) collective-permute-start(bf16[64,1024]{1,0:T(8,128)(2,1)S(1)} %get-tuple-element.14), channel_id=1, source_target_pairs={{0,4},{1,5},{2,6},{3,7},{4,0},{5,1},{6,2},{7,3},{8,12},{9,13},{10,... | collective-permute-start | bytes 393224 | tf_op jit(solution)/shard_map/ppermute | solution.py:24
  53.4 24.9 %collective-permute-start.28 = (bf16[256,1024]{1,0:T(8,128)(2,1)S(1)}, bf16[256,1024]{1,0:T(8,128)(2,1)S(1)}, u32[]{:S(2)}, u32[]{:S(2)}) collective-permute-start(bf16[256,1024]{1,0:T(8,128)(2,1)S(1)} %get-tuple-element.25.refs_0_), channel_id=1, source_target_pairs={{0,4},{1,5},{2,6},{3,7},{4,0},{5,1},{6,2},{7,3},{8,12},{9,13},{10,... | collective-permute-start | bytes 1572872 | tf_op jit(solution)/shard_map/ppermute | solution.py:24
  56.2 11.3 %collective-permute-start.4 = (bf16[32,1024]{1,0:T(8,128)(2,1)S(1)}, bf16[32,1024]{1,0:T(8,128)(2,1)S(1)}, u32[]{:S(2)}, u32[]{:S(2)}) collective-permute-start(bf16[32,1024]{1,0:T(8,128)(2,1)S(1)} %slice.92), channel_id=1, source_target_pairs={{0,4},{1,5},{2,6},{3,7},{4,0},{5,1},{6,2},{7,3},{8,12},{9,13},{10,... | collective-permute-start | bytes 196616 | tf_op jit(solution)/shard_map/ppermute | solution.py:24
  67.6 4.3 %collective-permute-start.5 = (bf16[32,1024]{1,0:T(8,128)(2,1)S(1)}, bf16[32,1024]{1,0:T(8,128)(2,1)S(1)}, u32[]{:S(2)}, u32[]{:S(2)}) collective-permute-start(bf16[32,1024]{1,0:T(8,128)(2,1)S(1)} %slice.93), channel_id=1, source_target_pairs={{0,2},{1,3},{2,0},{3,1},{4,6},{5,7},{6,4},{7,5},{8,10},{9,11},{10,... | collective-permute-start | bytes 196616 | tf_op jit(solution)/shard_map/ppermute | solution.py:24
  68.1 5.9 %collective-permute-start.23 = (bf16[32,1024]{1,0:T(8,128)(2,1)S(1)}, bf16[32,1024]{1,0:T(8,128)(2,1)S(1)}, u32[]{:S(2)}, u32[]{:S(2)}) collective-permute-start(bf16[32,1024]{1,0:T(8,128)(2,1)S(1)} %slice.98), channel_id=1, source_target_pairs={{0,4},{1,5},{2,6},{3,7},{4,0},{5,1},{6,2},{7,3},{8,12},{9,13},{10,... | collective-permute-start | bytes 196616 | tf_op jit(solution)/shard_map/ppermute | solution.py:24
  71.8 8.6 %collective-permute-start.8 = (bf16[128,1024]{1,0:T(8,128)(2,1)S(1)}, bf16[128,1024]{1,0:T(8,128)(2,1)S(1)}, u32[]{:S(2)}, u32[]{:S(2)}) collective-permute-start(bf16[128,1024]{1,0:T(8,128)(2,1)S(1)} %slice.94), channel_id=1, source_target_pairs={{0,4},{1,5},{2,6},{3,7},{4,0},{5,1},{6,2},{7,3},{8,12},{9,13},{10,... | collective-permute-start | bytes 786440 | tf_op jit(solution)/shard_map/ppermute | solution.py:24
  73.6 17.1 %copy-start.1 = (bf16[256,1024]{1,0:T(8,128)(2,1)}, bf16[256,1024]{1,0:T(8,128)(2,1)S(1)}, u32[]{:S(2)}) copy-start(bf16[256,1024]{1,0:T(8,128)(2,1)S(1)} %collective-permute-done.26.refs_1_) | copy-start | bytes 1572868
  73.6 4.3 %collective-permute-start.24 = (bf16[32,1024]{1,0:T(8,128)(2,1)S(1)}, bf16[32,1024]{1,0:T(8,128)(2,1)S(1)}, u32[]{:S(2)}, u32[]{:S(2)}) collective-permute-start(bf16[32,1024]{1,0:T(8,128)(2,1)S(1)} %slice.99), channel_id=1, source_target_pairs={{0,2},{1,3},{2,0},{3,1},{4,6},{5,7},{6,4},{7,5},{8,10},{9,11},{10,... | collective-permute-start | bytes 196616 | tf_op jit(solution)/shard_map/ppermute | solution.py:24
  74.0 9.3 %collective-permute-start.27 = (bf16[128,1024]{1,0:T(8,128)(2,1)S(1)}, bf16[128,1024]{1,0:T(8,128)(2,1)S(1)}, u32[]{:S(2)}, u32[]{:S(2)}) collective-permute-start(bf16[128,1024]{1,0:T(8,128)(2,1)S(1)} %slice.100), channel_id=1, source_target_pairs={{0,4},{1,5},{2,6},{3,7},{4,0},{5,1},{6,2},{7,3},{8,12},{9,13},{10,... | collective-permute-start | bytes 786440 | tf_op jit(solution)/shard_map/ppermute | solution.py:24
  74.6 15.5 %collective-permute-start.6 = (bf16[256,1024]{1,0:T(8,128)(2,1)S(1)}, bf16[256,1024]{1,0:T(8,128)(2,1)S(1)}, u32[]{:S(2)}, u32[]{:S(2)}) collective-permute-start(bf16[256,1024]{1,0:T(8,128)(2,1)S(1)} %get-tuple-element.38), channel_id=1, source_target_pairs={{0,1},{1,0},{2,3},{3,2},{4,5},{5,4},{6,7},{7,6},{8,9},{9,8},{10,11... | collective-permute-start | bytes 1572872 | tf_op jit(solution)/shard_map/ppermute | solution.py:24
  78.0 9.2 %collective-permute-start.10 = (bf16[128,1024]{1,0:T(8,128)(2,1)S(1)}, bf16[128,1024]{1,0:T(8,128)(2,1)S(1)}, u32[]{:S(2)}, u32[]{:S(2)}) collective-permute-start(bf16[128,1024]{1,0:T(8,128)(2,1)S(1)} %slice.95), channel_id=1, source_target_pairs={{0,2},{1,3},{2,0},{3,1},{4,6},{5,7},{6,4},{7,5},{8,10},{9,11},{10,... | collective-permute-start | bytes 786440 | tf_op jit(solution)/shard_map/ppermute | solution.py:24
  78.3 12.4 %collective-permute-start.25 = (bf16[256,1024]{1,0:T(8,128)(2,1)S(1)}, bf16[256,1024]{1,0:T(8,128)(2,1)S(1)}, u32[]{:S(2)}, u32[]{:S(2)}) collective-permute-start(bf16[256,1024]{1,0:T(8,128)(2,1)S(1)} %get-tuple-element.42), channel_id=1, source_target_pairs={{0,1},{1,0},{2,3},{3,2},{4,5},{5,4},{6,7},{7,6},{8,9},{9,8},{10,11... | collective-permute-start | bytes 1572872 | tf_op jit(solution)/shard_map/ppermute | solution.py:24
  80.5 9.6 %collective-permute-start.29 = (bf16[128,1024]{1,0:T(8,128)(2,1)S(1)}, bf16[128,1024]{1,0:T(8,128)(2,1)S(1)}, u32[]{:S(2)}, u32[]{:S(2)}) collective-permute-start(bf16[128,1024]{1,0:T(8,128)(2,1)S(1)} %slice.101), channel_id=1, source_target_pairs={{0,2},{1,3},{2,0},{3,1},{4,6},{5,7},{6,4},{7,5},{8,10},{9,11},{10,... | collective-permute-start | bytes 786440 | tf_op jit(solution)/shard_map/ppermute | solution.py:24
  83.3 8.0 %collective-permute-start.12 = (bf16[256,1024]{1,0:T(8,128)(2,1)S(1)}, bf16[256,1024]{1,0:T(8,128)(2,1)S(1)}, u32[]{:S(2)}, u32[]{:S(2)}) collective-permute-start(bf16[256,1024]{1,0:T(8,128)(2,1)S(1)} %get-tuple-element.24.refs_0_), channel_id=1, source_target_pairs={{0,1},{1,0},{2,3},{3,2},{4,5},{5,4},{6,7},{7,6},{8,9},{9,8},{10,11... | collective-permute-start | bytes 1572872 | tf_op jit(solution)/shard_map/ppermute | solution.py:24
  87.2 18.0 %collective-permute-start.31 = (bf16[256,1024]{1,0:T(8,128)(2,1)S(1)}, bf16[256,1024]{1,0:T(8,128)(2,1)S(1)}, u32[]{:S(2)}, u32[]{:S(2)}) collective-permute-start(bf16[256,1024]{1,0:T(8,128)(2,1)S(1)} %get-tuple-element.25.refs_0_), channel_id=1, source_target_pairs={{0,1},{1,0},{2,3},{3,2},{4,5},{5,4},{6,7},{7,6},{8,9},{9,8},{10,11... | collective-permute-start | bytes 1572872 | tf_op jit(solution)/shard_map/ppermute | solution.py:24
  90.1 2.3 %collective-permute-start.13 = (bf16[256,1024]{1,0:T(8,128)(2,1)}, bf16[256,1024]{1,0:T(8,128)(2,1)S(1)}, u32[]{:S(2)}, u32[]{:S(2)}) collective-permute-start(bf16[256,1024]{1,0:T(8,128)(2,1)} %collective-permute-done.7.refs_1_), channel_id=1, source_target_pairs={{0,1},{1,0},{2,3},{3,2},{4,5},{5,4},{6,7},{7,6},{8,9},{9,8},{10,11... | collective-permute-start | bytes 1572872 | tf_op jit(solution)/shard_map/ppermute | solution.py:24
  90.1 3.6 %collective-permute-start.14 = (bf16[256,1024]{1,0:T(8,128)(2,1)}, bf16[256,1024]{1,0:T(8,128)(2,1)S(1)}, u32[]{:S(2)}, u32[]{:S(2)}) collective-permute-start(bf16[256,1024]{1,0:T(8,128)(2,1)} %collective-permute-done.9.refs_2_), channel_id=1, source_target_pairs={{0,1},{1,0},{2,3},{3,2},{4,5},{5,4},{6,7},{7,6},{8,9},{9,8},{10,11... | collective-permute-start | bytes 1572872 | tf_op jit(solution)/shard_map/ppermute | solution.py:24
  90.7 8.9 %collective-permute-start.11 = (bf16[256,1024]{1,0:T(8,128)(2,1)S(1)}, bf16[256,1024]{1,0:T(8,128)(2,1)S(1)}, u32[]{:S(2)}, u32[]{:S(2)}) collective-permute-start(bf16[256,1024]{1,0:T(8,128)(2,1)S(1)} %constant_dynamic-update-slice_fusion.11.refs_0_), channel_id=1, source_target_pairs={{0,1},{1,0},{2,3},{3,2},{4,5},{5,4},{6,7},{7,6},{8,9},{9,8},{10,11... | collective-permute-start | bytes 1572872 | tf_op jit(solution)/shard_map/ppermute | solution.py:24
  90.8 1.0 copy-start.2
  90.9 3.0 %copy-start = (bf16[2048,1024]{1,0:T(8,128)(2,1)S(1)}, bf16[2048,1024]{1,0:T(8,128)(2,1)}, u32[]{:S(2)}) copy-start(bf16[2048,1024]{1,0:T(8,128)(2,1)} %refs_3_.3) | copy-start | bytes 12582916
  91.9 13.3 %collective-permute-start.32 = (bf16[256,1024]{1,0:T(8,128)(2,1)S(1)}, bf16[256,1024]{1,0:T(8,128)(2,1)S(1)}, u32[]{:S(2)}, u32[]{:S(2)}) collective-permute-start(bf16[256,1024]{1,0:T(8,128)(2,1)S(1)} %copy-done.2), channel_id=1, source_target_pairs={{0,1},{1,0},{2,3},{3,2},{4,5},{5,4},{6,7},{7,6},{8,9},{9,8},{10,11... | collective-permute-start | bytes 1572872 | tf_op jit(solution)/shard_map/ppermute | solution.py:24
  92.4 12.8 %collective-permute-start.33 = (bf16[256,1024]{1,0:T(8,128)(2,1)S(1)}, bf16[256,1024]{1,0:T(8,128)(2,1)S(1)}, u32[]{:S(2)}, u32[]{:S(2)}) collective-permute-start(bf16[256,1024]{1,0:T(8,128)(2,1)S(1)} %collective-permute-done.28.refs_2_), channel_id=1, source_target_pairs={{0,1},{1,0},{2,3},{3,2},{4,5},{5,4},{6,7},{7,6},{8,9},{9,8},{10,11... | collective-permute-start | bytes 1572872 | tf_op jit(solution)/shard_map/ppermute | solution.py:24
  93.7 16.5 %collective-permute-start.30 = (bf16[256,1024]{1,0:T(8,128)(2,1)S(1)}, bf16[256,1024]{1,0:T(8,128)(2,1)S(1)}, u32[]{:S(2)}, u32[]{:S(2)}) collective-permute-start(bf16[256,1024]{1,0:T(8,128)(2,1)S(1)} %constant_dynamic-update-slice_fusion.24.refs_0_), channel_id=1, source_target_pairs={{0,1},{1,0},{2,3},{3,2},{4,5},{5,4},{6,7},{7,6},{8,9},{9,8},{10,11... | collective-permute-start | bytes 1572872 | tf_op jit(solution)/shard_map/ppermute | solution.py:24
  104.6 14.8 %collective-permute-start.15 = (bf16[256,1024]{1,0:T(8,128)(2,1)S(1)}, bf16[256,1024]{1,0:T(8,128)(2,1)S(1)}, u32[]{:S(2)}, u32[]{:S(2)}) collective-permute-start(bf16[256,1024]{1,0:T(8,128)(2,1)S(1)} %get-tuple-element.8), channel_id=1, source_target_pairs={{0,8},{8,0},{16,24},{24,16},{1,9},{9,1},{17,25},{25,17},{2,10},{10... | collective-permute-start | bytes 1572872 | tf_op jit(solution)/shard_map/ppermute | solution.py:24
  115.3 20.5 %collective-permute-start.34 = (bf16[256,1024]{1,0:T(8,128)(2,1)S(1)}, bf16[256,1024]{1,0:T(8,128)(2,1)S(1)}, u32[]{:S(2)}, u32[]{:S(2)}) collective-permute-start(bf16[256,1024]{1,0:T(8,128)(2,1)S(1)} %get-tuple-element.10), channel_id=1, source_target_pairs={{0,8},{8,0},{16,24},{24,16},{1,9},{9,1},{17,25},{25,17},{2,10},{10... | collective-permute-start | bytes 1572872 | tf_op jit(solution)/shard_map/ppermute | solution.py:24
  119.6 30.7 %copy-start.5 = (f32[2,128,1024]{2,1,0:T(8,128)S(1)}, f32[2,128,1024]{2,1,0:T(8,128)}, u32[]{:S(2)}) copy-start(f32[2,128,1024]{2,1,0:T(8,128)} %param.10) | copy-start | bytes 3145732
  119.7 30.7 %copy-start.6 = (f32[2,128,1024]{2,1,0:T(8,128)S(1)}, f32[2,128,1024]{2,1,0:T(8,128)}, u32[]{:S(2)}) copy-start(f32[2,128,1024]{2,1,0:T(8,128)} %param.9) | copy-start | bytes 3145732
  119.7 17.9 %collective-permute-start.16 = (bf16[128,1024]{1,0:T(8,128)(2,1)S(1)}, bf16[128,1024]{1,0:T(8,128)(2,1)S(1)}, u32[]{:S(2)}, u32[]{:S(2)}) collective-permute-start(bf16[128,1024]{1,0:T(8,128)(2,1)S(1)} %slice.161), channel_id=1, source_target_pairs={{0,16},{8,24},{16,0},{24,8},{1,17},{9,25},{17,1},{25,9},{2,18},{10... | collective-permute-start | bytes 786440 | tf_op jit(solution)/shard_map/ppermute | solution.py:24
  136.0 14.3 %collective-permute-start.35 = (bf16[128,1024]{1,0:T(8,128)(2,1)S(1)}, bf16[128,1024]{1,0:T(8,128)(2,1)S(1)}, u32[]{:S(2)}, u32[]{:S(2)}) collective-permute-start(bf16[128,1024]{1,0:T(8,128)(2,1)S(1)} %slice.160), channel_id=1, source_target_pairs={{0,16},{8,24},{16,0},{24,8},{1,17},{9,25},{17,1},{25,9},{2,18},{10... | collective-permute-start | bytes 786440 | tf_op jit(solution)/shard_map/ppermute | solution.py:24
  152.0 25.5 %copy-start.3 = (bf16[128,1024]{1,0:T(8,128)(2,1)}, bf16[128,1024]{1,0:T(8,128)(2,1)S(1)}, u32[]{:S(2)}) copy-start(bf16[128,1024]{1,0:T(8,128)(2,1)S(1)} %get-tuple-element.22) | copy-start | bytes 786436
  152.0 20.0 %collective-permute-start.17 = (bf16[128,1024]{1,0:T(8,128)(2,1)S(1)}, bf16[128,1024]{1,0:T(8,128)(2,1)S(1)}, u32[]{:S(2)}, u32[]{:S(2)}) collective-permute-start(bf16[128,1024]{1,0:T(8,128)(2,1)S(1)} %get-tuple-element.22), channel_id=1, source_target_pairs={{0,16},{8,24},{16,0},{24,8},{1,17},{9,25},{17,1},{25,9},{2,18},{10... | collective-permute-start | bytes 786440 | tf_op jit(solution)/shard_map/ppermute | solution.py:24
  152.0 25.5 %collective-permute-start.36 = (bf16[128,1024]{1,0:T(8,128)(2,1)S(1)}, bf16[128,1024]{1,0:T(8,128)(2,1)S(1)}, u32[]{:S(2)}, u32[]{:S(2)}) collective-permute-start(bf16[128,1024]{1,0:T(8,128)(2,1)S(1)} %get-tuple-element.19), channel_id=1, source_target_pairs={{0,16},{8,24},{16,0},{24,8},{1,17},{9,25},{17,1},{25,9},{2,18},{10... | collective-permute-start | bytes 786440 | tf_op jit(solution)/shard_map/ppermute | solution.py:24
  172.0 6.4 %copy-start.9 = (bf16[128,1024]{1,0:T(8,128)(2,1)}, bf16[128,1024]{1,0:T(8,128)(2,1)S(1)}, u32[]{:S(2)}) copy-start(bf16[128,1024]{1,0:T(8,128)(2,1)S(1)} %collective-permute-done.17) | copy-start | bytes 786436
  172.9 16.0 %collective-permute-start.18 = (bf16[256,1024]{1,0:T(8,128)(2,1)}, bf16[256,1024]{1,0:T(8,128)(2,1)}, u32[]{:S(2)}, u32[]{:S(2)}) collective-permute-start(bf16[256,1024]{1,0:T(8,128)(2,1)} %pad_maximum_fusion.3), channel_id=1, source_target_pairs={{0,8},{8,0},{16,24},{24,16},{1,9},{9,1},{17,25},{25,17},{2,10},{10... | collective-permute-start | bytes 1572872 | tf_op jit(solution)/shard_map/ppermute | solution.py:24
  177.5 0.9 copy-start.7
  178.4 21.6 %collective-permute-start.37 = (bf16[256,1024]{1,0:T(8,128)(2,1)}, bf16[256,1024]{1,0:T(8,128)(2,1)}, u32[]{:S(2)}, u32[]{:S(2)}) collective-permute-start(bf16[256,1024]{1,0:T(8,128)(2,1)} %pad_maximum_fusion.4), channel_id=1, source_target_pairs={{0,8},{8,0},{16,24},{24,16},{1,9},{9,1},{17,25},{25,17},{2,10},{10... | collective-permute-start | bytes 1572872 | tf_op jit(solution)/shard_map/ppermute | solution.py:24
  178.4 10.4 %copy-start.4 = (bf16[128,1024]{1,0:T(8,128)(2,1)S(1)}, bf16[128,1024]{1,0:T(8,128)(2,1)}, u32[]{:S(2)}) copy-start(bf16[128,1024]{1,0:T(8,128)(2,1)} %copy-done.3) | copy-start | bytes 786436
  178.4 10.4 %copy-start.10 = (bf16[128,1024]{1,0:T(8,128)(2,1)S(1)}, bf16[128,1024]{1,0:T(8,128)(2,1)}, u32[]{:S(2)}) copy-start(bf16[128,1024]{1,0:T(8,128)(2,1)} %copy-done.9) | copy-start | bytes 786436
  180.8 19.2 %copy-start.8 = (bf16[128,1024]{1,0:T(8,128)(2,1)S(1)}, bf16[128,1024]{1,0:T(8,128)(2,1)}, u32[]{:S(2)}) copy-start(bf16[128,1024]{1,0:T(8,128)(2,1)} %copy-done.7) | copy-start | bytes 786436

commit v2 on v0

v2 whole, which is shorter than its diff:
```python
import functools
import math

import jax
import jax.numpy as jnp
from jax import lax
from jax.experimental import pallas as pl
from jax.experimental.pallas import tpu as pltpu
from jax.sharding import PartitionSpec as P

MATS = 2
STEP = 10

beta_first = 0.9
beta_second = 0.999
epsilon = 1e-08

TRANSPOSED = (((0,), (0,)), ((), ()))
MIB = 1 << 20


def swap(value, axis, mask):
    size = lax.axis_size(axis)
    return lax.ppermute(value, axis, [(i, i ^ mask) for i in range(size)])


def bits_of(size):
    return [1 << k for k in range(size.bit_length() - 1)]


def after(value, *others):
    return lax.optimization_barrier((value,) + others)[0]


def spread(block, bits):
    if len(bits) == 2:
        low, high = bits
        masks = (0, low, high, low | high)
        return {mask: swap(block, "fsdp", mask) if mask else block for mask in masks}
    blocks = {0: block}
    for bit in bits:
        blocks.update({mask ^ bit: swap(held, "fsdp", bit) for mask, held in list(blocks.items())})
    return blocks


def spread_near(block, bits):
    if len(bits) == 2:
        low, high = bits
        half = block.shape[0] // 2
        top, bottom = block[:half], block[half:]
        low_top, high_bottom = swap(top, "fsdp", low), swap(bottom, "fsdp", high)
        far = [swap(low_top, "fsdp", high), swap(high_bottom, "fsdp", low)]
        by_low = [low_top, swap(after(bottom, low_top), "fsdp", low)]
        by_high = [swap(after(top, high_bottom), "fsdp", high), high_bottom]
        first = [low_top, high_bottom]
        return {0: [block], low: by_low, high: by_high}, {low | high: far}, first
    blocks = {mask: [held] for mask, held in spread(block, bits).items()}
    last = max(blocks)
    near = {mask: held for mask, held in blocks.items() if mask != last}
    return near, {last: blocks[last]}, []


def with_partner(blocks, own=None):
    other = {
        mask ^ 1: [own] if mask == 0 and own is not None else [swap(x, "fsdp", 1) for x in held]
        for mask, held in blocks.items()
    }
    return {**blocks, **other}


def tile_of(size):
    return min(size, 256)


def whole(shape):
    return pl.BlockSpec(shape, lambda *_: (0,) * len(shape))


def gather_body(order, per, count, here, same, other, full):
    spot = 0
    for mask in order:
        for sub in range(per):
            away = ((here[0] ^ mask) * per + sub) ^ here[1]
            at = pl.multiple_of((away >> 1) * count, count)
            rows = jnp.where(
                (away & 1) == 0, same[pl.ds(at, count), :], other[pl.ds(at, count), :]
            )
            full[pl.ds(spot * count, count), :] = rows
            spot += 1


def gather_projector(same, other, here, order, per):
    rows, kv = same.shape
    count = 2 * rows // (len(order) * per)
    return pl.pallas_call(
        functools.partial(gather_body, order, per, count),
        grid_spec=pltpu.PrefetchScalarGridSpec(
            num_scalar_prefetch=1,
            grid=(1,),
            in_specs=[whole((rows, kv))] * 2,
            out_specs=whole((2 * rows, kv)),
        ),
        out_shape=jax.ShapeDtypeStruct((2 * rows, kv), same.dtype),
        compiler_params=pltpu.CompilerParams(vmem_limit_bytes=24 * MIB),
        cost_estimate=pl.CostEstimate(flops=0, bytes_accessed=8 * rows * kv, transcendentals=0),
    )(here, same, other)


def block_term(block, rows, here, mask, tile):
    pieces = [piece[:, tile] for piece in block]
    left = pieces[0] if len(pieces) == 1 else jnp.concatenate(pieces, axis=0)
    count = left.shape[0]
    start = pl.multiple_of((here[1] ^ mask) * count, count)
    return lax.dot_general(
        left, rows[pl.ds(start, count), :], TRANSPOSED, preferred_element_type=jnp.float32
    )


def regroup(refs, shape):
    refs = list(refs)
    return [[refs.pop(0) for _ in range(length)] for length in shape]


def call_in_vmem(body, here, operands, outputs, flops, cost=1.0):
    moved = sum(x.size * x.dtype.itemsize for x in list(operands) + list(outputs))
    return pl.pallas_call(
        body,
        grid_spec=pltpu.PrefetchScalarGridSpec(
            num_scalar_prefetch=1,
            grid=(),
            in_specs=[pl.BlockSpec(memory_space=pltpu.VMEM)] * len(operands),
            out_specs=[pl.BlockSpec(memory_space=pltpu.VMEM)] * len(outputs),
        ),
        out_shape=outputs,
        compiler_params=pltpu.CompilerParams(vmem_limit_bytes=32 * MIB),
        cost_estimate=pl.CostEstimate(
            flops=int(flops * cost), bytes_accessed=moved, transcendentals=0
        ),
    )(here, *operands)


def flat(blocks):
    return [piece for block in blocks.values() for piece in block]


def depth(blocks):
    return sum(piece.shape[0] for piece in flat(blocks))


def heads_body(masks, shape, part, scale, here, *refs):
    groups = regroup(refs[: sum(shape)], shape)
    rows, outs = refs[sum(shape)], refs[sum(shape) + 1 :]
    size = outs[0].shape[0] * len(outs)
    total = None
    for mask, block in zip(masks, groups):
        term = block_term(block, rows, here, mask, pl.ds(part * size, size))
        total = term if total is None else total + term
    for k, out in enumerate(outs):
        count = out.shape[0]
        out[...] = (total[k * count : (k + 1) * count] * scale).astype(out.dtype)


def heads_product(blocks, here, layer_input, part, pieces, dtype, scale):
    half = flat(blocks)[0].shape[1] // 2
    width = layer_input.shape[1]
    shape = [len(block) for block in blocks.values()]
    return call_in_vmem(
        functools.partial(heads_body, list(blocks), shape, part, scale),
        here,
        flat(blocks) + [layer_input],
        [jax.ShapeDtypeStruct((half // pieces, width), dtype)] * pieces,
        2 * depth(blocks) * half * width,
    )


def adam_body(aliased, keep, received, moment_first, moment_second, *refs):
    first_out, second_out, direction_out = refs[-3:]
    projected = keep[...] + received[...].astype(jnp.float32)
    first = beta_first * moment_first[0] + (1.0 - beta_first) * projected
    second = beta_second * moment_second[0] + (1.0 - beta_second) * projected * projected
    first_out[0] = first
    second_out[0] = second
    direction = (
        first
        / (1.0 - beta_first**STEP)
        / (jnp.sqrt(second / (1.0 - beta_second**STEP)) + epsilon)
    )
    direction_out[...] = direction.astype(direction_out.dtype)


def adam(matrix, keep, received, moment_first, moment_second, written):
    rows, width = keep.shape
    tile = tile_of(width)
    flat = pl.BlockSpec((rows, tile), lambda i: (0, i))
    deep = pl.BlockSpec((1, rows, tile), lambda i: (matrix, 0, i))
    in_specs = [flat, flat, deep, deep] + [pl.BlockSpec(memory_space=pl.ANY)] * len(written)
    return pl.pallas_call(
        functools.partial(adam_body, len(written)),
        grid=(width // tile,),
        in_specs=in_specs,
        out_specs=[deep, deep, flat],
        out_shape=[
            jax.ShapeDtypeStruct(moment_first.shape, jnp.float32),
            jax.ShapeDtypeStruct(moment_second.shape, jnp.float32),
            jax.ShapeDtypeStruct((rows, width), jnp.bfloat16),
        ],
        input_output_aliases={4 + k: k for k in range(len(written))},
        cost_estimate=pl.CostEstimate(
            flops=12 * rows * width, bytes_accessed=24 * rows * width, transcendentals=rows * width
        ),
    )(keep, received, moment_first, moment_second, *written)


def update_body(count, projector, *refs):
    out = refs[-1]
    rows = refs[0].shape[0]
    total = None
    for k in range(count):
        term = lax.dot_general(
            projector[pl.ds(k * rows, rows), :],
            refs[k][...],
            TRANSPOSED,
            preferred_element_type=jnp.float32,
        )
        total = term if total is None else total + term
    out[0] = total.astype(out.dtype)


def back_project(matrix, projector, directions, written):
    count = len(directions)
    rows, width = directions[0].shape
    rank, share = projector.shape
    tile = tile_of(width)
    in_specs = [whole((rank, share))]
    in_specs += [pl.BlockSpec((rows, tile), lambda i: (0, i))] * count
    in_specs += [pl.BlockSpec(memory_space=pl.ANY)] * len(written)
    return pl.pallas_call(
        functools.partial(update_body, count),
        grid=(width // tile,),
        in_specs=in_specs,
        out_specs=pl.BlockSpec((1, share, tile), lambda i: (matrix, 0, i)),
        out_shape=jax.ShapeDtypeStruct((MATS, share, width), jnp.bfloat16),
        input_output_aliases={1 + count + k: k for k in range(len(written))},
        cost_estimate=pl.CostEstimate(
            flops=2 * rank * share * width,
            bytes_accessed=2 * (rank + share) * width,
            transcendentals=0,
        ),
    )(projector, *directions, *written)


def product_body(masks, shape, here, *refs):
    groups = regroup(refs[: sum(shape)], shape)
    rows, out = refs[sum(shape) :]
    size = tile_of(out.shape[0])
    for at in range(0, out.shape[0], size):
        tile = pl.ds(at, size)
        total = None
        for mask, block in zip(masks, groups):
            term = block_term(block, rows, here, mask, tile)
            total = term if total is None else total + term
        out[tile, :] = total


def add_products(blocks, here, layer_input):
    kv = flat(blocks)[0].shape[1]
    width = layer_input.shape[1]
    shape = [len(block) for block in blocks.values()]
    return call_in_vmem(
        functools.partial(product_body, list(blocks), shape),
        here,
        flat(blocks) + [layer_input],
        [jax.ShapeDtypeStruct((kv, width), jnp.float32)],
        2 * depth(blocks) * kv * width,
        1.0,
    )[0]


def project_body(masks, shape, scale, here, *refs):
    groups = regroup(refs[: sum(shape)], shape)
    rows, partial, projector, product = refs[sum(shape) : sum(shape) + 4]
    outs = refs[sum(shape) + 4 :]
    size = tile_of(product.shape[0])
    for at in range(0, product.shape[0], size):
        tile = pl.ds(at, size)
        total = partial[tile, :]
        for mask, block in zip(masks, groups):
            total += block_term(block, rows, here, mask, tile)
        product[tile, :] = total.astype(product.dtype)
    apply_body(0, scale, here, projector, product, *outs)


def apply_body(first, scale, here, projector, product, *outs):
    size = outs[0].shape[0] * len(outs)
    term = jnp.dot(
        projector[pl.ds(first, size), :], product[...], preferred_element_type=jnp.float32
    )
    for k, out in enumerate(outs):
        count = out.shape[0]
        out[...] = (term[k * count : (k + 1) * count] * scale).astype(out.dtype)


def project(blocks, here, layer_input, partial, projector, pieces, scale):
    kv, width = partial.shape
    half = projector.shape[0] // 2
    shape = [len(block) for block in blocks.values()]
    product, *sends = call_in_vmem(
        functools.partial(project_body, list(blocks), shape, scale),
        here,
        flat(blocks) + [layer_input, partial, projector],
        [jax.ShapeDtypeStruct((kv, width), jnp.bfloat16)]
        + [jax.ShapeDtypeStruct((half // pieces, width), jnp.bfloat16)] * pieces,
        2 * depth(blocks) * kv * width + 2 * half * kv * width,
    )
    return product, sends


def apply_rest(projector, product, here, pieces, scale):
    half = projector.shape[0] // 2
    kv, width = product.shape
    return call_in_vmem(
        functools.partial(apply_body, half, scale),
        here,
        [projector, product],
        [jax.ShapeDtypeStruct((half // pieces, width), jnp.float32)] * pieces,
        2 * half * kv * width,
    )


def on_device(layer_input, cotangent, candidates, moment_first, moment_second, owners):
    replicas = lax.axis_size("dp")
    members = lax.axis_size("fsdp")
    me_dp = lax.axis_index("dp")
    me_fsdp = lax.axis_index("fsdp")
    dp_bits = bits_of(replicas)
    far_bits = bits_of(members)[1:]
    scale = 1.0 / math.sqrt(layer_input.shape[0] * replicas)
    kv_share = candidates.shape[2] // replicas
    per = members // replicas

    order = [0]
    for bit in reversed(dp_bits):
        order = [mask ^ bit for mask in order] + order

    here = jnp.stack([me_dp, me_fsdp]).astype(jnp.int32)

    def owned(matrix, value, *others):
        for at, bit in enumerate(dp_bits):
            if at == 1 and others:
                value = after(value, *others)
            other = swap(value, "dp", bit)
            mine = (me_dp & bit) == (owners[matrix] & bit)
            value = jnp.where(mine, value, other)
        return value

    def assembled(value, *others):
        blocks = spread(value, far_bits)
        same = jnp.concatenate([blocks[mask] for mask in sorted(blocks)], axis=0)
        other = swap(after(same, *others), "fsdp", 1)
        return gather_projector(same, other, here, order, per), same

    pieces = max(replicas // 2, 1)

    own_other = swap(cotangent[0], "fsdp", 1)
    near, far, arrived = spread_near(cotangent[0], far_bits)
    first_owned = owned(0, candidates[0, 0].T, own_other, *arrived)
    spread_first = flat(near) + [own_other]
    near_all = with_partner(near, own_other)
    projector_0, same_0 = assembled(after(first_owned, *spread_first), *flat(near_all))
    far_all = with_partner(far)
    partial = add_products(near_all, here, layer_input)
    product, send_0 = project(far_all, here, layer_input, partial, projector_0, pieces, scale)
    keep_0 = apply_rest(projector_0, product, here, pieces, scale)

    second_owned = owned(1, after(candidates[1, 0].T, first_owned))
    projector_1, _ = assembled(after(second_owned, same_0, *flat(far)))
    heads = lax.dot_general(
        cotangent[1], projector_1, (((1,), (1,)), ((), ())), preferred_element_type=jnp.float32
    ).astype(jnp.bfloat16)
    blocks = with_partner({mask: [held] for mask, held in spread(heads, far_bits).items()})
    send_1 = heads_product(blocks, here, layer_input, 0, pieces, jnp.bfloat16, scale)
    keep_1 = heads_product(blocks, here, layer_input, 1, pieces, jnp.float32, scale)

    def reduced(sends, keeps):
        for bit in dp_bits[:-1]:
            totals = [
                keep + swap(send, "dp", bit).astype(jnp.float32)
                for send, keep in zip(sends, keeps)
            ]
            half = len(totals) // 2
            sends = [total.astype(jnp.bfloat16) for total in totals[:half]]
            keeps = totals[half:]
        return keeps[0], swap(sends[0], "dp", dp_bits[-1])

    updates, moments = (), ()
    for matrix, sends, keeps, projector in (
        (0, send_0, keep_0, projector_0),
        (1, send_1, keep_1, projector_1),
    ):
        own = lax.dynamic_slice_in_dim(projector, me_dp * kv_share, kv_share, 1)
        keep, received = reduced(sends, keeps)
        first, second, direction = adam(
            matrix, keep, received, moment_first, moment_second, moments
        )
        moments = (first, second)
        directions = [direction]
        for bit in reversed(dp_bits):
            directions = [swap(piece, "dp", bit) for piece in directions] + directions
        updates = (back_project(matrix, own, directions, updates),)
    return updates + moments


def solution(mesh):
    placed = (
        P("dp", "fsdp"),
        P(None, ("dp", "fsdp"), None),
        P(None, "dp", None, "fsdp"),
        P(None, "dp", "fsdp"),
        P(None, "dp", "fsdp"),
        P(),
    )
    return jax.shard_map(
        on_device,
        mesh=mesh,
        in_specs=placed,
        out_specs=(P(None, "dp", "fsdp"), P(None, "dp", "fsdp"), P(None, "dp", "fsdp")),
        check_vma=False,
    )
```

time: 374 us -> 170 us (0.45)
  waiting for transfers between devices: 327 us -> 68.5 us
  starting transfers between devices: 0.37 us -> 41.6 us
  Pallas kernels: 0 us -> 29.1 us
  matrix products: 20.2 us -> 1.52 us
  local copies, waits for them, and re-layouts: 3.04 us -> 20.2 us
  between operations: 15.1 us -> 3.49 us
    all_gather x6 -> x0, waiting for transfers between devices: 152 us -> none  [the longest x2 52.5 us: on_device(): lax.all_gather(direction, 'dp', axis=0, tiled=True)]
    psum x1 -> x0, waiting for transfers between devices: 89 us -> none  [from_root(): return lax.psum(kept, axis)]
    reduce_scatter x2 -> x0, waiting for transfers between devices: 85.1 us -> none  [on_device(): lax.psum_scatter(partial_value, 'dp', scatter_dimension=0, tiled=True)]
    ppermute x0 -> x44, waiting for transfers between devices: none -> 68.5 us  [swap(): return lax.ppermute(value, axis, [(i, i ^ mask) for i in range(size)])]
    ppermute x0 -> x44, starting transfers between devices: none -> 41.6 us  [swap(): return lax.ppermute(value, axis, [(i, i ^ mask) for i in range(size)])]
    pallas_call x0 -> x11, Pallas kernels: none -> 29.1 us  [the longest x5 12.2 us: call_in_vmem(): pl.pallas_call(body, grid_spec=pltpu.PrefetchScalarGridSpec(num_scalar_pr...]
    dot_general x6 -> x1, matrix products: 20.2 us -> 1.52 us  [on_device(): lax.dot_general(cotangent[1], projector_1, (((1,), (1,)), ((), ())), pref...]
    unnamed x6 -> x60, local copies, waits for them, and re-layouts: 0.01 us -> 14 us
  transfers between devices with their start and end apart: 9 -> 44, of which waited for: 9 -> 17; matrix products, arithmetic and copies ran while one was open for 5% -> 7% of each run, Pallas kernels for 0% -> 15%
where the time goes in v2:
time: 170 us; the launch traced here: 169 us
  waiting for transfers between devices  68.5 us (40%)
  starting transfers between devices  41.6 us (24%)
  Pallas kernels  29.1 us (17%)
  local copies, waits for them, and re-layouts  20.2 us (12%)
  other arithmetic  4.55 us (3%)
  between operations  3.49 us (2%)
    ppermute x44, waiting for transfers between devices, swap(): return lax.ppermute(value, axis, [(i, i ^ mask) for i in range(size)])  68.5 us
    ppermute x44, starting transfers between devices, swap(): return lax.ppermute(value, axis, [(i, i ^ mask) for i in range(size)])  41.6 us
    unnamed x60, local copies, waits for them, and re-layouts  14 us
    pallas_call x5, Pallas kernels, call_in_vmem(): pl.pallas_call(body, grid_spec=pltpu.PrefetchScalarGridSpec(num_scalar_pr...  12.2 us
    pallas_call x2, Pallas kernels, back_project(): pl.pallas_call(functools.partial(update_body, count), grid=(width // tile...  8.21 us
    pallas_call x2, Pallas kernels, adam(): pl.pallas_call(functools.partial(adam_body, len(written)), grid=(width //...  7.35 us
  transfers between devices with their start and end apart: 44, of which 17 were waited for; matrix products, arithmetic and copies ran while one was open for 7% of the time, Pallas kernels for 15%

profile of v2, /device:TPU:0, one launch (start us, length us, event | category | flops | bytes accessed | tf_op | source)
XLA Modules:
  0.0 169.0 jit_solution(14511974293086282430)
XLA Ops:
  0.6 1.0 slice_bitcast_fusion.3
  1.6 3.1 %collective-permute-start = (bf16[64,1024]{1,0:T(8,128)(2,1)S(1)}, bf16[64,1024]{1,0:T(8,128)(2,1)S(1)}, u32[]{:S(2)}, u32[]{:S(2)}) collective-permute-start(bf16[64,1024]{1,0:T(8,128)(2,1)S(1)} %get-tuple-element.49), channel_id=1, source_target_pairs={{0,8},{8,0},{16,24},{24,16},{1,9},{9,1},{17,25},{25,17},{2,10},{10... | collective-permute-start | bytes 393224 | tf_op jit(solution)/shard_map/ppermute | solution.py:24
  4.7 1.1 slice_bitcast_fusion.refs_0_
  5.9 1.2 slice_bitcast_fusion.1
  7.1 1.6 collective-permute-start.2
  8.6 1.5 collective-permute-start.3
  10.2 1.3 fusion.3
  12.2 0.9 broadcast_select_fusion
  13.1 2.6 %collective-permute-done.2.refs_1_ = bf16[128,1024]{1,0:T(8,128)(2,1)S(1)} collective-permute-done((bf16[128,1024]{1,0:T(8,128)(2,1)S(1)}, bf16[128,1024]{1,0:T(8,128)(2,1)S(1)}, u32[]{:S(2)}, u32[]{:S(2)}) %collective-permute-start.2) | collective-permute-done | bytes 262176 | tf_op jit(solution)/shard_map/ppermute | solution.py:24
  15.7 1.2 collective-permute-done.3.refs_4_
  16.9 2.6 %collective-permute-start.4 = (bf16[64,1024]{1,0:T(8,128)(2,1)S(1)}, bf16[64,1024]{1,0:T(8,128)(2,1)S(1)}, u32[]{:S(2)}, u32[]{:S(2)}) collective-permute-start(bf16[64,1024]{1,0:T(8,128)(2,1)S(1)} %broadcast_select_fusion), channel_id=1, source_target_pairs={{0,16},{8,24},{16,0},{24,8},{1,17},{9,25},{17,1},{25,9},{2,18},{10... | collective-permute-start | bytes 393224 | tf_op jit(solution)/shard_map/ppermute | solution.py:24
  20.1 1.5 collective-permute-start.8
  22.3 2.9 %collective-permute-done.4 = bf16[64,1024]{1,0:T(8,128)(2,1)S(1)} collective-permute-done((bf16[64,1024]{1,0:T(8,128)(2,1)S(1)}, bf16[64,1024]{1,0:T(8,128)(2,1)S(1)}, u32[]{:S(2)}, u32[]{:S(2)}) %collective-permute-start.4) | collective-permute-done | bytes 131104 | tf_op jit(solution)/shard_map/ppermute | solution.py:24
  26.6 1.6 collective-permute-start.12
  28.8 1.5 collective-permute-start.9
  30.8 1.6 collective-permute-start.11
  32.4 7.6 %collective-permute-done.9 = bf16[64,1024]{1,0:T(8,128)(2,1)S(1)} collective-permute-done((bf16[64,1024]{1,0:T(8,128)(2,1)S(1)}, bf16[64,1024]{1,0:T(8,128)(2,1)S(1)}, u32[]{:S(2)}, u32[]{:S(2)}) %collective-permute-start.9) | collective-permute-done | bytes 131104 | tf_op jit(solution)/shard_map/ppermute | solution.py:24
  40.1 2.0 %collective-permute-start.6 = (bf16[64,1024]{1,0:T(8,128)(2,1)S(1)}, bf16[64,1024]{1,0:T(8,128)(2,1)S(1)}, u32[]{:S(2)}, u32[]{:S(2)}) collective-permute-start(bf16[64,1024]{1,0:T(8,128)(2,1)S(1)} %broadcast_select_fusion.2), channel_id=1, source_target_pairs={{0,16},{8,24},{16,0},{24,8},{1,17},{9,25},{17,1},{25,9},{2,18},{10... | collective-permute-start | bytes 393224 | tf_op jit(solution)/shard_map/ppermute | solution.py:24
  42.2 5.2 %collective-permute-done.6 = bf16[64,1024]{1,0:T(8,128)(2,1)S(1)} collective-permute-done((bf16[64,1024]{1,0:T(8,128)(2,1)S(1)}, bf16[64,1024]{1,0:T(8,128)(2,1)S(1)}, u32[]{:S(2)}, u32[]{:S(2)}) %collective-permute-start.6) | collective-permute-done | bytes 131104 | tf_op jit(solution)/shard_map/ppermute | solution.py:24
  47.4 0.8 collective-permute-start.14
  48.2 2.8 %collective-permute-start.16 = (bf16[64,1024]{1,0:T(8,128)(2,1)S(1)}, bf16[64,1024]{1,0:T(8,128)(2,1)S(1)}, u32[]{:S(2)}, u32[]{:S(2)}) collective-permute-start(bf16[64,1024]{1,0:T(8,128)(2,1)S(1)} %broadcast_select_fusion.3), channel_id=1, source_target_pairs={{0,6},{1,7},{2,4},{3,5},{4,2},{5,3},{6,0},{7,1},{8,14},{9,15},{10,... | collective-permute-start | bytes 393224 | tf_op jit(solution)/shard_map/ppermute | solution.py:24
  51.0 1.4 collective-permute-done.14
  52.4 2.1 %collective-permute-done.15 = bf16[64,1024]{1,0:T(8,128)(2,1)S(1)} collective-permute-done((bf16[64,1024]{1,0:T(8,128)(2,1)S(1)}, bf16[64,1024]{1,0:T(8,128)(2,1)S(1)}, u32[]{:S(2)}, u32[]{:S(2)}) %collective-permute-start.15) | collective-permute-done | bytes 131104 | tf_op jit(solution)/shard_map/ppermute | solution.py:24
  55.7 1.2 collective-permute-done.28.refs_6_
  61.2 1.5 fusion.refs_0_
  62.7 1.5 collective-permute-start.18
  64.2 1.5 collective-permute-start.19
  66.3 1.0 copy-done.2
  67.3 1.0 copy-done.4
  68.4 0.9 copy-done.6
  69.3 0.9 copy-done.8
  70.3 0.9 copy-done.10
  71.2 0.9 copy-done.12
  72.2 0.9 copy-done.14
  73.1 0.9 copy-done.16
  74.1 0.9 copy-done.18
  75.0 0.9 copy-done.20
  76.0 4.0 %shard_map.89.refs_5_ = f32[1024,1024]{1,0:T(8,128)S(1)} custom-call(s32[2]{0:T(128)S(1)} %pad_add_fusion.here, bf16[256,1024]{1,0:T(8,128)(2,1)S(1)} %copy-done.2, bf16[128,1024]{1,0:T(8,128)(2,1)S(1)} %copy-done.6, bf16[128,1024]{1,0:T(8,128)(2,1)S(1)} %copy-done.10, bf16[128,1024]{1,0:T(8,128)(2,1)S(1)} %copy-done.12, bf16[128,1024]{1,0:T(8,128)(2,1)S(1)} %copy-done.8, ...), custom_call_target="tpu_custom_call" | custom-call | flops 3221225472 | bytes 11534336 | tf_op jit(solution)/shard_map/pallas_call | solution.py:126
  81.7 3.4 %shard_map.90 = (bf16[1024,1024]{1,0:T(8,128)(2,1)S(1)}, bf16[128,1024]{1,0:T(8,128)(2,1)S(1)}, bf16[128,1024]{1,0:T(8,128)(2,1)S(1)}) custom-call(s32[2]{0:T(128)S(1)} %pad_add_fusion.here, bf16[128,1024]{1,0:T(8,128)(2,1)S(1)} %collective-permute-done.12.refs_0_, bf16[128,1024]{1,0:T(8,128)(2,1)} %collective-permute-done.13.refs_1_, ...), custom_call_target="tpu_custom_call" | custom-call | flops 1610612736 | bytes 13107200 | tf_op jit(solution)/shard_map/pallas_call | solution.py:126
  85.8 1.3 shard_map.91
  87.1 1.5 collective-permute-start.35
  88.6 1.8 %shard_map.87 = (bf16[128,1024]{1,0:T(8,128)(2,1)S(1)}, bf16[128,1024]{1,0:T(8,128)(2,1)S(1)}) custom-call(s32[2]{0:T(128)S(1)} %pad_add_fusion.here, bf16[256,512]{1,0:T(8,128)(2,1)S(1)} %fusion.refs_0_, bf16[256,512]{1,0:T(8,128)(2,1)S(1)} %collective-permute-done.18.refs_1_, bf16[256,512]{1,0:T(8,128)(2,1)S(1)} %collective-permute-done.19.refs_2_, ...), custom_call_target="tpu_custom_call" | custom-call | flops 1073741824 | bytes 6815744 | tf_op jit(solution)/shard_map/pallas_call | solution.py:126
  91.1 3.3 %collective-permute-done.36 = bf16[128,1024]{1,0:T(8,128)(2,1)S(1)} collective-permute-done((bf16[128,1024]{1,0:T(8,128)(2,1)S(1)}, bf16[128,1024]{1,0:T(8,128)(2,1)S(1)}, u32[]{:S(2)}, u32[]{:S(2)}) %collective-permute-start.36) | collective-permute-done | bytes 262176 | tf_op jit(solution)/shard_map/ppermute | solution.py:24
  95.1 1.6 collective-permute-start.25
  96.7 1.8 %shard_map.86 = (f32[128,1024]{1,0:T(8,128)S(1)}, f32[128,1024]{1,0:T(8,128)S(1)}) custom-call(s32[2]{0:T(128)S(1)} %pad_add_fusion.here, bf16[256,512]{1,0:T(8,128)(2,1)S(1)} %fusion.refs_0_, bf16[256,512]{1,0:T(8,128)(2,1)S(1)} %collective-permute-done.18.refs_1_, bf16[256,512]{1,0:T(8,128)(2,1)S(1)} %collective-permute-done.19.refs_2_, ...), custom_call_target="tpu_custom_call" | custom-call | flops 1073741824 | bytes 7340032 | tf_op jit(solution)/shard_map/pallas_call | solution.py:126
  98.5 12.7 %collective-permute-done.26 = bf16[128,1024]{1,0:T(8,128)(2,1)S(1)} collective-permute-done((bf16[128,1024]{1,0:T(8,128)(2,1)S(1)}, bf16[128,1024]{1,0:T(8,128)(2,1)S(1)}, u32[]{:S(2)}, u32[]{:S(2)}) %collective-permute-start.26) | collective-permute-done | bytes 262176 | tf_op jit(solution)/shard_map/ppermute | solution.py:24
  111.2 0.8 add_convert_fusion.1
  112.0 0.9 convert_add_fusion.keep
  113.6 3.7 %shard_map.92 = (f32[2,128,1024]{2,1,0:T(8,128)}, f32[2,128,1024]{2,1,0:T(8,128)}, bf16[128,1024]{1,0:T(8,128)(2,1)}) custom-call(f32[128,1024]{1,0:T(8,128)} %convert_add_fusion.keep, bf16[128,1024]{1,0:T(8,128)(2,1)} %copy-done.26, f32[2,128,1024]{2,1,0:T(8,128)} %moment_first.3, f32[2,128,1024]{2,1,0:T(8,128)} %moment_second.3), custom_call_target="tpu_custom_call" | custom-call | flops 1572864 | bytes 3145728 | tf_op jit(solution)/shard_map/pallas_call | solution.py:197
  117.3 3.0 %collective-permute-start.41 = (bf16[128,1024]{1,0:T(8,128)(2,1)}, bf16[128,1024]{1,0:T(8,128)(2,1)S(1)}, u32[]{:S(2)}, u32[]{:S(2)}) collective-permute-start(bf16[128,1024]{1,0:T(8,128)(2,1)} %get-tuple-element.44.refs_3_), channel_id=1, source_target_pairs={{0,16},{8,24},{16,0},{24,8},{1,17},{9,25},{17,1},{25,9},{2,18},{10... | collective-permute-start | bytes 786440 | tf_op jit(solution)/shard_map/ppermute | solution.py:24
  120.2 1.8 %convert_add_fusion.1.keep = f32[128,1024]{1,0:T(8,128)} fusion(f32[128,1024]{1,0:T(8,128)S(1)} %get-tuple-element.31, bf16[128,1024]{1,0:T(8,128)(2,1)} %collective-permute-done.25), kind=kLoop, calls=%fused_computation.6 | loop fusion | flops 262144 | bytes 1310720 | tf_op jit(solution)/shard_map/add | solution.py:387
  122.0 10.9 %collective-permute-done.27.received = bf16[128,1024]{1,0:T(8,128)(2,1)} collective-permute-done((bf16[128,1024]{1,0:T(8,128)(2,1)}, bf16[128,1024]{1,0:T(8,128)(2,1)}, u32[]{:S(2)}, u32[]{:S(2)}) %collective-permute-start.27) | collective-permute-done | bytes 262176 | tf_op jit(solution)/shard_map/ppermute | solution.py:24
  133.0 3.7 %shard_map.93 = (f32[2,128,1024]{2,1,0:T(8,128)}, f32[2,128,1024]{2,1,0:T(8,128)}, bf16[128,1024]{1,0:T(8,128)(2,1)}) custom-call(f32[128,1024]{1,0:T(8,128)} %convert_add_fusion.1.keep, bf16[128,1024]{1,0:T(8,128)(2,1)} %collective-permute-done.27.received, f32[2,128,1024]{2,1,0:T(8,128)} %moment_first.3, ...), custom_call_target="tpu_custom_call", output_to_operand_aliasing={{0}: (4, {}), {1}: (5, {})} | custom-call | flops 1572864 | bytes 3145728 | tf_op jit(solution)/shard_map/pallas_call | solution.py:197
  136.6 2.6 %collective-permute-start.43 = (bf16[128,1024]{1,0:T(8,128)(2,1)S(1)}, bf16[128,1024]{1,0:T(8,128)(2,1)S(1)}, u32[]{:S(2)}, u32[]{:S(2)}) collective-permute-start(bf16[128,1024]{1,0:T(8,128)(2,1)S(1)} %copy-done.21), channel_id=1, source_target_pairs={{0,8},{8,0},{16,24},{24,16},{1,9},{9,1},{17,25},{25,17},{2,10},{10... | collective-permute-start | bytes 786440 | tf_op jit(solution)/shard_map/ppermute | solution.py:24
  139.2 1.3 collective-permute-done.41.refs_2_
  140.5 2.0 %collective-permute-start.40 = (bf16[128,1024]{1,0:T(8,128)(2,1)}, bf16[128,1024]{1,0:T(8,128)(2,1)}, u32[]{:S(2)}, u32[]{:S(2)}) collective-permute-start(bf16[128,1024]{1,0:T(8,128)(2,1)} %get-tuple-element.43.refs_3_), channel_id=1, source_target_pairs={{0,8},{8,0},{16,24},{24,16},{1,9},{9,1},{17,25},{25,17},{2,10},{10... | collective-permute-start | bytes 786440 | tf_op jit(solution)/shard_map/ppermute | solution.py:24
  142.6 5.4 %collective-permute-done.38.refs_2_ = bf16[128,1024]{1,0:T(8,128)(2,1)S(1)} collective-permute-done((bf16[128,1024]{1,0:T(8,128)(2,1)}, bf16[128,1024]{1,0:T(8,128)(2,1)S(1)}, u32[]{:S(2)}, u32[]{:S(2)}) %collective-permute-start.38) | collective-permute-done | bytes 262176 | tf_op jit(solution)/shard_map/ppermute | solution.py:24
  147.9 0.8 constant_dynamic-slice_fusion.projector
  149.5 1.4 collective-permute-done.43.refs_1_
  150.9 5.6 %collective-permute-done.42.refs_0_ = bf16[128,1024]{1,0:T(8,128)(2,1)S(1)} collective-permute-done((bf16[128,1024]{1,0:T(8,128)(2,1)S(1)}, bf16[128,1024]{1,0:T(8,128)(2,1)S(1)}, u32[]{:S(2)}, u32[]{:S(2)}) %collective-permute-start.42) | collective-permute-done | bytes 262176 | tf_op jit(solution)/shard_map/ppermute | solution.py:24
  157.2 4.1 %shard_map.94.refs_4_ = bf16[2,256,1024]{2,1,0:T(8,128)(2,1)} custom-call(bf16[512,256]{1,0:T(8,128)(2,1)} %constant_dynamic-slice_fusion.projector, bf16[128,1024]{1,0:T(8,128)(2,1)} %copy-done.24, bf16[128,1024]{1,0:T(8,128)(2,1)} %copy-done.23, bf16[128,1024]{1,0:T(8,128)(2,1)} %copy-done.22, bf16[128,1024]{1,0:T(8,128)(2,1)} %get-tuple-element.44.refs_3_), custom_call_target="tpu_custom_call" | custom-call | flops 268435456 | bytes 1572864 | tf_op jit(solution)/shard_map/pallas_call | solution.py:237
  161.3 0.8 collective-permute-done.40.refs_1_
  162.1 2.8 %collective-permute-done.39.refs_0_ = bf16[128,1024]{1,0:T(8,128)(2,1)} collective-permute-done((bf16[128,1024]{1,0:T(8,128)(2,1)S(1)}, bf16[128,1024]{1,0:T(8,128)(2,1)}, u32[]{:S(2)}, u32[]{:S(2)}) %collective-permute-start.39) | collective-permute-done | bytes 262176 | tf_op jit(solution)/shard_map/ppermute | solution.py:24
  164.9 4.1 %shard_map.95 = bf16[2,256,1024]{2,1,0:T(8,128)(2,1)} custom-call(bf16[512,256]{1,0:T(8,128)(2,1)} %constant_dynamic-slice_fusion.1.projector, bf16[128,1024]{1,0:T(8,128)(2,1)} %collective-permute-done.39.refs_0_, bf16[128,1024]{1,0:T(8,128)(2,1)} %collective-permute-done.40.refs_1_, bf16[128,1024]{1,0:T(8,128)(2,1)} %copy-done.25, ...), custom_call_target="tpu_custom_call", output_to_operand_aliasing={{}: (5, {})} | custom-call | flops 268435456 | bytes 1572864 | tf_op jit(solution)/shard_map/pallas_call | solution.py:237
  (113 shorter events, 14.1 us)
Async XLA Ops:
  1.6 10.5 %collective-permute-start = (bf16[64,1024]{1,0:T(8,128)(2,1)S(1)}, bf16[64,1024]{1,0:T(8,128)(2,1)S(1)}, u32[]{:S(2)}, u32[]{:S(2)}) collective-permute-start(bf16[64,1024]{1,0:T(8,128)(2,1)S(1)} %get-tuple-element.49), channel_id=1, source_target_pairs={{0,8},{8,0},{16,24},{24,16},{1,9},{9,1},{17,25},{25,17},{2,10},{10... | collective-permute-start | bytes 393224 | tf_op jit(solution)/shard_map/ppermute | solution.py:24
  5.8 42.4 %copy-start.1 = (bf16[256,1024]{1,0:T(8,128)(2,1)}, bf16[256,1024]{1,0:T(8,128)(2,1)S(1)}, u32[]{:S(2)}) copy-start(bf16[256,1024]{1,0:T(8,128)(2,1)S(1)} %slice_bitcast_fusion.refs_0_) | copy-start | bytes 1572868
  5.8 11.1 %collective-permute-start.1 = (bf16[256,1024]{1,0:T(8,128)(2,1)S(1)}, bf16[256,1024]{1,0:T(8,128)(2,1)S(1)}, u32[]{:S(2)}, u32[]{:S(2)}) collective-permute-start(bf16[256,1024]{1,0:T(8,128)(2,1)S(1)} %slice_bitcast_fusion.refs_0_), channel_id=1, source_target_pairs={{0,1},{1,0},{2,3},{3,2},{4,5},{5,4},{6,7},{7,6},{8,9},{9,8},{10,11... | collective-permute-start | bytes 1572872 | tf_op jit(solution)/shard_map/ppermute | solution.py:24
  7.1 8.7 %collective-permute-start.2 = (bf16[128,1024]{1,0:T(8,128)(2,1)S(1)}, bf16[128,1024]{1,0:T(8,128)(2,1)S(1)}, u32[]{:S(2)}, u32[]{:S(2)}) collective-permute-start(bf16[128,1024]{1,0:T(8,128)(2,1)S(1)} %get-tuple-element.28), channel_id=1, source_target_pairs={{0,2},{1,3},{2,0},{3,1},{4,6},{5,7},{6,4},{7,5},{8,10},{9,11},{10,... | collective-permute-start | bytes 786440 | tf_op jit(solution)/shard_map/ppermute | solution.py:24
  8.6 8.3 %collective-permute-start.3 = (bf16[128,1024]{1,0:T(8,128)(2,1)S(1)}, bf16[128,1024]{1,0:T(8,128)(2,1)S(1)}, u32[]{:S(2)}, u32[]{:S(2)}) collective-permute-start(bf16[128,1024]{1,0:T(8,128)(2,1)S(1)} %get-tuple-element.27), channel_id=1, source_target_pairs={{0,4},{1,5},{2,6},{3,7},{4,0},{5,1},{6,2},{7,3},{8,12},{9,13},{10,... | collective-permute-start | bytes 786440 | tf_op jit(solution)/shard_map/ppermute | solution.py:24
  15.7 42.6 %copy-start.5 = (bf16[128,1024]{1,0:T(8,128)(2,1)}, bf16[128,1024]{1,0:T(8,128)(2,1)S(1)}, u32[]{:S(2)}) copy-start(bf16[128,1024]{1,0:T(8,128)(2,1)S(1)} %collective-permute-done.2.refs_1_) | copy-start | bytes 786436
  16.9 41.4 %copy-start.7 = (bf16[128,1024]{1,0:T(8,128)(2,1)}, bf16[128,1024]{1,0:T(8,128)(2,1)S(1)}, u32[]{:S(2)}) copy-start(bf16[128,1024]{1,0:T(8,128)(2,1)S(1)} %collective-permute-done.3.refs_4_) | copy-start | bytes 786436
  16.9 37.6 %copy-start.3 = (bf16[256,1024]{1,0:T(8,128)(2,1)}, bf16[256,1024]{1,0:T(8,128)(2,1)S(1)}, u32[]{:S(2)}) copy-start(bf16[256,1024]{1,0:T(8,128)(2,1)S(1)} %collective-permute-done.1.refs_5_) | copy-start | bytes 1572868
  16.9 8.3 %collective-permute-start.4 = (bf16[64,1024]{1,0:T(8,128)(2,1)S(1)}, bf16[64,1024]{1,0:T(8,128)(2,1)S(1)}, u32[]{:S(2)}, u32[]{:S(2)}) collective-permute-start(bf16[64,1024]{1,0:T(8,128)(2,1)S(1)} %broadcast_select_fusion), channel_id=1, source_target_pairs={{0,16},{8,24},{16,0},{24,8},{1,17},{9,25},{17,1},{25,9},{2,18},{10... | collective-permute-start | bytes 393224 | tf_op jit(solution)/shard_map/ppermute | solution.py:24
  19.6 9.2 %collective-permute-start.7 = (bf16[128,1024]{1,0:T(8,128)(2,1)S(1)}, bf16[128,1024]{1,0:T(8,128)(2,1)S(1)}, u32[]{:S(2)}, u32[]{:S(2)}) collective-permute-start(bf16[128,1024]{1,0:T(8,128)(2,1)S(1)} %get-tuple-element.27), channel_id=1, source_target_pairs={{0,2},{1,3},{2,0},{3,1},{4,6},{5,7},{6,4},{7,5},{8,10},{9,11},{10,... | collective-permute-start | bytes 786440 | tf_op jit(solution)/shard_map/ppermute | solution.py:24
  20.1 8.6 %collective-permute-start.8 = (bf16[128,1024]{1,0:T(8,128)(2,1)S(1)}, bf16[128,1024]{1,0:T(8,128)(2,1)S(1)}, u32[]{:S(2)}, u32[]{:S(2)}) collective-permute-start(bf16[128,1024]{1,0:T(8,128)(2,1)S(1)} %get-tuple-element.28), channel_id=1, source_target_pairs={{0,4},{1,5},{2,6},{3,7},{4,0},{5,1},{6,2},{7,3},{8,12},{9,13},{10,... | collective-permute-start | bytes 786440 | tf_op jit(solution)/shard_map/ppermute | solution.py:24
  25.3 5.5 %collective-permute-start.5 = (bf16[64,1024]{1,0:T(8,128)(2,1)S(1)}, bf16[64,1024]{1,0:T(8,128)(2,1)S(1)}, u32[]{:S(2)}, u32[]{:S(2)}) collective-permute-start(bf16[64,1024]{1,0:T(8,128)(2,1)S(1)} %get-tuple-element.26), channel_id=1, source_target_pairs={{0,8},{8,0},{16,24},{24,16},{1,9},{9,1},{17,25},{25,17},{2,10},{10... | collective-permute-start | bytes 393224 | tf_op jit(solution)/shard_map/ppermute | solution.py:24
  26.6 20.8 %collective-permute-start.12 = (bf16[128,1024]{1,0:T(8,128)(2,1)S(1)}, bf16[128,1024]{1,0:T(8,128)(2,1)S(1)}, u32[]{:S(2)}, u32[]{:S(2)}) collective-permute-start(bf16[128,1024]{1,0:T(8,128)(2,1)S(1)} %collective-permute-done.2.refs_1_), channel_id=1, source_target_pairs={{0,4},{1,5},{2,6},{3,7},{4,0},{5,1},{6,2},{7,3},{8,12},{9,13},{10,... | collective-permute-start | bytes 786440 | tf_op jit(solution)/shard_map/ppermute | solution.py:24
  28.1 19.2 %collective-permute-start.13 = (bf16[128,1024]{1,0:T(8,128)(2,1)S(1)}, bf16[128,1024]{1,0:T(8,128)(2,1)}, u32[]{:S(2)}, u32[]{:S(2)}) collective-permute-start(bf16[128,1024]{1,0:T(8,128)(2,1)S(1)} %collective-permute-done.3.refs_4_), channel_id=1, source_target_pairs={{0,2},{1,3},{2,0},{3,1},{4,6},{5,7},{6,4},{7,5},{8,10},{9,11},{10,... | collective-permute-start | bytes 786440 | tf_op jit(solution)/shard_map/ppermute | solution.py:24
  28.8 31.8 %copy-start.9 = (bf16[128,1024]{1,0:T(8,128)(2,1)}, bf16[128,1024]{1,0:T(8,128)(2,1)S(1)}, u32[]{:S(2)}) copy-start(bf16[128,1024]{1,0:T(8,128)(2,1)S(1)} %collective-permute-done.7.refs_2_) | copy-start | bytes 786436
  28.8 31.8 %copy-start.11 = (bf16[128,1024]{1,0:T(8,128)(2,1)}, bf16[128,1024]{1,0:T(8,128)(2,1)S(1)}, u32[]{:S(2)}) copy-start(bf16[128,1024]{1,0:T(8,128)(2,1)S(1)} %collective-permute-done.8.refs_3_) | copy-start | bytes 786436
  28.8 11.3 %collective-permute-start.9 = (bf16[64,1024]{1,0:T(8,128)(2,1)S(1)}, bf16[64,1024]{1,0:T(8,128)(2,1)S(1)}, u32[]{:S(2)}, u32[]{:S(2)}) collective-permute-start(bf16[64,1024]{1,0:T(8,128)(2,1)S(1)} %broadcast_select_fusion.1), channel_id=1, source_target_pairs={{0,2},{1,3},{2,0},{3,1},{4,6},{5,7},{6,4},{7,5},{8,10},{9,11},{10,... | collective-permute-start | bytes 393224 | tf_op jit(solution)/shard_map/ppermute | solution.py:24
  30.3 11.8 %collective-permute-start.10 = (bf16[64,1024]{1,0:T(8,128)(2,1)S(1)}, bf16[64,1024]{1,0:T(8,128)(2,1)S(1)}, u32[]{:S(2)}, u32[]{:S(2)}) collective-permute-start(bf16[64,1024]{1,0:T(8,128)(2,1)S(1)} %broadcast_select_fusion.1), channel_id=1, source_target_pairs={{0,4},{1,5},{2,6},{3,7},{4,0},{5,1},{6,2},{7,3},{8,12},{9,13},{10,... | collective-permute-start | bytes 393224 | tf_op jit(solution)/shard_map/ppermute | solution.py:24
  30.8 11.3 %collective-permute-start.11 = (bf16[64,1024]{1,0:T(8,128)(2,1)S(1)}, bf16[64,1024]{1,0:T(8,128)(2,1)S(1)}, u32[]{:S(2)}, u32[]{:S(2)}) collective-permute-start(bf16[64,1024]{1,0:T(8,128)(2,1)S(1)} %broadcast_select_fusion.1), channel_id=1, source_target_pairs={{0,6},{1,7},{2,4},{3,5},{4,2},{5,3},{6,0},{7,1},{8,14},{9,15},{10,... | collective-permute-start | bytes 393224 | tf_op jit(solution)/shard_map/ppermute | solution.py:24
  40.1 7.3 %collective-permute-start.6 = (bf16[64,1024]{1,0:T(8,128)(2,1)S(1)}, bf16[64,1024]{1,0:T(8,128)(2,1)S(1)}, u32[]{:S(2)}, u32[]{:S(2)}) collective-permute-start(bf16[64,1024]{1,0:T(8,128)(2,1)S(1)} %broadcast_select_fusion.2), channel_id=1, source_target_pairs={{0,16},{8,24},{16,0},{24,8},{1,17},{9,25},{17,1},{25,9},{2,18},{10... | collective-permute-start | bytes 393224 | tf_op jit(solution)/shard_map/ppermute | solution.py:24
  47.4 5.0 %collective-permute-start.14 = (bf16[64,1024]{1,0:T(8,128)(2,1)S(1)}, bf16[64,1024]{1,0:T(8,128)(2,1)S(1)}, u32[]{:S(2)}, u32[]{:S(2)}) collective-permute-start(bf16[64,1024]{1,0:T(8,128)(2,1)S(1)} %broadcast_select_fusion.3), channel_id=1, source_target_pairs={{0,2},{1,3},{2,0},{3,1},{4,6},{5,7},{6,4},{7,5},{8,10},{9,11},{10,... | collective-permute-start | bytes 393224 | tf_op jit(solution)/shard_map/ppermute | solution.py:24
  48.2 6.4 %collective-permute-start.15 = (bf16[64,1024]{1,0:T(8,128)(2,1)S(1)}, bf16[64,1024]{1,0:T(8,128)(2,1)S(1)}, u32[]{:S(2)}, u32[]{:S(2)}) collective-permute-start(bf16[64,1024]{1,0:T(8,128)(2,1)S(1)} %broadcast_select_fusion.3), channel_id=1, source_target_pairs={{0,4},{1,5},{2,6},{3,7},{4,0},{5,1},{6,2},{7,3},{8,12},{9,13},{10,... | collective-permute-start | bytes 393224 | tf_op jit(solution)/shard_map/ppermute | solution.py:24
  48.2 6.4 %collective-permute-start.16 = (bf16[64,1024]{1,0:T(8,128)(2,1)S(1)}, bf16[64,1024]{1,0:T(8,128)(2,1)S(1)}, u32[]{:S(2)}, u32[]{:S(2)}) collective-permute-start(bf16[64,1024]{1,0:T(8,128)(2,1)S(1)} %broadcast_select_fusion.3), channel_id=1, source_target_pairs={{0,6},{1,7},{2,4},{3,5},{4,2},{5,3},{6,0},{7,1},{8,14},{9,15},{10,... | collective-permute-start | bytes 393224 | tf_op jit(solution)/shard_map/ppermute | solution.py:24
  54.6 5.9 %collective-permute-start.17 = (bf16[256,1024]{1,0:T(8,128)(2,1)S(1)}, bf16[256,1024]{1,0:T(8,128)(2,1)S(1)}, u32[]{:S(2)}, u32[]{:S(2)}) collective-permute-start(bf16[256,1024]{1,0:T(8,128)(2,1)S(1)} %constant_dynamic-update-slice_fusion.4.same), channel_id=1, source_target_pairs={{0,1},{1,0},{2,3},{3,2},{4,5},{5,4},{6,7},{7,6},{8,9},{9,8},{10,11... | collective-permute-start | bytes 1572872 | tf_op jit(solution)/shard_map/ppermute | solution.py:24
  54.7 2.3 %collective-permute-start.28 = (bf16[128,1024]{1,0:T(8,128)(2,1)S(1)}, bf16[128,1024]{1,0:T(8,128)(2,1)S(1)}, u32[]{:S(2)}, u32[]{:S(2)}) collective-permute-start(bf16[128,1024]{1,0:T(8,128)(2,1)S(1)} %collective-permute-done.2.refs_1_), channel_id=1, source_target_pairs={{0,1},{1,0},{2,3},{3,2},{4,5},{5,4},{6,7},{7,6},{8,9},{9,8},{10,11... | collective-permute-start | bytes 786440 | tf_op jit(solution)/shard_map/ppermute | solution.py:24
  55.2 2.5 %collective-permute-start.31 = (bf16[128,1024]{1,0:T(8,128)(2,1)S(1)}, bf16[128,1024]{1,0:T(8,128)(2,1)S(1)}, u32[]{:S(2)}, u32[]{:S(2)}) collective-permute-start(bf16[128,1024]{1,0:T(8,128)(2,1)S(1)} %collective-permute-done.3.refs_4_), channel_id=1, source_target_pairs={{0,1},{1,0},{2,3},{3,2},{4,5},{5,4},{6,7},{7,6},{8,9},{9,8},{10,11... | collective-permute-start | bytes 786440 | tf_op jit(solution)/shard_map/ppermute | solution.py:24
  55.2 3.1 %collective-permute-start.29 = (bf16[128,1024]{1,0:T(8,128)(2,1)S(1)}, bf16[128,1024]{1,0:T(8,128)(2,1)S(1)}, u32[]{:S(2)}, u32[]{:S(2)}) collective-permute-start(bf16[128,1024]{1,0:T(8,128)(2,1)S(1)} %collective-permute-done.7.refs_2_), channel_id=1, source_target_pairs={{0,1},{1,0},{2,3},{3,2},{4,5},{5,4},{6,7},{7,6},{8,9},{9,8},{10,11... | collective-permute-start | bytes 786440 | tf_op jit(solution)/shard_map/ppermute | solution.py:24
  55.7 3.4 %collective-permute-start.30 = (bf16[128,1024]{1,0:T(8,128)(2,1)S(1)}, bf16[128,1024]{1,0:T(8,128)(2,1)S(1)}, u32[]{:S(2)}, u32[]{:S(2)}) collective-permute-start(bf16[128,1024]{1,0:T(8,128)(2,1)S(1)} %collective-permute-done.8.refs_3_), channel_id=1, source_target_pairs={{0,1},{1,0},{2,3},{3,2},{4,5},{5,4},{6,7},{7,6},{8,9},{9,8},{10,11... | collective-permute-start | bytes 786440 | tf_op jit(solution)/shard_map/ppermute | solution.py:24
  59.8 5.9 %collective-permute-start.32 = (bf16[256,1024]{1,0:T(8,128)(2,1)S(1)}, bf16[256,1024]{1,0:T(8,128)(2,1)S(1)}, u32[]{:S(2)}, u32[]{:S(2)}) collective-permute-start(bf16[256,1024]{1,0:T(8,128)(2,1)S(1)} %constant_dynamic-update-slice_fusion.same), channel_id=1, source_target_pairs={{0,1},{1,0},{2,3},{3,2},{4,5},{5,4},{6,7},{7,6},{8,9},{9,8},{10,11... | collective-permute-start | bytes 1572872 | tf_op jit(solution)/shard_map/ppermute | solution.py:24
  59.9 6.4 %copy-start = (bf16[2048,1024]{1,0:T(8,128)(2,1)S(1)}, bf16[2048,1024]{1,0:T(8,128)(2,1)}, u32[]{:S(2)}) copy-start(bf16[2048,1024]{1,0:T(8,128)(2,1)} %refs_4_.1) | copy-start | bytes 12582916
  60.0 20.6 %collective-permute-start.33 = (bf16[128,1024]{1,0:T(8,128)(2,1)S(1)}, bf16[128,1024]{1,0:T(8,128)(2,1)S(1)}, u32[]{:S(2)}, u32[]{:S(2)}) collective-permute-start(bf16[128,1024]{1,0:T(8,128)(2,1)S(1)} %collective-permute-done.12.refs_0_), channel_id=1, source_target_pairs={{0,1},{1,0},{2,3},{3,2},{4,5},{5,4},{6,7},{7,6},{8,9},{9,8},{10,11... | collective-permute-start | bytes 786440 | tf_op jit(solution)/shard_map/ppermute | solution.py:24
  60.4 21.4 %collective-permute-start.34 = (bf16[128,1024]{1,0:T(8,128)(2,1)}, bf16[128,1024]{1,0:T(8,128)(2,1)S(1)}, u32[]{:S(2)}, u32[]{:S(2)}) collective-permute-start(bf16[128,1024]{1,0:T(8,128)(2,1)} %collective-permute-done.13.refs_1_), channel_id=1, source_target_pairs={{0,1},{1,0},{2,3},{3,2},{4,5},{5,4},{6,7},{7,6},{8,9},{9,8},{10,11... | collective-permute-start | bytes 786440 | tf_op jit(solution)/shard_map/ppermute | solution.py:24
  62.7 18.0 %collective-permute-start.18 = (bf16[256,512]{1,0:T(8,128)(2,1)S(1)}, bf16[256,512]{1,0:T(8,128)(2,1)S(1)}, u32[]{:S(2)}, u32[]{:S(2)}) collective-permute-start(bf16[256,512]{1,0:T(8,128)(2,1)S(1)} %fusion.refs_0_), channel_id=1, source_target_pairs={{0,2},{1,3},{2,0},{3,1},{4,6},{5,7},{6,4},{7,5},{8,10},{9,11},{10,... | collective-permute-start | bytes 786440 | tf_op jit(solution)/shard_map/ppermute | solution.py:24
  64.2 17.0 %collective-permute-start.19 = (bf16[256,512]{1,0:T(8,128)(2,1)S(1)}, bf16[256,512]{1,0:T(8,128)(2,1)S(1)}, u32[]{:S(2)}, u32[]{:S(2)}) collective-permute-start(bf16[256,512]{1,0:T(8,128)(2,1)S(1)} %fusion.refs_0_), channel_id=1, source_target_pairs={{0,4},{1,5},{2,6},{3,7},{4,0},{5,1},{6,2},{7,3},{8,12},{9,13},{10,... | collective-permute-start | bytes 786440 | tf_op jit(solution)/shard_map/ppermute | solution.py:24
  65.7 15.6 %collective-permute-start.20 = (bf16[256,512]{1,0:T(8,128)(2,1)S(1)}, bf16[256,512]{1,0:T(8,128)(2,1)S(1)}, u32[]{:S(2)}, u32[]{:S(2)}) collective-permute-start(bf16[256,512]{1,0:T(8,128)(2,1)S(1)} %fusion.refs_0_), channel_id=1, source_target_pairs={{0,6},{1,7},{2,4},{3,5},{4,2},{5,3},{6,0},{7,1},{8,14},{9,15},{10,... | collective-permute-start | bytes 786440 | tf_op jit(solution)/shard_map/ppermute | solution.py:24
  66.3 1.0 copy-start.2
  67.3 1.0 copy-start.4
  68.4 0.9 copy-start.6
  69.3 0.9 copy-start.8
  70.3 0.9 copy-start.10
  71.2 0.9 copy-start.12
  72.2 0.9 copy-start.14
  73.1 0.9 copy-start.16
  74.1 0.9 copy-start.18
  80.6 6.4 %collective-permute-start.21 = (bf16[256,512]{1,0:T(8,128)(2,1)S(1)}, bf16[256,512]{1,0:T(8,128)(2,1)S(1)}, u32[]{:S(2)}, u32[]{:S(2)}) collective-permute-start(bf16[256,512]{1,0:T(8,128)(2,1)S(1)} %fusion.refs_0_), channel_id=1, source_target_pairs={{0,1},{1,0},{2,3},{3,2},{4,5},{5,4},{6,7},{7,6},{8,9},{9,8},{10,11... | collective-permute-start | bytes 786440 | tf_op jit(solution)/shard_map/ppermute | solution.py:24
  80.7 7.8 %collective-permute-start.22 = (bf16[256,512]{1,0:T(8,128)(2,1)S(1)}, bf16[256,512]{1,0:T(8,128)(2,1)S(1)}, u32[]{:S(2)}, u32[]{:S(2)}) collective-permute-start(bf16[256,512]{1,0:T(8,128)(2,1)S(1)} %collective-permute-done.18.refs_1_), channel_id=1, source_target_pairs={{0,1},{1,0},{2,3},{3,2},{4,5},{5,4},{6,7},{7,6},{8,9},{9,8},{10,11... | collective-permute-start | bytes 786440 | tf_op jit(solution)/shard_map/ppermute | solution.py:24
  81.2 7.4 %collective-permute-start.23 = (bf16[256,512]{1,0:T(8,128)(2,1)S(1)}, bf16[256,512]{1,0:T(8,128)(2,1)S(1)}, u32[]{:S(2)}, u32[]{:S(2)}) collective-permute-start(bf16[256,512]{1,0:T(8,128)(2,1)S(1)} %collective-permute-done.19.refs_2_), channel_id=1, source_target_pairs={{0,1},{1,0},{2,3},{3,2},{4,5},{5,4},{6,7},{7,6},{8,9},{9,8},{10,11... | collective-permute-start | bytes 786440 | tf_op jit(solution)/shard_map/ppermute | solution.py:24
  81.3 7.3 %collective-permute-start.24 = (bf16[256,512]{1,0:T(8,128)(2,1)S(1)}, bf16[256,512]{1,0:T(8,128)(2,1)S(1)}, u32[]{:S(2)}, u32[]{:S(2)}) collective-permute-start(bf16[256,512]{1,0:T(8,128)(2,1)S(1)} %collective-permute-done.20.refs_3_), channel_id=1, source_target_pairs={{0,1},{1,0},{2,3},{3,2},{4,5},{5,4},{6,7},{7,6},{8,9},{9,8},{10,11... | collective-permute-start | bytes 786440 | tf_op jit(solution)/shard_map/ppermute | solution.py:24
  85.1 9.2 %collective-permute-start.36 = (bf16[128,1024]{1,0:T(8,128)(2,1)S(1)}, bf16[128,1024]{1,0:T(8,128)(2,1)S(1)}, u32[]{:S(2)}, u32[]{:S(2)}) collective-permute-start(bf16[128,1024]{1,0:T(8,128)(2,1)S(1)} %get-tuple-element.40), channel_id=1, source_target_pairs={{0,8},{8,0},{16,24},{24,16},{1,9},{9,1},{17,25},{25,17},{2,10},{10... | collective-permute-start | bytes 786440 | tf_op jit(solution)/shard_map/ppermute | solution.py:24
  87.1 24.9 %collective-permute-start.35 = (bf16[128,1024]{1,0:T(8,128)(2,1)S(1)}, bf16[128,1024]{1,0:T(8,128)(2,1)S(1)}, u32[]{:S(2)}, u32[]{:S(2)}) collective-permute-start(bf16[128,1024]{1,0:T(8,128)(2,1)S(1)} %get-tuple-element.38), channel_id=1, source_target_pairs={{0,8},{8,0},{16,24},{24,16},{1,9},{9,1},{17,25},{25,17},{2,10},{10... | collective-permute-start | bytes 786440 | tf_op jit(solution)/shard_map/ppermute | solution.py:24
  90.4 20.8 %collective-permute-start.26 = (bf16[128,1024]{1,0:T(8,128)(2,1)S(1)}, bf16[128,1024]{1,0:T(8,128)(2,1)S(1)}, u32[]{:S(2)}, u32[]{:S(2)}) collective-permute-start(bf16[128,1024]{1,0:T(8,128)(2,1)S(1)} %get-tuple-element.34), channel_id=1, source_target_pairs={{0,8},{8,0},{16,24},{24,16},{1,9},{9,1},{17,25},{25,17},{2,10},{10... | collective-permute-start | bytes 786440 | tf_op jit(solution)/shard_map/ppermute | solution.py:24
  94.4 18.5 %collective-permute-start.37 = (bf16[128,1024]{1,0:T(8,128)(2,1)S(1)}, bf16[128,1024]{1,0:T(8,128)(2,1)S(1)}, u32[]{:S(2)}, u32[]{:S(2)}) collective-permute-start(bf16[128,1024]{1,0:T(8,128)(2,1)S(1)} %add_convert_fusion), channel_id=1, source_target_pairs={{0,16},{8,24},{16,0},{24,8},{1,17},{9,25},{17,1},{25,9},{2,18},{10... | collective-permute-start | bytes 786440 | tf_op jit(solution)/shard_map/ppermute | solution.py:24
  95.1 25.1 %collective-permute-start.25 = (bf16[128,1024]{1,0:T(8,128)(2,1)S(1)}, bf16[128,1024]{1,0:T(8,128)(2,1)}, u32[]{:S(2)}, u32[]{:S(2)}) collective-permute-start(bf16[128,1024]{1,0:T(8,128)(2,1)S(1)} %get-tuple-element.32), channel_id=1, source_target_pairs={{0,8},{8,0},{16,24},{24,16},{1,9},{9,1},{17,25},{25,17},{2,10},{10... | collective-permute-start | bytes 786440 | tf_op jit(solution)/shard_map/ppermute | solution.py:24
  112.0 21.0 %collective-permute-start.27 = (bf16[128,1024]{1,0:T(8,128)(2,1)}, bf16[128,1024]{1,0:T(8,128)(2,1)}, u32[]{:S(2)}, u32[]{:S(2)}) collective-permute-start(bf16[128,1024]{1,0:T(8,128)(2,1)} %add_convert_fusion.1), channel_id=1, source_target_pairs={{0,16},{8,24},{16,0},{24,8},{1,17},{9,25},{17,1},{25,9},{2,18},{10... | collective-permute-start | bytes 786440 | tf_op jit(solution)/shard_map/ppermute | solution.py:24
  117.3 19.4 %copy-start.21 = (bf16[128,1024]{1,0:T(8,128)(2,1)S(1)}, bf16[128,1024]{1,0:T(8,128)(2,1)}, u32[]{:S(2)}) copy-start(bf16[128,1024]{1,0:T(8,128)(2,1)} %get-tuple-element.44.refs_3_) | copy-start | bytes 786436
  117.3 23.3 %collective-permute-start.41 = (bf16[128,1024]{1,0:T(8,128)(2,1)}, bf16[128,1024]{1,0:T(8,128)(2,1)S(1)}, u32[]{:S(2)}, u32[]{:S(2)}) collective-permute-start(bf16[128,1024]{1,0:T(8,128)(2,1)} %get-tuple-element.44.refs_3_), channel_id=1, source_target_pairs={{0,16},{8,24},{16,0},{24,8},{1,17},{9,25},{17,1},{25,9},{2,18},{10... | collective-permute-start | bytes 786440 | tf_op jit(solution)/shard_map/ppermute | solution.py:24
  136.6 11.3 %collective-permute-start.38 = (bf16[128,1024]{1,0:T(8,128)(2,1)}, bf16[128,1024]{1,0:T(8,128)(2,1)S(1)}, u32[]{:S(2)}, u32[]{:S(2)}) collective-permute-start(bf16[128,1024]{1,0:T(8,128)(2,1)} %get-tuple-element.43.refs_3_), channel_id=1, source_target_pairs={{0,16},{8,24},{16,0},{24,8},{1,17},{9,25},{17,1},{25,9},{2,18},{10... | collective-permute-start | bytes 786440 | tf_op jit(solution)/shard_map/ppermute | solution.py:24
  136.6 14.3 %collective-permute-start.43 = (bf16[128,1024]{1,0:T(8,128)(2,1)S(1)}, bf16[128,1024]{1,0:T(8,128)(2,1)S(1)}, u32[]{:S(2)}, u32[]{:S(2)}) collective-permute-start(bf16[128,1024]{1,0:T(8,128)(2,1)S(1)} %copy-done.21), channel_id=1, source_target_pairs={{0,8},{8,0},{16,24},{24,16},{1,9},{9,1},{17,25},{25,17},{2,10},{10... | collective-permute-start | bytes 786440 | tf_op jit(solution)/shard_map/ppermute | solution.py:24
  140.5 16.0 %copy-start.22 = (bf16[128,1024]{1,0:T(8,128)(2,1)}, bf16[128,1024]{1,0:T(8,128)(2,1)S(1)}, u32[]{:S(2)}) copy-start(bf16[128,1024]{1,0:T(8,128)(2,1)S(1)} %collective-permute-done.41.refs_2_) | copy-start | bytes 786436
  140.5 16.0 %collective-permute-start.42 = (bf16[128,1024]{1,0:T(8,128)(2,1)S(1)}, bf16[128,1024]{1,0:T(8,128)(2,1)S(1)}, u32[]{:S(2)}, u32[]{:S(2)}) collective-permute-start(bf16[128,1024]{1,0:T(8,128)(2,1)S(1)} %collective-permute-done.41.refs_2_), channel_id=1, source_target_pairs={{0,8},{8,0},{16,24},{24,16},{1,9},{9,1},{17,25},{25,17},{2,10},{10... | collective-permute-start | bytes 786440 | tf_op jit(solution)/shard_map/ppermute | solution.py:24
  140.5 21.6 %collective-permute-start.40 = (bf16[128,1024]{1,0:T(8,128)(2,1)}, bf16[128,1024]{1,0:T(8,128)(2,1)}, u32[]{:S(2)}, u32[]{:S(2)}) collective-permute-start(bf16[128,1024]{1,0:T(8,128)(2,1)} %get-tuple-element.43.refs_3_), channel_id=1, source_target_pairs={{0,8},{8,0},{16,24},{24,16},{1,9},{9,1},{17,25},{25,17},{2,10},{10... | collective-permute-start | bytes 786440 | tf_op jit(solution)/shard_map/ppermute | solution.py:24
  147.9 17.0 %copy-start.25 = (bf16[128,1024]{1,0:T(8,128)(2,1)}, bf16[128,1024]{1,0:T(8,128)(2,1)S(1)}, u32[]{:S(2)}) copy-start(bf16[128,1024]{1,0:T(8,128)(2,1)S(1)} %collective-permute-done.38.refs_2_) | copy-start | bytes 786436
  147.9 17.0 %collective-permute-start.39 = (bf16[128,1024]{1,0:T(8,128)(2,1)S(1)}, bf16[128,1024]{1,0:T(8,128)(2,1)}, u32[]{:S(2)}, u32[]{:S(2)}) collective-permute-start(bf16[128,1024]{1,0:T(8,128)(2,1)S(1)} %collective-permute-done.38.refs_2_), channel_id=1, source_target_pairs={{0,8},{8,0},{16,24},{24,16},{1,9},{9,1},{17,25},{25,17},{2,10},{10... | collective-permute-start | bytes 786440 | tf_op jit(solution)/shard_map/ppermute | solution.py:24
  150.9 5.6 %copy-start.23 = (bf16[128,1024]{1,0:T(8,128)(2,1)}, bf16[128,1024]{1,0:T(8,128)(2,1)S(1)}, u32[]{:S(2)}) copy-start(bf16[128,1024]{1,0:T(8,128)(2,1)S(1)} %collective-permute-done.43.refs_1_) | copy-start | bytes 786436
  (7 other events, 5.2 us)

commit v3 on v2

v3 whole, which is shorter than its diff:
```python
import functools
import math

import jax
import jax.numpy as jnp
from jax import lax
from jax.experimental import pallas as pl
from jax.experimental.pallas import tpu as pltpu
from jax.sharding import PartitionSpec as P

MATS = 2
STEP = 10

beta_first = 0.9
beta_second = 0.999
epsilon = 1e-08

TRANSPOSED = (((0,), (0,)), ((), ()))
MIB = 1 << 20


def swap(value, axis, mask):
    size = lax.axis_size(axis)
    return lax.ppermute(value, axis, [(i, i ^ mask) for i in range(size)])


def bits_of(size):
    return [1 << k for k in range(size.bit_length() - 1)]


def after(value, others, tokens):
    corners = [other[:16, :128] for other in others]
    value, *held = lax.optimization_barrier((value, *corners))
    tokens.extend(held)
    return value


def spread(block, bits):
    if len(bits) == 2:
        low, high = bits
        masks = (0, low, high, low | high)
        return {mask: swap(block, "fsdp", mask) if mask else block for mask in masks}
    blocks = {0: block}
    for bit in bits:
        blocks.update({mask ^ bit: swap(held, "fsdp", bit) for mask, held in list(blocks.items())})
    return blocks


def spread_near(block, bits, tokens):
    if len(bits) == 2:
        low, high = bits
        half = block.shape[0] // 2
        top, bottom = block[:half], block[half:]
        low_top, high_bottom = swap(top, "fsdp", low), swap(bottom, "fsdp", high)
        far = [swap(low_top, "fsdp", high), swap(high_bottom, "fsdp", low)]
        by_low = [low_top, swap(after(bottom, [low_top], tokens), "fsdp", low)]
        by_high = [swap(after(top, [high_bottom], tokens), "fsdp", high), high_bottom]
        first = [low_top, high_bottom]
        return {0: [block], low: by_low, high: by_high}, {low | high: far}, first
    blocks = {mask: [held] for mask, held in spread(block, bits).items()}
    last = max(blocks)
    near = {mask: held for mask, held in blocks.items() if mask != last}
    return near, {last: blocks[last]}, []


def with_partner(blocks, own=None):
    other = {
        mask ^ 1: [own] if mask == 0 and own is not None else [swap(x, "fsdp", 1) for x in held]
        for mask, held in blocks.items()
    }
    return {**blocks, **other}


def tile_of(size):
    return min(size, 256)


def whole(shape):
    return pl.BlockSpec(shape, lambda *_: (0,) * len(shape))


def gather_body(order, per, count, here, same, other, *refs):
    outs = refs[-MATS:]
    for matrix, out in enumerate(outs):
        spot = 0
        for mask in order:
            for sub in range(per):
                away = ((here[0] ^ mask) * per + sub) ^ here[1]
                at = pl.multiple_of(((away >> 1) * MATS + matrix) * count, count)
                out[pl.ds(spot * count, count), :] = jnp.where(
                    (away & 1) == 0, same[pl.ds(at, count), :], other[pl.ds(at, count), :]
                )
                spot += 1


def gather_projector(same, other, here, order, per, tokens):
    rows, kv = same.shape
    rank = 2 * rows // MATS
    return pl.pallas_call(
        functools.partial(gather_body, order, per, rank // (len(order) * per)),
        grid_spec=pltpu.PrefetchScalarGridSpec(
            num_scalar_prefetch=1,
            grid=(1,),
            in_specs=[whole((rows, kv))] * 2
            + [pl.BlockSpec(memory_space=pl.ANY)] * len(tokens),
            out_specs=[whole((rank, kv))] * MATS,
        ),
        out_shape=[jax.ShapeDtypeStruct((rank, kv), same.dtype)] * MATS,
        compiler_params=pltpu.CompilerParams(vmem_limit_bytes=16 * MIB),
        cost_estimate=pl.CostEstimate(flops=0, bytes_accessed=8 * rows * kv, transcendentals=0),
    )(here, same, other, *tokens)


def block_term(block, rows, here, mask, tile):
    pieces = [piece[:, tile] for piece in block]
    left = pieces[0] if len(pieces) == 1 else jnp.concatenate(pieces, axis=0)
    count = left.shape[0]
    start = pl.multiple_of((here[1] ^ mask) * count, count)
    return lax.dot_general(
        left, rows[pl.ds(start, count), :], TRANSPOSED, preferred_element_type=jnp.float32
    )


def regroup(refs, shape):
    refs = list(refs)
    return [[refs.pop(0) for _ in range(length)] for length in shape]


def call_in_vmem(body, here, operands, outputs, flops, tokens=()):
    moved = sum(x.size * x.dtype.itemsize for x in list(operands) + list(outputs))
    vmem = pl.BlockSpec(memory_space=pltpu.VMEM)
    return pl.pallas_call(
        body,
        grid_spec=pltpu.PrefetchScalarGridSpec(
            num_scalar_prefetch=1,
            grid=(),
            in_specs=[vmem] * len(operands) + [pl.BlockSpec(memory_space=pl.ANY)] * len(tokens),
            out_specs=[vmem] * len(outputs),
        ),
        out_shape=outputs,
        compiler_params=pltpu.CompilerParams(vmem_limit_bytes=20 * MIB),
        cost_estimate=pl.CostEstimate(
            flops=int(flops), bytes_accessed=moved, transcendentals=0
        ),
    )(here, *operands, *tokens)


def flat(blocks):
    return [piece for block in blocks.values() for piece in block]


def depth(blocks):
    return sum(piece.shape[0] for piece in flat(blocks))


def heads_body(masks, shape, part, scale, here, *refs):
    groups = regroup(refs[: sum(shape)], shape)
    rows, outs = refs[sum(shape)], refs[sum(shape) + 1 :]
    size = outs[0].shape[0] * len(outs)
    total = None
    for mask, block in zip(masks, groups):
        term = block_term(block, rows, here, mask, pl.ds(part * size, size))
        total = term if total is None else total + term
    for k, out in enumerate(outs):
        count = out.shape[0]
        out[...] = (total[k * count : (k + 1) * count] * scale).astype(out.dtype)


def heads_product(blocks, here, layer_input, part, pieces, dtype, scale):
    half = flat(blocks)[0].shape[1] // 2
    width = layer_input.shape[1]
    shape = [len(block) for block in blocks.values()]
    return call_in_vmem(
        functools.partial(heads_body, list(blocks), shape, part, scale),
        here,
        flat(blocks) + [layer_input],
        [jax.ShapeDtypeStruct((half // pieces, width), dtype)] * pieces,
        2 * depth(blocks) * half * width,
    )


def product_body(shape, here, *refs):
    groups = regroup(refs[: sum(shape)], shape)
    out = refs[-1]
    total = None
    for block, rows in zip(groups, refs[sum(shape) : -1]):
        pieces = [piece[...] for piece in block]
        left = pieces[0] if len(pieces) == 1 else jnp.concatenate(pieces, axis=0)
        term = lax.dot_general(left, rows[...], TRANSPOSED, preferred_element_type=jnp.float32)
        total = term if total is None else total + term
    out[...] = total


def row_blocks(blocks, width):
    def at(mask, i, here):
        return here[1] ^ mask, 0

    return [
        pl.BlockSpec((depth({mask: block}), width), functools.partial(at, mask))
        for mask, block in blocks.items()
    ]


def add_products(blocks, here, layer_input):
    kv = flat(blocks)[0].shape[1]
    width = layer_input.shape[1]
    tile = tile_of(kv)
    shape = [len(block) for block in blocks.values()]
    return pl.pallas_call(
        functools.partial(product_body, shape),
        grid_spec=pltpu.PrefetchScalarGridSpec(
            num_scalar_prefetch=1,
            grid=(kv // tile,),
            in_specs=[
                pl.BlockSpec((piece.shape[0], tile), lambda i, here: (0, i))
                for piece in flat(blocks)
            ]
            + row_blocks(blocks, width),
            out_specs=pl.BlockSpec((tile, width), lambda i, here: (i, 0)),
        ),
        out_shape=jax.ShapeDtypeStruct((kv, width), jnp.float32),
        compiler_params=pltpu.CompilerParams(vmem_limit_bytes=20 * MIB),
        cost_estimate=pl.CostEstimate(
            flops=2 * depth(blocks) * kv * width,
            bytes_accessed=2 * depth(blocks) * (kv + width) + 4 * kv * width,
            transcendentals=0,
        ),
    )(here, *flat(blocks), *([layer_input] * len(blocks)))


def project_body(masks, shape, scale, here, *refs):
    groups = regroup(refs[: sum(shape)], shape)
    rows, partial, projector, product = refs[sum(shape) : sum(shape) + 4]
    outs = refs[sum(shape) + 4 :]
    size = tile_of(product.shape[0])
    for at in range(0, product.shape[0], size):
        tile = pl.ds(at, size)
        total = partial[tile, :]
        for mask, block in zip(masks, groups):
            total += block_term(block, rows, here, mask, tile)
        product[tile, :] = total.astype(product.dtype)
    apply_body(0, scale, here, projector, product, *outs)


def apply_body(first, scale, here, projector, product, *outs):
    size = outs[0].shape[0] * len(outs)
    term = jnp.dot(
        projector[pl.ds(first, size), :], product[...], preferred_element_type=jnp.float32
    )
    for k, out in enumerate(outs):
        count = out.shape[0]
        out[...] = (term[k * count : (k + 1) * count] * scale).astype(out.dtype)


def project(blocks, here, layer_input, partial, projector, pieces, scale):
    kv, width = partial.shape
    half = projector.shape[0] // 2
    shape = [len(block) for block in blocks.values()]
    product, *sends = call_in_vmem(
        functools.partial(project_body, list(blocks), shape, scale),
        here,
        flat(blocks) + [layer_input, partial, projector],
        [jax.ShapeDtypeStruct((kv, width), jnp.bfloat16)]
        + [jax.ShapeDtypeStruct((half // pieces, width), jnp.bfloat16)] * pieces,
        2 * depth(blocks) * kv * width + 2 * half * kv * width,
    )
    return product, sends


def apply_rest(projector, product, here, pieces, scale):
    half = projector.shape[0] // 2
    kv, width = product.shape
    return call_in_vmem(
        functools.partial(apply_body, half, scale),
        here,
        [projector, product],
        [jax.ShapeDtypeStruct((half // pieces, width), jnp.float32)] * pieces,
        2 * half * kv * width,
    )


def on_device(layer_input, cotangent, candidates, moment_first, moment_second, owners):
    replicas = lax.axis_size("dp")
    members = lax.axis_size("fsdp")
    me_dp = lax.axis_index("dp")
    me_fsdp = lax.axis_index("fsdp")
    dp_bits = bits_of(replicas)
    far_bits = bits_of(members)[1:]
    scale = 1.0 / math.sqrt(layer_input.shape[0] * replicas)
    kv_share = candidates.shape[2] // replicas
    per = members // replicas

    order = [0]
    for bit in reversed(dp_bits):
        order = [mask ^ bit for mask in order] + order

    here = jnp.stack([me_dp, me_fsdp]).astype(jnp.int32)

    def owned(value, others):
        for at, bit in enumerate(dp_bits):
            if at == 1 and others:
                value = after(value, others, tokens)
            other = swap(value, "dp", bit)
            mine = (me_dp & bit) == (owners & bit)
            rows = jnp.repeat(mine, value.shape[0] // MATS)[:, None]
            value = jnp.where(rows, value, other)
        return value

    def assembled(value, others):
        blocks = spread(value, far_bits)
        same = jnp.concatenate([blocks[mask] for mask in sorted(blocks)], axis=0)
        same = after(same, others, tokens)
        other = swap(same, "fsdp", 1)
        return gather_projector(same, other, here, order, per, tokens)

    pieces = max(replicas // 2, 1)
    tokens = []

    own_other = swap(cotangent[0], "fsdp", 1)
    near, far, arrived = spread_near(cotangent[0], far_bits, tokens)
    both = jnp.swapaxes(candidates[:, 0], 1, 2).reshape(-1, candidates.shape[2])
    both_owned = owned(both, arrived)
    near_all = with_partner(near, own_other)
    later = [(mask, k) for mask in far_bits for k, piece in enumerate(near[mask])]
    later = [(mask, k) for mask, k in later if all(near[mask][k] is not x for x in arrived)]
    later_other = [near_all[mask ^ 1][k] for mask, k in later]
    later = [near[mask][k] for mask, k in later]
    projector_0, projector_1 = assembled(
        after(both_owned, later + flat(far), tokens), later_other
    )
    far_all = with_partner(far)
    partial = add_products(near_all, here, layer_input)
    product, send_0 = project(far_all, here, layer_input, partial, projector_0, pieces, scale)
    keep_0 = apply_rest(projector_0, product, here, pieces, scale)

    heads = lax.dot_general(
        cotangent[1], projector_1, (((1,), (1,)), ((), ())), preferred_element_type=jnp.float32
    ).astype(jnp.bfloat16)
    blocks = with_partner({mask: [held] for mask, held in spread(heads, far_bits).items()})
    send_1 = heads_product(blocks, here, layer_input, 0, pieces, jnp.bfloat16, scale)
    keep_1 = heads_product(blocks, here, layer_input, 1, pieces, jnp.float32, scale)

    def reduced(sends, keeps):
        for bit in dp_bits[:-1]:
            totals = [
                keep + swap(send, "dp", bit).astype(jnp.float32)
                for send, keep in zip(sends, keeps)
            ]
            half = len(totals) // 2
            sends = [total.astype(jnp.bfloat16) for total in totals[:half]]
            keeps = totals[half:]
        return keeps[0], swap(sends[0], "dp", dp_bits[-1])

    updates, firsts, seconds, directions = [], [], [], []
    for matrix, sends, keeps in ((0, send_0, keep_0), (1, send_1, keep_1)):
        keep, received = reduced(sends, keeps)
        if firsts:
            received, firsts[0] = lax.optimization_barrier((received, firsts[0]))
        projected = keep + received.astype(jnp.float32)
        first = beta_first * moment_first[matrix] + (1.0 - beta_first) * projected
        second = beta_second * moment_second[matrix] + (1.0 - beta_second) * projected * projected
        direction = (
            first
            / (1.0 - beta_first**STEP)
            / (jnp.sqrt(second / (1.0 - beta_second**STEP)) + epsilon)
        )
        directions.append(direction.astype(jnp.bfloat16))
        firsts.append(first)
        seconds.append(second)
    for direction, projector in zip(directions, (projector_0, projector_1)):
        own = lax.dynamic_slice_in_dim(projector, me_dp * kv_share, kv_share, 1)
        parts = [direction]
        for bit in reversed(dp_bits):
            parts = [swap(piece, "dp", bit) for piece in parts] + parts
        update = lax.dot_general(
            own, jnp.concatenate(parts, axis=0), TRANSPOSED, preferred_element_type=jnp.float32
        )
        updates.append(update.astype(jnp.bfloat16))
    return (jnp.stack(updates), jnp.stack(firsts), jnp.stack(seconds))


def solution(mesh):
    placed = (
        P("dp", "fsdp"),
        P(None, ("dp", "fsdp"), None),
        P(None, "dp", None, "fsdp"),
        P(None, "dp", "fsdp"),
        P(None, "dp", "fsdp"),
        P(),
    )
    return jax.shard_map(
        on_device,
        mesh=mesh,
        in_specs=placed,
        out_specs=(P(None, "dp", "fsdp"), P(None, "dp", "fsdp"), P(None, "dp", "fsdp")),
        check_vma=False,
    )
```

time: 170 us -> 154 us (0.906)
  Pallas kernels: 29.1 us -> 13.2 us
  local copies, waits for them, and re-layouts: 20.2 us -> 10.9 us
  waiting for transfers between devices: 68.5 us -> 74.5 us
  matrix products: 1.52 us -> 5.07 us
  between operations: 3.49 us -> 0.92 us
    pallas_call x6 -> x2, Pallas kernels: 16.9 us -> 5.91 us  [the longest x1 5.1 us: add_products(): pl.pallas_call(functools.partial(product_body, shape), grid_spec=pltpu.Pr...]
    ppermute x44 -> x38, waiting for transfers between devices: 68.5 us -> 74.5 us  [swap(): return lax.ppermute(value, axis, [(i, i ^ mask) for i in range(size)])]
    unnamed x60 -> x40, local copies, waits for them, and re-layouts: 14 us -> 8.4 us
    pallas_call x5 -> x4, Pallas kernels: 12.2 us -> 7.29 us  [call_in_vmem(): pl.pallas_call(body, grid_spec=pltpu.PrefetchScalarGridSpec(num_scalar_pr...]
    another operation x0 -> x3, other arithmetic: none -> 3.63 us  [on_device(): return (jnp.stack(updates), jnp.stack(firsts), jnp.stack(seconds))]
    dot_general x0 -> x2, matrix products: none -> 3.17 us  [on_device(): lax.dot_general(own, jnp.concatenate(parts, axis=0), TRANSPOSED, preferre...]
    add x2 -> x0, other arithmetic: 2.66 us -> none  [reduced(): keep + swap(send, 'dp', bit).astype(jnp.float32)]
    ppermute x44 -> x38, starting transfers between devices: 41.6 us -> 42 us  [swap(): return lax.ppermute(value, axis, [(i, i ^ mask) for i in range(size)])]
  transfers between devices with their start and end apart: 44 -> 38, of which waited for: 17 -> 19; matrix products, arithmetic and copies ran while one was open for 7% -> 6% of each run, Pallas kernels for 15% -> 9%
where the time goes in v3:
time: 154 us; the launch traced here: 153 us
  waiting for transfers between devices  74.5 us (48%)
  starting transfers between devices  42 us (27%)
  Pallas kernels  13.2 us (9%)
  local copies, waits for them, and re-layouts  10.9 us (7%)
  other arithmetic  6.1 us (4%)
  matrix products  5.07 us (3%)
    ppermute x38, waiting for transfers between devices, swap(): return lax.ppermute(value, axis, [(i, i ^ mask) for i in range(size)])  74.5 us
    ppermute x38, starting transfers between devices, swap(): return lax.ppermute(value, axis, [(i, i ^ mask) for i in range(size)])  42 us
    unnamed x40, local copies, waits for them, and re-layouts  8.4 us
    pallas_call x4, Pallas kernels, call_in_vmem(): pl.pallas_call(body, grid_spec=pltpu.PrefetchScalarGridSpec(num_scalar_pr...  7.29 us
    pallas_call x1, Pallas kernels, add_products(): pl.pallas_call(functools.partial(product_body, shape), grid_spec=pltpu.Pr...  5.1 us
    another operation x3, other arithmetic, on_device(): return (jnp.stack(updates), jnp.stack(firsts), jnp.stack(seconds))  3.63 us
    dot_general x2, matrix products, on_device(): lax.dot_general(own, jnp.concatenate(parts, axis=0), TRANSPOSED, preferre...  3.17 us
  transfers between devices with their start and end apart: 38, of which 19 were waited for; matrix products, arithmetic and copies ran while one was open for 6% of the time, Pallas kernels for 9%

profile of v3, /device:TPU:0, one launch (start us, length us, event | category | flops | bytes accessed | tf_op | source)
XLA Modules:
  0.0 152.7 jit_solution(17341275279553372914)
XLA Ops:
  0.6 1.1 slice_bitcast_fusion.1
  1.7 3.0 %collective-permute-start.2 = (bf16[128,1024]{1,0:T(8,128)(2,1)S(1)}, bf16[128,1024]{1,0:T(8,128)(2,1)S(1)}, u32[]{:S(2)}, u32[]{:S(2)}) collective-permute-start(bf16[128,1024]{1,0:T(8,128)(2,1)S(1)} %get-tuple-element.32), channel_id=1, source_target_pairs={{0,4},{1,5},{2,6},{3,7},{4,0},{5,1},{6,2},{7,3},{8,12},{9,13},{10,... | collective-permute-start | bytes 786440 | tf_op jit(solution)/shard_map/ppermute | solution.py:24
  4.7 1.5 collective-permute-start.1
  6.2 1.6 %collective-permute-start = (bf16[128,1024]{1,0:T(8,128)(2,1)}, bf16[128,1024]{1,0:T(8,128)(2,1)S(1)}, u32[]{:S(2)}, u32[]{:S(2)}) collective-permute-start(bf16[128,1024]{1,0:T(8,128)(2,1)} %bitcast.53), channel_id=1, source_target_pairs={{0,8},{8,0},{16,24},{24,16},{1,9},{9,1},{17,25},{25,17},{2,10},{10... | collective-permute-start | bytes 786440 | tf_op jit(solution)/shard_map/ppermute | solution.py:24
  7.8 0.7 and_compare_fusion.1
  8.6 2.4 %collective-permute-done.2.refs_4_ = bf16[128,1024]{1,0:T(8,128)(2,1)S(1)} collective-permute-done((bf16[128,1024]{1,0:T(8,128)(2,1)S(1)}, bf16[128,1024]{1,0:T(8,128)(2,1)S(1)}, u32[]{:S(2)}, u32[]{:S(2)}) %collective-permute-start.2) | collective-permute-done | bytes 262176 | tf_op jit(solution)/shard_map/ppermute | solution.py:24
  11.0 1.7 %collective-permute-start.5 = (bf16[128,1024]{1,0:T(8,128)(2,1)S(1)}, bf16[128,1024]{1,0:T(8,128)(2,1)S(1)}, u32[]{:S(2)}, u32[]{:S(2)}) collective-permute-start(bf16[128,1024]{1,0:T(8,128)(2,1)S(1)} %get-tuple-element.33), channel_id=1, source_target_pairs={{0,4},{1,5},{2,6},{3,7},{4,0},{5,1},{6,2},{7,3},{8,12},{9,13},{10,... | collective-permute-start | bytes 786440 | tf_op jit(solution)/shard_map/ppermute | solution.py:24
  12.8 1.1 collective-permute-done
  13.9 1.0 broadcast_select_fusion
  15.0 0.6 collective-permute-start.7
  15.6 1.5 collective-permute-start.4
  17.6 2.6 %collective-permute-start.3 = (bf16[128,1024]{1,0:T(8,128)(2,1)S(1)}, bf16[128,1024]{1,0:T(8,128)(2,1)S(1)}, u32[]{:S(2)}, u32[]{:S(2)}) collective-permute-start(bf16[128,1024]{1,0:T(8,128)(2,1)S(1)} %broadcast_select_fusion), channel_id=1, source_target_pairs={{0,16},{8,24},{16,0},{24,8},{1,17},{9,25},{17,1},{25,9},{2,18},{10... | collective-permute-start | bytes 786440 | tf_op jit(solution)/shard_map/ppermute | solution.py:24
  20.3 3.9 %collective-permute-done.7.refs_1_ = bf16[128,1024]{1,0:T(8,128)(2,1)S(1)} collective-permute-done((bf16[128,1024]{1,0:T(8,128)(2,1)S(1)}, bf16[128,1024]{1,0:T(8,128)(2,1)S(1)}, u32[]{:S(2)}, u32[]{:S(2)}) %collective-permute-start.7) | collective-permute-done | bytes 262176 | tf_op jit(solution)/shard_map/ppermute | solution.py:24
  24.3 2.9 %collective-permute-done.4.refs_2_ = bf16[128,1024]{1,0:T(8,128)(2,1)S(1)} collective-permute-done((bf16[128,1024]{1,0:T(8,128)(2,1)S(1)}, bf16[128,1024]{1,0:T(8,128)(2,1)S(1)}, u32[]{:S(2)}, u32[]{:S(2)}) %collective-permute-start.4) | collective-permute-done | bytes 262176 | tf_op jit(solution)/shard_map/ppermute | solution.py:24
  27.3 2.6 %collective-permute-done.3 = bf16[128,1024]{1,0:T(8,128)(2,1)S(1)} collective-permute-done((bf16[128,1024]{1,0:T(8,128)(2,1)S(1)}, bf16[128,1024]{1,0:T(8,128)(2,1)S(1)}, u32[]{:S(2)}, u32[]{:S(2)}) %collective-permute-start.3) | collective-permute-done | bytes 262176 | tf_op jit(solution)/shard_map/ppermute | solution.py:24
  30.5 1.8 %collective-permute-start.10 = (bf16[128,1024]{1,0:T(8,128)(2,1)S(1)}, bf16[128,1024]{1,0:T(8,128)(2,1)S(1)}, u32[]{:S(2)}, u32[]{:S(2)}) collective-permute-start(bf16[128,1024]{1,0:T(8,128)(2,1)S(1)} %broadcast_select_fusion.1), channel_id=1, source_target_pairs={{0,6},{1,7},{2,4},{3,5},{4,2},{5,3},{6,0},{7,1},{8,14},{9,15},{10,... | collective-permute-start | bytes 786440 | tf_op jit(solution)/shard_map/ppermute | solution.py:24
  32.7 1.2 collective-permute-start.8
  34.0 0.7 copy-done.9
  34.7 0.7 copy-done.11
  35.4 5.2 %collective-permute-done.10 = bf16[128,1024]{1,0:T(8,128)(2,1)S(1)} collective-permute-done((bf16[128,1024]{1,0:T(8,128)(2,1)S(1)}, bf16[128,1024]{1,0:T(8,128)(2,1)S(1)}, u32[]{:S(2)}, u32[]{:S(2)}) %collective-permute-start.10) | collective-permute-done | bytes 262176 | tf_op jit(solution)/shard_map/ppermute | solution.py:24
  40.6 4.7 %collective-permute-done.9 = bf16[128,1024]{1,0:T(8,128)(2,1)S(1)} collective-permute-done((bf16[128,1024]{1,0:T(8,128)(2,1)S(1)}, bf16[128,1024]{1,0:T(8,128)(2,1)S(1)}, u32[]{:S(2)}, u32[]{:S(2)}) %collective-permute-start.9) | collective-permute-done | bytes 262176 | tf_op jit(solution)/shard_map/ppermute | solution.py:24
  45.6 1.1 slice_bitcast_fusion.refs_0_
  48.2 1.0 copy-done.1
  49.3 1.2 copy-done.2
  50.6 0.8 shard_map.85
  51.4 1.9 %fusion.2.refs_0_ = bf16[256,512]{1,0:T(8,128)(2,1)S(1)} fusion(bf16[512,1024]{1,0:T(8,128)(2,1)S(1)} %get-tuple-element.52, bf16[2,256,1024]{2,1,0:T(8,128)(2,1)} %param.7), kind=kOutput, calls=%fused_computation.5 | convolution fusion | flops 268566528 | bytes 1835008 | tf_op jit(solution)/shard_map/dot_general | solution.py:336
  53.3 1.7 %collective-permute-start.27 = (bf16[256,512]{1,0:T(8,128)(2,1)S(1)}, bf16[256,512]{1,0:T(8,128)(2,1)S(1)}, u32[]{:S(2)}, u32[]{:S(2)}) collective-permute-start(bf16[256,512]{1,0:T(8,128)(2,1)S(1)} %fusion.2.refs_0_), channel_id=1, source_target_pairs={{0,6},{1,7},{2,4},{3,5},{4,2},{5,3},{6,0},{7,1},{8,14},{9,15},{10,... | collective-permute-start | bytes 786440 | tf_op jit(solution)/shard_map/ppermute | solution.py:24
  55.0 0.6 collective-permute-start.26
  55.7 1.2 collective-permute-start.25
  56.9 0.9 copy-done.4
  57.8 0.9 copy-done.6
  58.8 0.9 copy-done.8
  59.8 0.9 copy-done.10
  60.7 0.9 copy-done.12
  61.7 5.1 %shard_map.86.refs_5_ = f32[1024,1024]{1,0:T(8,128)S(1)} custom-call(s32[2]{0:T(128)S(1)} %pad_add_fusion.here, bf16[256,1024]{1,0:T(8,128)(2,1)S(1)} %slice_bitcast_fusion.refs_0_, bf16[128,1024]{1,0:T(8,128)(2,1)S(1)} %copy-done.4, bf16[128,1024]{1,0:T(8,128)(2,1)S(1)} %copy-done.8, bf16[128,1024]{1,0:T(8,128)(2,1)S(1)} %copy-done.6, ...), custom_call_target="tpu_custom_call" | custom-call | flops 3221225472 | bytes 10485760 | tf_op jit(solution)/shard_map/pallas_call | solution.py:209
  67.3 1.1 collective-permute-done.26.refs_2_
  69.0 2.4 %shard_map.87 = (bf16[1024,1024]{1,0:T(8,128)(2,1)S(1)}, bf16[128,1024]{1,0:T(8,128)(2,1)S(1)}, bf16[128,1024]{1,0:T(8,128)(2,1)S(1)}) custom-call(s32[2]{0:T(128)S(1)} %pad_add_fusion.here, bf16[128,1024]{1,0:T(8,128)(2,1)S(1)} %copy-done.16, bf16[128,1024]{1,0:T(8,128)(2,1)S(1)} %copy-done.14, bf16[128,1024]{1,0:T(8,128)(2,1)S(1)} %collective-permute-done.14.refs_2_, ...), custom_call_target="tpu_custom_call" | custom-call | flops 1610612736 | bytes 13107200 | tf_op jit(solution)/shard_map/pallas_call | solution.py:132
  71.4 0.7 collective-permute-start.20
  72.2 1.3 shard_map.88
  73.4 1.4 collective-permute-start.19
  74.9 1.8 %shard_map.90 = (bf16[128,1024]{1,0:T(8,128)(2,1)S(1)}, bf16[128,1024]{1,0:T(8,128)(2,1)S(1)}) custom-call(s32[2]{0:T(128)S(1)} %pad_add_fusion.here, bf16[256,512]{1,0:T(8,128)(2,1)S(1)} %fusion.2.refs_0_, bf16[256,512]{1,0:T(8,128)(2,1)S(1)} %collective-permute-done.25.refs_1_, bf16[256,512]{1,0:T(8,128)(2,1)S(1)} %collective-permute-done.26.refs_2_, ...), custom_call_target="tpu_custom_call" | custom-call | flops 1073741824 | bytes 6815744 | tf_op jit(solution)/shard_map/pallas_call | solution.py:132
  76.7 0.7 collective-permute-start.33
  77.4 3.2 %collective-permute-done.20 = bf16[128,1024]{1,0:T(8,128)(2,1)S(1)} collective-permute-done((bf16[128,1024]{1,0:T(8,128)(2,1)S(1)}, bf16[128,1024]{1,0:T(8,128)(2,1)S(1)}, u32[]{:S(2)}, u32[]{:S(2)}) %collective-permute-start.20) | collective-permute-done | bytes 262176 | tf_op jit(solution)/shard_map/ppermute | solution.py:24
  80.7 2.1 %collective-permute-start.21 = (bf16[128,1024]{1,0:T(8,128)(2,1)S(1)}, bf16[128,1024]{1,0:T(8,128)(2,1)S(1)}, u32[]{:S(2)}, u32[]{:S(2)}) collective-permute-start(bf16[128,1024]{1,0:T(8,128)(2,1)S(1)} %add_convert_fusion.1), channel_id=1, source_target_pairs={{0,16},{8,24},{16,0},{24,8},{1,17},{9,25},{17,1},{25,9},{2,18},{10... | collective-permute-start | bytes 786440 | tf_op jit(solution)/shard_map/ppermute | solution.py:24
  82.8 2.1 %collective-permute-start.32 = (bf16[128,1024]{1,0:T(8,128)(2,1)S(1)}, bf16[128,1024]{1,0:T(8,128)(2,1)S(1)}, u32[]{:S(2)}, u32[]{:S(2)}) collective-permute-start(bf16[128,1024]{1,0:T(8,128)(2,1)S(1)} %get-tuple-element.54), channel_id=1, source_target_pairs={{0,8},{8,0},{16,24},{24,16},{1,9},{9,1},{17,25},{25,17},{2,10},{10... | collective-permute-start | bytes 786440 | tf_op jit(solution)/shard_map/ppermute | solution.py:24
  84.9 1.8 %shard_map.89 = (f32[128,1024]{1,0:T(8,128)S(1)}, f32[128,1024]{1,0:T(8,128)S(1)}) custom-call(s32[2]{0:T(128)S(1)} %pad_add_fusion.here, bf16[256,512]{1,0:T(8,128)(2,1)S(1)} %fusion.2.refs_0_, bf16[256,512]{1,0:T(8,128)(2,1)S(1)} %collective-permute-done.25.refs_1_, bf16[256,512]{1,0:T(8,128)(2,1)S(1)} %collective-permute-done.26.refs_2_, ...), custom_call_target="tpu_custom_call" | custom-call | flops 1073741824 | bytes 7340032 | tf_op jit(solution)/shard_map/pallas_call | solution.py:132
  86.7 10.9 %collective-permute-done.33 = bf16[128,1024]{1,0:T(8,128)(2,1)S(1)} collective-permute-done((bf16[128,1024]{1,0:T(8,128)(2,1)S(1)}, bf16[128,1024]{1,0:T(8,128)(2,1)S(1)}, u32[]{:S(2)}, u32[]{:S(2)}) %collective-permute-start.33) | collective-permute-done | bytes 262176 | tf_op jit(solution)/shard_map/ppermute | solution.py:24
  97.6 1.6 %collective-permute-start.34 = (bf16[128,1024]{1,0:T(8,128)(2,1)S(1)}, bf16[128,1024]{1,0:T(8,128)(2,1)S(1)}, u32[]{:S(2)}, u32[]{:S(2)}) collective-permute-start(bf16[128,1024]{1,0:T(8,128)(2,1)S(1)} %add_convert_fusion), channel_id=1, source_target_pairs={{0,16},{8,24},{16,0},{24,8},{1,17},{9,25},{17,1},{25,9},{2,18},{10... | collective-permute-start | bytes 786440 | tf_op jit(solution)/shard_map/ppermute | solution.py:24
  99.7 1.4 collective-permute-start.22
  101.1 17.9 %collective-permute-done.34 = bf16[128,1024]{1,0:T(8,128)(2,1)S(1)} collective-permute-done((bf16[128,1024]{1,0:T(8,128)(2,1)S(1)}, bf16[128,1024]{1,0:T(8,128)(2,1)S(1)}, u32[]{:S(2)}, u32[]{:S(2)}) %collective-permute-start.34) | collective-permute-done | bytes 262176 | tf_op jit(solution)/shard_map/ppermute | solution.py:24
  119.0 1.1 fusion.28
  120.1 5.9 %collective-permute-start.24 = (bf16[128,1024]{1,0:T(8,128)(2,1)S(1)}, bf16[128,1024]{1,0:T(8,128)(2,1)}, u32[]{:S(2)}, u32[]{:S(2)}) collective-permute-start(bf16[128,1024]{1,0:T(8,128)(2,1)S(1)} %get-tuple-element.59), channel_id=1, source_target_pairs={{0,8},{8,0},{16,24},{24,16},{1,9},{9,1},{17,25},{25,17},{2,10},{10... | collective-permute-start | bytes 786440 | tf_op jit(solution)/shard_map/ppermute | solution.py:24
  126.1 1.7 %collective-permute-done.22 = bf16[128,1024]{1,0:T(8,128)(2,1)} collective-permute-done((bf16[128,1024]{1,0:T(8,128)(2,1)S(1)}, bf16[128,1024]{1,0:T(8,128)(2,1)}, u32[]{:S(2)}, u32[]{:S(2)}) %collective-permute-start.22) | collective-permute-done | bytes 262176 | tf_op jit(solution)/shard_map/ppermute | solution.py:24
  127.8 2.3 %collective-permute-start.23 = (bf16[128,1024]{1,0:T(8,128)(2,1)}, bf16[128,1024]{1,0:T(8,128)(2,1)}, u32[]{:S(2)}, u32[]{:S(2)}) collective-permute-start(bf16[128,1024]{1,0:T(8,128)(2,1)} %collective-permute-done.22), channel_id=1, source_target_pairs={{0,8},{8,0},{16,24},{24,16},{1,9},{9,1},{17,25},{25,17},{2,10},{10... | collective-permute-start | bytes 786440 | tf_op jit(solution)/shard_map/ppermute | solution.py:24
  130.1 3.2 %collective-permute-done.35 = bf16[128,1024]{1,0:T(8,128)(2,1)} collective-permute-done((bf16[128,1024]{1,0:T(8,128)(2,1)}, bf16[128,1024]{1,0:T(8,128)(2,1)}, u32[]{:S(2)}, u32[]{:S(2)}) %collective-permute-start.35) | collective-permute-done | bytes 262176 | tf_op jit(solution)/shard_map/ppermute | solution.py:24
  133.3 0.6 collective-permute-start.36
  133.9 2.4 %collective-permute-done.24 = bf16[128,1024]{1,0:T(8,128)(2,1)} collective-permute-done((bf16[128,1024]{1,0:T(8,128)(2,1)S(1)}, bf16[128,1024]{1,0:T(8,128)(2,1)}, u32[]{:S(2)}, u32[]{:S(2)}) %collective-permute-start.24) | collective-permute-done | bytes 262176 | tf_op jit(solution)/shard_map/ppermute | solution.py:24
  136.3 5.6 %collective-permute-done.23 = bf16[128,1024]{1,0:T(8,128)(2,1)} collective-permute-done((bf16[128,1024]{1,0:T(8,128)(2,1)}, bf16[128,1024]{1,0:T(8,128)(2,1)}, u32[]{:S(2)}, u32[]{:S(2)}) %collective-permute-start.23) | collective-permute-done | bytes 262176 | tf_op jit(solution)/shard_map/ppermute | solution.py:24
  141.9 1.6 %fusion = bf16[1,256,1024]{2,1,0:T(8,128)(2,1)S(1)} fusion(bf16[128,1024]{1,0:T(8,128)(2,1)S(1)} %get-tuple-element.59, bf16[128,1024]{1,0:T(8,128)(2,1)} %collective-permute-done.22, bf16[128,1024]{1,0:T(8,128)(2,1)} %collective-permute-done.24, bf16[128,1024]{1,0:T(8,128)(2,1)} %collective-permute-done.23, ...), kind=kOutput, calls=%fused_computation.2 | convolution fusion | flops 272891904 | bytes 1835012 | tf_op jit(solution)/shard_map/dot_general | solution.py:375
  143.5 1.5 pad_maximum_fusion.2
  145.0 2.2 %collective-permute-done.37 = bf16[128,1024]{1,0:T(8,128)(2,1)S(1)} collective-permute-done((bf16[128,1024]{1,0:T(8,128)(2,1)}, bf16[128,1024]{1,0:T(8,128)(2,1)S(1)}, u32[]{:S(2)}, u32[]{:S(2)}) %collective-permute-start.37) | collective-permute-done | bytes 262176 | tf_op jit(solution)/shard_map/ppermute | solution.py:24
  147.2 2.8 %collective-permute-done.36 = bf16[128,1024]{1,0:T(8,128)(2,1)S(1)} collective-permute-done((bf16[128,1024]{1,0:T(8,128)(2,1)}, bf16[128,1024]{1,0:T(8,128)(2,1)S(1)}, u32[]{:S(2)}, u32[]{:S(2)}) %collective-permute-start.36) | collective-permute-done | bytes 262176 | tf_op jit(solution)/shard_map/ppermute | solution.py:24
  150.0 1.6 %fusion.1 = bf16[1,256,1024]{2,1,0:T(8,128)(2,1)S(1)} fusion(bf16[128,1024]{1,0:T(8,128)(2,1)} %get-tuple-element.63, bf16[128,1024]{1,0:T(8,128)(2,1)} %collective-permute-done.35, bf16[128,1024]{1,0:T(8,128)(2,1)S(1)} %collective-permute-done.37, bf16[128,1024]{1,0:T(8,128)(2,1)S(1)} %collective-permute-done.36, bf16[512,1024]{1,0:T(8,128)(2,1)} %copy-done.17, ...), kind=kOutput, calls=%fused_computation.3 | convolution fusion | flops 272891904 | bytes 1835012 | tf_op jit(solution)/shard_map/dot_general | solution.py:375
  151.6 1.1 pad_maximum_fusion.1
  (86 shorter events, 5.7 us)
Async XLA Ops:
  1.7 9.3 %collective-permute-start.2 = (bf16[128,1024]{1,0:T(8,128)(2,1)S(1)}, bf16[128,1024]{1,0:T(8,128)(2,1)S(1)}, u32[]{:S(2)}, u32[]{:S(2)}) collective-permute-start(bf16[128,1024]{1,0:T(8,128)(2,1)S(1)} %get-tuple-element.32), channel_id=1, source_target_pairs={{0,4},{1,5},{2,6},{3,7},{4,0},{5,1},{6,2},{7,3},{8,12},{9,13},{10,... | collective-permute-start | bytes 786440 | tf_op jit(solution)/shard_map/ppermute | solution.py:24
  4.7 8.1 %collective-permute-start.1 = (bf16[128,1024]{1,0:T(8,128)(2,1)S(1)}, bf16[128,1024]{1,0:T(8,128)(2,1)S(1)}, u32[]{:S(2)}, u32[]{:S(2)}) collective-permute-start(bf16[128,1024]{1,0:T(8,128)(2,1)S(1)} %get-tuple-element.33), channel_id=1, source_target_pairs={{0,2},{1,3},{2,0},{3,1},{4,6},{5,7},{6,4},{7,5},{8,10},{9,11},{10,... | collective-permute-start | bytes 786440 | tf_op jit(solution)/shard_map/ppermute | solution.py:24
  6.2 7.7 %collective-permute-start = (bf16[128,1024]{1,0:T(8,128)(2,1)}, bf16[128,1024]{1,0:T(8,128)(2,1)S(1)}, u32[]{:S(2)}, u32[]{:S(2)}) collective-permute-start(bf16[128,1024]{1,0:T(8,128)(2,1)} %bitcast.53), channel_id=1, source_target_pairs={{0,8},{8,0},{16,24},{24,16},{1,9},{9,1},{17,25},{25,17},{2,10},{10... | collective-permute-start | bytes 786440 | tf_op jit(solution)/shard_map/ppermute | solution.py:24
  11.0 9.3 %collective-permute-start.5 = (bf16[128,1024]{1,0:T(8,128)(2,1)S(1)}, bf16[128,1024]{1,0:T(8,128)(2,1)S(1)}, u32[]{:S(2)}, u32[]{:S(2)}) collective-permute-start(bf16[128,1024]{1,0:T(8,128)(2,1)S(1)} %get-tuple-element.33), channel_id=1, source_target_pairs={{0,4},{1,5},{2,6},{3,7},{4,0},{5,1},{6,2},{7,3},{8,12},{9,13},{10,... | collective-permute-start | bytes 786440 | tf_op jit(solution)/shard_map/ppermute | solution.py:24
  12.8 32.6 %copy-start.3 = (bf16[128,1024]{1,0:T(8,128)(2,1)}, bf16[128,1024]{1,0:T(8,128)(2,1)S(1)}, u32[]{:S(2)}) copy-start(bf16[128,1024]{1,0:T(8,128)(2,1)S(1)} %collective-permute-done.1.refs_1_) | copy-start | bytes 786436
  15.0 9.3 %collective-permute-start.7 = (bf16[128,1024]{1,0:T(8,128)(2,1)S(1)}, bf16[128,1024]{1,0:T(8,128)(2,1)S(1)}, u32[]{:S(2)}, u32[]{:S(2)}) collective-permute-start(bf16[128,1024]{1,0:T(8,128)(2,1)S(1)} %collective-permute-done.2.refs_4_), channel_id=1, source_target_pairs={{0,2},{1,3},{2,0},{3,1},{4,6},{5,7},{6,4},{7,5},{8,10},{9,11},{10,... | collective-permute-start | bytes 786440 | tf_op jit(solution)/shard_map/ppermute | solution.py:24
  15.6 11.6 %collective-permute-start.4 = (bf16[128,1024]{1,0:T(8,128)(2,1)S(1)}, bf16[128,1024]{1,0:T(8,128)(2,1)S(1)}, u32[]{:S(2)}, u32[]{:S(2)}) collective-permute-start(bf16[128,1024]{1,0:T(8,128)(2,1)S(1)} %get-tuple-element.32), channel_id=1, source_target_pairs={{0,2},{1,3},{2,0},{3,1},{4,6},{5,7},{6,4},{7,5},{8,10},{9,11},{10,... | collective-permute-start | bytes 786440 | tf_op jit(solution)/shard_map/ppermute | solution.py:24
  17.1 10.2 %collective-permute-start.6 = (bf16[128,1024]{1,0:T(8,128)(2,1)S(1)}, bf16[128,1024]{1,0:T(8,128)(2,1)S(1)}, u32[]{:S(2)}, u32[]{:S(2)}) collective-permute-start(bf16[128,1024]{1,0:T(8,128)(2,1)S(1)} %collective-permute-done.1.refs_1_), channel_id=1, source_target_pairs={{0,4},{1,5},{2,6},{3,7},{4,0},{5,1},{6,2},{7,3},{8,12},{9,13},{10,... | collective-permute-start | bytes 786440 | tf_op jit(solution)/shard_map/ppermute | solution.py:24
  17.6 12.2 %collective-permute-start.3 = (bf16[128,1024]{1,0:T(8,128)(2,1)S(1)}, bf16[128,1024]{1,0:T(8,128)(2,1)S(1)}, u32[]{:S(2)}, u32[]{:S(2)}) collective-permute-start(bf16[128,1024]{1,0:T(8,128)(2,1)S(1)} %broadcast_select_fusion), channel_id=1, source_target_pairs={{0,16},{8,24},{16,0},{24,8},{1,17},{9,25},{17,1},{25,9},{2,18},{10... | collective-permute-start | bytes 786440 | tf_op jit(solution)/shard_map/ppermute | solution.py:24
  20.3 25.1 %copy-start.5 = (bf16[128,1024]{1,0:T(8,128)(2,1)}, bf16[128,1024]{1,0:T(8,128)(2,1)S(1)}, u32[]{:S(2)}) copy-start(bf16[128,1024]{1,0:T(8,128)(2,1)S(1)} %collective-permute-done.5.refs_3_) | copy-start | bytes 786436
  24.3 21.1 %copy-start.13 = (bf16[128,1024]{1,0:T(8,128)(2,1)}, bf16[128,1024]{1,0:T(8,128)(2,1)S(1)}, u32[]{:S(2)}) copy-start(bf16[128,1024]{1,0:T(8,128)(2,1)S(1)} %collective-permute-done.7.refs_1_) | copy-start | bytes 786436
  27.2 18.2 %copy-start.7 = (bf16[128,1024]{1,0:T(8,128)(2,1)}, bf16[128,1024]{1,0:T(8,128)(2,1)S(1)}, u32[]{:S(2)}) copy-start(bf16[128,1024]{1,0:T(8,128)(2,1)S(1)} %collective-permute-done.4.refs_2_) | copy-start | bytes 786436
  27.2 18.3 %copy-start.15 = (bf16[128,1024]{1,0:T(8,128)(2,1)}, bf16[128,1024]{1,0:T(8,128)(2,1)S(1)}, u32[]{:S(2)}) copy-start(bf16[128,1024]{1,0:T(8,128)(2,1)S(1)} %collective-permute-done.6.refs_0_) | copy-start | bytes 786436
  29.9 4.1 %collective-permute-start.12 = (bf16[128,1024]{1,0:T(8,128)(2,1)S(1)}, bf16[128,1024]{1,0:T(8,128)(2,1)S(1)}, u32[]{:S(2)}, u32[]{:S(2)}) collective-permute-start(bf16[128,1024]{1,0:T(8,128)(2,1)S(1)} %collective-permute-done.5.refs_3_), channel_id=1, source_target_pairs={{0,1},{1,0},{2,3},{3,2},{4,5},{5,4},{6,7},{7,6},{8,9},{9,8},{10,11... | collective-permute-start | bytes 786440 | tf_op jit(solution)/shard_map/ppermute | solution.py:24
  30.0 4.7 %collective-permute-start.11 = (bf16[128,1024]{1,0:T(8,128)(2,1)S(1)}, bf16[128,1024]{1,0:T(8,128)(2,1)S(1)}, u32[]{:S(2)}, u32[]{:S(2)}) collective-permute-start(bf16[128,1024]{1,0:T(8,128)(2,1)S(1)} %collective-permute-done.4.refs_2_), channel_id=1, source_target_pairs={{0,1},{1,0},{2,3},{3,2},{4,5},{5,4},{6,7},{7,6},{8,9},{9,8},{10,11... | collective-permute-start | bytes 786440 | tf_op jit(solution)/shard_map/ppermute | solution.py:24
  30.5 10.1 %collective-permute-start.10 = (bf16[128,1024]{1,0:T(8,128)(2,1)S(1)}, bf16[128,1024]{1,0:T(8,128)(2,1)S(1)}, u32[]{:S(2)}, u32[]{:S(2)}) collective-permute-start(bf16[128,1024]{1,0:T(8,128)(2,1)S(1)} %broadcast_select_fusion.1), channel_id=1, source_target_pairs={{0,6},{1,7},{2,4},{3,5},{4,2},{5,3},{6,0},{7,1},{8,14},{9,15},{10,... | collective-permute-start | bytes 786440 | tf_op jit(solution)/shard_map/ppermute | solution.py:24
  32.2 13.1 %collective-permute-start.9 = (bf16[128,1024]{1,0:T(8,128)(2,1)S(1)}, bf16[128,1024]{1,0:T(8,128)(2,1)S(1)}, u32[]{:S(2)}, u32[]{:S(2)}) collective-permute-start(bf16[128,1024]{1,0:T(8,128)(2,1)S(1)} %broadcast_select_fusion.1), channel_id=1, source_target_pairs={{0,4},{1,5},{2,6},{3,7},{4,0},{5,1},{6,2},{7,3},{8,12},{9,13},{10,... | collective-permute-start | bytes 786440 | tf_op jit(solution)/shard_map/ppermute | solution.py:24
  32.7 12.6 %collective-permute-start.8 = (bf16[128,1024]{1,0:T(8,128)(2,1)S(1)}, bf16[128,1024]{1,0:T(8,128)(2,1)S(1)}, u32[]{:S(2)}, u32[]{:S(2)}) collective-permute-start(bf16[128,1024]{1,0:T(8,128)(2,1)S(1)} %broadcast_select_fusion.1), channel_id=1, source_target_pairs={{0,2},{1,3},{2,0},{3,1},{4,6},{5,7},{6,4},{7,5},{8,10},{9,11},{10,... | collective-permute-start | bytes 786440 | tf_op jit(solution)/shard_map/ppermute | solution.py:24
  34.0 0.7 copy-start.9
  34.7 0.7 copy-start.11
  45.5 2.7 %collective-permute-start.13 = (bf16[512,1024]{1,0:T(8,128)(2,1)S(1)}, bf16[512,1024]{1,0:T(8,128)(2,1)S(1)}, u32[]{:S(2)}, u32[]{:S(2)}) collective-permute-start(bf16[512,1024]{1,0:T(8,128)(2,1)S(1)} %pad_maximum_fusion.same), channel_id=1, source_target_pairs={{0,1},{1,0},{2,3},{3,2},{4,5},{5,4},{6,7},{7,6},{8,9},{9,8},{10,11... | collective-permute-start | bytes 3145736 | tf_op jit(solution)/shard_map/ppermute | solution.py:24
  46.7 9.0 %collective-permute-start.16 = (bf16[256,1024]{1,0:T(8,128)(2,1)S(1)}, bf16[256,1024]{1,0:T(8,128)(2,1)S(1)}, u32[]{:S(2)}, u32[]{:S(2)}) collective-permute-start(bf16[256,1024]{1,0:T(8,128)(2,1)S(1)} %slice_bitcast_fusion.refs_0_), channel_id=1, source_target_pairs={{0,1},{1,0},{2,3},{3,2},{4,5},{5,4},{6,7},{7,6},{8,9},{9,8},{10,11... | collective-permute-start | bytes 1572872 | tf_op jit(solution)/shard_map/ppermute | solution.py:24
  47.3 9.6 %copy-start = (bf16[2048,1024]{1,0:T(8,128)(2,1)S(1)}, bf16[2048,1024]{1,0:T(8,128)(2,1)}, u32[]{:S(2)}) copy-start(bf16[2048,1024]{1,0:T(8,128)(2,1)} %refs_8_.3) | copy-start | bytes 12582916
  47.3 6.0 %collective-permute-start.18 = (bf16[128,1024]{1,0:T(8,128)(2,1)S(1)}, bf16[128,1024]{1,0:T(8,128)(2,1)S(1)}, u32[]{:S(2)}, u32[]{:S(2)}) collective-permute-start(bf16[128,1024]{1,0:T(8,128)(2,1)S(1)} %collective-permute-done.2.refs_4_), channel_id=1, source_target_pairs={{0,1},{1,0},{2,3},{3,2},{4,5},{5,4},{6,7},{7,6},{8,9},{9,8},{10,11... | collective-permute-start | bytes 786440 | tf_op jit(solution)/shard_map/ppermute | solution.py:24
  47.3 7.7 %collective-permute-start.17 = (bf16[128,1024]{1,0:T(8,128)(2,1)}, bf16[128,1024]{1,0:T(8,128)(2,1)S(1)}, u32[]{:S(2)}, u32[]{:S(2)}) collective-permute-start(bf16[128,1024]{1,0:T(8,128)(2,1)} %copy-done.3), channel_id=1, source_target_pairs={{0,1},{1,0},{2,3},{3,2},{4,5},{5,4},{6,7},{7,6},{8,9},{9,8},{10,11... | collective-permute-start | bytes 786440 | tf_op jit(solution)/shard_map/ppermute | solution.py:24
  47.8 18.9 %collective-permute-start.15 = (bf16[128,1024]{1,0:T(8,128)(2,1)}, bf16[128,1024]{1,0:T(8,128)(2,1)S(1)}, u32[]{:S(2)}, u32[]{:S(2)}) collective-permute-start(bf16[128,1024]{1,0:T(8,128)(2,1)} %copy-done.13), channel_id=1, source_target_pairs={{0,1},{1,0},{2,3},{3,2},{4,5},{5,4},{6,7},{7,6},{8,9},{9,8},{10,11... | collective-permute-start | bytes 786440 | tf_op jit(solution)/shard_map/ppermute | solution.py:24
  48.2 1.0 copy-start.1
  49.2 19.8 %collective-permute-start.14 = (bf16[128,1024]{1,0:T(8,128)(2,1)}, bf16[128,1024]{1,0:T(8,128)(2,1)S(1)}, u32[]{:S(2)}, u32[]{:S(2)}) collective-permute-start(bf16[128,1024]{1,0:T(8,128)(2,1)} %copy-done.15), channel_id=1, source_target_pairs={{0,1},{1,0},{2,3},{3,2},{4,5},{5,4},{6,7},{7,6},{8,9},{9,8},{10,11... | collective-permute-start | bytes 786440 | tf_op jit(solution)/shard_map/ppermute | solution.py:24
  49.3 1.2 copy-start.2
  51.4 4.3 %copy-start.17 = (bf16[512,1024]{1,0:T(8,128)(2,1)}, bf16[512,1024]{1,0:T(8,128)(2,1)S(1)}, u32[]{:S(2)}) copy-start(bf16[512,1024]{1,0:T(8,128)(2,1)S(1)} %get-tuple-element.52) | copy-start | bytes 3145732
  53.3 13.5 %collective-permute-start.27 = (bf16[256,512]{1,0:T(8,128)(2,1)S(1)}, bf16[256,512]{1,0:T(8,128)(2,1)S(1)}, u32[]{:S(2)}, u32[]{:S(2)}) collective-permute-start(bf16[256,512]{1,0:T(8,128)(2,1)S(1)} %fusion.2.refs_0_), channel_id=1, source_target_pairs={{0,6},{1,7},{2,4},{3,5},{4,2},{5,3},{6,0},{7,1},{8,14},{9,15},{10,... | collective-permute-start | bytes 786440 | tf_op jit(solution)/shard_map/ppermute | solution.py:24
  55.0 13.4 %collective-permute-start.26 = (bf16[256,512]{1,0:T(8,128)(2,1)S(1)}, bf16[256,512]{1,0:T(8,128)(2,1)S(1)}, u32[]{:S(2)}, u32[]{:S(2)}) collective-permute-start(bf16[256,512]{1,0:T(8,128)(2,1)S(1)} %fusion.2.refs_0_), channel_id=1, source_target_pairs={{0,4},{1,5},{2,6},{3,7},{4,0},{5,1},{6,2},{7,3},{8,12},{9,13},{10,... | collective-permute-start | bytes 786440 | tf_op jit(solution)/shard_map/ppermute | solution.py:24
  55.7 12.8 %collective-permute-start.25 = (bf16[256,512]{1,0:T(8,128)(2,1)S(1)}, bf16[256,512]{1,0:T(8,128)(2,1)S(1)}, u32[]{:S(2)}, u32[]{:S(2)}) collective-permute-start(bf16[256,512]{1,0:T(8,128)(2,1)S(1)} %fusion.2.refs_0_), channel_id=1, source_target_pairs={{0,2},{1,3},{2,0},{3,1},{4,6},{5,7},{6,4},{7,5},{8,10},{9,11},{10,... | collective-permute-start | bytes 786440 | tf_op jit(solution)/shard_map/ppermute | solution.py:24
  56.9 1.0 copy-start.4
  57.8 0.9 copy-start.6
  58.8 0.9 copy-start.8
  59.7 0.9 copy-start.10
  60.7 0.9 copy-start.12
  61.6 7.4 %copy-start.14 = (bf16[128,1024]{1,0:T(8,128)(2,1)S(1)}, bf16[128,1024]{1,0:T(8,128)(2,1)}, u32[]{:S(2)}) copy-start(bf16[128,1024]{1,0:T(8,128)(2,1)} %copy-done.13) | copy-start | bytes 786436
  61.7 7.4 %copy-start.16 = (bf16[128,1024]{1,0:T(8,128)(2,1)S(1)}, bf16[128,1024]{1,0:T(8,128)(2,1)}, u32[]{:S(2)}) copy-start(bf16[128,1024]{1,0:T(8,128)(2,1)} %copy-done.15) | copy-start | bytes 786436
  66.8 6.7 %collective-permute-start.28 = (bf16[256,512]{1,0:T(8,128)(2,1)S(1)}, bf16[256,512]{1,0:T(8,128)(2,1)S(1)}, u32[]{:S(2)}, u32[]{:S(2)}) collective-permute-start(bf16[256,512]{1,0:T(8,128)(2,1)S(1)} %fusion.2.refs_0_), channel_id=1, source_target_pairs={{0,1},{1,0},{2,3},{3,2},{4,5},{5,4},{6,7},{7,6},{8,9},{9,8},{10,11... | collective-permute-start | bytes 786440 | tf_op jit(solution)/shard_map/ppermute | solution.py:24
  66.9 8.0 %collective-permute-start.31 = (bf16[256,512]{1,0:T(8,128)(2,1)S(1)}, bf16[256,512]{1,0:T(8,128)(2,1)S(1)}, u32[]{:S(2)}, u32[]{:S(2)}) collective-permute-start(bf16[256,512]{1,0:T(8,128)(2,1)S(1)} %collective-permute-done.27.refs_3_), channel_id=1, source_target_pairs={{0,1},{1,0},{2,3},{3,2},{4,5},{5,4},{6,7},{7,6},{8,9},{9,8},{10,11... | collective-permute-start | bytes 786440 | tf_op jit(solution)/shard_map/ppermute | solution.py:24
  68.5 6.4 %collective-permute-start.30 = (bf16[256,512]{1,0:T(8,128)(2,1)S(1)}, bf16[256,512]{1,0:T(8,128)(2,1)S(1)}, u32[]{:S(2)}, u32[]{:S(2)}) collective-permute-start(bf16[256,512]{1,0:T(8,128)(2,1)S(1)} %collective-permute-done.26.refs_2_), channel_id=1, source_target_pairs={{0,1},{1,0},{2,3},{3,2},{4,5},{5,4},{6,7},{7,6},{8,9},{9,8},{10,11... | collective-permute-start | bytes 786440 | tf_op jit(solution)/shard_map/ppermute | solution.py:24
  68.5 6.4 %collective-permute-start.29 = (bf16[256,512]{1,0:T(8,128)(2,1)S(1)}, bf16[256,512]{1,0:T(8,128)(2,1)S(1)}, u32[]{:S(2)}, u32[]{:S(2)}) collective-permute-start(bf16[256,512]{1,0:T(8,128)(2,1)S(1)} %collective-permute-done.25.refs_1_), channel_id=1, source_target_pairs={{0,1},{1,0},{2,3},{3,2},{4,5},{5,4},{6,7},{7,6},{8,9},{9,8},{10,11... | collective-permute-start | bytes 786440 | tf_op jit(solution)/shard_map/ppermute | solution.py:24
  71.4 9.2 %collective-permute-start.20 = (bf16[128,1024]{1,0:T(8,128)(2,1)S(1)}, bf16[128,1024]{1,0:T(8,128)(2,1)S(1)}, u32[]{:S(2)}, u32[]{:S(2)}) collective-permute-start(bf16[128,1024]{1,0:T(8,128)(2,1)S(1)} %get-tuple-element.51), channel_id=1, source_target_pairs={{0,8},{8,0},{16,24},{24,16},{1,9},{9,1},{17,25},{25,17},{2,10},{10... | collective-permute-start | bytes 786440 | tf_op jit(solution)/shard_map/ppermute | solution.py:24
  73.4 25.8 %collective-permute-start.19 = (bf16[128,1024]{1,0:T(8,128)(2,1)S(1)}, bf16[128,1024]{1,0:T(8,128)(2,1)S(1)}, u32[]{:S(2)}, u32[]{:S(2)}) collective-permute-start(bf16[128,1024]{1,0:T(8,128)(2,1)S(1)} %get-tuple-element.49), channel_id=1, source_target_pairs={{0,8},{8,0},{16,24},{24,16},{1,9},{9,1},{17,25},{25,17},{2,10},{10... | collective-permute-start | bytes 786440 | tf_op jit(solution)/shard_map/ppermute | solution.py:24
  76.7 20.8 %collective-permute-start.33 = (bf16[128,1024]{1,0:T(8,128)(2,1)S(1)}, bf16[128,1024]{1,0:T(8,128)(2,1)S(1)}, u32[]{:S(2)}, u32[]{:S(2)}) collective-permute-start(bf16[128,1024]{1,0:T(8,128)(2,1)S(1)} %get-tuple-element.56), channel_id=1, source_target_pairs={{0,8},{8,0},{16,24},{24,16},{1,9},{9,1},{17,25},{25,17},{2,10},{10... | collective-permute-start | bytes 786440 | tf_op jit(solution)/shard_map/ppermute | solution.py:24
  80.7 18.5 %collective-permute-start.21 = (bf16[128,1024]{1,0:T(8,128)(2,1)S(1)}, bf16[128,1024]{1,0:T(8,128)(2,1)S(1)}, u32[]{:S(2)}, u32[]{:S(2)}) collective-permute-start(bf16[128,1024]{1,0:T(8,128)(2,1)S(1)} %add_convert_fusion.1), channel_id=1, source_target_pairs={{0,16},{8,24},{16,0},{24,8},{1,17},{9,25},{17,1},{25,9},{2,18},{10... | collective-permute-start | bytes 786440 | tf_op jit(solution)/shard_map/ppermute | solution.py:24
  82.8 16.4 %copy-start.18 = (f32[2,128,1024]{2,1,0:T(8,128)S(1)}, f32[2,128,1024]{2,1,0:T(8,128)}, u32[]{:S(2)}) copy-start(f32[2,128,1024]{2,1,0:T(8,128)} %param.10) | copy-start | bytes 3145732
  82.8 16.4 %copy-start.19 = (f32[2,128,1024]{2,1,0:T(8,128)S(1)}, f32[2,128,1024]{2,1,0:T(8,128)}, u32[]{:S(2)}) copy-start(f32[2,128,1024]{2,1,0:T(8,128)} %param.9) | copy-start | bytes 3145732
  82.8 36.2 %collective-permute-start.32 = (bf16[128,1024]{1,0:T(8,128)(2,1)S(1)}, bf16[128,1024]{1,0:T(8,128)(2,1)S(1)}, u32[]{:S(2)}, u32[]{:S(2)}) collective-permute-start(bf16[128,1024]{1,0:T(8,128)(2,1)S(1)} %get-tuple-element.54), channel_id=1, source_target_pairs={{0,8},{8,0},{16,24},{24,16},{1,9},{9,1},{17,25},{25,17},{2,10},{10... | collective-permute-start | bytes 786440 | tf_op jit(solution)/shard_map/ppermute | solution.py:24
  97.6 21.4 %collective-permute-start.34 = (bf16[128,1024]{1,0:T(8,128)(2,1)S(1)}, bf16[128,1024]{1,0:T(8,128)(2,1)S(1)}, u32[]{:S(2)}, u32[]{:S(2)}) collective-permute-start(bf16[128,1024]{1,0:T(8,128)(2,1)S(1)} %add_convert_fusion), channel_id=1, source_target_pairs={{0,16},{8,24},{16,0},{24,8},{1,17},{9,25},{17,1},{25,9},{2,18},{10... | collective-permute-start | bytes 786440 | tf_op jit(solution)/shard_map/ppermute | solution.py:24
  99.7 28.1 %collective-permute-start.22 = (bf16[128,1024]{1,0:T(8,128)(2,1)S(1)}, bf16[128,1024]{1,0:T(8,128)(2,1)}, u32[]{:S(2)}, u32[]{:S(2)}) collective-permute-start(bf16[128,1024]{1,0:T(8,128)(2,1)S(1)} %get-tuple-element.59), channel_id=1, source_target_pairs={{0,16},{8,24},{16,0},{24,8},{1,17},{9,25},{17,1},{25,9},{2,18},{10... | collective-permute-start | bytes 786440 | tf_op jit(solution)/shard_map/ppermute | solution.py:24
  120.1 13.2 %collective-permute-start.35 = (bf16[128,1024]{1,0:T(8,128)(2,1)}, bf16[128,1024]{1,0:T(8,128)(2,1)}, u32[]{:S(2)}, u32[]{:S(2)}) collective-permute-start(bf16[128,1024]{1,0:T(8,128)(2,1)} %get-tuple-element.63), channel_id=1, source_target_pairs={{0,16},{8,24},{16,0},{24,8},{1,17},{9,25},{17,1},{25,9},{2,18},{10... | collective-permute-start | bytes 786440 | tf_op jit(solution)/shard_map/ppermute | solution.py:24
  120.1 16.2 %collective-permute-start.24 = (bf16[128,1024]{1,0:T(8,128)(2,1)S(1)}, bf16[128,1024]{1,0:T(8,128)(2,1)}, u32[]{:S(2)}, u32[]{:S(2)}) collective-permute-start(bf16[128,1024]{1,0:T(8,128)(2,1)S(1)} %get-tuple-element.59), channel_id=1, source_target_pairs={{0,8},{8,0},{16,24},{24,16},{1,9},{9,1},{17,25},{25,17},{2,10},{10... | collective-permute-start | bytes 786440 | tf_op jit(solution)/shard_map/ppermute | solution.py:24
  127.8 14.2 %collective-permute-start.23 = (bf16[128,1024]{1,0:T(8,128)(2,1)}, bf16[128,1024]{1,0:T(8,128)(2,1)}, u32[]{:S(2)}, u32[]{:S(2)}) collective-permute-start(bf16[128,1024]{1,0:T(8,128)(2,1)} %collective-permute-done.22), channel_id=1, source_target_pairs={{0,8},{8,0},{16,24},{24,16},{1,9},{9,1},{17,25},{25,17},{2,10},{10... | collective-permute-start | bytes 786440 | tf_op jit(solution)/shard_map/ppermute | solution.py:24
  130.0 17.1 %collective-permute-start.37 = (bf16[128,1024]{1,0:T(8,128)(2,1)}, bf16[128,1024]{1,0:T(8,128)(2,1)S(1)}, u32[]{:S(2)}, u32[]{:S(2)}) collective-permute-start(bf16[128,1024]{1,0:T(8,128)(2,1)} %get-tuple-element.63), channel_id=1, source_target_pairs={{0,8},{8,0},{16,24},{24,16},{1,9},{9,1},{17,25},{25,17},{2,10},{10... | collective-permute-start | bytes 786440 | tf_op jit(solution)/shard_map/ppermute | solution.py:24
  133.3 16.7 %collective-permute-start.36 = (bf16[128,1024]{1,0:T(8,128)(2,1)}, bf16[128,1024]{1,0:T(8,128)(2,1)S(1)}, u32[]{:S(2)}, u32[]{:S(2)}) collective-permute-start(bf16[128,1024]{1,0:T(8,128)(2,1)} %collective-permute-done.35), channel_id=1, source_target_pairs={{0,8},{8,0},{16,24},{24,16},{1,9},{9,1},{17,25},{25,17},{2,10},{10... | collective-permute-start | bytes 786440 | tf_op jit(solution)/shard_map/ppermute | solution.py:24

commit v4 on v3

--- a/solution.py
+++ b/solution.py
@@ -80,22 +80,21 @@
 
 
 def gather_body(order, per, count, here, same, other, *refs):
-    outs = refs[-MATS:]
-    for matrix, out in enumerate(outs):
-        spot = 0
-        for mask in order:
-            for sub in range(per):
-                away = ((here[0] ^ mask) * per + sub) ^ here[1]
-                at = pl.multiple_of(((away >> 1) * MATS + matrix) * count, count)
-                out[pl.ds(spot * count, count), :] = jnp.where(
-                    (away & 1) == 0, same[pl.ds(at, count), :], other[pl.ds(at, count), :]
-                )
-                spot += 1
+    out = refs[-1]
+    spot = 0
+    for mask in order:
+        for sub in range(per):
+            away = ((here[0] ^ mask) * per + sub) ^ here[1]
+            at = pl.multiple_of((away >> 1) * count, count)
+            out[pl.ds(spot * count, count), :] = jnp.where(
+                (away & 1) == 0, same[pl.ds(at, count), :], other[pl.ds(at, count), :]
+            )
+            spot += 1
 
 
 def gather_projector(same, other, here, order, per, tokens):
     rows, kv = same.shape
-    rank = 2 * rows // MATS
+    rank = 2 * rows
     return pl.pallas_call(
         functools.partial(gather_body, order, per, rank // (len(order) * per)),
         grid_spec=pltpu.PrefetchScalarGridSpec(
@@ -103,10 +102,10 @@
             grid=(1,),
             in_specs=[whole((rows, kv))] * 2
             + [pl.BlockSpec(memory_space=pl.ANY)] * len(tokens),
-            out_specs=[whole((rank, kv))] * MATS,
-        ),
-        out_shape=[jax.ShapeDtypeStruct((rank, kv), same.dtype)] * MATS,
-        compiler_params=pltpu.CompilerParams(vmem_limit_bytes=16 * MIB),
+            out_specs=whole((rank, kv)),
+        ),
+        out_shape=jax.ShapeDtypeStruct((rank, kv), same.dtype),
+        compiler_params=pltpu.CompilerParams(vmem_limit_bytes=12 * MIB),
         cost_estimate=pl.CostEstimate(flops=0, bytes_accessed=8 * rows * kv, transcendentals=0),
     )(here, same, other, *tokens)
 
@@ -153,9 +152,9 @@
     return sum(piece.shape[0] for piece in flat(blocks))
 
 
-def heads_body(masks, shape, part, scale, here, *refs):
+def heads_body(masks, shape, part, pieces, scale, here, *refs):
     groups = regroup(refs[: sum(shape)], shape)
-    rows, outs = refs[sum(shape)], refs[sum(shape) + 1 :]
+    rows, outs = refs[sum(shape)], refs[-pieces:]
     size = outs[0].shape[0] * len(outs)
     total = None
     for mask, block in zip(masks, groups):
@@ -166,16 +165,17 @@
         out[...] = (total[k * count : (k + 1) * count] * scale).astype(out.dtype)
 
 
-def heads_product(blocks, here, layer_input, part, pieces, dtype, scale):
+def heads_product(blocks, here, layer_input, part, pieces, dtype, scale, tokens=()):
     half = flat(blocks)[0].shape[1] // 2
     width = layer_input.shape[1]
     shape = [len(block) for block in blocks.values()]
     return call_in_vmem(
-        functools.partial(heads_body, list(blocks), shape, part, scale),
+        functools.partial(heads_body, list(blocks), shape, part, pieces, scale),
         here,
         flat(blocks) + [layer_input],
         [jax.ShapeDtypeStruct((half // pieces, width), dtype)] * pieces,
         2 * depth(blocks) * half * width,
+        tokens,
     )
 
 
@@ -296,66 +296,68 @@
 
     here = jnp.stack([me_dp, me_fsdp]).astype(jnp.int32)
 
-    def owned(value, others):
+    def owned(matrix, value, others, tokens):
+        steps = []
         for at, bit in enumerate(dp_bits):
             if at == 1 and others:
                 value = after(value, others, tokens)
             other = swap(value, "dp", bit)
-            mine = (me_dp & bit) == (owners & bit)
-            rows = jnp.repeat(mine, value.shape[0] // MATS)[:, None]
-            value = jnp.where(rows, value, other)
-        return value
-
-    def assembled(value, others):
+            mine = (me_dp & bit) == (owners[matrix] & bit)
+            value = jnp.where(mine, value, other)
+            steps.append(value)
+        return value, steps[0]
+
+    def same_core(value):
         blocks = spread(value, far_bits)
-        same = jnp.concatenate([blocks[mask] for mask in sorted(blocks)], axis=0)
-        same = after(same, others, tokens)
-        other = swap(same, "fsdp", 1)
-        return gather_projector(same, other, here, order, per, tokens)
+        return jnp.concatenate([blocks[mask] for mask in sorted(blocks)], axis=0)
+
+    def assembled(same, tokens):
+        return gather_projector(same, swap(same, "fsdp", 1), here, order, per, tokens)
 
     pieces = max(replicas // 2, 1)
-    tokens = []
-
-    own_other = swap(cotangent[0], "fsdp", 1)
+    tokens, tokens_1 = [], []
+
     near, far, arrived = spread_near(cotangent[0], far_bits, tokens)
-    both = jnp.swapaxes(candidates[:, 0], 1, 2).reshape(-1, candidates.shape[2])
-    both_owned = owned(both, arrived)
-    near_all = with_partner(near, own_other)
-    later = [(mask, k) for mask in far_bits for k, piece in enumerate(near[mask])]
-    later = [(mask, k) for mask, k in later if all(near[mask][k] is not x for x in arrived)]
-    later_other = [near_all[mask ^ 1][k] for mask, k in later]
-    later = [near[mask][k] for mask, k in later]
-    projector_0, projector_1 = assembled(
-        after(both_owned, later + flat(far), tokens), later_other
-    )
+    owned_0, step_0 = owned(0, candidates[0, 0].T, arrived, tokens)
+    later = [piece for mask in far_bits for piece in near.get(mask, ())]
+    later = [piece for piece in later if all(piece is not other for other in arrived)]
+    same_0 = same_core(after(owned_0, later + flat(far), tokens))
+    near_all = with_partner(near)
+    partial = add_products(near_all, here, layer_input)
     far_all = with_partner(far)
-    partial = add_products(near_all, here, layer_input)
+    projector_0 = assembled(after(same_0, [partial], tokens), tokens)
     product, send_0 = project(far_all, here, layer_input, partial, projector_0, pieces, scale)
     keep_0 = apply_rest(projector_0, product, here, pieces, scale)
 
+    owned_1, _ = owned(1, after(candidates[1, 0].T, [step_0], tokens_1), [owned_0], tokens_1)
+    same_1 = same_core(after(owned_1, [same_0], tokens_1))
+    projector_1 = assembled(after(same_1, send_0[:1], tokens_1), tokens_1)
     heads = lax.dot_general(
         cotangent[1], projector_1, (((1,), (1,)), ((), ())), preferred_element_type=jnp.float32
     ).astype(jnp.bfloat16)
     blocks = with_partner({mask: [held] for mask, held in spread(heads, far_bits).items()})
-    send_1 = heads_product(blocks, here, layer_input, 0, pieces, jnp.bfloat16, scale)
+    arrived_0 = [swap(piece, "dp", dp_bits[0]) for piece in send_0]
+    send_1 = heads_product(
+        blocks, here, layer_input, 0, pieces, jnp.bfloat16, scale, arrived_0[pieces // 2 :]
+    )
+    arrived_1 = [swap(piece, "dp", dp_bits[0]) for piece in send_1]
     keep_1 = heads_product(blocks, here, layer_input, 1, pieces, jnp.float32, scale)
 
-    def reduced(sends, keeps):
-        for bit in dp_bits[:-1]:
-            totals = [
-                keep + swap(send, "dp", bit).astype(jnp.float32)
-                for send, keep in zip(sends, keeps)
-            ]
+    def reduced(arrived, keeps):
+        for bit in dp_bits[1:]:
+            totals = [keep + piece.astype(jnp.float32) for piece, keep in zip(arrived, keeps)]
             half = len(totals) // 2
-            sends = [total.astype(jnp.bfloat16) for total in totals[:half]]
+            arrived = [swap(total.astype(jnp.bfloat16), "dp", bit) for total in totals[:half]]
             keeps = totals[half:]
-        return keeps[0], swap(sends[0], "dp", dp_bits[-1])
-
-    updates, firsts, seconds, directions = [], [], [], []
-    for matrix, sends, keeps in ((0, send_0, keep_0), (1, send_1, keep_1)):
-        keep, received = reduced(sends, keeps)
-        if firsts:
-            received, firsts[0] = lax.optimization_barrier((received, firsts[0]))
+        return keeps[0], arrived[0]
+
+    updates, firsts, seconds, gathered = [], [], [], []
+    for matrix, arrived, keeps in ((0, arrived_0, keep_0), (1, arrived_1, keep_1)):
+        keep, received = reduced(arrived, keeps)
+        if gathered:
+            received, firsts[0], *gathered[0][-3:-1] = lax.optimization_barrier(
+                (received, firsts[0], *gathered[0][-3:-1])
+            )
         projected = keep + received.astype(jnp.float32)
         first = beta_first * moment_first[matrix] + (1.0 - beta_first) * projected
         second = beta_second * moment_second[matrix] + (1.0 - beta_second) * projected * projected
@@ -364,14 +366,14 @@
             / (1.0 - beta_first**STEP)
             / (jnp.sqrt(second / (1.0 - beta_second**STEP)) + epsilon)
         )
-        directions.append(direction.astype(jnp.bfloat16))
+        parts = [direction.astype(jnp.bfloat16)]
+        for bit in reversed(dp_bits):
+            parts = [swap(piece, "dp", bit) for piece in parts] + parts
+        gathered.append(parts)
         firsts.append(first)
         seconds.append(second)
-    for direction, projector in zip(directions, (projector_0, projector_1)):
+    for parts, projector in zip(gathered, (projector_0, projector_1)):
         own = lax.dynamic_slice_in_dim(projector, me_dp * kv_share, kv_share, 1)
-        parts = [direction]
-        for bit in reversed(dp_bits):
-            parts = [swap(piece, "dp", bit) for piece in parts] + parts
         update = lax.dot_general(
             own, jnp.concatenate(parts, axis=0), TRANSPOSED, preferred_element_type=jnp.float32
         )

time: 154 us -> 151 us (0.981)
  waiting for transfers between devices: 74.5 us -> 82.3 us
  starting transfers between devices: 42 us -> 35.5 us
  local copies, waits for them, and re-layouts: 10.9 us -> 6.54 us
  between operations: 0.92 us -> 3.71 us
    ppermute x38 -> x44, waiting for transfers between devices: 74.5 us -> 82.3 us  [swap(): return lax.ppermute(value, axis, [(i, i ^ mask) for i in range(size)])]
    ppermute x38 -> x44, starting transfers between devices: 42 us -> 35.5 us  [swap(): return lax.ppermute(value, axis, [(i, i ^ mask) for i in range(size)])]
    unnamed x40 -> x18, local copies, waits for them, and re-layouts: 8.4 us -> 2.23 us
  transfers between devices with their start and end apart: 38 -> 44, of which waited for: 19 -> 26; matrix products, arithmetic and copies ran while one was open for 6% -> 6% of each run, Pallas kernels for 9% -> 7%
where the time goes in v4:
time: 151 us
  waiting for transfers between devices  82.3 us (55%)
  starting transfers between devices  35.5 us (24%)
  Pallas kernels  13.7 us (9%)
  local copies, waits for them, and re-layouts  6.54 us (4%)
  other arithmetic  5.68 us (4%)
  between operations  3.71 us (2%)
  matrix products  3.63 us (2%)
    ppermute x44, waiting for transfers between devices, swap(): return lax.ppermute(value, axis, [(i, i ^ mask) for i in range(size)])  82.3 us
    ppermute x44, starting transfers between devices, swap(): return lax.ppermute(value, axis, [(i, i ^ mask) for i in range(size)])  35.5 us
    pallas_call x4, Pallas kernels, call_in_vmem(): pl.pallas_call(body, grid_spec=pltpu.PrefetchScalarGridSpec(num_scalar_pr...  7.29 us
    pallas_call x1, Pallas kernels, add_products(): pl.pallas_call(functools.partial(product_body, shape), grid_spec=pltpu.Pr...  5.1 us
    another operation x3, other arithmetic, on_device(): return (jnp.stack(updates), jnp.stack(firsts), jnp.stack(seconds))  4.02 us
    dot_general x2, matrix products, on_device(): lax.dot_general(own, jnp.concatenate(parts, axis=0), TRANSPOSED, preferre...  3.1 us
  transfers between devices with their start and end apart: 44, of which 26 were waited for; matrix products, arithmetic and copies ran while one was open for 6% of the time, Pallas kernels for 7%

profile of v4, /device:TPU:0, one launch (start us, length us, event | category | flops | bytes accessed | tf_op | source)
XLA Modules:
  0.0 151.1 jit_solution(4104516331430223538)
XLA Ops:
  0.6 1.1 slice_bitcast_fusion.4
  1.7 3.1 %collective-permute-start = (bf16[64,1024]{1,0:T(8,128)(2,1)S(1)}, bf16[64,1024]{1,0:T(8,128)(2,1)S(1)}, u32[]{:S(2)}, u32[]{:S(2)}) collective-permute-start(bf16[64,1024]{1,0:T(8,128)(2,1)S(1)} %get-tuple-element.81), channel_id=1, source_target_pairs={{0,8},{8,0},{16,24},{24,16},{1,9},{9,1},{17,25},{25,17},{2,10},{10... | collective-permute-start | bytes 393224 | tf_op jit(solution)/shard_map/ppermute | solution.py:24
  4.8 1.9 %slice_bitcast_fusion.1 = (bf16[128,1024]{1,0:T(8,128)(2,1)}, bf16[128,1024]{1,0:T(8,128)(2,1)}) fusion(bf16[2,256,1024]{2,1,0:T(8,128)(2,1)} %param.7), kind=kLoop, calls=%fused_computation.42 | loop fusion | bytes 1048576 | tf_op jit(solution)/shard_map/slice | solution.py:53
  6.7 1.5 collective-permute-start.1
  8.2 1.5 %collective-permute-start.2 = (bf16[128,1024]{1,0:T(8,128)(2,1)}, bf16[128,1024]{1,0:T(8,128)(2,1)S(1)}, u32[]{:S(2)}, u32[]{:S(2)}) collective-permute-start(bf16[128,1024]{1,0:T(8,128)(2,1)} %get-tuple-element.39), channel_id=1, source_target_pairs={{0,4},{1,5},{2,6},{3,7},{4,0},{5,1},{6,2},{7,3},{8,12},{9,13},{10,... | collective-permute-start | bytes 786440 | tf_op jit(solution)/shard_map/ppermute | solution.py:24
  9.7 1.3 fusion.30
  11.7 0.9 broadcast_select_fusion.2
  12.6 2.0 %collective-permute-done.1.refs_1_ = bf16[128,1024]{1,0:T(8,128)(2,1)S(1)} collective-permute-done((bf16[128,1024]{1,0:T(8,128)(2,1)}, bf16[128,1024]{1,0:T(8,128)(2,1)S(1)}, u32[]{:S(2)}, u32[]{:S(2)}) %collective-permute-start.1) | collective-permute-done | bytes 262176 | tf_op jit(solution)/shard_map/ppermute | solution.py:24
  14.6 1.2 collective-permute-done.2.refs_4_
  15.9 2.6 %collective-permute-start.3 = (bf16[64,1024]{1,0:T(8,128)(2,1)S(1)}, bf16[64,1024]{1,0:T(8,128)(2,1)S(1)}, u32[]{:S(2)}, u32[]{:S(2)}) collective-permute-start(bf16[64,1024]{1,0:T(8,128)(2,1)S(1)} %broadcast_select_fusion.2), channel_id=1, source_target_pairs={{0,16},{8,24},{16,0},{24,8},{1,17},{9,25},{17,1},{25,9},{2,18},{10... | collective-permute-start | bytes 393224 | tf_op jit(solution)/shard_map/ppermute | solution.py:24
  18.4 0.5 collective-permute-start.4
  19.0 1.5 %collective-permute-start.5 = (bf16[128,1024]{1,0:T(8,128)(2,1)}, bf16[128,1024]{1,0:T(8,128)(2,1)S(1)}, u32[]{:S(2)}, u32[]{:S(2)}) collective-permute-start(bf16[128,1024]{1,0:T(8,128)(2,1)} %get-tuple-element.40), channel_id=1, source_target_pairs={{0,4},{1,5},{2,6},{3,7},{4,0},{5,1},{6,2},{7,3},{8,12},{9,13},{10,... | collective-permute-start | bytes 786440 | tf_op jit(solution)/shard_map/ppermute | solution.py:24
  21.0 1.5 collective-permute-start.7
  23.4 4.4 %collective-permute-done.4.refs_2_ = bf16[128,1024]{1,0:T(8,128)(2,1)S(1)} collective-permute-done((bf16[128,1024]{1,0:T(8,128)(2,1)}, bf16[128,1024]{1,0:T(8,128)(2,1)S(1)}, u32[]{:S(2)}, u32[]{:S(2)}) %collective-permute-start.4) | collective-permute-done | bytes 262176 | tf_op jit(solution)/shard_map/ppermute | solution.py:24
  28.2 2.7 %collective-permute-done.6.refs_0_ = bf16[128,1024]{1,0:T(8,128)(2,1)S(1)} collective-permute-done((bf16[128,1024]{1,0:T(8,128)(2,1)S(1)}, bf16[128,1024]{1,0:T(8,128)(2,1)S(1)}, u32[]{:S(2)}, u32[]{:S(2)}) %collective-permute-start.6) | collective-permute-done | bytes 262176 | tf_op jit(solution)/shard_map/ppermute | solution.py:24
  30.9 2.4 %collective-permute-start.10 = (bf16[64,1024]{1,0:T(8,128)(2,1)S(1)}, bf16[64,1024]{1,0:T(8,128)(2,1)S(1)}, u32[]{:S(2)}, u32[]{:S(2)}) collective-permute-start(bf16[64,1024]{1,0:T(8,128)(2,1)S(1)} %broadcast_select_fusion.3), channel_id=1, source_target_pairs={{0,6},{1,7},{2,4},{3,5},{4,2},{5,3},{6,0},{7,1},{8,14},{9,15},{10,... | collective-permute-start | bytes 393224 | tf_op jit(solution)/shard_map/ppermute | solution.py:24
  33.3 0.7 collective-permute-start.8
  35.9 1.0 collective-permute-done.10
  36.9 1.5 collective-permute-done.8
  38.3 0.6 collective-permute-done.9
  39.9 0.6 collective-permute-done.14.refs_8_
  40.5 2.2 %copy-done = bf16[2048,1024]{1,0:T(8,128)(2,1)S(1)} copy-done((bf16[2048,1024]{1,0:T(8,128)(2,1)S(1)}, bf16[2048,1024]{1,0:T(8,128)(2,1)}, u32[]{:S(2)}) %copy-start) | copy-done | bytes 4194328
  42.7 5.1 %shard_map.85.refs_5_ = f32[1024,1024]{1,0:T(8,128)S(1)} custom-call(s32[2]{0:T(128)S(1)} %pad_add_fusion.here, bf16[256,1024]{1,0:T(8,128)(2,1)S(1)} %slice_bitcast_fusion.refs_0_, bf16[128,1024]{1,0:T(8,128)(2,1)S(1)} %collective-permute-done.1.refs_1_, bf16[128,1024]{1,0:T(8,128)(2,1)S(1)} %collective-permute-done.4.refs_2_, ...), custom_call_target="tpu_custom_call" | custom-call | flops 3221225472 | bytes 10485760 | tf_op jit(solution)/shard_map/pallas_call | solution.py:209
  48.0 0.6 collective-permute-done.25
  48.6 1.4 collective-permute-start.26
  50.1 0.5 collective-permute-start.18
  50.6 0.8 collective-permute-start.27
  51.4 2.7 %collective-permute-done.26 = bf16[64,1024]{1,0:T(8,128)(2,1)S(1)} collective-permute-done((bf16[64,1024]{1,0:T(8,128)(2,1)S(1)}, bf16[64,1024]{1,0:T(8,128)(2,1)S(1)}, u32[]{:S(2)}, u32[]{:S(2)}) %collective-permute-start.26) | collective-permute-done | bytes 131104 | tf_op jit(solution)/shard_map/ppermute | solution.py:24
  54.2 1.7 %collective-permute-start.28 = (bf16[64,1024]{1,0:T(8,128)(2,1)S(1)}, bf16[64,1024]{1,0:T(8,128)(2,1)S(1)}, u32[]{:S(2)}, u32[]{:S(2)}) collective-permute-start(bf16[64,1024]{1,0:T(8,128)(2,1)S(1)} %broadcast_select_fusion.1), channel_id=1, source_target_pairs={{0,6},{1,7},{2,4},{3,5},{4,2},{5,3},{6,0},{7,1},{8,14},{9,15},{10,... | collective-permute-start | bytes 393224 | tf_op jit(solution)/shard_map/ppermute | solution.py:24
  56.0 4.0 %collective-permute-done.28 = bf16[64,1024]{1,0:T(8,128)(2,1)S(1)} collective-permute-done((bf16[64,1024]{1,0:T(8,128)(2,1)S(1)}, bf16[64,1024]{1,0:T(8,128)(2,1)S(1)}, u32[]{:S(2)}, u32[]{:S(2)}) %collective-permute-start.28) | collective-permute-done | bytes 131104 | tf_op jit(solution)/shard_map/ppermute | solution.py:24
  60.1 0.7 shard_map.86.refs_6_.projector
  60.8 2.4 %shard_map.87 = (bf16[1024,1024]{1,0:T(8,128)(2,1)S(1)}, bf16[128,1024]{1,0:T(8,128)(2,1)S(1)}, bf16[128,1024]{1,0:T(8,128)(2,1)S(1)}) custom-call(s32[2]{0:T(128)S(1)} %pad_add_fusion.here, bf16[128,1024]{1,0:T(8,128)(2,1)S(1)} %collective-permute-done.6.refs_0_, bf16[128,1024]{1,0:T(8,128)(2,1)S(1)} %collective-permute-done.7.refs_1_, ...), custom_call_target="tpu_custom_call" | custom-call | flops 1610612736 | bytes 13107200 | tf_op jit(solution)/shard_map/pallas_call | solution.py:131
  63.5 1.7 %collective-permute-done.29.other = bf16[256,1024]{1,0:T(8,128)(2,1)S(1)} collective-permute-done((bf16[256,1024]{1,0:T(8,128)(2,1)S(1)}, bf16[256,1024]{1,0:T(8,128)(2,1)S(1)}, u32[]{:S(2)}, u32[]{:S(2)}) %collective-permute-start.29) | collective-permute-done | bytes 524320 | tf_op jit(solution)/shard_map/ppermute | solution.py:24
  65.2 0.7 shard_map.89
  65.9 0.5 fusion.2.refs_0_
  66.4 1.4 collective-permute-start.30
  67.9 0.9 collective-permute-start.31
  68.7 1.3 collective-permute-start.32
  70.2 1.3 shard_map.88
  71.4 0.7 collective-permute-done.20
  72.2 3.5 %collective-permute-done.30.refs_1_ = bf16[256,512]{1,0:T(8,128)(2,1)S(1)} collective-permute-done((bf16[256,512]{1,0:T(8,128)(2,1)S(1)}, bf16[256,512]{1,0:T(8,128)(2,1)S(1)}, u32[]{:S(2)}, u32[]{:S(2)}) %collective-permute-start.30) | collective-permute-done | bytes 262176 | tf_op jit(solution)/shard_map/ppermute | solution.py:24
  75.7 5.9 %collective-permute-done.31.refs_2_ = bf16[256,512]{1,0:T(8,128)(2,1)S(1)} collective-permute-done((bf16[256,512]{1,0:T(8,128)(2,1)S(1)}, bf16[256,512]{1,0:T(8,128)(2,1)S(1)}, u32[]{:S(2)}, u32[]{:S(2)}) %collective-permute-start.31) | collective-permute-done | bytes 262176 | tf_op jit(solution)/shard_map/ppermute | solution.py:24
  81.6 0.5 collective-permute-start.36
  82.2 1.3 collective-permute-start.21
  83.5 1.8 %shard_map.91 = (bf16[128,1024]{1,0:T(8,128)(2,1)S(1)}, bf16[128,1024]{1,0:T(8,128)(2,1)S(1)}) custom-call(s32[2]{0:T(128)S(1)} %pad_add_fusion.here, bf16[256,512]{1,0:T(8,128)(2,1)S(1)} %fusion.2.refs_0_, bf16[256,512]{1,0:T(8,128)(2,1)S(1)} %collective-permute-done.30.refs_1_, bf16[256,512]{1,0:T(8,128)(2,1)S(1)} %collective-permute-done.31.refs_2_, ...), custom_call_target="tpu_custom_call" | custom-call | flops 1073741824 | bytes 6815744 | tf_op jit(solution)/shard_map/pallas_call | solution.py:131
  85.3 0.5 collective-permute-start.37
  85.8 10.9 %collective-permute-done.21 = bf16[128,1024]{1,0:T(8,128)(2,1)S(1)} collective-permute-done((bf16[128,1024]{1,0:T(8,128)(2,1)S(1)}, bf16[128,1024]{1,0:T(8,128)(2,1)S(1)}, u32[]{:S(2)}, u32[]{:S(2)}) %collective-permute-start.21) | collective-permute-done | bytes 262176 | tf_op jit(solution)/shard_map/ppermute | solution.py:24
  97.2 2.0 %collective-permute-start.39 = (bf16[128,1024]{1,0:T(8,128)(2,1)S(1)}, bf16[128,1024]{1,0:T(8,128)(2,1)S(1)}, u32[]{:S(2)}, u32[]{:S(2)}) collective-permute-start(bf16[128,1024]{1,0:T(8,128)(2,1)S(1)} %get-tuple-element.73), channel_id=1, source_target_pairs={{0,8},{8,0},{16,24},{24,16},{1,9},{9,1},{17,25},{25,17},{2,10},{10... | collective-permute-start | bytes 786440 | tf_op jit(solution)/shard_map/ppermute | solution.py:24
  99.3 1.8 %shard_map.90 = (f32[128,1024]{1,0:T(8,128)S(1)}, f32[128,1024]{1,0:T(8,128)S(1)}) custom-call(s32[2]{0:T(128)S(1)} %pad_add_fusion.here, bf16[256,512]{1,0:T(8,128)(2,1)S(1)} %fusion.2.refs_0_, bf16[256,512]{1,0:T(8,128)(2,1)S(1)} %collective-permute-done.30.refs_1_, bf16[256,512]{1,0:T(8,128)(2,1)S(1)} %collective-permute-done.31.refs_2_, ...), custom_call_target="tpu_custom_call" | custom-call | flops 1073741824 | bytes 7340032 | tf_op jit(solution)/shard_map/pallas_call | solution.py:131
  101.1 0.9 collective-permute-start.38
  102.1 2.0 %collective-permute-start.40 = (bf16[128,1024]{1,0:T(8,128)(2,1)S(1)}, bf16[128,1024]{1,0:T(8,128)(2,1)S(1)}, u32[]{:S(2)}, u32[]{:S(2)}) collective-permute-start(bf16[128,1024]{1,0:T(8,128)(2,1)S(1)} %get-tuple-element.70), channel_id=1, source_target_pairs={{0,8},{8,0},{16,24},{24,16},{1,9},{9,1},{17,25},{25,17},{2,10},{10... | collective-permute-start | bytes 786440 | tf_op jit(solution)/shard_map/ppermute | solution.py:24
  104.1 7.7 %collective-permute-done.22 = bf16[128,1024]{1,0:T(8,128)(2,1)} collective-permute-done((bf16[128,1024]{1,0:T(8,128)(2,1)S(1)}, bf16[128,1024]{1,0:T(8,128)(2,1)}, u32[]{:S(2)}, u32[]{:S(2)}) %collective-permute-start.22) | collective-permute-done | bytes 262176 | tf_op jit(solution)/shard_map/ppermute | solution.py:24
  112.2 9.1 %collective-permute-done.38 = bf16[128,1024]{1,0:T(8,128)(2,1)S(1)} collective-permute-done((bf16[128,1024]{1,0:T(8,128)(2,1)S(1)}, bf16[128,1024]{1,0:T(8,128)(2,1)S(1)}, u32[]{:S(2)}, u32[]{:S(2)}) %collective-permute-start.38) | collective-permute-done | bytes 262176 | tf_op jit(solution)/shard_map/ppermute | solution.py:24
  121.3 1.1 collective-permute-done.40
  122.3 1.5 fusion.28
  123.8 2.2 %collective-permute-start.23 = (bf16[128,1024]{1,0:T(8,128)(2,1)}, bf16[128,1024]{1,0:T(8,128)(2,1)}, u32[]{:S(2)}, u32[]{:S(2)}) collective-permute-start(bf16[128,1024]{1,0:T(8,128)(2,1)} %collective-permute-done.22), channel_id=1, source_target_pairs={{0,8},{8,0},{16,24},{24,16},{1,9},{9,1},{17,25},{25,17},{2,10},{10... | collective-permute-start | bytes 786440 | tf_op jit(solution)/shard_map/ppermute | solution.py:24
  126.0 12.1 %collective-permute-done.41 = bf16[128,1024]{1,0:T(8,128)(2,1)} collective-permute-done((bf16[128,1024]{1,0:T(8,128)(2,1)}, bf16[128,1024]{1,0:T(8,128)(2,1)}, u32[]{:S(2)}, u32[]{:S(2)}) %collective-permute-start.41) | collective-permute-done | bytes 262176 | tf_op jit(solution)/shard_map/ppermute | solution.py:24
  138.0 0.9 collective-permute-done.23
  139.0 1.6 %fusion = bf16[1,256,1024]{2,1,0:T(8,128)(2,1)S(1)} fusion(bf16[128,1024]{1,0:T(8,128)(2,1)S(1)} %get-tuple-element.73, bf16[128,1024]{1,0:T(8,128)(2,1)} %collective-permute-done.22, bf16[128,1024]{1,0:T(8,128)(2,1)} %copy-done.8, bf16[128,1024]{1,0:T(8,128)(2,1)} %collective-permute-done.23, bf16[512,1024]{1,0:T(8,128)(2,1)S(1)} %shard_map.86.refs_6_.projector, ...), kind=kOutput, calls=%fused_computation.2 | convolution fusion | flops 272891904 | bytes 1835012 | tf_op jit(solution)/shard_map/dot_general | solution.py:377
  140.6 1.5 pad_maximum_fusion.1
  142.1 2.4 %collective-permute-done.43 = bf16[128,1024]{1,0:T(8,128)(2,1)S(1)} collective-permute-done((bf16[128,1024]{1,0:T(8,128)(2,1)}, bf16[128,1024]{1,0:T(8,128)(2,1)S(1)}, u32[]{:S(2)}, u32[]{:S(2)}) %collective-permute-start.43) | collective-permute-done | bytes 262176 | tf_op jit(solution)/shard_map/ppermute | solution.py:24
  144.5 4.0 %collective-permute-done.42 = bf16[128,1024]{1,0:T(8,128)(2,1)S(1)} collective-permute-done((bf16[128,1024]{1,0:T(8,128)(2,1)}, bf16[128,1024]{1,0:T(8,128)(2,1)S(1)}, u32[]{:S(2)}, u32[]{:S(2)}) %collective-permute-start.42) | collective-permute-done | bytes 262176 | tf_op jit(solution)/shard_map/ppermute | solution.py:24
  148.5 1.5 %fusion.1 = bf16[1,256,1024]{2,1,0:T(8,128)(2,1)S(1)} fusion(bf16[128,1024]{1,0:T(8,128)(2,1)} %get-tuple-element.77, bf16[128,1024]{1,0:T(8,128)(2,1)} %collective-permute-done.41, bf16[128,1024]{1,0:T(8,128)(2,1)S(1)} %collective-permute-done.43, bf16[128,1024]{1,0:T(8,128)(2,1)S(1)} %collective-permute-done.42, bf16[512,1024]{1,0:T(8,128)(2,1)S(1)} %shard_map.89, ...), kind=kOutput, calls=%fused_computation.3 | convolution fusion | flops 272891904 | bytes 1835012 | tf_op jit(solution)/shard_map/dot_general | solution.py:377
  150.0 1.1 pad_maximum_fusion
  (80 shorter events, 4.6 us)
Async XLA Ops:
  0.6 21.9 %copy-start.4 = (bf16[2,256,1024]{2,1,0:T(8,128)(2,1)S(1)}, bf16[2,256,1024]{2,1,0:T(8,128)(2,1)}, u32[]{:S(2)}) copy-start(bf16[2,256,1024]{2,1,0:T(8,128)(2,1)} %param.7) | copy-start | bytes 3145732
  1.7 10.0 %collective-permute-start = (bf16[64,1024]{1,0:T(8,128)(2,1)S(1)}, bf16[64,1024]{1,0:T(8,128)(2,1)S(1)}, u32[]{:S(2)}, u32[]{:S(2)}) collective-permute-start(bf16[64,1024]{1,0:T(8,128)(2,1)S(1)} %get-tuple-element.81), channel_id=1, source_target_pairs={{0,8},{8,0},{16,24},{24,16},{1,9},{9,1},{17,25},{25,17},{2,10},{10... | collective-permute-start | bytes 393224 | tf_op jit(solution)/shard_map/ppermute | solution.py:24
  6.7 8.0 %collective-permute-start.1 = (bf16[128,1024]{1,0:T(8,128)(2,1)}, bf16[128,1024]{1,0:T(8,128)(2,1)S(1)}, u32[]{:S(2)}, u32[]{:S(2)}) collective-permute-start(bf16[128,1024]{1,0:T(8,128)(2,1)} %get-tuple-element.40), channel_id=1, source_target_pairs={{0,2},{1,3},{2,0},{3,1},{4,6},{5,7},{6,4},{7,5},{8,10},{9,11},{10,... | collective-permute-start | bytes 786440 | tf_op jit(solution)/shard_map/ppermute | solution.py:24
  8.2 7.7 %collective-permute-start.2 = (bf16[128,1024]{1,0:T(8,128)(2,1)}, bf16[128,1024]{1,0:T(8,128)(2,1)S(1)}, u32[]{:S(2)}, u32[]{:S(2)}) collective-permute-start(bf16[128,1024]{1,0:T(8,128)(2,1)} %get-tuple-element.39), channel_id=1, source_target_pairs={{0,4},{1,5},{2,6},{3,7},{4,0},{5,1},{6,2},{7,3},{8,12},{9,13},{10,... | collective-permute-start | bytes 786440 | tf_op jit(solution)/shard_map/ppermute | solution.py:24
  15.9 7.4 %collective-permute-start.3 = (bf16[64,1024]{1,0:T(8,128)(2,1)S(1)}, bf16[64,1024]{1,0:T(8,128)(2,1)S(1)}, u32[]{:S(2)}, u32[]{:S(2)}) collective-permute-start(bf16[64,1024]{1,0:T(8,128)(2,1)S(1)} %broadcast_select_fusion.2), channel_id=1, source_target_pairs={{0,16},{8,24},{16,0},{24,8},{1,17},{9,25},{17,1},{25,9},{2,18},{10... | collective-permute-start | bytes 393224 | tf_op jit(solution)/shard_map/ppermute | solution.py:24
  18.4 9.3 %collective-permute-start.4 = (bf16[128,1024]{1,0:T(8,128)(2,1)}, bf16[128,1024]{1,0:T(8,128)(2,1)S(1)}, u32[]{:S(2)}, u32[]{:S(2)}) collective-permute-start(bf16[128,1024]{1,0:T(8,128)(2,1)} %get-tuple-element.39), channel_id=1, source_target_pairs={{0,2},{1,3},{2,0},{3,1},{4,6},{5,7},{6,4},{7,5},{8,10},{9,11},{10,... | collective-permute-start | bytes 786440 | tf_op jit(solution)/shard_map/ppermute | solution.py:24
  19.0 9.2 %collective-permute-start.5 = (bf16[128,1024]{1,0:T(8,128)(2,1)}, bf16[128,1024]{1,0:T(8,128)(2,1)S(1)}, u32[]{:S(2)}, u32[]{:S(2)}) collective-permute-start(bf16[128,1024]{1,0:T(8,128)(2,1)} %get-tuple-element.40), channel_id=1, source_target_pairs={{0,4},{1,5},{2,6},{3,7},{4,0},{5,1},{6,2},{7,3},{8,12},{9,13},{10,... | collective-permute-start | bytes 786440 | tf_op jit(solution)/shard_map/ppermute | solution.py:24
  20.5 10.4 %collective-permute-start.6 = (bf16[128,1024]{1,0:T(8,128)(2,1)S(1)}, bf16[128,1024]{1,0:T(8,128)(2,1)S(1)}, u32[]{:S(2)}, u32[]{:S(2)}) collective-permute-start(bf16[128,1024]{1,0:T(8,128)(2,1)S(1)} %collective-permute-done.1.refs_1_), channel_id=1, source_target_pairs={{0,4},{1,5},{2,6},{3,7},{4,0},{5,1},{6,2},{7,3},{8,12},{9,13},{10,... | collective-permute-start | bytes 786440 | tf_op jit(solution)/shard_map/ppermute | solution.py:24
  21.0 9.9 %collective-permute-start.7 = (bf16[128,1024]{1,0:T(8,128)(2,1)S(1)}, bf16[128,1024]{1,0:T(8,128)(2,1)S(1)}, u32[]{:S(2)}, u32[]{:S(2)}) collective-permute-start(bf16[128,1024]{1,0:T(8,128)(2,1)S(1)} %collective-permute-done.2.refs_4_), channel_id=1, source_target_pairs={{0,2},{1,3},{2,0},{3,1},{4,6},{5,7},{6,4},{7,5},{8,10},{9,11},{10,... | collective-permute-start | bytes 786440 | tf_op jit(solution)/shard_map/ppermute | solution.py:24
  23.3 16.2 %collective-permute-start.11 = (bf16[256,1024]{1,0:T(8,128)(2,1)S(1)}, bf16[256,1024]{1,0:T(8,128)(2,1)S(1)}, u32[]{:S(2)}, u32[]{:S(2)}) collective-permute-start(bf16[256,1024]{1,0:T(8,128)(2,1)S(1)} %slice_bitcast_fusion.refs_0_), channel_id=1, source_target_pairs={{0,1},{1,0},{2,3},{3,2},{4,5},{5,4},{6,7},{7,6},{8,9},{9,8},{10,11... | collective-permute-start | bytes 1572872 | tf_op jit(solution)/shard_map/ppermute | solution.py:24
  27.7 8.1 %collective-permute-start.24 = (bf16[64,1024]{1,0:T(8,128)(2,1)S(1)}, bf16[64,1024]{1,0:T(8,128)(2,1)S(1)}, u32[]{:S(2)}, u32[]{:S(2)}) collective-permute-start(bf16[64,1024]{1,0:T(8,128)(2,1)S(1)} %get-tuple-element.57), channel_id=1, source_target_pairs={{0,8},{8,0},{16,24},{24,16},{1,9},{9,1},{17,25},{25,17},{2,10},{10... | collective-permute-start | bytes 393224 | tf_op jit(solution)/shard_map/ppermute | solution.py:24
  30.9 5.9 %collective-permute-start.10 = (bf16[64,1024]{1,0:T(8,128)(2,1)S(1)}, bf16[64,1024]{1,0:T(8,128)(2,1)S(1)}, u32[]{:S(2)}, u32[]{:S(2)}) collective-permute-start(bf16[64,1024]{1,0:T(8,128)(2,1)S(1)} %broadcast_select_fusion.3), channel_id=1, source_target_pairs={{0,6},{1,7},{2,4},{3,5},{4,2},{5,3},{6,0},{7,1},{8,14},{9,15},{10,... | collective-permute-start | bytes 393224 | tf_op jit(solution)/shard_map/ppermute | solution.py:24
  33.3 5.0 %collective-permute-start.8 = (bf16[64,1024]{1,0:T(8,128)(2,1)S(1)}, bf16[64,1024]{1,0:T(8,128)(2,1)S(1)}, u32[]{:S(2)}, u32[]{:S(2)}) collective-permute-start(bf16[64,1024]{1,0:T(8,128)(2,1)S(1)} %broadcast_select_fusion.3), channel_id=1, source_target_pairs={{0,2},{1,3},{2,0},{3,1},{4,6},{5,7},{6,4},{7,5},{8,10},{9,11},{10,... | collective-permute-start | bytes 393224 | tf_op jit(solution)/shard_map/ppermute | solution.py:24
  34.0 5.0 %collective-permute-start.9 = (bf16[64,1024]{1,0:T(8,128)(2,1)S(1)}, bf16[64,1024]{1,0:T(8,128)(2,1)S(1)}, u32[]{:S(2)}, u32[]{:S(2)}) collective-permute-start(bf16[64,1024]{1,0:T(8,128)(2,1)S(1)} %broadcast_select_fusion.3), channel_id=1, source_target_pairs={{0,4},{1,5},{2,6},{3,7},{4,0},{5,1},{6,2},{7,3},{8,12},{9,13},{10,... | collective-permute-start | bytes 393224 | tf_op jit(solution)/shard_map/ppermute | solution.py:24
  35.9 3.2 %collective-permute-start.12 = (bf16[128,1024]{1,0:T(8,128)(2,1)S(1)}, bf16[128,1024]{1,0:T(8,128)(2,1)S(1)}, u32[]{:S(2)}, u32[]{:S(2)}) collective-permute-start(bf16[128,1024]{1,0:T(8,128)(2,1)S(1)} %collective-permute-done.1.refs_1_), channel_id=1, source_target_pairs={{0,1},{1,0},{2,3},{3,2},{4,5},{5,4},{6,7},{7,6},{8,9},{9,8},{10,11... | collective-permute-start | bytes 786440 | tf_op jit(solution)/shard_map/ppermute | solution.py:24
  36.9 2.6 %collective-permute-start.15 = (bf16[128,1024]{1,0:T(8,128)(2,1)S(1)}, bf16[128,1024]{1,0:T(8,128)(2,1)S(1)}, u32[]{:S(2)}, u32[]{:S(2)}) collective-permute-start(bf16[128,1024]{1,0:T(8,128)(2,1)S(1)} %collective-permute-done.2.refs_4_), channel_id=1, source_target_pairs={{0,1},{1,0},{2,3},{3,2},{4,5},{5,4},{6,7},{7,6},{8,9},{9,8},{10,11... | collective-permute-start | bytes 786440 | tf_op jit(solution)/shard_map/ppermute | solution.py:24
  38.3 1.5 %collective-permute-start.13 = (bf16[128,1024]{1,0:T(8,128)(2,1)S(1)}, bf16[128,1024]{1,0:T(8,128)(2,1)S(1)}, u32[]{:S(2)}, u32[]{:S(2)}) collective-permute-start(bf16[128,1024]{1,0:T(8,128)(2,1)S(1)} %collective-permute-done.4.refs_2_), channel_id=1, source_target_pairs={{0,1},{1,0},{2,3},{3,2},{4,5},{5,4},{6,7},{7,6},{8,9},{9,8},{10,11... | collective-permute-start | bytes 786440 | tf_op jit(solution)/shard_map/ppermute | solution.py:24
  38.9 1.5 %collective-permute-start.14 = (bf16[128,1024]{1,0:T(8,128)(2,1)S(1)}, bf16[128,1024]{1,0:T(8,128)(2,1)S(1)}, u32[]{:S(2)}, u32[]{:S(2)}) collective-permute-start(bf16[128,1024]{1,0:T(8,128)(2,1)S(1)} %collective-permute-done.5.refs_3_), channel_id=1, source_target_pairs={{0,1},{1,0},{2,3},{3,2},{4,5},{5,4},{6,7},{7,6},{8,9},{9,8},{10,11... | collective-permute-start | bytes 786440 | tf_op jit(solution)/shard_map/ppermute | solution.py:24
  39.0 9.6 %collective-permute-start.25 = (bf16[64,1024]{1,0:T(8,128)(2,1)S(1)}, bf16[64,1024]{1,0:T(8,128)(2,1)S(1)}, u32[]{:S(2)}, u32[]{:S(2)}) collective-permute-start(bf16[64,1024]{1,0:T(8,128)(2,1)S(1)} %broadcast_select_fusion), channel_id=1, source_target_pairs={{0,16},{8,24},{16,0},{24,8},{1,17},{9,25},{17,1},{25,9},{2,18},{10... | collective-permute-start | bytes 393224 | tf_op jit(solution)/shard_map/ppermute | solution.py:24
  40.5 2.2 %copy-start = (bf16[2048,1024]{1,0:T(8,128)(2,1)S(1)}, bf16[2048,1024]{1,0:T(8,128)(2,1)}, u32[]{:S(2)}) copy-start(bf16[2048,1024]{1,0:T(8,128)(2,1)} %refs_8_.3) | copy-start | bytes 12582916
  42.7 18.1 %copy-start.1 = (bf16[2048,1024]{1,0:T(8,128)(2,1)S(1)}, bf16[2048,1024]{1,0:T(8,128)(2,1)}, u32[]{:S(2)}) copy-start(bf16[2048,1024]{1,0:T(8,128)(2,1)} %refs_8_.3) | copy-start | bytes 12582916
  47.8 12.3 %collective-permute-start.16 = (bf16[256,1024]{1,0:T(8,128)(2,1)S(1)}, bf16[256,1024]{1,0:T(8,128)(2,1)S(1)}, u32[]{:S(2)}, u32[]{:S(2)}) collective-permute-start(bf16[256,1024]{1,0:T(8,128)(2,1)S(1)} %pad_maximum_fusion.3.same), channel_id=1, source_target_pairs={{0,1},{1,0},{2,3},{3,2},{4,5},{5,4},{6,7},{7,6},{8,9},{9,8},{10,11... | collective-permute-start | bytes 1572872 | tf_op jit(solution)/shard_map/ppermute | solution.py:24
  48.6 5.5 %collective-permute-start.26 = (bf16[64,1024]{1,0:T(8,128)(2,1)S(1)}, bf16[64,1024]{1,0:T(8,128)(2,1)S(1)}, u32[]{:S(2)}, u32[]{:S(2)}) collective-permute-start(bf16[64,1024]{1,0:T(8,128)(2,1)S(1)} %broadcast_select_fusion.1), channel_id=1, source_target_pairs={{0,2},{1,3},{2,0},{3,1},{4,6},{5,7},{6,4},{7,5},{8,10},{9,11},{10,... | collective-permute-start | bytes 393224 | tf_op jit(solution)/shard_map/ppermute | solution.py:24
  50.1 10.7 %collective-permute-start.17 = (bf16[128,1024]{1,0:T(8,128)(2,1)S(1)}, bf16[128,1024]{1,0:T(8,128)(2,1)S(1)}, u32[]{:S(2)}, u32[]{:S(2)}) collective-permute-start(bf16[128,1024]{1,0:T(8,128)(2,1)S(1)} %collective-permute-done.6.refs_0_), channel_id=1, source_target_pairs={{0,1},{1,0},{2,3},{3,2},{4,5},{5,4},{6,7},{7,6},{8,9},{9,8},{10,11... | collective-permute-start | bytes 786440 | tf_op jit(solution)/shard_map/ppermute | solution.py:24
  50.1 10.7 %collective-permute-start.18 = (bf16[128,1024]{1,0:T(8,128)(2,1)S(1)}, bf16[128,1024]{1,0:T(8,128)(2,1)S(1)}, u32[]{:S(2)}, u32[]{:S(2)}) collective-permute-start(bf16[128,1024]{1,0:T(8,128)(2,1)S(1)} %collective-permute-done.7.refs_1_), channel_id=1, source_target_pairs={{0,1},{1,0},{2,3},{3,2},{4,5},{5,4},{6,7},{7,6},{8,9},{9,8},{10,11... | collective-permute-start | bytes 786440 | tf_op jit(solution)/shard_map/ppermute | solution.py:24
  50.6 5.4 %collective-permute-start.27 = (bf16[64,1024]{1,0:T(8,128)(2,1)S(1)}, bf16[64,1024]{1,0:T(8,128)(2,1)S(1)}, u32[]{:S(2)}, u32[]{:S(2)}) collective-permute-start(bf16[64,1024]{1,0:T(8,128)(2,1)S(1)} %broadcast_select_fusion.1), channel_id=1, source_target_pairs={{0,4},{1,5},{2,6},{3,7},{4,0},{5,1},{6,2},{7,3},{8,12},{9,13},{10,... | collective-permute-start | bytes 393224 | tf_op jit(solution)/shard_map/ppermute | solution.py:24
  54.2 5.9 %collective-permute-start.28 = (bf16[64,1024]{1,0:T(8,128)(2,1)S(1)}, bf16[64,1024]{1,0:T(8,128)(2,1)S(1)}, u32[]{:S(2)}, u32[]{:S(2)}) collective-permute-start(bf16[64,1024]{1,0:T(8,128)(2,1)S(1)} %broadcast_select_fusion.1), channel_id=1, source_target_pairs={{0,6},{1,7},{2,4},{3,5},{4,2},{5,3},{6,0},{7,1},{8,14},{9,15},{10,... | collective-permute-start | bytes 393224 | tf_op jit(solution)/shard_map/ppermute | solution.py:24
  63.2 2.7 %copy-start.5 = (bf16[2,256,1024]{2,1,0:T(8,128)(2,1)S(1)}, bf16[2,256,1024]{2,1,0:T(8,128)(2,1)}, u32[]{:S(2)}) copy-start(bf16[2,256,1024]{2,1,0:T(8,128)(2,1)} %param.7) | copy-start | bytes 3145732
  63.2 2.0 %collective-permute-start.29 = (bf16[256,1024]{1,0:T(8,128)(2,1)S(1)}, bf16[256,1024]{1,0:T(8,128)(2,1)S(1)}, u32[]{:S(2)}, u32[]{:S(2)}) collective-permute-start(bf16[256,1024]{1,0:T(8,128)(2,1)S(1)} %pad_maximum_fusion.4.same), channel_id=1, source_target_pairs={{0,1},{1,0},{2,3},{3,2},{4,5},{5,4},{6,7},{7,6},{8,9},{9,8},{10,11... | collective-permute-start | bytes 1572872 | tf_op jit(solution)/shard_map/ppermute | solution.py:24
  63.3 8.8 %collective-permute-start.20 = (bf16[128,1024]{1,0:T(8,128)(2,1)S(1)}, bf16[128,1024]{1,0:T(8,128)(2,1)S(1)}, u32[]{:S(2)}, u32[]{:S(2)}) collective-permute-start(bf16[128,1024]{1,0:T(8,128)(2,1)S(1)} %get-tuple-element.56), channel_id=1, source_target_pairs={{0,8},{8,0},{16,24},{24,16},{1,9},{9,1},{17,25},{25,17},{2,10},{10... | collective-permute-start | bytes 786440 | tf_op jit(solution)/shard_map/ppermute | solution.py:24
  66.4 9.2 %collective-permute-start.30 = (bf16[256,512]{1,0:T(8,128)(2,1)S(1)}, bf16[256,512]{1,0:T(8,128)(2,1)S(1)}, u32[]{:S(2)}, u32[]{:S(2)}) collective-permute-start(bf16[256,512]{1,0:T(8,128)(2,1)S(1)} %fusion.2.refs_0_), channel_id=1, source_target_pairs={{0,2},{1,3},{2,0},{3,1},{4,6},{5,7},{6,4},{7,5},{8,10},{9,11},{10,... | collective-permute-start | bytes 786440 | tf_op jit(solution)/shard_map/ppermute | solution.py:24
  67.9 13.7 %collective-permute-start.31 = (bf16[256,512]{1,0:T(8,128)(2,1)S(1)}, bf16[256,512]{1,0:T(8,128)(2,1)S(1)}, u32[]{:S(2)}, u32[]{:S(2)}) collective-permute-start(bf16[256,512]{1,0:T(8,128)(2,1)S(1)} %fusion.2.refs_0_), channel_id=1, source_target_pairs={{0,4},{1,5},{2,6},{3,7},{4,0},{5,1},{6,2},{7,3},{8,12},{9,13},{10,... | collective-permute-start | bytes 786440 | tf_op jit(solution)/shard_map/ppermute | solution.py:24
  68.7 12.8 %collective-permute-start.32 = (bf16[256,512]{1,0:T(8,128)(2,1)S(1)}, bf16[256,512]{1,0:T(8,128)(2,1)S(1)}, u32[]{:S(2)}, u32[]{:S(2)}) collective-permute-start(bf16[256,512]{1,0:T(8,128)(2,1)S(1)} %fusion.2.refs_0_), channel_id=1, source_target_pairs={{0,6},{1,7},{2,4},{3,5},{4,2},{5,3},{6,0},{7,1},{8,14},{9,15},{10,... | collective-permute-start | bytes 786440 | tf_op jit(solution)/shard_map/ppermute | solution.py:24
  70.0 12.2 %collective-permute-start.19 = (bf16[128,1024]{1,0:T(8,128)(2,1)S(1)}, bf16[128,1024]{1,0:T(8,128)(2,1)S(1)}, u32[]{:S(2)}, u32[]{:S(2)}) collective-permute-start(bf16[128,1024]{1,0:T(8,128)(2,1)S(1)} %get-tuple-element.54), channel_id=1, source_target_pairs={{0,8},{8,0},{16,24},{24,16},{1,9},{9,1},{17,25},{25,17},{2,10},{10... | collective-permute-start | bytes 786440 | tf_op jit(solution)/shard_map/ppermute | solution.py:24
  72.2 11.3 %collective-permute-start.33 = (bf16[256,512]{1,0:T(8,128)(2,1)S(1)}, bf16[256,512]{1,0:T(8,128)(2,1)S(1)}, u32[]{:S(2)}, u32[]{:S(2)}) collective-permute-start(bf16[256,512]{1,0:T(8,128)(2,1)S(1)} %fusion.2.refs_0_), channel_id=1, source_target_pairs={{0,1},{1,0},{2,3},{3,2},{4,5},{5,4},{6,7},{7,6},{8,9},{9,8},{10,11... | collective-permute-start | bytes 786440 | tf_op jit(solution)/shard_map/ppermute | solution.py:24
  75.7 7.8 %collective-permute-start.34 = (bf16[256,512]{1,0:T(8,128)(2,1)S(1)}, bf16[256,512]{1,0:T(8,128)(2,1)S(1)}, u32[]{:S(2)}, u32[]{:S(2)}) collective-permute-start(bf16[256,512]{1,0:T(8,128)(2,1)S(1)} %collective-permute-done.30.refs_1_), channel_id=1, source_target_pairs={{0,1},{1,0},{2,3},{3,2},{4,5},{5,4},{6,7},{7,6},{8,9},{9,8},{10,11... | collective-permute-start | bytes 786440 | tf_op jit(solution)/shard_map/ppermute | solution.py:24
  81.5 1.9 %collective-permute-start.35 = (bf16[256,512]{1,0:T(8,128)(2,1)S(1)}, bf16[256,512]{1,0:T(8,128)(2,1)S(1)}, u32[]{:S(2)}, u32[]{:S(2)}) collective-permute-start(bf16[256,512]{1,0:T(8,128)(2,1)S(1)} %collective-permute-done.31.refs_2_), channel_id=1, source_target_pairs={{0,1},{1,0},{2,3},{3,2},{4,5},{5,4},{6,7},{7,6},{8,9},{9,8},{10,11... | collective-permute-start | bytes 786440 | tf_op jit(solution)/shard_map/ppermute | solution.py:24
  81.6 1.9 %collective-permute-start.36 = (bf16[256,512]{1,0:T(8,128)(2,1)S(1)}, bf16[256,512]{1,0:T(8,128)(2,1)S(1)}, u32[]{:S(2)}, u32[]{:S(2)}) collective-permute-start(bf16[256,512]{1,0:T(8,128)(2,1)S(1)} %collective-permute-done.32.refs_3_), channel_id=1, source_target_pairs={{0,1},{1,0},{2,3},{3,2},{4,5},{5,4},{6,7},{7,6},{8,9},{9,8},{10,11... | collective-permute-start | bytes 786440 | tf_op jit(solution)/shard_map/ppermute | solution.py:24
  82.1 14.6 %copy-start.6 = (f32[2,128,1024]{2,1,0:T(8,128)S(1)}, f32[2,128,1024]{2,1,0:T(8,128)}, u32[]{:S(2)}) copy-start(f32[2,128,1024]{2,1,0:T(8,128)} %param.10) | copy-start | bytes 3145732
  82.1 14.6 %copy-start.7 = (f32[2,128,1024]{2,1,0:T(8,128)S(1)}, f32[2,128,1024]{2,1,0:T(8,128)}, u32[]{:S(2)}) copy-start(f32[2,128,1024]{2,1,0:T(8,128)} %param.9) | copy-start | bytes 3145732
  82.2 14.6 %collective-permute-start.21 = (bf16[128,1024]{1,0:T(8,128)(2,1)S(1)}, bf16[128,1024]{1,0:T(8,128)(2,1)S(1)}, u32[]{:S(2)}, u32[]{:S(2)}) collective-permute-start(bf16[128,1024]{1,0:T(8,128)(2,1)S(1)} %add_convert_fusion.1), channel_id=1, source_target_pairs={{0,16},{8,24},{16,0},{24,8},{1,17},{9,25},{17,1},{25,9},{2,18},{10... | collective-permute-start | bytes 786440 | tf_op jit(solution)/shard_map/ppermute | solution.py:24
  85.3 15.7 %collective-permute-start.37 = (bf16[128,1024]{1,0:T(8,128)(2,1)S(1)}, bf16[128,1024]{1,0:T(8,128)(2,1)S(1)}, u32[]{:S(2)}, u32[]{:S(2)}) collective-permute-start(bf16[128,1024]{1,0:T(8,128)(2,1)S(1)} %get-tuple-element.66), channel_id=1, source_target_pairs={{0,8},{8,0},{16,24},{24,16},{1,9},{9,1},{17,25},{25,17},{2,10},{10... | collective-permute-start | bytes 786440 | tf_op jit(solution)/shard_map/ppermute | solution.py:24
  97.1 14.6 %collective-permute-start.22 = (bf16[128,1024]{1,0:T(8,128)(2,1)S(1)}, bf16[128,1024]{1,0:T(8,128)(2,1)}, u32[]{:S(2)}, u32[]{:S(2)}) collective-permute-start(bf16[128,1024]{1,0:T(8,128)(2,1)S(1)} %get-tuple-element.73), channel_id=1, source_target_pairs={{0,16},{8,24},{16,0},{24,8},{1,17},{9,25},{17,1},{25,9},{2,18},{10... | collective-permute-start | bytes 786440 | tf_op jit(solution)/shard_map/ppermute | solution.py:24
  97.2 14.9 %collective-permute-start.39 = (bf16[128,1024]{1,0:T(8,128)(2,1)S(1)}, bf16[128,1024]{1,0:T(8,128)(2,1)S(1)}, u32[]{:S(2)}, u32[]{:S(2)}) collective-permute-start(bf16[128,1024]{1,0:T(8,128)(2,1)S(1)} %get-tuple-element.73), channel_id=1, source_target_pairs={{0,8},{8,0},{16,24},{24,16},{1,9},{9,1},{17,25},{25,17},{2,10},{10... | collective-permute-start | bytes 786440 | tf_op jit(solution)/shard_map/ppermute | solution.py:24
  101.1 20.1 %collective-permute-start.38 = (bf16[128,1024]{1,0:T(8,128)(2,1)S(1)}, bf16[128,1024]{1,0:T(8,128)(2,1)S(1)}, u32[]{:S(2)}, u32[]{:S(2)}) collective-permute-start(bf16[128,1024]{1,0:T(8,128)(2,1)S(1)} %add_convert_fusion), channel_id=1, source_target_pairs={{0,16},{8,24},{16,0},{24,8},{1,17},{9,25},{17,1},{25,9},{2,18},{10... | collective-permute-start | bytes 786440 | tf_op jit(solution)/shard_map/ppermute | solution.py:24
  102.1 20.2 %collective-permute-start.40 = (bf16[128,1024]{1,0:T(8,128)(2,1)S(1)}, bf16[128,1024]{1,0:T(8,128)(2,1)S(1)}, u32[]{:S(2)}, u32[]{:S(2)}) collective-permute-start(bf16[128,1024]{1,0:T(8,128)(2,1)S(1)} %get-tuple-element.70), channel_id=1, source_target_pairs={{0,8},{8,0},{16,24},{24,16},{1,9},{9,1},{17,25},{25,17},{2,10},{10... | collective-permute-start | bytes 786440 | tf_op jit(solution)/shard_map/ppermute | solution.py:24
  112.2 11.6 %copy-start.8 = (bf16[128,1024]{1,0:T(8,128)(2,1)}, bf16[128,1024]{1,0:T(8,128)(2,1)S(1)}, u32[]{:S(2)}) copy-start(bf16[128,1024]{1,0:T(8,128)(2,1)S(1)} %collective-permute-done.39) | copy-start | bytes 786436
  123.8 14.3 %collective-permute-start.41 = (bf16[128,1024]{1,0:T(8,128)(2,1)}, bf16[128,1024]{1,0:T(8,128)(2,1)}, u32[]{:S(2)}, u32[]{:S(2)}) collective-permute-start(bf16[128,1024]{1,0:T(8,128)(2,1)} %get-tuple-element.77), channel_id=1, source_target_pairs={{0,16},{8,24},{16,0},{24,8},{1,17},{9,25},{17,1},{25,9},{2,18},{10... | collective-permute-start | bytes 786440 | tf_op jit(solution)/shard_map/ppermute | solution.py:24
  123.8 15.2 %collective-permute-start.23 = (bf16[128,1024]{1,0:T(8,128)(2,1)}, bf16[128,1024]{1,0:T(8,128)(2,1)}, u32[]{:S(2)}, u32[]{:S(2)}) collective-permute-start(bf16[128,1024]{1,0:T(8,128)(2,1)} %collective-permute-done.22), channel_id=1, source_target_pairs={{0,8},{8,0},{16,24},{24,16},{1,9},{9,1},{17,25},{25,17},{2,10},{10... | collective-permute-start | bytes 786440 | tf_op jit(solution)/shard_map/ppermute | solution.py:24
  125.9 14.6 %copy-start.2 = (f32[1,128,1024]{2,1,0:T(8,128)S(1)}, f32[1,128,1024]{2,1,0:T(8,128)}, u32[]{:S(2)}) copy-start(f32[1,128,1024]{2,1,0:T(8,128)} %get-tuple-element.76) | copy-start | bytes 1572868
  125.9 14.6 %copy-start.3 = (f32[1,128,1024]{2,1,0:T(8,128)S(1)}, f32[1,128,1024]{2,1,0:T(8,128)}, u32[]{:S(2)}) copy-start(f32[1,128,1024]{2,1,0:T(8,128)} %get-tuple-element.78) | copy-start | bytes 1572868
  125.9 18.5 %collective-permute-start.43 = (bf16[128,1024]{1,0:T(8,128)(2,1)}, bf16[128,1024]{1,0:T(8,128)(2,1)S(1)}, u32[]{:S(2)}, u32[]{:S(2)}) collective-permute-start(bf16[128,1024]{1,0:T(8,128)(2,1)} %get-tuple-element.77), channel_id=1, source_target_pairs={{0,8},{8,0},{16,24},{24,16},{1,9},{9,1},{17,25},{25,17},{2,10},{10... | collective-permute-start | bytes 786440 | tf_op jit(solution)/shard_map/ppermute | solution.py:24
  138.0 10.4 %collective-permute-start.42 = (bf16[128,1024]{1,0:T(8,128)(2,1)}, bf16[128,1024]{1,0:T(8,128)(2,1)S(1)}, u32[]{:S(2)}, u32[]{:S(2)}) collective-permute-start(bf16[128,1024]{1,0:T(8,128)(2,1)} %collective-permute-done.41), channel_id=1, source_target_pairs={{0,8},{8,0},{16,24},{24,16},{1,9},{9,1},{17,25},{25,17},{2,10},{10... | collective-permute-start | bytes 786440 | tf_op jit(solution)/shard_map/ppermute | solution.py:24

commit v5 on v4

--- a/solution.py
+++ b/solution.py
@@ -17,6 +17,8 @@
 
 TRANSPOSED = (((0,), (0,)), ((), ()))
 MIB = 1 << 20
+ORDER_HEADS = True
+COST = 0.0
 
 
 def swap(value, axis, mask):
@@ -80,21 +82,21 @@
 
 
 def gather_body(order, per, count, here, same, other, *refs):
-    out = refs[-1]
-    spot = 0
-    for mask in order:
-        for sub in range(per):
-            away = ((here[0] ^ mask) * per + sub) ^ here[1]
-            at = pl.multiple_of((away >> 1) * count, count)
-            out[pl.ds(spot * count, count), :] = jnp.where(
-                (away & 1) == 0, same[pl.ds(at, count), :], other[pl.ds(at, count), :]
-            )
-            spot += 1
+    for matrix, out in enumerate(refs[-MATS:]):
+        spot = 0
+        for mask in order:
+            for sub in range(per):
+                away = ((here[0] ^ mask) * per + sub) ^ here[1]
+                at = pl.multiple_of(((away >> 1) * MATS + matrix) * count, count)
+                out[pl.ds(spot * count, count), :] = jnp.where(
+                    (away & 1) == 0, same[pl.ds(at, count), :], other[pl.ds(at, count), :]
+                )
+                spot += 1
 
 
 def gather_projector(same, other, here, order, per, tokens):
     rows, kv = same.shape
-    rank = 2 * rows
+    rank = 2 * rows // MATS
     return pl.pallas_call(
         functools.partial(gather_body, order, per, rank // (len(order) * per)),
         grid_spec=pltpu.PrefetchScalarGridSpec(
@@ -102,10 +104,10 @@
             grid=(1,),
             in_specs=[whole((rows, kv))] * 2
             + [pl.BlockSpec(memory_space=pl.ANY)] * len(tokens),
-            out_specs=whole((rank, kv)),
+            out_specs=[whole((rank, kv))] * MATS,
         ),
-        out_shape=jax.ShapeDtypeStruct((rank, kv), same.dtype),
-        compiler_params=pltpu.CompilerParams(vmem_limit_bytes=12 * MIB),
+        out_shape=[jax.ShapeDtypeStruct((rank, kv), same.dtype)] * MATS,
+        compiler_params=pltpu.CompilerParams(vmem_limit_bytes=16 * MIB),
         cost_estimate=pl.CostEstimate(flops=0, bytes_accessed=8 * rows * kv, transcendentals=0),
     )(here, same, other, *tokens)
 
@@ -139,7 +141,7 @@
         out_shape=outputs,
         compiler_params=pltpu.CompilerParams(vmem_limit_bytes=20 * MIB),
         cost_estimate=pl.CostEstimate(
-            flops=int(flops), bytes_accessed=moved, transcendentals=0
+            flops=int(flops * COST), bytes_accessed=int(moved * COST), transcendentals=0
         ),
     )(here, *operands, *tokens)
 
@@ -296,67 +298,72 @@
 
     here = jnp.stack([me_dp, me_fsdp]).astype(jnp.int32)
 
-    def owned(matrix, value, others, tokens):
-        steps = []
+    def owned(value, others, tokens):
         for at, bit in enumerate(dp_bits):
             if at == 1 and others:
                 value = after(value, others, tokens)
             other = swap(value, "dp", bit)
-            mine = (me_dp & bit) == (owners[matrix] & bit)
-            value = jnp.where(mine, value, other)
-            steps.append(value)
-        return value, steps[0]
-
-    def same_core(value):
-        blocks = spread(value, far_bits)
-        return jnp.concatenate([blocks[mask] for mask in sorted(blocks)], axis=0)
-
-    def assembled(same, tokens):
-        return gather_projector(same, swap(same, "fsdp", 1), here, order, per, tokens)
+            mine = (me_dp & bit) == (owners & bit)
+            rows = jnp.repeat(mine, value.shape[0] // MATS)[:, None]
+            value = jnp.where(rows, value, other)
+        return value
 
     pieces = max(replicas // 2, 1)
     tokens, tokens_1 = [], []
 
     near, far, arrived = spread_near(cotangent[0], far_bits, tokens)
-    owned_0, step_0 = owned(0, candidates[0, 0].T, arrived, tokens)
+    both = jnp.swapaxes(candidates[:, 0], 1, 2).reshape(-1, candidates.shape[2])
+    both = owned(both, arrived, tokens)
     later = [piece for mask in far_bits for piece in near.get(mask, ())]
     later = [piece for piece in later if all(piece is not other for other in arrived)]
-    same_0 = same_core(after(owned_0, later + flat(far), tokens))
+    blocks = spread(after(both, later + flat(far), tokens), far_bits)
+    same = jnp.concatenate([blocks[mask] for mask in sorted(blocks)], axis=0)
     near_all = with_partner(near)
     partial = add_products(near_all, here, layer_input)
     far_all = with_partner(far)
-    projector_0 = assembled(after(same_0, [partial], tokens), tokens)
-    product, send_0 = project(far_all, here, layer_input, partial, projector_0, pieces, scale)
-    keep_0 = apply_rest(projector_0, product, here, pieces, scale)
-
-    owned_1, _ = owned(1, after(candidates[1, 0].T, [step_0], tokens_1), [owned_0], tokens_1)
-    same_1 = same_core(after(owned_1, [same_0], tokens_1))
-    projector_1 = assembled(after(same_1, send_0[:1], tokens_1), tokens_1)
+    same = after(same, [partial], tokens)
+    projectors = gather_projector(same, swap(same, "fsdp", 1), here, order, per, tokens)
+    product, send_0 = project(far_all, here, layer_input, partial, projectors[0], pieces, scale)
+    keep_0 = apply_rest(projectors[0], product, here, pieces, scale)
+    arrived_0 = [swap(piece, "dp", dp_bits[0]) for piece in send_0]
+
+    def forward(arrived, keeps):
+        totals = [keep + piece.astype(jnp.float32) for piece, keep in zip(arrived, keeps)]
+        half = len(totals) // 2
+        return [total.astype(jnp.bfloat16) for total in totals[:half]], totals[half:]
+
+    def reduced(arrived, keeps, sends=None):
+        for bit in dp_bits[1:]:
+            made, keeps = forward(arrived, keeps)
+            arrived = [swap(piece, "dp", bit) for piece in (sends or made)]
+            sends = None
+        return keeps[0], arrived[0]
+
     heads = lax.dot_general(
-        cotangent[1], projector_1, (((1,), (1,)), ((), ())), preferred_element_type=jnp.float32
+        cotangent[1], projectors[1], (((1,), (1,)), ((), ())), preferred_element_type=jnp.float32
     ).astype(jnp.bfloat16)
-    blocks = with_partner({mask: [held] for mask, held in spread(heads, far_bits).items()})
-    arrived_0 = [swap(piece, "dp", dp_bits[0]) for piece in send_0]
+    if ORDER_HEADS:
+        heads = after(heads, send_0[:1], tokens_1)
+    blocks = spread(heads, far_bits)
+    if len(dp_bits) > 1:
+        next_0, _ = forward(arrived_0, keep_0)
+        moved = [mask for mask in blocks if mask]
+        held = lax.optimization_barrier(tuple(blocks[mask] for mask in moved) + (next_0[0],))
+        blocks.update(zip(moved, held))
+        tokens_1.append(held[-1])
+    blocks = with_partner({mask: [held] for mask, held in blocks.items()})
     send_1 = heads_product(
-        blocks, here, layer_input, 0, pieces, jnp.bfloat16, scale, arrived_0[pieces // 2 :]
-    )
-    arrived_1 = [swap(piece, "dp", dp_bits[0]) for piece in send_1]
+        blocks, here, layer_input, 0, 1, jnp.bfloat16, scale, arrived_0[pieces // 2 :] + tokens_1
+    )
     keep_1 = heads_product(blocks, here, layer_input, 1, pieces, jnp.float32, scale)
-
-    def reduced(arrived, keeps):
-        for bit in dp_bits[1:]:
-            totals = [keep + piece.astype(jnp.float32) for piece, keep in zip(arrived, keeps)]
-            half = len(totals) // 2
-            arrived = [swap(total.astype(jnp.bfloat16), "dp", bit) for total in totals[:half]]
-            keeps = totals[half:]
-        return keeps[0], arrived[0]
+    arrived_1 = jnp.split(swap(send_1[0], "dp", dp_bits[0]), pieces)
 
     updates, firsts, seconds, gathered = [], [], [], []
     for matrix, arrived, keeps in ((0, arrived_0, keep_0), (1, arrived_1, keep_1)):
         keep, received = reduced(arrived, keeps)
         if gathered:
-            received, firsts[0], *gathered[0][-3:-1] = lax.optimization_barrier(
-                (received, firsts[0], *gathered[0][-3:-1])
+            received, firsts[0], *gathered[0][:-1] = lax.optimization_barrier(
+                (received, firsts[0], *gathered[0][:-1])
             )
         projected = keep + received.astype(jnp.float32)
         first = beta_first * moment_first[matrix] + (1.0 - beta_first) * projected
@@ -372,7 +379,7 @@
         gathered.append(parts)
         firsts.append(first)
         seconds.append(second)
-    for parts, projector in zip(gathered, (projector_0, projector_1)):
+    for parts, projector in zip(gathered, projectors):
         own = lax.dynamic_slice_in_dim(projector, me_dp * kv_share, kv_share, 1)
         update = lax.dot_general(
             own, jnp.concatenate(parts, axis=0), TRANSPOSED, preferred_element_type=jnp.float32

time: 151 us -> 141 us (0.934)
  starting transfers between devices: 35.5 us -> 30.5 us
  between operations: 3.71 us -> 0.96 us
  waiting for transfers between devices: 82.3 us -> 79.7 us
  local copies, waits for them, and re-layouts: 6.54 us -> 4.56 us
    ppermute x44 -> x37, starting transfers between devices: 35.5 us -> 30.5 us  [swap(): return lax.ppermute(value, axis, [(i, i ^ mask) for i in range(size)])]
    ppermute x44 -> x37, waiting for transfers between devices: 82.3 us -> 79.7 us  [swap(): return lax.ppermute(value, axis, [(i, i ^ mask) for i in range(size)])]
  transfers between devices with their start and end apart: 44 -> 37, of which waited for: 26 -> 16; matrix products, arithmetic and copies ran while one was open for 6% -> 5% of each run, Pallas kernels for 7% -> 8%
where the time goes in v5:
time: 141 us; the launch traced here: 140 us
  waiting for transfers between devices  79.7 us (57%)
  starting transfers between devices  30.5 us (22%)
  Pallas kernels  13.9 us (10%)
  other arithmetic  7.14 us (5%)
  local copies, waits for them, and re-layouts  4.56 us (3%)
  matrix products  3.65 us (3%)
    ppermute x37, waiting for transfers between devices, swap(): return lax.ppermute(value, axis, [(i, i ^ mask) for i in range(size)])  79.7 us
    ppermute x37, starting transfers between devices, swap(): return lax.ppermute(value, axis, [(i, i ^ mask) for i in range(size)])  30.5 us
    pallas_call x4, Pallas kernels, call_in_vmem(): pl.pallas_call(body, grid_spec=pltpu.PrefetchScalarGridSpec(num_scalar_pr...  7.35 us
    pallas_call x1, Pallas kernels, add_products(): pl.pallas_call(functools.partial(product_body, shape), grid_spec=pltpu.Pr...  5.8 us
    another operation x3, other arithmetic, on_device(): return (jnp.stack(updates), jnp.stack(firsts), jnp.stack(seconds))  3.64 us
    dot_general x2, matrix products, on_device(): lax.dot_general(own, jnp.concatenate(parts, axis=0), TRANSPOSED, preferre...  3.17 us
  transfers between devices with their start and end apart: 37, of which 16 were waited for; matrix products, arithmetic and copies ran while one was open for 5% of the time, Pallas kernels for 8%

profile of v5, /device:TPU:0, one launch (start us, length us, event | category | flops | bytes accessed | tf_op | source)
XLA Modules:
  0.0 140.4 jit_solution(2354872264291275614)
XLA Ops:
  0.6 1.9 %slice_bitcast_fusion.1 = (bf16[128,1024]{1,0:T(8,128)(2,1)}, bf16[128,1024]{1,0:T(8,128)(2,1)}) fusion(bf16[2,256,1024]{2,1,0:T(8,128)(2,1)} %param.7), kind=kLoop, calls=%fused_computation.41 | loop fusion | bytes 1048576 | tf_op jit(solution)/shard_map/slice | solution.py:55
  2.6 3.0 %collective-permute-start.2 = (bf16[128,1024]{1,0:T(8,128)(2,1)}, bf16[128,1024]{1,0:T(8,128)(2,1)S(1)}, u32[]{:S(2)}, u32[]{:S(2)}) collective-permute-start(bf16[128,1024]{1,0:T(8,128)(2,1)} %get-tuple-element.38), channel_id=1, source_target_pairs={{0,4},{1,5},{2,6},{3,7},{4,0},{5,1},{6,2},{7,3},{8,12},{9,13},{10,... | collective-permute-start | bytes 786440 | tf_op jit(solution)/shard_map/ppermute | solution.py:26
  5.5 1.6 %collective-permute-start = (bf16[128,1024]{1,0:T(8,128)(2,1)}, bf16[128,1024]{1,0:T(8,128)(2,1)S(1)}, u32[]{:S(2)}, u32[]{:S(2)}) collective-permute-start(bf16[128,1024]{1,0:T(8,128)(2,1)} %bitcast.53), channel_id=1, source_target_pairs={{0,8},{8,0},{16,24},{24,16},{1,9},{9,1},{17,25},{25,17},{2,10},{10... | collective-permute-start | bytes 786440 | tf_op jit(solution)/shard_map/ppermute | solution.py:26
  7.1 1.5 %collective-permute-start.1 = (bf16[128,1024]{1,0:T(8,128)(2,1)}, bf16[128,1024]{1,0:T(8,128)(2,1)S(1)}, u32[]{:S(2)}, u32[]{:S(2)}) collective-permute-start(bf16[128,1024]{1,0:T(8,128)(2,1)} %get-tuple-element.39), channel_id=1, source_target_pairs={{0,2},{1,3},{2,0},{3,1},{4,6},{5,7},{6,4},{7,5},{8,10},{9,11},{10,... | collective-permute-start | bytes 786440 | tf_op jit(solution)/shard_map/ppermute | solution.py:26
  8.6 0.7 and_compare_fusion.1
  9.4 0.1 broadcast_in_dim.27
  9.4 2.6 %collective-permute-done.2.refs_4_ = bf16[128,1024]{1,0:T(8,128)(2,1)S(1)} collective-permute-done((bf16[128,1024]{1,0:T(8,128)(2,1)}, bf16[128,1024]{1,0:T(8,128)(2,1)S(1)}, u32[]{:S(2)}, u32[]{:S(2)}) %collective-permute-start.2) | collective-permute-done | bytes 262176 | tf_op jit(solution)/shard_map/ppermute | solution.py:26
  12.1 1.7 %collective-permute-start.5 = (bf16[128,1024]{1,0:T(8,128)(2,1)}, bf16[128,1024]{1,0:T(8,128)(2,1)S(1)}, u32[]{:S(2)}, u32[]{:S(2)}) collective-permute-start(bf16[128,1024]{1,0:T(8,128)(2,1)} %get-tuple-element.39), channel_id=1, source_target_pairs={{0,4},{1,5},{2,6},{3,7},{4,0},{5,1},{6,2},{7,3},{8,12},{9,13},{10,... | collective-permute-start | bytes 786440 | tf_op jit(solution)/shard_map/ppermute | solution.py:26
  13.8 1.1 broadcast_select_fusion
  14.9 2.7 %collective-permute-start.3 = (bf16[128,1024]{1,0:T(8,128)(2,1)S(1)}, bf16[128,1024]{1,0:T(8,128)(2,1)}, u32[]{:S(2)}, u32[]{:S(2)}) collective-permute-start(bf16[128,1024]{1,0:T(8,128)(2,1)S(1)} %broadcast_select_fusion), channel_id=1, source_target_pairs={{0,16},{8,24},{16,0},{24,8},{1,17},{9,25},{17,1},{25,9},{2,18},{10... | collective-permute-start | bytes 786440 | tf_op jit(solution)/shard_map/ppermute | solution.py:26
  17.6 1.5 %collective-permute-start.4 = (bf16[128,1024]{1,0:T(8,128)(2,1)}, bf16[128,1024]{1,0:T(8,128)(2,1)S(1)}, u32[]{:S(2)}, u32[]{:S(2)}) collective-permute-start(bf16[128,1024]{1,0:T(8,128)(2,1)} %get-tuple-element.38), channel_id=1, source_target_pairs={{0,2},{1,3},{2,0},{3,1},{4,6},{5,7},{6,4},{7,5},{8,10},{9,11},{10,... | collective-permute-start | bytes 786440 | tf_op jit(solution)/shard_map/ppermute | solution.py:26
  19.1 0.5 collective-permute-start.7
  19.6 0.5 collective-permute-start.6
  20.2 9.8 %collective-permute-done.7.refs_1_ = bf16[128,1024]{1,0:T(8,128)(2,1)S(1)} collective-permute-done((bf16[128,1024]{1,0:T(8,128)(2,1)S(1)}, bf16[128,1024]{1,0:T(8,128)(2,1)S(1)}, u32[]{:S(2)}, u32[]{:S(2)}) %collective-permute-start.7) | collective-permute-done | bytes 262176 | tf_op jit(solution)/shard_map/ppermute | solution.py:26
  30.0 0.5 collective-permute-start.12
  30.5 0.1 collective-permute-start.14
  30.6 0.4 collective-permute-start.13
  31.2 0.1 broadcast_in_dim.24
  31.3 1.1 broadcast_select_fusion.1
  32.4 1.5 %collective-permute-start.10 = (bf16[128,1024]{1,0:T(8,128)(2,1)S(1)}, bf16[128,1024]{1,0:T(8,128)(2,1)S(1)}, u32[]{:S(2)}, u32[]{:S(2)}) collective-permute-start(bf16[128,1024]{1,0:T(8,128)(2,1)S(1)} %broadcast_select_fusion.1), channel_id=1, source_target_pairs={{0,6},{1,7},{2,4},{3,5},{4,2},{5,3},{6,0},{7,1},{8,14},{9,15},{10,... | collective-permute-start | bytes 786440 | tf_op jit(solution)/shard_map/ppermute | solution.py:26
  33.9 1.5 %collective-permute-start.9 = (bf16[128,1024]{1,0:T(8,128)(2,1)S(1)}, bf16[128,1024]{1,0:T(8,128)(2,1)S(1)}, u32[]{:S(2)}, u32[]{:S(2)}) collective-permute-start(bf16[128,1024]{1,0:T(8,128)(2,1)S(1)} %broadcast_select_fusion.1), channel_id=1, source_target_pairs={{0,4},{1,5},{2,6},{3,7},{4,0},{5,1},{6,2},{7,3},{8,12},{9,13},{10,... | collective-permute-start | bytes 786440 | tf_op jit(solution)/shard_map/ppermute | solution.py:26
  35.5 0.5 collective-permute-start.8
  36.0 2.2 %copy-done = bf16[2048,1024]{1,0:T(8,128)(2,1)S(1)} copy-done((bf16[2048,1024]{1,0:T(8,128)(2,1)S(1)}, bf16[2048,1024]{1,0:T(8,128)(2,1)}, u32[]{:S(2)}) %copy-start) | copy-done | bytes 4194328
  38.2 5.8 %shard_map.85.refs_5_ = f32[1024,1024]{1,0:T(8,128)S(1)} custom-call(s32[2]{0:T(128)S(1)} %pad_add_fusion.here, bf16[256,1024]{1,0:T(8,128)(2,1)S(1)} %slice_bitcast_fusion.refs_0_, bf16[128,1024]{1,0:T(8,128)(2,1)S(1)} %collective-permute-done.1.refs_1_, bf16[128,1024]{1,0:T(8,128)(2,1)S(1)} %collective-permute-done.4.refs_2_, ...), custom_call_target="tpu_custom_call" | custom-call | flops 3221225472 | bytes 10485760 | tf_op jit(solution)/shard_map/pallas_call | solution.py:211
  44.0 3.3 %collective-permute-done.9 = bf16[128,1024]{1,0:T(8,128)(2,1)S(1)} collective-permute-done((bf16[128,1024]{1,0:T(8,128)(2,1)S(1)}, bf16[128,1024]{1,0:T(8,128)(2,1)S(1)}, u32[]{:S(2)}, u32[]{:S(2)}) %collective-permute-start.9) | collective-permute-done | bytes 262176 | tf_op jit(solution)/shard_map/ppermute | solution.py:26
  47.4 0.1 collective-permute-start.16
  47.5 0.5 collective-permute-start.18
  48.0 0.1 collective-permute-start.17
  48.0 2.1 %collective-permute-done.16.other = bf16[512,1024]{1,0:T(8,128)(2,1)S(1)} collective-permute-done((bf16[512,1024]{1,0:T(8,128)(2,1)S(1)}, bf16[512,1024]{1,0:T(8,128)(2,1)S(1)}, u32[]{:S(2)}, u32[]{:S(2)}) %collective-permute-start.16) | collective-permute-done | bytes 1048608 | tf_op jit(solution)/shard_map/ppermute | solution.py:26
  50.1 0.8 shard_map.86
  50.9 2.5 %shard_map.87 = (bf16[1024,1024]{1,0:T(8,128)(2,1)S(1)}, bf16[128,1024]{1,0:T(8,128)(2,1)S(1)}, bf16[128,1024]{1,0:T(8,128)(2,1)S(1)}) custom-call(s32[2]{0:T(128)S(1)} %pad_add_fusion.here, bf16[128,1024]{1,0:T(8,128)(2,1)S(1)} %collective-permute-done.6.refs_0_, bf16[128,1024]{1,0:T(8,128)(2,1)S(1)} %collective-permute-done.7.refs_1_, ...), custom_call_target="tpu_custom_call" | custom-call | tf_op jit(solution)/shard_map/pallas_call | solution.py:133
  53.4 1.6 %collective-permute-start.22 = (bf16[128,1024]{1,0:T(8,128)(2,1)S(1)}, bf16[128,1024]{1,0:T(8,128)(2,1)S(1)}, u32[]{:S(2)}, u32[]{:S(2)}) collective-permute-start(bf16[128,1024]{1,0:T(8,128)(2,1)S(1)} %get-tuple-element.53), channel_id=1, source_target_pairs={{0,8},{8,0},{16,24},{24,16},{1,9},{9,1},{17,25},{25,17},{2,10},{10... | collective-permute-start | bytes 786440 | tf_op jit(solution)/shard_map/ppermute | solution.py:26
  55.1 0.5 fusion.2.refs_0_
  55.6 1.6 %collective-permute-start.21 = (bf16[256,512]{1,0:T(8,128)(2,1)S(1)}, bf16[256,512]{1,0:T(8,128)(2,1)S(1)}, u32[]{:S(2)}, u32[]{:S(2)}) collective-permute-start(bf16[256,512]{1,0:T(8,128)(2,1)S(1)} %fusion.2.refs_0_), channel_id=1, source_target_pairs={{0,6},{1,7},{2,4},{3,5},{4,2},{5,3},{6,0},{7,1},{8,14},{9,15},{10,... | collective-permute-start | bytes 786440 | tf_op jit(solution)/shard_map/ppermute | solution.py:26
  57.2 0.7 collective-permute-start.20
  57.9 1.3 collective-permute-start.19
  59.1 1.3 shard_map.88
  60.4 1.5 %collective-permute-done.22 = bf16[128,1024]{1,0:T(8,128)(2,1)S(1)} collective-permute-done((bf16[128,1024]{1,0:T(8,128)(2,1)S(1)}, bf16[128,1024]{1,0:T(8,128)(2,1)S(1)}, u32[]{:S(2)}, u32[]{:S(2)}) %collective-permute-start.22) | collective-permute-done | bytes 262176 | tf_op jit(solution)/shard_map/ppermute | solution.py:26
  61.8 1.6 %collective-permute-start.27 = (bf16[128,1024]{1,0:T(8,128)(2,1)S(1)}, bf16[128,1024]{1,0:T(8,128)(2,1)S(1)}, u32[]{:S(2)}, u32[]{:S(2)}) collective-permute-start(bf16[128,1024]{1,0:T(8,128)(2,1)S(1)} %get-tuple-element.61), channel_id=1, source_target_pairs={{0,8},{8,0},{16,24},{24,16},{1,9},{9,1},{17,25},{25,17},{2,10},{10... | collective-permute-start | bytes 786440 | tf_op jit(solution)/shard_map/ppermute | solution.py:26
  63.5 2.3 %collective-permute-done.21.refs_3_ = bf16[256,512]{1,0:T(8,128)(2,1)S(1)} collective-permute-done((bf16[256,512]{1,0:T(8,128)(2,1)S(1)}, bf16[256,512]{1,0:T(8,128)(2,1)S(1)}, u32[]{:S(2)}, u32[]{:S(2)}) %collective-permute-start.21) | collective-permute-done | bytes 262176 | tf_op jit(solution)/shard_map/ppermute | solution.py:26
  65.8 4.4 %collective-permute-done.20.refs_2_ = bf16[256,512]{1,0:T(8,128)(2,1)S(1)} collective-permute-done((bf16[256,512]{1,0:T(8,128)(2,1)S(1)}, bf16[256,512]{1,0:T(8,128)(2,1)S(1)}, u32[]{:S(2)}, u32[]{:S(2)}) %collective-permute-start.20) | collective-permute-done | bytes 262176 | tf_op jit(solution)/shard_map/ppermute | solution.py:26
  70.2 0.5 collective-permute-start.25
  70.7 0.9 collective-permute-start.30
  71.6 0.1 collective-permute-done.24.refs_5_
  71.7 0.4 collective-permute-done.25.refs_6_
  72.1 0.4 collective-permute-done.26.refs_7_
  72.5 1.8 %shard_map.90 = bf16[256,1024]{1,0:T(8,128)(2,1)S(1)} custom-call(s32[2]{0:T(128)S(1)} %pad_add_fusion.here, bf16[256,512]{1,0:T(8,128)(2,1)S(1)} %fusion.2.refs_0_, bf16[256,512]{1,0:T(8,128)(2,1)S(1)} %collective-permute-done.19.refs_1_, bf16[256,512]{1,0:T(8,128)(2,1)S(1)} %collective-permute-done.20.refs_2_, ...), custom_call_target="tpu_custom_call" | custom-call | tf_op jit(solution)/shard_map/pallas_call | solution.py:133
  74.3 0.5 collective-permute-start.28
  74.8 11.1 %collective-permute-done.30 = bf16[128,1024]{1,0:T(8,128)(2,1)S(1)} collective-permute-done((bf16[128,1024]{1,0:T(8,128)(2,1)S(1)}, bf16[128,1024]{1,0:T(8,128)(2,1)S(1)}, u32[]{:S(2)}, u32[]{:S(2)}) %collective-permute-start.30) | collective-permute-done | bytes 262176 | tf_op jit(solution)/shard_map/ppermute | solution.py:26
  86.0 0.4 divide_convert_fusion.1
  86.5 1.3 collective-permute-start.33
  87.8 1.8 %shard_map.89 = (f32[128,1024]{1,0:T(8,128)S(1)}, f32[128,1024]{1,0:T(8,128)S(1)}) custom-call(s32[2]{0:T(128)S(1)} %pad_add_fusion.here, bf16[256,512]{1,0:T(8,128)(2,1)S(1)} %fusion.2.refs_0_, bf16[256,512]{1,0:T(8,128)(2,1)S(1)} %collective-permute-done.19.refs_1_, bf16[256,512]{1,0:T(8,128)(2,1)S(1)} %collective-permute-done.20.refs_2_, ...), custom_call_target="tpu_custom_call" | custom-call | tf_op jit(solution)/shard_map/pallas_call | solution.py:133
  89.6 11.7 %collective-permute-done.31 = bf16[128,1024]{1,0:T(8,128)(2,1)S(1)} collective-permute-done((bf16[128,1024]{1,0:T(8,128)(2,1)S(1)}, bf16[128,1024]{1,0:T(8,128)(2,1)S(1)}, u32[]{:S(2)}, u32[]{:S(2)}) %collective-permute-start.31) | collective-permute-done | bytes 262176 | tf_op jit(solution)/shard_map/ppermute | solution.py:26
  101.4 1.0 collective-permute-start.29
  102.4 7.9 %collective-permute-done.33 = bf16[128,1024]{1,0:T(8,128)(2,1)S(1)} collective-permute-done((bf16[128,1024]{1,0:T(8,128)(2,1)S(1)}, bf16[128,1024]{1,0:T(8,128)(2,1)S(1)}, u32[]{:S(2)}, u32[]{:S(2)}) %collective-permute-start.33) | collective-permute-done | bytes 262176 | tf_op jit(solution)/shard_map/ppermute | solution.py:26
  110.3 6.0 %collective-permute-done.32 = bf16[128,1024]{1,0:T(8,128)(2,1)S(1)} collective-permute-done((bf16[128,1024]{1,0:T(8,128)(2,1)S(1)}, bf16[128,1024]{1,0:T(8,128)(2,1)S(1)}, u32[]{:S(2)}, u32[]{:S(2)}) %collective-permute-start.32) | collective-permute-done | bytes 262176 | tf_op jit(solution)/shard_map/ppermute | solution.py:26
  116.3 1.1 fusion.29
  117.5 1.0 collective-permute-start.36
  118.6 11.1 %collective-permute-done.34 = bf16[128,1024]{1,0:T(8,128)(2,1)} collective-permute-done((bf16[128,1024]{1,0:T(8,128)(2,1)}, bf16[128,1024]{1,0:T(8,128)(2,1)}, u32[]{:S(2)}, u32[]{:S(2)}) %collective-permute-start.34) | collective-permute-done | bytes 262176 | tf_op jit(solution)/shard_map/ppermute | solution.py:26
  129.7 1.6 %fusion = bf16[1,256,1024]{2,1,0:T(8,128)(2,1)S(1)} fusion(bf16[128,1024]{1,0:T(8,128)(2,1)S(1)} %get-tuple-element.71, bf16[128,1024]{1,0:T(8,128)(2,1)} %copy-done.8, bf16[128,1024]{1,0:T(8,128)(2,1)} %copy-done.9, bf16[128,1024]{1,0:T(8,128)(2,1)} %copy-done.10, bf16[512,1024]{1,0:T(8,128)(2,1)S(1)} %get-tuple-element.51.refs_6_.projector, s32[]{:T(128)S(6)} %select_n.13), kind=kOutput, calls=%fused_computation.2 | convolution fusion | flops 272891904 | bytes 1835012 | tf_op jit(solution)/shard_map/dot_general | solution.py:384
  131.3 1.5 %pad_maximum_fusion.2 = (f32[2,128,1024]{2,1,0:T(8,128)}, f32[2,128,1024]{2,1,0:T(8,128)}) fusion(f32[1,128,1024]{2,1,0:T(8,128)S(1)} %get-tuple-element.75, f32[1,128,1024]{2,1,0:T(8,128)S(1)} %bitcast.52, f32[1,128,1024]{2,1,0:T(8,128)S(1)} %get-tuple-element.73, f32[1,128,1024]{2,1,0:T(8,128)S(1)} %get-tuple-element.76), kind=kLoop, calls=%fused_computation.22 | loop fusion | flops 524288 | bytes 4194304 | tf_op jit(solution)/shard_map/stack | solution.py:388
  132.7 5.0 %collective-permute-done.35 = bf16[128,1024]{1,0:T(8,128)(2,1)S(1)} collective-permute-done((bf16[128,1024]{1,0:T(8,128)(2,1)}, bf16[128,1024]{1,0:T(8,128)(2,1)S(1)}, u32[]{:S(2)}, u32[]{:S(2)}) %collective-permute-start.35) | collective-permute-done | bytes 262176 | tf_op jit(solution)/shard_map/ppermute | solution.py:26
  137.7 1.6 %fusion.1 = bf16[1,256,1024]{2,1,0:T(8,128)(2,1)S(1)} fusion(bf16[128,1024]{1,0:T(8,128)(2,1)} %get-tuple-element.74, bf16[128,1024]{1,0:T(8,128)(2,1)} %collective-permute-done.34, bf16[128,1024]{1,0:T(8,128)(2,1)S(1)} %collective-permute-done.36, bf16[128,1024]{1,0:T(8,128)(2,1)S(1)} %collective-permute-done.35, bf16[512,1024]{1,0:T(8,128)(2,1)} %copy-done.2, ...), kind=kOutput, calls=%fused_computation.3 | convolution fusion | flops 272891904 | bytes 1835012 | tf_op jit(solution)/shard_map/dot_general | solution.py:384
  139.3 1.1 pad_maximum_fusion.1
  (66 shorter events, 0.8 us)
Async XLA Ops:
  0.6 19.5 %copy-start.3 = (bf16[2,256,1024]{2,1,0:T(8,128)(2,1)S(1)}, bf16[2,256,1024]{2,1,0:T(8,128)(2,1)}, u32[]{:S(2)}) copy-start(bf16[2,256,1024]{2,1,0:T(8,128)(2,1)} %param.7) | copy-start | bytes 3145732
  2.6 9.5 %collective-permute-start.2 = (bf16[128,1024]{1,0:T(8,128)(2,1)}, bf16[128,1024]{1,0:T(8,128)(2,1)S(1)}, u32[]{:S(2)}, u32[]{:S(2)}) collective-permute-start(bf16[128,1024]{1,0:T(8,128)(2,1)} %get-tuple-element.38), channel_id=1, source_target_pairs={{0,4},{1,5},{2,6},{3,7},{4,0},{5,1},{6,2},{7,3},{8,12},{9,13},{10,... | collective-permute-start | bytes 786440 | tf_op jit(solution)/shard_map/ppermute | solution.py:26
  5.5 8.3 %collective-permute-start = (bf16[128,1024]{1,0:T(8,128)(2,1)}, bf16[128,1024]{1,0:T(8,128)(2,1)S(1)}, u32[]{:S(2)}, u32[]{:S(2)}) collective-permute-start(bf16[128,1024]{1,0:T(8,128)(2,1)} %bitcast.53), channel_id=1, source_target_pairs={{0,8},{8,0},{16,24},{24,16},{1,9},{9,1},{17,25},{25,17},{2,10},{10... | collective-permute-start | bytes 786440 | tf_op jit(solution)/shard_map/ppermute | solution.py:26
  7.1 7.8 %collective-permute-start.1 = (bf16[128,1024]{1,0:T(8,128)(2,1)}, bf16[128,1024]{1,0:T(8,128)(2,1)S(1)}, u32[]{:S(2)}, u32[]{:S(2)}) collective-permute-start(bf16[128,1024]{1,0:T(8,128)(2,1)} %get-tuple-element.39), channel_id=1, source_target_pairs={{0,2},{1,3},{2,0},{3,1},{4,6},{5,7},{6,4},{7,5},{8,10},{9,11},{10,... | collective-permute-start | bytes 786440 | tf_op jit(solution)/shard_map/ppermute | solution.py:26
  12.1 8.1 %collective-permute-start.5 = (bf16[128,1024]{1,0:T(8,128)(2,1)}, bf16[128,1024]{1,0:T(8,128)(2,1)S(1)}, u32[]{:S(2)}, u32[]{:S(2)}) collective-permute-start(bf16[128,1024]{1,0:T(8,128)(2,1)} %get-tuple-element.39), channel_id=1, source_target_pairs={{0,4},{1,5},{2,6},{3,7},{4,0},{5,1},{6,2},{7,3},{8,12},{9,13},{10,... | collective-permute-start | bytes 786440 | tf_op jit(solution)/shard_map/ppermute | solution.py:26
  14.9 15.6 %copy-start.7 = (bf16[128,1024]{1,0:T(8,128)(2,1)}, bf16[128,1024]{1,0:T(8,128)(2,1)S(1)}, u32[]{:S(2)}) copy-start(bf16[128,1024]{1,0:T(8,128)(2,1)S(1)} %broadcast_select_fusion) | copy-start | bytes 786436
  14.9 15.1 %collective-permute-start.3 = (bf16[128,1024]{1,0:T(8,128)(2,1)S(1)}, bf16[128,1024]{1,0:T(8,128)(2,1)}, u32[]{:S(2)}, u32[]{:S(2)}) collective-permute-start(bf16[128,1024]{1,0:T(8,128)(2,1)S(1)} %broadcast_select_fusion), channel_id=1, source_target_pairs={{0,16},{8,24},{16,0},{24,8},{1,17},{9,25},{17,1},{25,9},{2,18},{10... | collective-permute-start | bytes 786440 | tf_op jit(solution)/shard_map/ppermute | solution.py:26
  17.6 13.0 %collective-permute-start.4 = (bf16[128,1024]{1,0:T(8,128)(2,1)}, bf16[128,1024]{1,0:T(8,128)(2,1)S(1)}, u32[]{:S(2)}, u32[]{:S(2)}) collective-permute-start(bf16[128,1024]{1,0:T(8,128)(2,1)} %get-tuple-element.38), channel_id=1, source_target_pairs={{0,2},{1,3},{2,0},{3,1},{4,6},{5,7},{6,4},{7,5},{8,10},{9,11},{10,... | collective-permute-start | bytes 786440 | tf_op jit(solution)/shard_map/ppermute | solution.py:26
  19.1 11.0 %collective-permute-start.7 = (bf16[128,1024]{1,0:T(8,128)(2,1)S(1)}, bf16[128,1024]{1,0:T(8,128)(2,1)S(1)}, u32[]{:S(2)}, u32[]{:S(2)}) collective-permute-start(bf16[128,1024]{1,0:T(8,128)(2,1)S(1)} %collective-permute-done.2.refs_4_), channel_id=1, source_target_pairs={{0,2},{1,3},{2,0},{3,1},{4,6},{5,7},{6,4},{7,5},{8,10},{9,11},{10,... | collective-permute-start | bytes 786440 | tf_op jit(solution)/shard_map/ppermute | solution.py:26
  19.6 11.0 %collective-permute-start.6 = (bf16[128,1024]{1,0:T(8,128)(2,1)S(1)}, bf16[128,1024]{1,0:T(8,128)(2,1)S(1)}, u32[]{:S(2)}, u32[]{:S(2)}) collective-permute-start(bf16[128,1024]{1,0:T(8,128)(2,1)S(1)} %collective-permute-done.1.refs_1_), channel_id=1, source_target_pairs={{0,4},{1,5},{2,6},{3,7},{4,0},{5,1},{6,2},{7,3},{8,12},{9,13},{10,... | collective-permute-start | bytes 786440 | tf_op jit(solution)/shard_map/ppermute | solution.py:26
  20.1 15.3 %collective-permute-start.11 = (bf16[256,1024]{1,0:T(8,128)(2,1)S(1)}, bf16[256,1024]{1,0:T(8,128)(2,1)S(1)}, u32[]{:S(2)}, u32[]{:S(2)}) collective-permute-start(bf16[256,1024]{1,0:T(8,128)(2,1)S(1)} %slice_bitcast_fusion.refs_0_), channel_id=1, source_target_pairs={{0,1},{1,0},{2,3},{3,2},{4,5},{5,4},{6,7},{7,6},{8,9},{9,8},{10,11... | collective-permute-start | bytes 1572872 | tf_op jit(solution)/shard_map/ppermute | solution.py:26
  30.0 2.4 %collective-permute-start.15 = (bf16[128,1024]{1,0:T(8,128)(2,1)S(1)}, bf16[128,1024]{1,0:T(8,128)(2,1)S(1)}, u32[]{:S(2)}, u32[]{:S(2)}) collective-permute-start(bf16[128,1024]{1,0:T(8,128)(2,1)S(1)} %collective-permute-done.2.refs_4_), channel_id=1, source_target_pairs={{0,1},{1,0},{2,3},{3,2},{4,5},{5,4},{6,7},{7,6},{8,9},{9,8},{10,11... | collective-permute-start | bytes 786440 | tf_op jit(solution)/shard_map/ppermute | solution.py:26
  30.0 3.9 %collective-permute-start.12 = (bf16[128,1024]{1,0:T(8,128)(2,1)S(1)}, bf16[128,1024]{1,0:T(8,128)(2,1)S(1)}, u32[]{:S(2)}, u32[]{:S(2)}) collective-permute-start(bf16[128,1024]{1,0:T(8,128)(2,1)S(1)} %collective-permute-done.1.refs_1_), channel_id=1, source_target_pairs={{0,1},{1,0},{2,3},{3,2},{4,5},{5,4},{6,7},{7,6},{8,9},{9,8},{10,11... | collective-permute-start | bytes 786440 | tf_op jit(solution)/shard_map/ppermute | solution.py:26
  30.5 5.5 %collective-permute-start.14 = (bf16[128,1024]{1,0:T(8,128)(2,1)S(1)}, bf16[128,1024]{1,0:T(8,128)(2,1)S(1)}, u32[]{:S(2)}, u32[]{:S(2)}) collective-permute-start(bf16[128,1024]{1,0:T(8,128)(2,1)S(1)} %collective-permute-done.5.refs_3_), channel_id=1, source_target_pairs={{0,1},{1,0},{2,3},{3,2},{4,5},{5,4},{6,7},{7,6},{8,9},{9,8},{10,11... | collective-permute-start | bytes 786440 | tf_op jit(solution)/shard_map/ppermute | solution.py:26
  30.6 5.4 %collective-permute-start.13 = (bf16[128,1024]{1,0:T(8,128)(2,1)S(1)}, bf16[128,1024]{1,0:T(8,128)(2,1)}, u32[]{:S(2)}, u32[]{:S(2)}) collective-permute-start(bf16[128,1024]{1,0:T(8,128)(2,1)S(1)} %collective-permute-done.4.refs_2_), channel_id=1, source_target_pairs={{0,1},{1,0},{2,3},{3,2},{4,5},{5,4},{6,7},{7,6},{8,9},{9,8},{10,11... | collective-permute-start | bytes 786440 | tf_op jit(solution)/shard_map/ppermute | solution.py:26
  32.4 11.6 %collective-permute-start.10 = (bf16[128,1024]{1,0:T(8,128)(2,1)S(1)}, bf16[128,1024]{1,0:T(8,128)(2,1)S(1)}, u32[]{:S(2)}, u32[]{:S(2)}) collective-permute-start(bf16[128,1024]{1,0:T(8,128)(2,1)S(1)} %broadcast_select_fusion.1), channel_id=1, source_target_pairs={{0,6},{1,7},{2,4},{3,5},{4,2},{5,3},{6,0},{7,1},{8,14},{9,15},{10,... | collective-permute-start | bytes 786440 | tf_op jit(solution)/shard_map/ppermute | solution.py:26
  33.9 13.4 %collective-permute-start.9 = (bf16[128,1024]{1,0:T(8,128)(2,1)S(1)}, bf16[128,1024]{1,0:T(8,128)(2,1)S(1)}, u32[]{:S(2)}, u32[]{:S(2)}) collective-permute-start(bf16[128,1024]{1,0:T(8,128)(2,1)S(1)} %broadcast_select_fusion.1), channel_id=1, source_target_pairs={{0,4},{1,5},{2,6},{3,7},{4,0},{5,1},{6,2},{7,3},{8,12},{9,13},{10,... | collective-permute-start | bytes 786440 | tf_op jit(solution)/shard_map/ppermute | solution.py:26
  35.5 11.8 %collective-permute-start.8 = (bf16[128,1024]{1,0:T(8,128)(2,1)S(1)}, bf16[128,1024]{1,0:T(8,128)(2,1)S(1)}, u32[]{:S(2)}, u32[]{:S(2)}) collective-permute-start(bf16[128,1024]{1,0:T(8,128)(2,1)S(1)} %broadcast_select_fusion.1), channel_id=1, source_target_pairs={{0,2},{1,3},{2,0},{3,1},{4,6},{5,7},{6,4},{7,5},{8,10},{9,11},{10,... | collective-permute-start | bytes 786440 | tf_op jit(solution)/shard_map/ppermute | solution.py:26
  36.0 2.2 %copy-start = (bf16[2048,1024]{1,0:T(8,128)(2,1)S(1)}, bf16[2048,1024]{1,0:T(8,128)(2,1)}, u32[]{:S(2)}) copy-start(bf16[2048,1024]{1,0:T(8,128)(2,1)} %refs_8_.3) | copy-start | bytes 12582916
  44.0 6.9 %copy-start.1 = (bf16[2048,1024]{1,0:T(8,128)(2,1)S(1)}, bf16[2048,1024]{1,0:T(8,128)(2,1)}, u32[]{:S(2)}) copy-start(bf16[2048,1024]{1,0:T(8,128)(2,1)} %refs_8_.3) | copy-start | bytes 12582916
  47.4 2.7 %collective-permute-start.16 = (bf16[512,1024]{1,0:T(8,128)(2,1)S(1)}, bf16[512,1024]{1,0:T(8,128)(2,1)S(1)}, u32[]{:S(2)}, u32[]{:S(2)}) collective-permute-start(bf16[512,1024]{1,0:T(8,128)(2,1)S(1)} %pad_maximum_fusion.same), channel_id=1, source_target_pairs={{0,1},{1,0},{2,3},{3,2},{4,5},{5,4},{6,7},{7,6},{8,9},{9,8},{10,11... | collective-permute-start | bytes 3145736 | tf_op jit(solution)/shard_map/ppermute | solution.py:26
  47.5 3.4 %collective-permute-start.18 = (bf16[128,1024]{1,0:T(8,128)(2,1)S(1)}, bf16[128,1024]{1,0:T(8,128)(2,1)S(1)}, u32[]{:S(2)}, u32[]{:S(2)}) collective-permute-start(bf16[128,1024]{1,0:T(8,128)(2,1)S(1)} %collective-permute-done.7.refs_1_), channel_id=1, source_target_pairs={{0,1},{1,0},{2,3},{3,2},{4,5},{5,4},{6,7},{7,6},{8,9},{9,8},{10,11... | collective-permute-start | bytes 786440 | tf_op jit(solution)/shard_map/ppermute | solution.py:26
  48.0 2.9 %collective-permute-start.17 = (bf16[128,1024]{1,0:T(8,128)(2,1)S(1)}, bf16[128,1024]{1,0:T(8,128)(2,1)S(1)}, u32[]{:S(2)}, u32[]{:S(2)}) collective-permute-start(bf16[128,1024]{1,0:T(8,128)(2,1)S(1)} %collective-permute-done.6.refs_0_), channel_id=1, source_target_pairs={{0,1},{1,0},{2,3},{3,2},{4,5},{5,4},{6,7},{7,6},{8,9},{9,8},{10,11... | collective-permute-start | bytes 786440 | tf_op jit(solution)/shard_map/ppermute | solution.py:26
  50.9 4.2 %copy-start.2 = (bf16[512,1024]{1,0:T(8,128)(2,1)}, bf16[512,1024]{1,0:T(8,128)(2,1)S(1)}, u32[]{:S(2)}) copy-start(bf16[512,1024]{1,0:T(8,128)(2,1)S(1)} %get-tuple-element.52) | copy-start | bytes 3145732
  50.9 4.1 %copy-start.4 = (bf16[2,256,1024]{2,1,0:T(8,128)(2,1)S(1)}, bf16[2,256,1024]{2,1,0:T(8,128)(2,1)}, u32[]{:S(2)}) copy-start(bf16[2,256,1024]{2,1,0:T(8,128)(2,1)} %param.7) | copy-start | bytes 3145732
  53.4 8.4 %collective-permute-start.22 = (bf16[128,1024]{1,0:T(8,128)(2,1)S(1)}, bf16[128,1024]{1,0:T(8,128)(2,1)S(1)}, u32[]{:S(2)}, u32[]{:S(2)}) collective-permute-start(bf16[128,1024]{1,0:T(8,128)(2,1)S(1)} %get-tuple-element.53), channel_id=1, source_target_pairs={{0,8},{8,0},{16,24},{24,16},{1,9},{9,1},{17,25},{25,17},{2,10},{10... | collective-permute-start | bytes 786440 | tf_op jit(solution)/shard_map/ppermute | solution.py:26
  55.6 10.2 %collective-permute-start.21 = (bf16[256,512]{1,0:T(8,128)(2,1)S(1)}, bf16[256,512]{1,0:T(8,128)(2,1)S(1)}, u32[]{:S(2)}, u32[]{:S(2)}) collective-permute-start(bf16[256,512]{1,0:T(8,128)(2,1)S(1)} %fusion.2.refs_0_), channel_id=1, source_target_pairs={{0,6},{1,7},{2,4},{3,5},{4,2},{5,3},{6,0},{7,1},{8,14},{9,15},{10,... | collective-permute-start | bytes 786440 | tf_op jit(solution)/shard_map/ppermute | solution.py:26
  57.2 13.1 %collective-permute-start.20 = (bf16[256,512]{1,0:T(8,128)(2,1)S(1)}, bf16[256,512]{1,0:T(8,128)(2,1)S(1)}, u32[]{:S(2)}, u32[]{:S(2)}) collective-permute-start(bf16[256,512]{1,0:T(8,128)(2,1)S(1)} %fusion.2.refs_0_), channel_id=1, source_target_pairs={{0,4},{1,5},{2,6},{3,7},{4,0},{5,1},{6,2},{7,3},{8,12},{9,13},{10,... | collective-permute-start | bytes 786440 | tf_op jit(solution)/shard_map/ppermute | solution.py:26
  57.9 12.3 %collective-permute-start.19 = (bf16[256,512]{1,0:T(8,128)(2,1)S(1)}, bf16[256,512]{1,0:T(8,128)(2,1)S(1)}, u32[]{:S(2)}, u32[]{:S(2)}) collective-permute-start(bf16[256,512]{1,0:T(8,128)(2,1)S(1)} %fusion.2.refs_0_), channel_id=1, source_target_pairs={{0,2},{1,3},{2,0},{3,1},{4,6},{5,7},{6,4},{7,5},{8,10},{9,11},{10,... | collective-permute-start | bytes 786440 | tf_op jit(solution)/shard_map/ppermute | solution.py:26
  59.1 11.6 %collective-permute-start.23 = (bf16[256,512]{1,0:T(8,128)(2,1)S(1)}, bf16[256,512]{1,0:T(8,128)(2,1)S(1)}, u32[]{:S(2)}, u32[]{:S(2)}) collective-permute-start(bf16[256,512]{1,0:T(8,128)(2,1)S(1)} %fusion.2.refs_0_), channel_id=1, source_target_pairs={{0,1},{1,0},{2,3},{3,2},{4,5},{5,4},{6,7},{7,6},{8,9},{9,8},{10,11... | collective-permute-start | bytes 786440 | tf_op jit(solution)/shard_map/ppermute | solution.py:26
  61.8 9.8 %collective-permute-start.27 = (bf16[128,1024]{1,0:T(8,128)(2,1)S(1)}, bf16[128,1024]{1,0:T(8,128)(2,1)S(1)}, u32[]{:S(2)}, u32[]{:S(2)}) collective-permute-start(bf16[128,1024]{1,0:T(8,128)(2,1)S(1)} %get-tuple-element.61), channel_id=1, source_target_pairs={{0,8},{8,0},{16,24},{24,16},{1,9},{9,1},{17,25},{25,17},{2,10},{10... | collective-permute-start | bytes 786440 | tf_op jit(solution)/shard_map/ppermute | solution.py:26
  63.5 22.5 %copy-start.5 = (f32[2,128,1024]{2,1,0:T(8,128)S(1)}, f32[2,128,1024]{2,1,0:T(8,128)}, u32[]{:S(2)}) copy-start(f32[2,128,1024]{2,1,0:T(8,128)} %param.10) | copy-start | bytes 3145732
  63.5 22.5 %copy-start.6 = (f32[2,128,1024]{2,1,0:T(8,128)S(1)}, f32[2,128,1024]{2,1,0:T(8,128)}, u32[]{:S(2)}) copy-start(f32[2,128,1024]{2,1,0:T(8,128)} %param.9) | copy-start | bytes 3145732
  70.2 1.5 %collective-permute-start.24 = (bf16[256,512]{1,0:T(8,128)(2,1)S(1)}, bf16[256,512]{1,0:T(8,128)(2,1)S(1)}, u32[]{:S(2)}, u32[]{:S(2)}) collective-permute-start(bf16[256,512]{1,0:T(8,128)(2,1)S(1)} %collective-permute-done.19.refs_1_), channel_id=1, source_target_pairs={{0,1},{1,0},{2,3},{3,2},{4,5},{5,4},{6,7},{7,6},{8,9},{9,8},{10,11... | collective-permute-start | bytes 786440 | tf_op jit(solution)/shard_map/ppermute | solution.py:26
  70.2 1.9 %collective-permute-start.25 = (bf16[256,512]{1,0:T(8,128)(2,1)S(1)}, bf16[256,512]{1,0:T(8,128)(2,1)S(1)}, u32[]{:S(2)}, u32[]{:S(2)}) collective-permute-start(bf16[256,512]{1,0:T(8,128)(2,1)S(1)} %collective-permute-done.20.refs_2_), channel_id=1, source_target_pairs={{0,1},{1,0},{2,3},{3,2},{4,5},{5,4},{6,7},{7,6},{8,9},{9,8},{10,11... | collective-permute-start | bytes 786440 | tf_op jit(solution)/shard_map/ppermute | solution.py:26
  70.7 1.8 %collective-permute-start.26 = (bf16[256,512]{1,0:T(8,128)(2,1)S(1)}, bf16[256,512]{1,0:T(8,128)(2,1)S(1)}, u32[]{:S(2)}, u32[]{:S(2)}) collective-permute-start(bf16[256,512]{1,0:T(8,128)(2,1)S(1)} %collective-permute-done.21.refs_3_), channel_id=1, source_target_pairs={{0,1},{1,0},{2,3},{3,2},{4,5},{5,4},{6,7},{7,6},{8,9},{9,8},{10,11... | collective-permute-start | bytes 786440 | tf_op jit(solution)/shard_map/ppermute | solution.py:26
  70.7 15.2 %collective-permute-start.30 = (bf16[128,1024]{1,0:T(8,128)(2,1)S(1)}, bf16[128,1024]{1,0:T(8,128)(2,1)S(1)}, u32[]{:S(2)}, u32[]{:S(2)}) collective-permute-start(bf16[128,1024]{1,0:T(8,128)(2,1)S(1)} %add_convert_fusion.1.refs_11_), channel_id=1, source_target_pairs={{0,16},{8,24},{16,0},{24,8},{1,17},{9,25},{17,1},{25,9},{2,18},{10... | collective-permute-start | bytes 786440 | tf_op jit(solution)/shard_map/ppermute | solution.py:26
  74.3 27.0 %collective-permute-start.28 = (bf16[256,1024]{1,0:T(8,128)(2,1)S(1)}, bf16[256,1024]{1,0:T(8,128)(2,1)S(1)}, u32[]{:S(2)}, u32[]{:S(2)}) collective-permute-start(bf16[256,1024]{1,0:T(8,128)(2,1)S(1)} %shard_map.90), channel_id=1, source_target_pairs={{0,8},{8,0},{16,24},{24,16},{1,9},{9,1},{17,25},{25,17},{2,10},{10... | collective-permute-start | bytes 1572872 | tf_op jit(solution)/shard_map/ppermute | solution.py:26
  86.4 15.0 %collective-permute-start.31 = (bf16[128,1024]{1,0:T(8,128)(2,1)S(1)}, bf16[128,1024]{1,0:T(8,128)(2,1)S(1)}, u32[]{:S(2)}, u32[]{:S(2)}) collective-permute-start(bf16[128,1024]{1,0:T(8,128)(2,1)S(1)} %get-tuple-element.71), channel_id=1, source_target_pairs={{0,16},{8,24},{16,0},{24,8},{1,17},{9,25},{17,1},{25,9},{2,18},{10... | collective-permute-start | bytes 786440 | tf_op jit(solution)/shard_map/ppermute | solution.py:26
  86.5 23.8 %collective-permute-start.33 = (bf16[128,1024]{1,0:T(8,128)(2,1)S(1)}, bf16[128,1024]{1,0:T(8,128)(2,1)S(1)}, u32[]{:S(2)}, u32[]{:S(2)}) collective-permute-start(bf16[128,1024]{1,0:T(8,128)(2,1)S(1)} %get-tuple-element.71), channel_id=1, source_target_pairs={{0,8},{8,0},{16,24},{24,16},{1,9},{9,1},{17,25},{25,17},{2,10},{10... | collective-permute-start | bytes 786440 | tf_op jit(solution)/shard_map/ppermute | solution.py:26
  101.3 16.1 %copy-start.8 = (bf16[128,1024]{1,0:T(8,128)(2,1)}, bf16[128,1024]{1,0:T(8,128)(2,1)S(1)}, u32[]{:S(2)}) copy-start(bf16[128,1024]{1,0:T(8,128)(2,1)S(1)} %collective-permute-done.31) | copy-start | bytes 786436
  101.3 15.0 %collective-permute-start.32 = (bf16[128,1024]{1,0:T(8,128)(2,1)S(1)}, bf16[128,1024]{1,0:T(8,128)(2,1)S(1)}, u32[]{:S(2)}, u32[]{:S(2)}) collective-permute-start(bf16[128,1024]{1,0:T(8,128)(2,1)S(1)} %collective-permute-done.31), channel_id=1, source_target_pairs={{0,8},{8,0},{16,24},{24,16},{1,9},{9,1},{17,25},{25,17},{2,10},{10... | collective-permute-start | bytes 786440 | tf_op jit(solution)/shard_map/ppermute | solution.py:26
  101.4 14.9 %collective-permute-start.29 = (bf16[128,1024]{1,0:T(8,128)(2,1)S(1)}, bf16[128,1024]{1,0:T(8,128)(2,1)S(1)}, u32[]{:S(2)}, u32[]{:S(2)}) collective-permute-start(bf16[128,1024]{1,0:T(8,128)(2,1)S(1)} %add_convert_fusion), channel_id=1, source_target_pairs={{0,16},{8,24},{16,0},{24,8},{1,17},{9,25},{17,1},{25,9},{2,18},{10... | collective-permute-start | bytes 786440 | tf_op jit(solution)/shard_map/ppermute | solution.py:26
  110.3 7.2 %copy-start.9 = (bf16[128,1024]{1,0:T(8,128)(2,1)}, bf16[128,1024]{1,0:T(8,128)(2,1)S(1)}, u32[]{:S(2)}) copy-start(bf16[128,1024]{1,0:T(8,128)(2,1)S(1)} %collective-permute-done.33) | copy-start | bytes 786436
  116.3 1.1 copy-start.10
  117.5 12.2 %collective-permute-start.34 = (bf16[128,1024]{1,0:T(8,128)(2,1)}, bf16[128,1024]{1,0:T(8,128)(2,1)}, u32[]{:S(2)}, u32[]{:S(2)}) collective-permute-start(bf16[128,1024]{1,0:T(8,128)(2,1)} %get-tuple-element.74), channel_id=1, source_target_pairs={{0,16},{8,24},{16,0},{24,8},{1,17},{9,25},{17,1},{25,9},{2,18},{10... | collective-permute-start | bytes 786440 | tf_op jit(solution)/shard_map/ppermute | solution.py:26
  117.5 15.2 %collective-permute-start.36 = (bf16[128,1024]{1,0:T(8,128)(2,1)}, bf16[128,1024]{1,0:T(8,128)(2,1)S(1)}, u32[]{:S(2)}, u32[]{:S(2)}) collective-permute-start(bf16[128,1024]{1,0:T(8,128)(2,1)} %get-tuple-element.74), channel_id=1, source_target_pairs={{0,8},{8,0},{16,24},{24,16},{1,9},{9,1},{17,25},{25,17},{2,10},{10... | collective-permute-start | bytes 786440 | tf_op jit(solution)/shard_map/ppermute | solution.py:26
  129.7 8.1 %collective-permute-start.35 = (bf16[128,1024]{1,0:T(8,128)(2,1)}, bf16[128,1024]{1,0:T(8,128)(2,1)S(1)}, u32[]{:S(2)}, u32[]{:S(2)}) collective-permute-start(bf16[128,1024]{1,0:T(8,128)(2,1)} %collective-permute-done.34), channel_id=1, source_target_pairs={{0,8},{8,0},{16,24},{24,16},{1,9},{9,1},{17,25},{25,17},{2,10},{10... | collective-permute-start | bytes 786440 | tf_op jit(solution)/shard_map/ppermute | solution.py:26

commit v6 on v5

--- a/solution.py
+++ b/solution.py
@@ -17,8 +17,6 @@
 
 TRANSPOSED = (((0,), (0,)), ((), ()))
 MIB = 1 << 20
-ORDER_HEADS = True
-COST = 0.0
 
 
 def swap(value, axis, mask):
@@ -141,7 +139,7 @@
         out_shape=outputs,
         compiler_params=pltpu.CompilerParams(vmem_limit_bytes=20 * MIB),
         cost_estimate=pl.CostEstimate(
-            flops=int(flops * COST), bytes_accessed=int(moved * COST), transcendentals=0
+            flops=int(flops), bytes_accessed=int(moved), transcendentals=0
         ),
     )(here, *operands, *tokens)
 
@@ -327,40 +325,27 @@
     keep_0 = apply_rest(projectors[0], product, here, pieces, scale)
     arrived_0 = [swap(piece, "dp", dp_bits[0]) for piece in send_0]
 
-    def forward(arrived, keeps):
-        totals = [keep + piece.astype(jnp.float32) for piece, keep in zip(arrived, keeps)]
-        half = len(totals) // 2
-        return [total.astype(jnp.bfloat16) for total in totals[:half]], totals[half:]
-
-    def reduced(arrived, keeps, sends=None):
+    def reduced(arrived, keeps):
         for bit in dp_bits[1:]:
-            made, keeps = forward(arrived, keeps)
-            arrived = [swap(piece, "dp", bit) for piece in (sends or made)]
-            sends = None
+            totals = [keep + piece.astype(jnp.float32) for piece, keep in zip(arrived, keeps)]
+            half = len(totals) // 2
+            arrived = [swap(total.astype(jnp.bfloat16), "dp", bit) for total in totals[:half]]
+            keeps = totals[half:]
         return keeps[0], arrived[0]
 
     heads = lax.dot_general(
         cotangent[1], projectors[1], (((1,), (1,)), ((), ())), preferred_element_type=jnp.float32
     ).astype(jnp.bfloat16)
-    if ORDER_HEADS:
-        heads = after(heads, send_0[:1], tokens_1)
     blocks = spread(heads, far_bits)
-    if len(dp_bits) > 1:
-        next_0, _ = forward(arrived_0, keep_0)
-        moved = [mask for mask in blocks if mask]
-        held = lax.optimization_barrier(tuple(blocks[mask] for mask in moved) + (next_0[0],))
-        blocks.update(zip(moved, held))
-        tokens_1.append(held[-1])
+    open_0 = reduced(arrived_0, keep_0)
+    tokens_1 += arrived_0[pieces // 2 :]
     blocks = with_partner({mask: [held] for mask, held in blocks.items()})
-    send_1 = heads_product(
-        blocks, here, layer_input, 0, 1, jnp.bfloat16, scale, arrived_0[pieces // 2 :] + tokens_1
-    )
+    send_1 = heads_product(blocks, here, layer_input, 0, pieces, jnp.bfloat16, scale, tokens_1)
     keep_1 = heads_product(blocks, here, layer_input, 1, pieces, jnp.float32, scale)
-    arrived_1 = jnp.split(swap(send_1[0], "dp", dp_bits[0]), pieces)
+    arrived_1 = [swap(piece, "dp", dp_bits[0]) for piece in send_1]
 
     updates, firsts, seconds, gathered = [], [], [], []
-    for matrix, arrived, keeps in ((0, arrived_0, keep_0), (1, arrived_1, keep_1)):
-        keep, received = reduced(arrived, keeps)
+    for matrix, (keep, received) in enumerate((open_0, reduced(arrived_1, keep_1))):
         if gathered:
             received, firsts[0], *gathered[0][:-1] = lax.optimization_barrier(
                 (received, firsts[0], *gathered[0][:-1])
@@ -385,7 +370,10 @@
             own, jnp.concatenate(parts, axis=0), TRANSPOSED, preferred_element_type=jnp.float32
         )
         updates.append(update.astype(jnp.bfloat16))
-    return (jnp.stack(updates), jnp.stack(firsts), jnp.stack(seconds))
+    update = jnp.zeros((MATS,) + updates[0].shape, updates[0].dtype)
+    for matrix in range(MATS):
+        update = lax.dynamic_update_slice(update, updates[matrix][None], (matrix, 0, 0))
+    return (update, jnp.stack(firsts), jnp.stack(seconds))
 
 
 def solution(mesh):

time: 141 us -> 135 us (0.957)
  waiting for transfers between devices: 79.7 us -> 68.3 us
  starting transfers between devices: 30.5 us -> 35.3 us
    ppermute x37 -> x38, waiting for transfers between devices: 79.7 us -> 68.3 us  [swap(): return lax.ppermute(value, axis, [(i, i ^ mask) for i in range(size)])]
    ppermute x37 -> x38, starting transfers between devices: 30.5 us -> 35.3 us  [swap(): return lax.ppermute(value, axis, [(i, i ^ mask) for i in range(size)])]
    another operation x3 -> x2, other arithmetic: 3.64 us -> 2.82 us  [on_device(): return (update, jnp.stack(firsts), jnp.stack(seconds))]
  transfers between devices with their start and end apart: 37 -> 38, of which waited for: 16 -> 14; matrix products, arithmetic and copies ran while one was open for 5% -> 7% of each run, Pallas kernels for 8% -> 10%
where the time goes in v6:
time: 135 us
  waiting for transfers between devices  68.3 us (51%)
  starting transfers between devices  35.3 us (26%)
  Pallas kernels  13.8 us (10%)
  other arithmetic  8.14 us (6%)
  local copies, waits for them, and re-layouts  4.73 us (4%)
  matrix products  3.42 us (3%)
    ppermute x38, waiting for transfers between devices, swap(): return lax.ppermute(value, axis, [(i, i ^ mask) for i in range(size)])  68.3 us
    ppermute x38, starting transfers between devices, swap(): return lax.ppermute(value, axis, [(i, i ^ mask) for i in range(size)])  35.3 us
    pallas_call x4, Pallas kernels, call_in_vmem(): pl.pallas_call(body, grid_spec=pltpu.PrefetchScalarGridSpec(num_scalar_pr...  7.26 us
    pallas_call x1, Pallas kernels, add_products(): pl.pallas_call(functools.partial(product_body, shape), grid_spec=pltpu.Pr...  5.8 us
    dot_general x2, matrix products, on_device(): lax.dot_general(own, jnp.concatenate(parts, axis=0), TRANSPOSED, preferre...  2.94 us
    another operation x2, other arithmetic, on_device(): return (update, jnp.stack(firsts), jnp.stack(seconds))  2.82 us
  transfers between devices with their start and end apart: 38, of which 14 were waited for; matrix products, arithmetic and copies ran while one was open for 7% of the time, Pallas kernels for 10%

profile of v6, /device:TPU:0, one launch (start us, length us, event | category | flops | bytes accessed | tf_op | source)
XLA Modules:
  0.0 134.7 jit_solution(3138317919778144406)
XLA Ops:
  0.6 1.1 slice_bitcast_fusion.1
  1.7 3.0 %collective-permute-start.2 = (bf16[128,1024]{1,0:T(8,128)(2,1)S(1)}, bf16[128,1024]{1,0:T(8,128)(2,1)S(1)}, u32[]{:S(2)}, u32[]{:S(2)}) collective-permute-start(bf16[128,1024]{1,0:T(8,128)(2,1)S(1)} %get-tuple-element.34), channel_id=1, source_target_pairs={{0,4},{1,5},{2,6},{3,7},{4,0},{5,1},{6,2},{7,3},{8,12},{9,13},{10,... | collective-permute-start | bytes 786440 | tf_op jit(solution)/shard_map/ppermute | solution.py:24
  4.7 1.6 %collective-permute-start = (bf16[128,1024]{1,0:T(8,128)(2,1)}, bf16[128,1024]{1,0:T(8,128)(2,1)S(1)}, u32[]{:S(2)}, u32[]{:S(2)}) collective-permute-start(bf16[128,1024]{1,0:T(8,128)(2,1)} %bitcast.53), channel_id=1, source_target_pairs={{0,8},{8,0},{16,24},{24,16},{1,9},{9,1},{17,25},{25,17},{2,10},{10... | collective-permute-start | bytes 786440 | tf_op jit(solution)/shard_map/ppermute | solution.py:24
  6.3 1.5 %collective-permute-start.1 = (bf16[128,1024]{1,0:T(8,128)(2,1)S(1)}, bf16[128,1024]{1,0:T(8,128)(2,1)S(1)}, u32[]{:S(2)}, u32[]{:S(2)}) collective-permute-start(bf16[128,1024]{1,0:T(8,128)(2,1)S(1)} %get-tuple-element.35), channel_id=1, source_target_pairs={{0,2},{1,3},{2,0},{3,1},{4,6},{5,7},{6,4},{7,5},{8,10},{9,11},{10,... | collective-permute-start | bytes 786440 | tf_op jit(solution)/shard_map/ppermute | solution.py:24
  7.8 0.7 and_compare_fusion.1
  8.5 0.1 broadcast_in_dim.34
  8.6 2.4 %collective-permute-done.2.refs_4_ = bf16[128,1024]{1,0:T(8,128)(2,1)S(1)} collective-permute-done((bf16[128,1024]{1,0:T(8,128)(2,1)S(1)}, bf16[128,1024]{1,0:T(8,128)(2,1)S(1)}, u32[]{:S(2)}, u32[]{:S(2)}) %collective-permute-start.2) | collective-permute-done | bytes 262176 | tf_op jit(solution)/shard_map/ppermute | solution.py:24
  11.0 1.7 %collective-permute-start.5 = (bf16[128,1024]{1,0:T(8,128)(2,1)S(1)}, bf16[128,1024]{1,0:T(8,128)(2,1)S(1)}, u32[]{:S(2)}, u32[]{:S(2)}) collective-permute-start(bf16[128,1024]{1,0:T(8,128)(2,1)S(1)} %get-tuple-element.35), channel_id=1, source_target_pairs={{0,4},{1,5},{2,6},{3,7},{4,0},{5,1},{6,2},{7,3},{8,12},{9,13},{10,... | collective-permute-start | bytes 786440 | tf_op jit(solution)/shard_map/ppermute | solution.py:24
  12.8 1.0 broadcast_select_fusion
  13.9 2.7 %collective-permute-start.3 = (bf16[128,1024]{1,0:T(8,128)(2,1)S(1)}, bf16[128,1024]{1,0:T(8,128)(2,1)}, u32[]{:S(2)}, u32[]{:S(2)}) collective-permute-start(bf16[128,1024]{1,0:T(8,128)(2,1)S(1)} %broadcast_select_fusion), channel_id=1, source_target_pairs={{0,16},{8,24},{16,0},{24,8},{1,17},{9,25},{17,1},{25,9},{2,18},{10... | collective-permute-start | bytes 786440 | tf_op jit(solution)/shard_map/ppermute | solution.py:24
  16.5 1.5 %collective-permute-start.4 = (bf16[128,1024]{1,0:T(8,128)(2,1)S(1)}, bf16[128,1024]{1,0:T(8,128)(2,1)S(1)}, u32[]{:S(2)}, u32[]{:S(2)}) collective-permute-start(bf16[128,1024]{1,0:T(8,128)(2,1)S(1)} %get-tuple-element.34), channel_id=1, source_target_pairs={{0,2},{1,3},{2,0},{3,1},{4,6},{5,7},{6,4},{7,5},{8,10},{9,11},{10,... | collective-permute-start | bytes 786440 | tf_op jit(solution)/shard_map/ppermute | solution.py:24
  18.0 0.5 collective-permute-start.7
  18.5 0.5 collective-permute-start.6
  19.1 1.1 slice_bitcast_fusion.refs_0_
  20.2 8.5 %collective-permute-done.7.refs_1_ = bf16[128,1024]{1,0:T(8,128)(2,1)S(1)} collective-permute-done((bf16[128,1024]{1,0:T(8,128)(2,1)S(1)}, bf16[128,1024]{1,0:T(8,128)(2,1)S(1)}, u32[]{:S(2)}, u32[]{:S(2)}) %collective-permute-start.7) | collective-permute-done | bytes 262176 | tf_op jit(solution)/shard_map/ppermute | solution.py:24
  28.8 0.5 collective-permute-start.12
  29.3 0.1 collective-permute-start.14
  29.4 0.4 collective-permute-start.13
  29.9 0.1 broadcast_in_dim.31
  30.0 1.1 broadcast_select_fusion.1
  31.2 1.5 %collective-permute-start.10 = (bf16[128,1024]{1,0:T(8,128)(2,1)S(1)}, bf16[128,1024]{1,0:T(8,128)(2,1)S(1)}, u32[]{:S(2)}, u32[]{:S(2)}) collective-permute-start(bf16[128,1024]{1,0:T(8,128)(2,1)S(1)} %broadcast_select_fusion.1), channel_id=1, source_target_pairs={{0,6},{1,7},{2,4},{3,5},{4,2},{5,3},{6,0},{7,1},{8,14},{9,15},{10,... | collective-permute-start | bytes 786440 | tf_op jit(solution)/shard_map/ppermute | solution.py:24
  32.7 1.5 %collective-permute-start.9 = (bf16[128,1024]{1,0:T(8,128)(2,1)S(1)}, bf16[128,1024]{1,0:T(8,128)(2,1)S(1)}, u32[]{:S(2)}, u32[]{:S(2)}) collective-permute-start(bf16[128,1024]{1,0:T(8,128)(2,1)S(1)} %broadcast_select_fusion.1), channel_id=1, source_target_pairs={{0,4},{1,5},{2,6},{3,7},{4,0},{5,1},{6,2},{7,3},{8,12},{9,13},{10,... | collective-permute-start | bytes 786440 | tf_op jit(solution)/shard_map/ppermute | solution.py:24
  34.2 0.5 collective-permute-start.8
  34.8 2.2 %copy-done = bf16[2048,1024]{1,0:T(8,128)(2,1)S(1)} copy-done((bf16[2048,1024]{1,0:T(8,128)(2,1)S(1)}, bf16[2048,1024]{1,0:T(8,128)(2,1)}, u32[]{:S(2)}) %copy-start) | copy-done | bytes 4194328
  36.9 5.8 %shard_map.85.refs_5_ = f32[1024,1024]{1,0:T(8,128)S(1)} custom-call(s32[2]{0:T(128)S(1)} %pad_add_fusion.here, bf16[256,1024]{1,0:T(8,128)(2,1)S(1)} %slice_bitcast_fusion.refs_0_, bf16[128,1024]{1,0:T(8,128)(2,1)S(1)} %collective-permute-done.1.refs_1_, bf16[128,1024]{1,0:T(8,128)(2,1)S(1)} %collective-permute-done.4.refs_2_, ...), custom_call_target="tpu_custom_call" | custom-call | flops 3221225472 | bytes 10485760 | tf_op jit(solution)/shard_map/pallas_call | solution.py:209
  42.8 3.3 %collective-permute-done.9 = bf16[128,1024]{1,0:T(8,128)(2,1)S(1)} collective-permute-done((bf16[128,1024]{1,0:T(8,128)(2,1)S(1)}, bf16[128,1024]{1,0:T(8,128)(2,1)S(1)}, u32[]{:S(2)}, u32[]{:S(2)}) %collective-permute-start.9) | collective-permute-done | bytes 262176 | tf_op jit(solution)/shard_map/ppermute | solution.py:24
  46.1 0.1 collective-permute-start.16
  46.2 0.5 collective-permute-start.25
  46.7 0.1 collective-permute-start.24
  46.8 2.1 %collective-permute-done.16.other = bf16[512,1024]{1,0:T(8,128)(2,1)S(1)} collective-permute-done((bf16[512,1024]{1,0:T(8,128)(2,1)S(1)}, bf16[512,1024]{1,0:T(8,128)(2,1)S(1)}, u32[]{:S(2)}, u32[]{:S(2)}) %collective-permute-start.16) | collective-permute-done | bytes 1048608 | tf_op jit(solution)/shard_map/ppermute | solution.py:24
  48.9 0.8 shard_map.86
  49.7 0.5 fusion.2.refs_0_
  50.1 1.6 %collective-permute-start.19 = (bf16[256,512]{1,0:T(8,128)(2,1)S(1)}, bf16[256,512]{1,0:T(8,128)(2,1)S(1)}, u32[]{:S(2)}, u32[]{:S(2)}) collective-permute-start(bf16[256,512]{1,0:T(8,128)(2,1)S(1)} %fusion.2.refs_0_), channel_id=1, source_target_pairs={{0,6},{1,7},{2,4},{3,5},{4,2},{5,3},{6,0},{7,1},{8,14},{9,15},{10,... | collective-permute-start | bytes 786440 | tf_op jit(solution)/shard_map/ppermute | solution.py:24
  51.7 0.7 collective-permute-start.18
  52.5 1.2 collective-permute-start.17
  53.7 2.4 %shard_map.88 = (bf16[1024,1024]{1,0:T(8,128)(2,1)S(1)}, bf16[128,1024]{1,0:T(8,128)(2,1)S(1)}, bf16[128,1024]{1,0:T(8,128)(2,1)S(1)}) custom-call(s32[2]{0:T(128)S(1)} %pad_add_fusion.here, bf16[128,1024]{1,0:T(8,128)(2,1)S(1)} %collective-permute-done.6.refs_0_, bf16[128,1024]{1,0:T(8,128)(2,1)S(1)} %collective-permute-done.7.refs_1_, ...), custom_call_target="tpu_custom_call" | custom-call | flops 1610612736 | bytes 13107200 | tf_op jit(solution)/shard_map/pallas_call | solution.py:131
  56.1 1.6 %collective-permute-start.29 = (bf16[128,1024]{1,0:T(8,128)(2,1)S(1)}, bf16[128,1024]{1,0:T(8,128)(2,1)S(1)}, u32[]{:S(2)}, u32[]{:S(2)}) collective-permute-start(bf16[128,1024]{1,0:T(8,128)(2,1)S(1)} %get-tuple-element.55), channel_id=1, source_target_pairs={{0,8},{8,0},{16,24},{24,16},{1,9},{9,1},{17,25},{25,17},{2,10},{10... | collective-permute-start | bytes 786440 | tf_op jit(solution)/shard_map/ppermute | solution.py:24
  57.8 1.2 shard_map.90
  59.0 1.3 collective-permute-done.19.refs_3_
  60.3 1.6 %collective-permute-start.26 = (bf16[128,1024]{1,0:T(8,128)(2,1)S(1)}, bf16[128,1024]{1,0:T(8,128)(2,1)S(1)}, u32[]{:S(2)}, u32[]{:S(2)}) collective-permute-start(bf16[128,1024]{1,0:T(8,128)(2,1)S(1)} %get-tuple-element.50), channel_id=1, source_target_pairs={{0,8},{8,0},{16,24},{24,16},{1,9},{9,1},{17,25},{25,17},{2,10},{10... | collective-permute-start | bytes 786440 | tf_op jit(solution)/shard_map/ppermute | solution.py:24
  61.9 3.2 %collective-permute-done.18.refs_2_ = bf16[256,512]{1,0:T(8,128)(2,1)S(1)} collective-permute-done((bf16[256,512]{1,0:T(8,128)(2,1)S(1)}, bf16[256,512]{1,0:T(8,128)(2,1)S(1)}, u32[]{:S(2)}, u32[]{:S(2)}) %collective-permute-start.18) | collective-permute-done | bytes 262176 | tf_op jit(solution)/shard_map/ppermute | solution.py:24
  65.1 0.5 collective-permute-start.22
  65.8 0.4 collective-permute-start.30
  66.2 3.8 %collective-permute-done.26.refs_9_ = bf16[128,1024]{1,0:T(8,128)(2,1)S(1)} collective-permute-done((bf16[128,1024]{1,0:T(8,128)(2,1)S(1)}, bf16[128,1024]{1,0:T(8,128)(2,1)S(1)}, u32[]{:S(2)}, u32[]{:S(2)}) %collective-permute-start.26) | collective-permute-done | bytes 262176 | tf_op jit(solution)/shard_map/ppermute | solution.py:24
  70.0 1.8 %shard_map.89 = (bf16[128,1024]{1,0:T(8,128)(2,1)S(1)}, bf16[128,1024]{1,0:T(8,128)(2,1)S(1)}) custom-call(s32[2]{0:T(128)S(1)} %pad_add_fusion.here, bf16[256,512]{1,0:T(8,128)(2,1)S(1)} %fusion.2.refs_0_, bf16[256,512]{1,0:T(8,128)(2,1)S(1)} %collective-permute-done.17.refs_1_, bf16[256,512]{1,0:T(8,128)(2,1)S(1)} %collective-permute-done.18.refs_2_, ...), custom_call_target="tpu_custom_call" | custom-call | flops 1073741824 | bytes 6815744 | tf_op jit(solution)/shard_map/pallas_call | solution.py:131
  71.8 2.5 %collective-permute-start.27 = (bf16[128,1024]{1,0:T(8,128)(2,1)S(1)}, bf16[128,1024]{1,0:T(8,128)(2,1)S(1)}, u32[]{:S(2)}, u32[]{:S(2)}) collective-permute-start(bf16[128,1024]{1,0:T(8,128)(2,1)S(1)} %get-tuple-element.51), channel_id=1, source_target_pairs={{0,8},{8,0},{16,24},{24,16},{1,9},{9,1},{17,25},{25,17},{2,10},{10... | collective-permute-start | bytes 786440 | tf_op jit(solution)/shard_map/ppermute | solution.py:24
  74.4 6.7 %collective-permute-done.30 = bf16[128,1024]{1,0:T(8,128)(2,1)S(1)} collective-permute-done((bf16[128,1024]{1,0:T(8,128)(2,1)S(1)}, bf16[128,1024]{1,0:T(8,128)(2,1)S(1)}, u32[]{:S(2)}, u32[]{:S(2)}) %collective-permute-start.30) | collective-permute-done | bytes 262176 | tf_op jit(solution)/shard_map/ppermute | solution.py:24
  81.1 1.2 divide_convert_fusion.1
  82.3 2.3 %collective-permute-start.31 = (bf16[128,1024]{1,0:T(8,128)(2,1)S(1)}, bf16[128,1024]{1,0:T(8,128)(2,1)S(1)}, u32[]{:S(2)}, u32[]{:S(2)}) collective-permute-start(bf16[128,1024]{1,0:T(8,128)(2,1)S(1)} %get-tuple-element.63), channel_id=1, source_target_pairs={{0,16},{8,24},{16,0},{24,8},{1,17},{9,25},{17,1},{25,9},{2,18},{10... | collective-permute-start | bytes 786440 | tf_op jit(solution)/shard_map/ppermute | solution.py:24
  84.6 1.8 %shard_map.87 = (f32[128,1024]{1,0:T(8,128)S(1)}, f32[128,1024]{1,0:T(8,128)S(1)}) custom-call(s32[2]{0:T(128)S(1)} %pad_add_fusion.here, bf16[256,512]{1,0:T(8,128)(2,1)S(1)} %fusion.2.refs_0_, bf16[256,512]{1,0:T(8,128)(2,1)S(1)} %collective-permute-done.17.refs_1_, bf16[256,512]{1,0:T(8,128)(2,1)S(1)} %collective-permute-done.18.refs_2_, ...), custom_call_target="tpu_custom_call" | custom-call | flops 1073741824 | bytes 7340032 | tf_op jit(solution)/shard_map/pallas_call | solution.py:131
  86.4 0.7 collective-permute-start.28
  87.2 16.6 %collective-permute-done.31 = bf16[128,1024]{1,0:T(8,128)(2,1)S(1)} collective-permute-done((bf16[128,1024]{1,0:T(8,128)(2,1)S(1)}, bf16[128,1024]{1,0:T(8,128)(2,1)S(1)}, u32[]{:S(2)}, u32[]{:S(2)}) %collective-permute-start.31) | collective-permute-done | bytes 262176 | tf_op jit(solution)/shard_map/ppermute | solution.py:24
  103.8 2.0 %collective-permute-start.34 = (bf16[128,1024]{1,0:T(8,128)(2,1)S(1)}, bf16[128,1024]{1,0:T(8,128)(2,1)S(1)}, u32[]{:S(2)}, u32[]{:S(2)}) collective-permute-start(bf16[128,1024]{1,0:T(8,128)(2,1)S(1)} %get-tuple-element.60), channel_id=1, source_target_pairs={{0,8},{8,0},{16,24},{24,16},{1,9},{9,1},{17,25},{25,17},{2,10},{10... | collective-permute-start | bytes 786440 | tf_op jit(solution)/shard_map/ppermute | solution.py:24
  105.8 2.2 %collective-permute-done.28 = bf16[128,1024]{1,0:T(8,128)(2,1)S(1)} collective-permute-done((bf16[128,1024]{1,0:T(8,128)(2,1)S(1)}, bf16[128,1024]{1,0:T(8,128)(2,1)S(1)}, u32[]{:S(2)}, u32[]{:S(2)}) %collective-permute-start.28) | collective-permute-done | bytes 262176 | tf_op jit(solution)/shard_map/ppermute | solution.py:24
  108.0 3.3 %collective-permute-done.32 = bf16[128,1024]{1,0:T(8,128)(2,1)S(1)} collective-permute-done((bf16[128,1024]{1,0:T(8,128)(2,1)S(1)}, bf16[128,1024]{1,0:T(8,128)(2,1)S(1)}, u32[]{:S(2)}, u32[]{:S(2)}) %collective-permute-start.32) | collective-permute-done | bytes 262176 | tf_op jit(solution)/shard_map/ppermute | solution.py:24
  111.3 3.8 %collective-permute-done.34 = bf16[128,1024]{1,0:T(8,128)(2,1)S(1)} collective-permute-done((bf16[128,1024]{1,0:T(8,128)(2,1)S(1)}, bf16[128,1024]{1,0:T(8,128)(2,1)S(1)}, u32[]{:S(2)}, u32[]{:S(2)}) %collective-permute-start.34) | collective-permute-done | bytes 262176 | tf_op jit(solution)/shard_map/ppermute | solution.py:24
  115.1 1.4 %fusion.28 = (f32[1,128,1024]{2,1,0:T(8,128)}, bf16[128,1024]{1,0:T(8,128)(2,1)S(1)}, f32[1,128,1024]{2,1,0:T(8,128)}) fusion(bf16[128,1024]{1,0:T(8,128)(2,1)S(1)} %collective-permute-done.28, f32[128,1024]{1,0:T(8,128)S(1)} %get-tuple-element.59, bf16[128,1024]{1,0:T(8,128)(2,1)S(1)} %collective-permute-done.34, f32[2,128,1024]{2,1,0:T(8,128)S(1)} %copy-done.6, ...), kind=kLoop, calls=%fused_computation.53 | loop fusion | flops 2097152 | bytes 3407872 | tf_op jit(solution)/shard_map/stack | solution.py:376
  116.5 1.6 %collective-permute-start.37 = (bf16[128,1024]{1,0:T(8,128)(2,1)S(1)}, bf16[128,1024]{1,0:T(8,128)(2,1)S(1)}, u32[]{:S(2)}, u32[]{:S(2)}) collective-permute-start(bf16[128,1024]{1,0:T(8,128)(2,1)S(1)} %get-tuple-element.67), channel_id=1, source_target_pairs={{0,8},{8,0},{16,24},{24,16},{1,9},{9,1},{17,25},{25,17},{2,10},{10... | collective-permute-start | bytes 786440 | tf_op jit(solution)/shard_map/ppermute | solution.py:24
  118.2 7.5 %collective-permute-done.35 = bf16[128,1024]{1,0:T(8,128)(2,1)} collective-permute-done((bf16[128,1024]{1,0:T(8,128)(2,1)S(1)}, bf16[128,1024]{1,0:T(8,128)(2,1)}, u32[]{:S(2)}, u32[]{:S(2)}) %collective-permute-start.35) | collective-permute-done | bytes 262176 | tf_op jit(solution)/shard_map/ppermute | solution.py:24
  125.6 1.5 %fusion = bf16[1,256,1024]{2,1,0:T(8,128)(2,1)S(1)} fusion(bf16[128,1024]{1,0:T(8,128)(2,1)S(1)} %get-tuple-element.63, bf16[128,1024]{1,0:T(8,128)(2,1)} %copy-done.9, bf16[128,1024]{1,0:T(8,128)(2,1)S(1)} %collective-permute-done.33, bf16[128,1024]{1,0:T(8,128)(2,1)} %copy-done.10, bf16[512,1024]{1,0:T(8,128)(2,1)S(1)} %get-tuple-element.47.refs_6_.projector, ...), kind=kOutput, calls=%fused_computation.2 | convolution fusion | flops 272891904 | bytes 1835012 | tf_op jit(solution)/shard_map/dot_general | solution.py:369
  127.2 1.5 %pad_maximum_fusion.2 = (f32[2,128,1024]{2,1,0:T(8,128)}, f32[2,128,1024]{2,1,0:T(8,128)}) fusion(f32[1,128,1024]{2,1,0:T(8,128)S(1)} %copy-done.4, f32[1,128,1024]{2,1,0:T(8,128)S(1)} %bitcast.52, f32[1,128,1024]{2,1,0:T(8,128)S(1)} %copy-done.3, f32[1,128,1024]{2,1,0:T(8,128)S(1)} %copy-done.2), kind=kLoop, calls=%fused_computation.22 | loop fusion | flops 524288 | bytes 4194304 | tf_op jit(solution)/shard_map/stack | solution.py:376
  128.6 3.6 %collective-permute-done.36 = bf16[128,1024]{1,0:T(8,128)(2,1)S(1)} collective-permute-done((bf16[128,1024]{1,0:T(8,128)(2,1)}, bf16[128,1024]{1,0:T(8,128)(2,1)S(1)}, u32[]{:S(2)}, u32[]{:S(2)}) %collective-permute-start.36) | collective-permute-done | bytes 262176 | tf_op jit(solution)/shard_map/ppermute | solution.py:24
  132.2 1.4 %fusion.1 = bf16[1,256,1024]{2,1,0:T(8,128)(2,1)S(1)} fusion(bf16[128,1024]{1,0:T(8,128)(2,1)S(1)} %get-tuple-element.67, bf16[128,1024]{1,0:T(8,128)(2,1)} %collective-permute-done.35, bf16[128,1024]{1,0:T(8,128)(2,1)S(1)} %collective-permute-done.37, bf16[128,1024]{1,0:T(8,128)(2,1)S(1)} %collective-permute-done.36, ...), kind=kOutput, calls=%fused_computation.3 | convolution fusion | flops 272891904 | bytes 1835012 | tf_op jit(solution)/shard_map/dot_general | solution.py:369
  133.6 1.1 pad_maximum_fusion.1
  (67 shorter events, 0.7 us)
Async XLA Ops:
  1.7 9.3 %collective-permute-start.2 = (bf16[128,1024]{1,0:T(8,128)(2,1)S(1)}, bf16[128,1024]{1,0:T(8,128)(2,1)S(1)}, u32[]{:S(2)}, u32[]{:S(2)}) collective-permute-start(bf16[128,1024]{1,0:T(8,128)(2,1)S(1)} %get-tuple-element.34), channel_id=1, source_target_pairs={{0,4},{1,5},{2,6},{3,7},{4,0},{5,1},{6,2},{7,3},{8,12},{9,13},{10,... | collective-permute-start | bytes 786440 | tf_op jit(solution)/shard_map/ppermute | solution.py:24
  4.7 8.1 %collective-permute-start = (bf16[128,1024]{1,0:T(8,128)(2,1)}, bf16[128,1024]{1,0:T(8,128)(2,1)S(1)}, u32[]{:S(2)}, u32[]{:S(2)}) collective-permute-start(bf16[128,1024]{1,0:T(8,128)(2,1)} %bitcast.53), channel_id=1, source_target_pairs={{0,8},{8,0},{16,24},{24,16},{1,9},{9,1},{17,25},{25,17},{2,10},{10... | collective-permute-start | bytes 786440 | tf_op jit(solution)/shard_map/ppermute | solution.py:24
  6.3 7.5 %collective-permute-start.1 = (bf16[128,1024]{1,0:T(8,128)(2,1)S(1)}, bf16[128,1024]{1,0:T(8,128)(2,1)S(1)}, u32[]{:S(2)}, u32[]{:S(2)}) collective-permute-start(bf16[128,1024]{1,0:T(8,128)(2,1)S(1)} %get-tuple-element.35), channel_id=1, source_target_pairs={{0,2},{1,3},{2,0},{3,1},{4,6},{5,7},{6,4},{7,5},{8,10},{9,11},{10,... | collective-permute-start | bytes 786440 | tf_op jit(solution)/shard_map/ppermute | solution.py:24
  11.0 9.1 %collective-permute-start.5 = (bf16[128,1024]{1,0:T(8,128)(2,1)S(1)}, bf16[128,1024]{1,0:T(8,128)(2,1)S(1)}, u32[]{:S(2)}, u32[]{:S(2)}) collective-permute-start(bf16[128,1024]{1,0:T(8,128)(2,1)S(1)} %get-tuple-element.35), channel_id=1, source_target_pairs={{0,4},{1,5},{2,6},{3,7},{4,0},{5,1},{6,2},{7,3},{8,12},{9,13},{10,... | collective-permute-start | bytes 786440 | tf_op jit(solution)/shard_map/ppermute | solution.py:24
  13.8 14.9 %copy-start.8 = (bf16[128,1024]{1,0:T(8,128)(2,1)}, bf16[128,1024]{1,0:T(8,128)(2,1)S(1)}, u32[]{:S(2)}) copy-start(bf16[128,1024]{1,0:T(8,128)(2,1)S(1)} %broadcast_select_fusion) | copy-start | bytes 786436
  13.9 14.9 %collective-permute-start.3 = (bf16[128,1024]{1,0:T(8,128)(2,1)S(1)}, bf16[128,1024]{1,0:T(8,128)(2,1)}, u32[]{:S(2)}, u32[]{:S(2)}) collective-permute-start(bf16[128,1024]{1,0:T(8,128)(2,1)S(1)} %broadcast_select_fusion), channel_id=1, source_target_pairs={{0,16},{8,24},{16,0},{24,8},{1,17},{9,25},{17,1},{25,9},{2,18},{10... | collective-permute-start | bytes 786440 | tf_op jit(solution)/shard_map/ppermute | solution.py:24
  16.5 12.8 %collective-permute-start.4 = (bf16[128,1024]{1,0:T(8,128)(2,1)S(1)}, bf16[128,1024]{1,0:T(8,128)(2,1)S(1)}, u32[]{:S(2)}, u32[]{:S(2)}) collective-permute-start(bf16[128,1024]{1,0:T(8,128)(2,1)S(1)} %get-tuple-element.34), channel_id=1, source_target_pairs={{0,2},{1,3},{2,0},{3,1},{4,6},{5,7},{6,4},{7,5},{8,10},{9,11},{10,... | collective-permute-start | bytes 786440 | tf_op jit(solution)/shard_map/ppermute | solution.py:24
  18.0 10.7 %collective-permute-start.7 = (bf16[128,1024]{1,0:T(8,128)(2,1)S(1)}, bf16[128,1024]{1,0:T(8,128)(2,1)S(1)}, u32[]{:S(2)}, u32[]{:S(2)}) collective-permute-start(bf16[128,1024]{1,0:T(8,128)(2,1)S(1)} %collective-permute-done.2.refs_4_), channel_id=1, source_target_pairs={{0,2},{1,3},{2,0},{3,1},{4,6},{5,7},{6,4},{7,5},{8,10},{9,11},{10,... | collective-permute-start | bytes 786440 | tf_op jit(solution)/shard_map/ppermute | solution.py:24
  18.5 10.8 %collective-permute-start.6 = (bf16[128,1024]{1,0:T(8,128)(2,1)S(1)}, bf16[128,1024]{1,0:T(8,128)(2,1)S(1)}, u32[]{:S(2)}, u32[]{:S(2)}) collective-permute-start(bf16[128,1024]{1,0:T(8,128)(2,1)S(1)} %collective-permute-done.1.refs_1_), channel_id=1, source_target_pairs={{0,4},{1,5},{2,6},{3,7},{4,0},{5,1},{6,2},{7,3},{8,12},{9,13},{10,... | collective-permute-start | bytes 786440 | tf_op jit(solution)/shard_map/ppermute | solution.py:24
  20.1 14.1 %collective-permute-start.11 = (bf16[256,1024]{1,0:T(8,128)(2,1)S(1)}, bf16[256,1024]{1,0:T(8,128)(2,1)S(1)}, u32[]{:S(2)}, u32[]{:S(2)}) collective-permute-start(bf16[256,1024]{1,0:T(8,128)(2,1)S(1)} %slice_bitcast_fusion.refs_0_), channel_id=1, source_target_pairs={{0,1},{1,0},{2,3},{3,2},{4,5},{5,4},{6,7},{7,6},{8,9},{9,8},{10,11... | collective-permute-start | bytes 1572872 | tf_op jit(solution)/shard_map/ppermute | solution.py:24
  28.8 2.4 %collective-permute-start.15 = (bf16[128,1024]{1,0:T(8,128)(2,1)S(1)}, bf16[128,1024]{1,0:T(8,128)(2,1)S(1)}, u32[]{:S(2)}, u32[]{:S(2)}) collective-permute-start(bf16[128,1024]{1,0:T(8,128)(2,1)S(1)} %collective-permute-done.2.refs_4_), channel_id=1, source_target_pairs={{0,1},{1,0},{2,3},{3,2},{4,5},{5,4},{6,7},{7,6},{8,9},{9,8},{10,11... | collective-permute-start | bytes 786440 | tf_op jit(solution)/shard_map/ppermute | solution.py:24
  28.8 3.9 %collective-permute-start.12 = (bf16[128,1024]{1,0:T(8,128)(2,1)S(1)}, bf16[128,1024]{1,0:T(8,128)(2,1)S(1)}, u32[]{:S(2)}, u32[]{:S(2)}) collective-permute-start(bf16[128,1024]{1,0:T(8,128)(2,1)S(1)} %collective-permute-done.1.refs_1_), channel_id=1, source_target_pairs={{0,1},{1,0},{2,3},{3,2},{4,5},{5,4},{6,7},{7,6},{8,9},{9,8},{10,11... | collective-permute-start | bytes 786440 | tf_op jit(solution)/shard_map/ppermute | solution.py:24
  29.3 5.5 %collective-permute-start.14 = (bf16[128,1024]{1,0:T(8,128)(2,1)S(1)}, bf16[128,1024]{1,0:T(8,128)(2,1)S(1)}, u32[]{:S(2)}, u32[]{:S(2)}) collective-permute-start(bf16[128,1024]{1,0:T(8,128)(2,1)S(1)} %collective-permute-done.5.refs_3_), channel_id=1, source_target_pairs={{0,1},{1,0},{2,3},{3,2},{4,5},{5,4},{6,7},{7,6},{8,9},{9,8},{10,11... | collective-permute-start | bytes 786440 | tf_op jit(solution)/shard_map/ppermute | solution.py:24
  29.4 5.4 %collective-permute-start.13 = (bf16[128,1024]{1,0:T(8,128)(2,1)S(1)}, bf16[128,1024]{1,0:T(8,128)(2,1)}, u32[]{:S(2)}, u32[]{:S(2)}) collective-permute-start(bf16[128,1024]{1,0:T(8,128)(2,1)S(1)} %collective-permute-done.4.refs_2_), channel_id=1, source_target_pairs={{0,1},{1,0},{2,3},{3,2},{4,5},{5,4},{6,7},{7,6},{8,9},{9,8},{10,11... | collective-permute-start | bytes 786440 | tf_op jit(solution)/shard_map/ppermute | solution.py:24
  31.2 11.6 %collective-permute-start.10 = (bf16[128,1024]{1,0:T(8,128)(2,1)S(1)}, bf16[128,1024]{1,0:T(8,128)(2,1)S(1)}, u32[]{:S(2)}, u32[]{:S(2)}) collective-permute-start(bf16[128,1024]{1,0:T(8,128)(2,1)S(1)} %broadcast_select_fusion.1), channel_id=1, source_target_pairs={{0,6},{1,7},{2,4},{3,5},{4,2},{5,3},{6,0},{7,1},{8,14},{9,15},{10,... | collective-permute-start | bytes 786440 | tf_op jit(solution)/shard_map/ppermute | solution.py:24
  32.7 13.4 %collective-permute-start.9 = (bf16[128,1024]{1,0:T(8,128)(2,1)S(1)}, bf16[128,1024]{1,0:T(8,128)(2,1)S(1)}, u32[]{:S(2)}, u32[]{:S(2)}) collective-permute-start(bf16[128,1024]{1,0:T(8,128)(2,1)S(1)} %broadcast_select_fusion.1), channel_id=1, source_target_pairs={{0,4},{1,5},{2,6},{3,7},{4,0},{5,1},{6,2},{7,3},{8,12},{9,13},{10,... | collective-permute-start | bytes 786440 | tf_op jit(solution)/shard_map/ppermute | solution.py:24
  34.2 11.8 %collective-permute-start.8 = (bf16[128,1024]{1,0:T(8,128)(2,1)S(1)}, bf16[128,1024]{1,0:T(8,128)(2,1)S(1)}, u32[]{:S(2)}, u32[]{:S(2)}) collective-permute-start(bf16[128,1024]{1,0:T(8,128)(2,1)S(1)} %broadcast_select_fusion.1), channel_id=1, source_target_pairs={{0,2},{1,3},{2,0},{3,1},{4,6},{5,7},{6,4},{7,5},{8,10},{9,11},{10,... | collective-permute-start | bytes 786440 | tf_op jit(solution)/shard_map/ppermute | solution.py:24
  34.8 2.2 %copy-start = (bf16[2048,1024]{1,0:T(8,128)(2,1)S(1)}, bf16[2048,1024]{1,0:T(8,128)(2,1)}, u32[]{:S(2)}) copy-start(bf16[2048,1024]{1,0:T(8,128)(2,1)} %refs_8_.3) | copy-start | bytes 12582916
  42.8 6.9 %copy-start.5 = (bf16[2,256,1024]{2,1,0:T(8,128)(2,1)S(1)}, bf16[2,256,1024]{2,1,0:T(8,128)(2,1)}, u32[]{:S(2)}) copy-start(bf16[2,256,1024]{2,1,0:T(8,128)(2,1)} %param.7) | copy-start | bytes 3145732
  46.1 7.6 %copy-start.1 = (bf16[2048,1024]{1,0:T(8,128)(2,1)S(1)}, bf16[2048,1024]{1,0:T(8,128)(2,1)}, u32[]{:S(2)}) copy-start(bf16[2048,1024]{1,0:T(8,128)(2,1)} %refs_8_.3) | copy-start | bytes 12582916
  46.1 2.7 %collective-permute-start.16 = (bf16[512,1024]{1,0:T(8,128)(2,1)S(1)}, bf16[512,1024]{1,0:T(8,128)(2,1)S(1)}, u32[]{:S(2)}, u32[]{:S(2)}) collective-permute-start(bf16[512,1024]{1,0:T(8,128)(2,1)S(1)} %pad_maximum_fusion.same), channel_id=1, source_target_pairs={{0,1},{1,0},{2,3},{3,2},{4,5},{5,4},{6,7},{7,6},{8,9},{9,8},{10,11... | collective-permute-start | bytes 3145736 | tf_op jit(solution)/shard_map/ppermute | solution.py:24
  46.2 7.5 %collective-permute-start.25 = (bf16[128,1024]{1,0:T(8,128)(2,1)S(1)}, bf16[128,1024]{1,0:T(8,128)(2,1)S(1)}, u32[]{:S(2)}, u32[]{:S(2)}) collective-permute-start(bf16[128,1024]{1,0:T(8,128)(2,1)S(1)} %collective-permute-done.7.refs_1_), channel_id=1, source_target_pairs={{0,1},{1,0},{2,3},{3,2},{4,5},{5,4},{6,7},{7,6},{8,9},{9,8},{10,11... | collective-permute-start | bytes 786440 | tf_op jit(solution)/shard_map/ppermute | solution.py:24
  46.7 7.0 %collective-permute-start.24 = (bf16[128,1024]{1,0:T(8,128)(2,1)S(1)}, bf16[128,1024]{1,0:T(8,128)(2,1)S(1)}, u32[]{:S(2)}, u32[]{:S(2)}) collective-permute-start(bf16[128,1024]{1,0:T(8,128)(2,1)S(1)} %collective-permute-done.6.refs_0_), channel_id=1, source_target_pairs={{0,1},{1,0},{2,3},{3,2},{4,5},{5,4},{6,7},{7,6},{8,9},{9,8},{10,11... | collective-permute-start | bytes 786440 | tf_op jit(solution)/shard_map/ppermute | solution.py:24
  50.1 10.2 %collective-permute-start.19 = (bf16[256,512]{1,0:T(8,128)(2,1)S(1)}, bf16[256,512]{1,0:T(8,128)(2,1)S(1)}, u32[]{:S(2)}, u32[]{:S(2)}) collective-permute-start(bf16[256,512]{1,0:T(8,128)(2,1)S(1)} %fusion.2.refs_0_), channel_id=1, source_target_pairs={{0,6},{1,7},{2,4},{3,5},{4,2},{5,3},{6,0},{7,1},{8,14},{9,15},{10,... | collective-permute-start | bytes 786440 | tf_op jit(solution)/shard_map/ppermute | solution.py:24
  51.7 13.3 %collective-permute-start.18 = (bf16[256,512]{1,0:T(8,128)(2,1)S(1)}, bf16[256,512]{1,0:T(8,128)(2,1)S(1)}, u32[]{:S(2)}, u32[]{:S(2)}) collective-permute-start(bf16[256,512]{1,0:T(8,128)(2,1)S(1)} %fusion.2.refs_0_), channel_id=1, source_target_pairs={{0,4},{1,5},{2,6},{3,7},{4,0},{5,1},{6,2},{7,3},{8,12},{9,13},{10,... | collective-permute-start | bytes 786440 | tf_op jit(solution)/shard_map/ppermute | solution.py:24
  52.5 12.6 %collective-permute-start.17 = (bf16[256,512]{1,0:T(8,128)(2,1)S(1)}, bf16[256,512]{1,0:T(8,128)(2,1)S(1)}, u32[]{:S(2)}, u32[]{:S(2)}) collective-permute-start(bf16[256,512]{1,0:T(8,128)(2,1)S(1)} %fusion.2.refs_0_), channel_id=1, source_target_pairs={{0,2},{1,3},{2,0},{3,1},{4,6},{5,7},{6,4},{7,5},{8,10},{9,11},{10,... | collective-permute-start | bytes 786440 | tf_op jit(solution)/shard_map/ppermute | solution.py:24
  56.1 9.5 %collective-permute-start.29 = (bf16[128,1024]{1,0:T(8,128)(2,1)S(1)}, bf16[128,1024]{1,0:T(8,128)(2,1)S(1)}, u32[]{:S(2)}, u32[]{:S(2)}) collective-permute-start(bf16[128,1024]{1,0:T(8,128)(2,1)S(1)} %get-tuple-element.55), channel_id=1, source_target_pairs={{0,8},{8,0},{16,24},{24,16},{1,9},{9,1},{17,25},{25,17},{2,10},{10... | collective-permute-start | bytes 786440 | tf_op jit(solution)/shard_map/ppermute | solution.py:24
  57.8 8.0 %collective-permute-start.20 = (bf16[256,512]{1,0:T(8,128)(2,1)S(1)}, bf16[256,512]{1,0:T(8,128)(2,1)S(1)}, u32[]{:S(2)}, u32[]{:S(2)}) collective-permute-start(bf16[256,512]{1,0:T(8,128)(2,1)S(1)} %fusion.2.refs_0_), channel_id=1, source_target_pairs={{0,1},{1,0},{2,3},{3,2},{4,5},{5,4},{6,7},{7,6},{8,9},{9,8},{10,11... | collective-permute-start | bytes 786440 | tf_op jit(solution)/shard_map/ppermute | solution.py:24
  60.3 9.7 %collective-permute-start.26 = (bf16[128,1024]{1,0:T(8,128)(2,1)S(1)}, bf16[128,1024]{1,0:T(8,128)(2,1)S(1)}, u32[]{:S(2)}, u32[]{:S(2)}) collective-permute-start(bf16[128,1024]{1,0:T(8,128)(2,1)S(1)} %get-tuple-element.50), channel_id=1, source_target_pairs={{0,8},{8,0},{16,24},{24,16},{1,9},{9,1},{17,25},{25,17},{2,10},{10... | collective-permute-start | bytes 786440 | tf_op jit(solution)/shard_map/ppermute | solution.py:24
  65.1 4.9 %collective-permute-start.23 = (bf16[256,512]{1,0:T(8,128)(2,1)S(1)}, bf16[256,512]{1,0:T(8,128)(2,1)S(1)}, u32[]{:S(2)}, u32[]{:S(2)}) collective-permute-start(bf16[256,512]{1,0:T(8,128)(2,1)S(1)} %collective-permute-done.19.refs_3_), channel_id=1, source_target_pairs={{0,1},{1,0},{2,3},{3,2},{4,5},{5,4},{6,7},{7,6},{8,9},{9,8},{10,11... | collective-permute-start | bytes 786440 | tf_op jit(solution)/shard_map/ppermute | solution.py:24
  65.1 4.9 %collective-permute-start.22 = (bf16[256,512]{1,0:T(8,128)(2,1)S(1)}, bf16[256,512]{1,0:T(8,128)(2,1)S(1)}, u32[]{:S(2)}, u32[]{:S(2)}) collective-permute-start(bf16[256,512]{1,0:T(8,128)(2,1)S(1)} %collective-permute-done.18.refs_2_), channel_id=1, source_target_pairs={{0,1},{1,0},{2,3},{3,2},{4,5},{5,4},{6,7},{7,6},{8,9},{9,8},{10,11... | collective-permute-start | bytes 786440 | tf_op jit(solution)/shard_map/ppermute | solution.py:24
  65.6 4.4 %collective-permute-start.21 = (bf16[256,512]{1,0:T(8,128)(2,1)S(1)}, bf16[256,512]{1,0:T(8,128)(2,1)S(1)}, u32[]{:S(2)}, u32[]{:S(2)}) collective-permute-start(bf16[256,512]{1,0:T(8,128)(2,1)S(1)} %collective-permute-done.17.refs_1_), channel_id=1, source_target_pairs={{0,1},{1,0},{2,3},{3,2},{4,5},{5,4},{6,7},{7,6},{8,9},{9,8},{10,11... | collective-permute-start | bytes 786440 | tf_op jit(solution)/shard_map/ppermute | solution.py:24
  65.7 15.4 %copy-start.6 = (f32[2,128,1024]{2,1,0:T(8,128)S(1)}, f32[2,128,1024]{2,1,0:T(8,128)}, u32[]{:S(2)}) copy-start(f32[2,128,1024]{2,1,0:T(8,128)} %param.10) | copy-start | bytes 3145732
  65.7 15.4 %copy-start.7 = (f32[2,128,1024]{2,1,0:T(8,128)S(1)}, f32[2,128,1024]{2,1,0:T(8,128)}, u32[]{:S(2)}) copy-start(f32[2,128,1024]{2,1,0:T(8,128)} %param.9) | copy-start | bytes 3145732
  65.8 15.3 %collective-permute-start.30 = (bf16[128,1024]{1,0:T(8,128)(2,1)S(1)}, bf16[128,1024]{1,0:T(8,128)(2,1)S(1)}, u32[]{:S(2)}, u32[]{:S(2)}) collective-permute-start(bf16[128,1024]{1,0:T(8,128)(2,1)S(1)} %add_convert_fusion), channel_id=1, source_target_pairs={{0,16},{8,24},{16,0},{24,8},{1,17},{9,25},{17,1},{25,9},{2,18},{10... | collective-permute-start | bytes 786440 | tf_op jit(solution)/shard_map/ppermute | solution.py:24
  71.8 14.5 %collective-permute-start.27 = (bf16[128,1024]{1,0:T(8,128)(2,1)S(1)}, bf16[128,1024]{1,0:T(8,128)(2,1)S(1)}, u32[]{:S(2)}, u32[]{:S(2)}) collective-permute-start(bf16[128,1024]{1,0:T(8,128)(2,1)S(1)} %get-tuple-element.51), channel_id=1, source_target_pairs={{0,8},{8,0},{16,24},{24,16},{1,9},{9,1},{17,25},{25,17},{2,10},{10... | collective-permute-start | bytes 786440 | tf_op jit(solution)/shard_map/ppermute | solution.py:24
  82.3 23.5 %collective-permute-start.33 = (bf16[128,1024]{1,0:T(8,128)(2,1)S(1)}, bf16[128,1024]{1,0:T(8,128)(2,1)S(1)}, u32[]{:S(2)}, u32[]{:S(2)}) collective-permute-start(bf16[128,1024]{1,0:T(8,128)(2,1)S(1)} %get-tuple-element.63), channel_id=1, source_target_pairs={{0,8},{8,0},{16,24},{24,16},{1,9},{9,1},{17,25},{25,17},{2,10},{10... | collective-permute-start | bytes 786440 | tf_op jit(solution)/shard_map/ppermute | solution.py:24
  82.3 21.5 %collective-permute-start.31 = (bf16[128,1024]{1,0:T(8,128)(2,1)S(1)}, bf16[128,1024]{1,0:T(8,128)(2,1)S(1)}, u32[]{:S(2)}, u32[]{:S(2)}) collective-permute-start(bf16[128,1024]{1,0:T(8,128)(2,1)S(1)} %get-tuple-element.63), channel_id=1, source_target_pairs={{0,16},{8,24},{16,0},{24,8},{1,17},{9,25},{17,1},{25,9},{2,18},{10... | collective-permute-start | bytes 786440 | tf_op jit(solution)/shard_map/ppermute | solution.py:24
  86.4 21.5 %collective-permute-start.28 = (bf16[128,1024]{1,0:T(8,128)(2,1)S(1)}, bf16[128,1024]{1,0:T(8,128)(2,1)S(1)}, u32[]{:S(2)}, u32[]{:S(2)}) collective-permute-start(bf16[128,1024]{1,0:T(8,128)(2,1)S(1)} %add_convert_fusion.1), channel_id=1, source_target_pairs={{0,16},{8,24},{16,0},{24,8},{1,17},{9,25},{17,1},{25,9},{2,18},{10... | collective-permute-start | bytes 786440 | tf_op jit(solution)/shard_map/ppermute | solution.py:24
  103.8 12.7 %copy-start.9 = (bf16[128,1024]{1,0:T(8,128)(2,1)}, bf16[128,1024]{1,0:T(8,128)(2,1)S(1)}, u32[]{:S(2)}) copy-start(bf16[128,1024]{1,0:T(8,128)(2,1)S(1)} %collective-permute-done.31) | copy-start | bytes 786436
  103.8 7.5 %collective-permute-start.32 = (bf16[128,1024]{1,0:T(8,128)(2,1)S(1)}, bf16[128,1024]{1,0:T(8,128)(2,1)S(1)}, u32[]{:S(2)}, u32[]{:S(2)}) collective-permute-start(bf16[128,1024]{1,0:T(8,128)(2,1)S(1)} %collective-permute-done.31), channel_id=1, source_target_pairs={{0,8},{8,0},{16,24},{24,16},{1,9},{9,1},{17,25},{25,17},{2,10},{10... | collective-permute-start | bytes 786440 | tf_op jit(solution)/shard_map/ppermute | solution.py:24
  103.8 11.4 %collective-permute-start.34 = (bf16[128,1024]{1,0:T(8,128)(2,1)S(1)}, bf16[128,1024]{1,0:T(8,128)(2,1)S(1)}, u32[]{:S(2)}, u32[]{:S(2)}) collective-permute-start(bf16[128,1024]{1,0:T(8,128)(2,1)S(1)} %get-tuple-element.60), channel_id=1, source_target_pairs={{0,8},{8,0},{16,24},{24,16},{1,9},{9,1},{17,25},{25,17},{2,10},{10... | collective-permute-start | bytes 786440 | tf_op jit(solution)/shard_map/ppermute | solution.py:24
  111.3 5.2 %copy-start.10 = (bf16[128,1024]{1,0:T(8,128)(2,1)}, bf16[128,1024]{1,0:T(8,128)(2,1)S(1)}, u32[]{:S(2)}) copy-start(bf16[128,1024]{1,0:T(8,128)(2,1)S(1)} %collective-permute-done.32) | copy-start | bytes 786436
  116.5 9.1 %collective-permute-start.35 = (bf16[128,1024]{1,0:T(8,128)(2,1)S(1)}, bf16[128,1024]{1,0:T(8,128)(2,1)}, u32[]{:S(2)}, u32[]{:S(2)}) collective-permute-start(bf16[128,1024]{1,0:T(8,128)(2,1)S(1)} %get-tuple-element.67), channel_id=1, source_target_pairs={{0,16},{8,24},{16,0},{24,8},{1,17},{9,25},{17,1},{25,9},{2,18},{10... | collective-permute-start | bytes 786440 | tf_op jit(solution)/shard_map/ppermute | solution.py:24
  116.5 10.6 %copy-start.2 = (f32[1,128,1024]{2,1,0:T(8,128)S(1)}, f32[1,128,1024]{2,1,0:T(8,128)}, u32[]{:S(2)}) copy-start(f32[1,128,1024]{2,1,0:T(8,128)} %get-tuple-element.65) | copy-start | bytes 1572868
  116.5 10.6 %copy-start.3 = (f32[1,128,1024]{2,1,0:T(8,128)S(1)}, f32[1,128,1024]{2,1,0:T(8,128)}, u32[]{:S(2)}) copy-start(f32[1,128,1024]{2,1,0:T(8,128)} %get-tuple-element.66) | copy-start | bytes 1572868
  116.5 10.6 %copy-start.4 = (f32[1,128,1024]{2,1,0:T(8,128)S(1)}, f32[1,128,1024]{2,1,0:T(8,128)}, u32[]{:S(2)}) copy-start(f32[1,128,1024]{2,1,0:T(8,128)} %get-tuple-element.68) | copy-start | bytes 1572868
  116.5 12.1 %collective-permute-start.37 = (bf16[128,1024]{1,0:T(8,128)(2,1)S(1)}, bf16[128,1024]{1,0:T(8,128)(2,1)S(1)}, u32[]{:S(2)}, u32[]{:S(2)}) collective-permute-start(bf16[128,1024]{1,0:T(8,128)(2,1)S(1)} %get-tuple-element.67), channel_id=1, source_target_pairs={{0,8},{8,0},{16,24},{24,16},{1,9},{9,1},{17,25},{25,17},{2,10},{10... | collective-permute-start | bytes 786440 | tf_op jit(solution)/shard_map/ppermute | solution.py:24
  125.6 6.6 %collective-permute-start.36 = (bf16[128,1024]{1,0:T(8,128)(2,1)}, bf16[128,1024]{1,0:T(8,128)(2,1)S(1)}, u32[]{:S(2)}, u32[]{:S(2)}) collective-permute-start(bf16[128,1024]{1,0:T(8,128)(2,1)} %collective-permute-done.35), channel_id=1, source_target_pairs={{0,8},{8,0},{16,24},{24,16},{1,9},{9,1},{17,25},{25,17},{2,10},{10... | collective-permute-start | bytes 786440 | tf_op jit(solution)/shard_map/ppermute | solution.py:24

commit v7 on v6

--- a/solution.py
+++ b/solution.py
@@ -345,7 +345,8 @@
     arrived_1 = [swap(piece, "dp", dp_bits[0]) for piece in send_1]
 
     updates, firsts, seconds, gathered = [], [], [], []
-    for matrix, (keep, received) in enumerate((open_0, reduced(arrived_1, keep_1))):
+    open_1 = list(reduced(arrived_1, keep_1))
+    for matrix, (keep, received) in enumerate((open_0, open_1)):
         if gathered:
             received, firsts[0], *gathered[0][:-1] = lax.optimization_barrier(
                 (received, firsts[0], *gathered[0][:-1])
@@ -360,6 +361,8 @@
         )
         parts = [direction.astype(jnp.bfloat16)]
         for bit in reversed(dp_bits):
+            if matrix == 0 and bit == dp_bits[0] and len(parts) > 1:
+                parts[0], open_1[0] = lax.optimization_barrier((parts[0], open_1[0]))
             parts = [swap(piece, "dp", bit) for piece in parts] + parts
         gathered.append(parts)
         firsts.append(first)

time: 135 us -> 140 us (1.037)
  waiting for transfers between devices: 68.3 us -> 71.9 us
    ppermute x38, waiting for transfers between devices: 68.3 us -> 71.9 us  [swap(): return lax.ppermute(value, axis, [(i, i ^ mask) for i in range(size)])]
  transfers between devices with their start and end apart: 38 -> 38, of which waited for: 14 -> 13; matrix products, arithmetic and copies ran while one was open for 7% -> 7% of each run, Pallas kernels for 10% -> 10%
where the time goes in v7:
time: 140 us; the launch traced here: 139 us
  waiting for transfers between devices  71.9 us (51%)
  starting transfers between devices  36.2 us (26%)
  Pallas kernels  13.8 us (10%)
  other arithmetic  8.16 us (6%)
  local copies, waits for them, and re-layouts  4.71 us (3%)
  matrix products  3.41 us (2%)
    ppermute x38, waiting for transfers between devices, swap(): return lax.ppermute(value, axis, [(i, i ^ mask) for i in range(size)])  71.9 us
    ppermute x38, starting transfers between devices, swap(): return lax.ppermute(value, axis, [(i, i ^ mask) for i in range(size)])  36.2 us
    pallas_call x4, Pallas kernels, call_in_vmem(): pl.pallas_call(body, grid_spec=pltpu.PrefetchScalarGridSpec(num_scalar_pr...  7.26 us
    pallas_call x1, Pallas kernels, add_products(): pl.pallas_call(functools.partial(product_body, shape), grid_spec=pltpu.Pr...  5.8 us
    dot_general x2, matrix products, on_device(): lax.dot_general(own, jnp.concatenate(parts, axis=0), TRANSPOSED, preferre...  2.93 us
  transfers between devices with their start and end apart: 38, of which 13 were waited for; matrix products, arithmetic and copies ran while one was open for 7% of the time, Pallas kernels for 10%

profile of v7, /device:TPU:0, one launch (start us, length us, event | category | flops | bytes accessed | tf_op | source)
XLA Modules:
  0.0 139.2 jit_solution(11830925757751400972)
XLA Ops:
  0.6 1.1 slice_bitcast_fusion.1
  1.7 3.0 %collective-permute-start.2 = (bf16[128,1024]{1,0:T(8,128)(2,1)S(1)}, bf16[128,1024]{1,0:T(8,128)(2,1)S(1)}, u32[]{:S(2)}, u32[]{:S(2)}) collective-permute-start(bf16[128,1024]{1,0:T(8,128)(2,1)S(1)} %get-tuple-element.36), channel_id=1, source_target_pairs={{0,4},{1,5},{2,6},{3,7},{4,0},{5,1},{6,2},{7,3},{8,12},{9,13},{10,... | collective-permute-start | bytes 786440 | tf_op jit(solution)/shard_map/ppermute | solution.py:24
  4.7 1.6 %collective-permute-start = (bf16[128,1024]{1,0:T(8,128)(2,1)}, bf16[128,1024]{1,0:T(8,128)(2,1)S(1)}, u32[]{:S(2)}, u32[]{:S(2)}) collective-permute-start(bf16[128,1024]{1,0:T(8,128)(2,1)} %bitcast.53), channel_id=1, source_target_pairs={{0,8},{8,0},{16,24},{24,16},{1,9},{9,1},{17,25},{25,17},{2,10},{10... | collective-permute-start | bytes 786440 | tf_op jit(solution)/shard_map/ppermute | solution.py:24
  6.3 1.5 %collective-permute-start.1 = (bf16[128,1024]{1,0:T(8,128)(2,1)S(1)}, bf16[128,1024]{1,0:T(8,128)(2,1)S(1)}, u32[]{:S(2)}, u32[]{:S(2)}) collective-permute-start(bf16[128,1024]{1,0:T(8,128)(2,1)S(1)} %get-tuple-element.37), channel_id=1, source_target_pairs={{0,2},{1,3},{2,0},{3,1},{4,6},{5,7},{6,4},{7,5},{8,10},{9,11},{10,... | collective-permute-start | bytes 786440 | tf_op jit(solution)/shard_map/ppermute | solution.py:24
  7.8 0.7 and_compare_fusion.1
  8.5 0.1 broadcast_in_dim.33
  8.5 0.1 broadcast_in_dim.34
  8.6 2.4 %collective-permute-done.2.refs_4_ = bf16[128,1024]{1,0:T(8,128)(2,1)S(1)} collective-permute-done((bf16[128,1024]{1,0:T(8,128)(2,1)S(1)}, bf16[128,1024]{1,0:T(8,128)(2,1)S(1)}, u32[]{:S(2)}, u32[]{:S(2)}) %collective-permute-start.2) | collective-permute-done | bytes 262176 | tf_op jit(solution)/shard_map/ppermute | solution.py:24
  11.0 1.7 %collective-permute-start.5 = (bf16[128,1024]{1,0:T(8,128)(2,1)S(1)}, bf16[128,1024]{1,0:T(8,128)(2,1)S(1)}, u32[]{:S(2)}, u32[]{:S(2)}) collective-permute-start(bf16[128,1024]{1,0:T(8,128)(2,1)S(1)} %get-tuple-element.37), channel_id=1, source_target_pairs={{0,4},{1,5},{2,6},{3,7},{4,0},{5,1},{6,2},{7,3},{8,12},{9,13},{10,... | collective-permute-start | bytes 786440 | tf_op jit(solution)/shard_map/ppermute | solution.py:24
  12.8 1.0 broadcast_select_fusion
  13.9 2.7 %collective-permute-start.3 = (bf16[128,1024]{1,0:T(8,128)(2,1)S(1)}, bf16[128,1024]{1,0:T(8,128)(2,1)}, u32[]{:S(2)}, u32[]{:S(2)}) collective-permute-start(bf16[128,1024]{1,0:T(8,128)(2,1)S(1)} %broadcast_select_fusion), channel_id=1, source_target_pairs={{0,16},{8,24},{16,0},{24,8},{1,17},{9,25},{17,1},{25,9},{2,18},{10... | collective-permute-start | bytes 786440 | tf_op jit(solution)/shard_map/ppermute | solution.py:24
  16.5 1.5 %collective-permute-start.4 = (bf16[128,1024]{1,0:T(8,128)(2,1)S(1)}, bf16[128,1024]{1,0:T(8,128)(2,1)S(1)}, u32[]{:S(2)}, u32[]{:S(2)}) collective-permute-start(bf16[128,1024]{1,0:T(8,128)(2,1)S(1)} %get-tuple-element.36), channel_id=1, source_target_pairs={{0,2},{1,3},{2,0},{3,1},{4,6},{5,7},{6,4},{7,5},{8,10},{9,11},{10,... | collective-permute-start | bytes 786440 | tf_op jit(solution)/shard_map/ppermute | solution.py:24
  18.0 0.5 collective-permute-start.7
  18.5 0.5 collective-permute-start.6
  19.1 1.1 slice_bitcast_fusion.refs_0_
  20.2 8.5 %collective-permute-done.7.refs_1_ = bf16[128,1024]{1,0:T(8,128)(2,1)S(1)} collective-permute-done((bf16[128,1024]{1,0:T(8,128)(2,1)S(1)}, bf16[128,1024]{1,0:T(8,128)(2,1)S(1)}, u32[]{:S(2)}, u32[]{:S(2)}) %collective-permute-start.7) | collective-permute-done | bytes 262176 | tf_op jit(solution)/shard_map/ppermute | solution.py:24
  28.8 0.5 collective-permute-start.12
  29.3 0.1 collective-permute-start.14
  29.4 0.4 collective-permute-start.13
  29.9 0.1 broadcast_in_dim.31
  30.0 1.1 broadcast_select_fusion.1
  31.2 1.5 %collective-permute-start.10 = (bf16[128,1024]{1,0:T(8,128)(2,1)S(1)}, bf16[128,1024]{1,0:T(8,128)(2,1)S(1)}, u32[]{:S(2)}, u32[]{:S(2)}) collective-permute-start(bf16[128,1024]{1,0:T(8,128)(2,1)S(1)} %broadcast_select_fusion.1), channel_id=1, source_target_pairs={{0,6},{1,7},{2,4},{3,5},{4,2},{5,3},{6,0},{7,1},{8,14},{9,15},{10,... | collective-permute-start | bytes 786440 | tf_op jit(solution)/shard_map/ppermute | solution.py:24
  32.7 1.5 %collective-permute-start.9 = (bf16[128,1024]{1,0:T(8,128)(2,1)S(1)}, bf16[128,1024]{1,0:T(8,128)(2,1)S(1)}, u32[]{:S(2)}, u32[]{:S(2)}) collective-permute-start(bf16[128,1024]{1,0:T(8,128)(2,1)S(1)} %broadcast_select_fusion.1), channel_id=1, source_target_pairs={{0,4},{1,5},{2,6},{3,7},{4,0},{5,1},{6,2},{7,3},{8,12},{9,13},{10,... | collective-permute-start | bytes 786440 | tf_op jit(solution)/shard_map/ppermute | solution.py:24
  34.2 0.5 collective-permute-start.8
  34.8 2.2 %copy-done = bf16[2048,1024]{1,0:T(8,128)(2,1)S(1)} copy-done((bf16[2048,1024]{1,0:T(8,128)(2,1)S(1)}, bf16[2048,1024]{1,0:T(8,128)(2,1)}, u32[]{:S(2)}) %copy-start) | copy-done | bytes 4194328
  36.9 5.8 %shard_map.85.refs_5_ = f32[1024,1024]{1,0:T(8,128)S(1)} custom-call(s32[2]{0:T(128)S(1)} %pad_add_fusion.here, bf16[256,1024]{1,0:T(8,128)(2,1)S(1)} %slice_bitcast_fusion.refs_0_, bf16[128,1024]{1,0:T(8,128)(2,1)S(1)} %collective-permute-done.1.refs_1_, bf16[128,1024]{1,0:T(8,128)(2,1)S(1)} %collective-permute-done.4.refs_2_, ...), custom_call_target="tpu_custom_call" | custom-call | flops 3221225472 | bytes 10485760 | tf_op jit(solution)/shard_map/pallas_call | solution.py:209
  42.8 3.3 %collective-permute-done.9 = bf16[128,1024]{1,0:T(8,128)(2,1)S(1)} collective-permute-done((bf16[128,1024]{1,0:T(8,128)(2,1)S(1)}, bf16[128,1024]{1,0:T(8,128)(2,1)S(1)}, u32[]{:S(2)}, u32[]{:S(2)}) %collective-permute-start.9) | collective-permute-done | bytes 262176 | tf_op jit(solution)/shard_map/ppermute | solution.py:24
  46.1 0.1 collective-permute-start.16
  46.2 0.5 collective-permute-start.25
  46.7 0.1 collective-permute-start.24
  46.8 2.1 %collective-permute-done.16.other = bf16[512,1024]{1,0:T(8,128)(2,1)S(1)} collective-permute-done((bf16[512,1024]{1,0:T(8,128)(2,1)S(1)}, bf16[512,1024]{1,0:T(8,128)(2,1)S(1)}, u32[]{:S(2)}, u32[]{:S(2)}) %collective-permute-start.16) | collective-permute-done | bytes 1048608 | tf_op jit(solution)/shard_map/ppermute | solution.py:24
  48.9 0.8 shard_map.86
  49.7 0.5 fusion.2.refs_0_
  50.1 1.6 %collective-permute-start.19 = (bf16[256,512]{1,0:T(8,128)(2,1)S(1)}, bf16[256,512]{1,0:T(8,128)(2,1)S(1)}, u32[]{:S(2)}, u32[]{:S(2)}) collective-permute-start(bf16[256,512]{1,0:T(8,128)(2,1)S(1)} %fusion.2.refs_0_), channel_id=1, source_target_pairs={{0,6},{1,7},{2,4},{3,5},{4,2},{5,3},{6,0},{7,1},{8,14},{9,15},{10,... | collective-permute-start | bytes 786440 | tf_op jit(solution)/shard_map/ppermute | solution.py:24
  51.7 0.7 collective-permute-start.18
  52.5 1.2 collective-permute-start.17
  53.7 2.4 %shard_map.88 = (bf16[1024,1024]{1,0:T(8,128)(2,1)S(1)}, bf16[128,1024]{1,0:T(8,128)(2,1)S(1)}, bf16[128,1024]{1,0:T(8,128)(2,1)S(1)}) custom-call(s32[2]{0:T(128)S(1)} %pad_add_fusion.here, bf16[128,1024]{1,0:T(8,128)(2,1)S(1)} %collective-permute-done.6.refs_0_, bf16[128,1024]{1,0:T(8,128)(2,1)S(1)} %collective-permute-done.7.refs_1_, ...), custom_call_target="tpu_custom_call" | custom-call | flops 1610612736 | bytes 13107200 | tf_op jit(solution)/shard_map/pallas_call | solution.py:131
  56.1 1.6 %collective-permute-start.29 = (bf16[128,1024]{1,0:T(8,128)(2,1)S(1)}, bf16[128,1024]{1,0:T(8,128)(2,1)S(1)}, u32[]{:S(2)}, u32[]{:S(2)}) collective-permute-start(bf16[128,1024]{1,0:T(8,128)(2,1)S(1)} %get-tuple-element.57), channel_id=1, source_target_pairs={{0,8},{8,0},{16,24},{24,16},{1,9},{9,1},{17,25},{25,17},{2,10},{10... | collective-permute-start | bytes 786440 | tf_op jit(solution)/shard_map/ppermute | solution.py:24
  57.8 1.2 shard_map.90
  59.0 1.3 collective-permute-done.19.refs_3_
  60.3 1.6 %collective-permute-start.26 = (bf16[128,1024]{1,0:T(8,128)(2,1)S(1)}, bf16[128,1024]{1,0:T(8,128)(2,1)S(1)}, u32[]{:S(2)}, u32[]{:S(2)}) collective-permute-start(bf16[128,1024]{1,0:T(8,128)(2,1)S(1)} %get-tuple-element.52), channel_id=1, source_target_pairs={{0,8},{8,0},{16,24},{24,16},{1,9},{9,1},{17,25},{25,17},{2,10},{10... | collective-permute-start | bytes 786440 | tf_op jit(solution)/shard_map/ppermute | solution.py:24
  61.9 3.2 %collective-permute-done.18.refs_2_ = bf16[256,512]{1,0:T(8,128)(2,1)S(1)} collective-permute-done((bf16[256,512]{1,0:T(8,128)(2,1)S(1)}, bf16[256,512]{1,0:T(8,128)(2,1)S(1)}, u32[]{:S(2)}, u32[]{:S(2)}) %collective-permute-start.18) | collective-permute-done | bytes 262176 | tf_op jit(solution)/shard_map/ppermute | solution.py:24
  65.1 0.5 collective-permute-start.22
  65.8 0.4 collective-permute-start.30
  66.2 3.8 %collective-permute-done.26.refs_9_ = bf16[128,1024]{1,0:T(8,128)(2,1)S(1)} collective-permute-done((bf16[128,1024]{1,0:T(8,128)(2,1)S(1)}, bf16[128,1024]{1,0:T(8,128)(2,1)S(1)}, u32[]{:S(2)}, u32[]{:S(2)}) %collective-permute-start.26) | collective-permute-done | bytes 262176 | tf_op jit(solution)/shard_map/ppermute | solution.py:24
  70.0 1.8 %shard_map.89 = (bf16[128,1024]{1,0:T(8,128)(2,1)S(1)}, bf16[128,1024]{1,0:T(8,128)(2,1)S(1)}) custom-call(s32[2]{0:T(128)S(1)} %pad_add_fusion.here, bf16[256,512]{1,0:T(8,128)(2,1)S(1)} %fusion.2.refs_0_, bf16[256,512]{1,0:T(8,128)(2,1)S(1)} %collective-permute-done.17.refs_1_, bf16[256,512]{1,0:T(8,128)(2,1)S(1)} %collective-permute-done.18.refs_2_, ...), custom_call_target="tpu_custom_call" | custom-call | flops 1073741824 | bytes 6815744 | tf_op jit(solution)/shard_map/pallas_call | solution.py:131
  71.8 2.5 %collective-permute-start.27 = (bf16[128,1024]{1,0:T(8,128)(2,1)S(1)}, bf16[128,1024]{1,0:T(8,128)(2,1)S(1)}, u32[]{:S(2)}, u32[]{:S(2)}) collective-permute-start(bf16[128,1024]{1,0:T(8,128)(2,1)S(1)} %get-tuple-element.53), channel_id=1, source_target_pairs={{0,8},{8,0},{16,24},{24,16},{1,9},{9,1},{17,25},{25,17},{2,10},{10... | collective-permute-start | bytes 786440 | tf_op jit(solution)/shard_map/ppermute | solution.py:24
  74.4 6.7 %collective-permute-done.30 = bf16[128,1024]{1,0:T(8,128)(2,1)S(1)} collective-permute-done((bf16[128,1024]{1,0:T(8,128)(2,1)S(1)}, bf16[128,1024]{1,0:T(8,128)(2,1)S(1)}, u32[]{:S(2)}, u32[]{:S(2)}) %collective-permute-start.30) | collective-permute-done | bytes 262176 | tf_op jit(solution)/shard_map/ppermute | solution.py:24
  81.1 1.2 divide_convert_fusion.1
  82.3 2.3 %collective-permute-start.31 = (bf16[128,1024]{1,0:T(8,128)(2,1)S(1)}, bf16[128,1024]{1,0:T(8,128)(2,1)}, u32[]{:S(2)}, u32[]{:S(2)}) collective-permute-start(bf16[128,1024]{1,0:T(8,128)(2,1)S(1)} %get-tuple-element.67), channel_id=1, source_target_pairs={{0,16},{8,24},{16,0},{24,8},{1,17},{9,25},{17,1},{25,9},{2,18},{10... | collective-permute-start | bytes 786440 | tf_op jit(solution)/shard_map/ppermute | solution.py:24
  84.6 1.8 %shard_map.87 = (f32[128,1024]{1,0:T(8,128)S(1)}, f32[128,1024]{1,0:T(8,128)S(1)}) custom-call(s32[2]{0:T(128)S(1)} %pad_add_fusion.here, bf16[256,512]{1,0:T(8,128)(2,1)S(1)} %fusion.2.refs_0_, bf16[256,512]{1,0:T(8,128)(2,1)S(1)} %collective-permute-done.17.refs_1_, bf16[256,512]{1,0:T(8,128)(2,1)S(1)} %collective-permute-done.18.refs_2_, ...), custom_call_target="tpu_custom_call" | custom-call | flops 1073741824 | bytes 7340032 | tf_op jit(solution)/shard_map/pallas_call | solution.py:131
  86.5 2.7 %collective-permute-start.28 = (bf16[128,1024]{1,0:T(8,128)(2,1)S(1)}, bf16[128,1024]{1,0:T(8,128)(2,1)S(1)}, u32[]{:S(2)}, u32[]{:S(2)}) collective-permute-start(bf16[128,1024]{1,0:T(8,128)(2,1)S(1)} %add_convert_fusion.1), channel_id=1, source_target_pairs={{0,16},{8,24},{16,0},{24,8},{1,17},{9,25},{17,1},{25,9},{2,18},{10... | collective-permute-start | bytes 786440 | tf_op jit(solution)/shard_map/ppermute | solution.py:24
  89.2 17.1 %collective-permute-done.32 = bf16[128,1024]{1,0:T(8,128)(2,1)S(1)} collective-permute-done((bf16[128,1024]{1,0:T(8,128)(2,1)S(1)}, bf16[128,1024]{1,0:T(8,128)(2,1)S(1)}, u32[]{:S(2)}, u32[]{:S(2)}) %collective-permute-start.32) | collective-permute-done | bytes 262176 | tf_op jit(solution)/shard_map/ppermute | solution.py:24
  106.4 1.5 %collective-permute-done.28 = bf16[128,1024]{1,0:T(8,128)(2,1)S(1)} collective-permute-done((bf16[128,1024]{1,0:T(8,128)(2,1)S(1)}, bf16[128,1024]{1,0:T(8,128)(2,1)S(1)}, u32[]{:S(2)}, u32[]{:S(2)}) %collective-permute-start.28) | collective-permute-done | bytes 262176 | tf_op jit(solution)/shard_map/ppermute | solution.py:24
  107.9 6.1 %collective-permute-done.33 = bf16[128,1024]{1,0:T(8,128)(2,1)} collective-permute-done((bf16[128,1024]{1,0:T(8,128)(2,1)}, bf16[128,1024]{1,0:T(8,128)(2,1)}, u32[]{:S(2)}, u32[]{:S(2)}) %collective-permute-start.33) | collective-permute-done | bytes 262176 | tf_op jit(solution)/shard_map/ppermute | solution.py:24
  114.0 1.3 fusion.28
  115.3 0.8 collective-permute-start.35
  116.1 1.7 %collective-permute-start.37 = (bf16[128,1024]{1,0:T(8,128)(2,1)S(1)}, bf16[128,1024]{1,0:T(8,128)(2,1)S(1)}, u32[]{:S(2)}, u32[]{:S(2)}) collective-permute-start(bf16[128,1024]{1,0:T(8,128)(2,1)S(1)} %get-tuple-element.71), channel_id=1, source_target_pairs={{0,8},{8,0},{16,24},{24,16},{1,9},{9,1},{17,25},{25,17},{2,10},{10... | collective-permute-start | bytes 786440 | tf_op jit(solution)/shard_map/ppermute | solution.py:24
  117.8 10.5 %collective-permute-done.35 = bf16[128,1024]{1,0:T(8,128)(2,1)} collective-permute-done((bf16[128,1024]{1,0:T(8,128)(2,1)S(1)}, bf16[128,1024]{1,0:T(8,128)(2,1)}, u32[]{:S(2)}, u32[]{:S(2)}) %collective-permute-start.35) | collective-permute-done | bytes 262176 | tf_op jit(solution)/shard_map/ppermute | solution.py:24
  128.3 1.5 %fusion = bf16[1,256,1024]{2,1,0:T(8,128)(2,1)S(1)} fusion(bf16[128,1024]{1,0:T(8,128)(2,1)S(1)} %get-tuple-element.67, bf16[128,1024]{1,0:T(8,128)(2,1)} %collective-permute-done.31, bf16[128,1024]{1,0:T(8,128)(2,1)S(1)} %collective-permute-done.34, bf16[128,1024]{1,0:T(8,128)(2,1)} %collective-permute-done.33, ...), kind=kOutput, calls=%fused_computation.2 | convolution fusion | flops 272891904 | bytes 1835012 | tf_op jit(solution)/shard_map/dot_general | solution.py:372
  129.8 1.5 %pad_maximum_fusion.2 = (f32[2,128,1024]{2,1,0:T(8,128)}, f32[2,128,1024]{2,1,0:T(8,128)}) fusion(f32[1,128,1024]{2,1,0:T(8,128)S(1)} %copy-done.4, f32[1,128,1024]{2,1,0:T(8,128)S(1)} %bitcast.52, f32[1,128,1024]{2,1,0:T(8,128)S(1)} %copy-done.3, f32[1,128,1024]{2,1,0:T(8,128)S(1)} %copy-done.2), kind=kLoop, calls=%fused_computation.22 | loop fusion | flops 524288 | bytes 4194304 | tf_op jit(solution)/shard_map/stack | solution.py:379
  131.3 5.4 %collective-permute-done.36 = bf16[128,1024]{1,0:T(8,128)(2,1)S(1)} collective-permute-done((bf16[128,1024]{1,0:T(8,128)(2,1)}, bf16[128,1024]{1,0:T(8,128)(2,1)S(1)}, u32[]{:S(2)}, u32[]{:S(2)}) %collective-permute-start.36) | collective-permute-done | bytes 262176 | tf_op jit(solution)/shard_map/ppermute | solution.py:24
  136.7 1.4 %fusion.1 = bf16[1,256,1024]{2,1,0:T(8,128)(2,1)S(1)} fusion(bf16[128,1024]{1,0:T(8,128)(2,1)S(1)} %get-tuple-element.71, bf16[128,1024]{1,0:T(8,128)(2,1)} %collective-permute-done.35, bf16[128,1024]{1,0:T(8,128)(2,1)S(1)} %collective-permute-done.37, bf16[128,1024]{1,0:T(8,128)(2,1)S(1)} %collective-permute-done.36, ...), kind=kOutput, calls=%fused_computation.3 | convolution fusion | flops 272891904 | bytes 1835012 | tf_op jit(solution)/shard_map/dot_general | solution.py:372
  138.2 1.1 pad_maximum_fusion.1
  (64 shorter events, 0.7 us)
Async XLA Ops:
  1.7 9.3 %collective-permute-start.2 = (bf16[128,1024]{1,0:T(8,128)(2,1)S(1)}, bf16[128,1024]{1,0:T(8,128)(2,1)S(1)}, u32[]{:S(2)}, u32[]{:S(2)}) collective-permute-start(bf16[128,1024]{1,0:T(8,128)(2,1)S(1)} %get-tuple-element.36), channel_id=1, source_target_pairs={{0,4},{1,5},{2,6},{3,7},{4,0},{5,1},{6,2},{7,3},{8,12},{9,13},{10,... | collective-permute-start | bytes 786440 | tf_op jit(solution)/shard_map/ppermute | solution.py:24
  4.7 8.1 %collective-permute-start = (bf16[128,1024]{1,0:T(8,128)(2,1)}, bf16[128,1024]{1,0:T(8,128)(2,1)S(1)}, u32[]{:S(2)}, u32[]{:S(2)}) collective-permute-start(bf16[128,1024]{1,0:T(8,128)(2,1)} %bitcast.53), channel_id=1, source_target_pairs={{0,8},{8,0},{16,24},{24,16},{1,9},{9,1},{17,25},{25,17},{2,10},{10... | collective-permute-start | bytes 786440 | tf_op jit(solution)/shard_map/ppermute | solution.py:24
  6.3 7.5 %collective-permute-start.1 = (bf16[128,1024]{1,0:T(8,128)(2,1)S(1)}, bf16[128,1024]{1,0:T(8,128)(2,1)S(1)}, u32[]{:S(2)}, u32[]{:S(2)}) collective-permute-start(bf16[128,1024]{1,0:T(8,128)(2,1)S(1)} %get-tuple-element.37), channel_id=1, source_target_pairs={{0,2},{1,3},{2,0},{3,1},{4,6},{5,7},{6,4},{7,5},{8,10},{9,11},{10,... | collective-permute-start | bytes 786440 | tf_op jit(solution)/shard_map/ppermute | solution.py:24
  11.0 9.1 %collective-permute-start.5 = (bf16[128,1024]{1,0:T(8,128)(2,1)S(1)}, bf16[128,1024]{1,0:T(8,128)(2,1)S(1)}, u32[]{:S(2)}, u32[]{:S(2)}) collective-permute-start(bf16[128,1024]{1,0:T(8,128)(2,1)S(1)} %get-tuple-element.37), channel_id=1, source_target_pairs={{0,4},{1,5},{2,6},{3,7},{4,0},{5,1},{6,2},{7,3},{8,12},{9,13},{10,... | collective-permute-start | bytes 786440 | tf_op jit(solution)/shard_map/ppermute | solution.py:24
  13.8 14.9 %copy-start.8 = (bf16[128,1024]{1,0:T(8,128)(2,1)}, bf16[128,1024]{1,0:T(8,128)(2,1)S(1)}, u32[]{:S(2)}) copy-start(bf16[128,1024]{1,0:T(8,128)(2,1)S(1)} %broadcast_select_fusion) | copy-start | bytes 786436
  13.9 14.9 %collective-permute-start.3 = (bf16[128,1024]{1,0:T(8,128)(2,1)S(1)}, bf16[128,1024]{1,0:T(8,128)(2,1)}, u32[]{:S(2)}, u32[]{:S(2)}) collective-permute-start(bf16[128,1024]{1,0:T(8,128)(2,1)S(1)} %broadcast_select_fusion), channel_id=1, source_target_pairs={{0,16},{8,24},{16,0},{24,8},{1,17},{9,25},{17,1},{25,9},{2,18},{10... | collective-permute-start | bytes 786440 | tf_op jit(solution)/shard_map/ppermute | solution.py:24
  16.5 12.8 %collective-permute-start.4 = (bf16[128,1024]{1,0:T(8,128)(2,1)S(1)}, bf16[128,1024]{1,0:T(8,128)(2,1)S(1)}, u32[]{:S(2)}, u32[]{:S(2)}) collective-permute-start(bf16[128,1024]{1,0:T(8,128)(2,1)S(1)} %get-tuple-element.36), channel_id=1, source_target_pairs={{0,2},{1,3},{2,0},{3,1},{4,6},{5,7},{6,4},{7,5},{8,10},{9,11},{10,... | collective-permute-start | bytes 786440 | tf_op jit(solution)/shard_map/ppermute | solution.py:24
  18.0 10.7 %collective-permute-start.7 = (bf16[128,1024]{1,0:T(8,128)(2,1)S(1)}, bf16[128,1024]{1,0:T(8,128)(2,1)S(1)}, u32[]{:S(2)}, u32[]{:S(2)}) collective-permute-start(bf16[128,1024]{1,0:T(8,128)(2,1)S(1)} %collective-permute-done.2.refs_4_), channel_id=1, source_target_pairs={{0,2},{1,3},{2,0},{3,1},{4,6},{5,7},{6,4},{7,5},{8,10},{9,11},{10,... | collective-permute-start | bytes 786440 | tf_op jit(solution)/shard_map/ppermute | solution.py:24
  18.5 10.8 %collective-permute-start.6 = (bf16[128,1024]{1,0:T(8,128)(2,1)S(1)}, bf16[128,1024]{1,0:T(8,128)(2,1)S(1)}, u32[]{:S(2)}, u32[]{:S(2)}) collective-permute-start(bf16[128,1024]{1,0:T(8,128)(2,1)S(1)} %collective-permute-done.1.refs_1_), channel_id=1, source_target_pairs={{0,4},{1,5},{2,6},{3,7},{4,0},{5,1},{6,2},{7,3},{8,12},{9,13},{10,... | collective-permute-start | bytes 786440 | tf_op jit(solution)/shard_map/ppermute | solution.py:24
  20.1 14.1 %collective-permute-start.11 = (bf16[256,1024]{1,0:T(8,128)(2,1)S(1)}, bf16[256,1024]{1,0:T(8,128)(2,1)S(1)}, u32[]{:S(2)}, u32[]{:S(2)}) collective-permute-start(bf16[256,1024]{1,0:T(8,128)(2,1)S(1)} %slice_bitcast_fusion.refs_0_), channel_id=1, source_target_pairs={{0,1},{1,0},{2,3},{3,2},{4,5},{5,4},{6,7},{7,6},{8,9},{9,8},{10,11... | collective-permute-start | bytes 1572872 | tf_op jit(solution)/shard_map/ppermute | solution.py:24
  28.8 2.4 %collective-permute-start.15 = (bf16[128,1024]{1,0:T(8,128)(2,1)S(1)}, bf16[128,1024]{1,0:T(8,128)(2,1)S(1)}, u32[]{:S(2)}, u32[]{:S(2)}) collective-permute-start(bf16[128,1024]{1,0:T(8,128)(2,1)S(1)} %collective-permute-done.2.refs_4_), channel_id=1, source_target_pairs={{0,1},{1,0},{2,3},{3,2},{4,5},{5,4},{6,7},{7,6},{8,9},{9,8},{10,11... | collective-permute-start | bytes 786440 | tf_op jit(solution)/shard_map/ppermute | solution.py:24
  28.8 3.9 %collective-permute-start.12 = (bf16[128,1024]{1,0:T(8,128)(2,1)S(1)}, bf16[128,1024]{1,0:T(8,128)(2,1)S(1)}, u32[]{:S(2)}, u32[]{:S(2)}) collective-permute-start(bf16[128,1024]{1,0:T(8,128)(2,1)S(1)} %collective-permute-done.1.refs_1_), channel_id=1, source_target_pairs={{0,1},{1,0},{2,3},{3,2},{4,5},{5,4},{6,7},{7,6},{8,9},{9,8},{10,11... | collective-permute-start | bytes 786440 | tf_op jit(solution)/shard_map/ppermute | solution.py:24
  29.3 5.5 %collective-permute-start.14 = (bf16[128,1024]{1,0:T(8,128)(2,1)S(1)}, bf16[128,1024]{1,0:T(8,128)(2,1)S(1)}, u32[]{:S(2)}, u32[]{:S(2)}) collective-permute-start(bf16[128,1024]{1,0:T(8,128)(2,1)S(1)} %collective-permute-done.5.refs_3_), channel_id=1, source_target_pairs={{0,1},{1,0},{2,3},{3,2},{4,5},{5,4},{6,7},{7,6},{8,9},{9,8},{10,11... | collective-permute-start | bytes 786440 | tf_op jit(solution)/shard_map/ppermute | solution.py:24
  29.4 5.4 %collective-permute-start.13 = (bf16[128,1024]{1,0:T(8,128)(2,1)S(1)}, bf16[128,1024]{1,0:T(8,128)(2,1)}, u32[]{:S(2)}, u32[]{:S(2)}) collective-permute-start(bf16[128,1024]{1,0:T(8,128)(2,1)S(1)} %collective-permute-done.4.refs_2_), channel_id=1, source_target_pairs={{0,1},{1,0},{2,3},{3,2},{4,5},{5,4},{6,7},{7,6},{8,9},{9,8},{10,11... | collective-permute-start | bytes 786440 | tf_op jit(solution)/shard_map/ppermute | solution.py:24
  31.2 11.6 %collective-permute-start.10 = (bf16[128,1024]{1,0:T(8,128)(2,1)S(1)}, bf16[128,1024]{1,0:T(8,128)(2,1)S(1)}, u32[]{:S(2)}, u32[]{:S(2)}) collective-permute-start(bf16[128,1024]{1,0:T(8,128)(2,1)S(1)} %broadcast_select_fusion.1), channel_id=1, source_target_pairs={{0,6},{1,7},{2,4},{3,5},{4,2},{5,3},{6,0},{7,1},{8,14},{9,15},{10,... | collective-permute-start | bytes 786440 | tf_op jit(solution)/shard_map/ppermute | solution.py:24
  32.7 13.4 %collective-permute-start.9 = (bf16[128,1024]{1,0:T(8,128)(2,1)S(1)}, bf16[128,1024]{1,0:T(8,128)(2,1)S(1)}, u32[]{:S(2)}, u32[]{:S(2)}) collective-permute-start(bf16[128,1024]{1,0:T(8,128)(2,1)S(1)} %broadcast_select_fusion.1), channel_id=1, source_target_pairs={{0,4},{1,5},{2,6},{3,7},{4,0},{5,1},{6,2},{7,3},{8,12},{9,13},{10,... | collective-permute-start | bytes 786440 | tf_op jit(solution)/shard_map/ppermute | solution.py:24
  34.2 11.8 %collective-permute-start.8 = (bf16[128,1024]{1,0:T(8,128)(2,1)S(1)}, bf16[128,1024]{1,0:T(8,128)(2,1)S(1)}, u32[]{:S(2)}, u32[]{:S(2)}) collective-permute-start(bf16[128,1024]{1,0:T(8,128)(2,1)S(1)} %broadcast_select_fusion.1), channel_id=1, source_target_pairs={{0,2},{1,3},{2,0},{3,1},{4,6},{5,7},{6,4},{7,5},{8,10},{9,11},{10,... | collective-permute-start | bytes 786440 | tf_op jit(solution)/shard_map/ppermute | solution.py:24
  34.8 2.2 %copy-start = (bf16[2048,1024]{1,0:T(8,128)(2,1)S(1)}, bf16[2048,1024]{1,0:T(8,128)(2,1)}, u32[]{:S(2)}) copy-start(bf16[2048,1024]{1,0:T(8,128)(2,1)} %refs_8_.3) | copy-start | bytes 12582916
  42.8 6.9 %copy-start.5 = (bf16[2,256,1024]{2,1,0:T(8,128)(2,1)S(1)}, bf16[2,256,1024]{2,1,0:T(8,128)(2,1)}, u32[]{:S(2)}) copy-start(bf16[2,256,1024]{2,1,0:T(8,128)(2,1)} %param.7) | copy-start | bytes 3145732
  46.1 7.6 %copy-start.1 = (bf16[2048,1024]{1,0:T(8,128)(2,1)S(1)}, bf16[2048,1024]{1,0:T(8,128)(2,1)}, u32[]{:S(2)}) copy-start(bf16[2048,1024]{1,0:T(8,128)(2,1)} %refs_8_.3) | copy-start | bytes 12582916
  46.1 2.7 %collective-permute-start.16 = (bf16[512,1024]{1,0:T(8,128)(2,1)S(1)}, bf16[512,1024]{1,0:T(8,128)(2,1)S(1)}, u32[]{:S(2)}, u32[]{:S(2)}) collective-permute-start(bf16[512,1024]{1,0:T(8,128)(2,1)S(1)} %pad_maximum_fusion.same), channel_id=1, source_target_pairs={{0,1},{1,0},{2,3},{3,2},{4,5},{5,4},{6,7},{7,6},{8,9},{9,8},{10,11... | collective-permute-start | bytes 3145736 | tf_op jit(solution)/shard_map/ppermute | solution.py:24
  46.2 7.5 %collective-permute-start.25 = (bf16[128,1024]{1,0:T(8,128)(2,1)S(1)}, bf16[128,1024]{1,0:T(8,128)(2,1)S(1)}, u32[]{:S(2)}, u32[]{:S(2)}) collective-permute-start(bf16[128,1024]{1,0:T(8,128)(2,1)S(1)} %collective-permute-done.7.refs_1_), channel_id=1, source_target_pairs={{0,1},{1,0},{2,3},{3,2},{4,5},{5,4},{6,7},{7,6},{8,9},{9,8},{10,11... | collective-permute-start | bytes 786440 | tf_op jit(solution)/shard_map/ppermute | solution.py:24
  46.7 7.0 %collective-permute-start.24 = (bf16[128,1024]{1,0:T(8,128)(2,1)S(1)}, bf16[128,1024]{1,0:T(8,128)(2,1)S(1)}, u32[]{:S(2)}, u32[]{:S(2)}) collective-permute-start(bf16[128,1024]{1,0:T(8,128)(2,1)S(1)} %collective-permute-done.6.refs_0_), channel_id=1, source_target_pairs={{0,1},{1,0},{2,3},{3,2},{4,5},{5,4},{6,7},{7,6},{8,9},{9,8},{10,11... | collective-permute-start | bytes 786440 | tf_op jit(solution)/shard_map/ppermute | solution.py:24
  50.1 10.2 %collective-permute-start.19 = (bf16[256,512]{1,0:T(8,128)(2,1)S(1)}, bf16[256,512]{1,0:T(8,128)(2,1)S(1)}, u32[]{:S(2)}, u32[]{:S(2)}) collective-permute-start(bf16[256,512]{1,0:T(8,128)(2,1)S(1)} %fusion.2.refs_0_), channel_id=1, source_target_pairs={{0,6},{1,7},{2,4},{3,5},{4,2},{5,3},{6,0},{7,1},{8,14},{9,15},{10,... | collective-permute-start | bytes 786440 | tf_op jit(solution)/shard_map/ppermute | solution.py:24
  51.7 13.3 %collective-permute-start.18 = (bf16[256,512]{1,0:T(8,128)(2,1)S(1)}, bf16[256,512]{1,0:T(8,128)(2,1)S(1)}, u32[]{:S(2)}, u32[]{:S(2)}) collective-permute-start(bf16[256,512]{1,0:T(8,128)(2,1)S(1)} %fusion.2.refs_0_), channel_id=1, source_target_pairs={{0,4},{1,5},{2,6},{3,7},{4,0},{5,1},{6,2},{7,3},{8,12},{9,13},{10,... | collective-permute-start | bytes 786440 | tf_op jit(solution)/shard_map/ppermute | solution.py:24
  52.5 12.6 %collective-permute-start.17 = (bf16[256,512]{1,0:T(8,128)(2,1)S(1)}, bf16[256,512]{1,0:T(8,128)(2,1)S(1)}, u32[]{:S(2)}, u32[]{:S(2)}) collective-permute-start(bf16[256,512]{1,0:T(8,128)(2,1)S(1)} %fusion.2.refs_0_), channel_id=1, source_target_pairs={{0,2},{1,3},{2,0},{3,1},{4,6},{5,7},{6,4},{7,5},{8,10},{9,11},{10,... | collective-permute-start | bytes 786440 | tf_op jit(solution)/shard_map/ppermute | solution.py:24
  56.1 9.5 %collective-permute-start.29 = (bf16[128,1024]{1,0:T(8,128)(2,1)S(1)}, bf16[128,1024]{1,0:T(8,128)(2,1)S(1)}, u32[]{:S(2)}, u32[]{:S(2)}) collective-permute-start(bf16[128,1024]{1,0:T(8,128)(2,1)S(1)} %get-tuple-element.57), channel_id=1, source_target_pairs={{0,8},{8,0},{16,24},{24,16},{1,9},{9,1},{17,25},{25,17},{2,10},{10... | collective-permute-start | bytes 786440 | tf_op jit(solution)/shard_map/ppermute | solution.py:24
  57.8 8.0 %collective-permute-start.20 = (bf16[256,512]{1,0:T(8,128)(2,1)S(1)}, bf16[256,512]{1,0:T(8,128)(2,1)S(1)}, u32[]{:S(2)}, u32[]{:S(2)}) collective-permute-start(bf16[256,512]{1,0:T(8,128)(2,1)S(1)} %fusion.2.refs_0_), channel_id=1, source_target_pairs={{0,1},{1,0},{2,3},{3,2},{4,5},{5,4},{6,7},{7,6},{8,9},{9,8},{10,11... | collective-permute-start | bytes 786440 | tf_op jit(solution)/shard_map/ppermute | solution.py:24
  60.3 9.7 %collective-permute-start.26 = (bf16[128,1024]{1,0:T(8,128)(2,1)S(1)}, bf16[128,1024]{1,0:T(8,128)(2,1)S(1)}, u32[]{:S(2)}, u32[]{:S(2)}) collective-permute-start(bf16[128,1024]{1,0:T(8,128)(2,1)S(1)} %get-tuple-element.52), channel_id=1, source_target_pairs={{0,8},{8,0},{16,24},{24,16},{1,9},{9,1},{17,25},{25,17},{2,10},{10... | collective-permute-start | bytes 786440 | tf_op jit(solution)/shard_map/ppermute | solution.py:24
  65.1 4.9 %collective-permute-start.23 = (bf16[256,512]{1,0:T(8,128)(2,1)S(1)}, bf16[256,512]{1,0:T(8,128)(2,1)S(1)}, u32[]{:S(2)}, u32[]{:S(2)}) collective-permute-start(bf16[256,512]{1,0:T(8,128)(2,1)S(1)} %collective-permute-done.19.refs_3_), channel_id=1, source_target_pairs={{0,1},{1,0},{2,3},{3,2},{4,5},{5,4},{6,7},{7,6},{8,9},{9,8},{10,11... | collective-permute-start | bytes 786440 | tf_op jit(solution)/shard_map/ppermute | solution.py:24
  65.1 4.9 %collective-permute-start.22 = (bf16[256,512]{1,0:T(8,128)(2,1)S(1)}, bf16[256,512]{1,0:T(8,128)(2,1)S(1)}, u32[]{:S(2)}, u32[]{:S(2)}) collective-permute-start(bf16[256,512]{1,0:T(8,128)(2,1)S(1)} %collective-permute-done.18.refs_2_), channel_id=1, source_target_pairs={{0,1},{1,0},{2,3},{3,2},{4,5},{5,4},{6,7},{7,6},{8,9},{9,8},{10,11... | collective-permute-start | bytes 786440 | tf_op jit(solution)/shard_map/ppermute | solution.py:24
  65.6 4.4 %collective-permute-start.21 = (bf16[256,512]{1,0:T(8,128)(2,1)S(1)}, bf16[256,512]{1,0:T(8,128)(2,1)S(1)}, u32[]{:S(2)}, u32[]{:S(2)}) collective-permute-start(bf16[256,512]{1,0:T(8,128)(2,1)S(1)} %collective-permute-done.17.refs_1_), channel_id=1, source_target_pairs={{0,1},{1,0},{2,3},{3,2},{4,5},{5,4},{6,7},{7,6},{8,9},{9,8},{10,11... | collective-permute-start | bytes 786440 | tf_op jit(solution)/shard_map/ppermute | solution.py:24
  65.7 15.4 %copy-start.6 = (f32[2,128,1024]{2,1,0:T(8,128)S(1)}, f32[2,128,1024]{2,1,0:T(8,128)}, u32[]{:S(2)}) copy-start(f32[2,128,1024]{2,1,0:T(8,128)} %param.10) | copy-start | bytes 3145732
  65.7 15.4 %copy-start.7 = (f32[2,128,1024]{2,1,0:T(8,128)S(1)}, f32[2,128,1024]{2,1,0:T(8,128)}, u32[]{:S(2)}) copy-start(f32[2,128,1024]{2,1,0:T(8,128)} %param.9) | copy-start | bytes 3145732
  65.8 15.3 %collective-permute-start.30 = (bf16[128,1024]{1,0:T(8,128)(2,1)S(1)}, bf16[128,1024]{1,0:T(8,128)(2,1)S(1)}, u32[]{:S(2)}, u32[]{:S(2)}) collective-permute-start(bf16[128,1024]{1,0:T(8,128)(2,1)S(1)} %add_convert_fusion), channel_id=1, source_target_pairs={{0,16},{8,24},{16,0},{24,8},{1,17},{9,25},{17,1},{25,9},{2,18},{10... | collective-permute-start | bytes 786440 | tf_op jit(solution)/shard_map/ppermute | solution.py:24
  71.8 14.6 %collective-permute-start.27 = (bf16[128,1024]{1,0:T(8,128)(2,1)S(1)}, bf16[128,1024]{1,0:T(8,128)(2,1)S(1)}, u32[]{:S(2)}, u32[]{:S(2)}) collective-permute-start(bf16[128,1024]{1,0:T(8,128)(2,1)S(1)} %get-tuple-element.53), channel_id=1, source_target_pairs={{0,8},{8,0},{16,24},{24,16},{1,9},{9,1},{17,25},{25,17},{2,10},{10... | collective-permute-start | bytes 786440 | tf_op jit(solution)/shard_map/ppermute | solution.py:24
  82.3 24.1 %collective-permute-start.34 = (bf16[128,1024]{1,0:T(8,128)(2,1)S(1)}, bf16[128,1024]{1,0:T(8,128)(2,1)S(1)}, u32[]{:S(2)}, u32[]{:S(2)}) collective-permute-start(bf16[128,1024]{1,0:T(8,128)(2,1)S(1)} %get-tuple-element.67), channel_id=1, source_target_pairs={{0,8},{8,0},{16,24},{24,16},{1,9},{9,1},{17,25},{25,17},{2,10},{10... | collective-permute-start | bytes 786440 | tf_op jit(solution)/shard_map/ppermute | solution.py:24
  82.3 24.0 %collective-permute-start.31 = (bf16[128,1024]{1,0:T(8,128)(2,1)S(1)}, bf16[128,1024]{1,0:T(8,128)(2,1)}, u32[]{:S(2)}, u32[]{:S(2)}) collective-permute-start(bf16[128,1024]{1,0:T(8,128)(2,1)S(1)} %get-tuple-element.67), channel_id=1, source_target_pairs={{0,16},{8,24},{16,0},{24,8},{1,17},{9,25},{17,1},{25,9},{2,18},{10... | collective-permute-start | bytes 786440 | tf_op jit(solution)/shard_map/ppermute | solution.py:24
  84.6 21.7 %collective-permute-start.32 = (bf16[128,1024]{1,0:T(8,128)(2,1)S(1)}, bf16[128,1024]{1,0:T(8,128)(2,1)S(1)}, u32[]{:S(2)}, u32[]{:S(2)}) collective-permute-start(bf16[128,1024]{1,0:T(8,128)(2,1)S(1)} %get-tuple-element.59), channel_id=1, source_target_pairs={{0,8},{8,0},{16,24},{24,16},{1,9},{9,1},{17,25},{25,17},{2,10},{10... | collective-permute-start | bytes 786440 | tf_op jit(solution)/shard_map/ppermute | solution.py:24
  86.5 21.5 %collective-permute-start.28 = (bf16[128,1024]{1,0:T(8,128)(2,1)S(1)}, bf16[128,1024]{1,0:T(8,128)(2,1)S(1)}, u32[]{:S(2)}, u32[]{:S(2)}) collective-permute-start(bf16[128,1024]{1,0:T(8,128)(2,1)S(1)} %add_convert_fusion.1), channel_id=1, source_target_pairs={{0,16},{8,24},{16,0},{24,8},{1,17},{9,25},{17,1},{25,9},{2,18},{10... | collective-permute-start | bytes 786440 | tf_op jit(solution)/shard_map/ppermute | solution.py:24
  106.3 7.7 %collective-permute-start.33 = (bf16[128,1024]{1,0:T(8,128)(2,1)}, bf16[128,1024]{1,0:T(8,128)(2,1)}, u32[]{:S(2)}, u32[]{:S(2)}) collective-permute-start(bf16[128,1024]{1,0:T(8,128)(2,1)} %collective-permute-done.31), channel_id=1, source_target_pairs={{0,8},{8,0},{16,24},{24,16},{1,9},{9,1},{17,25},{25,17},{2,10},{10... | collective-permute-start | bytes 786440 | tf_op jit(solution)/shard_map/ppermute | solution.py:24
  115.3 13.0 %collective-permute-start.35 = (bf16[128,1024]{1,0:T(8,128)(2,1)S(1)}, bf16[128,1024]{1,0:T(8,128)(2,1)}, u32[]{:S(2)}, u32[]{:S(2)}) collective-permute-start(bf16[128,1024]{1,0:T(8,128)(2,1)S(1)} %get-tuple-element.71), channel_id=1, source_target_pairs={{0,16},{8,24},{16,0},{24,8},{1,17},{9,25},{17,1},{25,9},{2,18},{10... | collective-permute-start | bytes 786440 | tf_op jit(solution)/shard_map/ppermute | solution.py:24
  116.1 13.7 %copy-start.2 = (f32[1,128,1024]{2,1,0:T(8,128)S(1)}, f32[1,128,1024]{2,1,0:T(8,128)}, u32[]{:S(2)}) copy-start(f32[1,128,1024]{2,1,0:T(8,128)} %get-tuple-element.69) | copy-start | bytes 1572868
  116.1 13.7 %copy-start.3 = (f32[1,128,1024]{2,1,0:T(8,128)S(1)}, f32[1,128,1024]{2,1,0:T(8,128)}, u32[]{:S(2)}) copy-start(f32[1,128,1024]{2,1,0:T(8,128)} %get-tuple-element.70) | copy-start | bytes 1572868
  116.1 13.7 %copy-start.4 = (f32[1,128,1024]{2,1,0:T(8,128)S(1)}, f32[1,128,1024]{2,1,0:T(8,128)}, u32[]{:S(2)}) copy-start(f32[1,128,1024]{2,1,0:T(8,128)} %get-tuple-element.72) | copy-start | bytes 1572868
  116.1 15.2 %collective-permute-start.37 = (bf16[128,1024]{1,0:T(8,128)(2,1)S(1)}, bf16[128,1024]{1,0:T(8,128)(2,1)S(1)}, u32[]{:S(2)}, u32[]{:S(2)}) collective-permute-start(bf16[128,1024]{1,0:T(8,128)(2,1)S(1)} %get-tuple-element.71), channel_id=1, source_target_pairs={{0,8},{8,0},{16,24},{24,16},{1,9},{9,1},{17,25},{25,17},{2,10},{10... | collective-permute-start | bytes 786440 | tf_op jit(solution)/shard_map/ppermute | solution.py:24
  128.3 8.4 %collective-permute-start.36 = (bf16[128,1024]{1,0:T(8,128)(2,1)}, bf16[128,1024]{1,0:T(8,128)(2,1)S(1)}, u32[]{:S(2)}, u32[]{:S(2)}) collective-permute-start(bf16[128,1024]{1,0:T(8,128)(2,1)} %collective-permute-done.35), channel_id=1, source_target_pairs={{0,8},{8,0},{16,24},{24,16},{1,9},{9,1},{17,25},{25,17},{2,10},{10... | collective-permute-start | bytes 786440 | tf_op jit(solution)/shard_map/ppermute | solution.py:24

commit v8 on v7

--- a/solution.py
+++ b/solution.py
@@ -348,8 +348,8 @@
     open_1 = list(reduced(arrived_1, keep_1))
     for matrix, (keep, received) in enumerate((open_0, open_1)):
         if gathered:
-            received, firsts[0], *gathered[0][:-1] = lax.optimization_barrier(
-                (received, firsts[0], *gathered[0][:-1])
+            received, firsts[0], *gathered[0][-3:-1] = lax.optimization_barrier(
+                (received, firsts[0], *gathered[0][-3:-1])
             )
         projected = keep + received.astype(jnp.float32)
         first = beta_first * moment_first[matrix] + (1.0 - beta_first) * projected

time: 140 us -> 136 us (0.971)
  waiting for transfers between devices: 71.9 us -> 67.9 us
    ppermute x38, waiting for transfers between devices: 71.9 us -> 67.9 us  [swap(): return lax.ppermute(value, axis, [(i, i ^ mask) for i in range(size)])]
  transfers between devices with their start and end apart: 38 -> 38, of which waited for: 13 -> 14; matrix products, arithmetic and copies ran while one was open for 7% -> 7% of each run, Pallas kernels for 10% -> 10%
where the time goes in v8:
time: 136 us; the launch traced here: 135 us
  waiting for transfers between devices  67.9 us (50%)
  starting transfers between devices  36.2 us (27%)
  Pallas kernels  13.8 us (10%)
  other arithmetic  8.16 us (6%)
  local copies, waits for them, and re-layouts  4.71 us (3%)
  matrix products  3.41 us (3%)
    ppermute x38, waiting for transfers between devices, swap(): return lax.ppermute(value, axis, [(i, i ^ mask) for i in range(size)])  67.9 us
    ppermute x38, starting transfers between devices, swap(): return lax.ppermute(value, axis, [(i, i ^ mask) for i in range(size)])  36.2 us
    pallas_call x4, Pallas kernels, call_in_vmem(): pl.pallas_call(body, grid_spec=pltpu.PrefetchScalarGridSpec(num_scalar_pr...  7.26 us
    pallas_call x1, Pallas kernels, add_products(): pl.pallas_call(functools.partial(product_body, shape), grid_spec=pltpu.Pr...  5.8 us
    dot_general x2, matrix products, on_device(): lax.dot_general(own, jnp.concatenate(parts, axis=0), TRANSPOSED, preferre...  2.93 us
    another operation x2, other arithmetic, on_device(): return (update, jnp.stack(firsts), jnp.stack(seconds))  2.78 us
  transfers between devices with their start and end apart: 38, of which 14 were waited for; matrix products, arithmetic and copies ran while one was open for 7% of the time, Pallas kernels for 10%

profile of v8, /device:TPU:0, one launch (start us, length us, event | category | flops | bytes accessed | tf_op | source)
XLA Modules:
  0.0 135.2 jit_solution(7295796448130152807)
XLA Ops:
  0.6 1.1 slice_bitcast_fusion.1
  1.7 3.0 %collective-permute-start.2 = (bf16[128,1024]{1,0:T(8,128)(2,1)S(1)}, bf16[128,1024]{1,0:T(8,128)(2,1)S(1)}, u32[]{:S(2)}, u32[]{:S(2)}) collective-permute-start(bf16[128,1024]{1,0:T(8,128)(2,1)S(1)} %get-tuple-element.35), channel_id=1, source_target_pairs={{0,4},{1,5},{2,6},{3,7},{4,0},{5,1},{6,2},{7,3},{8,12},{9,13},{10,... | collective-permute-start | bytes 786440 | tf_op jit(solution)/shard_map/ppermute | solution.py:24
  4.7 1.6 %collective-permute-start = (bf16[128,1024]{1,0:T(8,128)(2,1)}, bf16[128,1024]{1,0:T(8,128)(2,1)S(1)}, u32[]{:S(2)}, u32[]{:S(2)}) collective-permute-start(bf16[128,1024]{1,0:T(8,128)(2,1)} %bitcast.53), channel_id=1, source_target_pairs={{0,8},{8,0},{16,24},{24,16},{1,9},{9,1},{17,25},{25,17},{2,10},{10... | collective-permute-start | bytes 786440 | tf_op jit(solution)/shard_map/ppermute | solution.py:24
  6.3 1.5 %collective-permute-start.1 = (bf16[128,1024]{1,0:T(8,128)(2,1)S(1)}, bf16[128,1024]{1,0:T(8,128)(2,1)S(1)}, u32[]{:S(2)}, u32[]{:S(2)}) collective-permute-start(bf16[128,1024]{1,0:T(8,128)(2,1)S(1)} %get-tuple-element.36), channel_id=1, source_target_pairs={{0,2},{1,3},{2,0},{3,1},{4,6},{5,7},{6,4},{7,5},{8,10},{9,11},{10,... | collective-permute-start | bytes 786440 | tf_op jit(solution)/shard_map/ppermute | solution.py:24
  7.8 0.7 and_compare_fusion.1
  8.5 0.1 broadcast_in_dim.34
  8.6 2.4 %collective-permute-done.2.refs_4_ = bf16[128,1024]{1,0:T(8,128)(2,1)S(1)} collective-permute-done((bf16[128,1024]{1,0:T(8,128)(2,1)S(1)}, bf16[128,1024]{1,0:T(8,128)(2,1)S(1)}, u32[]{:S(2)}, u32[]{:S(2)}) %collective-permute-start.2) | collective-permute-done | bytes 262176 | tf_op jit(solution)/shard_map/ppermute | solution.py:24
  11.0 1.7 %collective-permute-start.5 = (bf16[128,1024]{1,0:T(8,128)(2,1)S(1)}, bf16[128,1024]{1,0:T(8,128)(2,1)S(1)}, u32[]{:S(2)}, u32[]{:S(2)}) collective-permute-start(bf16[128,1024]{1,0:T(8,128)(2,1)S(1)} %get-tuple-element.36), channel_id=1, source_target_pairs={{0,4},{1,5},{2,6},{3,7},{4,0},{5,1},{6,2},{7,3},{8,12},{9,13},{10,... | collective-permute-start | bytes 786440 | tf_op jit(solution)/shard_map/ppermute | solution.py:24
  12.8 1.0 broadcast_select_fusion
  13.9 2.7 %collective-permute-start.3 = (bf16[128,1024]{1,0:T(8,128)(2,1)S(1)}, bf16[128,1024]{1,0:T(8,128)(2,1)}, u32[]{:S(2)}, u32[]{:S(2)}) collective-permute-start(bf16[128,1024]{1,0:T(8,128)(2,1)S(1)} %broadcast_select_fusion), channel_id=1, source_target_pairs={{0,16},{8,24},{16,0},{24,8},{1,17},{9,25},{17,1},{25,9},{2,18},{10... | collective-permute-start | bytes 786440 | tf_op jit(solution)/shard_map/ppermute | solution.py:24
  16.5 1.5 %collective-permute-start.4 = (bf16[128,1024]{1,0:T(8,128)(2,1)S(1)}, bf16[128,1024]{1,0:T(8,128)(2,1)S(1)}, u32[]{:S(2)}, u32[]{:S(2)}) collective-permute-start(bf16[128,1024]{1,0:T(8,128)(2,1)S(1)} %get-tuple-element.35), channel_id=1, source_target_pairs={{0,2},{1,3},{2,0},{3,1},{4,6},{5,7},{6,4},{7,5},{8,10},{9,11},{10,... | collective-permute-start | bytes 786440 | tf_op jit(solution)/shard_map/ppermute | solution.py:24
  18.0 0.5 collective-permute-start.7
  18.5 0.5 collective-permute-start.6
  19.1 1.1 slice_bitcast_fusion.refs_0_
  20.2 8.5 %collective-permute-done.7.refs_1_ = bf16[128,1024]{1,0:T(8,128)(2,1)S(1)} collective-permute-done((bf16[128,1024]{1,0:T(8,128)(2,1)S(1)}, bf16[128,1024]{1,0:T(8,128)(2,1)S(1)}, u32[]{:S(2)}, u32[]{:S(2)}) %collective-permute-start.7) | collective-permute-done | bytes 262176 | tf_op jit(solution)/shard_map/ppermute | solution.py:24
  28.8 0.5 collective-permute-start.12
  29.3 0.1 collective-permute-start.14
  29.4 0.4 collective-permute-start.13
  29.9 0.1 broadcast_in_dim.31
  30.0 1.1 broadcast_select_fusion.1
  31.2 1.5 %collective-permute-start.10 = (bf16[128,1024]{1,0:T(8,128)(2,1)S(1)}, bf16[128,1024]{1,0:T(8,128)(2,1)S(1)}, u32[]{:S(2)}, u32[]{:S(2)}) collective-permute-start(bf16[128,1024]{1,0:T(8,128)(2,1)S(1)} %broadcast_select_fusion.1), channel_id=1, source_target_pairs={{0,6},{1,7},{2,4},{3,5},{4,2},{5,3},{6,0},{7,1},{8,14},{9,15},{10,... | collective-permute-start | bytes 786440 | tf_op jit(solution)/shard_map/ppermute | solution.py:24
  32.7 1.5 %collective-permute-start.9 = (bf16[128,1024]{1,0:T(8,128)(2,1)S(1)}, bf16[128,1024]{1,0:T(8,128)(2,1)S(1)}, u32[]{:S(2)}, u32[]{:S(2)}) collective-permute-start(bf16[128,1024]{1,0:T(8,128)(2,1)S(1)} %broadcast_select_fusion.1), channel_id=1, source_target_pairs={{0,4},{1,5},{2,6},{3,7},{4,0},{5,1},{6,2},{7,3},{8,12},{9,13},{10,... | collective-permute-start | bytes 786440 | tf_op jit(solution)/shard_map/ppermute | solution.py:24
  34.2 0.5 collective-permute-start.8
  34.8 2.2 %copy-done = bf16[2048,1024]{1,0:T(8,128)(2,1)S(1)} copy-done((bf16[2048,1024]{1,0:T(8,128)(2,1)S(1)}, bf16[2048,1024]{1,0:T(8,128)(2,1)}, u32[]{:S(2)}) %copy-start) | copy-done | bytes 4194328
  36.9 5.8 %shard_map.85.refs_5_ = f32[1024,1024]{1,0:T(8,128)S(1)} custom-call(s32[2]{0:T(128)S(1)} %pad_add_fusion.here, bf16[256,1024]{1,0:T(8,128)(2,1)S(1)} %slice_bitcast_fusion.refs_0_, bf16[128,1024]{1,0:T(8,128)(2,1)S(1)} %collective-permute-done.1.refs_1_, bf16[128,1024]{1,0:T(8,128)(2,1)S(1)} %collective-permute-done.4.refs_2_, ...), custom_call_target="tpu_custom_call" | custom-call | flops 3221225472 | bytes 10485760 | tf_op jit(solution)/shard_map/pallas_call | solution.py:209
  42.8 3.3 %collective-permute-done.9 = bf16[128,1024]{1,0:T(8,128)(2,1)S(1)} collective-permute-done((bf16[128,1024]{1,0:T(8,128)(2,1)S(1)}, bf16[128,1024]{1,0:T(8,128)(2,1)S(1)}, u32[]{:S(2)}, u32[]{:S(2)}) %collective-permute-start.9) | collective-permute-done | bytes 262176 | tf_op jit(solution)/shard_map/ppermute | solution.py:24
  46.1 0.1 collective-permute-start.16
  46.2 0.5 collective-permute-start.18
  46.7 0.1 collective-permute-start.17
  46.8 2.1 %collective-permute-done.16.other = bf16[512,1024]{1,0:T(8,128)(2,1)S(1)} collective-permute-done((bf16[512,1024]{1,0:T(8,128)(2,1)S(1)}, bf16[512,1024]{1,0:T(8,128)(2,1)S(1)}, u32[]{:S(2)}, u32[]{:S(2)}) %collective-permute-start.16) | collective-permute-done | bytes 1048608 | tf_op jit(solution)/shard_map/ppermute | solution.py:24
  48.9 0.8 shard_map.86
  49.7 0.5 fusion.2.refs_0_
  50.1 1.6 %collective-permute-start.25 = (bf16[256,512]{1,0:T(8,128)(2,1)S(1)}, bf16[256,512]{1,0:T(8,128)(2,1)S(1)}, u32[]{:S(2)}, u32[]{:S(2)}) collective-permute-start(bf16[256,512]{1,0:T(8,128)(2,1)S(1)} %fusion.2.refs_0_), channel_id=1, source_target_pairs={{0,6},{1,7},{2,4},{3,5},{4,2},{5,3},{6,0},{7,1},{8,14},{9,15},{10,... | collective-permute-start | bytes 786440 | tf_op jit(solution)/shard_map/ppermute | solution.py:24
  51.7 0.7 collective-permute-start.24
  52.5 1.2 collective-permute-start.23
  53.7 2.4 %shard_map.87 = (bf16[1024,1024]{1,0:T(8,128)(2,1)S(1)}, bf16[128,1024]{1,0:T(8,128)(2,1)S(1)}, bf16[128,1024]{1,0:T(8,128)(2,1)S(1)}) custom-call(s32[2]{0:T(128)S(1)} %pad_add_fusion.here, bf16[128,1024]{1,0:T(8,128)(2,1)S(1)} %collective-permute-done.6.refs_0_, bf16[128,1024]{1,0:T(8,128)(2,1)S(1)} %collective-permute-done.7.refs_1_, ...), custom_call_target="tpu_custom_call" | custom-call | flops 1610612736 | bytes 13107200 | tf_op jit(solution)/shard_map/pallas_call | solution.py:131
  56.1 1.6 %collective-permute-start.20 = (bf16[128,1024]{1,0:T(8,128)(2,1)S(1)}, bf16[128,1024]{1,0:T(8,128)(2,1)S(1)}, u32[]{:S(2)}, u32[]{:S(2)}) collective-permute-start(bf16[128,1024]{1,0:T(8,128)(2,1)S(1)} %get-tuple-element.53), channel_id=1, source_target_pairs={{0,8},{8,0},{16,24},{24,16},{1,9},{9,1},{17,25},{25,17},{2,10},{10... | collective-permute-start | bytes 786440 | tf_op jit(solution)/shard_map/ppermute | solution.py:24
  57.8 1.2 shard_map.88
  59.0 1.3 collective-permute-done.25.refs_3_
  60.3 1.6 %collective-permute-start.19 = (bf16[128,1024]{1,0:T(8,128)(2,1)S(1)}, bf16[128,1024]{1,0:T(8,128)(2,1)S(1)}, u32[]{:S(2)}, u32[]{:S(2)}) collective-permute-start(bf16[128,1024]{1,0:T(8,128)(2,1)S(1)} %get-tuple-element.51), channel_id=1, source_target_pairs={{0,8},{8,0},{16,24},{24,16},{1,9},{9,1},{17,25},{25,17},{2,10},{10... | collective-permute-start | bytes 786440 | tf_op jit(solution)/shard_map/ppermute | solution.py:24
  61.9 3.2 %collective-permute-done.24.refs_2_ = bf16[256,512]{1,0:T(8,128)(2,1)S(1)} collective-permute-done((bf16[256,512]{1,0:T(8,128)(2,1)S(1)}, bf16[256,512]{1,0:T(8,128)(2,1)S(1)}, u32[]{:S(2)}, u32[]{:S(2)}) %collective-permute-start.24) | collective-permute-done | bytes 262176 | tf_op jit(solution)/shard_map/ppermute | solution.py:24
  65.1 0.5 collective-permute-start.28
  65.8 0.4 collective-permute-start.21
  66.2 3.8 %collective-permute-done.19.refs_9_ = bf16[128,1024]{1,0:T(8,128)(2,1)S(1)} collective-permute-done((bf16[128,1024]{1,0:T(8,128)(2,1)S(1)}, bf16[128,1024]{1,0:T(8,128)(2,1)S(1)}, u32[]{:S(2)}, u32[]{:S(2)}) %collective-permute-start.19) | collective-permute-done | bytes 262176 | tf_op jit(solution)/shard_map/ppermute | solution.py:24
  70.0 1.8 %shard_map.90 = (bf16[128,1024]{1,0:T(8,128)(2,1)S(1)}, bf16[128,1024]{1,0:T(8,128)(2,1)S(1)}) custom-call(s32[2]{0:T(128)S(1)} %pad_add_fusion.here, bf16[256,512]{1,0:T(8,128)(2,1)S(1)} %fusion.2.refs_0_, bf16[256,512]{1,0:T(8,128)(2,1)S(1)} %collective-permute-done.23.refs_1_, bf16[256,512]{1,0:T(8,128)(2,1)S(1)} %collective-permute-done.24.refs_2_, ...), custom_call_target="tpu_custom_call" | custom-call | flops 1073741824 | bytes 6815744 | tf_op jit(solution)/shard_map/pallas_call | solution.py:131
  71.8 2.5 %collective-permute-start.32 = (bf16[128,1024]{1,0:T(8,128)(2,1)S(1)}, bf16[128,1024]{1,0:T(8,128)(2,1)S(1)}, u32[]{:S(2)}, u32[]{:S(2)}) collective-permute-start(bf16[128,1024]{1,0:T(8,128)(2,1)S(1)} %get-tuple-element.59), channel_id=1, source_target_pairs={{0,8},{8,0},{16,24},{24,16},{1,9},{9,1},{17,25},{25,17},{2,10},{10... | collective-permute-start | bytes 786440 | tf_op jit(solution)/shard_map/ppermute | solution.py:24
  74.4 6.7 %collective-permute-done.21 = bf16[128,1024]{1,0:T(8,128)(2,1)S(1)} collective-permute-done((bf16[128,1024]{1,0:T(8,128)(2,1)S(1)}, bf16[128,1024]{1,0:T(8,128)(2,1)S(1)}, u32[]{:S(2)}, u32[]{:S(2)}) %collective-permute-start.21) | collective-permute-done | bytes 262176 | tf_op jit(solution)/shard_map/ppermute | solution.py:24
  81.1 1.2 divide_convert_fusion.1
  82.3 2.3 %collective-permute-start.22 = (bf16[128,1024]{1,0:T(8,128)(2,1)S(1)}, bf16[128,1024]{1,0:T(8,128)(2,1)}, u32[]{:S(2)}, u32[]{:S(2)}) collective-permute-start(bf16[128,1024]{1,0:T(8,128)(2,1)S(1)} %get-tuple-element.65), channel_id=1, source_target_pairs={{0,16},{8,24},{16,0},{24,8},{1,17},{9,25},{17,1},{25,9},{2,18},{10... | collective-permute-start | bytes 786440 | tf_op jit(solution)/shard_map/ppermute | solution.py:24
  84.6 1.8 %shard_map.89 = (f32[128,1024]{1,0:T(8,128)S(1)}, f32[128,1024]{1,0:T(8,128)S(1)}) custom-call(s32[2]{0:T(128)S(1)} %pad_add_fusion.here, bf16[256,512]{1,0:T(8,128)(2,1)S(1)} %fusion.2.refs_0_, bf16[256,512]{1,0:T(8,128)(2,1)S(1)} %collective-permute-done.23.refs_1_, bf16[256,512]{1,0:T(8,128)(2,1)S(1)} %collective-permute-done.24.refs_2_, ...), custom_call_target="tpu_custom_call" | custom-call | flops 1073741824 | bytes 7340032 | tf_op jit(solution)/shard_map/pallas_call | solution.py:131
  86.5 2.7 %collective-permute-start.33 = (bf16[128,1024]{1,0:T(8,128)(2,1)S(1)}, bf16[128,1024]{1,0:T(8,128)(2,1)S(1)}, u32[]{:S(2)}, u32[]{:S(2)}) collective-permute-start(bf16[128,1024]{1,0:T(8,128)(2,1)S(1)} %add_convert_fusion), channel_id=1, source_target_pairs={{0,16},{8,24},{16,0},{24,8},{1,17},{9,25},{17,1},{25,9},{2,18},{10... | collective-permute-start | bytes 786440 | tf_op jit(solution)/shard_map/ppermute | solution.py:24
  89.2 17.1 %collective-permute-done.30 = bf16[128,1024]{1,0:T(8,128)(2,1)S(1)} collective-permute-done((bf16[128,1024]{1,0:T(8,128)(2,1)S(1)}, bf16[128,1024]{1,0:T(8,128)(2,1)S(1)}, u32[]{:S(2)}, u32[]{:S(2)}) %collective-permute-start.30) | collective-permute-done | bytes 262176 | tf_op jit(solution)/shard_map/ppermute | solution.py:24
  106.3 1.6 %collective-permute-done.33 = bf16[128,1024]{1,0:T(8,128)(2,1)S(1)} collective-permute-done((bf16[128,1024]{1,0:T(8,128)(2,1)S(1)}, bf16[128,1024]{1,0:T(8,128)(2,1)S(1)}, u32[]{:S(2)}, u32[]{:S(2)}) %collective-permute-start.33) | collective-permute-done | bytes 262176 | tf_op jit(solution)/shard_map/ppermute | solution.py:24
  107.9 1.3 fusion.28
  109.3 0.3 collective-permute-start.35
  109.6 2.1 %collective-permute-start.31 = (bf16[128,1024]{1,0:T(8,128)(2,1)}, bf16[128,1024]{1,0:T(8,128)(2,1)}, u32[]{:S(2)}, u32[]{:S(2)}) collective-permute-start(bf16[128,1024]{1,0:T(8,128)(2,1)} %collective-permute-done.22), channel_id=1, source_target_pairs={{0,8},{8,0},{16,24},{24,16},{1,9},{9,1},{17,25},{25,17},{2,10},{10... | collective-permute-start | bytes 786440 | tf_op jit(solution)/shard_map/ppermute | solution.py:24
  111.8 9.9 %collective-permute-done.35 = bf16[128,1024]{1,0:T(8,128)(2,1)} collective-permute-done((bf16[128,1024]{1,0:T(8,128)(2,1)S(1)}, bf16[128,1024]{1,0:T(8,128)(2,1)}, u32[]{:S(2)}, u32[]{:S(2)}) %collective-permute-start.35) | collective-permute-done | bytes 262176 | tf_op jit(solution)/shard_map/ppermute | solution.py:24
  121.7 2.1 %collective-permute-done.31 = bf16[128,1024]{1,0:T(8,128)(2,1)} collective-permute-done((bf16[128,1024]{1,0:T(8,128)(2,1)}, bf16[128,1024]{1,0:T(8,128)(2,1)}, u32[]{:S(2)}, u32[]{:S(2)}) %collective-permute-start.31) | collective-permute-done | bytes 262176 | tf_op jit(solution)/shard_map/ppermute | solution.py:24
  123.8 1.5 %fusion = bf16[1,256,1024]{2,1,0:T(8,128)(2,1)S(1)} fusion(bf16[128,1024]{1,0:T(8,128)(2,1)S(1)} %get-tuple-element.65, bf16[128,1024]{1,0:T(8,128)(2,1)} %collective-permute-done.22, bf16[128,1024]{1,0:T(8,128)(2,1)S(1)} %collective-permute-done.34, bf16[128,1024]{1,0:T(8,128)(2,1)} %collective-permute-done.31, ...), kind=kOutput, calls=%fused_computation.2 | convolution fusion | flops 272891904 | bytes 1835012 | tf_op jit(solution)/shard_map/dot_general | solution.py:372
  125.3 1.5 %pad_maximum_fusion.2 = (f32[2,128,1024]{2,1,0:T(8,128)}, f32[2,128,1024]{2,1,0:T(8,128)}) fusion(f32[1,128,1024]{2,1,0:T(8,128)S(1)} %copy-done.4, f32[1,128,1024]{2,1,0:T(8,128)S(1)} %bitcast.52, f32[1,128,1024]{2,1,0:T(8,128)S(1)} %copy-done.3, f32[1,128,1024]{2,1,0:T(8,128)S(1)} %copy-done.2), kind=kLoop, calls=%fused_computation.22 | loop fusion | flops 524288 | bytes 4194304 | tf_op jit(solution)/shard_map/stack | solution.py:379
  126.8 2.5 %collective-permute-done.37 = bf16[128,1024]{1,0:T(8,128)(2,1)S(1)} collective-permute-done((bf16[128,1024]{1,0:T(8,128)(2,1)S(1)}, bf16[128,1024]{1,0:T(8,128)(2,1)S(1)}, u32[]{:S(2)}, u32[]{:S(2)}) %collective-permute-start.37) | collective-permute-done | bytes 262176 | tf_op jit(solution)/shard_map/ppermute | solution.py:24
  129.3 3.4 %collective-permute-done.36 = bf16[128,1024]{1,0:T(8,128)(2,1)S(1)} collective-permute-done((bf16[128,1024]{1,0:T(8,128)(2,1)}, bf16[128,1024]{1,0:T(8,128)(2,1)S(1)}, u32[]{:S(2)}, u32[]{:S(2)}) %collective-permute-start.36) | collective-permute-done | bytes 262176 | tf_op jit(solution)/shard_map/ppermute | solution.py:24
  132.7 1.4 %fusion.1 = bf16[1,256,1024]{2,1,0:T(8,128)(2,1)S(1)} fusion(bf16[128,1024]{1,0:T(8,128)(2,1)S(1)} %get-tuple-element.69, bf16[128,1024]{1,0:T(8,128)(2,1)} %collective-permute-done.35, bf16[128,1024]{1,0:T(8,128)(2,1)S(1)} %collective-permute-done.37, bf16[128,1024]{1,0:T(8,128)(2,1)S(1)} %collective-permute-done.36, ...), kind=kOutput, calls=%fused_computation.3 | convolution fusion | flops 272891904 | bytes 1835012 | tf_op jit(solution)/shard_map/dot_general | solution.py:372
  134.2 1.1 pad_maximum_fusion.1
  (64 shorter events, 0.8 us)
Async XLA Ops:
  1.7 9.3 %collective-permute-start.2 = (bf16[128,1024]{1,0:T(8,128)(2,1)S(1)}, bf16[128,1024]{1,0:T(8,128)(2,1)S(1)}, u32[]{:S(2)}, u32[]{:S(2)}) collective-permute-start(bf16[128,1024]{1,0:T(8,128)(2,1)S(1)} %get-tuple-element.35), channel_id=1, source_target_pairs={{0,4},{1,5},{2,6},{3,7},{4,0},{5,1},{6,2},{7,3},{8,12},{9,13},{10,... | collective-permute-start | bytes 786440 | tf_op jit(solution)/shard_map/ppermute | solution.py:24
  4.7 8.1 %collective-permute-start = (bf16[128,1024]{1,0:T(8,128)(2,1)}, bf16[128,1024]{1,0:T(8,128)(2,1)S(1)}, u32[]{:S(2)}, u32[]{:S(2)}) collective-permute-start(bf16[128,1024]{1,0:T(8,128)(2,1)} %bitcast.53), channel_id=1, source_target_pairs={{0,8},{8,0},{16,24},{24,16},{1,9},{9,1},{17,25},{25,17},{2,10},{10... | collective-permute-start | bytes 786440 | tf_op jit(solution)/shard_map/ppermute | solution.py:24
  6.3 7.5 %collective-permute-start.1 = (bf16[128,1024]{1,0:T(8,128)(2,1)S(1)}, bf16[128,1024]{1,0:T(8,128)(2,1)S(1)}, u32[]{:S(2)}, u32[]{:S(2)}) collective-permute-start(bf16[128,1024]{1,0:T(8,128)(2,1)S(1)} %get-tuple-element.36), channel_id=1, source_target_pairs={{0,2},{1,3},{2,0},{3,1},{4,6},{5,7},{6,4},{7,5},{8,10},{9,11},{10,... | collective-permute-start | bytes 786440 | tf_op jit(solution)/shard_map/ppermute | solution.py:24
  11.0 9.1 %collective-permute-start.5 = (bf16[128,1024]{1,0:T(8,128)(2,1)S(1)}, bf16[128,1024]{1,0:T(8,128)(2,1)S(1)}, u32[]{:S(2)}, u32[]{:S(2)}) collective-permute-start(bf16[128,1024]{1,0:T(8,128)(2,1)S(1)} %get-tuple-element.36), channel_id=1, source_target_pairs={{0,4},{1,5},{2,6},{3,7},{4,0},{5,1},{6,2},{7,3},{8,12},{9,13},{10,... | collective-permute-start | bytes 786440 | tf_op jit(solution)/shard_map/ppermute | solution.py:24
  13.8 14.9 %copy-start.8 = (bf16[128,1024]{1,0:T(8,128)(2,1)}, bf16[128,1024]{1,0:T(8,128)(2,1)S(1)}, u32[]{:S(2)}) copy-start(bf16[128,1024]{1,0:T(8,128)(2,1)S(1)} %broadcast_select_fusion) | copy-start | bytes 786436
  13.9 14.9 %collective-permute-start.3 = (bf16[128,1024]{1,0:T(8,128)(2,1)S(1)}, bf16[128,1024]{1,0:T(8,128)(2,1)}, u32[]{:S(2)}, u32[]{:S(2)}) collective-permute-start(bf16[128,1024]{1,0:T(8,128)(2,1)S(1)} %broadcast_select_fusion), channel_id=1, source_target_pairs={{0,16},{8,24},{16,0},{24,8},{1,17},{9,25},{17,1},{25,9},{2,18},{10... | collective-permute-start | bytes 786440 | tf_op jit(solution)/shard_map/ppermute | solution.py:24
  16.5 12.8 %collective-permute-start.4 = (bf16[128,1024]{1,0:T(8,128)(2,1)S(1)}, bf16[128,1024]{1,0:T(8,128)(2,1)S(1)}, u32[]{:S(2)}, u32[]{:S(2)}) collective-permute-start(bf16[128,1024]{1,0:T(8,128)(2,1)S(1)} %get-tuple-element.35), channel_id=1, source_target_pairs={{0,2},{1,3},{2,0},{3,1},{4,6},{5,7},{6,4},{7,5},{8,10},{9,11},{10,... | collective-permute-start | bytes 786440 | tf_op jit(solution)/shard_map/ppermute | solution.py:24
  18.0 10.7 %collective-permute-start.7 = (bf16[128,1024]{1,0:T(8,128)(2,1)S(1)}, bf16[128,1024]{1,0:T(8,128)(2,1)S(1)}, u32[]{:S(2)}, u32[]{:S(2)}) collective-permute-start(bf16[128,1024]{1,0:T(8,128)(2,1)S(1)} %collective-permute-done.2.refs_4_), channel_id=1, source_target_pairs={{0,2},{1,3},{2,0},{3,1},{4,6},{5,7},{6,4},{7,5},{8,10},{9,11},{10,... | collective-permute-start | bytes 786440 | tf_op jit(solution)/shard_map/ppermute | solution.py:24
  18.5 10.8 %collective-permute-start.6 = (bf16[128,1024]{1,0:T(8,128)(2,1)S(1)}, bf16[128,1024]{1,0:T(8,128)(2,1)S(1)}, u32[]{:S(2)}, u32[]{:S(2)}) collective-permute-start(bf16[128,1024]{1,0:T(8,128)(2,1)S(1)} %collective-permute-done.1.refs_1_), channel_id=1, source_target_pairs={{0,4},{1,5},{2,6},{3,7},{4,0},{5,1},{6,2},{7,3},{8,12},{9,13},{10,... | collective-permute-start | bytes 786440 | tf_op jit(solution)/shard_map/ppermute | solution.py:24
  20.1 14.1 %collective-permute-start.11 = (bf16[256,1024]{1,0:T(8,128)(2,1)S(1)}, bf16[256,1024]{1,0:T(8,128)(2,1)S(1)}, u32[]{:S(2)}, u32[]{:S(2)}) collective-permute-start(bf16[256,1024]{1,0:T(8,128)(2,1)S(1)} %slice_bitcast_fusion.refs_0_), channel_id=1, source_target_pairs={{0,1},{1,0},{2,3},{3,2},{4,5},{5,4},{6,7},{7,6},{8,9},{9,8},{10,11... | collective-permute-start | bytes 1572872 | tf_op jit(solution)/shard_map/ppermute | solution.py:24
  28.8 2.4 %collective-permute-start.15 = (bf16[128,1024]{1,0:T(8,128)(2,1)S(1)}, bf16[128,1024]{1,0:T(8,128)(2,1)S(1)}, u32[]{:S(2)}, u32[]{:S(2)}) collective-permute-start(bf16[128,1024]{1,0:T(8,128)(2,1)S(1)} %collective-permute-done.2.refs_4_), channel_id=1, source_target_pairs={{0,1},{1,0},{2,3},{3,2},{4,5},{5,4},{6,7},{7,6},{8,9},{9,8},{10,11... | collective-permute-start | bytes 786440 | tf_op jit(solution)/shard_map/ppermute | solution.py:24
  28.8 3.9 %collective-permute-start.12 = (bf16[128,1024]{1,0:T(8,128)(2,1)S(1)}, bf16[128,1024]{1,0:T(8,128)(2,1)S(1)}, u32[]{:S(2)}, u32[]{:S(2)}) collective-permute-start(bf16[128,1024]{1,0:T(8,128)(2,1)S(1)} %collective-permute-done.1.refs_1_), channel_id=1, source_target_pairs={{0,1},{1,0},{2,3},{3,2},{4,5},{5,4},{6,7},{7,6},{8,9},{9,8},{10,11... | collective-permute-start | bytes 786440 | tf_op jit(solution)/shard_map/ppermute | solution.py:24
  29.3 5.5 %collective-permute-start.14 = (bf16[128,1024]{1,0:T(8,128)(2,1)S(1)}, bf16[128,1024]{1,0:T(8,128)(2,1)S(1)}, u32[]{:S(2)}, u32[]{:S(2)}) collective-permute-start(bf16[128,1024]{1,0:T(8,128)(2,1)S(1)} %collective-permute-done.5.refs_3_), channel_id=1, source_target_pairs={{0,1},{1,0},{2,3},{3,2},{4,5},{5,4},{6,7},{7,6},{8,9},{9,8},{10,11... | collective-permute-start | bytes 786440 | tf_op jit(solution)/shard_map/ppermute | solution.py:24
  29.4 5.4 %collective-permute-start.13 = (bf16[128,1024]{1,0:T(8,128)(2,1)S(1)}, bf16[128,1024]{1,0:T(8,128)(2,1)}, u32[]{:S(2)}, u32[]{:S(2)}) collective-permute-start(bf16[128,1024]{1,0:T(8,128)(2,1)S(1)} %collective-permute-done.4.refs_2_), channel_id=1, source_target_pairs={{0,1},{1,0},{2,3},{3,2},{4,5},{5,4},{6,7},{7,6},{8,9},{9,8},{10,11... | collective-permute-start | bytes 786440 | tf_op jit(solution)/shard_map/ppermute | solution.py:24
  31.2 11.6 %collective-permute-start.10 = (bf16[128,1024]{1,0:T(8,128)(2,1)S(1)}, bf16[128,1024]{1,0:T(8,128)(2,1)S(1)}, u32[]{:S(2)}, u32[]{:S(2)}) collective-permute-start(bf16[128,1024]{1,0:T(8,128)(2,1)S(1)} %broadcast_select_fusion.1), channel_id=1, source_target_pairs={{0,6},{1,7},{2,4},{3,5},{4,2},{5,3},{6,0},{7,1},{8,14},{9,15},{10,... | collective-permute-start | bytes 786440 | tf_op jit(solution)/shard_map/ppermute | solution.py:24
  32.7 13.4 %collective-permute-start.9 = (bf16[128,1024]{1,0:T(8,128)(2,1)S(1)}, bf16[128,1024]{1,0:T(8,128)(2,1)S(1)}, u32[]{:S(2)}, u32[]{:S(2)}) collective-permute-start(bf16[128,1024]{1,0:T(8,128)(2,1)S(1)} %broadcast_select_fusion.1), channel_id=1, source_target_pairs={{0,4},{1,5},{2,6},{3,7},{4,0},{5,1},{6,2},{7,3},{8,12},{9,13},{10,... | collective-permute-start | bytes 786440 | tf_op jit(solution)/shard_map/ppermute | solution.py:24
  34.2 11.8 %collective-permute-start.8 = (bf16[128,1024]{1,0:T(8,128)(2,1)S(1)}, bf16[128,1024]{1,0:T(8,128)(2,1)S(1)}, u32[]{:S(2)}, u32[]{:S(2)}) collective-permute-start(bf16[128,1024]{1,0:T(8,128)(2,1)S(1)} %broadcast_select_fusion.1), channel_id=1, source_target_pairs={{0,2},{1,3},{2,0},{3,1},{4,6},{5,7},{6,4},{7,5},{8,10},{9,11},{10,... | collective-permute-start | bytes 786440 | tf_op jit(solution)/shard_map/ppermute | solution.py:24
  34.8 2.2 %copy-start = (bf16[2048,1024]{1,0:T(8,128)(2,1)S(1)}, bf16[2048,1024]{1,0:T(8,128)(2,1)}, u32[]{:S(2)}) copy-start(bf16[2048,1024]{1,0:T(8,128)(2,1)} %refs_8_.3) | copy-start | bytes 12582916
  42.8 6.9 %copy-start.5 = (bf16[2,256,1024]{2,1,0:T(8,128)(2,1)S(1)}, bf16[2,256,1024]{2,1,0:T(8,128)(2,1)}, u32[]{:S(2)}) copy-start(bf16[2,256,1024]{2,1,0:T(8,128)(2,1)} %param.7) | copy-start | bytes 3145732
  46.1 7.6 %copy-start.1 = (bf16[2048,1024]{1,0:T(8,128)(2,1)S(1)}, bf16[2048,1024]{1,0:T(8,128)(2,1)}, u32[]{:S(2)}) copy-start(bf16[2048,1024]{1,0:T(8,128)(2,1)} %refs_8_.3) | copy-start | bytes 12582916
  46.1 2.7 %collective-permute-start.16 = (bf16[512,1024]{1,0:T(8,128)(2,1)S(1)}, bf16[512,1024]{1,0:T(8,128)(2,1)S(1)}, u32[]{:S(2)}, u32[]{:S(2)}) collective-permute-start(bf16[512,1024]{1,0:T(8,128)(2,1)S(1)} %pad_maximum_fusion.same), channel_id=1, source_target_pairs={{0,1},{1,0},{2,3},{3,2},{4,5},{5,4},{6,7},{7,6},{8,9},{9,8},{10,11... | collective-permute-start | bytes 3145736 | tf_op jit(solution)/shard_map/ppermute | solution.py:24
  46.2 7.5 %collective-permute-start.18 = (bf16[128,1024]{1,0:T(8,128)(2,1)S(1)}, bf16[128,1024]{1,0:T(8,128)(2,1)S(1)}, u32[]{:S(2)}, u32[]{:S(2)}) collective-permute-start(bf16[128,1024]{1,0:T(8,128)(2,1)S(1)} %collective-permute-done.7.refs_1_), channel_id=1, source_target_pairs={{0,1},{1,0},{2,3},{3,2},{4,5},{5,4},{6,7},{7,6},{8,9},{9,8},{10,11... | collective-permute-start | bytes 786440 | tf_op jit(solution)/shard_map/ppermute | solution.py:24
  46.7 7.0 %collective-permute-start.17 = (bf16[128,1024]{1,0:T(8,128)(2,1)S(1)}, bf16[128,1024]{1,0:T(8,128)(2,1)S(1)}, u32[]{:S(2)}, u32[]{:S(2)}) collective-permute-start(bf16[128,1024]{1,0:T(8,128)(2,1)S(1)} %collective-permute-done.6.refs_0_), channel_id=1, source_target_pairs={{0,1},{1,0},{2,3},{3,2},{4,5},{5,4},{6,7},{7,6},{8,9},{9,8},{10,11... | collective-permute-start | bytes 786440 | tf_op jit(solution)/shard_map/ppermute | solution.py:24
  50.1 10.2 %collective-permute-start.25 = (bf16[256,512]{1,0:T(8,128)(2,1)S(1)}, bf16[256,512]{1,0:T(8,128)(2,1)S(1)}, u32[]{:S(2)}, u32[]{:S(2)}) collective-permute-start(bf16[256,512]{1,0:T(8,128)(2,1)S(1)} %fusion.2.refs_0_), channel_id=1, source_target_pairs={{0,6},{1,7},{2,4},{3,5},{4,2},{5,3},{6,0},{7,1},{8,14},{9,15},{10,... | collective-permute-start | bytes 786440 | tf_op jit(solution)/shard_map/ppermute | solution.py:24
  51.7 13.3 %collective-permute-start.24 = (bf16[256,512]{1,0:T(8,128)(2,1)S(1)}, bf16[256,512]{1,0:T(8,128)(2,1)S(1)}, u32[]{:S(2)}, u32[]{:S(2)}) collective-permute-start(bf16[256,512]{1,0:T(8,128)(2,1)S(1)} %fusion.2.refs_0_), channel_id=1, source_target_pairs={{0,4},{1,5},{2,6},{3,7},{4,0},{5,1},{6,2},{7,3},{8,12},{9,13},{10,... | collective-permute-start | bytes 786440 | tf_op jit(solution)/shard_map/ppermute | solution.py:24
  52.5 12.6 %collective-permute-start.23 = (bf16[256,512]{1,0:T(8,128)(2,1)S(1)}, bf16[256,512]{1,0:T(8,128)(2,1)S(1)}, u32[]{:S(2)}, u32[]{:S(2)}) collective-permute-start(bf16[256,512]{1,0:T(8,128)(2,1)S(1)} %fusion.2.refs_0_), channel_id=1, source_target_pairs={{0,2},{1,3},{2,0},{3,1},{4,6},{5,7},{6,4},{7,5},{8,10},{9,11},{10,... | collective-permute-start | bytes 786440 | tf_op jit(solution)/shard_map/ppermute | solution.py:24
  56.1 9.5 %collective-permute-start.20 = (bf16[128,1024]{1,0:T(8,128)(2,1)S(1)}, bf16[128,1024]{1,0:T(8,128)(2,1)S(1)}, u32[]{:S(2)}, u32[]{:S(2)}) collective-permute-start(bf16[128,1024]{1,0:T(8,128)(2,1)S(1)} %get-tuple-element.53), channel_id=1, source_target_pairs={{0,8},{8,0},{16,24},{24,16},{1,9},{9,1},{17,25},{25,17},{2,10},{10... | collective-permute-start | bytes 786440 | tf_op jit(solution)/shard_map/ppermute | solution.py:24
  57.8 8.0 %collective-permute-start.26 = (bf16[256,512]{1,0:T(8,128)(2,1)S(1)}, bf16[256,512]{1,0:T(8,128)(2,1)S(1)}, u32[]{:S(2)}, u32[]{:S(2)}) collective-permute-start(bf16[256,512]{1,0:T(8,128)(2,1)S(1)} %fusion.2.refs_0_), channel_id=1, source_target_pairs={{0,1},{1,0},{2,3},{3,2},{4,5},{5,4},{6,7},{7,6},{8,9},{9,8},{10,11... | collective-permute-start | bytes 786440 | tf_op jit(solution)/shard_map/ppermute | solution.py:24
  60.3 9.7 %collective-permute-start.19 = (bf16[128,1024]{1,0:T(8,128)(2,1)S(1)}, bf16[128,1024]{1,0:T(8,128)(2,1)S(1)}, u32[]{:S(2)}, u32[]{:S(2)}) collective-permute-start(bf16[128,1024]{1,0:T(8,128)(2,1)S(1)} %get-tuple-element.51), channel_id=1, source_target_pairs={{0,8},{8,0},{16,24},{24,16},{1,9},{9,1},{17,25},{25,17},{2,10},{10... | collective-permute-start | bytes 786440 | tf_op jit(solution)/shard_map/ppermute | solution.py:24
  65.1 4.9 %collective-permute-start.29 = (bf16[256,512]{1,0:T(8,128)(2,1)S(1)}, bf16[256,512]{1,0:T(8,128)(2,1)S(1)}, u32[]{:S(2)}, u32[]{:S(2)}) collective-permute-start(bf16[256,512]{1,0:T(8,128)(2,1)S(1)} %collective-permute-done.25.refs_3_), channel_id=1, source_target_pairs={{0,1},{1,0},{2,3},{3,2},{4,5},{5,4},{6,7},{7,6},{8,9},{9,8},{10,11... | collective-permute-start | bytes 786440 | tf_op jit(solution)/shard_map/ppermute | solution.py:24
  65.1 4.9 %collective-permute-start.28 = (bf16[256,512]{1,0:T(8,128)(2,1)S(1)}, bf16[256,512]{1,0:T(8,128)(2,1)S(1)}, u32[]{:S(2)}, u32[]{:S(2)}) collective-permute-start(bf16[256,512]{1,0:T(8,128)(2,1)S(1)} %collective-permute-done.24.refs_2_), channel_id=1, source_target_pairs={{0,1},{1,0},{2,3},{3,2},{4,5},{5,4},{6,7},{7,6},{8,9},{9,8},{10,11... | collective-permute-start | bytes 786440 | tf_op jit(solution)/shard_map/ppermute | solution.py:24
  65.6 4.4 %collective-permute-start.27 = (bf16[256,512]{1,0:T(8,128)(2,1)S(1)}, bf16[256,512]{1,0:T(8,128)(2,1)S(1)}, u32[]{:S(2)}, u32[]{:S(2)}) collective-permute-start(bf16[256,512]{1,0:T(8,128)(2,1)S(1)} %collective-permute-done.23.refs_1_), channel_id=1, source_target_pairs={{0,1},{1,0},{2,3},{3,2},{4,5},{5,4},{6,7},{7,6},{8,9},{9,8},{10,11... | collective-permute-start | bytes 786440 | tf_op jit(solution)/shard_map/ppermute | solution.py:24
  65.7 15.4 %copy-start.6 = (f32[2,128,1024]{2,1,0:T(8,128)S(1)}, f32[2,128,1024]{2,1,0:T(8,128)}, u32[]{:S(2)}) copy-start(f32[2,128,1024]{2,1,0:T(8,128)} %param.10) | copy-start | bytes 3145732
  65.7 15.4 %copy-start.7 = (f32[2,128,1024]{2,1,0:T(8,128)S(1)}, f32[2,128,1024]{2,1,0:T(8,128)}, u32[]{:S(2)}) copy-start(f32[2,128,1024]{2,1,0:T(8,128)} %param.9) | copy-start | bytes 3145732
  65.8 15.3 %collective-permute-start.21 = (bf16[128,1024]{1,0:T(8,128)(2,1)S(1)}, bf16[128,1024]{1,0:T(8,128)(2,1)S(1)}, u32[]{:S(2)}, u32[]{:S(2)}) collective-permute-start(bf16[128,1024]{1,0:T(8,128)(2,1)S(1)} %add_convert_fusion.1), channel_id=1, source_target_pairs={{0,16},{8,24},{16,0},{24,8},{1,17},{9,25},{17,1},{25,9},{2,18},{10... | collective-permute-start | bytes 786440 | tf_op jit(solution)/shard_map/ppermute | solution.py:24
  71.8 14.6 %collective-permute-start.32 = (bf16[128,1024]{1,0:T(8,128)(2,1)S(1)}, bf16[128,1024]{1,0:T(8,128)(2,1)S(1)}, u32[]{:S(2)}, u32[]{:S(2)}) collective-permute-start(bf16[128,1024]{1,0:T(8,128)(2,1)S(1)} %get-tuple-element.59), channel_id=1, source_target_pairs={{0,8},{8,0},{16,24},{24,16},{1,9},{9,1},{17,25},{25,17},{2,10},{10... | collective-permute-start | bytes 786440 | tf_op jit(solution)/shard_map/ppermute | solution.py:24
  82.3 24.1 %collective-permute-start.34 = (bf16[128,1024]{1,0:T(8,128)(2,1)S(1)}, bf16[128,1024]{1,0:T(8,128)(2,1)S(1)}, u32[]{:S(2)}, u32[]{:S(2)}) collective-permute-start(bf16[128,1024]{1,0:T(8,128)(2,1)S(1)} %get-tuple-element.65), channel_id=1, source_target_pairs={{0,8},{8,0},{16,24},{24,16},{1,9},{9,1},{17,25},{25,17},{2,10},{10... | collective-permute-start | bytes 786440 | tf_op jit(solution)/shard_map/ppermute | solution.py:24
  82.3 24.0 %collective-permute-start.22 = (bf16[128,1024]{1,0:T(8,128)(2,1)S(1)}, bf16[128,1024]{1,0:T(8,128)(2,1)}, u32[]{:S(2)}, u32[]{:S(2)}) collective-permute-start(bf16[128,1024]{1,0:T(8,128)(2,1)S(1)} %get-tuple-element.65), channel_id=1, source_target_pairs={{0,16},{8,24},{16,0},{24,8},{1,17},{9,25},{17,1},{25,9},{2,18},{10... | collective-permute-start | bytes 786440 | tf_op jit(solution)/shard_map/ppermute | solution.py:24
  84.6 21.7 %collective-permute-start.30 = (bf16[128,1024]{1,0:T(8,128)(2,1)S(1)}, bf16[128,1024]{1,0:T(8,128)(2,1)S(1)}, u32[]{:S(2)}, u32[]{:S(2)}) collective-permute-start(bf16[128,1024]{1,0:T(8,128)(2,1)S(1)} %get-tuple-element.56), channel_id=1, source_target_pairs={{0,8},{8,0},{16,24},{24,16},{1,9},{9,1},{17,25},{25,17},{2,10},{10... | collective-permute-start | bytes 786440 | tf_op jit(solution)/shard_map/ppermute | solution.py:24
  86.5 21.5 %collective-permute-start.33 = (bf16[128,1024]{1,0:T(8,128)(2,1)S(1)}, bf16[128,1024]{1,0:T(8,128)(2,1)S(1)}, u32[]{:S(2)}, u32[]{:S(2)}) collective-permute-start(bf16[128,1024]{1,0:T(8,128)(2,1)S(1)} %add_convert_fusion), channel_id=1, source_target_pairs={{0,16},{8,24},{16,0},{24,8},{1,17},{9,25},{17,1},{25,9},{2,18},{10... | collective-permute-start | bytes 786440 | tf_op jit(solution)/shard_map/ppermute | solution.py:24
  109.3 12.4 %collective-permute-start.35 = (bf16[128,1024]{1,0:T(8,128)(2,1)S(1)}, bf16[128,1024]{1,0:T(8,128)(2,1)}, u32[]{:S(2)}, u32[]{:S(2)}) collective-permute-start(bf16[128,1024]{1,0:T(8,128)(2,1)S(1)} %get-tuple-element.69), channel_id=1, source_target_pairs={{0,16},{8,24},{16,0},{24,8},{1,17},{9,25},{17,1},{25,9},{2,18},{10... | collective-permute-start | bytes 786440 | tf_op jit(solution)/shard_map/ppermute | solution.py:24
  109.6 14.2 %collective-permute-start.31 = (bf16[128,1024]{1,0:T(8,128)(2,1)}, bf16[128,1024]{1,0:T(8,128)(2,1)}, u32[]{:S(2)}, u32[]{:S(2)}) collective-permute-start(bf16[128,1024]{1,0:T(8,128)(2,1)} %collective-permute-done.22), channel_id=1, source_target_pairs={{0,8},{8,0},{16,24},{24,16},{1,9},{9,1},{17,25},{25,17},{2,10},{10... | collective-permute-start | bytes 786440 | tf_op jit(solution)/shard_map/ppermute | solution.py:24
  111.7 13.5 %copy-start.2 = (f32[1,128,1024]{2,1,0:T(8,128)S(1)}, f32[1,128,1024]{2,1,0:T(8,128)}, u32[]{:S(2)}) copy-start(f32[1,128,1024]{2,1,0:T(8,128)} %get-tuple-element.67) | copy-start | bytes 1572868
  111.7 13.6 %copy-start.3 = (f32[1,128,1024]{2,1,0:T(8,128)S(1)}, f32[1,128,1024]{2,1,0:T(8,128)}, u32[]{:S(2)}) copy-start(f32[1,128,1024]{2,1,0:T(8,128)} %get-tuple-element.68) | copy-start | bytes 1572868
  111.7 13.6 %copy-start.4 = (f32[1,128,1024]{2,1,0:T(8,128)S(1)}, f32[1,128,1024]{2,1,0:T(8,128)}, u32[]{:S(2)}) copy-start(f32[1,128,1024]{2,1,0:T(8,128)} %get-tuple-element.70) | copy-start | bytes 1572868
  111.7 17.5 %collective-permute-start.37 = (bf16[128,1024]{1,0:T(8,128)(2,1)S(1)}, bf16[128,1024]{1,0:T(8,128)(2,1)S(1)}, u32[]{:S(2)}, u32[]{:S(2)}) collective-permute-start(bf16[128,1024]{1,0:T(8,128)(2,1)S(1)} %get-tuple-element.69), channel_id=1, source_target_pairs={{0,8},{8,0},{16,24},{24,16},{1,9},{9,1},{17,25},{25,17},{2,10},{10... | collective-permute-start | bytes 786440 | tf_op jit(solution)/shard_map/ppermute | solution.py:24
  121.7 11.0 %collective-permute-start.36 = (bf16[128,1024]{1,0:T(8,128)(2,1)}, bf16[128,1024]{1,0:T(8,128)(2,1)S(1)}, u32[]{:S(2)}, u32[]{:S(2)}) collective-permute-start(bf16[128,1024]{1,0:T(8,128)(2,1)} %collective-permute-done.35), channel_id=1, source_target_pairs={{0,8},{8,0},{16,24},{24,16},{1,9},{9,1},{17,25},{25,17},{2,10},{10... | collective-permute-start | bytes 786440 | tf_op jit(solution)/shard_map/ppermute | solution.py:24

commit v9 on v8

--- a/solution.py
+++ b/solution.py
@@ -338,10 +338,11 @@
     ).astype(jnp.bfloat16)
     blocks = spread(heads, far_bits)
     open_0 = reduced(arrived_0, keep_0)
-    tokens_1 += arrived_0[pieces // 2 :]
     blocks = with_partner({mask: [held] for mask, held in blocks.items()})
     send_1 = heads_product(blocks, here, layer_input, 0, pieces, jnp.bfloat16, scale, tokens_1)
-    keep_1 = heads_product(blocks, here, layer_input, 1, pieces, jnp.float32, scale)
+    keep_1 = heads_product(
+        blocks, here, layer_input, 1, pieces, jnp.float32, scale, arrived_0[pieces // 2 :]
+    )
     arrived_1 = [swap(piece, "dp", dp_bits[0]) for piece in send_1]
 
     updates, firsts, seconds, gathered = [], [], [], []

time: 136 us -> 136 us (level)
  transfers between devices with their start and end apart: 38 -> 38, of which waited for: 14 -> 16; matrix products, arithmetic and copies ran while one was open for 7% -> 7% of each run, Pallas kernels for 10% -> 10%
where the time goes in v9:
time: 136 us; the launch traced here: 135 us
  waiting for transfers between devices  68.8 us (51%)
  starting transfers between devices  35.3 us (26%)
  Pallas kernels  13.8 us (10%)
  other arithmetic  8.17 us (6%)
  local copies, waits for them, and re-layouts  4.71 us (3%)
  matrix products  3.42 us (3%)
    ppermute x38, waiting for transfers between devices, swap(): return lax.ppermute(value, axis, [(i, i ^ mask) for i in range(size)])  68.8 us
    ppermute x38, starting transfers between devices, swap(): return lax.ppermute(value, axis, [(i, i ^ mask) for i in range(size)])  35.3 us
    pallas_call x4, Pallas kernels, call_in_vmem(): pl.pallas_call(body, grid_spec=pltpu.PrefetchScalarGridSpec(num_scalar_pr...  7.25 us
    pallas_call x1, Pallas kernels, add_products(): pl.pallas_call(functools.partial(product_body, shape), grid_spec=pltpu.Pr...  5.8 us
    dot_general x2, matrix products, on_device(): lax.dot_general(own, jnp.concatenate(parts, axis=0), TRANSPOSED, preferre...  2.94 us
    another operation x2, other arithmetic, on_device(): return (update, jnp.stack(firsts), jnp.stack(seconds))  2.78 us
  transfers between devices with their start and end apart: 38, of which 16 were waited for; matrix products, arithmetic and copies ran while one was open for 7% of the time, Pallas kernels for 10%

profile of v9, /device:TPU:0, one launch (start us, length us, event | category | flops | bytes accessed | tf_op | source)
XLA Modules:
  0.0 135.2 jit_solution(9569460062106506748)
XLA Ops:
  0.6 1.1 slice_bitcast_fusion.1
  1.7 3.0 %collective-permute-start.2 = (bf16[128,1024]{1,0:T(8,128)(2,1)S(1)}, bf16[128,1024]{1,0:T(8,128)(2,1)S(1)}, u32[]{:S(2)}, u32[]{:S(2)}) collective-permute-start(bf16[128,1024]{1,0:T(8,128)(2,1)S(1)} %get-tuple-element.35), channel_id=1, source_target_pairs={{0,4},{1,5},{2,6},{3,7},{4,0},{5,1},{6,2},{7,3},{8,12},{9,13},{10,... | collective-permute-start | bytes 786440 | tf_op jit(solution)/shard_map/ppermute | solution.py:24
  4.7 1.6 %collective-permute-start = (bf16[128,1024]{1,0:T(8,128)(2,1)}, bf16[128,1024]{1,0:T(8,128)(2,1)S(1)}, u32[]{:S(2)}, u32[]{:S(2)}) collective-permute-start(bf16[128,1024]{1,0:T(8,128)(2,1)} %bitcast.53), channel_id=1, source_target_pairs={{0,8},{8,0},{16,24},{24,16},{1,9},{9,1},{17,25},{25,17},{2,10},{10... | collective-permute-start | bytes 786440 | tf_op jit(solution)/shard_map/ppermute | solution.py:24
  6.3 1.5 %collective-permute-start.1 = (bf16[128,1024]{1,0:T(8,128)(2,1)S(1)}, bf16[128,1024]{1,0:T(8,128)(2,1)S(1)}, u32[]{:S(2)}, u32[]{:S(2)}) collective-permute-start(bf16[128,1024]{1,0:T(8,128)(2,1)S(1)} %get-tuple-element.36), channel_id=1, source_target_pairs={{0,2},{1,3},{2,0},{3,1},{4,6},{5,7},{6,4},{7,5},{8,10},{9,11},{10,... | collective-permute-start | bytes 786440 | tf_op jit(solution)/shard_map/ppermute | solution.py:24
  7.8 0.7 and_compare_fusion.1
  8.5 0.1 broadcast_in_dim.34
  8.6 2.4 %collective-permute-done.2.refs_4_ = bf16[128,1024]{1,0:T(8,128)(2,1)S(1)} collective-permute-done((bf16[128,1024]{1,0:T(8,128)(2,1)S(1)}, bf16[128,1024]{1,0:T(8,128)(2,1)S(1)}, u32[]{:S(2)}, u32[]{:S(2)}) %collective-permute-start.2) | collective-permute-done | bytes 262176 | tf_op jit(solution)/shard_map/ppermute | solution.py:24
  11.0 1.7 %collective-permute-start.5 = (bf16[128,1024]{1,0:T(8,128)(2,1)S(1)}, bf16[128,1024]{1,0:T(8,128)(2,1)S(1)}, u32[]{:S(2)}, u32[]{:S(2)}) collective-permute-start(bf16[128,1024]{1,0:T(8,128)(2,1)S(1)} %get-tuple-element.36), channel_id=1, source_target_pairs={{0,4},{1,5},{2,6},{3,7},{4,0},{5,1},{6,2},{7,3},{8,12},{9,13},{10,... | collective-permute-start | bytes 786440 | tf_op jit(solution)/shard_map/ppermute | solution.py:24
  12.8 1.0 broadcast_select_fusion
  13.9 2.7 %collective-permute-start.3 = (bf16[128,1024]{1,0:T(8,128)(2,1)S(1)}, bf16[128,1024]{1,0:T(8,128)(2,1)}, u32[]{:S(2)}, u32[]{:S(2)}) collective-permute-start(bf16[128,1024]{1,0:T(8,128)(2,1)S(1)} %broadcast_select_fusion), channel_id=1, source_target_pairs={{0,16},{8,24},{16,0},{24,8},{1,17},{9,25},{17,1},{25,9},{2,18},{10... | collective-permute-start | bytes 786440 | tf_op jit(solution)/shard_map/ppermute | solution.py:24
  16.5 1.5 %collective-permute-start.4 = (bf16[128,1024]{1,0:T(8,128)(2,1)S(1)}, bf16[128,1024]{1,0:T(8,128)(2,1)S(1)}, u32[]{:S(2)}, u32[]{:S(2)}) collective-permute-start(bf16[128,1024]{1,0:T(8,128)(2,1)S(1)} %get-tuple-element.35), channel_id=1, source_target_pairs={{0,2},{1,3},{2,0},{3,1},{4,6},{5,7},{6,4},{7,5},{8,10},{9,11},{10,... | collective-permute-start | bytes 786440 | tf_op jit(solution)/shard_map/ppermute | solution.py:24
  18.0 0.5 collective-permute-start.7
  18.5 0.5 collective-permute-start.6
  19.1 1.1 slice_bitcast_fusion.refs_0_
  20.2 8.5 %collective-permute-done.7.refs_1_ = bf16[128,1024]{1,0:T(8,128)(2,1)S(1)} collective-permute-done((bf16[128,1024]{1,0:T(8,128)(2,1)S(1)}, bf16[128,1024]{1,0:T(8,128)(2,1)S(1)}, u32[]{:S(2)}, u32[]{:S(2)}) %collective-permute-start.7) | collective-permute-done | bytes 262176 | tf_op jit(solution)/shard_map/ppermute | solution.py:24
  28.8 0.5 collective-permute-start.12
  29.4 0.4 collective-permute-start.13
  29.9 0.1 broadcast_in_dim.31
  30.0 1.1 broadcast_select_fusion.1
  31.2 1.5 %collective-permute-start.10 = (bf16[128,1024]{1,0:T(8,128)(2,1)S(1)}, bf16[128,1024]{1,0:T(8,128)(2,1)S(1)}, u32[]{:S(2)}, u32[]{:S(2)}) collective-permute-start(bf16[128,1024]{1,0:T(8,128)(2,1)S(1)} %broadcast_select_fusion.1), channel_id=1, source_target_pairs={{0,6},{1,7},{2,4},{3,5},{4,2},{5,3},{6,0},{7,1},{8,14},{9,15},{10,... | collective-permute-start | bytes 786440 | tf_op jit(solution)/shard_map/ppermute | solution.py:24
  32.7 1.5 %collective-permute-start.9 = (bf16[128,1024]{1,0:T(8,128)(2,1)S(1)}, bf16[128,1024]{1,0:T(8,128)(2,1)S(1)}, u32[]{:S(2)}, u32[]{:S(2)}) collective-permute-start(bf16[128,1024]{1,0:T(8,128)(2,1)S(1)} %broadcast_select_fusion.1), channel_id=1, source_target_pairs={{0,4},{1,5},{2,6},{3,7},{4,0},{5,1},{6,2},{7,3},{8,12},{9,13},{10,... | collective-permute-start | bytes 786440 | tf_op jit(solution)/shard_map/ppermute | solution.py:24
  34.2 0.5 collective-permute-start.8
  34.8 2.2 %copy-done = bf16[2048,1024]{1,0:T(8,128)(2,1)S(1)} copy-done((bf16[2048,1024]{1,0:T(8,128)(2,1)S(1)}, bf16[2048,1024]{1,0:T(8,128)(2,1)}, u32[]{:S(2)}) %copy-start) | copy-done | bytes 4194328
  36.9 5.8 %shard_map.85.refs_5_ = f32[1024,1024]{1,0:T(8,128)S(1)} custom-call(s32[2]{0:T(128)S(1)} %pad_add_fusion.here, bf16[256,1024]{1,0:T(8,128)(2,1)S(1)} %slice_bitcast_fusion.refs_0_, bf16[128,1024]{1,0:T(8,128)(2,1)S(1)} %collective-permute-done.1.refs_1_, bf16[128,1024]{1,0:T(8,128)(2,1)S(1)} %collective-permute-done.4.refs_2_, ...), custom_call_target="tpu_custom_call" | custom-call | flops 3221225472 | bytes 10485760 | tf_op jit(solution)/shard_map/pallas_call | solution.py:209
  42.8 3.3 %collective-permute-done.9 = bf16[128,1024]{1,0:T(8,128)(2,1)S(1)} collective-permute-done((bf16[128,1024]{1,0:T(8,128)(2,1)S(1)}, bf16[128,1024]{1,0:T(8,128)(2,1)S(1)}, u32[]{:S(2)}, u32[]{:S(2)}) %collective-permute-start.9) | collective-permute-done | bytes 262176 | tf_op jit(solution)/shard_map/ppermute | solution.py:24
  46.1 0.1 collective-permute-start.16
  46.2 0.5 collective-permute-start.18
  46.8 2.1 %collective-permute-done.16.other = bf16[512,1024]{1,0:T(8,128)(2,1)S(1)} collective-permute-done((bf16[512,1024]{1,0:T(8,128)(2,1)S(1)}, bf16[512,1024]{1,0:T(8,128)(2,1)S(1)}, u32[]{:S(2)}, u32[]{:S(2)}) %collective-permute-start.16) | collective-permute-done | bytes 1048608 | tf_op jit(solution)/shard_map/ppermute | solution.py:24
  48.9 0.8 shard_map.86
  49.7 0.5 fusion.2.refs_0_
  50.1 1.6 %collective-permute-start.25 = (bf16[256,512]{1,0:T(8,128)(2,1)S(1)}, bf16[256,512]{1,0:T(8,128)(2,1)S(1)}, u32[]{:S(2)}, u32[]{:S(2)}) collective-permute-start(bf16[256,512]{1,0:T(8,128)(2,1)S(1)} %fusion.2.refs_0_), channel_id=1, source_target_pairs={{0,6},{1,7},{2,4},{3,5},{4,2},{5,3},{6,0},{7,1},{8,14},{9,15},{10,... | collective-permute-start | bytes 786440 | tf_op jit(solution)/shard_map/ppermute | solution.py:24
  51.7 0.7 collective-permute-start.24
  52.5 1.2 collective-permute-start.23
  53.7 2.4 %shard_map.87 = (bf16[1024,1024]{1,0:T(8,128)(2,1)S(1)}, bf16[128,1024]{1,0:T(8,128)(2,1)S(1)}, bf16[128,1024]{1,0:T(8,128)(2,1)S(1)}) custom-call(s32[2]{0:T(128)S(1)} %pad_add_fusion.here, bf16[128,1024]{1,0:T(8,128)(2,1)S(1)} %collective-permute-done.6.refs_0_, bf16[128,1024]{1,0:T(8,128)(2,1)S(1)} %collective-permute-done.7.refs_1_, ...), custom_call_target="tpu_custom_call" | custom-call | flops 1610612736 | bytes 13107200 | tf_op jit(solution)/shard_map/pallas_call | solution.py:131
  56.1 1.6 %collective-permute-start.20 = (bf16[128,1024]{1,0:T(8,128)(2,1)S(1)}, bf16[128,1024]{1,0:T(8,128)(2,1)S(1)}, u32[]{:S(2)}, u32[]{:S(2)}) collective-permute-start(bf16[128,1024]{1,0:T(8,128)(2,1)S(1)} %get-tuple-element.53), channel_id=1, source_target_pairs={{0,8},{8,0},{16,24},{24,16},{1,9},{9,1},{17,25},{25,17},{2,10},{10... | collective-permute-start | bytes 786440 | tf_op jit(solution)/shard_map/ppermute | solution.py:24
  57.8 1.2 shard_map.88
  59.0 1.3 collective-permute-done.25.refs_3_
  60.3 1.6 %collective-permute-start.19 = (bf16[128,1024]{1,0:T(8,128)(2,1)S(1)}, bf16[128,1024]{1,0:T(8,128)(2,1)S(1)}, u32[]{:S(2)}, u32[]{:S(2)}) collective-permute-start(bf16[128,1024]{1,0:T(8,128)(2,1)S(1)} %get-tuple-element.51), channel_id=1, source_target_pairs={{0,8},{8,0},{16,24},{24,16},{1,9},{9,1},{17,25},{25,17},{2,10},{10... | collective-permute-start | bytes 786440 | tf_op jit(solution)/shard_map/ppermute | solution.py:24
  61.9 3.2 %collective-permute-done.24.refs_2_ = bf16[256,512]{1,0:T(8,128)(2,1)S(1)} collective-permute-done((bf16[256,512]{1,0:T(8,128)(2,1)S(1)}, bf16[256,512]{1,0:T(8,128)(2,1)S(1)}, u32[]{:S(2)}, u32[]{:S(2)}) %collective-permute-start.24) | collective-permute-done | bytes 262176 | tf_op jit(solution)/shard_map/ppermute | solution.py:24
  65.1 0.5 collective-permute-start.28
  65.8 0.4 collective-permute-start.21
  66.2 0.4 collective-permute-done.29.refs_7_
  66.6 0.4 collective-permute-done.28.refs_6_
  67.0 0.4 collective-permute-done.27.refs_5_
  67.4 1.8 %shard_map.90 = (bf16[128,1024]{1,0:T(8,128)(2,1)S(1)}, bf16[128,1024]{1,0:T(8,128)(2,1)S(1)}) custom-call(s32[2]{0:T(128)S(1)} %pad_add_fusion.here, bf16[256,512]{1,0:T(8,128)(2,1)S(1)} %fusion.2.refs_0_, bf16[256,512]{1,0:T(8,128)(2,1)S(1)} %collective-permute-done.23.refs_1_, bf16[256,512]{1,0:T(8,128)(2,1)S(1)} %collective-permute-done.24.refs_2_, ...), custom_call_target="tpu_custom_call" | custom-call | flops 1073741824 | bytes 6815744 | tf_op jit(solution)/shard_map/pallas_call | solution.py:131
  69.2 1.6 %collective-permute-start.32 = (bf16[128,1024]{1,0:T(8,128)(2,1)S(1)}, bf16[128,1024]{1,0:T(8,128)(2,1)S(1)}, u32[]{:S(2)}, u32[]{:S(2)}) collective-permute-start(bf16[128,1024]{1,0:T(8,128)(2,1)S(1)} %get-tuple-element.59), channel_id=1, source_target_pairs={{0,8},{8,0},{16,24},{24,16},{1,9},{9,1},{17,25},{25,17},{2,10},{10... | collective-permute-start | bytes 786440 | tf_op jit(solution)/shard_map/ppermute | solution.py:24
  70.8 10.3 %collective-permute-done.21 = bf16[128,1024]{1,0:T(8,128)(2,1)S(1)} collective-permute-done((bf16[128,1024]{1,0:T(8,128)(2,1)S(1)}, bf16[128,1024]{1,0:T(8,128)(2,1)S(1)}, u32[]{:S(2)}, u32[]{:S(2)}) %collective-permute-start.21) | collective-permute-done | bytes 262176 | tf_op jit(solution)/shard_map/ppermute | solution.py:24
  81.1 1.2 divide_convert_fusion.1
  82.3 2.3 %collective-permute-start.22 = (bf16[128,1024]{1,0:T(8,128)(2,1)S(1)}, bf16[128,1024]{1,0:T(8,128)(2,1)}, u32[]{:S(2)}, u32[]{:S(2)}) collective-permute-start(bf16[128,1024]{1,0:T(8,128)(2,1)S(1)} %get-tuple-element.65), channel_id=1, source_target_pairs={{0,16},{8,24},{16,0},{24,8},{1,17},{9,25},{17,1},{25,9},{2,18},{10... | collective-permute-start | bytes 786440 | tf_op jit(solution)/shard_map/ppermute | solution.py:24
  84.6 1.8 %shard_map.89 = (f32[128,1024]{1,0:T(8,128)S(1)}, f32[128,1024]{1,0:T(8,128)S(1)}) custom-call(s32[2]{0:T(128)S(1)} %pad_add_fusion.here, bf16[256,512]{1,0:T(8,128)(2,1)S(1)} %fusion.2.refs_0_, bf16[256,512]{1,0:T(8,128)(2,1)S(1)} %collective-permute-done.23.refs_1_, bf16[256,512]{1,0:T(8,128)(2,1)S(1)} %collective-permute-done.24.refs_2_, ...), custom_call_target="tpu_custom_call" | custom-call | flops 1073741824 | bytes 7340032 | tf_op jit(solution)/shard_map/pallas_call | solution.py:131
  86.5 2.7 %collective-permute-start.33 = (bf16[128,1024]{1,0:T(8,128)(2,1)S(1)}, bf16[128,1024]{1,0:T(8,128)(2,1)S(1)}, u32[]{:S(2)}, u32[]{:S(2)}) collective-permute-start(bf16[128,1024]{1,0:T(8,128)(2,1)S(1)} %add_convert_fusion), channel_id=1, source_target_pairs={{0,16},{8,24},{16,0},{24,8},{1,17},{9,25},{17,1},{25,9},{2,18},{10... | collective-permute-start | bytes 786440 | tf_op jit(solution)/shard_map/ppermute | solution.py:24
  89.2 17.1 %collective-permute-done.30 = bf16[128,1024]{1,0:T(8,128)(2,1)S(1)} collective-permute-done((bf16[128,1024]{1,0:T(8,128)(2,1)S(1)}, bf16[128,1024]{1,0:T(8,128)(2,1)S(1)}, u32[]{:S(2)}, u32[]{:S(2)}) %collective-permute-start.30) | collective-permute-done | bytes 262176 | tf_op jit(solution)/shard_map/ppermute | solution.py:24
  106.4 1.6 %collective-permute-done.33 = bf16[128,1024]{1,0:T(8,128)(2,1)S(1)} collective-permute-done((bf16[128,1024]{1,0:T(8,128)(2,1)S(1)}, bf16[128,1024]{1,0:T(8,128)(2,1)S(1)}, u32[]{:S(2)}, u32[]{:S(2)}) %collective-permute-start.33) | collective-permute-done | bytes 262176 | tf_op jit(solution)/shard_map/ppermute | solution.py:24
  107.9 1.3 fusion.28
  109.3 0.3 collective-permute-start.35
  109.6 2.1 %collective-permute-start.31 = (bf16[128,1024]{1,0:T(8,128)(2,1)}, bf16[128,1024]{1,0:T(8,128)(2,1)}, u32[]{:S(2)}, u32[]{:S(2)}) collective-permute-start(bf16[128,1024]{1,0:T(8,128)(2,1)} %collective-permute-done.22), channel_id=1, source_target_pairs={{0,8},{8,0},{16,24},{24,16},{1,9},{9,1},{17,25},{25,17},{2,10},{10... | collective-permute-start | bytes 786440 | tf_op jit(solution)/shard_map/ppermute | solution.py:24
  111.8 9.9 %collective-permute-done.35 = bf16[128,1024]{1,0:T(8,128)(2,1)} collective-permute-done((bf16[128,1024]{1,0:T(8,128)(2,1)S(1)}, bf16[128,1024]{1,0:T(8,128)(2,1)}, u32[]{:S(2)}, u32[]{:S(2)}) %collective-permute-start.35) | collective-permute-done | bytes 262176 | tf_op jit(solution)/shard_map/ppermute | solution.py:24
  121.7 2.1 %collective-permute-done.31 = bf16[128,1024]{1,0:T(8,128)(2,1)} collective-permute-done((bf16[128,1024]{1,0:T(8,128)(2,1)}, bf16[128,1024]{1,0:T(8,128)(2,1)}, u32[]{:S(2)}, u32[]{:S(2)}) %collective-permute-start.31) | collective-permute-done | bytes 262176 | tf_op jit(solution)/shard_map/ppermute | solution.py:24
  123.8 1.5 %fusion = bf16[1,256,1024]{2,1,0:T(8,128)(2,1)S(1)} fusion(bf16[128,1024]{1,0:T(8,128)(2,1)S(1)} %get-tuple-element.65, bf16[128,1024]{1,0:T(8,128)(2,1)} %collective-permute-done.22, bf16[128,1024]{1,0:T(8,128)(2,1)S(1)} %collective-permute-done.34, bf16[128,1024]{1,0:T(8,128)(2,1)} %collective-permute-done.31, ...), kind=kOutput, calls=%fused_computation.2 | convolution fusion | flops 272891904 | bytes 1835012 | tf_op jit(solution)/shard_map/dot_general | solution.py:373
  125.3 1.5 %pad_maximum_fusion.2 = (f32[2,128,1024]{2,1,0:T(8,128)}, f32[2,128,1024]{2,1,0:T(8,128)}) fusion(f32[1,128,1024]{2,1,0:T(8,128)S(1)} %copy-done.4, f32[1,128,1024]{2,1,0:T(8,128)S(1)} %bitcast.52, f32[1,128,1024]{2,1,0:T(8,128)S(1)} %copy-done.3, f32[1,128,1024]{2,1,0:T(8,128)S(1)} %copy-done.2), kind=kLoop, calls=%fused_computation.22 | loop fusion | flops 524288 | bytes 4194304 | tf_op jit(solution)/shard_map/stack | solution.py:380
  126.8 2.5 %collective-permute-done.37 = bf16[128,1024]{1,0:T(8,128)(2,1)S(1)} collective-permute-done((bf16[128,1024]{1,0:T(8,128)(2,1)S(1)}, bf16[128,1024]{1,0:T(8,128)(2,1)S(1)}, u32[]{:S(2)}, u32[]{:S(2)}) %collective-permute-start.37) | collective-permute-done | bytes 262176 | tf_op jit(solution)/shard_map/ppermute | solution.py:24
  129.3 3.4 %collective-permute-done.36 = bf16[128,1024]{1,0:T(8,128)(2,1)S(1)} collective-permute-done((bf16[128,1024]{1,0:T(8,128)(2,1)}, bf16[128,1024]{1,0:T(8,128)(2,1)S(1)}, u32[]{:S(2)}, u32[]{:S(2)}) %collective-permute-start.36) | collective-permute-done | bytes 262176 | tf_op jit(solution)/shard_map/ppermute | solution.py:24
  132.7 1.4 %fusion.1 = bf16[1,256,1024]{2,1,0:T(8,128)(2,1)S(1)} fusion(bf16[128,1024]{1,0:T(8,128)(2,1)S(1)} %get-tuple-element.69, bf16[128,1024]{1,0:T(8,128)(2,1)} %collective-permute-done.35, bf16[128,1024]{1,0:T(8,128)(2,1)S(1)} %collective-permute-done.37, bf16[128,1024]{1,0:T(8,128)(2,1)S(1)} %collective-permute-done.36, ...), kind=kOutput, calls=%fused_computation.3 | convolution fusion | flops 272891904 | bytes 1835012 | tf_op jit(solution)/shard_map/dot_general | solution.py:373
  134.2 1.1 pad_maximum_fusion.1
  (64 shorter events, 1.0 us)
Async XLA Ops:
  1.7 9.3 %collective-permute-start.2 = (bf16[128,1024]{1,0:T(8,128)(2,1)S(1)}, bf16[128,1024]{1,0:T(8,128)(2,1)S(1)}, u32[]{:S(2)}, u32[]{:S(2)}) collective-permute-start(bf16[128,1024]{1,0:T(8,128)(2,1)S(1)} %get-tuple-element.35), channel_id=1, source_target_pairs={{0,4},{1,5},{2,6},{3,7},{4,0},{5,1},{6,2},{7,3},{8,12},{9,13},{10,... | collective-permute-start | bytes 786440 | tf_op jit(solution)/shard_map/ppermute | solution.py:24
  4.7 8.1 %collective-permute-start = (bf16[128,1024]{1,0:T(8,128)(2,1)}, bf16[128,1024]{1,0:T(8,128)(2,1)S(1)}, u32[]{:S(2)}, u32[]{:S(2)}) collective-permute-start(bf16[128,1024]{1,0:T(8,128)(2,1)} %bitcast.53), channel_id=1, source_target_pairs={{0,8},{8,0},{16,24},{24,16},{1,9},{9,1},{17,25},{25,17},{2,10},{10... | collective-permute-start | bytes 786440 | tf_op jit(solution)/shard_map/ppermute | solution.py:24
  6.3 7.5 %collective-permute-start.1 = (bf16[128,1024]{1,0:T(8,128)(2,1)S(1)}, bf16[128,1024]{1,0:T(8,128)(2,1)S(1)}, u32[]{:S(2)}, u32[]{:S(2)}) collective-permute-start(bf16[128,1024]{1,0:T(8,128)(2,1)S(1)} %get-tuple-element.36), channel_id=1, source_target_pairs={{0,2},{1,3},{2,0},{3,1},{4,6},{5,7},{6,4},{7,5},{8,10},{9,11},{10,... | collective-permute-start | bytes 786440 | tf_op jit(solution)/shard_map/ppermute | solution.py:24
  11.0 9.1 %collective-permute-start.5 = (bf16[128,1024]{1,0:T(8,128)(2,1)S(1)}, bf16[128,1024]{1,0:T(8,128)(2,1)S(1)}, u32[]{:S(2)}, u32[]{:S(2)}) collective-permute-start(bf16[128,1024]{1,0:T(8,128)(2,1)S(1)} %get-tuple-element.36), channel_id=1, source_target_pairs={{0,4},{1,5},{2,6},{3,7},{4,0},{5,1},{6,2},{7,3},{8,12},{9,13},{10,... | collective-permute-start | bytes 786440 | tf_op jit(solution)/shard_map/ppermute | solution.py:24
  13.8 14.9 %copy-start.8 = (bf16[128,1024]{1,0:T(8,128)(2,1)}, bf16[128,1024]{1,0:T(8,128)(2,1)S(1)}, u32[]{:S(2)}) copy-start(bf16[128,1024]{1,0:T(8,128)(2,1)S(1)} %broadcast_select_fusion) | copy-start | bytes 786436
  13.9 14.9 %collective-permute-start.3 = (bf16[128,1024]{1,0:T(8,128)(2,1)S(1)}, bf16[128,1024]{1,0:T(8,128)(2,1)}, u32[]{:S(2)}, u32[]{:S(2)}) collective-permute-start(bf16[128,1024]{1,0:T(8,128)(2,1)S(1)} %broadcast_select_fusion), channel_id=1, source_target_pairs={{0,16},{8,24},{16,0},{24,8},{1,17},{9,25},{17,1},{25,9},{2,18},{10... | collective-permute-start | bytes 786440 | tf_op jit(solution)/shard_map/ppermute | solution.py:24
  16.5 12.8 %collective-permute-start.4 = (bf16[128,1024]{1,0:T(8,128)(2,1)S(1)}, bf16[128,1024]{1,0:T(8,128)(2,1)S(1)}, u32[]{:S(2)}, u32[]{:S(2)}) collective-permute-start(bf16[128,1024]{1,0:T(8,128)(2,1)S(1)} %get-tuple-element.35), channel_id=1, source_target_pairs={{0,2},{1,3},{2,0},{3,1},{4,6},{5,7},{6,4},{7,5},{8,10},{9,11},{10,... | collective-permute-start | bytes 786440 | tf_op jit(solution)/shard_map/ppermute | solution.py:24
  18.0 10.7 %collective-permute-start.7 = (bf16[128,1024]{1,0:T(8,128)(2,1)S(1)}, bf16[128,1024]{1,0:T(8,128)(2,1)S(1)}, u32[]{:S(2)}, u32[]{:S(2)}) collective-permute-start(bf16[128,1024]{1,0:T(8,128)(2,1)S(1)} %collective-permute-done.2.refs_4_), channel_id=1, source_target_pairs={{0,2},{1,3},{2,0},{3,1},{4,6},{5,7},{6,4},{7,5},{8,10},{9,11},{10,... | collective-permute-start | bytes 786440 | tf_op jit(solution)/shard_map/ppermute | solution.py:24
  18.5 10.8 %collective-permute-start.6 = (bf16[128,1024]{1,0:T(8,128)(2,1)S(1)}, bf16[128,1024]{1,0:T(8,128)(2,1)S(1)}, u32[]{:S(2)}, u32[]{:S(2)}) collective-permute-start(bf16[128,1024]{1,0:T(8,128)(2,1)S(1)} %collective-permute-done.1.refs_1_), channel_id=1, source_target_pairs={{0,4},{1,5},{2,6},{3,7},{4,0},{5,1},{6,2},{7,3},{8,12},{9,13},{10,... | collective-permute-start | bytes 786440 | tf_op jit(solution)/shard_map/ppermute | solution.py:24
  20.1 14.1 %collective-permute-start.11 = (bf16[256,1024]{1,0:T(8,128)(2,1)S(1)}, bf16[256,1024]{1,0:T(8,128)(2,1)S(1)}, u32[]{:S(2)}, u32[]{:S(2)}) collective-permute-start(bf16[256,1024]{1,0:T(8,128)(2,1)S(1)} %slice_bitcast_fusion.refs_0_), channel_id=1, source_target_pairs={{0,1},{1,0},{2,3},{3,2},{4,5},{5,4},{6,7},{7,6},{8,9},{9,8},{10,11... | collective-permute-start | bytes 1572872 | tf_op jit(solution)/shard_map/ppermute | solution.py:24
  28.8 2.4 %collective-permute-start.15 = (bf16[128,1024]{1,0:T(8,128)(2,1)S(1)}, bf16[128,1024]{1,0:T(8,128)(2,1)S(1)}, u32[]{:S(2)}, u32[]{:S(2)}) collective-permute-start(bf16[128,1024]{1,0:T(8,128)(2,1)S(1)} %collective-permute-done.2.refs_4_), channel_id=1, source_target_pairs={{0,1},{1,0},{2,3},{3,2},{4,5},{5,4},{6,7},{7,6},{8,9},{9,8},{10,11... | collective-permute-start | bytes 786440 | tf_op jit(solution)/shard_map/ppermute | solution.py:24
  28.8 3.9 %collective-permute-start.12 = (bf16[128,1024]{1,0:T(8,128)(2,1)S(1)}, bf16[128,1024]{1,0:T(8,128)(2,1)S(1)}, u32[]{:S(2)}, u32[]{:S(2)}) collective-permute-start(bf16[128,1024]{1,0:T(8,128)(2,1)S(1)} %collective-permute-done.1.refs_1_), channel_id=1, source_target_pairs={{0,1},{1,0},{2,3},{3,2},{4,5},{5,4},{6,7},{7,6},{8,9},{9,8},{10,11... | collective-permute-start | bytes 786440 | tf_op jit(solution)/shard_map/ppermute | solution.py:24
  29.3 5.5 %collective-permute-start.14 = (bf16[128,1024]{1,0:T(8,128)(2,1)S(1)}, bf16[128,1024]{1,0:T(8,128)(2,1)S(1)}, u32[]{:S(2)}, u32[]{:S(2)}) collective-permute-start(bf16[128,1024]{1,0:T(8,128)(2,1)S(1)} %collective-permute-done.5.refs_3_), channel_id=1, source_target_pairs={{0,1},{1,0},{2,3},{3,2},{4,5},{5,4},{6,7},{7,6},{8,9},{9,8},{10,11... | collective-permute-start | bytes 786440 | tf_op jit(solution)/shard_map/ppermute | solution.py:24
  29.4 5.4 %collective-permute-start.13 = (bf16[128,1024]{1,0:T(8,128)(2,1)S(1)}, bf16[128,1024]{1,0:T(8,128)(2,1)}, u32[]{:S(2)}, u32[]{:S(2)}) collective-permute-start(bf16[128,1024]{1,0:T(8,128)(2,1)S(1)} %collective-permute-done.4.refs_2_), channel_id=1, source_target_pairs={{0,1},{1,0},{2,3},{3,2},{4,5},{5,4},{6,7},{7,6},{8,9},{9,8},{10,11... | collective-permute-start | bytes 786440 | tf_op jit(solution)/shard_map/ppermute | solution.py:24
  31.2 11.6 %collective-permute-start.10 = (bf16[128,1024]{1,0:T(8,128)(2,1)S(1)}, bf16[128,1024]{1,0:T(8,128)(2,1)S(1)}, u32[]{:S(2)}, u32[]{:S(2)}) collective-permute-start(bf16[128,1024]{1,0:T(8,128)(2,1)S(1)} %broadcast_select_fusion.1), channel_id=1, source_target_pairs={{0,6},{1,7},{2,4},{3,5},{4,2},{5,3},{6,0},{7,1},{8,14},{9,15},{10,... | collective-permute-start | bytes 786440 | tf_op jit(solution)/shard_map/ppermute | solution.py:24
  32.7 13.4 %collective-permute-start.9 = (bf16[128,1024]{1,0:T(8,128)(2,1)S(1)}, bf16[128,1024]{1,0:T(8,128)(2,1)S(1)}, u32[]{:S(2)}, u32[]{:S(2)}) collective-permute-start(bf16[128,1024]{1,0:T(8,128)(2,1)S(1)} %broadcast_select_fusion.1), channel_id=1, source_target_pairs={{0,4},{1,5},{2,6},{3,7},{4,0},{5,1},{6,2},{7,3},{8,12},{9,13},{10,... | collective-permute-start | bytes 786440 | tf_op jit(solution)/shard_map/ppermute | solution.py:24
  34.2 11.8 %collective-permute-start.8 = (bf16[128,1024]{1,0:T(8,128)(2,1)S(1)}, bf16[128,1024]{1,0:T(8,128)(2,1)S(1)}, u32[]{:S(2)}, u32[]{:S(2)}) collective-permute-start(bf16[128,1024]{1,0:T(8,128)(2,1)S(1)} %broadcast_select_fusion.1), channel_id=1, source_target_pairs={{0,2},{1,3},{2,0},{3,1},{4,6},{5,7},{6,4},{7,5},{8,10},{9,11},{10,... | collective-permute-start | bytes 786440 | tf_op jit(solution)/shard_map/ppermute | solution.py:24
  34.8 2.2 %copy-start = (bf16[2048,1024]{1,0:T(8,128)(2,1)S(1)}, bf16[2048,1024]{1,0:T(8,128)(2,1)}, u32[]{:S(2)}) copy-start(bf16[2048,1024]{1,0:T(8,128)(2,1)} %refs_8_.3) | copy-start | bytes 12582916
  42.8 6.9 %copy-start.5 = (bf16[2,256,1024]{2,1,0:T(8,128)(2,1)S(1)}, bf16[2,256,1024]{2,1,0:T(8,128)(2,1)}, u32[]{:S(2)}) copy-start(bf16[2,256,1024]{2,1,0:T(8,128)(2,1)} %param.7) | copy-start | bytes 3145732
  46.1 7.6 %copy-start.1 = (bf16[2048,1024]{1,0:T(8,128)(2,1)S(1)}, bf16[2048,1024]{1,0:T(8,128)(2,1)}, u32[]{:S(2)}) copy-start(bf16[2048,1024]{1,0:T(8,128)(2,1)} %refs_8_.3) | copy-start | bytes 12582916
  46.1 2.7 %collective-permute-start.16 = (bf16[512,1024]{1,0:T(8,128)(2,1)S(1)}, bf16[512,1024]{1,0:T(8,128)(2,1)S(1)}, u32[]{:S(2)}, u32[]{:S(2)}) collective-permute-start(bf16[512,1024]{1,0:T(8,128)(2,1)S(1)} %pad_maximum_fusion.same), channel_id=1, source_target_pairs={{0,1},{1,0},{2,3},{3,2},{4,5},{5,4},{6,7},{7,6},{8,9},{9,8},{10,11... | collective-permute-start | bytes 3145736 | tf_op jit(solution)/shard_map/ppermute | solution.py:24
  46.2 7.5 %collective-permute-start.18 = (bf16[128,1024]{1,0:T(8,128)(2,1)S(1)}, bf16[128,1024]{1,0:T(8,128)(2,1)S(1)}, u32[]{:S(2)}, u32[]{:S(2)}) collective-permute-start(bf16[128,1024]{1,0:T(8,128)(2,1)S(1)} %collective-permute-done.7.refs_1_), channel_id=1, source_target_pairs={{0,1},{1,0},{2,3},{3,2},{4,5},{5,4},{6,7},{7,6},{8,9},{9,8},{10,11... | collective-permute-start | bytes 786440 | tf_op jit(solution)/shard_map/ppermute | solution.py:24
  46.7 7.0 %collective-permute-start.17 = (bf16[128,1024]{1,0:T(8,128)(2,1)S(1)}, bf16[128,1024]{1,0:T(8,128)(2,1)S(1)}, u32[]{:S(2)}, u32[]{:S(2)}) collective-permute-start(bf16[128,1024]{1,0:T(8,128)(2,1)S(1)} %collective-permute-done.6.refs_0_), channel_id=1, source_target_pairs={{0,1},{1,0},{2,3},{3,2},{4,5},{5,4},{6,7},{7,6},{8,9},{9,8},{10,11... | collective-permute-start | bytes 786440 | tf_op jit(solution)/shard_map/ppermute | solution.py:24
  50.1 10.2 %collective-permute-start.25 = (bf16[256,512]{1,0:T(8,128)(2,1)S(1)}, bf16[256,512]{1,0:T(8,128)(2,1)S(1)}, u32[]{:S(2)}, u32[]{:S(2)}) collective-permute-start(bf16[256,512]{1,0:T(8,128)(2,1)S(1)} %fusion.2.refs_0_), channel_id=1, source_target_pairs={{0,6},{1,7},{2,4},{3,5},{4,2},{5,3},{6,0},{7,1},{8,14},{9,15},{10,... | collective-permute-start | bytes 786440 | tf_op jit(solution)/shard_map/ppermute | solution.py:24
  51.7 13.3 %collective-permute-start.24 = (bf16[256,512]{1,0:T(8,128)(2,1)S(1)}, bf16[256,512]{1,0:T(8,128)(2,1)S(1)}, u32[]{:S(2)}, u32[]{:S(2)}) collective-permute-start(bf16[256,512]{1,0:T(8,128)(2,1)S(1)} %fusion.2.refs_0_), channel_id=1, source_target_pairs={{0,4},{1,5},{2,6},{3,7},{4,0},{5,1},{6,2},{7,3},{8,12},{9,13},{10,... | collective-permute-start | bytes 786440 | tf_op jit(solution)/shard_map/ppermute | solution.py:24
  52.5 12.6 %collective-permute-start.23 = (bf16[256,512]{1,0:T(8,128)(2,1)S(1)}, bf16[256,512]{1,0:T(8,128)(2,1)S(1)}, u32[]{:S(2)}, u32[]{:S(2)}) collective-permute-start(bf16[256,512]{1,0:T(8,128)(2,1)S(1)} %fusion.2.refs_0_), channel_id=1, source_target_pairs={{0,2},{1,3},{2,0},{3,1},{4,6},{5,7},{6,4},{7,5},{8,10},{9,11},{10,... | collective-permute-start | bytes 786440 | tf_op jit(solution)/shard_map/ppermute | solution.py:24
  56.1 9.5 %collective-permute-start.20 = (bf16[128,1024]{1,0:T(8,128)(2,1)S(1)}, bf16[128,1024]{1,0:T(8,128)(2,1)S(1)}, u32[]{:S(2)}, u32[]{:S(2)}) collective-permute-start(bf16[128,1024]{1,0:T(8,128)(2,1)S(1)} %get-tuple-element.53), channel_id=1, source_target_pairs={{0,8},{8,0},{16,24},{24,16},{1,9},{9,1},{17,25},{25,17},{2,10},{10... | collective-permute-start | bytes 786440 | tf_op jit(solution)/shard_map/ppermute | solution.py:24
  57.8 8.0 %collective-permute-start.26 = (bf16[256,512]{1,0:T(8,128)(2,1)S(1)}, bf16[256,512]{1,0:T(8,128)(2,1)S(1)}, u32[]{:S(2)}, u32[]{:S(2)}) collective-permute-start(bf16[256,512]{1,0:T(8,128)(2,1)S(1)} %fusion.2.refs_0_), channel_id=1, source_target_pairs={{0,1},{1,0},{2,3},{3,2},{4,5},{5,4},{6,7},{7,6},{8,9},{9,8},{10,11... | collective-permute-start | bytes 786440 | tf_op jit(solution)/shard_map/ppermute | solution.py:24
  60.3 10.5 %collective-permute-start.19 = (bf16[128,1024]{1,0:T(8,128)(2,1)S(1)}, bf16[128,1024]{1,0:T(8,128)(2,1)S(1)}, u32[]{:S(2)}, u32[]{:S(2)}) collective-permute-start(bf16[128,1024]{1,0:T(8,128)(2,1)S(1)} %get-tuple-element.51), channel_id=1, source_target_pairs={{0,8},{8,0},{16,24},{24,16},{1,9},{9,1},{17,25},{25,17},{2,10},{10... | collective-permute-start | bytes 786440 | tf_op jit(solution)/shard_map/ppermute | solution.py:24
  65.1 1.5 %collective-permute-start.29 = (bf16[256,512]{1,0:T(8,128)(2,1)S(1)}, bf16[256,512]{1,0:T(8,128)(2,1)S(1)}, u32[]{:S(2)}, u32[]{:S(2)}) collective-permute-start(bf16[256,512]{1,0:T(8,128)(2,1)S(1)} %collective-permute-done.25.refs_3_), channel_id=1, source_target_pairs={{0,1},{1,0},{2,3},{3,2},{4,5},{5,4},{6,7},{7,6},{8,9},{9,8},{10,11... | collective-permute-start | bytes 786440 | tf_op jit(solution)/shard_map/ppermute | solution.py:24
  65.1 1.9 %collective-permute-start.28 = (bf16[256,512]{1,0:T(8,128)(2,1)S(1)}, bf16[256,512]{1,0:T(8,128)(2,1)S(1)}, u32[]{:S(2)}, u32[]{:S(2)}) collective-permute-start(bf16[256,512]{1,0:T(8,128)(2,1)S(1)} %collective-permute-done.24.refs_2_), channel_id=1, source_target_pairs={{0,1},{1,0},{2,3},{3,2},{4,5},{5,4},{6,7},{7,6},{8,9},{9,8},{10,11... | collective-permute-start | bytes 786440 | tf_op jit(solution)/shard_map/ppermute | solution.py:24
  65.6 1.8 %collective-permute-start.27 = (bf16[256,512]{1,0:T(8,128)(2,1)S(1)}, bf16[256,512]{1,0:T(8,128)(2,1)S(1)}, u32[]{:S(2)}, u32[]{:S(2)}) collective-permute-start(bf16[256,512]{1,0:T(8,128)(2,1)S(1)} %collective-permute-done.23.refs_1_), channel_id=1, source_target_pairs={{0,1},{1,0},{2,3},{3,2},{4,5},{5,4},{6,7},{7,6},{8,9},{9,8},{10,11... | collective-permute-start | bytes 786440 | tf_op jit(solution)/shard_map/ppermute | solution.py:24
  65.7 15.4 %copy-start.6 = (f32[2,128,1024]{2,1,0:T(8,128)S(1)}, f32[2,128,1024]{2,1,0:T(8,128)}, u32[]{:S(2)}) copy-start(f32[2,128,1024]{2,1,0:T(8,128)} %param.10) | copy-start | bytes 3145732
  65.7 15.4 %copy-start.7 = (f32[2,128,1024]{2,1,0:T(8,128)S(1)}, f32[2,128,1024]{2,1,0:T(8,128)}, u32[]{:S(2)}) copy-start(f32[2,128,1024]{2,1,0:T(8,128)} %param.9) | copy-start | bytes 3145732
  65.8 15.3 %collective-permute-start.21 = (bf16[128,1024]{1,0:T(8,128)(2,1)S(1)}, bf16[128,1024]{1,0:T(8,128)(2,1)S(1)}, u32[]{:S(2)}, u32[]{:S(2)}) collective-permute-start(bf16[128,1024]{1,0:T(8,128)(2,1)S(1)} %add_convert_fusion.1), channel_id=1, source_target_pairs={{0,16},{8,24},{16,0},{24,8},{1,17},{9,25},{17,1},{25,9},{2,18},{10... | collective-permute-start | bytes 786440 | tf_op jit(solution)/shard_map/ppermute | solution.py:24
  69.2 17.2 %collective-permute-start.32 = (bf16[128,1024]{1,0:T(8,128)(2,1)S(1)}, bf16[128,1024]{1,0:T(8,128)(2,1)S(1)}, u32[]{:S(2)}, u32[]{:S(2)}) collective-permute-start(bf16[128,1024]{1,0:T(8,128)(2,1)S(1)} %get-tuple-element.59), channel_id=1, source_target_pairs={{0,8},{8,0},{16,24},{24,16},{1,9},{9,1},{17,25},{25,17},{2,10},{10... | collective-permute-start | bytes 786440 | tf_op jit(solution)/shard_map/ppermute | solution.py:24
  82.3 24.1 %collective-permute-start.34 = (bf16[128,1024]{1,0:T(8,128)(2,1)S(1)}, bf16[128,1024]{1,0:T(8,128)(2,1)S(1)}, u32[]{:S(2)}, u32[]{:S(2)}) collective-permute-start(bf16[128,1024]{1,0:T(8,128)(2,1)S(1)} %get-tuple-element.65), channel_id=1, source_target_pairs={{0,8},{8,0},{16,24},{24,16},{1,9},{9,1},{17,25},{25,17},{2,10},{10... | collective-permute-start | bytes 786440 | tf_op jit(solution)/shard_map/ppermute | solution.py:24
  82.3 24.0 %collective-permute-start.22 = (bf16[128,1024]{1,0:T(8,128)(2,1)S(1)}, bf16[128,1024]{1,0:T(8,128)(2,1)}, u32[]{:S(2)}, u32[]{:S(2)}) collective-permute-start(bf16[128,1024]{1,0:T(8,128)(2,1)S(1)} %get-tuple-element.65), channel_id=1, source_target_pairs={{0,16},{8,24},{16,0},{24,8},{1,17},{9,25},{17,1},{25,9},{2,18},{10... | collective-permute-start | bytes 786440 | tf_op jit(solution)/shard_map/ppermute | solution.py:24
  84.6 21.7 %collective-permute-start.30 = (bf16[128,1024]{1,0:T(8,128)(2,1)S(1)}, bf16[128,1024]{1,0:T(8,128)(2,1)S(1)}, u32[]{:S(2)}, u32[]{:S(2)}) collective-permute-start(bf16[128,1024]{1,0:T(8,128)(2,1)S(1)} %get-tuple-element.56), channel_id=1, source_target_pairs={{0,8},{8,0},{16,24},{24,16},{1,9},{9,1},{17,25},{25,17},{2,10},{10... | collective-permute-start | bytes 786440 | tf_op jit(solution)/shard_map/ppermute | solution.py:24
  86.5 21.5 %collective-permute-start.33 = (bf16[128,1024]{1,0:T(8,128)(2,1)S(1)}, bf16[128,1024]{1,0:T(8,128)(2,1)S(1)}, u32[]{:S(2)}, u32[]{:S(2)}) collective-permute-start(bf16[128,1024]{1,0:T(8,128)(2,1)S(1)} %add_convert_fusion), channel_id=1, source_target_pairs={{0,16},{8,24},{16,0},{24,8},{1,17},{9,25},{17,1},{25,9},{2,18},{10... | collective-permute-start | bytes 786440 | tf_op jit(solution)/shard_map/ppermute | solution.py:24
  109.3 12.4 %collective-permute-start.35 = (bf16[128,1024]{1,0:T(8,128)(2,1)S(1)}, bf16[128,1024]{1,0:T(8,128)(2,1)}, u32[]{:S(2)}, u32[]{:S(2)}) collective-permute-start(bf16[128,1024]{1,0:T(8,128)(2,1)S(1)} %get-tuple-element.69), channel_id=1, source_target_pairs={{0,16},{8,24},{16,0},{24,8},{1,17},{9,25},{17,1},{25,9},{2,18},{10... | collective-permute-start | bytes 786440 | tf_op jit(solution)/shard_map/ppermute | solution.py:24
  109.6 14.2 %collective-permute-start.31 = (bf16[128,1024]{1,0:T(8,128)(2,1)}, bf16[128,1024]{1,0:T(8,128)(2,1)}, u32[]{:S(2)}, u32[]{:S(2)}) collective-permute-start(bf16[128,1024]{1,0:T(8,128)(2,1)} %collective-permute-done.22), channel_id=1, source_target_pairs={{0,8},{8,0},{16,24},{24,16},{1,9},{9,1},{17,25},{25,17},{2,10},{10... | collective-permute-start | bytes 786440 | tf_op jit(solution)/shard_map/ppermute | solution.py:24
  111.8 13.6 %copy-start.2 = (f32[1,128,1024]{2,1,0:T(8,128)S(1)}, f32[1,128,1024]{2,1,0:T(8,128)}, u32[]{:S(2)}) copy-start(f32[1,128,1024]{2,1,0:T(8,128)} %get-tuple-element.67) | copy-start | bytes 1572868
  111.8 13.6 %copy-start.3 = (f32[1,128,1024]{2,1,0:T(8,128)S(1)}, f32[1,128,1024]{2,1,0:T(8,128)}, u32[]{:S(2)}) copy-start(f32[1,128,1024]{2,1,0:T(8,128)} %get-tuple-element.68) | copy-start | bytes 1572868
  111.8 13.6 %copy-start.4 = (f32[1,128,1024]{2,1,0:T(8,128)S(1)}, f32[1,128,1024]{2,1,0:T(8,128)}, u32[]{:S(2)}) copy-start(f32[1,128,1024]{2,1,0:T(8,128)} %get-tuple-element.70) | copy-start | bytes 1572868
  111.8 17.5 %collective-permute-start.37 = (bf16[128,1024]{1,0:T(8,128)(2,1)S(1)}, bf16[128,1024]{1,0:T(8,128)(2,1)S(1)}, u32[]{:S(2)}, u32[]{:S(2)}) collective-permute-start(bf16[128,1024]{1,0:T(8,128)(2,1)S(1)} %get-tuple-element.69), channel_id=1, source_target_pairs={{0,8},{8,0},{16,24},{24,16},{1,9},{9,1},{17,25},{25,17},{2,10},{10... | collective-permute-start | bytes 786440 | tf_op jit(solution)/shard_map/ppermute | solution.py:24
  121.7 11.0 %collective-permute-start.36 = (bf16[128,1024]{1,0:T(8,128)(2,1)}, bf16[128,1024]{1,0:T(8,128)(2,1)S(1)}, u32[]{:S(2)}, u32[]{:S(2)}) collective-permute-start(bf16[128,1024]{1,0:T(8,128)(2,1)} %collective-permute-done.35), channel_id=1, source_target_pairs={{0,8},{8,0},{16,24},{24,16},{1,9},{9,1},{17,25},{25,17},{2,10},{10... | collective-permute-start | bytes 786440 | tf_op jit(solution)/shard_map/ppermute | solution.py:24

commit v10 on v9

--- a/solution.py
+++ b/solution.py
@@ -17,6 +17,7 @@
 
 TRANSPOSED = (((0,), (0,)), ((), ()))
 MIB = 1 << 20
+CUTS = 2
 
 
 def swap(value, axis, mask):
@@ -289,6 +290,7 @@
     scale = 1.0 / math.sqrt(layer_input.shape[0] * replicas)
     kv_share = candidates.shape[2] // replicas
     per = members // replicas
+    rank_share = moment_first.shape[1]
 
     order = [0]
     for bit in reversed(dp_bits):
@@ -325,13 +327,16 @@
     keep_0 = apply_rest(projectors[0], product, here, pieces, scale)
     arrived_0 = [swap(piece, "dp", dp_bits[0]) for piece in send_0]
 
-    def reduced(arrived, keeps):
+    def reduced(arrived, keeps, cuts=1):
         for bit in dp_bits[1:]:
             totals = [keep + piece.astype(jnp.float32) for piece, keep in zip(arrived, keeps)]
             half = len(totals) // 2
-            arrived = [swap(total.astype(jnp.bfloat16), "dp", bit) for total in totals[:half]]
+            sends = [total.astype(jnp.bfloat16) for total in totals[:half]]
+            if half == 1:
+                sends = jnp.split(sends[0], cuts)
+            arrived = [swap(piece, "dp", bit) for piece in sends]
             keeps = totals[half:]
-        return keeps[0], arrived[0]
+        return keeps[0], arrived
 
     heads = lax.dot_general(
         cotangent[1], projectors[1], (((1,), (1,)), ((), ())), preferred_element_type=jnp.float32
@@ -345,16 +350,24 @@
     )
     arrived_1 = [swap(piece, "dp", dp_bits[0]) for piece in send_1]
 
-    updates, firsts, seconds, gathered = [], [], [], []
-    open_1 = list(reduced(arrived_1, keep_1))
-    for matrix, (keep, received) in enumerate((open_0, open_1)):
-        if gathered:
-            received, firsts[0], *gathered[0][-3:-1] = lax.optimization_barrier(
-                (received, firsts[0], *gathered[0][-3:-1])
-            )
+    keep_1, received_1 = reduced(arrived_1, keep_1, CUTS)
+    units = [(0, 0, open_0[0], open_0[1][0])]
+    rows = rank_share // CUTS
+    for cut, piece in enumerate(received_1):
+        units.append((1, cut * rows, keep_1[cut * rows : (cut + 1) * rows], piece))
+    firsts, seconds, gathered = [], [], []
+    for unit, (matrix, start, keep, received) in enumerate(units):
+        if unit:
+            ahead = gathered[-1][-3 : -1 if unit == 1 else -2]
+            received, firsts[-1], *ahead = lax.optimization_barrier((received, firsts[-1], *ahead))
+            gathered[-1][-3 : -3 + len(ahead)] = ahead
         projected = keep + received.astype(jnp.float32)
-        first = beta_first * moment_first[matrix] + (1.0 - beta_first) * projected
-        second = beta_second * moment_second[matrix] + (1.0 - beta_second) * projected * projected
+        here_rows = slice(start, start + keep.shape[0])
+        first = beta_first * moment_first[matrix, here_rows] + (1.0 - beta_first) * projected
+        second = (
+            beta_second * moment_second[matrix, here_rows]
+            + (1.0 - beta_second) * projected * projected
+        )
         direction = (
             first
             / (1.0 - beta_first**STEP)
@@ -362,22 +375,32 @@
         )
         parts = [direction.astype(jnp.bfloat16)]
         for bit in reversed(dp_bits):
-            if matrix == 0 and bit == dp_bits[0] and len(parts) > 1:
-                parts[0], open_1[0] = lax.optimization_barrier((parts[0], open_1[0]))
+            if unit == 0 and bit == dp_bits[0] and len(parts) > 1:
+                parts[0], kept = lax.optimization_barrier((parts[0], keep_1))
+                units[1:] = [
+                    (m, at, kept[at : at + k.shape[0]], piece) for m, at, k, piece in units[1:]
+                ]
             parts = [swap(piece, "dp", bit) for piece in parts] + parts
         gathered.append(parts)
         firsts.append(first)
         seconds.append(second)
-    for parts, projector in zip(gathered, projectors):
-        own = lax.dynamic_slice_in_dim(projector, me_dp * kv_share, kv_share, 1)
-        update = lax.dot_general(
-            own, jnp.concatenate(parts, axis=0), TRANSPOSED, preferred_element_type=jnp.float32
+    values = [None] * MATS
+    for (matrix, start, keep, _), parts in zip(units, gathered):
+        own = lax.dynamic_slice_in_dim(projectors[matrix], me_dp * kv_share, kv_share, 1)
+        own = own.reshape(replicas, rank_share, kv_share)[:, start : start + keep.shape[0]]
+        value = lax.dot_general(
+            own.reshape(-1, kv_share),
+            jnp.concatenate(parts, axis=0),
+            TRANSPOSED,
+            preferred_element_type=jnp.float32,
         )
-        updates.append(update.astype(jnp.bfloat16))
-    update = jnp.zeros((MATS,) + updates[0].shape, updates[0].dtype)
-    for matrix in range(MATS):
-        update = lax.dynamic_update_slice(update, updates[matrix][None], (matrix, 0, 0))
-    return (update, jnp.stack(firsts), jnp.stack(seconds))
+        values[matrix] = value if values[matrix] is None else values[matrix] + value
+    update = jnp.stack([value.astype(jnp.bfloat16) for value in values])
+    return (
+        update,
+        jnp.concatenate(firsts, axis=0).reshape(moment_first.shape),
+        jnp.concatenate(seconds, axis=0).reshape(moment_second.shape),
+    )
 
 
 def solution(mesh):

time: 136 us -> 137 us (level)
  starting transfers between devices: 35.3 us -> 39.9 us
  waiting for transfers between devices: 68.8 us -> 64.7 us
    ppermute x38 -> x42, starting transfers between devices: 35.3 us -> 39.9 us  [swap(): return lax.ppermute(value, axis, [(i, i ^ mask) for i in range(size)])]
    ppermute x38 -> x42, waiting for transfers between devices: 68.8 us -> 64.7 us  [swap(): return lax.ppermute(value, axis, [(i, i ^ mask) for i in range(size)])]
    convert_element_type x1 -> x3, other arithmetic: 1.2 us -> 3.36 us  [on_device(): parts = [direction.astype(jnp.bfloat16)]]
    another operation x2 -> x1, other arithmetic: 2.78 us -> 1.06 us  [on_device(): update = jnp.stack([value.astype(jnp.bfloat16) for value in values])]
    concatenate x0 -> x1, other arithmetic: none -> 1.48 us  [on_device(): jnp.concatenate(firsts, axis=0).reshape(moment_first.shape)]
    dot_general x2 -> x3, matrix products: 2.94 us -> 2.03 us  [on_device(): lax.dot_general(own.reshape(-1, kv_share), jnp.concatenate(parts, axis=0)...]
  transfers between devices with their start and end apart: 38 -> 42, of which waited for: 16 -> 17; matrix products, arithmetic and copies ran while one was open for 7% -> 8% of each run, Pallas kernels for 10% -> 10%
where the time goes in v10:
time: 137 us
  waiting for transfers between devices  64.7 us (47%)
  starting transfers between devices  39.9 us (29%)
  Pallas kernels  13.9 us (10%)
  other arithmetic  9.03 us (7%)
  local copies, waits for them, and re-layouts  5.46 us (4%)
  matrix products  2.51 us (2%)
    ppermute x42, waiting for transfers between devices, swap(): return lax.ppermute(value, axis, [(i, i ^ mask) for i in range(size)])  64.7 us
    ppermute x42, starting transfers between devices, swap(): return lax.ppermute(value, axis, [(i, i ^ mask) for i in range(size)])  39.9 us
    pallas_call x4, Pallas kernels, call_in_vmem(): pl.pallas_call(body, grid_spec=pltpu.PrefetchScalarGridSpec(num_scalar_pr...  7.24 us
    pallas_call x1, Pallas kernels, add_products(): pl.pallas_call(functools.partial(product_body, shape), grid_spec=pltpu.Pr...  5.8 us
    convert_element_type x3, other arithmetic, on_device(): parts = [direction.astype(jnp.bfloat16)]  3.36 us
  transfers between devices with their start and end apart: 42, of which 17 were waited for; matrix products, arithmetic and copies ran while one was open for 8% of the time, Pallas kernels for 10%

profile of v10, /device:TPU:0, one launch (start us, length us, event | category | flops | bytes accessed | tf_op | source)
XLA Modules:
  0.0 136.5 jit_solution(5261962341003847745)
XLA Ops:
  0.6 1.1 slice_bitcast_fusion.1
  1.7 3.0 %collective-permute-start.2 = (bf16[128,1024]{1,0:T(8,128)(2,1)S(1)}, bf16[128,1024]{1,0:T(8,128)(2,1)S(1)}, u32[]{:S(2)}, u32[]{:S(2)}) collective-permute-start(bf16[128,1024]{1,0:T(8,128)(2,1)S(1)} %get-tuple-element.38), channel_id=1, source_target_pairs={{0,4},{1,5},{2,6},{3,7},{4,0},{5,1},{6,2},{7,3},{8,12},{9,13},{10,... | collective-permute-start | bytes 786440 | tf_op jit(solution)/shard_map/ppermute | solution.py:25
  4.7 1.6 %collective-permute-start = (bf16[128,1024]{1,0:T(8,128)(2,1)}, bf16[128,1024]{1,0:T(8,128)(2,1)S(1)}, u32[]{:S(2)}, u32[]{:S(2)}) collective-permute-start(bf16[128,1024]{1,0:T(8,128)(2,1)} %bitcast.52), channel_id=1, source_target_pairs={{0,8},{8,0},{16,24},{24,16},{1,9},{9,1},{17,25},{25,17},{2,10},{10... | collective-permute-start | bytes 786440 | tf_op jit(solution)/shard_map/ppermute | solution.py:25
  6.3 1.5 %collective-permute-start.1 = (bf16[128,1024]{1,0:T(8,128)(2,1)S(1)}, bf16[128,1024]{1,0:T(8,128)(2,1)S(1)}, u32[]{:S(2)}, u32[]{:S(2)}) collective-permute-start(bf16[128,1024]{1,0:T(8,128)(2,1)S(1)} %get-tuple-element.39), channel_id=1, source_target_pairs={{0,2},{1,3},{2,0},{3,1},{4,6},{5,7},{6,4},{7,5},{8,10},{9,11},{10,... | collective-permute-start | bytes 786440 | tf_op jit(solution)/shard_map/ppermute | solution.py:25
  7.8 0.7 and_compare_fusion.1
  8.6 2.4 %collective-permute-done.2.refs_4_ = bf16[128,1024]{1,0:T(8,128)(2,1)S(1)} collective-permute-done((bf16[128,1024]{1,0:T(8,128)(2,1)S(1)}, bf16[128,1024]{1,0:T(8,128)(2,1)S(1)}, u32[]{:S(2)}, u32[]{:S(2)}) %collective-permute-start.2) | collective-permute-done | bytes 262176 | tf_op jit(solution)/shard_map/ppermute | solution.py:25
  11.0 1.7 %collective-permute-start.5 = (bf16[128,1024]{1,0:T(8,128)(2,1)S(1)}, bf16[128,1024]{1,0:T(8,128)(2,1)S(1)}, u32[]{:S(2)}, u32[]{:S(2)}) collective-permute-start(bf16[128,1024]{1,0:T(8,128)(2,1)S(1)} %get-tuple-element.39), channel_id=1, source_target_pairs={{0,4},{1,5},{2,6},{3,7},{4,0},{5,1},{6,2},{7,3},{8,12},{9,13},{10,... | collective-permute-start | bytes 786440 | tf_op jit(solution)/shard_map/ppermute | solution.py:25
  12.8 1.0 broadcast_select_fusion
  13.9 2.7 %collective-permute-start.3 = (bf16[128,1024]{1,0:T(8,128)(2,1)S(1)}, bf16[128,1024]{1,0:T(8,128)(2,1)}, u32[]{:S(2)}, u32[]{:S(2)}) collective-permute-start(bf16[128,1024]{1,0:T(8,128)(2,1)S(1)} %broadcast_select_fusion), channel_id=1, source_target_pairs={{0,16},{8,24},{16,0},{24,8},{1,17},{9,25},{17,1},{25,9},{2,18},{10... | collective-permute-start | bytes 786440 | tf_op jit(solution)/shard_map/ppermute | solution.py:25
  16.5 1.5 %collective-permute-start.4 = (bf16[128,1024]{1,0:T(8,128)(2,1)S(1)}, bf16[128,1024]{1,0:T(8,128)(2,1)S(1)}, u32[]{:S(2)}, u32[]{:S(2)}) collective-permute-start(bf16[128,1024]{1,0:T(8,128)(2,1)S(1)} %get-tuple-element.38), channel_id=1, source_target_pairs={{0,2},{1,3},{2,0},{3,1},{4,6},{5,7},{6,4},{7,5},{8,10},{9,11},{10,... | collective-permute-start | bytes 786440 | tf_op jit(solution)/shard_map/ppermute | solution.py:25
  18.0 0.5 collective-permute-start.7
  18.5 0.5 collective-permute-start.6
  19.1 1.1 slice_bitcast_fusion.refs_0_
  20.2 8.5 %collective-permute-done.7.refs_1_ = bf16[128,1024]{1,0:T(8,128)(2,1)S(1)} collective-permute-done((bf16[128,1024]{1,0:T(8,128)(2,1)S(1)}, bf16[128,1024]{1,0:T(8,128)(2,1)S(1)}, u32[]{:S(2)}, u32[]{:S(2)}) %collective-permute-start.7) | collective-permute-done | bytes 262176 | tf_op jit(solution)/shard_map/ppermute | solution.py:25
  28.8 0.5 collective-permute-start.12
  29.4 0.4 collective-permute-start.13
  30.0 1.1 broadcast_select_fusion.1
  31.2 1.5 %collective-permute-start.10 = (bf16[128,1024]{1,0:T(8,128)(2,1)S(1)}, bf16[128,1024]{1,0:T(8,128)(2,1)S(1)}, u32[]{:S(2)}, u32[]{:S(2)}) collective-permute-start(bf16[128,1024]{1,0:T(8,128)(2,1)S(1)} %broadcast_select_fusion.1), channel_id=1, source_target_pairs={{0,6},{1,7},{2,4},{3,5},{4,2},{5,3},{6,0},{7,1},{8,14},{9,15},{10,... | collective-permute-start | bytes 786440 | tf_op jit(solution)/shard_map/ppermute | solution.py:25
  32.7 1.5 %collective-permute-start.9 = (bf16[128,1024]{1,0:T(8,128)(2,1)S(1)}, bf16[128,1024]{1,0:T(8,128)(2,1)S(1)}, u32[]{:S(2)}, u32[]{:S(2)}) collective-permute-start(bf16[128,1024]{1,0:T(8,128)(2,1)S(1)} %broadcast_select_fusion.1), channel_id=1, source_target_pairs={{0,4},{1,5},{2,6},{3,7},{4,0},{5,1},{6,2},{7,3},{8,12},{9,13},{10,... | collective-permute-start | bytes 786440 | tf_op jit(solution)/shard_map/ppermute | solution.py:25
  34.2 0.5 collective-permute-start.8
  34.8 2.2 %copy-done = bf16[2048,1024]{1,0:T(8,128)(2,1)S(1)} copy-done((bf16[2048,1024]{1,0:T(8,128)(2,1)S(1)}, bf16[2048,1024]{1,0:T(8,128)(2,1)}, u32[]{:S(2)}) %copy-start) | copy-done | bytes 4194328
  36.9 5.8 %shard_map.85.refs_5_ = f32[1024,1024]{1,0:T(8,128)S(1)} custom-call(s32[2]{0:T(128)S(1)} %pad_add_fusion.here, bf16[256,1024]{1,0:T(8,128)(2,1)S(1)} %slice_bitcast_fusion.refs_0_, bf16[128,1024]{1,0:T(8,128)(2,1)S(1)} %collective-permute-done.1.refs_1_, bf16[128,1024]{1,0:T(8,128)(2,1)S(1)} %collective-permute-done.4.refs_2_, ...), custom_call_target="tpu_custom_call" | custom-call | flops 3221225472 | bytes 10485760 | tf_op jit(solution)/shard_map/pallas_call | solution.py:210
  42.8 3.3 %collective-permute-done.9 = bf16[128,1024]{1,0:T(8,128)(2,1)S(1)} collective-permute-done((bf16[128,1024]{1,0:T(8,128)(2,1)S(1)}, bf16[128,1024]{1,0:T(8,128)(2,1)S(1)}, u32[]{:S(2)}, u32[]{:S(2)}) %collective-permute-start.9) | collective-permute-done | bytes 262176 | tf_op jit(solution)/shard_map/ppermute | solution.py:25
  46.2 0.5 collective-permute-start.18
  46.8 2.1 %collective-permute-done.16.other = bf16[512,1024]{1,0:T(8,128)(2,1)S(1)} collective-permute-done((bf16[512,1024]{1,0:T(8,128)(2,1)S(1)}, bf16[512,1024]{1,0:T(8,128)(2,1)S(1)}, u32[]{:S(2)}, u32[]{:S(2)}) %collective-permute-start.16) | collective-permute-done | bytes 1048608 | tf_op jit(solution)/shard_map/ppermute | solution.py:25
  48.9 0.8 shard_map.86
  49.7 0.5 fusion.3.refs_0_
  50.2 1.6 %collective-permute-start.25 = (bf16[256,512]{1,0:T(8,128)(2,1)S(1)}, bf16[256,512]{1,0:T(8,128)(2,1)S(1)}, u32[]{:S(2)}, u32[]{:S(2)}) collective-permute-start(bf16[256,512]{1,0:T(8,128)(2,1)S(1)} %fusion.3.refs_0_), channel_id=1, source_target_pairs={{0,6},{1,7},{2,4},{3,5},{4,2},{5,3},{6,0},{7,1},{8,14},{9,15},{10,... | collective-permute-start | bytes 786440 | tf_op jit(solution)/shard_map/ppermute | solution.py:25
  51.8 0.7 collective-permute-start.24
  52.5 1.2 collective-permute-start.23
  53.8 2.4 %shard_map.87 = (bf16[1024,1024]{1,0:T(8,128)(2,1)S(1)}, bf16[128,1024]{1,0:T(8,128)(2,1)S(1)}, bf16[128,1024]{1,0:T(8,128)(2,1)S(1)}) custom-call(s32[2]{0:T(128)S(1)} %pad_add_fusion.here, bf16[128,1024]{1,0:T(8,128)(2,1)S(1)} %collective-permute-done.6.refs_0_, bf16[128,1024]{1,0:T(8,128)(2,1)S(1)} %collective-permute-done.7.refs_1_, ...), custom_call_target="tpu_custom_call" | custom-call | flops 1610612736 | bytes 13107200 | tf_op jit(solution)/shard_map/pallas_call | solution.py:132
  56.1 1.6 %collective-permute-start.20 = (bf16[128,1024]{1,0:T(8,128)(2,1)S(1)}, bf16[128,1024]{1,0:T(8,128)(2,1)S(1)}, u32[]{:S(2)}, u32[]{:S(2)}) collective-permute-start(bf16[128,1024]{1,0:T(8,128)(2,1)S(1)} %get-tuple-element.56), channel_id=1, source_target_pairs={{0,8},{8,0},{16,24},{24,16},{1,9},{9,1},{17,25},{25,17},{2,10},{10... | collective-permute-start | bytes 786440 | tf_op jit(solution)/shard_map/ppermute | solution.py:25
  57.8 1.2 shard_map.88
  59.0 1.3 collective-permute-done.25.refs_3_
  60.3 1.6 %collective-permute-start.19 = (bf16[128,1024]{1,0:T(8,128)(2,1)S(1)}, bf16[128,1024]{1,0:T(8,128)(2,1)S(1)}, u32[]{:S(2)}, u32[]{:S(2)}) collective-permute-start(bf16[128,1024]{1,0:T(8,128)(2,1)S(1)} %get-tuple-element.54), channel_id=1, source_target_pairs={{0,8},{8,0},{16,24},{24,16},{1,9},{9,1},{17,25},{25,17},{2,10},{10... | collective-permute-start | bytes 786440 | tf_op jit(solution)/shard_map/ppermute | solution.py:25
  61.9 3.2 %collective-permute-done.24.refs_2_ = bf16[256,512]{1,0:T(8,128)(2,1)S(1)} collective-permute-done((bf16[256,512]{1,0:T(8,128)(2,1)S(1)}, bf16[256,512]{1,0:T(8,128)(2,1)S(1)}, u32[]{:S(2)}, u32[]{:S(2)}) %collective-permute-start.24) | collective-permute-done | bytes 262176 | tf_op jit(solution)/shard_map/ppermute | solution.py:25
  65.1 0.5 collective-permute-start.28
  65.8 0.4 collective-permute-start.21
  66.2 0.4 collective-permute-done.29.refs_7_
  66.7 0.4 collective-permute-done.28.refs_6_
  67.0 0.4 collective-permute-done.27.refs_5_
  67.4 1.8 %shard_map.90 = (bf16[128,1024]{1,0:T(8,128)(2,1)S(1)}, bf16[128,1024]{1,0:T(8,128)(2,1)S(1)}) custom-call(s32[2]{0:T(128)S(1)} %pad_add_fusion.here, bf16[256,512]{1,0:T(8,128)(2,1)S(1)} %fusion.3.refs_0_, bf16[256,512]{1,0:T(8,128)(2,1)S(1)} %collective-permute-done.23.refs_1_, bf16[256,512]{1,0:T(8,128)(2,1)S(1)} %collective-permute-done.24.refs_2_, ...), custom_call_target="tpu_custom_call" | custom-call | flops 1073741824 | bytes 6815744 | tf_op jit(solution)/shard_map/pallas_call | solution.py:132
  69.2 1.6 %collective-permute-start.32 = (bf16[128,1024]{1,0:T(8,128)(2,1)S(1)}, bf16[128,1024]{1,0:T(8,128)(2,1)S(1)}, u32[]{:S(2)}, u32[]{:S(2)}) collective-permute-start(bf16[128,1024]{1,0:T(8,128)(2,1)S(1)} %get-tuple-element.62), channel_id=1, source_target_pairs={{0,8},{8,0},{16,24},{24,16},{1,9},{9,1},{17,25},{25,17},{2,10},{10... | collective-permute-start | bytes 786440 | tf_op jit(solution)/shard_map/ppermute | solution.py:25
  70.9 10.3 %collective-permute-done.21 = bf16[128,1024]{1,0:T(8,128)(2,1)S(1)} collective-permute-done((bf16[128,1024]{1,0:T(8,128)(2,1)S(1)}, bf16[128,1024]{1,0:T(8,128)(2,1)S(1)}, u32[]{:S(2)}, u32[]{:S(2)}) %collective-permute-start.21) | collective-permute-done | bytes 262176 | tf_op jit(solution)/shard_map/ppermute | solution.py:25
  81.1 1.2 divide_convert_fusion
  82.3 2.3 %collective-permute-start.22 = (bf16[128,1024]{1,0:T(8,128)(2,1)S(1)}, bf16[128,1024]{1,0:T(8,128)(2,1)S(1)}, u32[]{:S(2)}, u32[]{:S(2)}) collective-permute-start(bf16[128,1024]{1,0:T(8,128)(2,1)S(1)} %get-tuple-element.77), channel_id=1, source_target_pairs={{0,16},{8,24},{16,0},{24,8},{1,17},{9,25},{17,1},{25,9},{2,18},{10... | collective-permute-start | bytes 786440 | tf_op jit(solution)/shard_map/ppermute | solution.py:25
  84.6 1.8 %shard_map.89 = (f32[128,1024]{1,0:T(8,128)S(1)}, f32[128,1024]{1,0:T(8,128)S(1)}) custom-call(s32[2]{0:T(128)S(1)} %pad_add_fusion.here, bf16[256,512]{1,0:T(8,128)(2,1)S(1)} %fusion.3.refs_0_, bf16[256,512]{1,0:T(8,128)(2,1)S(1)} %collective-permute-done.23.refs_1_, bf16[256,512]{1,0:T(8,128)(2,1)S(1)} %collective-permute-done.24.refs_2_, ...), custom_call_target="tpu_custom_call" | custom-call | flops 1073741824 | bytes 7340032 | tf_op jit(solution)/shard_map/pallas_call | solution.py:132
  86.5 0.7 fusion.40
  87.2 2.7 %collective-permute-start.33 = (bf16[64,1024]{1,0:T(8,128)(2,1)S(1)}, bf16[64,1024]{1,0:T(8,128)(2,1)S(1)}, u32[]{:S(2)}, u32[]{:S(2)}) collective-permute-start(bf16[64,1024]{1,0:T(8,128)(2,1)S(1)} %get-tuple-element.84), channel_id=1, source_target_pairs={{0,16},{8,24},{16,0},{24,8},{1,17},{9,25},{17,1},{25,9},{2,18},{10... | collective-permute-start | bytes 393224 | tf_op jit(solution)/shard_map/ppermute | solution.py:25
  89.9 14.3 %collective-permute-done.30 = bf16[128,1024]{1,0:T(8,128)(2,1)S(1)} collective-permute-done((bf16[128,1024]{1,0:T(8,128)(2,1)S(1)}, bf16[128,1024]{1,0:T(8,128)(2,1)S(1)}, u32[]{:S(2)}, u32[]{:S(2)}) %collective-permute-start.30) | collective-permute-done | bytes 262176 | tf_op jit(solution)/shard_map/ppermute | solution.py:25
  104.4 0.9 divide_convert_fusion.2
  105.3 2.4 %collective-permute-start.38 = (bf16[64,1024]{1,0:T(8,128)(2,1)S(1)}, bf16[64,1024]{1,0:T(8,128)(2,1)}, u32[]{:S(2)}, u32[]{:S(2)}) collective-permute-start(bf16[64,1024]{1,0:T(8,128)(2,1)S(1)} %get-tuple-element.74), channel_id=1, source_target_pairs={{0,8},{8,0},{16,24},{24,16},{1,9},{9,1},{17,25},{25,17},{2,10},{10... | collective-permute-start | bytes 393224 | tf_op jit(solution)/shard_map/ppermute | solution.py:25
  107.9 2.4 %collective-permute-start.35 = (bf16[64,1024]{1,0:T(8,128)(2,1)S(1)}, bf16[64,1024]{1,0:T(8,128)(2,1)S(1)}, u32[]{:S(2)}, u32[]{:S(2)}) collective-permute-start(bf16[64,1024]{1,0:T(8,128)(2,1)S(1)} %get-tuple-element.74), channel_id=1, source_target_pairs={{0,16},{8,24},{16,0},{24,8},{1,17},{9,25},{17,1},{25,9},{2,18},{10... | collective-permute-start | bytes 393224 | tf_op jit(solution)/shard_map/ppermute | solution.py:25
  110.3 2.1 %collective-permute-done.37 = bf16[64,1024]{1,0:T(8,128)(2,1)} collective-permute-done((bf16[64,1024]{1,0:T(8,128)(2,1)}, bf16[64,1024]{1,0:T(8,128)(2,1)}, u32[]{:S(2)}, u32[]{:S(2)}) %collective-permute-start.37) | collective-permute-done | bytes 131104 | tf_op jit(solution)/shard_map/ppermute | solution.py:25
  112.4 5.4 %collective-permute-done.38 = bf16[64,1024]{1,0:T(8,128)(2,1)} collective-permute-done((bf16[64,1024]{1,0:T(8,128)(2,1)S(1)}, bf16[64,1024]{1,0:T(8,128)(2,1)}, u32[]{:S(2)}, u32[]{:S(2)}) %collective-permute-start.38) | collective-permute-done | bytes 131104 | tf_op jit(solution)/shard_map/ppermute | solution.py:25
  117.8 1.3 divide_convert_fusion.1
  119.3 3.6 %collective-permute-done.31 = bf16[128,1024]{1,0:T(8,128)(2,1)S(1)} collective-permute-done((bf16[128,1024]{1,0:T(8,128)(2,1)}, bf16[128,1024]{1,0:T(8,128)(2,1)S(1)}, u32[]{:S(2)}, u32[]{:S(2)}) %collective-permute-start.31) | collective-permute-done | bytes 262176 | tf_op jit(solution)/shard_map/ppermute | solution.py:25
  122.9 0.5 fusion.2
  123.5 2.0 %collective-permute-start.36 = (bf16[64,1024]{1,0:T(8,128)(2,1)S(1)}, bf16[64,1024]{1,0:T(8,128)(2,1)S(1)}, u32[]{:S(2)}, u32[]{:S(2)}) collective-permute-start(bf16[64,1024]{1,0:T(8,128)(2,1)S(1)} %collective-permute-done.35), channel_id=1, source_target_pairs={{0,8},{8,0},{16,24},{24,16},{1,9},{9,1},{17,25},{25,17},{2,10},{10... | collective-permute-start | bytes 393224 | tf_op jit(solution)/shard_map/ppermute | solution.py:25
  125.6 1.5 %pad_maximum_fusion.2 = (f32[256,1024]{1,0:T(8,128)}, f32[256,1024]{1,0:T(8,128)}) fusion(f32[64,1024]{1,0:T(8,128)S(1)} %get-tuple-element.72, f32[64,1024]{1,0:T(8,128)S(1)} %copy-done.4, f32[128,1024]{1,0:T(8,128)S(1)} %copy-done.2, f32[64,1024]{1,0:T(8,128)S(1)} %get-tuple-element.73, f32[64,1024]{1,0:T(8,128)S(1)} %get-tuple-element.75, ...), kind=kLoop, calls=%fused_computation.16 | loop fusion | flops 1048576 | bytes 4194304 | tf_op jit(solution)/shard_map/concatenate | solution.py:401
  127.1 2.8 %collective-permute-done.41 = bf16[64,1024]{1,0:T(8,128)(2,1)S(1)} collective-permute-done((bf16[64,1024]{1,0:T(8,128)(2,1)S(1)}, bf16[64,1024]{1,0:T(8,128)(2,1)S(1)}, u32[]{:S(2)}, u32[]{:S(2)}) %collective-permute-start.41) | collective-permute-done | bytes 131104 | tf_op jit(solution)/shard_map/ppermute | solution.py:25
  129.9 4.0 %collective-permute-done.40 = bf16[64,1024]{1,0:T(8,128)(2,1)S(1)} collective-permute-done((bf16[64,1024]{1,0:T(8,128)(2,1)S(1)}, bf16[64,1024]{1,0:T(8,128)(2,1)S(1)}, u32[]{:S(2)}, u32[]{:S(2)}) %collective-permute-start.40) | collective-permute-done | bytes 131104 | tf_op jit(solution)/shard_map/ppermute | solution.py:25
  134.2 1.2 fusion.1
  135.5 1.1 pad_maximum_fusion.1
  (87 shorter events, 2.0 us)
Async XLA Ops:
  1.7 9.3 %collective-permute-start.2 = (bf16[128,1024]{1,0:T(8,128)(2,1)S(1)}, bf16[128,1024]{1,0:T(8,128)(2,1)S(1)}, u32[]{:S(2)}, u32[]{:S(2)}) collective-permute-start(bf16[128,1024]{1,0:T(8,128)(2,1)S(1)} %get-tuple-element.38), channel_id=1, source_target_pairs={{0,4},{1,5},{2,6},{3,7},{4,0},{5,1},{6,2},{7,3},{8,12},{9,13},{10,... | collective-permute-start | bytes 786440 | tf_op jit(solution)/shard_map/ppermute | solution.py:25
  4.7 8.1 %collective-permute-start = (bf16[128,1024]{1,0:T(8,128)(2,1)}, bf16[128,1024]{1,0:T(8,128)(2,1)S(1)}, u32[]{:S(2)}, u32[]{:S(2)}) collective-permute-start(bf16[128,1024]{1,0:T(8,128)(2,1)} %bitcast.52), channel_id=1, source_target_pairs={{0,8},{8,0},{16,24},{24,16},{1,9},{9,1},{17,25},{25,17},{2,10},{10... | collective-permute-start | bytes 786440 | tf_op jit(solution)/shard_map/ppermute | solution.py:25
  6.3 7.5 %collective-permute-start.1 = (bf16[128,1024]{1,0:T(8,128)(2,1)S(1)}, bf16[128,1024]{1,0:T(8,128)(2,1)S(1)}, u32[]{:S(2)}, u32[]{:S(2)}) collective-permute-start(bf16[128,1024]{1,0:T(8,128)(2,1)S(1)} %get-tuple-element.39), channel_id=1, source_target_pairs={{0,2},{1,3},{2,0},{3,1},{4,6},{5,7},{6,4},{7,5},{8,10},{9,11},{10,... | collective-permute-start | bytes 786440 | tf_op jit(solution)/shard_map/ppermute | solution.py:25
  11.0 9.1 %collective-permute-start.5 = (bf16[128,1024]{1,0:T(8,128)(2,1)S(1)}, bf16[128,1024]{1,0:T(8,128)(2,1)S(1)}, u32[]{:S(2)}, u32[]{:S(2)}) collective-permute-start(bf16[128,1024]{1,0:T(8,128)(2,1)S(1)} %get-tuple-element.39), channel_id=1, source_target_pairs={{0,4},{1,5},{2,6},{3,7},{4,0},{5,1},{6,2},{7,3},{8,12},{9,13},{10,... | collective-permute-start | bytes 786440 | tf_op jit(solution)/shard_map/ppermute | solution.py:25
  13.8 14.9 %copy-start.7 = (bf16[128,1024]{1,0:T(8,128)(2,1)}, bf16[128,1024]{1,0:T(8,128)(2,1)S(1)}, u32[]{:S(2)}) copy-start(bf16[128,1024]{1,0:T(8,128)(2,1)S(1)} %broadcast_select_fusion) | copy-start | bytes 786436
  13.9 14.9 %collective-permute-start.3 = (bf16[128,1024]{1,0:T(8,128)(2,1)S(1)}, bf16[128,1024]{1,0:T(8,128)(2,1)}, u32[]{:S(2)}, u32[]{:S(2)}) collective-permute-start(bf16[128,1024]{1,0:T(8,128)(2,1)S(1)} %broadcast_select_fusion), channel_id=1, source_target_pairs={{0,16},{8,24},{16,0},{24,8},{1,17},{9,25},{17,1},{25,9},{2,18},{10... | collective-permute-start | bytes 786440 | tf_op jit(solution)/shard_map/ppermute | solution.py:25
  16.5 12.8 %collective-permute-start.4 = (bf16[128,1024]{1,0:T(8,128)(2,1)S(1)}, bf16[128,1024]{1,0:T(8,128)(2,1)S(1)}, u32[]{:S(2)}, u32[]{:S(2)}) collective-permute-start(bf16[128,1024]{1,0:T(8,128)(2,1)S(1)} %get-tuple-element.38), channel_id=1, source_target_pairs={{0,2},{1,3},{2,0},{3,1},{4,6},{5,7},{6,4},{7,5},{8,10},{9,11},{10,... | collective-permute-start | bytes 786440 | tf_op jit(solution)/shard_map/ppermute | solution.py:25
  18.0 10.7 %collective-permute-start.7 = (bf16[128,1024]{1,0:T(8,128)(2,1)S(1)}, bf16[128,1024]{1,0:T(8,128)(2,1)S(1)}, u32[]{:S(2)}, u32[]{:S(2)}) collective-permute-start(bf16[128,1024]{1,0:T(8,128)(2,1)S(1)} %collective-permute-done.2.refs_4_), channel_id=1, source_target_pairs={{0,2},{1,3},{2,0},{3,1},{4,6},{5,7},{6,4},{7,5},{8,10},{9,11},{10,... | collective-permute-start | bytes 786440 | tf_op jit(solution)/shard_map/ppermute | solution.py:25
  18.5 10.8 %collective-permute-start.6 = (bf16[128,1024]{1,0:T(8,128)(2,1)S(1)}, bf16[128,1024]{1,0:T(8,128)(2,1)S(1)}, u32[]{:S(2)}, u32[]{:S(2)}) collective-permute-start(bf16[128,1024]{1,0:T(8,128)(2,1)S(1)} %collective-permute-done.1.refs_1_), channel_id=1, source_target_pairs={{0,4},{1,5},{2,6},{3,7},{4,0},{5,1},{6,2},{7,3},{8,12},{9,13},{10,... | collective-permute-start | bytes 786440 | tf_op jit(solution)/shard_map/ppermute | solution.py:25
  20.1 14.1 %collective-permute-start.11 = (bf16[256,1024]{1,0:T(8,128)(2,1)S(1)}, bf16[256,1024]{1,0:T(8,128)(2,1)S(1)}, u32[]{:S(2)}, u32[]{:S(2)}) collective-permute-start(bf16[256,1024]{1,0:T(8,128)(2,1)S(1)} %slice_bitcast_fusion.refs_0_), channel_id=1, source_target_pairs={{0,1},{1,0},{2,3},{3,2},{4,5},{5,4},{6,7},{7,6},{8,9},{9,8},{10,11... | collective-permute-start | bytes 1572872 | tf_op jit(solution)/shard_map/ppermute | solution.py:25
  28.8 2.4 %collective-permute-start.15 = (bf16[128,1024]{1,0:T(8,128)(2,1)S(1)}, bf16[128,1024]{1,0:T(8,128)(2,1)S(1)}, u32[]{:S(2)}, u32[]{:S(2)}) collective-permute-start(bf16[128,1024]{1,0:T(8,128)(2,1)S(1)} %collective-permute-done.2.refs_4_), channel_id=1, source_target_pairs={{0,1},{1,0},{2,3},{3,2},{4,5},{5,4},{6,7},{7,6},{8,9},{9,8},{10,11... | collective-permute-start | bytes 786440 | tf_op jit(solution)/shard_map/ppermute | solution.py:25
  28.8 3.9 %collective-permute-start.12 = (bf16[128,1024]{1,0:T(8,128)(2,1)S(1)}, bf16[128,1024]{1,0:T(8,128)(2,1)S(1)}, u32[]{:S(2)}, u32[]{:S(2)}) collective-permute-start(bf16[128,1024]{1,0:T(8,128)(2,1)S(1)} %collective-permute-done.1.refs_1_), channel_id=1, source_target_pairs={{0,1},{1,0},{2,3},{3,2},{4,5},{5,4},{6,7},{7,6},{8,9},{9,8},{10,11... | collective-permute-start | bytes 786440 | tf_op jit(solution)/shard_map/ppermute | solution.py:25
  29.3 5.5 %collective-permute-start.14 = (bf16[128,1024]{1,0:T(8,128)(2,1)S(1)}, bf16[128,1024]{1,0:T(8,128)(2,1)S(1)}, u32[]{:S(2)}, u32[]{:S(2)}) collective-permute-start(bf16[128,1024]{1,0:T(8,128)(2,1)S(1)} %collective-permute-done.5.refs_3_), channel_id=1, source_target_pairs={{0,1},{1,0},{2,3},{3,2},{4,5},{5,4},{6,7},{7,6},{8,9},{9,8},{10,11... | collective-permute-start | bytes 786440 | tf_op jit(solution)/shard_map/ppermute | solution.py:25
  29.4 5.4 %collective-permute-start.13 = (bf16[128,1024]{1,0:T(8,128)(2,1)S(1)}, bf16[128,1024]{1,0:T(8,128)(2,1)}, u32[]{:S(2)}, u32[]{:S(2)}) collective-permute-start(bf16[128,1024]{1,0:T(8,128)(2,1)S(1)} %collective-permute-done.4.refs_2_), channel_id=1, source_target_pairs={{0,1},{1,0},{2,3},{3,2},{4,5},{5,4},{6,7},{7,6},{8,9},{9,8},{10,11... | collective-permute-start | bytes 786440 | tf_op jit(solution)/shard_map/ppermute | solution.py:25
  31.2 11.6 %collective-permute-start.10 = (bf16[128,1024]{1,0:T(8,128)(2,1)S(1)}, bf16[128,1024]{1,0:T(8,128)(2,1)S(1)}, u32[]{:S(2)}, u32[]{:S(2)}) collective-permute-start(bf16[128,1024]{1,0:T(8,128)(2,1)S(1)} %broadcast_select_fusion.1), channel_id=1, source_target_pairs={{0,6},{1,7},{2,4},{3,5},{4,2},{5,3},{6,0},{7,1},{8,14},{9,15},{10,... | collective-permute-start | bytes 786440 | tf_op jit(solution)/shard_map/ppermute | solution.py:25
  32.7 13.4 %collective-permute-start.9 = (bf16[128,1024]{1,0:T(8,128)(2,1)S(1)}, bf16[128,1024]{1,0:T(8,128)(2,1)S(1)}, u32[]{:S(2)}, u32[]{:S(2)}) collective-permute-start(bf16[128,1024]{1,0:T(8,128)(2,1)S(1)} %broadcast_select_fusion.1), channel_id=1, source_target_pairs={{0,4},{1,5},{2,6},{3,7},{4,0},{5,1},{6,2},{7,3},{8,12},{9,13},{10,... | collective-permute-start | bytes 786440 | tf_op jit(solution)/shard_map/ppermute | solution.py:25
  34.2 11.8 %collective-permute-start.8 = (bf16[128,1024]{1,0:T(8,128)(2,1)S(1)}, bf16[128,1024]{1,0:T(8,128)(2,1)S(1)}, u32[]{:S(2)}, u32[]{:S(2)}) collective-permute-start(bf16[128,1024]{1,0:T(8,128)(2,1)S(1)} %broadcast_select_fusion.1), channel_id=1, source_target_pairs={{0,2},{1,3},{2,0},{3,1},{4,6},{5,7},{6,4},{7,5},{8,10},{9,11},{10,... | collective-permute-start | bytes 786440 | tf_op jit(solution)/shard_map/ppermute | solution.py:25
  34.8 2.2 %copy-start = (bf16[2048,1024]{1,0:T(8,128)(2,1)S(1)}, bf16[2048,1024]{1,0:T(8,128)(2,1)}, u32[]{:S(2)}) copy-start(bf16[2048,1024]{1,0:T(8,128)(2,1)} %refs_8_.3) | copy-start | bytes 12582916
  42.8 6.9 %copy-start.3 = (bf16[2,256,1024]{2,1,0:T(8,128)(2,1)S(1)}, bf16[2,256,1024]{2,1,0:T(8,128)(2,1)}, u32[]{:S(2)}) copy-start(bf16[2,256,1024]{2,1,0:T(8,128)(2,1)} %param.7) | copy-start | bytes 3145732
  46.1 7.6 %copy-start.1 = (bf16[2048,1024]{1,0:T(8,128)(2,1)S(1)}, bf16[2048,1024]{1,0:T(8,128)(2,1)}, u32[]{:S(2)}) copy-start(bf16[2048,1024]{1,0:T(8,128)(2,1)} %refs_8_.3) | copy-start | bytes 12582916
  46.1 2.7 %collective-permute-start.16 = (bf16[512,1024]{1,0:T(8,128)(2,1)S(1)}, bf16[512,1024]{1,0:T(8,128)(2,1)S(1)}, u32[]{:S(2)}, u32[]{:S(2)}) collective-permute-start(bf16[512,1024]{1,0:T(8,128)(2,1)S(1)} %pad_maximum_fusion.same), channel_id=1, source_target_pairs={{0,1},{1,0},{2,3},{3,2},{4,5},{5,4},{6,7},{7,6},{8,9},{9,8},{10,11... | collective-permute-start | bytes 3145736 | tf_op jit(solution)/shard_map/ppermute | solution.py:25
  46.2 7.5 %collective-permute-start.18 = (bf16[128,1024]{1,0:T(8,128)(2,1)S(1)}, bf16[128,1024]{1,0:T(8,128)(2,1)S(1)}, u32[]{:S(2)}, u32[]{:S(2)}) collective-permute-start(bf16[128,1024]{1,0:T(8,128)(2,1)S(1)} %collective-permute-done.7.refs_1_), channel_id=1, source_target_pairs={{0,1},{1,0},{2,3},{3,2},{4,5},{5,4},{6,7},{7,6},{8,9},{9,8},{10,11... | collective-permute-start | bytes 786440 | tf_op jit(solution)/shard_map/ppermute | solution.py:25
  46.7 7.0 %collective-permute-start.17 = (bf16[128,1024]{1,0:T(8,128)(2,1)S(1)}, bf16[128,1024]{1,0:T(8,128)(2,1)S(1)}, u32[]{:S(2)}, u32[]{:S(2)}) collective-permute-start(bf16[128,1024]{1,0:T(8,128)(2,1)S(1)} %collective-permute-done.6.refs_0_), channel_id=1, source_target_pairs={{0,1},{1,0},{2,3},{3,2},{4,5},{5,4},{6,7},{7,6},{8,9},{9,8},{10,11... | collective-permute-start | bytes 786440 | tf_op jit(solution)/shard_map/ppermute | solution.py:25
  50.2 10.2 %collective-permute-start.25 = (bf16[256,512]{1,0:T(8,128)(2,1)S(1)}, bf16[256,512]{1,0:T(8,128)(2,1)S(1)}, u32[]{:S(2)}, u32[]{:S(2)}) collective-permute-start(bf16[256,512]{1,0:T(8,128)(2,1)S(1)} %fusion.3.refs_0_), channel_id=1, source_target_pairs={{0,6},{1,7},{2,4},{3,5},{4,2},{5,3},{6,0},{7,1},{8,14},{9,15},{10,... | collective-permute-start | bytes 786440 | tf_op jit(solution)/shard_map/ppermute | solution.py:25
  51.8 13.3 %collective-permute-start.24 = (bf16[256,512]{1,0:T(8,128)(2,1)S(1)}, bf16[256,512]{1,0:T(8,128)(2,1)S(1)}, u32[]{:S(2)}, u32[]{:S(2)}) collective-permute-start(bf16[256,512]{1,0:T(8,128)(2,1)S(1)} %fusion.3.refs_0_), channel_id=1, source_target_pairs={{0,4},{1,5},{2,6},{3,7},{4,0},{5,1},{6,2},{7,3},{8,12},{9,13},{10,... | collective-permute-start | bytes 786440 | tf_op jit(solution)/shard_map/ppermute | solution.py:25
  52.5 12.6 %collective-permute-start.23 = (bf16[256,512]{1,0:T(8,128)(2,1)S(1)}, bf16[256,512]{1,0:T(8,128)(2,1)S(1)}, u32[]{:S(2)}, u32[]{:S(2)}) collective-permute-start(bf16[256,512]{1,0:T(8,128)(2,1)S(1)} %fusion.3.refs_0_), channel_id=1, source_target_pairs={{0,2},{1,3},{2,0},{3,1},{4,6},{5,7},{6,4},{7,5},{8,10},{9,11},{10,... | collective-permute-start | bytes 786440 | tf_op jit(solution)/shard_map/ppermute | solution.py:25
  56.1 9.5 %collective-permute-start.20 = (bf16[128,1024]{1,0:T(8,128)(2,1)S(1)}, bf16[128,1024]{1,0:T(8,128)(2,1)S(1)}, u32[]{:S(2)}, u32[]{:S(2)}) collective-permute-start(bf16[128,1024]{1,0:T(8,128)(2,1)S(1)} %get-tuple-element.56), channel_id=1, source_target_pairs={{0,8},{8,0},{16,24},{24,16},{1,9},{9,1},{17,25},{25,17},{2,10},{10... | collective-permute-start | bytes 786440 | tf_op jit(solution)/shard_map/ppermute | solution.py:25
  57.8 8.0 %collective-permute-start.26 = (bf16[256,512]{1,0:T(8,128)(2,1)S(1)}, bf16[256,512]{1,0:T(8,128)(2,1)S(1)}, u32[]{:S(2)}, u32[]{:S(2)}) collective-permute-start(bf16[256,512]{1,0:T(8,128)(2,1)S(1)} %fusion.3.refs_0_), channel_id=1, source_target_pairs={{0,1},{1,0},{2,3},{3,2},{4,5},{5,4},{6,7},{7,6},{8,9},{9,8},{10,11... | collective-permute-start | bytes 786440 | tf_op jit(solution)/shard_map/ppermute | solution.py:25
  60.3 10.5 %collective-permute-start.19 = (bf16[128,1024]{1,0:T(8,128)(2,1)S(1)}, bf16[128,1024]{1,0:T(8,128)(2,1)S(1)}, u32[]{:S(2)}, u32[]{:S(2)}) collective-permute-start(bf16[128,1024]{1,0:T(8,128)(2,1)S(1)} %get-tuple-element.54), channel_id=1, source_target_pairs={{0,8},{8,0},{16,24},{24,16},{1,9},{9,1},{17,25},{25,17},{2,10},{10... | collective-permute-start | bytes 786440 | tf_op jit(solution)/shard_map/ppermute | solution.py:25
  65.1 1.5 %collective-permute-start.29 = (bf16[256,512]{1,0:T(8,128)(2,1)S(1)}, bf16[256,512]{1,0:T(8,128)(2,1)S(1)}, u32[]{:S(2)}, u32[]{:S(2)}) collective-permute-start(bf16[256,512]{1,0:T(8,128)(2,1)S(1)} %collective-permute-done.25.refs_3_), channel_id=1, source_target_pairs={{0,1},{1,0},{2,3},{3,2},{4,5},{5,4},{6,7},{7,6},{8,9},{9,8},{10,11... | collective-permute-start | bytes 786440 | tf_op jit(solution)/shard_map/ppermute | solution.py:25
  65.1 1.9 %collective-permute-start.28 = (bf16[256,512]{1,0:T(8,128)(2,1)S(1)}, bf16[256,512]{1,0:T(8,128)(2,1)S(1)}, u32[]{:S(2)}, u32[]{:S(2)}) collective-permute-start(bf16[256,512]{1,0:T(8,128)(2,1)S(1)} %collective-permute-done.24.refs_2_), channel_id=1, source_target_pairs={{0,1},{1,0},{2,3},{3,2},{4,5},{5,4},{6,7},{7,6},{8,9},{9,8},{10,11... | collective-permute-start | bytes 786440 | tf_op jit(solution)/shard_map/ppermute | solution.py:25
  65.6 1.8 %collective-permute-start.27 = (bf16[256,512]{1,0:T(8,128)(2,1)S(1)}, bf16[256,512]{1,0:T(8,128)(2,1)S(1)}, u32[]{:S(2)}, u32[]{:S(2)}) collective-permute-start(bf16[256,512]{1,0:T(8,128)(2,1)S(1)} %collective-permute-done.23.refs_1_), channel_id=1, source_target_pairs={{0,1},{1,0},{2,3},{3,2},{4,5},{5,4},{6,7},{7,6},{8,9},{9,8},{10,11... | collective-permute-start | bytes 786440 | tf_op jit(solution)/shard_map/ppermute | solution.py:25
  65.8 15.4 %copy-start.5 = (f32[2,128,1024]{2,1,0:T(8,128)S(1)}, f32[2,128,1024]{2,1,0:T(8,128)}, u32[]{:S(2)}) copy-start(f32[2,128,1024]{2,1,0:T(8,128)} %param.9) | copy-start | bytes 3145732
  65.8 15.4 %copy-start.6 = (f32[2,128,1024]{2,1,0:T(8,128)S(1)}, f32[2,128,1024]{2,1,0:T(8,128)}, u32[]{:S(2)}) copy-start(f32[2,128,1024]{2,1,0:T(8,128)} %param.10) | copy-start | bytes 3145732
  65.8 15.3 %collective-permute-start.21 = (bf16[128,1024]{1,0:T(8,128)(2,1)S(1)}, bf16[128,1024]{1,0:T(8,128)(2,1)S(1)}, u32[]{:S(2)}, u32[]{:S(2)}) collective-permute-start(bf16[128,1024]{1,0:T(8,128)(2,1)S(1)} %add_convert_fusion.1), channel_id=1, source_target_pairs={{0,16},{8,24},{16,0},{24,8},{1,17},{9,25},{17,1},{25,9},{2,18},{10... | collective-permute-start | bytes 786440 | tf_op jit(solution)/shard_map/ppermute | solution.py:25
  69.2 17.2 %collective-permute-start.32 = (bf16[128,1024]{1,0:T(8,128)(2,1)S(1)}, bf16[128,1024]{1,0:T(8,128)(2,1)S(1)}, u32[]{:S(2)}, u32[]{:S(2)}) collective-permute-start(bf16[128,1024]{1,0:T(8,128)(2,1)S(1)} %get-tuple-element.62), channel_id=1, source_target_pairs={{0,8},{8,0},{16,24},{24,16},{1,9},{9,1},{17,25},{25,17},{2,10},{10... | collective-permute-start | bytes 786440 | tf_op jit(solution)/shard_map/ppermute | solution.py:25
  82.3 4.1 %copy-start.8 = (bf16[128,1024]{1,0:T(8,128)(2,1)}, bf16[128,1024]{1,0:T(8,128)(2,1)S(1)}, u32[]{:S(2)}) copy-start(bf16[128,1024]{1,0:T(8,128)(2,1)S(1)} %get-tuple-element.77) | copy-start | bytes 786436
  82.3 22.0 %collective-permute-start.34 = (bf16[128,1024]{1,0:T(8,128)(2,1)S(1)}, bf16[128,1024]{1,0:T(8,128)(2,1)S(1)}, u32[]{:S(2)}, u32[]{:S(2)}) collective-permute-start(bf16[128,1024]{1,0:T(8,128)(2,1)S(1)} %get-tuple-element.77), channel_id=1, source_target_pairs={{0,8},{8,0},{16,24},{24,16},{1,9},{9,1},{17,25},{25,17},{2,10},{10... | collective-permute-start | bytes 786440 | tf_op jit(solution)/shard_map/ppermute | solution.py:25
  82.3 21.9 %collective-permute-start.22 = (bf16[128,1024]{1,0:T(8,128)(2,1)S(1)}, bf16[128,1024]{1,0:T(8,128)(2,1)S(1)}, u32[]{:S(2)}, u32[]{:S(2)}) collective-permute-start(bf16[128,1024]{1,0:T(8,128)(2,1)S(1)} %get-tuple-element.77), channel_id=1, source_target_pairs={{0,16},{8,24},{16,0},{24,8},{1,17},{9,25},{17,1},{25,9},{2,18},{10... | collective-permute-start | bytes 786440 | tf_op jit(solution)/shard_map/ppermute | solution.py:25
  84.6 19.6 %collective-permute-start.30 = (bf16[128,1024]{1,0:T(8,128)(2,1)S(1)}, bf16[128,1024]{1,0:T(8,128)(2,1)S(1)}, u32[]{:S(2)}, u32[]{:S(2)}) collective-permute-start(bf16[128,1024]{1,0:T(8,128)(2,1)S(1)} %get-tuple-element.59), channel_id=1, source_target_pairs={{0,8},{8,0},{16,24},{24,16},{1,9},{9,1},{17,25},{25,17},{2,10},{10... | collective-permute-start | bytes 786440 | tf_op jit(solution)/shard_map/ppermute | solution.py:25
  87.2 17.2 %collective-permute-start.33 = (bf16[64,1024]{1,0:T(8,128)(2,1)S(1)}, bf16[64,1024]{1,0:T(8,128)(2,1)S(1)}, u32[]{:S(2)}, u32[]{:S(2)}) collective-permute-start(bf16[64,1024]{1,0:T(8,128)(2,1)S(1)} %get-tuple-element.84), channel_id=1, source_target_pairs={{0,16},{8,24},{16,0},{24,8},{1,17},{9,25},{17,1},{25,9},{2,18},{10... | collective-permute-start | bytes 393224 | tf_op jit(solution)/shard_map/ppermute | solution.py:25
  104.3 1.0 copy-start.12
  104.3 8.2 %collective-permute-start.37 = (bf16[64,1024]{1,0:T(8,128)(2,1)}, bf16[64,1024]{1,0:T(8,128)(2,1)}, u32[]{:S(2)}, u32[]{:S(2)}) collective-permute-start(bf16[64,1024]{1,0:T(8,128)(2,1)} %get-tuple-element.85), channel_id=1, source_target_pairs={{0,16},{8,24},{16,0},{24,8},{1,17},{9,25},{17,1},{25,9},{2,18},{10... | collective-permute-start | bytes 393224 | tf_op jit(solution)/shard_map/ppermute | solution.py:25
  104.4 0.9 copy-start.10
  105.3 12.6 %collective-permute-start.38 = (bf16[64,1024]{1,0:T(8,128)(2,1)S(1)}, bf16[64,1024]{1,0:T(8,128)(2,1)}, u32[]{:S(2)}, u32[]{:S(2)}) collective-permute-start(bf16[64,1024]{1,0:T(8,128)(2,1)S(1)} %get-tuple-element.74), channel_id=1, source_target_pairs={{0,8},{8,0},{16,24},{24,16},{1,9},{9,1},{17,25},{25,17},{2,10},{10... | collective-permute-start | bytes 393224 | tf_op jit(solution)/shard_map/ppermute | solution.py:25
  107.7 15.2 %copy-start.9 = (bf16[128,1024]{1,0:T(8,128)(2,1)S(1)}, bf16[128,1024]{1,0:T(8,128)(2,1)}, u32[]{:S(2)}) copy-start(bf16[128,1024]{1,0:T(8,128)(2,1)} %copy-done.8) | copy-start | bytes 786436
  107.7 15.2 %copy-start.11 = (bf16[128,1024]{1,0:T(8,128)(2,1)S(1)}, bf16[128,1024]{1,0:T(8,128)(2,1)}, u32[]{:S(2)}) copy-start(bf16[128,1024]{1,0:T(8,128)(2,1)} %copy-done.10) | copy-start | bytes 786436
  107.7 15.2 %copy-start.13 = (bf16[128,1024]{1,0:T(8,128)(2,1)S(1)}, bf16[128,1024]{1,0:T(8,128)(2,1)}, u32[]{:S(2)}) copy-start(bf16[128,1024]{1,0:T(8,128)(2,1)} %copy-done.12) | copy-start | bytes 786436
  107.8 15.1 %collective-permute-start.31 = (bf16[128,1024]{1,0:T(8,128)(2,1)}, bf16[128,1024]{1,0:T(8,128)(2,1)S(1)}, u32[]{:S(2)}, u32[]{:S(2)}) collective-permute-start(bf16[128,1024]{1,0:T(8,128)(2,1)} %copy-done.12), channel_id=1, source_target_pairs={{0,8},{8,0},{16,24},{24,16},{1,9},{9,1},{17,25},{25,17},{2,10},{10... | collective-permute-start | bytes 786440 | tf_op jit(solution)/shard_map/ppermute | solution.py:25
  107.9 15.6 %collective-permute-start.35 = (bf16[64,1024]{1,0:T(8,128)(2,1)S(1)}, bf16[64,1024]{1,0:T(8,128)(2,1)S(1)}, u32[]{:S(2)}, u32[]{:S(2)}) collective-permute-start(bf16[64,1024]{1,0:T(8,128)(2,1)S(1)} %get-tuple-element.74), channel_id=1, source_target_pairs={{0,16},{8,24},{16,0},{24,8},{1,17},{9,25},{17,1},{25,9},{2,18},{10... | collective-permute-start | bytes 393224 | tf_op jit(solution)/shard_map/ppermute | solution.py:25
  119.1 6.4 %collective-permute-start.39 = (bf16[64,1024]{1,0:T(8,128)(2,1)S(1)}, bf16[64,1024]{1,0:T(8,128)(2,1)S(1)}, u32[]{:S(2)}, u32[]{:S(2)}) collective-permute-start(bf16[64,1024]{1,0:T(8,128)(2,1)S(1)} %get-tuple-element.71), channel_id=1, source_target_pairs={{0,16},{8,24},{16,0},{24,8},{1,17},{9,25},{17,1},{25,9},{2,18},{10... | collective-permute-start | bytes 393224 | tf_op jit(solution)/shard_map/ppermute | solution.py:25
  119.2 6.4 %copy-start.2 = (f32[128,1024]{1,0:T(8,128)S(1)}, f32[128,1024]{1,0:T(8,128)}, u32[]{:S(2)}) copy-start(f32[128,1024]{1,0:T(8,128)} %get-tuple-element.69) | copy-start | bytes 1572868
  119.3 6.3 %copy-start.4 = (f32[64,1024]{1,0:T(8,128)S(1)}, f32[64,1024]{1,0:T(8,128)}, u32[]{:S(2)}) copy-start(f32[64,1024]{1,0:T(8,128)} %get-tuple-element.70) | copy-start | bytes 786436
  123.4 6.5 %collective-permute-start.41 = (bf16[64,1024]{1,0:T(8,128)(2,1)S(1)}, bf16[64,1024]{1,0:T(8,128)(2,1)S(1)}, u32[]{:S(2)}, u32[]{:S(2)}) collective-permute-start(bf16[64,1024]{1,0:T(8,128)(2,1)S(1)} %get-tuple-element.71), channel_id=1, source_target_pairs={{0,8},{8,0},{16,24},{24,16},{1,9},{9,1},{17,25},{25,17},{2,10},{10... | collective-permute-start | bytes 393224 | tf_op jit(solution)/shard_map/ppermute | solution.py:25
  123.5 10.7 %collective-permute-start.36 = (bf16[64,1024]{1,0:T(8,128)(2,1)S(1)}, bf16[64,1024]{1,0:T(8,128)(2,1)S(1)}, u32[]{:S(2)}, u32[]{:S(2)}) collective-permute-start(bf16[64,1024]{1,0:T(8,128)(2,1)S(1)} %collective-permute-done.35), channel_id=1, source_target_pairs={{0,8},{8,0},{16,24},{24,16},{1,9},{9,1},{17,25},{25,17},{2,10},{10... | collective-permute-start | bytes 393224 | tf_op jit(solution)/shard_map/ppermute | solution.py:25
  125.6 8.3 %collective-permute-start.40 = (bf16[64,1024]{1,0:T(8,128)(2,1)S(1)}, bf16[64,1024]{1,0:T(8,128)(2,1)S(1)}, u32[]{:S(2)}, u32[]{:S(2)}) collective-permute-start(bf16[64,1024]{1,0:T(8,128)(2,1)S(1)} %collective-permute-done.39), channel_id=1, source_target_pairs={{0,8},{8,0},{16,24},{24,16},{1,9},{9,1},{17,25},{25,17},{2,10},{10... | collective-permute-start | bytes 393224 | tf_op jit(solution)/shard_map/ppermute | solution.py:25

commit v11 on v9

--- a/solution.py
+++ b/solution.py
@@ -307,7 +307,7 @@
         return value
 
     pieces = max(replicas // 2, 1)
-    tokens, tokens_1 = [], []
+    tokens = []
 
     near, far, arrived = spread_near(cotangent[0], far_bits, tokens)
     both = jnp.swapaxes(candidates[:, 0], 1, 2).reshape(-1, candidates.shape[2])
@@ -339,11 +339,11 @@
     blocks = spread(heads, far_bits)
     open_0 = reduced(arrived_0, keep_0)
     blocks = with_partner({mask: [held] for mask, held in blocks.items()})
-    send_1 = heads_product(blocks, here, layer_input, 0, pieces, jnp.bfloat16, scale, tokens_1)
+    send_1 = heads_product(blocks, here, layer_input, 0, 1, jnp.bfloat16, scale)
     keep_1 = heads_product(
         blocks, here, layer_input, 1, pieces, jnp.float32, scale, arrived_0[pieces // 2 :]
     )
-    arrived_1 = [swap(piece, "dp", dp_bits[0]) for piece in send_1]
+    arrived_1 = jnp.split(swap(send_1[0], "dp", dp_bits[0]), pieces)
 
     updates, firsts, seconds, gathered = [], [], [], []
     open_1 = list(reduced(arrived_1, keep_1))

time: 136 us -> 140 us (1.029)
  waiting for transfers between devices: 68.8 us -> 76.3 us
  starting transfers between devices: 35.3 us -> 33 us
    ppermute x38 -> x37, waiting for transfers between devices: 68.8 us -> 76.3 us  [swap(): return lax.ppermute(value, axis, [(i, i ^ mask) for i in range(size)])]
    ppermute x38 -> x37, starting transfers between devices: 35.3 us -> 33 us  [swap(): return lax.ppermute(value, axis, [(i, i ^ mask) for i in range(size)])]
  transfers between devices with their start and end apart: 38 -> 37, of which waited for: 16 -> 18; matrix products, arithmetic and copies ran while one was open for 7% -> 6% of each run, Pallas kernels for 10% -> 10%
where the time goes in v11:
time: 140 us
  waiting for transfers between devices  76.3 us (54%)
  starting transfers between devices  33 us (24%)
  Pallas kernels  13.8 us (10%)
  other arithmetic  7.42 us (5%)
  local copies, waits for them, and re-layouts  4.72 us (3%)
  matrix products  3.58 us (3%)
    ppermute x37, waiting for transfers between devices, swap(): return lax.ppermute(value, axis, [(i, i ^ mask) for i in range(size)])  76.3 us
    ppermute x37, starting transfers between devices, swap(): return lax.ppermute(value, axis, [(i, i ^ mask) for i in range(size)])  33 us
    pallas_call x4, Pallas kernels, call_in_vmem(): pl.pallas_call(body, grid_spec=pltpu.PrefetchScalarGridSpec(num_scalar_pr...  7.26 us
    pallas_call x1, Pallas kernels, add_products(): pl.pallas_call(functools.partial(product_body, shape), grid_spec=pltpu.Pr...  5.8 us
    dot_general x2, matrix products, on_device(): lax.dot_general(own, jnp.concatenate(parts, axis=0), TRANSPOSED, preferre...  3.11 us
  transfers between devices with their start and end apart: 37, of which 18 were waited for; matrix products, arithmetic and copies ran while one was open for 6% of the time, Pallas kernels for 10%

profile of v11, /device:TPU:0, one launch (start us, length us, event | category | flops | bytes accessed | tf_op | source)
XLA Modules:
  0.0 139.7 jit_solution(3814914064386272106)
XLA Ops:
  0.6 1.1 slice_bitcast_fusion.1
  1.7 3.0 %collective-permute-start.2 = (bf16[128,1024]{1,0:T(8,128)(2,1)S(1)}, bf16[128,1024]{1,0:T(8,128)(2,1)S(1)}, u32[]{:S(2)}, u32[]{:S(2)}) collective-permute-start(bf16[128,1024]{1,0:T(8,128)(2,1)S(1)} %get-tuple-element.33), channel_id=1, source_target_pairs={{0,4},{1,5},{2,6},{3,7},{4,0},{5,1},{6,2},{7,3},{8,12},{9,13},{10,... | collective-permute-start | bytes 786440 | tf_op jit(solution)/shard_map/ppermute | solution.py:24
  4.7 1.6 %collective-permute-start = (bf16[128,1024]{1,0:T(8,128)(2,1)}, bf16[128,1024]{1,0:T(8,128)(2,1)S(1)}, u32[]{:S(2)}, u32[]{:S(2)}) collective-permute-start(bf16[128,1024]{1,0:T(8,128)(2,1)} %bitcast.53), channel_id=1, source_target_pairs={{0,8},{8,0},{16,24},{24,16},{1,9},{9,1},{17,25},{25,17},{2,10},{10... | collective-permute-start | bytes 786440 | tf_op jit(solution)/shard_map/ppermute | solution.py:24
  6.3 1.5 %collective-permute-start.1 = (bf16[128,1024]{1,0:T(8,128)(2,1)S(1)}, bf16[128,1024]{1,0:T(8,128)(2,1)S(1)}, u32[]{:S(2)}, u32[]{:S(2)}) collective-permute-start(bf16[128,1024]{1,0:T(8,128)(2,1)S(1)} %get-tuple-element.34), channel_id=1, source_target_pairs={{0,2},{1,3},{2,0},{3,1},{4,6},{5,7},{6,4},{7,5},{8,10},{9,11},{10,... | collective-permute-start | bytes 786440 | tf_op jit(solution)/shard_map/ppermute | solution.py:24
  7.8 0.7 and_compare_fusion.1
  8.5 0.1 broadcast_in_dim.34
  8.6 2.4 %collective-permute-done.2.refs_4_ = bf16[128,1024]{1,0:T(8,128)(2,1)S(1)} collective-permute-done((bf16[128,1024]{1,0:T(8,128)(2,1)S(1)}, bf16[128,1024]{1,0:T(8,128)(2,1)S(1)}, u32[]{:S(2)}, u32[]{:S(2)}) %collective-permute-start.2) | collective-permute-done | bytes 262176 | tf_op jit(solution)/shard_map/ppermute | solution.py:24
  11.0 1.7 %collective-permute-start.5 = (bf16[128,1024]{1,0:T(8,128)(2,1)S(1)}, bf16[128,1024]{1,0:T(8,128)(2,1)S(1)}, u32[]{:S(2)}, u32[]{:S(2)}) collective-permute-start(bf16[128,1024]{1,0:T(8,128)(2,1)S(1)} %get-tuple-element.34), channel_id=1, source_target_pairs={{0,4},{1,5},{2,6},{3,7},{4,0},{5,1},{6,2},{7,3},{8,12},{9,13},{10,... | collective-permute-start | bytes 786440 | tf_op jit(solution)/shard_map/ppermute | solution.py:24
  12.8 1.1 broadcast_select_fusion
  13.9 2.7 %collective-permute-start.3 = (bf16[128,1024]{1,0:T(8,128)(2,1)S(1)}, bf16[128,1024]{1,0:T(8,128)(2,1)}, u32[]{:S(2)}, u32[]{:S(2)}) collective-permute-start(bf16[128,1024]{1,0:T(8,128)(2,1)S(1)} %broadcast_select_fusion), channel_id=1, source_target_pairs={{0,16},{8,24},{16,0},{24,8},{1,17},{9,25},{17,1},{25,9},{2,18},{10... | collective-permute-start | bytes 786440 | tf_op jit(solution)/shard_map/ppermute | solution.py:24
  16.5 1.5 %collective-permute-start.4 = (bf16[128,1024]{1,0:T(8,128)(2,1)S(1)}, bf16[128,1024]{1,0:T(8,128)(2,1)S(1)}, u32[]{:S(2)}, u32[]{:S(2)}) collective-permute-start(bf16[128,1024]{1,0:T(8,128)(2,1)S(1)} %get-tuple-element.33), channel_id=1, source_target_pairs={{0,2},{1,3},{2,0},{3,1},{4,6},{5,7},{6,4},{7,5},{8,10},{9,11},{10,... | collective-permute-start | bytes 786440 | tf_op jit(solution)/shard_map/ppermute | solution.py:24
  18.0 0.5 collective-permute-start.7
  18.6 0.5 collective-permute-start.6
  19.1 1.1 slice_bitcast_fusion.refs_0_
  20.2 8.5 %collective-permute-done.7.refs_1_ = bf16[128,1024]{1,0:T(8,128)(2,1)S(1)} collective-permute-done((bf16[128,1024]{1,0:T(8,128)(2,1)S(1)}, bf16[128,1024]{1,0:T(8,128)(2,1)S(1)}, u32[]{:S(2)}, u32[]{:S(2)}) %collective-permute-start.7) | collective-permute-done | bytes 262176 | tf_op jit(solution)/shard_map/ppermute | solution.py:24
  28.8 0.5 collective-permute-start.12
  29.4 0.4 collective-permute-start.13
  30.1 1.1 broadcast_select_fusion.1
  31.2 1.5 %collective-permute-start.10 = (bf16[128,1024]{1,0:T(8,128)(2,1)S(1)}, bf16[128,1024]{1,0:T(8,128)(2,1)S(1)}, u32[]{:S(2)}, u32[]{:S(2)}) collective-permute-start(bf16[128,1024]{1,0:T(8,128)(2,1)S(1)} %broadcast_select_fusion.1), channel_id=1, source_target_pairs={{0,6},{1,7},{2,4},{3,5},{4,2},{5,3},{6,0},{7,1},{8,14},{9,15},{10,... | collective-permute-start | bytes 786440 | tf_op jit(solution)/shard_map/ppermute | solution.py:24
  32.7 1.5 %collective-permute-start.9 = (bf16[128,1024]{1,0:T(8,128)(2,1)S(1)}, bf16[128,1024]{1,0:T(8,128)(2,1)S(1)}, u32[]{:S(2)}, u32[]{:S(2)}) collective-permute-start(bf16[128,1024]{1,0:T(8,128)(2,1)S(1)} %broadcast_select_fusion.1), channel_id=1, source_target_pairs={{0,4},{1,5},{2,6},{3,7},{4,0},{5,1},{6,2},{7,3},{8,12},{9,13},{10,... | collective-permute-start | bytes 786440 | tf_op jit(solution)/shard_map/ppermute | solution.py:24
  34.2 0.5 collective-permute-start.8
  34.8 2.2 %copy-done = bf16[2048,1024]{1,0:T(8,128)(2,1)S(1)} copy-done((bf16[2048,1024]{1,0:T(8,128)(2,1)S(1)}, bf16[2048,1024]{1,0:T(8,128)(2,1)}, u32[]{:S(2)}) %copy-start) | copy-done | bytes 4194328
  37.0 5.8 %shard_map.85.refs_5_ = f32[1024,1024]{1,0:T(8,128)S(1)} custom-call(s32[2]{0:T(128)S(1)} %pad_add_fusion.here, bf16[256,1024]{1,0:T(8,128)(2,1)S(1)} %slice_bitcast_fusion.refs_0_, bf16[128,1024]{1,0:T(8,128)(2,1)S(1)} %collective-permute-done.1.refs_1_, bf16[128,1024]{1,0:T(8,128)(2,1)S(1)} %collective-permute-done.4.refs_2_, ...), custom_call_target="tpu_custom_call" | custom-call | flops 3221225472 | bytes 10485760 | tf_op jit(solution)/shard_map/pallas_call | solution.py:209
  42.8 3.3 %collective-permute-done.9 = bf16[128,1024]{1,0:T(8,128)(2,1)S(1)} collective-permute-done((bf16[128,1024]{1,0:T(8,128)(2,1)S(1)}, bf16[128,1024]{1,0:T(8,128)(2,1)S(1)}, u32[]{:S(2)}, u32[]{:S(2)}) %collective-permute-start.9) | collective-permute-done | bytes 262176 | tf_op jit(solution)/shard_map/ppermute | solution.py:24
  46.2 0.5 collective-permute-start.18
  46.8 2.1 %collective-permute-done.16.other = bf16[512,1024]{1,0:T(8,128)(2,1)S(1)} collective-permute-done((bf16[512,1024]{1,0:T(8,128)(2,1)S(1)}, bf16[512,1024]{1,0:T(8,128)(2,1)S(1)}, u32[]{:S(2)}, u32[]{:S(2)}) %collective-permute-start.16) | collective-permute-done | bytes 1048608 | tf_op jit(solution)/shard_map/ppermute | solution.py:24
  48.9 0.8 shard_map.86
  49.7 0.5 fusion.2.refs_0_
  50.1 1.6 %collective-permute-start.25 = (bf16[256,512]{1,0:T(8,128)(2,1)S(1)}, bf16[256,512]{1,0:T(8,128)(2,1)S(1)}, u32[]{:S(2)}, u32[]{:S(2)}) collective-permute-start(bf16[256,512]{1,0:T(8,128)(2,1)S(1)} %fusion.2.refs_0_), channel_id=1, source_target_pairs={{0,6},{1,7},{2,4},{3,5},{4,2},{5,3},{6,0},{7,1},{8,14},{9,15},{10,... | collective-permute-start | bytes 786440 | tf_op jit(solution)/shard_map/ppermute | solution.py:24
  51.8 0.7 collective-permute-start.24
  52.5 1.2 collective-permute-start.23
  53.7 2.4 %shard_map.87 = (bf16[1024,1024]{1,0:T(8,128)(2,1)S(1)}, bf16[128,1024]{1,0:T(8,128)(2,1)S(1)}, bf16[128,1024]{1,0:T(8,128)(2,1)S(1)}) custom-call(s32[2]{0:T(128)S(1)} %pad_add_fusion.here, bf16[128,1024]{1,0:T(8,128)(2,1)S(1)} %collective-permute-done.6.refs_0_, bf16[128,1024]{1,0:T(8,128)(2,1)S(1)} %collective-permute-done.7.refs_1_, ...), custom_call_target="tpu_custom_call" | custom-call | flops 1610612736 | bytes 13107200 | tf_op jit(solution)/shard_map/pallas_call | solution.py:131
  56.1 1.6 %collective-permute-start.20 = (bf16[128,1024]{1,0:T(8,128)(2,1)S(1)}, bf16[128,1024]{1,0:T(8,128)(2,1)S(1)}, u32[]{:S(2)}, u32[]{:S(2)}) collective-permute-start(bf16[128,1024]{1,0:T(8,128)(2,1)S(1)} %get-tuple-element.51), channel_id=1, source_target_pairs={{0,8},{8,0},{16,24},{24,16},{1,9},{9,1},{17,25},{25,17},{2,10},{10... | collective-permute-start | bytes 786440 | tf_op jit(solution)/shard_map/ppermute | solution.py:24
  57.8 1.2 shard_map.88
  59.0 1.3 collective-permute-done.25.refs_3_
  60.3 1.6 %collective-permute-start.19 = (bf16[128,1024]{1,0:T(8,128)(2,1)S(1)}, bf16[128,1024]{1,0:T(8,128)(2,1)S(1)}, u32[]{:S(2)}, u32[]{:S(2)}) collective-permute-start(bf16[128,1024]{1,0:T(8,128)(2,1)S(1)} %get-tuple-element.49), channel_id=1, source_target_pairs={{0,8},{8,0},{16,24},{24,16},{1,9},{9,1},{17,25},{25,17},{2,10},{10... | collective-permute-start | bytes 786440 | tf_op jit(solution)/shard_map/ppermute | solution.py:24
  61.9 3.2 %collective-permute-done.24.refs_2_ = bf16[256,512]{1,0:T(8,128)(2,1)S(1)} collective-permute-done((bf16[256,512]{1,0:T(8,128)(2,1)S(1)}, bf16[256,512]{1,0:T(8,128)(2,1)S(1)}, u32[]{:S(2)}, u32[]{:S(2)}) %collective-permute-start.24) | collective-permute-done | bytes 262176 | tf_op jit(solution)/shard_map/ppermute | solution.py:24
  65.1 0.5 collective-permute-start.28
  65.8 0.4 collective-permute-start.21
  66.2 0.4 collective-permute-done.29.refs_7_
  66.6 0.4 collective-permute-done.28.refs_6_
  67.0 0.4 collective-permute-done.27.refs_5_
  67.4 1.8 %shard_map.90 = bf16[256,1024]{1,0:T(8,128)(2,1)S(1)} custom-call(s32[2]{0:T(128)S(1)} %pad_add_fusion.here, bf16[256,512]{1,0:T(8,128)(2,1)S(1)} %fusion.2.refs_0_, bf16[256,512]{1,0:T(8,128)(2,1)S(1)} %collective-permute-done.23.refs_1_, bf16[256,512]{1,0:T(8,128)(2,1)S(1)} %collective-permute-done.24.refs_2_, ...), custom_call_target="tpu_custom_call" | custom-call | flops 1073741824 | bytes 6815744 | tf_op jit(solution)/shard_map/pallas_call | solution.py:131
  69.2 1.6 %collective-permute-start.30 = (bf16[256,1024]{1,0:T(8,128)(2,1)S(1)}, bf16[256,1024]{1,0:T(8,128)(2,1)S(1)}, u32[]{:S(2)}, u32[]{:S(2)}) collective-permute-start(bf16[256,1024]{1,0:T(8,128)(2,1)S(1)} %shard_map.90), channel_id=1, source_target_pairs={{0,8},{8,0},{16,24},{24,16},{1,9},{9,1},{17,25},{25,17},{2,10},{10... | collective-permute-start | bytes 1572872 | tf_op jit(solution)/shard_map/ppermute | solution.py:24
  70.8 10.3 %collective-permute-done.21 = bf16[128,1024]{1,0:T(8,128)(2,1)S(1)} collective-permute-done((bf16[128,1024]{1,0:T(8,128)(2,1)S(1)}, bf16[128,1024]{1,0:T(8,128)(2,1)S(1)}, u32[]{:S(2)}, u32[]{:S(2)}) %collective-permute-start.21) | collective-permute-done | bytes 262176 | tf_op jit(solution)/shard_map/ppermute | solution.py:24
  81.1 0.4 divide_convert_fusion.1
  81.6 2.3 %collective-permute-start.22 = (bf16[128,1024]{1,0:T(8,128)(2,1)S(1)}, bf16[128,1024]{1,0:T(8,128)(2,1)}, u32[]{:S(2)}, u32[]{:S(2)}) collective-permute-start(bf16[128,1024]{1,0:T(8,128)(2,1)S(1)} %get-tuple-element.61), channel_id=1, source_target_pairs={{0,16},{8,24},{16,0},{24,8},{1,17},{9,25},{17,1},{25,9},{2,18},{10... | collective-permute-start | bytes 786440 | tf_op jit(solution)/shard_map/ppermute | solution.py:24
  83.9 1.8 %shard_map.89 = (f32[128,1024]{1,0:T(8,128)S(1)}, f32[128,1024]{1,0:T(8,128)S(1)}) custom-call(s32[2]{0:T(128)S(1)} %pad_add_fusion.here, bf16[256,512]{1,0:T(8,128)(2,1)S(1)} %fusion.2.refs_0_, bf16[256,512]{1,0:T(8,128)(2,1)S(1)} %collective-permute-done.23.refs_1_, bf16[256,512]{1,0:T(8,128)(2,1)S(1)} %collective-permute-done.24.refs_2_, ...), custom_call_target="tpu_custom_call" | custom-call | flops 1073741824 | bytes 7340032 | tf_op jit(solution)/shard_map/pallas_call | solution.py:131
  85.7 8.4 %collective-permute-done.30 = bf16[256,1024]{1,0:T(8,128)(2,1)S(1)} collective-permute-done((bf16[256,1024]{1,0:T(8,128)(2,1)S(1)}, bf16[256,1024]{1,0:T(8,128)(2,1)S(1)}, u32[]{:S(2)}, u32[]{:S(2)}) %collective-permute-start.30) | collective-permute-done | bytes 524320 | tf_op jit(solution)/shard_map/ppermute | solution.py:24
  94.1 0.1 add_convert_fusion
  94.3 0.4 collective-permute-start.32
  94.6 3.5 %collective-permute-done.22 = bf16[128,1024]{1,0:T(8,128)(2,1)} collective-permute-done((bf16[128,1024]{1,0:T(8,128)(2,1)S(1)}, bf16[128,1024]{1,0:T(8,128)(2,1)}, u32[]{:S(2)}, u32[]{:S(2)}) %collective-permute-start.22) | collective-permute-done | bytes 262176 | tf_op jit(solution)/shard_map/ppermute | solution.py:24
  98.2 0.9 collective-permute-done.33
  99.1 11.1 %collective-permute-done.32 = bf16[128,1024]{1,0:T(8,128)(2,1)S(1)} collective-permute-done((bf16[128,1024]{1,0:T(8,128)(2,1)S(1)}, bf16[128,1024]{1,0:T(8,128)(2,1)S(1)}, u32[]{:S(2)}, u32[]{:S(2)}) %collective-permute-start.32) | collective-permute-done | bytes 262176 | tf_op jit(solution)/shard_map/ppermute | solution.py:24
  110.1 1.3 fusion.28
  111.5 2.5 %collective-permute-start.31 = (bf16[128,1024]{1,0:T(8,128)(2,1)}, bf16[128,1024]{1,0:T(8,128)(2,1)}, u32[]{:S(2)}, u32[]{:S(2)}) collective-permute-start(bf16[128,1024]{1,0:T(8,128)(2,1)} %collective-permute-done.22), channel_id=1, source_target_pairs={{0,8},{8,0},{16,24},{24,16},{1,9},{9,1},{17,25},{25,17},{2,10},{10... | collective-permute-start | bytes 786440 | tf_op jit(solution)/shard_map/ppermute | solution.py:24
  114.0 11.7 %collective-permute-done.34 = bf16[128,1024]{1,0:T(8,128)(2,1)} collective-permute-done((bf16[128,1024]{1,0:T(8,128)(2,1)S(1)}, bf16[128,1024]{1,0:T(8,128)(2,1)}, u32[]{:S(2)}, u32[]{:S(2)}) %collective-permute-start.34) | collective-permute-done | bytes 262176 | tf_op jit(solution)/shard_map/ppermute | solution.py:24
  125.7 1.3 collective-permute-done.31
  127.0 1.7 %fusion = bf16[1,256,1024]{2,1,0:T(8,128)(2,1)S(1)} fusion(bf16[128,1024]{1,0:T(8,128)(2,1)} %copy-done.8, bf16[128,1024]{1,0:T(8,128)(2,1)} %collective-permute-done.22, bf16[128,1024]{1,0:T(8,128)(2,1)} %copy-done.9, bf16[128,1024]{1,0:T(8,128)(2,1)} %collective-permute-done.31, bf16[512,1024]{1,0:T(8,128)(2,1)S(1)} %get-tuple-element.46.refs_6_.projector, ...), kind=kOutput, calls=%fused_computation.2 | convolution fusion | flops 272891904 | bytes 1835012 | tf_op jit(solution)/shard_map/dot_general | solution.py:373
  128.7 1.5 %pad_maximum_fusion.2 = (f32[2,128,1024]{2,1,0:T(8,128)}, f32[2,128,1024]{2,1,0:T(8,128)}) fusion(f32[1,128,1024]{2,1,0:T(8,128)S(1)} %copy-done.3, f32[1,128,1024]{2,1,0:T(8,128)S(1)} %bitcast.52, f32[1,128,1024]{2,1,0:T(8,128)S(1)} %copy-done.2, f32[1,128,1024]{2,1,0:T(8,128)S(1)} %get-tuple-element.63), kind=kLoop, calls=%fused_computation.22 | loop fusion | flops 524288 | bytes 4194304 | tf_op jit(solution)/shard_map/stack | solution.py:380
  130.1 2.4 %collective-permute-done.36 = bf16[128,1024]{1,0:T(8,128)(2,1)S(1)} collective-permute-done((bf16[128,1024]{1,0:T(8,128)(2,1)S(1)}, bf16[128,1024]{1,0:T(8,128)(2,1)S(1)}, u32[]{:S(2)}, u32[]{:S(2)}) %collective-permute-start.36) | collective-permute-done | bytes 262176 | tf_op jit(solution)/shard_map/ppermute | solution.py:24
  132.5 4.7 %collective-permute-done.35 = bf16[128,1024]{1,0:T(8,128)(2,1)S(1)} collective-permute-done((bf16[128,1024]{1,0:T(8,128)(2,1)}, bf16[128,1024]{1,0:T(8,128)(2,1)S(1)}, u32[]{:S(2)}, u32[]{:S(2)}) %collective-permute-start.35) | collective-permute-done | bytes 262176 | tf_op jit(solution)/shard_map/ppermute | solution.py:24
  137.2 1.4 %fusion.1 = bf16[1,256,1024]{2,1,0:T(8,128)(2,1)S(1)} fusion(bf16[128,1024]{1,0:T(8,128)(2,1)S(1)} %get-tuple-element.65, bf16[128,1024]{1,0:T(8,128)(2,1)} %collective-permute-done.34, bf16[128,1024]{1,0:T(8,128)(2,1)S(1)} %collective-permute-done.36, bf16[128,1024]{1,0:T(8,128)(2,1)S(1)} %collective-permute-done.35, ...), kind=kOutput, calls=%fused_computation.3 | convolution fusion | flops 272891904 | bytes 1835012 | tf_op jit(solution)/shard_map/dot_general | solution.py:373
  138.7 1.1 pad_maximum_fusion.1
  (63 shorter events, 1.1 us)
Async XLA Ops:
  1.7 9.3 %collective-permute-start.2 = (bf16[128,1024]{1,0:T(8,128)(2,1)S(1)}, bf16[128,1024]{1,0:T(8,128)(2,1)S(1)}, u32[]{:S(2)}, u32[]{:S(2)}) collective-permute-start(bf16[128,1024]{1,0:T(8,128)(2,1)S(1)} %get-tuple-element.33), channel_id=1, source_target_pairs={{0,4},{1,5},{2,6},{3,7},{4,0},{5,1},{6,2},{7,3},{8,12},{9,13},{10,... | collective-permute-start | bytes 786440 | tf_op jit(solution)/shard_map/ppermute | solution.py:24
  4.7 8.1 %collective-permute-start = (bf16[128,1024]{1,0:T(8,128)(2,1)}, bf16[128,1024]{1,0:T(8,128)(2,1)S(1)}, u32[]{:S(2)}, u32[]{:S(2)}) collective-permute-start(bf16[128,1024]{1,0:T(8,128)(2,1)} %bitcast.53), channel_id=1, source_target_pairs={{0,8},{8,0},{16,24},{24,16},{1,9},{9,1},{17,25},{25,17},{2,10},{10... | collective-permute-start | bytes 786440 | tf_op jit(solution)/shard_map/ppermute | solution.py:24
  6.3 7.6 %collective-permute-start.1 = (bf16[128,1024]{1,0:T(8,128)(2,1)S(1)}, bf16[128,1024]{1,0:T(8,128)(2,1)S(1)}, u32[]{:S(2)}, u32[]{:S(2)}) collective-permute-start(bf16[128,1024]{1,0:T(8,128)(2,1)S(1)} %get-tuple-element.34), channel_id=1, source_target_pairs={{0,2},{1,3},{2,0},{3,1},{4,6},{5,7},{6,4},{7,5},{8,10},{9,11},{10,... | collective-permute-start | bytes 786440 | tf_op jit(solution)/shard_map/ppermute | solution.py:24
  11.0 9.1 %collective-permute-start.5 = (bf16[128,1024]{1,0:T(8,128)(2,1)S(1)}, bf16[128,1024]{1,0:T(8,128)(2,1)S(1)}, u32[]{:S(2)}, u32[]{:S(2)}) collective-permute-start(bf16[128,1024]{1,0:T(8,128)(2,1)S(1)} %get-tuple-element.34), channel_id=1, source_target_pairs={{0,4},{1,5},{2,6},{3,7},{4,0},{5,1},{6,2},{7,3},{8,12},{9,13},{10,... | collective-permute-start | bytes 786440 | tf_op jit(solution)/shard_map/ppermute | solution.py:24
  13.8 14.9 %copy-start.7 = (bf16[128,1024]{1,0:T(8,128)(2,1)}, bf16[128,1024]{1,0:T(8,128)(2,1)S(1)}, u32[]{:S(2)}) copy-start(bf16[128,1024]{1,0:T(8,128)(2,1)S(1)} %broadcast_select_fusion) | copy-start | bytes 786436
  13.9 14.9 %collective-permute-start.3 = (bf16[128,1024]{1,0:T(8,128)(2,1)S(1)}, bf16[128,1024]{1,0:T(8,128)(2,1)}, u32[]{:S(2)}, u32[]{:S(2)}) collective-permute-start(bf16[128,1024]{1,0:T(8,128)(2,1)S(1)} %broadcast_select_fusion), channel_id=1, source_target_pairs={{0,16},{8,24},{16,0},{24,8},{1,17},{9,25},{17,1},{25,9},{2,18},{10... | collective-permute-start | bytes 786440 | tf_op jit(solution)/shard_map/ppermute | solution.py:24
  16.5 12.8 %collective-permute-start.4 = (bf16[128,1024]{1,0:T(8,128)(2,1)S(1)}, bf16[128,1024]{1,0:T(8,128)(2,1)S(1)}, u32[]{:S(2)}, u32[]{:S(2)}) collective-permute-start(bf16[128,1024]{1,0:T(8,128)(2,1)S(1)} %get-tuple-element.33), channel_id=1, source_target_pairs={{0,2},{1,3},{2,0},{3,1},{4,6},{5,7},{6,4},{7,5},{8,10},{9,11},{10,... | collective-permute-start | bytes 786440 | tf_op jit(solution)/shard_map/ppermute | solution.py:24
  18.0 10.7 %collective-permute-start.7 = (bf16[128,1024]{1,0:T(8,128)(2,1)S(1)}, bf16[128,1024]{1,0:T(8,128)(2,1)S(1)}, u32[]{:S(2)}, u32[]{:S(2)}) collective-permute-start(bf16[128,1024]{1,0:T(8,128)(2,1)S(1)} %collective-permute-done.2.refs_4_), channel_id=1, source_target_pairs={{0,2},{1,3},{2,0},{3,1},{4,6},{5,7},{6,4},{7,5},{8,10},{9,11},{10,... | collective-permute-start | bytes 786440 | tf_op jit(solution)/shard_map/ppermute | solution.py:24
  18.6 10.8 %collective-permute-start.6 = (bf16[128,1024]{1,0:T(8,128)(2,1)S(1)}, bf16[128,1024]{1,0:T(8,128)(2,1)S(1)}, u32[]{:S(2)}, u32[]{:S(2)}) collective-permute-start(bf16[128,1024]{1,0:T(8,128)(2,1)S(1)} %collective-permute-done.1.refs_1_), channel_id=1, source_target_pairs={{0,4},{1,5},{2,6},{3,7},{4,0},{5,1},{6,2},{7,3},{8,12},{9,13},{10,... | collective-permute-start | bytes 786440 | tf_op jit(solution)/shard_map/ppermute | solution.py:24
  20.2 14.1 %collective-permute-start.11 = (bf16[256,1024]{1,0:T(8,128)(2,1)S(1)}, bf16[256,1024]{1,0:T(8,128)(2,1)S(1)}, u32[]{:S(2)}, u32[]{:S(2)}) collective-permute-start(bf16[256,1024]{1,0:T(8,128)(2,1)S(1)} %slice_bitcast_fusion.refs_0_), channel_id=1, source_target_pairs={{0,1},{1,0},{2,3},{3,2},{4,5},{5,4},{6,7},{7,6},{8,9},{9,8},{10,11... | collective-permute-start | bytes 1572872 | tf_op jit(solution)/shard_map/ppermute | solution.py:24
  28.8 2.4 %collective-permute-start.15 = (bf16[128,1024]{1,0:T(8,128)(2,1)S(1)}, bf16[128,1024]{1,0:T(8,128)(2,1)S(1)}, u32[]{:S(2)}, u32[]{:S(2)}) collective-permute-start(bf16[128,1024]{1,0:T(8,128)(2,1)S(1)} %collective-permute-done.2.refs_4_), channel_id=1, source_target_pairs={{0,1},{1,0},{2,3},{3,2},{4,5},{5,4},{6,7},{7,6},{8,9},{9,8},{10,11... | collective-permute-start | bytes 786440 | tf_op jit(solution)/shard_map/ppermute | solution.py:24
  28.8 3.9 %collective-permute-start.12 = (bf16[128,1024]{1,0:T(8,128)(2,1)S(1)}, bf16[128,1024]{1,0:T(8,128)(2,1)S(1)}, u32[]{:S(2)}, u32[]{:S(2)}) collective-permute-start(bf16[128,1024]{1,0:T(8,128)(2,1)S(1)} %collective-permute-done.1.refs_1_), channel_id=1, source_target_pairs={{0,1},{1,0},{2,3},{3,2},{4,5},{5,4},{6,7},{7,6},{8,9},{9,8},{10,11... | collective-permute-start | bytes 786440 | tf_op jit(solution)/shard_map/ppermute | solution.py:24
  29.3 5.5 %collective-permute-start.14 = (bf16[128,1024]{1,0:T(8,128)(2,1)S(1)}, bf16[128,1024]{1,0:T(8,128)(2,1)S(1)}, u32[]{:S(2)}, u32[]{:S(2)}) collective-permute-start(bf16[128,1024]{1,0:T(8,128)(2,1)S(1)} %collective-permute-done.5.refs_3_), channel_id=1, source_target_pairs={{0,1},{1,0},{2,3},{3,2},{4,5},{5,4},{6,7},{7,6},{8,9},{9,8},{10,11... | collective-permute-start | bytes 786440 | tf_op jit(solution)/shard_map/ppermute | solution.py:24
  29.4 5.4 %collective-permute-start.13 = (bf16[128,1024]{1,0:T(8,128)(2,1)S(1)}, bf16[128,1024]{1,0:T(8,128)(2,1)}, u32[]{:S(2)}, u32[]{:S(2)}) collective-permute-start(bf16[128,1024]{1,0:T(8,128)(2,1)S(1)} %collective-permute-done.4.refs_2_), channel_id=1, source_target_pairs={{0,1},{1,0},{2,3},{3,2},{4,5},{5,4},{6,7},{7,6},{8,9},{9,8},{10,11... | collective-permute-start | bytes 786440 | tf_op jit(solution)/shard_map/ppermute | solution.py:24
  31.2 11.6 %collective-permute-start.10 = (bf16[128,1024]{1,0:T(8,128)(2,1)S(1)}, bf16[128,1024]{1,0:T(8,128)(2,1)S(1)}, u32[]{:S(2)}, u32[]{:S(2)}) collective-permute-start(bf16[128,1024]{1,0:T(8,128)(2,1)S(1)} %broadcast_select_fusion.1), channel_id=1, source_target_pairs={{0,6},{1,7},{2,4},{3,5},{4,2},{5,3},{6,0},{7,1},{8,14},{9,15},{10,... | collective-permute-start | bytes 786440 | tf_op jit(solution)/shard_map/ppermute | solution.py:24
  32.7 13.4 %collective-permute-start.9 = (bf16[128,1024]{1,0:T(8,128)(2,1)S(1)}, bf16[128,1024]{1,0:T(8,128)(2,1)S(1)}, u32[]{:S(2)}, u32[]{:S(2)}) collective-permute-start(bf16[128,1024]{1,0:T(8,128)(2,1)S(1)} %broadcast_select_fusion.1), channel_id=1, source_target_pairs={{0,4},{1,5},{2,6},{3,7},{4,0},{5,1},{6,2},{7,3},{8,12},{9,13},{10,... | collective-permute-start | bytes 786440 | tf_op jit(solution)/shard_map/ppermute | solution.py:24
  34.2 11.8 %collective-permute-start.8 = (bf16[128,1024]{1,0:T(8,128)(2,1)S(1)}, bf16[128,1024]{1,0:T(8,128)(2,1)S(1)}, u32[]{:S(2)}, u32[]{:S(2)}) collective-permute-start(bf16[128,1024]{1,0:T(8,128)(2,1)S(1)} %broadcast_select_fusion.1), channel_id=1, source_target_pairs={{0,2},{1,3},{2,0},{3,1},{4,6},{5,7},{6,4},{7,5},{8,10},{9,11},{10,... | collective-permute-start | bytes 786440 | tf_op jit(solution)/shard_map/ppermute | solution.py:24
  34.8 2.2 %copy-start = (bf16[2048,1024]{1,0:T(8,128)(2,1)S(1)}, bf16[2048,1024]{1,0:T(8,128)(2,1)}, u32[]{:S(2)}) copy-start(bf16[2048,1024]{1,0:T(8,128)(2,1)} %refs_8_.3) | copy-start | bytes 12582916
  42.8 6.9 %copy-start.4 = (bf16[2,256,1024]{2,1,0:T(8,128)(2,1)S(1)}, bf16[2,256,1024]{2,1,0:T(8,128)(2,1)}, u32[]{:S(2)}) copy-start(bf16[2,256,1024]{2,1,0:T(8,128)(2,1)} %param.7) | copy-start | bytes 3145732
  46.1 7.6 %copy-start.1 = (bf16[2048,1024]{1,0:T(8,128)(2,1)S(1)}, bf16[2048,1024]{1,0:T(8,128)(2,1)}, u32[]{:S(2)}) copy-start(bf16[2048,1024]{1,0:T(8,128)(2,1)} %refs_8_.3) | copy-start | bytes 12582916
  46.2 2.7 %collective-permute-start.16 = (bf16[512,1024]{1,0:T(8,128)(2,1)S(1)}, bf16[512,1024]{1,0:T(8,128)(2,1)S(1)}, u32[]{:S(2)}, u32[]{:S(2)}) collective-permute-start(bf16[512,1024]{1,0:T(8,128)(2,1)S(1)} %pad_maximum_fusion.same), channel_id=1, source_target_pairs={{0,1},{1,0},{2,3},{3,2},{4,5},{5,4},{6,7},{7,6},{8,9},{9,8},{10,11... | collective-permute-start | bytes 3145736 | tf_op jit(solution)/shard_map/ppermute | solution.py:24
  46.2 7.5 %collective-permute-start.18 = (bf16[128,1024]{1,0:T(8,128)(2,1)S(1)}, bf16[128,1024]{1,0:T(8,128)(2,1)S(1)}, u32[]{:S(2)}, u32[]{:S(2)}) collective-permute-start(bf16[128,1024]{1,0:T(8,128)(2,1)S(1)} %collective-permute-done.7.refs_1_), channel_id=1, source_target_pairs={{0,1},{1,0},{2,3},{3,2},{4,5},{5,4},{6,7},{7,6},{8,9},{9,8},{10,11... | collective-permute-start | bytes 786440 | tf_op jit(solution)/shard_map/ppermute | solution.py:24
  46.7 7.0 %collective-permute-start.17 = (bf16[128,1024]{1,0:T(8,128)(2,1)S(1)}, bf16[128,1024]{1,0:T(8,128)(2,1)S(1)}, u32[]{:S(2)}, u32[]{:S(2)}) collective-permute-start(bf16[128,1024]{1,0:T(8,128)(2,1)S(1)} %collective-permute-done.6.refs_0_), channel_id=1, source_target_pairs={{0,1},{1,0},{2,3},{3,2},{4,5},{5,4},{6,7},{7,6},{8,9},{9,8},{10,11... | collective-permute-start | bytes 786440 | tf_op jit(solution)/shard_map/ppermute | solution.py:24
  50.1 10.2 %collective-permute-start.25 = (bf16[256,512]{1,0:T(8,128)(2,1)S(1)}, bf16[256,512]{1,0:T(8,128)(2,1)S(1)}, u32[]{:S(2)}, u32[]{:S(2)}) collective-permute-start(bf16[256,512]{1,0:T(8,128)(2,1)S(1)} %fusion.2.refs_0_), channel_id=1, source_target_pairs={{0,6},{1,7},{2,4},{3,5},{4,2},{5,3},{6,0},{7,1},{8,14},{9,15},{10,... | collective-permute-start | bytes 786440 | tf_op jit(solution)/shard_map/ppermute | solution.py:24
  51.8 13.3 %collective-permute-start.24 = (bf16[256,512]{1,0:T(8,128)(2,1)S(1)}, bf16[256,512]{1,0:T(8,128)(2,1)S(1)}, u32[]{:S(2)}, u32[]{:S(2)}) collective-permute-start(bf16[256,512]{1,0:T(8,128)(2,1)S(1)} %fusion.2.refs_0_), channel_id=1, source_target_pairs={{0,4},{1,5},{2,6},{3,7},{4,0},{5,1},{6,2},{7,3},{8,12},{9,13},{10,... | collective-permute-start | bytes 786440 | tf_op jit(solution)/shard_map/ppermute | solution.py:24
  52.5 12.6 %collective-permute-start.23 = (bf16[256,512]{1,0:T(8,128)(2,1)S(1)}, bf16[256,512]{1,0:T(8,128)(2,1)S(1)}, u32[]{:S(2)}, u32[]{:S(2)}) collective-permute-start(bf16[256,512]{1,0:T(8,128)(2,1)S(1)} %fusion.2.refs_0_), channel_id=1, source_target_pairs={{0,2},{1,3},{2,0},{3,1},{4,6},{5,7},{6,4},{7,5},{8,10},{9,11},{10,... | collective-permute-start | bytes 786440 | tf_op jit(solution)/shard_map/ppermute | solution.py:24
  56.1 9.5 %collective-permute-start.20 = (bf16[128,1024]{1,0:T(8,128)(2,1)S(1)}, bf16[128,1024]{1,0:T(8,128)(2,1)S(1)}, u32[]{:S(2)}, u32[]{:S(2)}) collective-permute-start(bf16[128,1024]{1,0:T(8,128)(2,1)S(1)} %get-tuple-element.51), channel_id=1, source_target_pairs={{0,8},{8,0},{16,24},{24,16},{1,9},{9,1},{17,25},{25,17},{2,10},{10... | collective-permute-start | bytes 786440 | tf_op jit(solution)/shard_map/ppermute | solution.py:24
  57.8 8.0 %collective-permute-start.26 = (bf16[256,512]{1,0:T(8,128)(2,1)S(1)}, bf16[256,512]{1,0:T(8,128)(2,1)S(1)}, u32[]{:S(2)}, u32[]{:S(2)}) collective-permute-start(bf16[256,512]{1,0:T(8,128)(2,1)S(1)} %fusion.2.refs_0_), channel_id=1, source_target_pairs={{0,1},{1,0},{2,3},{3,2},{4,5},{5,4},{6,7},{7,6},{8,9},{9,8},{10,11... | collective-permute-start | bytes 786440 | tf_op jit(solution)/shard_map/ppermute | solution.py:24
  60.3 10.5 %collective-permute-start.19 = (bf16[128,1024]{1,0:T(8,128)(2,1)S(1)}, bf16[128,1024]{1,0:T(8,128)(2,1)S(1)}, u32[]{:S(2)}, u32[]{:S(2)}) collective-permute-start(bf16[128,1024]{1,0:T(8,128)(2,1)S(1)} %get-tuple-element.49), channel_id=1, source_target_pairs={{0,8},{8,0},{16,24},{24,16},{1,9},{9,1},{17,25},{25,17},{2,10},{10... | collective-permute-start | bytes 786440 | tf_op jit(solution)/shard_map/ppermute | solution.py:24
  65.1 1.5 %collective-permute-start.29 = (bf16[256,512]{1,0:T(8,128)(2,1)S(1)}, bf16[256,512]{1,0:T(8,128)(2,1)S(1)}, u32[]{:S(2)}, u32[]{:S(2)}) collective-permute-start(bf16[256,512]{1,0:T(8,128)(2,1)S(1)} %collective-permute-done.25.refs_3_), channel_id=1, source_target_pairs={{0,1},{1,0},{2,3},{3,2},{4,5},{5,4},{6,7},{7,6},{8,9},{9,8},{10,11... | collective-permute-start | bytes 786440 | tf_op jit(solution)/shard_map/ppermute | solution.py:24
  65.1 1.9 %collective-permute-start.28 = (bf16[256,512]{1,0:T(8,128)(2,1)S(1)}, bf16[256,512]{1,0:T(8,128)(2,1)S(1)}, u32[]{:S(2)}, u32[]{:S(2)}) collective-permute-start(bf16[256,512]{1,0:T(8,128)(2,1)S(1)} %collective-permute-done.24.refs_2_), channel_id=1, source_target_pairs={{0,1},{1,0},{2,3},{3,2},{4,5},{5,4},{6,7},{7,6},{8,9},{9,8},{10,11... | collective-permute-start | bytes 786440 | tf_op jit(solution)/shard_map/ppermute | solution.py:24
  65.6 1.8 %collective-permute-start.27 = (bf16[256,512]{1,0:T(8,128)(2,1)S(1)}, bf16[256,512]{1,0:T(8,128)(2,1)S(1)}, u32[]{:S(2)}, u32[]{:S(2)}) collective-permute-start(bf16[256,512]{1,0:T(8,128)(2,1)S(1)} %collective-permute-done.23.refs_1_), channel_id=1, source_target_pairs={{0,1},{1,0},{2,3},{3,2},{4,5},{5,4},{6,7},{7,6},{8,9},{9,8},{10,11... | collective-permute-start | bytes 786440 | tf_op jit(solution)/shard_map/ppermute | solution.py:24
  65.7 15.4 %copy-start.5 = (f32[2,128,1024]{2,1,0:T(8,128)S(1)}, f32[2,128,1024]{2,1,0:T(8,128)}, u32[]{:S(2)}) copy-start(f32[2,128,1024]{2,1,0:T(8,128)} %param.10) | copy-start | bytes 3145732
  65.7 15.4 %copy-start.6 = (f32[2,128,1024]{2,1,0:T(8,128)S(1)}, f32[2,128,1024]{2,1,0:T(8,128)}, u32[]{:S(2)}) copy-start(f32[2,128,1024]{2,1,0:T(8,128)} %param.9) | copy-start | bytes 3145732
  65.8 15.3 %collective-permute-start.21 = (bf16[128,1024]{1,0:T(8,128)(2,1)S(1)}, bf16[128,1024]{1,0:T(8,128)(2,1)S(1)}, u32[]{:S(2)}, u32[]{:S(2)}) collective-permute-start(bf16[128,1024]{1,0:T(8,128)(2,1)S(1)} %add_convert_fusion.1), channel_id=1, source_target_pairs={{0,16},{8,24},{16,0},{24,8},{1,17},{9,25},{17,1},{25,9},{2,18},{10... | collective-permute-start | bytes 786440 | tf_op jit(solution)/shard_map/ppermute | solution.py:24
  69.2 25.0 %collective-permute-start.30 = (bf16[256,1024]{1,0:T(8,128)(2,1)S(1)}, bf16[256,1024]{1,0:T(8,128)(2,1)S(1)}, u32[]{:S(2)}, u32[]{:S(2)}) collective-permute-start(bf16[256,1024]{1,0:T(8,128)(2,1)S(1)} %shard_map.90), channel_id=1, source_target_pairs={{0,8},{8,0},{16,24},{24,16},{1,9},{9,1},{17,25},{25,17},{2,10},{10... | collective-permute-start | bytes 1572872 | tf_op jit(solution)/shard_map/ppermute | solution.py:24
  81.5 4.2 %copy-start.8 = (bf16[128,1024]{1,0:T(8,128)(2,1)}, bf16[128,1024]{1,0:T(8,128)(2,1)S(1)}, u32[]{:S(2)}) copy-start(bf16[128,1024]{1,0:T(8,128)(2,1)S(1)} %get-tuple-element.61) | copy-start | bytes 786436
  81.5 17.5 %collective-permute-start.33 = (bf16[128,1024]{1,0:T(8,128)(2,1)S(1)}, bf16[128,1024]{1,0:T(8,128)(2,1)S(1)}, u32[]{:S(2)}, u32[]{:S(2)}) collective-permute-start(bf16[128,1024]{1,0:T(8,128)(2,1)S(1)} %get-tuple-element.61), channel_id=1, source_target_pairs={{0,8},{8,0},{16,24},{24,16},{1,9},{9,1},{17,25},{25,17},{2,10},{10... | collective-permute-start | bytes 786440 | tf_op jit(solution)/shard_map/ppermute | solution.py:24
  81.6 16.6 %collective-permute-start.22 = (bf16[128,1024]{1,0:T(8,128)(2,1)S(1)}, bf16[128,1024]{1,0:T(8,128)(2,1)}, u32[]{:S(2)}, u32[]{:S(2)}) collective-permute-start(bf16[128,1024]{1,0:T(8,128)(2,1)S(1)} %get-tuple-element.61), channel_id=1, source_target_pairs={{0,16},{8,24},{16,0},{24,8},{1,17},{9,25},{17,1},{25,9},{2,18},{10... | collective-permute-start | bytes 786440 | tf_op jit(solution)/shard_map/ppermute | solution.py:24
  94.3 15.9 %collective-permute-start.32 = (bf16[128,1024]{1,0:T(8,128)(2,1)S(1)}, bf16[128,1024]{1,0:T(8,128)(2,1)S(1)}, u32[]{:S(2)}, u32[]{:S(2)}) collective-permute-start(bf16[128,1024]{1,0:T(8,128)(2,1)S(1)} %get-tuple-element.69), channel_id=1, source_target_pairs={{0,16},{8,24},{16,0},{24,8},{1,17},{9,25},{17,1},{25,9},{2,18},{10... | collective-permute-start | bytes 786440 | tf_op jit(solution)/shard_map/ppermute | solution.py:24
  99.1 12.4 %copy-start.9 = (bf16[128,1024]{1,0:T(8,128)(2,1)}, bf16[128,1024]{1,0:T(8,128)(2,1)S(1)}, u32[]{:S(2)}) copy-start(bf16[128,1024]{1,0:T(8,128)(2,1)S(1)} %collective-permute-done.33) | copy-start | bytes 786436
  111.5 14.2 %collective-permute-start.34 = (bf16[128,1024]{1,0:T(8,128)(2,1)S(1)}, bf16[128,1024]{1,0:T(8,128)(2,1)}, u32[]{:S(2)}, u32[]{:S(2)}) collective-permute-start(bf16[128,1024]{1,0:T(8,128)(2,1)S(1)} %get-tuple-element.65), channel_id=1, source_target_pairs={{0,16},{8,24},{16,0},{24,8},{1,17},{9,25},{17,1},{25,9},{2,18},{10... | collective-permute-start | bytes 786440 | tf_op jit(solution)/shard_map/ppermute | solution.py:24
  111.5 15.5 %collective-permute-start.31 = (bf16[128,1024]{1,0:T(8,128)(2,1)}, bf16[128,1024]{1,0:T(8,128)(2,1)}, u32[]{:S(2)}, u32[]{:S(2)}) collective-permute-start(bf16[128,1024]{1,0:T(8,128)(2,1)} %collective-permute-done.22), channel_id=1, source_target_pairs={{0,8},{8,0},{16,24},{24,16},{1,9},{9,1},{17,25},{25,17},{2,10},{10... | collective-permute-start | bytes 786440 | tf_op jit(solution)/shard_map/ppermute | solution.py:24
  114.0 14.7 %copy-start.2 = (f32[1,128,1024]{2,1,0:T(8,128)S(1)}, f32[1,128,1024]{2,1,0:T(8,128)}, u32[]{:S(2)}) copy-start(f32[1,128,1024]{2,1,0:T(8,128)} %get-tuple-element.64) | copy-start | bytes 1572868
  114.0 14.7 %copy-start.3 = (f32[1,128,1024]{2,1,0:T(8,128)S(1)}, f32[1,128,1024]{2,1,0:T(8,128)}, u32[]{:S(2)}) copy-start(f32[1,128,1024]{2,1,0:T(8,128)} %get-tuple-element.66) | copy-start | bytes 1572868
  114.0 18.5 %collective-permute-start.36 = (bf16[128,1024]{1,0:T(8,128)(2,1)S(1)}, bf16[128,1024]{1,0:T(8,128)(2,1)S(1)}, u32[]{:S(2)}, u32[]{:S(2)}) collective-permute-start(bf16[128,1024]{1,0:T(8,128)(2,1)S(1)} %get-tuple-element.65), channel_id=1, source_target_pairs={{0,8},{8,0},{16,24},{24,16},{1,9},{9,1},{17,25},{25,17},{2,10},{10... | collective-permute-start | bytes 786440 | tf_op jit(solution)/shard_map/ppermute | solution.py:24
  125.7 11.5 %collective-permute-start.35 = (bf16[128,1024]{1,0:T(8,128)(2,1)}, bf16[128,1024]{1,0:T(8,128)(2,1)S(1)}, u32[]{:S(2)}, u32[]{:S(2)}) collective-permute-start(bf16[128,1024]{1,0:T(8,128)(2,1)} %collective-permute-done.34), channel_id=1, source_target_pairs={{0,8},{8,0},{16,24},{24,16},{1,9},{9,1},{17,25},{25,17},{2,10},{10... | collective-permute-start | bytes 786440 | tf_op jit(solution)/shard_map/ppermute | solution.py:24

commit v12 on v6

--- a/solution.py
+++ b/solution.py
@@ -307,7 +307,7 @@
         return value
 
     pieces = max(replicas // 2, 1)
-    tokens, tokens_1 = [], []
+    tokens = []
 
     near, far, arrived = spread_near(cotangent[0], far_bits, tokens)
     both = jnp.swapaxes(candidates[:, 0], 1, 2).reshape(-1, candidates.shape[2])
@@ -338,10 +338,11 @@
     ).astype(jnp.bfloat16)
     blocks = spread(heads, far_bits)
     open_0 = reduced(arrived_0, keep_0)
-    tokens_1 += arrived_0[pieces // 2 :]
     blocks = with_partner({mask: [held] for mask, held in blocks.items()})
-    send_1 = heads_product(blocks, here, layer_input, 0, pieces, jnp.bfloat16, scale, tokens_1)
-    keep_1 = heads_product(blocks, here, layer_input, 1, pieces, jnp.float32, scale)
+    send_1 = heads_product(blocks, here, layer_input, 0, pieces, jnp.bfloat16, scale)
+    keep_1 = heads_product(
+        blocks, here, layer_input, 1, pieces, jnp.float32, scale, arrived_0[pieces // 2 :]
+    )
     arrived_1 = [swap(piece, "dp", dp_bits[0]) for piece in send_1]
 
     updates, firsts, seconds, gathered = [], [], [], []

time: 135 us -> 135 us (level)
  transfers between devices with their start and end apart: 38 -> 38, of which waited for: 14 -> 16; matrix products, arithmetic and copies ran while one was open for 7% -> 7% of each run, Pallas kernels for 10% -> 10%
where the time goes in v12:
time: 135 us
  waiting for transfers between devices  69.1 us (51%)
  starting transfers between devices  34.4 us (25%)
  Pallas kernels  13.8 us (10%)
  other arithmetic  8.14 us (6%)
  local copies, waits for them, and re-layouts  4.72 us (3%)
  matrix products  3.41 us (3%)
    ppermute x38, waiting for transfers between devices, swap(): return lax.ppermute(value, axis, [(i, i ^ mask) for i in range(size)])  69.1 us
    ppermute x38, starting transfers between devices, swap(): return lax.ppermute(value, axis, [(i, i ^ mask) for i in range(size)])  34.4 us
    pallas_call x4, Pallas kernels, call_in_vmem(): pl.pallas_call(body, grid_spec=pltpu.PrefetchScalarGridSpec(num_scalar_pr...  7.25 us
    pallas_call x1, Pallas kernels, add_products(): pl.pallas_call(functools.partial(product_body, shape), grid_spec=pltpu.Pr...  5.8 us
    dot_general x2, matrix products, on_device(): lax.dot_general(own, jnp.concatenate(parts, axis=0), TRANSPOSED, preferre...  2.94 us
    another operation x2, other arithmetic, on_device(): return (update, jnp.stack(firsts), jnp.stack(seconds))  2.82 us
  transfers between devices with their start and end apart: 38, of which 16 were waited for; matrix products, arithmetic and copies ran while one was open for 7% of the time, Pallas kernels for 10%

profile of v12, /device:TPU:0, one launch (start us, length us, event | category | flops | bytes accessed | tf_op | source)
XLA Modules:
  0.0 134.6 jit_solution(13406327067515929732)
XLA Ops:
  0.6 1.1 slice_bitcast_fusion.1
  1.7 3.0 %collective-permute-start.2 = (bf16[128,1024]{1,0:T(8,128)(2,1)S(1)}, bf16[128,1024]{1,0:T(8,128)(2,1)S(1)}, u32[]{:S(2)}, u32[]{:S(2)}) collective-permute-start(bf16[128,1024]{1,0:T(8,128)(2,1)S(1)} %get-tuple-element.34), channel_id=1, source_target_pairs={{0,4},{1,5},{2,6},{3,7},{4,0},{5,1},{6,2},{7,3},{8,12},{9,13},{10,... | collective-permute-start | bytes 786440 | tf_op jit(solution)/shard_map/ppermute | solution.py:24
  4.7 1.6 %collective-permute-start = (bf16[128,1024]{1,0:T(8,128)(2,1)}, bf16[128,1024]{1,0:T(8,128)(2,1)S(1)}, u32[]{:S(2)}, u32[]{:S(2)}) collective-permute-start(bf16[128,1024]{1,0:T(8,128)(2,1)} %bitcast.53), channel_id=1, source_target_pairs={{0,8},{8,0},{16,24},{24,16},{1,9},{9,1},{17,25},{25,17},{2,10},{10... | collective-permute-start | bytes 786440 | tf_op jit(solution)/shard_map/ppermute | solution.py:24
  6.3 1.5 %collective-permute-start.1 = (bf16[128,1024]{1,0:T(8,128)(2,1)S(1)}, bf16[128,1024]{1,0:T(8,128)(2,1)S(1)}, u32[]{:S(2)}, u32[]{:S(2)}) collective-permute-start(bf16[128,1024]{1,0:T(8,128)(2,1)S(1)} %get-tuple-element.35), channel_id=1, source_target_pairs={{0,2},{1,3},{2,0},{3,1},{4,6},{5,7},{6,4},{7,5},{8,10},{9,11},{10,... | collective-permute-start | bytes 786440 | tf_op jit(solution)/shard_map/ppermute | solution.py:24
  7.8 0.7 and_compare_fusion.1
  8.5 0.1 broadcast_in_dim.34
  8.6 2.4 %collective-permute-done.2.refs_4_ = bf16[128,1024]{1,0:T(8,128)(2,1)S(1)} collective-permute-done((bf16[128,1024]{1,0:T(8,128)(2,1)S(1)}, bf16[128,1024]{1,0:T(8,128)(2,1)S(1)}, u32[]{:S(2)}, u32[]{:S(2)}) %collective-permute-start.2) | collective-permute-done | bytes 262176 | tf_op jit(solution)/shard_map/ppermute | solution.py:24
  11.0 1.7 %collective-permute-start.5 = (bf16[128,1024]{1,0:T(8,128)(2,1)S(1)}, bf16[128,1024]{1,0:T(8,128)(2,1)S(1)}, u32[]{:S(2)}, u32[]{:S(2)}) collective-permute-start(bf16[128,1024]{1,0:T(8,128)(2,1)S(1)} %get-tuple-element.35), channel_id=1, source_target_pairs={{0,4},{1,5},{2,6},{3,7},{4,0},{5,1},{6,2},{7,3},{8,12},{9,13},{10,... | collective-permute-start | bytes 786440 | tf_op jit(solution)/shard_map/ppermute | solution.py:24
  12.8 1.0 broadcast_select_fusion
  13.9 2.7 %collective-permute-start.3 = (bf16[128,1024]{1,0:T(8,128)(2,1)S(1)}, bf16[128,1024]{1,0:T(8,128)(2,1)}, u32[]{:S(2)}, u32[]{:S(2)}) collective-permute-start(bf16[128,1024]{1,0:T(8,128)(2,1)S(1)} %broadcast_select_fusion), channel_id=1, source_target_pairs={{0,16},{8,24},{16,0},{24,8},{1,17},{9,25},{17,1},{25,9},{2,18},{10... | collective-permute-start | bytes 786440 | tf_op jit(solution)/shard_map/ppermute | solution.py:24
  16.5 1.5 %collective-permute-start.4 = (bf16[128,1024]{1,0:T(8,128)(2,1)S(1)}, bf16[128,1024]{1,0:T(8,128)(2,1)S(1)}, u32[]{:S(2)}, u32[]{:S(2)}) collective-permute-start(bf16[128,1024]{1,0:T(8,128)(2,1)S(1)} %get-tuple-element.34), channel_id=1, source_target_pairs={{0,2},{1,3},{2,0},{3,1},{4,6},{5,7},{6,4},{7,5},{8,10},{9,11},{10,... | collective-permute-start | bytes 786440 | tf_op jit(solution)/shard_map/ppermute | solution.py:24
  18.0 0.5 collective-permute-start.7
  18.5 0.5 collective-permute-start.6
  19.1 1.1 slice_bitcast_fusion.refs_0_
  20.2 8.5 %collective-permute-done.7.refs_1_ = bf16[128,1024]{1,0:T(8,128)(2,1)S(1)} collective-permute-done((bf16[128,1024]{1,0:T(8,128)(2,1)S(1)}, bf16[128,1024]{1,0:T(8,128)(2,1)S(1)}, u32[]{:S(2)}, u32[]{:S(2)}) %collective-permute-start.7) | collective-permute-done | bytes 262176 | tf_op jit(solution)/shard_map/ppermute | solution.py:24
  28.8 0.5 collective-permute-start.12
  29.4 0.4 collective-permute-start.13
  29.9 0.1 broadcast_in_dim.31
  30.0 1.1 broadcast_select_fusion.1
  31.2 1.5 %collective-permute-start.10 = (bf16[128,1024]{1,0:T(8,128)(2,1)S(1)}, bf16[128,1024]{1,0:T(8,128)(2,1)S(1)}, u32[]{:S(2)}, u32[]{:S(2)}) collective-permute-start(bf16[128,1024]{1,0:T(8,128)(2,1)S(1)} %broadcast_select_fusion.1), channel_id=1, source_target_pairs={{0,6},{1,7},{2,4},{3,5},{4,2},{5,3},{6,0},{7,1},{8,14},{9,15},{10,... | collective-permute-start | bytes 786440 | tf_op jit(solution)/shard_map/ppermute | solution.py:24
  32.7 1.5 %collective-permute-start.9 = (bf16[128,1024]{1,0:T(8,128)(2,1)S(1)}, bf16[128,1024]{1,0:T(8,128)(2,1)S(1)}, u32[]{:S(2)}, u32[]{:S(2)}) collective-permute-start(bf16[128,1024]{1,0:T(8,128)(2,1)S(1)} %broadcast_select_fusion.1), channel_id=1, source_target_pairs={{0,4},{1,5},{2,6},{3,7},{4,0},{5,1},{6,2},{7,3},{8,12},{9,13},{10,... | collective-permute-start | bytes 786440 | tf_op jit(solution)/shard_map/ppermute | solution.py:24
  34.2 0.5 collective-permute-start.8
  34.8 2.2 %copy-done = bf16[2048,1024]{1,0:T(8,128)(2,1)S(1)} copy-done((bf16[2048,1024]{1,0:T(8,128)(2,1)S(1)}, bf16[2048,1024]{1,0:T(8,128)(2,1)}, u32[]{:S(2)}) %copy-start) | copy-done | bytes 4194328
  36.9 5.8 %shard_map.85.refs_5_ = f32[1024,1024]{1,0:T(8,128)S(1)} custom-call(s32[2]{0:T(128)S(1)} %pad_add_fusion.here, bf16[256,1024]{1,0:T(8,128)(2,1)S(1)} %slice_bitcast_fusion.refs_0_, bf16[128,1024]{1,0:T(8,128)(2,1)S(1)} %collective-permute-done.1.refs_1_, bf16[128,1024]{1,0:T(8,128)(2,1)S(1)} %collective-permute-done.4.refs_2_, ...), custom_call_target="tpu_custom_call" | custom-call | flops 3221225472 | bytes 10485760 | tf_op jit(solution)/shard_map/pallas_call | solution.py:209
  42.8 3.3 %collective-permute-done.9 = bf16[128,1024]{1,0:T(8,128)(2,1)S(1)} collective-permute-done((bf16[128,1024]{1,0:T(8,128)(2,1)S(1)}, bf16[128,1024]{1,0:T(8,128)(2,1)S(1)}, u32[]{:S(2)}, u32[]{:S(2)}) %collective-permute-start.9) | collective-permute-done | bytes 262176 | tf_op jit(solution)/shard_map/ppermute | solution.py:24
  46.1 0.1 collective-permute-start.16
  46.2 0.5 collective-permute-start.25
  46.8 2.1 %collective-permute-done.16.other = bf16[512,1024]{1,0:T(8,128)(2,1)S(1)} collective-permute-done((bf16[512,1024]{1,0:T(8,128)(2,1)S(1)}, bf16[512,1024]{1,0:T(8,128)(2,1)S(1)}, u32[]{:S(2)}, u32[]{:S(2)}) %collective-permute-start.16) | collective-permute-done | bytes 1048608 | tf_op jit(solution)/shard_map/ppermute | solution.py:24
  48.9 0.8 shard_map.86
  49.7 0.5 fusion.2.refs_0_
  50.1 1.6 %collective-permute-start.19 = (bf16[256,512]{1,0:T(8,128)(2,1)S(1)}, bf16[256,512]{1,0:T(8,128)(2,1)S(1)}, u32[]{:S(2)}, u32[]{:S(2)}) collective-permute-start(bf16[256,512]{1,0:T(8,128)(2,1)S(1)} %fusion.2.refs_0_), channel_id=1, source_target_pairs={{0,6},{1,7},{2,4},{3,5},{4,2},{5,3},{6,0},{7,1},{8,14},{9,15},{10,... | collective-permute-start | bytes 786440 | tf_op jit(solution)/shard_map/ppermute | solution.py:24
  51.7 0.7 collective-permute-start.18
  52.5 1.2 collective-permute-start.17
  53.7 2.4 %shard_map.87 = (bf16[1024,1024]{1,0:T(8,128)(2,1)S(1)}, bf16[128,1024]{1,0:T(8,128)(2,1)S(1)}, bf16[128,1024]{1,0:T(8,128)(2,1)S(1)}) custom-call(s32[2]{0:T(128)S(1)} %pad_add_fusion.here, bf16[128,1024]{1,0:T(8,128)(2,1)S(1)} %collective-permute-done.6.refs_0_, bf16[128,1024]{1,0:T(8,128)(2,1)S(1)} %collective-permute-done.7.refs_1_, ...), custom_call_target="tpu_custom_call" | custom-call | flops 1610612736 | bytes 13107200 | tf_op jit(solution)/shard_map/pallas_call | solution.py:131
  56.1 1.6 %collective-permute-start.29 = (bf16[128,1024]{1,0:T(8,128)(2,1)S(1)}, bf16[128,1024]{1,0:T(8,128)(2,1)S(1)}, u32[]{:S(2)}, u32[]{:S(2)}) collective-permute-start(bf16[128,1024]{1,0:T(8,128)(2,1)S(1)} %get-tuple-element.55), channel_id=1, source_target_pairs={{0,8},{8,0},{16,24},{24,16},{1,9},{9,1},{17,25},{25,17},{2,10},{10... | collective-permute-start | bytes 786440 | tf_op jit(solution)/shard_map/ppermute | solution.py:24
  57.8 1.2 shard_map.90
  59.0 1.3 collective-permute-done.19.refs_3_
  60.3 1.6 %collective-permute-start.26 = (bf16[128,1024]{1,0:T(8,128)(2,1)S(1)}, bf16[128,1024]{1,0:T(8,128)(2,1)S(1)}, u32[]{:S(2)}, u32[]{:S(2)}) collective-permute-start(bf16[128,1024]{1,0:T(8,128)(2,1)S(1)} %get-tuple-element.49), channel_id=1, source_target_pairs={{0,8},{8,0},{16,24},{24,16},{1,9},{9,1},{17,25},{25,17},{2,10},{10... | collective-permute-start | bytes 786440 | tf_op jit(solution)/shard_map/ppermute | solution.py:24
  61.9 3.2 %collective-permute-done.18.refs_2_ = bf16[256,512]{1,0:T(8,128)(2,1)S(1)} collective-permute-done((bf16[256,512]{1,0:T(8,128)(2,1)S(1)}, bf16[256,512]{1,0:T(8,128)(2,1)S(1)}, u32[]{:S(2)}, u32[]{:S(2)}) %collective-permute-start.18) | collective-permute-done | bytes 262176 | tf_op jit(solution)/shard_map/ppermute | solution.py:24
  65.1 0.5 collective-permute-start.22
  65.8 0.4 collective-permute-start.30
  66.2 0.4 collective-permute-done.23.refs_7_
  66.6 0.4 collective-permute-done.22.refs_6_
  67.0 0.4 collective-permute-done.21.refs_5_
  67.4 1.8 %shard_map.89 = (bf16[128,1024]{1,0:T(8,128)(2,1)S(1)}, bf16[128,1024]{1,0:T(8,128)(2,1)S(1)}) custom-call(s32[2]{0:T(128)S(1)} %pad_add_fusion.here, bf16[256,512]{1,0:T(8,128)(2,1)S(1)} %fusion.2.refs_0_, bf16[256,512]{1,0:T(8,128)(2,1)S(1)} %collective-permute-done.17.refs_1_, bf16[256,512]{1,0:T(8,128)(2,1)S(1)} %collective-permute-done.18.refs_2_, ...), custom_call_target="tpu_custom_call" | custom-call | flops 1073741824 | bytes 6815744 | tf_op jit(solution)/shard_map/pallas_call | solution.py:131
  69.2 1.6 %collective-permute-start.27 = (bf16[128,1024]{1,0:T(8,128)(2,1)S(1)}, bf16[128,1024]{1,0:T(8,128)(2,1)S(1)}, u32[]{:S(2)}, u32[]{:S(2)}) collective-permute-start(bf16[128,1024]{1,0:T(8,128)(2,1)S(1)} %get-tuple-element.51), channel_id=1, source_target_pairs={{0,8},{8,0},{16,24},{24,16},{1,9},{9,1},{17,25},{25,17},{2,10},{10... | collective-permute-start | bytes 786440 | tf_op jit(solution)/shard_map/ppermute | solution.py:24
  70.8 10.3 %collective-permute-done.30 = bf16[128,1024]{1,0:T(8,128)(2,1)S(1)} collective-permute-done((bf16[128,1024]{1,0:T(8,128)(2,1)S(1)}, bf16[128,1024]{1,0:T(8,128)(2,1)S(1)}, u32[]{:S(2)}, u32[]{:S(2)}) %collective-permute-start.30) | collective-permute-done | bytes 262176 | tf_op jit(solution)/shard_map/ppermute | solution.py:24
  81.1 1.2 divide_convert_fusion.1
  82.3 2.3 %collective-permute-start.31 = (bf16[128,1024]{1,0:T(8,128)(2,1)S(1)}, bf16[128,1024]{1,0:T(8,128)(2,1)}, u32[]{:S(2)}, u32[]{:S(2)}) collective-permute-start(bf16[128,1024]{1,0:T(8,128)(2,1)S(1)} %get-tuple-element.63), channel_id=1, source_target_pairs={{0,16},{8,24},{16,0},{24,8},{1,17},{9,25},{17,1},{25,9},{2,18},{10... | collective-permute-start | bytes 786440 | tf_op jit(solution)/shard_map/ppermute | solution.py:24
  84.6 1.8 %shard_map.88 = (f32[128,1024]{1,0:T(8,128)S(1)}, f32[128,1024]{1,0:T(8,128)S(1)}) custom-call(s32[2]{0:T(128)S(1)} %pad_add_fusion.here, bf16[256,512]{1,0:T(8,128)(2,1)S(1)} %fusion.2.refs_0_, bf16[256,512]{1,0:T(8,128)(2,1)S(1)} %collective-permute-done.17.refs_1_, bf16[256,512]{1,0:T(8,128)(2,1)S(1)} %collective-permute-done.18.refs_2_, ...), custom_call_target="tpu_custom_call" | custom-call | flops 1073741824 | bytes 7340032 | tf_op jit(solution)/shard_map/pallas_call | solution.py:131
  86.5 0.7 collective-permute-start.28
  87.2 16.7 %collective-permute-done.31 = bf16[128,1024]{1,0:T(8,128)(2,1)} collective-permute-done((bf16[128,1024]{1,0:T(8,128)(2,1)S(1)}, bf16[128,1024]{1,0:T(8,128)(2,1)}, u32[]{:S(2)}, u32[]{:S(2)}) %collective-permute-start.31) | collective-permute-done | bytes 262176 | tf_op jit(solution)/shard_map/ppermute | solution.py:24
  103.9 2.0 %collective-permute-start.34 = (bf16[128,1024]{1,0:T(8,128)(2,1)S(1)}, bf16[128,1024]{1,0:T(8,128)(2,1)S(1)}, u32[]{:S(2)}, u32[]{:S(2)}) collective-permute-start(bf16[128,1024]{1,0:T(8,128)(2,1)S(1)} %get-tuple-element.60), channel_id=1, source_target_pairs={{0,8},{8,0},{16,24},{24,16},{1,9},{9,1},{17,25},{25,17},{2,10},{10... | collective-permute-start | bytes 786440 | tf_op jit(solution)/shard_map/ppermute | solution.py:24
  105.9 2.1 %collective-permute-done.28 = bf16[128,1024]{1,0:T(8,128)(2,1)S(1)} collective-permute-done((bf16[128,1024]{1,0:T(8,128)(2,1)S(1)}, bf16[128,1024]{1,0:T(8,128)(2,1)S(1)}, u32[]{:S(2)}, u32[]{:S(2)}) %collective-permute-start.28) | collective-permute-done | bytes 262176 | tf_op jit(solution)/shard_map/ppermute | solution.py:24
  108.0 3.7 %collective-permute-done.32 = bf16[128,1024]{1,0:T(8,128)(2,1)} collective-permute-done((bf16[128,1024]{1,0:T(8,128)(2,1)}, bf16[128,1024]{1,0:T(8,128)(2,1)}, u32[]{:S(2)}, u32[]{:S(2)}) %collective-permute-start.32) | collective-permute-done | bytes 262176 | tf_op jit(solution)/shard_map/ppermute | solution.py:24
  111.7 3.3 %collective-permute-done.34 = bf16[128,1024]{1,0:T(8,128)(2,1)S(1)} collective-permute-done((bf16[128,1024]{1,0:T(8,128)(2,1)S(1)}, bf16[128,1024]{1,0:T(8,128)(2,1)S(1)}, u32[]{:S(2)}, u32[]{:S(2)}) %collective-permute-start.34) | collective-permute-done | bytes 262176 | tf_op jit(solution)/shard_map/ppermute | solution.py:24
  115.0 1.4 %fusion.28 = (f32[1,128,1024]{2,1,0:T(8,128)}, bf16[128,1024]{1,0:T(8,128)(2,1)S(1)}, f32[1,128,1024]{2,1,0:T(8,128)}) fusion(bf16[128,1024]{1,0:T(8,128)(2,1)S(1)} %collective-permute-done.28, f32[128,1024]{1,0:T(8,128)S(1)} %get-tuple-element.59, bf16[128,1024]{1,0:T(8,128)(2,1)S(1)} %collective-permute-done.34, f32[2,128,1024]{2,1,0:T(8,128)S(1)} %copy-done.6, ...), kind=kLoop, calls=%fused_computation.53 | loop fusion | flops 2097152 | bytes 3407872 | tf_op jit(solution)/shard_map/stack | solution.py:377
  116.4 1.7 %collective-permute-start.37 = (bf16[128,1024]{1,0:T(8,128)(2,1)S(1)}, bf16[128,1024]{1,0:T(8,128)(2,1)S(1)}, u32[]{:S(2)}, u32[]{:S(2)}) collective-permute-start(bf16[128,1024]{1,0:T(8,128)(2,1)S(1)} %get-tuple-element.67), channel_id=1, source_target_pairs={{0,8},{8,0},{16,24},{24,16},{1,9},{9,1},{17,25},{25,17},{2,10},{10... | collective-permute-start | bytes 786440 | tf_op jit(solution)/shard_map/ppermute | solution.py:24
  118.0 7.5 %collective-permute-done.35 = bf16[128,1024]{1,0:T(8,128)(2,1)} collective-permute-done((bf16[128,1024]{1,0:T(8,128)(2,1)S(1)}, bf16[128,1024]{1,0:T(8,128)(2,1)}, u32[]{:S(2)}, u32[]{:S(2)}) %collective-permute-start.35) | collective-permute-done | bytes 262176 | tf_op jit(solution)/shard_map/ppermute | solution.py:24
  125.5 1.5 %fusion = bf16[1,256,1024]{2,1,0:T(8,128)(2,1)S(1)} fusion(bf16[128,1024]{1,0:T(8,128)(2,1)S(1)} %get-tuple-element.63, bf16[128,1024]{1,0:T(8,128)(2,1)} %collective-permute-done.31, bf16[128,1024]{1,0:T(8,128)(2,1)S(1)} %collective-permute-done.33, bf16[128,1024]{1,0:T(8,128)(2,1)} %collective-permute-done.32, ...), kind=kOutput, calls=%fused_computation.2 | convolution fusion | flops 272891904 | bytes 1835012 | tf_op jit(solution)/shard_map/dot_general | solution.py:370
  127.1 1.5 %pad_maximum_fusion.2 = (f32[2,128,1024]{2,1,0:T(8,128)}, f32[2,128,1024]{2,1,0:T(8,128)}) fusion(f32[1,128,1024]{2,1,0:T(8,128)S(1)} %copy-done.4, f32[1,128,1024]{2,1,0:T(8,128)S(1)} %bitcast.52, f32[1,128,1024]{2,1,0:T(8,128)S(1)} %copy-done.3, f32[1,128,1024]{2,1,0:T(8,128)S(1)} %copy-done.2), kind=kLoop, calls=%fused_computation.22 | loop fusion | flops 524288 | bytes 4194304 | tf_op jit(solution)/shard_map/stack | solution.py:377
  128.5 3.6 %collective-permute-done.36 = bf16[128,1024]{1,0:T(8,128)(2,1)S(1)} collective-permute-done((bf16[128,1024]{1,0:T(8,128)(2,1)}, bf16[128,1024]{1,0:T(8,128)(2,1)S(1)}, u32[]{:S(2)}, u32[]{:S(2)}) %collective-permute-start.36) | collective-permute-done | bytes 262176 | tf_op jit(solution)/shard_map/ppermute | solution.py:24
  132.1 1.4 %fusion.1 = bf16[1,256,1024]{2,1,0:T(8,128)(2,1)S(1)} fusion(bf16[128,1024]{1,0:T(8,128)(2,1)S(1)} %get-tuple-element.67, bf16[128,1024]{1,0:T(8,128)(2,1)} %collective-permute-done.35, bf16[128,1024]{1,0:T(8,128)(2,1)S(1)} %collective-permute-done.37, bf16[128,1024]{1,0:T(8,128)(2,1)S(1)} %collective-permute-done.36, ...), kind=kOutput, calls=%fused_computation.3 | convolution fusion | flops 272891904 | bytes 1835012 | tf_op jit(solution)/shard_map/dot_general | solution.py:370
  133.5 1.1 pad_maximum_fusion.1
  (63 shorter events, 0.8 us)
Async XLA Ops:
  1.7 9.3 %collective-permute-start.2 = (bf16[128,1024]{1,0:T(8,128)(2,1)S(1)}, bf16[128,1024]{1,0:T(8,128)(2,1)S(1)}, u32[]{:S(2)}, u32[]{:S(2)}) collective-permute-start(bf16[128,1024]{1,0:T(8,128)(2,1)S(1)} %get-tuple-element.34), channel_id=1, source_target_pairs={{0,4},{1,5},{2,6},{3,7},{4,0},{5,1},{6,2},{7,3},{8,12},{9,13},{10,... | collective-permute-start | bytes 786440 | tf_op jit(solution)/shard_map/ppermute | solution.py:24
  4.7 8.1 %collective-permute-start = (bf16[128,1024]{1,0:T(8,128)(2,1)}, bf16[128,1024]{1,0:T(8,128)(2,1)S(1)}, u32[]{:S(2)}, u32[]{:S(2)}) collective-permute-start(bf16[128,1024]{1,0:T(8,128)(2,1)} %bitcast.53), channel_id=1, source_target_pairs={{0,8},{8,0},{16,24},{24,16},{1,9},{9,1},{17,25},{25,17},{2,10},{10... | collective-permute-start | bytes 786440 | tf_op jit(solution)/shard_map/ppermute | solution.py:24
  6.3 7.5 %collective-permute-start.1 = (bf16[128,1024]{1,0:T(8,128)(2,1)S(1)}, bf16[128,1024]{1,0:T(8,128)(2,1)S(1)}, u32[]{:S(2)}, u32[]{:S(2)}) collective-permute-start(bf16[128,1024]{1,0:T(8,128)(2,1)S(1)} %get-tuple-element.35), channel_id=1, source_target_pairs={{0,2},{1,3},{2,0},{3,1},{4,6},{5,7},{6,4},{7,5},{8,10},{9,11},{10,... | collective-permute-start | bytes 786440 | tf_op jit(solution)/shard_map/ppermute | solution.py:24
  11.0 9.1 %collective-permute-start.5 = (bf16[128,1024]{1,0:T(8,128)(2,1)S(1)}, bf16[128,1024]{1,0:T(8,128)(2,1)S(1)}, u32[]{:S(2)}, u32[]{:S(2)}) collective-permute-start(bf16[128,1024]{1,0:T(8,128)(2,1)S(1)} %get-tuple-element.35), channel_id=1, source_target_pairs={{0,4},{1,5},{2,6},{3,7},{4,0},{5,1},{6,2},{7,3},{8,12},{9,13},{10,... | collective-permute-start | bytes 786440 | tf_op jit(solution)/shard_map/ppermute | solution.py:24
  13.8 14.9 %copy-start.8 = (bf16[128,1024]{1,0:T(8,128)(2,1)}, bf16[128,1024]{1,0:T(8,128)(2,1)S(1)}, u32[]{:S(2)}) copy-start(bf16[128,1024]{1,0:T(8,128)(2,1)S(1)} %broadcast_select_fusion) | copy-start | bytes 786436
  13.9 14.9 %collective-permute-start.3 = (bf16[128,1024]{1,0:T(8,128)(2,1)S(1)}, bf16[128,1024]{1,0:T(8,128)(2,1)}, u32[]{:S(2)}, u32[]{:S(2)}) collective-permute-start(bf16[128,1024]{1,0:T(8,128)(2,1)S(1)} %broadcast_select_fusion), channel_id=1, source_target_pairs={{0,16},{8,24},{16,0},{24,8},{1,17},{9,25},{17,1},{25,9},{2,18},{10... | collective-permute-start | bytes 786440 | tf_op jit(solution)/shard_map/ppermute | solution.py:24
  16.5 12.8 %collective-permute-start.4 = (bf16[128,1024]{1,0:T(8,128)(2,1)S(1)}, bf16[128,1024]{1,0:T(8,128)(2,1)S(1)}, u32[]{:S(2)}, u32[]{:S(2)}) collective-permute-start(bf16[128,1024]{1,0:T(8,128)(2,1)S(1)} %get-tuple-element.34), channel_id=1, source_target_pairs={{0,2},{1,3},{2,0},{3,1},{4,6},{5,7},{6,4},{7,5},{8,10},{9,11},{10,... | collective-permute-start | bytes 786440 | tf_op jit(solution)/shard_map/ppermute | solution.py:24
  18.0 10.7 %collective-permute-start.7 = (bf16[128,1024]{1,0:T(8,128)(2,1)S(1)}, bf16[128,1024]{1,0:T(8,128)(2,1)S(1)}, u32[]{:S(2)}, u32[]{:S(2)}) collective-permute-start(bf16[128,1024]{1,0:T(8,128)(2,1)S(1)} %collective-permute-done.2.refs_4_), channel_id=1, source_target_pairs={{0,2},{1,3},{2,0},{3,1},{4,6},{5,7},{6,4},{7,5},{8,10},{9,11},{10,... | collective-permute-start | bytes 786440 | tf_op jit(solution)/shard_map/ppermute | solution.py:24
  18.5 10.8 %collective-permute-start.6 = (bf16[128,1024]{1,0:T(8,128)(2,1)S(1)}, bf16[128,1024]{1,0:T(8,128)(2,1)S(1)}, u32[]{:S(2)}, u32[]{:S(2)}) collective-permute-start(bf16[128,1024]{1,0:T(8,128)(2,1)S(1)} %collective-permute-done.1.refs_1_), channel_id=1, source_target_pairs={{0,4},{1,5},{2,6},{3,7},{4,0},{5,1},{6,2},{7,3},{8,12},{9,13},{10,... | collective-permute-start | bytes 786440 | tf_op jit(solution)/shard_map/ppermute | solution.py:24
  20.1 14.1 %collective-permute-start.11 = (bf16[256,1024]{1,0:T(8,128)(2,1)S(1)}, bf16[256,1024]{1,0:T(8,128)(2,1)S(1)}, u32[]{:S(2)}, u32[]{:S(2)}) collective-permute-start(bf16[256,1024]{1,0:T(8,128)(2,1)S(1)} %slice_bitcast_fusion.refs_0_), channel_id=1, source_target_pairs={{0,1},{1,0},{2,3},{3,2},{4,5},{5,4},{6,7},{7,6},{8,9},{9,8},{10,11... | collective-permute-start | bytes 1572872 | tf_op jit(solution)/shard_map/ppermute | solution.py:24
  28.8 2.4 %collective-permute-start.15 = (bf16[128,1024]{1,0:T(8,128)(2,1)S(1)}, bf16[128,1024]{1,0:T(8,128)(2,1)S(1)}, u32[]{:S(2)}, u32[]{:S(2)}) collective-permute-start(bf16[128,1024]{1,0:T(8,128)(2,1)S(1)} %collective-permute-done.2.refs_4_), channel_id=1, source_target_pairs={{0,1},{1,0},{2,3},{3,2},{4,5},{5,4},{6,7},{7,6},{8,9},{9,8},{10,11... | collective-permute-start | bytes 786440 | tf_op jit(solution)/shard_map/ppermute | solution.py:24
  28.8 3.9 %collective-permute-start.12 = (bf16[128,1024]{1,0:T(8,128)(2,1)S(1)}, bf16[128,1024]{1,0:T(8,128)(2,1)S(1)}, u32[]{:S(2)}, u32[]{:S(2)}) collective-permute-start(bf16[128,1024]{1,0:T(8,128)(2,1)S(1)} %collective-permute-done.1.refs_1_), channel_id=1, source_target_pairs={{0,1},{1,0},{2,3},{3,2},{4,5},{5,4},{6,7},{7,6},{8,9},{9,8},{10,11... | collective-permute-start | bytes 786440 | tf_op jit(solution)/shard_map/ppermute | solution.py:24
  29.3 5.5 %collective-permute-start.14 = (bf16[128,1024]{1,0:T(8,128)(2,1)S(1)}, bf16[128,1024]{1,0:T(8,128)(2,1)S(1)}, u32[]{:S(2)}, u32[]{:S(2)}) collective-permute-start(bf16[128,1024]{1,0:T(8,128)(2,1)S(1)} %collective-permute-done.5.refs_3_), channel_id=1, source_target_pairs={{0,1},{1,0},{2,3},{3,2},{4,5},{5,4},{6,7},{7,6},{8,9},{9,8},{10,11... | collective-permute-start | bytes 786440 | tf_op jit(solution)/shard_map/ppermute | solution.py:24
  29.4 5.4 %collective-permute-start.13 = (bf16[128,1024]{1,0:T(8,128)(2,1)S(1)}, bf16[128,1024]{1,0:T(8,128)(2,1)}, u32[]{:S(2)}, u32[]{:S(2)}) collective-permute-start(bf16[128,1024]{1,0:T(8,128)(2,1)S(1)} %collective-permute-done.4.refs_2_), channel_id=1, source_target_pairs={{0,1},{1,0},{2,3},{3,2},{4,5},{5,4},{6,7},{7,6},{8,9},{9,8},{10,11... | collective-permute-start | bytes 786440 | tf_op jit(solution)/shard_map/ppermute | solution.py:24
  31.2 11.6 %collective-permute-start.10 = (bf16[128,1024]{1,0:T(8,128)(2,1)S(1)}, bf16[128,1024]{1,0:T(8,128)(2,1)S(1)}, u32[]{:S(2)}, u32[]{:S(2)}) collective-permute-start(bf16[128,1024]{1,0:T(8,128)(2,1)S(1)} %broadcast_select_fusion.1), channel_id=1, source_target_pairs={{0,6},{1,7},{2,4},{3,5},{4,2},{5,3},{6,0},{7,1},{8,14},{9,15},{10,... | collective-permute-start | bytes 786440 | tf_op jit(solution)/shard_map/ppermute | solution.py:24
  32.7 13.4 %collective-permute-start.9 = (bf16[128,1024]{1,0:T(8,128)(2,1)S(1)}, bf16[128,1024]{1,0:T(8,128)(2,1)S(1)}, u32[]{:S(2)}, u32[]{:S(2)}) collective-permute-start(bf16[128,1024]{1,0:T(8,128)(2,1)S(1)} %broadcast_select_fusion.1), channel_id=1, source_target_pairs={{0,4},{1,5},{2,6},{3,7},{4,0},{5,1},{6,2},{7,3},{8,12},{9,13},{10,... | collective-permute-start | bytes 786440 | tf_op jit(solution)/shard_map/ppermute | solution.py:24
  34.2 11.8 %collective-permute-start.8 = (bf16[128,1024]{1,0:T(8,128)(2,1)S(1)}, bf16[128,1024]{1,0:T(8,128)(2,1)S(1)}, u32[]{:S(2)}, u32[]{:S(2)}) collective-permute-start(bf16[128,1024]{1,0:T(8,128)(2,1)S(1)} %broadcast_select_fusion.1), channel_id=1, source_target_pairs={{0,2},{1,3},{2,0},{3,1},{4,6},{5,7},{6,4},{7,5},{8,10},{9,11},{10,... | collective-permute-start | bytes 786440 | tf_op jit(solution)/shard_map/ppermute | solution.py:24
  34.8 2.2 %copy-start = (bf16[2048,1024]{1,0:T(8,128)(2,1)S(1)}, bf16[2048,1024]{1,0:T(8,128)(2,1)}, u32[]{:S(2)}) copy-start(bf16[2048,1024]{1,0:T(8,128)(2,1)} %refs_8_.3) | copy-start | bytes 12582916
  42.8 6.9 %copy-start.5 = (bf16[2,256,1024]{2,1,0:T(8,128)(2,1)S(1)}, bf16[2,256,1024]{2,1,0:T(8,128)(2,1)}, u32[]{:S(2)}) copy-start(bf16[2,256,1024]{2,1,0:T(8,128)(2,1)} %param.7) | copy-start | bytes 3145732
  46.1 7.6 %copy-start.1 = (bf16[2048,1024]{1,0:T(8,128)(2,1)S(1)}, bf16[2048,1024]{1,0:T(8,128)(2,1)}, u32[]{:S(2)}) copy-start(bf16[2048,1024]{1,0:T(8,128)(2,1)} %refs_8_.3) | copy-start | bytes 12582916
  46.1 2.7 %collective-permute-start.16 = (bf16[512,1024]{1,0:T(8,128)(2,1)S(1)}, bf16[512,1024]{1,0:T(8,128)(2,1)S(1)}, u32[]{:S(2)}, u32[]{:S(2)}) collective-permute-start(bf16[512,1024]{1,0:T(8,128)(2,1)S(1)} %pad_maximum_fusion.same), channel_id=1, source_target_pairs={{0,1},{1,0},{2,3},{3,2},{4,5},{5,4},{6,7},{7,6},{8,9},{9,8},{10,11... | collective-permute-start | bytes 3145736 | tf_op jit(solution)/shard_map/ppermute | solution.py:24
  46.2 7.5 %collective-permute-start.25 = (bf16[128,1024]{1,0:T(8,128)(2,1)S(1)}, bf16[128,1024]{1,0:T(8,128)(2,1)S(1)}, u32[]{:S(2)}, u32[]{:S(2)}) collective-permute-start(bf16[128,1024]{1,0:T(8,128)(2,1)S(1)} %collective-permute-done.7.refs_1_), channel_id=1, source_target_pairs={{0,1},{1,0},{2,3},{3,2},{4,5},{5,4},{6,7},{7,6},{8,9},{9,8},{10,11... | collective-permute-start | bytes 786440 | tf_op jit(solution)/shard_map/ppermute | solution.py:24
  46.7 7.0 %collective-permute-start.24 = (bf16[128,1024]{1,0:T(8,128)(2,1)S(1)}, bf16[128,1024]{1,0:T(8,128)(2,1)S(1)}, u32[]{:S(2)}, u32[]{:S(2)}) collective-permute-start(bf16[128,1024]{1,0:T(8,128)(2,1)S(1)} %collective-permute-done.6.refs_0_), channel_id=1, source_target_pairs={{0,1},{1,0},{2,3},{3,2},{4,5},{5,4},{6,7},{7,6},{8,9},{9,8},{10,11... | collective-permute-start | bytes 786440 | tf_op jit(solution)/shard_map/ppermute | solution.py:24
  50.1 10.2 %collective-permute-start.19 = (bf16[256,512]{1,0:T(8,128)(2,1)S(1)}, bf16[256,512]{1,0:T(8,128)(2,1)S(1)}, u32[]{:S(2)}, u32[]{:S(2)}) collective-permute-start(bf16[256,512]{1,0:T(8,128)(2,1)S(1)} %fusion.2.refs_0_), channel_id=1, source_target_pairs={{0,6},{1,7},{2,4},{3,5},{4,2},{5,3},{6,0},{7,1},{8,14},{9,15},{10,... | collective-permute-start | bytes 786440 | tf_op jit(solution)/shard_map/ppermute | solution.py:24
  51.7 13.3 %collective-permute-start.18 = (bf16[256,512]{1,0:T(8,128)(2,1)S(1)}, bf16[256,512]{1,0:T(8,128)(2,1)S(1)}, u32[]{:S(2)}, u32[]{:S(2)}) collective-permute-start(bf16[256,512]{1,0:T(8,128)(2,1)S(1)} %fusion.2.refs_0_), channel_id=1, source_target_pairs={{0,4},{1,5},{2,6},{3,7},{4,0},{5,1},{6,2},{7,3},{8,12},{9,13},{10,... | collective-permute-start | bytes 786440 | tf_op jit(solution)/shard_map/ppermute | solution.py:24
  52.5 12.6 %collective-permute-start.17 = (bf16[256,512]{1,0:T(8,128)(2,1)S(1)}, bf16[256,512]{1,0:T(8,128)(2,1)S(1)}, u32[]{:S(2)}, u32[]{:S(2)}) collective-permute-start(bf16[256,512]{1,0:T(8,128)(2,1)S(1)} %fusion.2.refs_0_), channel_id=1, source_target_pairs={{0,2},{1,3},{2,0},{3,1},{4,6},{5,7},{6,4},{7,5},{8,10},{9,11},{10,... | collective-permute-start | bytes 786440 | tf_op jit(solution)/shard_map/ppermute | solution.py:24
  56.1 9.5 %collective-permute-start.29 = (bf16[128,1024]{1,0:T(8,128)(2,1)S(1)}, bf16[128,1024]{1,0:T(8,128)(2,1)S(1)}, u32[]{:S(2)}, u32[]{:S(2)}) collective-permute-start(bf16[128,1024]{1,0:T(8,128)(2,1)S(1)} %get-tuple-element.55), channel_id=1, source_target_pairs={{0,8},{8,0},{16,24},{24,16},{1,9},{9,1},{17,25},{25,17},{2,10},{10... | collective-permute-start | bytes 786440 | tf_op jit(solution)/shard_map/ppermute | solution.py:24
  57.8 8.0 %collective-permute-start.20 = (bf16[256,512]{1,0:T(8,128)(2,1)S(1)}, bf16[256,512]{1,0:T(8,128)(2,1)S(1)}, u32[]{:S(2)}, u32[]{:S(2)}) collective-permute-start(bf16[256,512]{1,0:T(8,128)(2,1)S(1)} %fusion.2.refs_0_), channel_id=1, source_target_pairs={{0,1},{1,0},{2,3},{3,2},{4,5},{5,4},{6,7},{7,6},{8,9},{9,8},{10,11... | collective-permute-start | bytes 786440 | tf_op jit(solution)/shard_map/ppermute | solution.py:24
  60.3 10.5 %collective-permute-start.26 = (bf16[128,1024]{1,0:T(8,128)(2,1)S(1)}, bf16[128,1024]{1,0:T(8,128)(2,1)S(1)}, u32[]{:S(2)}, u32[]{:S(2)}) collective-permute-start(bf16[128,1024]{1,0:T(8,128)(2,1)S(1)} %get-tuple-element.49), channel_id=1, source_target_pairs={{0,8},{8,0},{16,24},{24,16},{1,9},{9,1},{17,25},{25,17},{2,10},{10... | collective-permute-start | bytes 786440 | tf_op jit(solution)/shard_map/ppermute | solution.py:24
  65.1 1.5 %collective-permute-start.23 = (bf16[256,512]{1,0:T(8,128)(2,1)S(1)}, bf16[256,512]{1,0:T(8,128)(2,1)S(1)}, u32[]{:S(2)}, u32[]{:S(2)}) collective-permute-start(bf16[256,512]{1,0:T(8,128)(2,1)S(1)} %collective-permute-done.19.refs_3_), channel_id=1, source_target_pairs={{0,1},{1,0},{2,3},{3,2},{4,5},{5,4},{6,7},{7,6},{8,9},{9,8},{10,11... | collective-permute-start | bytes 786440 | tf_op jit(solution)/shard_map/ppermute | solution.py:24
  65.1 1.9 %collective-permute-start.22 = (bf16[256,512]{1,0:T(8,128)(2,1)S(1)}, bf16[256,512]{1,0:T(8,128)(2,1)S(1)}, u32[]{:S(2)}, u32[]{:S(2)}) collective-permute-start(bf16[256,512]{1,0:T(8,128)(2,1)S(1)} %collective-permute-done.18.refs_2_), channel_id=1, source_target_pairs={{0,1},{1,0},{2,3},{3,2},{4,5},{5,4},{6,7},{7,6},{8,9},{9,8},{10,11... | collective-permute-start | bytes 786440 | tf_op jit(solution)/shard_map/ppermute | solution.py:24
  65.6 1.8 %collective-permute-start.21 = (bf16[256,512]{1,0:T(8,128)(2,1)S(1)}, bf16[256,512]{1,0:T(8,128)(2,1)S(1)}, u32[]{:S(2)}, u32[]{:S(2)}) collective-permute-start(bf16[256,512]{1,0:T(8,128)(2,1)S(1)} %collective-permute-done.17.refs_1_), channel_id=1, source_target_pairs={{0,1},{1,0},{2,3},{3,2},{4,5},{5,4},{6,7},{7,6},{8,9},{9,8},{10,11... | collective-permute-start | bytes 786440 | tf_op jit(solution)/shard_map/ppermute | solution.py:24
  65.7 15.4 %copy-start.6 = (f32[2,128,1024]{2,1,0:T(8,128)S(1)}, f32[2,128,1024]{2,1,0:T(8,128)}, u32[]{:S(2)}) copy-start(f32[2,128,1024]{2,1,0:T(8,128)} %param.10) | copy-start | bytes 3145732
  65.7 15.4 %copy-start.7 = (f32[2,128,1024]{2,1,0:T(8,128)S(1)}, f32[2,128,1024]{2,1,0:T(8,128)}, u32[]{:S(2)}) copy-start(f32[2,128,1024]{2,1,0:T(8,128)} %param.9) | copy-start | bytes 3145732
  65.8 15.3 %collective-permute-start.30 = (bf16[128,1024]{1,0:T(8,128)(2,1)S(1)}, bf16[128,1024]{1,0:T(8,128)(2,1)S(1)}, u32[]{:S(2)}, u32[]{:S(2)}) collective-permute-start(bf16[128,1024]{1,0:T(8,128)(2,1)S(1)} %add_convert_fusion), channel_id=1, source_target_pairs={{0,16},{8,24},{16,0},{24,8},{1,17},{9,25},{17,1},{25,9},{2,18},{10... | collective-permute-start | bytes 786440 | tf_op jit(solution)/shard_map/ppermute | solution.py:24
  69.2 17.2 %collective-permute-start.27 = (bf16[128,1024]{1,0:T(8,128)(2,1)S(1)}, bf16[128,1024]{1,0:T(8,128)(2,1)S(1)}, u32[]{:S(2)}, u32[]{:S(2)}) collective-permute-start(bf16[128,1024]{1,0:T(8,128)(2,1)S(1)} %get-tuple-element.51), channel_id=1, source_target_pairs={{0,8},{8,0},{16,24},{24,16},{1,9},{9,1},{17,25},{25,17},{2,10},{10... | collective-permute-start | bytes 786440 | tf_op jit(solution)/shard_map/ppermute | solution.py:24
  82.3 23.6 %collective-permute-start.33 = (bf16[128,1024]{1,0:T(8,128)(2,1)S(1)}, bf16[128,1024]{1,0:T(8,128)(2,1)S(1)}, u32[]{:S(2)}, u32[]{:S(2)}) collective-permute-start(bf16[128,1024]{1,0:T(8,128)(2,1)S(1)} %get-tuple-element.63), channel_id=1, source_target_pairs={{0,8},{8,0},{16,24},{24,16},{1,9},{9,1},{17,25},{25,17},{2,10},{10... | collective-permute-start | bytes 786440 | tf_op jit(solution)/shard_map/ppermute | solution.py:24
  82.3 21.6 %collective-permute-start.31 = (bf16[128,1024]{1,0:T(8,128)(2,1)S(1)}, bf16[128,1024]{1,0:T(8,128)(2,1)}, u32[]{:S(2)}, u32[]{:S(2)}) collective-permute-start(bf16[128,1024]{1,0:T(8,128)(2,1)S(1)} %get-tuple-element.63), channel_id=1, source_target_pairs={{0,16},{8,24},{16,0},{24,8},{1,17},{9,25},{17,1},{25,9},{2,18},{10... | collective-permute-start | bytes 786440 | tf_op jit(solution)/shard_map/ppermute | solution.py:24
  86.5 21.5 %collective-permute-start.28 = (bf16[128,1024]{1,0:T(8,128)(2,1)S(1)}, bf16[128,1024]{1,0:T(8,128)(2,1)S(1)}, u32[]{:S(2)}, u32[]{:S(2)}) collective-permute-start(bf16[128,1024]{1,0:T(8,128)(2,1)S(1)} %add_convert_fusion.1), channel_id=1, source_target_pairs={{0,16},{8,24},{16,0},{24,8},{1,17},{9,25},{17,1},{25,9},{2,18},{10... | collective-permute-start | bytes 786440 | tf_op jit(solution)/shard_map/ppermute | solution.py:24
  103.9 7.8 %collective-permute-start.32 = (bf16[128,1024]{1,0:T(8,128)(2,1)}, bf16[128,1024]{1,0:T(8,128)(2,1)}, u32[]{:S(2)}, u32[]{:S(2)}) collective-permute-start(bf16[128,1024]{1,0:T(8,128)(2,1)} %collective-permute-done.31), channel_id=1, source_target_pairs={{0,8},{8,0},{16,24},{24,16},{1,9},{9,1},{17,25},{25,17},{2,10},{10... | collective-permute-start | bytes 786440 | tf_op jit(solution)/shard_map/ppermute | solution.py:24
  103.9 11.1 %collective-permute-start.34 = (bf16[128,1024]{1,0:T(8,128)(2,1)S(1)}, bf16[128,1024]{1,0:T(8,128)(2,1)S(1)}, u32[]{:S(2)}, u32[]{:S(2)}) collective-permute-start(bf16[128,1024]{1,0:T(8,128)(2,1)S(1)} %get-tuple-element.60), channel_id=1, source_target_pairs={{0,8},{8,0},{16,24},{24,16},{1,9},{9,1},{17,25},{25,17},{2,10},{10... | collective-permute-start | bytes 786440 | tf_op jit(solution)/shard_map/ppermute | solution.py:24
  116.4 9.2 %collective-permute-start.35 = (bf16[128,1024]{1,0:T(8,128)(2,1)S(1)}, bf16[128,1024]{1,0:T(8,128)(2,1)}, u32[]{:S(2)}, u32[]{:S(2)}) collective-permute-start(bf16[128,1024]{1,0:T(8,128)(2,1)S(1)} %get-tuple-element.67), channel_id=1, source_target_pairs={{0,16},{8,24},{16,0},{24,8},{1,17},{9,25},{17,1},{25,9},{2,18},{10... | collective-permute-start | bytes 786440 | tf_op jit(solution)/shard_map/ppermute | solution.py:24
  116.4 10.7 %copy-start.2 = (f32[1,128,1024]{2,1,0:T(8,128)S(1)}, f32[1,128,1024]{2,1,0:T(8,128)}, u32[]{:S(2)}) copy-start(f32[1,128,1024]{2,1,0:T(8,128)} %get-tuple-element.65) | copy-start | bytes 1572868
  116.4 10.7 %copy-start.3 = (f32[1,128,1024]{2,1,0:T(8,128)S(1)}, f32[1,128,1024]{2,1,0:T(8,128)}, u32[]{:S(2)}) copy-start(f32[1,128,1024]{2,1,0:T(8,128)} %get-tuple-element.66) | copy-start | bytes 1572868
  116.4 10.7 %copy-start.4 = (f32[1,128,1024]{2,1,0:T(8,128)S(1)}, f32[1,128,1024]{2,1,0:T(8,128)}, u32[]{:S(2)}) copy-start(f32[1,128,1024]{2,1,0:T(8,128)} %get-tuple-element.68) | copy-start | bytes 1572868
  116.4 12.1 %collective-permute-start.37 = (bf16[128,1024]{1,0:T(8,128)(2,1)S(1)}, bf16[128,1024]{1,0:T(8,128)(2,1)S(1)}, u32[]{:S(2)}, u32[]{:S(2)}) collective-permute-start(bf16[128,1024]{1,0:T(8,128)(2,1)S(1)} %get-tuple-element.67), channel_id=1, source_target_pairs={{0,8},{8,0},{16,24},{24,16},{1,9},{9,1},{17,25},{25,17},{2,10},{10... | collective-permute-start | bytes 786440 | tf_op jit(solution)/shard_map/ppermute | solution.py:24
  125.5 6.6 %collective-permute-start.36 = (bf16[128,1024]{1,0:T(8,128)(2,1)}, bf16[128,1024]{1,0:T(8,128)(2,1)S(1)}, u32[]{:S(2)}, u32[]{:S(2)}) collective-permute-start(bf16[128,1024]{1,0:T(8,128)(2,1)} %collective-permute-done.35), channel_id=1, source_target_pairs={{0,8},{8,0},{16,24},{24,16},{1,9},{9,1},{17,25},{25,17},{2,10},{10... | collective-permute-start | bytes 786440 | tf_op jit(solution)/shard_map/ppermute | solution.py:24

commit v13 on v12

--- a/solution.py
+++ b/solution.py
@@ -345,21 +345,28 @@
     )
     arrived_1 = [swap(piece, "dp", dp_bits[0]) for piece in send_1]
 
+    def moments(matrix, keep, received):
+        projected = keep + received.astype(jnp.float32)
+        return (
+            beta_first * moment_first[matrix] + (1.0 - beta_first) * projected,
+            beta_second * moment_second[matrix] + (1.0 - beta_second) * projected * projected,
+        )
+
     updates, firsts, seconds, gathered = [], [], [], []
     for matrix, (keep, received) in enumerate((open_0, reduced(arrived_1, keep_1))):
         if gathered:
-            received, firsts[0], *gathered[0][:-1] = lax.optimization_barrier(
-                (received, firsts[0], *gathered[0][:-1])
+            received, *gathered[0][-3:-1] = lax.optimization_barrier(
+                (received, *gathered[0][-3:-1])
             )
-        projected = keep + received.astype(jnp.float32)
-        first = beta_first * moment_first[matrix] + (1.0 - beta_first) * projected
-        second = beta_second * moment_second[matrix] + (1.0 - beta_second) * projected * projected
+        first, second = moments(matrix, keep, received)
         direction = (
             first
             / (1.0 - beta_first**STEP)
             / (jnp.sqrt(second / (1.0 - beta_second**STEP)) + epsilon)
-        )
-        parts = [direction.astype(jnp.bfloat16)]
+        ).astype(jnp.bfloat16)
+        direction, keep, received = lax.optimization_barrier((direction, keep, received))
+        first, second = moments(matrix, keep, received)
+        parts = [direction]
         for bit in reversed(dp_bits):
             parts = [swap(piece, "dp", bit) for piece in parts] + parts
         gathered.append(parts)

time: 135 us -> 134 us (level)
  waiting for transfers between devices: 69.1 us -> 62.9 us
  starting transfers between devices: 34.4 us -> 37.9 us
  other arithmetic: 8.14 us -> 10.4 us
    ppermute x38, waiting for transfers between devices: 69.1 us -> 62.9 us  [swap(): return lax.ppermute(value, axis, [(i, i ^ mask) for i in range(size)])]
    ppermute x38, starting transfers between devices: 34.4 us -> 37.9 us  [swap(): return lax.ppermute(value, axis, [(i, i ^ mask) for i in range(size)])]
    convert_element_type x1 -> x2, other arithmetic: 1.19 us -> 2.72 us  [on_device(): direction = (first / (1.0 - beta_first ** STEP) / (jnp.sqrt(second / (1.0...]
  transfers between devices with their start and end apart: 38 -> 38, of which waited for: 16 -> 14; matrix products, arithmetic and copies ran while one was open for 7% -> 9% of each run, Pallas kernels for 10% -> 10%
where the time goes in v13:
time: 134 us
  waiting for transfers between devices  62.9 us (47%)
  starting transfers between devices  37.9 us (28%)
  Pallas kernels  13.8 us (10%)
  other arithmetic  10.4 us (8%)
  local copies, waits for them, and re-layouts  4.56 us (3%)
  matrix products  3.47 us (3%)
    ppermute x38, waiting for transfers between devices, swap(): return lax.ppermute(value, axis, [(i, i ^ mask) for i in range(size)])  62.9 us
    ppermute x38, starting transfers between devices, swap(): return lax.ppermute(value, axis, [(i, i ^ mask) for i in range(size)])  37.9 us
    pallas_call x4, Pallas kernels, call_in_vmem(): pl.pallas_call(body, grid_spec=pltpu.PrefetchScalarGridSpec(num_scalar_pr...  7.26 us
    pallas_call x1, Pallas kernels, add_products(): pl.pallas_call(functools.partial(product_body, shape), grid_spec=pltpu.Pr...  5.8 us
    dot_general x2, matrix products, on_device(): lax.dot_general(own, jnp.concatenate(parts, axis=0), TRANSPOSED, preferre...  2.99 us
    another operation x2, other arithmetic, on_device(): return (update, jnp.stack(firsts), jnp.stack(seconds))  2.87 us
    convert_element_type x2, other arithmetic, on_device(): direction = (first / (1.0 - beta_first ** STEP) / (jnp.sqrt(second / (1.0...  2.72 us
  transfers between devices with their start and end apart: 38, of which 14 were waited for; matrix products, arithmetic and copies ran while one was open for 9% of the time, Pallas kernels for 10%

profile of v13, /device:TPU:0, one launch (start us, length us, event | category | flops | bytes accessed | tf_op | source)
XLA Modules:
  0.0 134.0 jit_solution(6318691044443274470)
XLA Ops:
  0.6 1.9 %slice_bitcast_fusion.1 = (bf16[128,1024]{1,0:T(8,128)(2,1)}, bf16[128,1024]{1,0:T(8,128)(2,1)}) fusion(bf16[2,256,1024]{2,1,0:T(8,128)(2,1)} %param.7), kind=kLoop, calls=%fused_computation.67 | loop fusion | bytes 1048576 | tf_op jit(solution)/shard_map/slice | solution.py:53
  2.6 3.0 %collective-permute-start.2 = (bf16[128,1024]{1,0:T(8,128)(2,1)}, bf16[128,1024]{1,0:T(8,128)(2,1)S(1)}, u32[]{:S(2)}, u32[]{:S(2)}) collective-permute-start(bf16[128,1024]{1,0:T(8,128)(2,1)} %get-tuple-element.38), channel_id=1, source_target_pairs={{0,4},{1,5},{2,6},{3,7},{4,0},{5,1},{6,2},{7,3},{8,12},{9,13},{10,... | collective-permute-start | bytes 786440 | tf_op jit(solution)/shard_map/ppermute | solution.py:24
  5.5 1.6 %collective-permute-start = (bf16[128,1024]{1,0:T(8,128)(2,1)}, bf16[128,1024]{1,0:T(8,128)(2,1)S(1)}, u32[]{:S(2)}, u32[]{:S(2)}) collective-permute-start(bf16[128,1024]{1,0:T(8,128)(2,1)} %bitcast.64), channel_id=1, source_target_pairs={{0,8},{8,0},{16,24},{24,16},{1,9},{9,1},{17,25},{25,17},{2,10},{10... | collective-permute-start | bytes 786440 | tf_op jit(solution)/shard_map/ppermute | solution.py:24
  7.1 1.5 %collective-permute-start.1 = (bf16[128,1024]{1,0:T(8,128)(2,1)}, bf16[128,1024]{1,0:T(8,128)(2,1)S(1)}, u32[]{:S(2)}, u32[]{:S(2)}) collective-permute-start(bf16[128,1024]{1,0:T(8,128)(2,1)} %get-tuple-element.39), channel_id=1, source_target_pairs={{0,2},{1,3},{2,0},{3,1},{4,6},{5,7},{6,4},{7,5},{8,10},{9,11},{10,... | collective-permute-start | bytes 786440 | tf_op jit(solution)/shard_map/ppermute | solution.py:24
  8.6 0.7 and_compare_fusion.1
  9.4 0.1 broadcast_in_dim.34
  9.4 2.6 %collective-permute-done.2.refs_4_ = bf16[128,1024]{1,0:T(8,128)(2,1)S(1)} collective-permute-done((bf16[128,1024]{1,0:T(8,128)(2,1)}, bf16[128,1024]{1,0:T(8,128)(2,1)S(1)}, u32[]{:S(2)}, u32[]{:S(2)}) %collective-permute-start.2) | collective-permute-done | bytes 262176 | tf_op jit(solution)/shard_map/ppermute | solution.py:24
  12.1 1.7 %collective-permute-start.5 = (bf16[128,1024]{1,0:T(8,128)(2,1)}, bf16[128,1024]{1,0:T(8,128)(2,1)S(1)}, u32[]{:S(2)}, u32[]{:S(2)}) collective-permute-start(bf16[128,1024]{1,0:T(8,128)(2,1)} %get-tuple-element.39), channel_id=1, source_target_pairs={{0,4},{1,5},{2,6},{3,7},{4,0},{5,1},{6,2},{7,3},{8,12},{9,13},{10,... | collective-permute-start | bytes 786440 | tf_op jit(solution)/shard_map/ppermute | solution.py:24
  13.8 1.0 broadcast_select_fusion
  14.9 2.7 %collective-permute-start.3 = (bf16[128,1024]{1,0:T(8,128)(2,1)S(1)}, bf16[128,1024]{1,0:T(8,128)(2,1)}, u32[]{:S(2)}, u32[]{:S(2)}) collective-permute-start(bf16[128,1024]{1,0:T(8,128)(2,1)S(1)} %broadcast_select_fusion), channel_id=1, source_target_pairs={{0,16},{8,24},{16,0},{24,8},{1,17},{9,25},{17,1},{25,9},{2,18},{10... | collective-permute-start | bytes 786440 | tf_op jit(solution)/shard_map/ppermute | solution.py:24
  17.5 1.5 %collective-permute-start.4 = (bf16[128,1024]{1,0:T(8,128)(2,1)}, bf16[128,1024]{1,0:T(8,128)(2,1)S(1)}, u32[]{:S(2)}, u32[]{:S(2)}) collective-permute-start(bf16[128,1024]{1,0:T(8,128)(2,1)} %get-tuple-element.38), channel_id=1, source_target_pairs={{0,2},{1,3},{2,0},{3,1},{4,6},{5,7},{6,4},{7,5},{8,10},{9,11},{10,... | collective-permute-start | bytes 786440 | tf_op jit(solution)/shard_map/ppermute | solution.py:24
  19.0 0.5 collective-permute-start.7
  19.6 0.5 collective-permute-start.6
  20.2 9.8 %collective-permute-done.7.refs_1_ = bf16[128,1024]{1,0:T(8,128)(2,1)S(1)} collective-permute-done((bf16[128,1024]{1,0:T(8,128)(2,1)S(1)}, bf16[128,1024]{1,0:T(8,128)(2,1)S(1)}, u32[]{:S(2)}, u32[]{:S(2)}) %collective-permute-start.7) | collective-permute-done | bytes 262176 | tf_op jit(solution)/shard_map/ppermute | solution.py:24
  30.0 0.5 collective-permute-start.12
  30.6 0.4 collective-permute-start.13
  31.2 0.1 broadcast_in_dim.31
  31.3 1.1 broadcast_select_fusion.1
  32.4 1.5 %collective-permute-start.10 = (bf16[128,1024]{1,0:T(8,128)(2,1)S(1)}, bf16[128,1024]{1,0:T(8,128)(2,1)S(1)}, u32[]{:S(2)}, u32[]{:S(2)}) collective-permute-start(bf16[128,1024]{1,0:T(8,128)(2,1)S(1)} %broadcast_select_fusion.1), channel_id=1, source_target_pairs={{0,6},{1,7},{2,4},{3,5},{4,2},{5,3},{6,0},{7,1},{8,14},{9,15},{10,... | collective-permute-start | bytes 786440 | tf_op jit(solution)/shard_map/ppermute | solution.py:24
  33.9 1.5 %collective-permute-start.9 = (bf16[128,1024]{1,0:T(8,128)(2,1)S(1)}, bf16[128,1024]{1,0:T(8,128)(2,1)S(1)}, u32[]{:S(2)}, u32[]{:S(2)}) collective-permute-start(bf16[128,1024]{1,0:T(8,128)(2,1)S(1)} %broadcast_select_fusion.1), channel_id=1, source_target_pairs={{0,4},{1,5},{2,6},{3,7},{4,0},{5,1},{6,2},{7,3},{8,12},{9,13},{10,... | collective-permute-start | bytes 786440 | tf_op jit(solution)/shard_map/ppermute | solution.py:24
  35.5 0.5 collective-permute-start.8
  36.0 2.2 %copy-done = bf16[2048,1024]{1,0:T(8,128)(2,1)S(1)} copy-done((bf16[2048,1024]{1,0:T(8,128)(2,1)S(1)}, bf16[2048,1024]{1,0:T(8,128)(2,1)}, u32[]{:S(2)}) %copy-start) | copy-done | bytes 4194328
  38.2 5.8 %shard_map.85.refs_5_ = f32[1024,1024]{1,0:T(8,128)S(1)} custom-call(s32[2]{0:T(128)S(1)} %pad_add_fusion.here, bf16[256,1024]{1,0:T(8,128)(2,1)S(1)} %slice_bitcast_fusion.refs_0_, bf16[128,1024]{1,0:T(8,128)(2,1)S(1)} %collective-permute-done.1.refs_1_, bf16[128,1024]{1,0:T(8,128)(2,1)S(1)} %collective-permute-done.4.refs_2_, ...), custom_call_target="tpu_custom_call" | custom-call | flops 3221225472 | bytes 10485760 | tf_op jit(solution)/shard_map/pallas_call | solution.py:209
  44.0 3.3 %collective-permute-done.9 = bf16[128,1024]{1,0:T(8,128)(2,1)S(1)} collective-permute-done((bf16[128,1024]{1,0:T(8,128)(2,1)S(1)}, bf16[128,1024]{1,0:T(8,128)(2,1)S(1)}, u32[]{:S(2)}, u32[]{:S(2)}) %collective-permute-start.9) | collective-permute-done | bytes 262176 | tf_op jit(solution)/shard_map/ppermute | solution.py:24
  47.5 0.5 collective-permute-start.18
  48.0 2.1 %collective-permute-done.16.other = bf16[512,1024]{1,0:T(8,128)(2,1)S(1)} collective-permute-done((bf16[512,1024]{1,0:T(8,128)(2,1)S(1)}, bf16[512,1024]{1,0:T(8,128)(2,1)S(1)}, u32[]{:S(2)}, u32[]{:S(2)}) %collective-permute-start.16) | collective-permute-done | bytes 1048608 | tf_op jit(solution)/shard_map/ppermute | solution.py:24
  50.1 0.8 shard_map.86
  50.9 0.5 fusion.2.refs_0_
  51.4 1.6 %collective-permute-start.26 = (bf16[256,512]{1,0:T(8,128)(2,1)S(1)}, bf16[256,512]{1,0:T(8,128)(2,1)S(1)}, u32[]{:S(2)}, u32[]{:S(2)}) collective-permute-start(bf16[256,512]{1,0:T(8,128)(2,1)S(1)} %fusion.2.refs_0_), channel_id=1, source_target_pairs={{0,6},{1,7},{2,4},{3,5},{4,2},{5,3},{6,0},{7,1},{8,14},{9,15},{10,... | collective-permute-start | bytes 786440 | tf_op jit(solution)/shard_map/ppermute | solution.py:24
  53.0 0.7 collective-permute-start.25
  53.7 1.2 collective-permute-start.24
  55.0 2.4 %shard_map.87 = (bf16[1024,1024]{1,0:T(8,128)(2,1)S(1)}, bf16[128,1024]{1,0:T(8,128)(2,1)S(1)}, bf16[128,1024]{1,0:T(8,128)(2,1)S(1)}) custom-call(s32[2]{0:T(128)S(1)} %pad_add_fusion.here, bf16[128,1024]{1,0:T(8,128)(2,1)S(1)} %collective-permute-done.6.refs_0_, bf16[128,1024]{1,0:T(8,128)(2,1)S(1)} %collective-permute-done.7.refs_1_, ...), custom_call_target="tpu_custom_call" | custom-call | flops 1610612736 | bytes 13107200 | tf_op jit(solution)/shard_map/pallas_call | solution.py:131
  57.4 1.7 %collective-permute-start.20 = (bf16[128,1024]{1,0:T(8,128)(2,1)S(1)}, bf16[128,1024]{1,0:T(8,128)(2,1)S(1)}, u32[]{:S(2)}, u32[]{:S(2)}) collective-permute-start(bf16[128,1024]{1,0:T(8,128)(2,1)S(1)} %get-tuple-element.56), channel_id=1, source_target_pairs={{0,8},{8,0},{16,24},{24,16},{1,9},{9,1},{17,25},{25,17},{2,10},{10... | collective-permute-start | bytes 786440 | tf_op jit(solution)/shard_map/ppermute | solution.py:24
  59.0 1.2 shard_map.88
  60.3 1.3 collective-permute-done.26.refs_3_
  61.6 1.6 %collective-permute-start.19 = (bf16[128,1024]{1,0:T(8,128)(2,1)S(1)}, bf16[128,1024]{1,0:T(8,128)(2,1)S(1)}, u32[]{:S(2)}, u32[]{:S(2)}) collective-permute-start(bf16[128,1024]{1,0:T(8,128)(2,1)S(1)} %get-tuple-element.54), channel_id=1, source_target_pairs={{0,8},{8,0},{16,24},{24,16},{1,9},{9,1},{17,25},{25,17},{2,10},{10... | collective-permute-start | bytes 786440 | tf_op jit(solution)/shard_map/ppermute | solution.py:24
  63.1 3.2 %collective-permute-done.25.refs_2_ = bf16[256,512]{1,0:T(8,128)(2,1)S(1)} collective-permute-done((bf16[256,512]{1,0:T(8,128)(2,1)S(1)}, bf16[256,512]{1,0:T(8,128)(2,1)S(1)}, u32[]{:S(2)}, u32[]{:S(2)}) %collective-permute-start.25) | collective-permute-done | bytes 262176 | tf_op jit(solution)/shard_map/ppermute | solution.py:24
  66.3 0.5 collective-permute-start.29
  67.0 0.4 collective-permute-start.21
  67.4 0.4 collective-permute-done.30.refs_7_
  67.8 0.4 collective-permute-done.29.refs_6_
  68.2 0.4 collective-permute-done.28.refs_5_
  68.6 1.8 %shard_map.90 = (bf16[128,1024]{1,0:T(8,128)(2,1)S(1)}, bf16[128,1024]{1,0:T(8,128)(2,1)S(1)}) custom-call(s32[2]{0:T(128)S(1)} %pad_add_fusion.here, bf16[256,512]{1,0:T(8,128)(2,1)S(1)} %fusion.2.refs_0_, bf16[256,512]{1,0:T(8,128)(2,1)S(1)} %collective-permute-done.24.refs_1_, bf16[256,512]{1,0:T(8,128)(2,1)S(1)} %collective-permute-done.25.refs_2_, ...), custom_call_target="tpu_custom_call" | custom-call | flops 1073741824 | bytes 6815744 | tf_op jit(solution)/shard_map/pallas_call | solution.py:131
  70.4 1.6 %collective-permute-start.31 = (bf16[128,1024]{1,0:T(8,128)(2,1)S(1)}, bf16[128,1024]{1,0:T(8,128)(2,1)S(1)}, u32[]{:S(2)}, u32[]{:S(2)}) collective-permute-start(bf16[128,1024]{1,0:T(8,128)(2,1)S(1)} %get-tuple-element.60), channel_id=1, source_target_pairs={{0,8},{8,0},{16,24},{24,16},{1,9},{9,1},{17,25},{25,17},{2,10},{10... | collective-permute-start | bytes 786440 | tf_op jit(solution)/shard_map/ppermute | solution.py:24
  72.1 10.3 %collective-permute-done.21 = bf16[128,1024]{1,0:T(8,128)(2,1)S(1)} collective-permute-done((bf16[128,1024]{1,0:T(8,128)(2,1)S(1)}, bf16[128,1024]{1,0:T(8,128)(2,1)S(1)}, u32[]{:S(2)}, u32[]{:S(2)}) %collective-permute-start.21) | collective-permute-done | bytes 262176 | tf_op jit(solution)/shard_map/ppermute | solution.py:24
  82.3 1.1 fusion.38
  83.5 2.2 %collective-permute-start.22 = (bf16[128,1024]{1,0:T(8,128)(2,1)}, bf16[128,1024]{1,0:T(8,128)(2,1)}, u32[]{:S(2)}, u32[]{:S(2)}) collective-permute-start(bf16[128,1024]{1,0:T(8,128)(2,1)} %get-tuple-element.57), channel_id=1, source_target_pairs={{0,16},{8,24},{16,0},{24,8},{1,17},{9,25},{17,1},{25,9},{2,18},{10... | collective-permute-start | bytes 786440 | tf_op jit(solution)/shard_map/ppermute | solution.py:24
  85.6 1.8 %shard_map.89 = (f32[128,1024]{1,0:T(8,128)S(1)}, f32[128,1024]{1,0:T(8,128)S(1)}) custom-call(s32[2]{0:T(128)S(1)} %pad_add_fusion.here, bf16[256,512]{1,0:T(8,128)(2,1)S(1)} %fusion.2.refs_0_, bf16[256,512]{1,0:T(8,128)(2,1)S(1)} %collective-permute-done.24.refs_1_, bf16[256,512]{1,0:T(8,128)(2,1)S(1)} %collective-permute-done.25.refs_2_, ...), custom_call_target="tpu_custom_call" | custom-call | flops 1073741824 | bytes 7340032 | tf_op jit(solution)/shard_map/pallas_call | solution.py:131
  87.5 0.8 add_convert_fusion
  88.2 0.7 collective-permute-start.32
  89.0 2.0 %collective-permute-start.34 = (bf16[128,1024]{1,0:T(8,128)(2,1)S(1)}, bf16[128,1024]{1,0:T(8,128)(2,1)}, u32[]{:S(2)}, u32[]{:S(2)}) collective-permute-start(bf16[128,1024]{1,0:T(8,128)(2,1)S(1)} %get-tuple-element.64), channel_id=1, source_target_pairs={{0,8},{8,0},{16,24},{24,16},{1,9},{9,1},{17,25},{25,17},{2,10},{10... | collective-permute-start | bytes 786440 | tf_op jit(solution)/shard_map/ppermute | solution.py:24
  91.0 14.2 %collective-permute-done.22 = bf16[128,1024]{1,0:T(8,128)(2,1)} collective-permute-done((bf16[128,1024]{1,0:T(8,128)(2,1)}, bf16[128,1024]{1,0:T(8,128)(2,1)}, u32[]{:S(2)}, u32[]{:S(2)}) %collective-permute-start.22) | collective-permute-done | bytes 262176 | tf_op jit(solution)/shard_map/ppermute | solution.py:24
  105.3 4.2 %collective-permute-done.32 = bf16[128,1024]{1,0:T(8,128)(2,1)} collective-permute-done((bf16[128,1024]{1,0:T(8,128)(2,1)}, bf16[128,1024]{1,0:T(8,128)(2,1)}, u32[]{:S(2)}, u32[]{:S(2)}) %collective-permute-start.32) | collective-permute-done | bytes 262176 | tf_op jit(solution)/shard_map/ppermute | solution.py:24
  109.5 1.6 %fusion.37 = (bf16[128,1024]{1,0:T(8,128)(2,1)S(1)}, f32[128,1024]{1,0:T(8,128)S(1)}) fusion(bf16[128,1024]{1,0:T(8,128)(2,1)} %collective-permute-done.32, f32[2,128,1024]{2,1,0:T(8,128)S(1)} %copy-done.3, f32[2,128,1024]{2,1,0:T(8,128)} %param.10, f32[128,1024]{1,0:T(8,128)S(1)} %get-tuple-element.63, bf16[128,1024]{1,0:T(8,128)(2,1)} %collective-permute-done.34), kind=kLoop, calls=%fused_computation.63 | loop fusion | flops 2097152 | bytes 2883584 | tf_op jit(solution)/shard_map/convert_element_type | solution.py:366
  111.1 0.4 collective-permute-start.37
  111.5 2.0 %collective-permute-start.35 = (bf16[128,1024]{1,0:T(8,128)(2,1)S(1)}, bf16[128,1024]{1,0:T(8,128)(2,1)S(1)}, u32[]{:S(2)}, u32[]{:S(2)}) collective-permute-start(bf16[128,1024]{1,0:T(8,128)(2,1)S(1)} %get-tuple-element.66), channel_id=1, source_target_pairs={{0,16},{8,24},{16,0},{24,8},{1,17},{9,25},{17,1},{25,9},{2,18},{10... | collective-permute-start | bytes 786440 | tf_op jit(solution)/shard_map/ppermute | solution.py:24
  113.5 1.4 %fusion.35 = (f32[1,128,1024]{2,1,0:T(8,128)S(1)}, f32[1,128,1024]{2,1,0:T(8,128)S(1)}, f32[1,128,1024]{2,1,0:T(8,128)S(1)}, f32[1,128,1024]{2,1,0:T(8,128)S(1)}) fusion(f32[2,128,1024]{2,1,0:T(8,128)S(1)} %copy-done.3, f32[128,1024]{1,0:T(8,128)S(1)} %get-tuple-element.67, bf16[128,1024]{1,0:T(8,128)(2,1)S(1)} %copy-done.9, ...), kind=kLoop, calls=%fused_computation.50 | loop fusion | flops 2359296 | bytes 5767168 | tf_op jit(solution)/shard_map/stack | solution.py:384
  115.0 8.1 %collective-permute-done.35 = bf16[128,1024]{1,0:T(8,128)(2,1)S(1)} collective-permute-done((bf16[128,1024]{1,0:T(8,128)(2,1)S(1)}, bf16[128,1024]{1,0:T(8,128)(2,1)S(1)}, u32[]{:S(2)}, u32[]{:S(2)}) %collective-permute-start.35) | collective-permute-done | bytes 262176 | tf_op jit(solution)/shard_map/ppermute | solution.py:24
  123.0 2.8 %collective-permute-start.36 = (bf16[128,1024]{1,0:T(8,128)(2,1)S(1)}, bf16[128,1024]{1,0:T(8,128)(2,1)S(1)}, u32[]{:S(2)}, u32[]{:S(2)}) collective-permute-start(bf16[128,1024]{1,0:T(8,128)(2,1)S(1)} %collective-permute-done.35), channel_id=1, source_target_pairs={{0,8},{8,0},{16,24},{24,16},{1,9},{9,1},{17,25},{25,17},{2,10},{10... | collective-permute-start | bytes 786440 | tf_op jit(solution)/shard_map/ppermute | solution.py:24
  125.9 1.6 %fusion = bf16[1,256,1024]{2,1,0:T(8,128)(2,1)S(1)} fusion(bf16[128,1024]{1,0:T(8,128)(2,1)} %get-tuple-element.57, bf16[128,1024]{1,0:T(8,128)(2,1)} %collective-permute-done.22, bf16[128,1024]{1,0:T(8,128)(2,1)} %collective-permute-done.33, bf16[128,1024]{1,0:T(8,128)(2,1)S(1)} %collective-permute-done.23, ...), kind=kOutput, calls=%fused_computation.2 | convolution fusion | flops 272891904 | bytes 1835012 | tf_op jit(solution)/shard_map/dot_general | solution.py:377
  127.5 1.5 %pad_maximum_fusion.2 = (f32[2,128,1024]{2,1,0:T(8,128)}, f32[2,128,1024]{2,1,0:T(8,128)}) fusion(f32[1,128,1024]{2,1,0:T(8,128)S(1)} %get-tuple-element.78, f32[1,128,1024]{2,1,0:T(8,128)S(1)} %get-tuple-element.77, f32[1,128,1024]{2,1,0:T(8,128)S(1)} %get-tuple-element.79, f32[1,128,1024]{2,1,0:T(8,128)S(1)} %get-tuple-element.80), kind=kLoop, calls=%fused_computation.22 | loop fusion | flops 524288 | bytes 4194304 | tf_op jit(solution)/shard_map/stack | solution.py:384
  128.9 2.6 %collective-permute-done.36 = bf16[128,1024]{1,0:T(8,128)(2,1)S(1)} collective-permute-done((bf16[128,1024]{1,0:T(8,128)(2,1)S(1)}, bf16[128,1024]{1,0:T(8,128)(2,1)S(1)}, u32[]{:S(2)}, u32[]{:S(2)}) %collective-permute-start.36) | collective-permute-done | bytes 262176 | tf_op jit(solution)/shard_map/ppermute | solution.py:24
  131.6 1.4 %fusion.1 = bf16[1,256,1024]{2,1,0:T(8,128)(2,1)S(1)} fusion(bf16[128,1024]{1,0:T(8,128)(2,1)S(1)} %get-tuple-element.66, bf16[128,1024]{1,0:T(8,128)(2,1)S(1)} %collective-permute-done.35, bf16[128,1024]{1,0:T(8,128)(2,1)S(1)} %collective-permute-done.37, bf16[128,1024]{1,0:T(8,128)(2,1)S(1)} %collective-permute-done.36, bf16[512,1024]{1,0:T(8,128)(2,1)} %copy-done.2, ...), kind=kOutput, calls=%fused_computation.3 | convolution fusion | flops 272891904 | bytes 1835012 | tf_op jit(solution)/shard_map/dot_general | solution.py:377
  133.0 1.1 pad_maximum_fusion.1
  (68 shorter events, 0.9 us)
Async XLA Ops:
  0.6 19.5 %copy-start.6 = (bf16[2,256,1024]{2,1,0:T(8,128)(2,1)S(1)}, bf16[2,256,1024]{2,1,0:T(8,128)(2,1)}, u32[]{:S(2)}) copy-start(bf16[2,256,1024]{2,1,0:T(8,128)(2,1)} %param.7) | copy-start | bytes 3145732
  2.6 9.5 %collective-permute-start.2 = (bf16[128,1024]{1,0:T(8,128)(2,1)}, bf16[128,1024]{1,0:T(8,128)(2,1)S(1)}, u32[]{:S(2)}, u32[]{:S(2)}) collective-permute-start(bf16[128,1024]{1,0:T(8,128)(2,1)} %get-tuple-element.38), channel_id=1, source_target_pairs={{0,4},{1,5},{2,6},{3,7},{4,0},{5,1},{6,2},{7,3},{8,12},{9,13},{10,... | collective-permute-start | bytes 786440 | tf_op jit(solution)/shard_map/ppermute | solution.py:24
  5.5 8.3 %collective-permute-start = (bf16[128,1024]{1,0:T(8,128)(2,1)}, bf16[128,1024]{1,0:T(8,128)(2,1)S(1)}, u32[]{:S(2)}, u32[]{:S(2)}) collective-permute-start(bf16[128,1024]{1,0:T(8,128)(2,1)} %bitcast.64), channel_id=1, source_target_pairs={{0,8},{8,0},{16,24},{24,16},{1,9},{9,1},{17,25},{25,17},{2,10},{10... | collective-permute-start | bytes 786440 | tf_op jit(solution)/shard_map/ppermute | solution.py:24
  7.1 7.7 %collective-permute-start.1 = (bf16[128,1024]{1,0:T(8,128)(2,1)}, bf16[128,1024]{1,0:T(8,128)(2,1)S(1)}, u32[]{:S(2)}, u32[]{:S(2)}) collective-permute-start(bf16[128,1024]{1,0:T(8,128)(2,1)} %get-tuple-element.39), channel_id=1, source_target_pairs={{0,2},{1,3},{2,0},{3,1},{4,6},{5,7},{6,4},{7,5},{8,10},{9,11},{10,... | collective-permute-start | bytes 786440 | tf_op jit(solution)/shard_map/ppermute | solution.py:24
  12.1 8.1 %collective-permute-start.5 = (bf16[128,1024]{1,0:T(8,128)(2,1)}, bf16[128,1024]{1,0:T(8,128)(2,1)S(1)}, u32[]{:S(2)}, u32[]{:S(2)}) collective-permute-start(bf16[128,1024]{1,0:T(8,128)(2,1)} %get-tuple-element.39), channel_id=1, source_target_pairs={{0,4},{1,5},{2,6},{3,7},{4,0},{5,1},{6,2},{7,3},{8,12},{9,13},{10,... | collective-permute-start | bytes 786440 | tf_op jit(solution)/shard_map/ppermute | solution.py:24
  14.9 15.6 %copy-start.10 = (bf16[128,1024]{1,0:T(8,128)(2,1)}, bf16[128,1024]{1,0:T(8,128)(2,1)S(1)}, u32[]{:S(2)}) copy-start(bf16[128,1024]{1,0:T(8,128)(2,1)S(1)} %broadcast_select_fusion) | copy-start | bytes 786436
  14.9 15.1 %collective-permute-start.3 = (bf16[128,1024]{1,0:T(8,128)(2,1)S(1)}, bf16[128,1024]{1,0:T(8,128)(2,1)}, u32[]{:S(2)}, u32[]{:S(2)}) collective-permute-start(bf16[128,1024]{1,0:T(8,128)(2,1)S(1)} %broadcast_select_fusion), channel_id=1, source_target_pairs={{0,16},{8,24},{16,0},{24,8},{1,17},{9,25},{17,1},{25,9},{2,18},{10... | collective-permute-start | bytes 786440 | tf_op jit(solution)/shard_map/ppermute | solution.py:24
  17.5 13.0 %collective-permute-start.4 = (bf16[128,1024]{1,0:T(8,128)(2,1)}, bf16[128,1024]{1,0:T(8,128)(2,1)S(1)}, u32[]{:S(2)}, u32[]{:S(2)}) collective-permute-start(bf16[128,1024]{1,0:T(8,128)(2,1)} %get-tuple-element.38), channel_id=1, source_target_pairs={{0,2},{1,3},{2,0},{3,1},{4,6},{5,7},{6,4},{7,5},{8,10},{9,11},{10,... | collective-permute-start | bytes 786440 | tf_op jit(solution)/shard_map/ppermute | solution.py:24
  19.0 11.0 %collective-permute-start.7 = (bf16[128,1024]{1,0:T(8,128)(2,1)S(1)}, bf16[128,1024]{1,0:T(8,128)(2,1)S(1)}, u32[]{:S(2)}, u32[]{:S(2)}) collective-permute-start(bf16[128,1024]{1,0:T(8,128)(2,1)S(1)} %collective-permute-done.2.refs_4_), channel_id=1, source_target_pairs={{0,2},{1,3},{2,0},{3,1},{4,6},{5,7},{6,4},{7,5},{8,10},{9,11},{10,... | collective-permute-start | bytes 786440 | tf_op jit(solution)/shard_map/ppermute | solution.py:24
  19.6 11.0 %collective-permute-start.6 = (bf16[128,1024]{1,0:T(8,128)(2,1)S(1)}, bf16[128,1024]{1,0:T(8,128)(2,1)S(1)}, u32[]{:S(2)}, u32[]{:S(2)}) collective-permute-start(bf16[128,1024]{1,0:T(8,128)(2,1)S(1)} %collective-permute-done.1.refs_1_), channel_id=1, source_target_pairs={{0,4},{1,5},{2,6},{3,7},{4,0},{5,1},{6,2},{7,3},{8,12},{9,13},{10,... | collective-permute-start | bytes 786440 | tf_op jit(solution)/shard_map/ppermute | solution.py:24
  20.1 15.3 %collective-permute-start.11 = (bf16[256,1024]{1,0:T(8,128)(2,1)S(1)}, bf16[256,1024]{1,0:T(8,128)(2,1)S(1)}, u32[]{:S(2)}, u32[]{:S(2)}) collective-permute-start(bf16[256,1024]{1,0:T(8,128)(2,1)S(1)} %slice_bitcast_fusion.refs_0_), channel_id=1, source_target_pairs={{0,1},{1,0},{2,3},{3,2},{4,5},{5,4},{6,7},{7,6},{8,9},{9,8},{10,11... | collective-permute-start | bytes 1572872 | tf_op jit(solution)/shard_map/ppermute | solution.py:24
  30.0 2.4 %collective-permute-start.15 = (bf16[128,1024]{1,0:T(8,128)(2,1)S(1)}, bf16[128,1024]{1,0:T(8,128)(2,1)S(1)}, u32[]{:S(2)}, u32[]{:S(2)}) collective-permute-start(bf16[128,1024]{1,0:T(8,128)(2,1)S(1)} %collective-permute-done.2.refs_4_), channel_id=1, source_target_pairs={{0,1},{1,0},{2,3},{3,2},{4,5},{5,4},{6,7},{7,6},{8,9},{9,8},{10,11... | collective-permute-start | bytes 786440 | tf_op jit(solution)/shard_map/ppermute | solution.py:24
  30.0 3.9 %collective-permute-start.12 = (bf16[128,1024]{1,0:T(8,128)(2,1)S(1)}, bf16[128,1024]{1,0:T(8,128)(2,1)S(1)}, u32[]{:S(2)}, u32[]{:S(2)}) collective-permute-start(bf16[128,1024]{1,0:T(8,128)(2,1)S(1)} %collective-permute-done.1.refs_1_), channel_id=1, source_target_pairs={{0,1},{1,0},{2,3},{3,2},{4,5},{5,4},{6,7},{7,6},{8,9},{9,8},{10,11... | collective-permute-start | bytes 786440 | tf_op jit(solution)/shard_map/ppermute | solution.py:24
  30.5 5.5 %collective-permute-start.14 = (bf16[128,1024]{1,0:T(8,128)(2,1)S(1)}, bf16[128,1024]{1,0:T(8,128)(2,1)S(1)}, u32[]{:S(2)}, u32[]{:S(2)}) collective-permute-start(bf16[128,1024]{1,0:T(8,128)(2,1)S(1)} %collective-permute-done.5.refs_3_), channel_id=1, source_target_pairs={{0,1},{1,0},{2,3},{3,2},{4,5},{5,4},{6,7},{7,6},{8,9},{9,8},{10,11... | collective-permute-start | bytes 786440 | tf_op jit(solution)/shard_map/ppermute | solution.py:24
  30.6 5.4 %collective-permute-start.13 = (bf16[128,1024]{1,0:T(8,128)(2,1)S(1)}, bf16[128,1024]{1,0:T(8,128)(2,1)}, u32[]{:S(2)}, u32[]{:S(2)}) collective-permute-start(bf16[128,1024]{1,0:T(8,128)(2,1)S(1)} %collective-permute-done.4.refs_2_), channel_id=1, source_target_pairs={{0,1},{1,0},{2,3},{3,2},{4,5},{5,4},{6,7},{7,6},{8,9},{9,8},{10,11... | collective-permute-start | bytes 786440 | tf_op jit(solution)/shard_map/ppermute | solution.py:24
  32.4 11.6 %collective-permute-start.10 = (bf16[128,1024]{1,0:T(8,128)(2,1)S(1)}, bf16[128,1024]{1,0:T(8,128)(2,1)S(1)}, u32[]{:S(2)}, u32[]{:S(2)}) collective-permute-start(bf16[128,1024]{1,0:T(8,128)(2,1)S(1)} %broadcast_select_fusion.1), channel_id=1, source_target_pairs={{0,6},{1,7},{2,4},{3,5},{4,2},{5,3},{6,0},{7,1},{8,14},{9,15},{10,... | collective-permute-start | bytes 786440 | tf_op jit(solution)/shard_map/ppermute | solution.py:24
  33.9 13.4 %collective-permute-start.9 = (bf16[128,1024]{1,0:T(8,128)(2,1)S(1)}, bf16[128,1024]{1,0:T(8,128)(2,1)S(1)}, u32[]{:S(2)}, u32[]{:S(2)}) collective-permute-start(bf16[128,1024]{1,0:T(8,128)(2,1)S(1)} %broadcast_select_fusion.1), channel_id=1, source_target_pairs={{0,4},{1,5},{2,6},{3,7},{4,0},{5,1},{6,2},{7,3},{8,12},{9,13},{10,... | collective-permute-start | bytes 786440 | tf_op jit(solution)/shard_map/ppermute | solution.py:24
  35.5 11.8 %collective-permute-start.8 = (bf16[128,1024]{1,0:T(8,128)(2,1)S(1)}, bf16[128,1024]{1,0:T(8,128)(2,1)S(1)}, u32[]{:S(2)}, u32[]{:S(2)}) collective-permute-start(bf16[128,1024]{1,0:T(8,128)(2,1)S(1)} %broadcast_select_fusion.1), channel_id=1, source_target_pairs={{0,2},{1,3},{2,0},{3,1},{4,6},{5,7},{6,4},{7,5},{8,10},{9,11},{10,... | collective-permute-start | bytes 786440 | tf_op jit(solution)/shard_map/ppermute | solution.py:24
  36.0 2.2 %copy-start = (bf16[2048,1024]{1,0:T(8,128)(2,1)S(1)}, bf16[2048,1024]{1,0:T(8,128)(2,1)}, u32[]{:S(2)}) copy-start(bf16[2048,1024]{1,0:T(8,128)(2,1)} %refs_8_.3) | copy-start | bytes 12582916
  44.0 6.9 %copy-start.7 = (bf16[2,256,1024]{2,1,0:T(8,128)(2,1)S(1)}, bf16[2,256,1024]{2,1,0:T(8,128)(2,1)}, u32[]{:S(2)}) copy-start(bf16[2,256,1024]{2,1,0:T(8,128)(2,1)} %param.7) | copy-start | bytes 3145732
  47.4 7.6 %copy-start.1 = (bf16[2048,1024]{1,0:T(8,128)(2,1)S(1)}, bf16[2048,1024]{1,0:T(8,128)(2,1)}, u32[]{:S(2)}) copy-start(bf16[2048,1024]{1,0:T(8,128)(2,1)} %refs_8_.3) | copy-start | bytes 12582916
  47.4 2.7 %collective-permute-start.16 = (bf16[512,1024]{1,0:T(8,128)(2,1)S(1)}, bf16[512,1024]{1,0:T(8,128)(2,1)S(1)}, u32[]{:S(2)}, u32[]{:S(2)}) collective-permute-start(bf16[512,1024]{1,0:T(8,128)(2,1)S(1)} %pad_maximum_fusion.same), channel_id=1, source_target_pairs={{0,1},{1,0},{2,3},{3,2},{4,5},{5,4},{6,7},{7,6},{8,9},{9,8},{10,11... | collective-permute-start | bytes 3145736 | tf_op jit(solution)/shard_map/ppermute | solution.py:24
  47.5 7.5 %collective-permute-start.18 = (bf16[128,1024]{1,0:T(8,128)(2,1)S(1)}, bf16[128,1024]{1,0:T(8,128)(2,1)S(1)}, u32[]{:S(2)}, u32[]{:S(2)}) collective-permute-start(bf16[128,1024]{1,0:T(8,128)(2,1)S(1)} %collective-permute-done.7.refs_1_), channel_id=1, source_target_pairs={{0,1},{1,0},{2,3},{3,2},{4,5},{5,4},{6,7},{7,6},{8,9},{9,8},{10,11... | collective-permute-start | bytes 786440 | tf_op jit(solution)/shard_map/ppermute | solution.py:24
  48.0 7.0 %collective-permute-start.17 = (bf16[128,1024]{1,0:T(8,128)(2,1)S(1)}, bf16[128,1024]{1,0:T(8,128)(2,1)S(1)}, u32[]{:S(2)}, u32[]{:S(2)}) collective-permute-start(bf16[128,1024]{1,0:T(8,128)(2,1)S(1)} %collective-permute-done.6.refs_0_), channel_id=1, source_target_pairs={{0,1},{1,0},{2,3},{3,2},{4,5},{5,4},{6,7},{7,6},{8,9},{9,8},{10,11... | collective-permute-start | bytes 786440 | tf_op jit(solution)/shard_map/ppermute | solution.py:24
  50.9 6.5 %copy-start.2 = (bf16[512,1024]{1,0:T(8,128)(2,1)}, bf16[512,1024]{1,0:T(8,128)(2,1)S(1)}, u32[]{:S(2)}) copy-start(bf16[512,1024]{1,0:T(8,128)(2,1)S(1)} %get-tuple-element.58) | copy-start | bytes 3145732
  51.4 10.2 %collective-permute-start.26 = (bf16[256,512]{1,0:T(8,128)(2,1)S(1)}, bf16[256,512]{1,0:T(8,128)(2,1)S(1)}, u32[]{:S(2)}, u32[]{:S(2)}) collective-permute-start(bf16[256,512]{1,0:T(8,128)(2,1)S(1)} %fusion.2.refs_0_), channel_id=1, source_target_pairs={{0,6},{1,7},{2,4},{3,5},{4,2},{5,3},{6,0},{7,1},{8,14},{9,15},{10,... | collective-permute-start | bytes 786440 | tf_op jit(solution)/shard_map/ppermute | solution.py:24
  53.0 13.3 %collective-permute-start.25 = (bf16[256,512]{1,0:T(8,128)(2,1)S(1)}, bf16[256,512]{1,0:T(8,128)(2,1)S(1)}, u32[]{:S(2)}, u32[]{:S(2)}) collective-permute-start(bf16[256,512]{1,0:T(8,128)(2,1)S(1)} %fusion.2.refs_0_), channel_id=1, source_target_pairs={{0,4},{1,5},{2,6},{3,7},{4,0},{5,1},{6,2},{7,3},{8,12},{9,13},{10,... | collective-permute-start | bytes 786440 | tf_op jit(solution)/shard_map/ppermute | solution.py:24
  53.7 12.6 %collective-permute-start.24 = (bf16[256,512]{1,0:T(8,128)(2,1)S(1)}, bf16[256,512]{1,0:T(8,128)(2,1)S(1)}, u32[]{:S(2)}, u32[]{:S(2)}) collective-permute-start(bf16[256,512]{1,0:T(8,128)(2,1)S(1)} %fusion.2.refs_0_), channel_id=1, source_target_pairs={{0,2},{1,3},{2,0},{3,1},{4,6},{5,7},{6,4},{7,5},{8,10},{9,11},{10,... | collective-permute-start | bytes 786440 | tf_op jit(solution)/shard_map/ppermute | solution.py:24
  57.4 9.4 %collective-permute-start.20 = (bf16[128,1024]{1,0:T(8,128)(2,1)S(1)}, bf16[128,1024]{1,0:T(8,128)(2,1)S(1)}, u32[]{:S(2)}, u32[]{:S(2)}) collective-permute-start(bf16[128,1024]{1,0:T(8,128)(2,1)S(1)} %get-tuple-element.56), channel_id=1, source_target_pairs={{0,8},{8,0},{16,24},{24,16},{1,9},{9,1},{17,25},{25,17},{2,10},{10... | collective-permute-start | bytes 786440 | tf_op jit(solution)/shard_map/ppermute | solution.py:24
  59.0 7.9 %collective-permute-start.27 = (bf16[256,512]{1,0:T(8,128)(2,1)S(1)}, bf16[256,512]{1,0:T(8,128)(2,1)S(1)}, u32[]{:S(2)}, u32[]{:S(2)}) collective-permute-start(bf16[256,512]{1,0:T(8,128)(2,1)S(1)} %fusion.2.refs_0_), channel_id=1, source_target_pairs={{0,1},{1,0},{2,3},{3,2},{4,5},{5,4},{6,7},{7,6},{8,9},{9,8},{10,11... | collective-permute-start | bytes 786440 | tf_op jit(solution)/shard_map/ppermute | solution.py:24
  61.6 10.5 %collective-permute-start.19 = (bf16[128,1024]{1,0:T(8,128)(2,1)S(1)}, bf16[128,1024]{1,0:T(8,128)(2,1)S(1)}, u32[]{:S(2)}, u32[]{:S(2)}) collective-permute-start(bf16[128,1024]{1,0:T(8,128)(2,1)S(1)} %get-tuple-element.54), channel_id=1, source_target_pairs={{0,8},{8,0},{16,24},{24,16},{1,9},{9,1},{17,25},{25,17},{2,10},{10... | collective-permute-start | bytes 786440 | tf_op jit(solution)/shard_map/ppermute | solution.py:24
  66.3 1.5 %collective-permute-start.30 = (bf16[256,512]{1,0:T(8,128)(2,1)S(1)}, bf16[256,512]{1,0:T(8,128)(2,1)S(1)}, u32[]{:S(2)}, u32[]{:S(2)}) collective-permute-start(bf16[256,512]{1,0:T(8,128)(2,1)S(1)} %collective-permute-done.26.refs_3_), channel_id=1, source_target_pairs={{0,1},{1,0},{2,3},{3,2},{4,5},{5,4},{6,7},{7,6},{8,9},{9,8},{10,11... | collective-permute-start | bytes 786440 | tf_op jit(solution)/shard_map/ppermute | solution.py:24
  66.3 1.9 %collective-permute-start.29 = (bf16[256,512]{1,0:T(8,128)(2,1)S(1)}, bf16[256,512]{1,0:T(8,128)(2,1)S(1)}, u32[]{:S(2)}, u32[]{:S(2)}) collective-permute-start(bf16[256,512]{1,0:T(8,128)(2,1)S(1)} %collective-permute-done.25.refs_2_), channel_id=1, source_target_pairs={{0,1},{1,0},{2,3},{3,2},{4,5},{5,4},{6,7},{7,6},{8,9},{9,8},{10,11... | collective-permute-start | bytes 786440 | tf_op jit(solution)/shard_map/ppermute | solution.py:24
  66.8 1.8 %collective-permute-start.28 = (bf16[256,512]{1,0:T(8,128)(2,1)S(1)}, bf16[256,512]{1,0:T(8,128)(2,1)S(1)}, u32[]{:S(2)}, u32[]{:S(2)}) collective-permute-start(bf16[256,512]{1,0:T(8,128)(2,1)S(1)} %collective-permute-done.24.refs_1_), channel_id=1, source_target_pairs={{0,1},{1,0},{2,3},{3,2},{4,5},{5,4},{6,7},{7,6},{8,9},{9,8},{10,11... | collective-permute-start | bytes 786440 | tf_op jit(solution)/shard_map/ppermute | solution.py:24
  67.0 15.4 %copy-start.3 = (f32[2,128,1024]{2,1,0:T(8,128)S(1)}, f32[2,128,1024]{2,1,0:T(8,128)}, u32[]{:S(2)}) copy-start(f32[2,128,1024]{2,1,0:T(8,128)} %param.9) | copy-start | bytes 3145732
  67.0 15.4 %copy-start.4 = (f32[2,128,1024]{2,1,0:T(8,128)S(1)}, f32[2,128,1024]{2,1,0:T(8,128)}, u32[]{:S(2)}) copy-start(f32[2,128,1024]{2,1,0:T(8,128)} %param.10) | copy-start | bytes 3145732
  67.0 15.3 %collective-permute-start.21 = (bf16[128,1024]{1,0:T(8,128)(2,1)S(1)}, bf16[128,1024]{1,0:T(8,128)(2,1)S(1)}, u32[]{:S(2)}, u32[]{:S(2)}) collective-permute-start(bf16[128,1024]{1,0:T(8,128)(2,1)S(1)} %add_convert_fusion.1), channel_id=1, source_target_pairs={{0,16},{8,24},{16,0},{24,8},{1,17},{9,25},{17,1},{25,9},{2,18},{10... | collective-permute-start | bytes 786440 | tf_op jit(solution)/shard_map/ppermute | solution.py:24
  70.4 17.1 %collective-permute-start.31 = (bf16[128,1024]{1,0:T(8,128)(2,1)S(1)}, bf16[128,1024]{1,0:T(8,128)(2,1)S(1)}, u32[]{:S(2)}, u32[]{:S(2)}) collective-permute-start(bf16[128,1024]{1,0:T(8,128)(2,1)S(1)} %get-tuple-element.60), channel_id=1, source_target_pairs={{0,8},{8,0},{16,24},{24,16},{1,9},{9,1},{17,25},{25,17},{2,10},{10... | collective-permute-start | bytes 786440 | tf_op jit(solution)/shard_map/ppermute | solution.py:24
  82.3 1.1 copy-start.8
  83.5 21.8 %collective-permute-start.33 = (bf16[128,1024]{1,0:T(8,128)(2,1)}, bf16[128,1024]{1,0:T(8,128)(2,1)}, u32[]{:S(2)}, u32[]{:S(2)}) collective-permute-start(bf16[128,1024]{1,0:T(8,128)(2,1)} %get-tuple-element.57), channel_id=1, source_target_pairs={{0,8},{8,0},{16,24},{24,16},{1,9},{9,1},{17,25},{25,17},{2,10},{10... | collective-permute-start | bytes 786440 | tf_op jit(solution)/shard_map/ppermute | solution.py:24
  83.5 21.8 %collective-permute-start.22 = (bf16[128,1024]{1,0:T(8,128)(2,1)}, bf16[128,1024]{1,0:T(8,128)(2,1)}, u32[]{:S(2)}, u32[]{:S(2)}) collective-permute-start(bf16[128,1024]{1,0:T(8,128)(2,1)} %get-tuple-element.57), channel_id=1, source_target_pairs={{0,16},{8,24},{16,0},{24,8},{1,17},{9,25},{17,1},{25,9},{2,18},{10... | collective-permute-start | bytes 786440 | tf_op jit(solution)/shard_map/ppermute | solution.py:24
  88.2 21.3 %collective-permute-start.32 = (bf16[128,1024]{1,0:T(8,128)(2,1)}, bf16[128,1024]{1,0:T(8,128)(2,1)}, u32[]{:S(2)}, u32[]{:S(2)}) collective-permute-start(bf16[128,1024]{1,0:T(8,128)(2,1)} %add_convert_fusion), channel_id=1, source_target_pairs={{0,16},{8,24},{16,0},{24,8},{1,17},{9,25},{17,1},{25,9},{2,18},{10... | collective-permute-start | bytes 786440 | tf_op jit(solution)/shard_map/ppermute | solution.py:24
  89.0 20.5 %collective-permute-start.34 = (bf16[128,1024]{1,0:T(8,128)(2,1)S(1)}, bf16[128,1024]{1,0:T(8,128)(2,1)}, u32[]{:S(2)}, u32[]{:S(2)}) collective-permute-start(bf16[128,1024]{1,0:T(8,128)(2,1)S(1)} %get-tuple-element.64), channel_id=1, source_target_pairs={{0,8},{8,0},{16,24},{24,16},{1,9},{9,1},{17,25},{25,17},{2,10},{10... | collective-permute-start | bytes 786440 | tf_op jit(solution)/shard_map/ppermute | solution.py:24
  91.0 22.5 %copy-start.5 = (f32[2,128,1024]{2,1,0:T(8,128)S(1)}, f32[2,128,1024]{2,1,0:T(8,128)}, u32[]{:S(2)}) copy-start(f32[2,128,1024]{2,1,0:T(8,128)} %param.10) | copy-start | bytes 3145732
  91.0 22.6 %copy-start.9 = (bf16[128,1024]{1,0:T(8,128)(2,1)S(1)}, bf16[128,1024]{1,0:T(8,128)(2,1)}, u32[]{:S(2)}) copy-start(bf16[128,1024]{1,0:T(8,128)(2,1)} %copy-done.8) | copy-start | bytes 786436
  105.2 20.6 %collective-permute-start.23 = (bf16[128,1024]{1,0:T(8,128)(2,1)}, bf16[128,1024]{1,0:T(8,128)(2,1)S(1)}, u32[]{:S(2)}, u32[]{:S(2)}) collective-permute-start(bf16[128,1024]{1,0:T(8,128)(2,1)} %collective-permute-done.22), channel_id=1, source_target_pairs={{0,8},{8,0},{16,24},{24,16},{1,9},{9,1},{17,25},{25,17},{2,10},{10... | collective-permute-start | bytes 786440 | tf_op jit(solution)/shard_map/ppermute | solution.py:24
  111.1 17.8 %collective-permute-start.37 = (bf16[128,1024]{1,0:T(8,128)(2,1)S(1)}, bf16[128,1024]{1,0:T(8,128)(2,1)S(1)}, u32[]{:S(2)}, u32[]{:S(2)}) collective-permute-start(bf16[128,1024]{1,0:T(8,128)(2,1)S(1)} %get-tuple-element.66), channel_id=1, source_target_pairs={{0,8},{8,0},{16,24},{24,16},{1,9},{9,1},{17,25},{25,17},{2,10},{10... | collective-permute-start | bytes 786440 | tf_op jit(solution)/shard_map/ppermute | solution.py:24
  111.5 11.5 %collective-permute-start.35 = (bf16[128,1024]{1,0:T(8,128)(2,1)S(1)}, bf16[128,1024]{1,0:T(8,128)(2,1)S(1)}, u32[]{:S(2)}, u32[]{:S(2)}) collective-permute-start(bf16[128,1024]{1,0:T(8,128)(2,1)S(1)} %get-tuple-element.66), channel_id=1, source_target_pairs={{0,16},{8,24},{16,0},{24,8},{1,17},{9,25},{17,1},{25,9},{2,18},{10... | collective-permute-start | bytes 786440 | tf_op jit(solution)/shard_map/ppermute | solution.py:24
  123.0 8.5 %collective-permute-start.36 = (bf16[128,1024]{1,0:T(8,128)(2,1)S(1)}, bf16[128,1024]{1,0:T(8,128)(2,1)S(1)}, u32[]{:S(2)}, u32[]{:S(2)}) collective-permute-start(bf16[128,1024]{1,0:T(8,128)(2,1)S(1)} %collective-permute-done.35), channel_id=1, source_target_pairs={{0,8},{8,0},{16,24},{24,16},{1,9},{9,1},{17,25},{25,17},{2,10},{10... | collective-permute-start | bytes 786440 | tf_op jit(solution)/shard_map/ppermute | solution.py:24

commit v14 on v13

--- a/solution.py
+++ b/solution.py
@@ -310,6 +310,8 @@
     tokens = []
 
     near, far, arrived = spread_near(cotangent[0], far_bits, tokens)
+    if arrived:
+        near[0] = [after(cotangent, arrived, tokens)[0]]
     both = jnp.swapaxes(candidates[:, 0], 1, 2).reshape(-1, candidates.shape[2])
     both = owned(both, arrived, tokens)
     later = [piece for mask in far_bits for piece in near.get(mask, ())]

time: 134 us -> 134 us (level)
  no operation moved by 1% of the time
where the time goes in v14:
time: 134 us
  waiting for transfers between devices  62.9 us (47%)
  starting transfers between devices  37.9 us (28%)
  Pallas kernels  13.8 us (10%)
  other arithmetic  10.4 us (8%)
  local copies, waits for them, and re-layouts  4.56 us (3%)
  matrix products  3.47 us (3%)
    ppermute x38, waiting for transfers between devices, swap(): return lax.ppermute(value, axis, [(i, i ^ mask) for i in range(size)])  62.9 us
    ppermute x38, starting transfers between devices, swap(): return lax.ppermute(value, axis, [(i, i ^ mask) for i in range(size)])  37.9 us
    pallas_call x4, Pallas kernels, call_in_vmem(): pl.pallas_call(body, grid_spec=pltpu.PrefetchScalarGridSpec(num_scalar_pr...  7.26 us
    pallas_call x1, Pallas kernels, add_products(): pl.pallas_call(functools.partial(product_body, shape), grid_spec=pltpu.Pr...  5.8 us
    dot_general x2, matrix products, on_device(): lax.dot_general(own, jnp.concatenate(parts, axis=0), TRANSPOSED, preferre...  2.99 us
    another operation x2, other arithmetic, on_device(): return (update, jnp.stack(firsts), jnp.stack(seconds))  2.87 us
    convert_element_type x2, other arithmetic, on_device(): direction = (first / (1.0 - beta_first ** STEP) / (jnp.sqrt(second / (1.0...  2.72 us
  transfers between devices with their start and end apart: 38, of which 14 were waited for; matrix products, arithmetic and copies ran while one was open for 9% of the time, Pallas kernels for 10%

profile of v14, /device:TPU:0, one launch (start us, length us, event | category | flops | bytes accessed | tf_op | source)
XLA Modules:
  0.0 134.0 jit_solution(294498494873464568)
XLA Ops:
  0.6 1.9 %slice_bitcast_fusion.1 = (bf16[128,1024]{1,0:T(8,128)(2,1)}, bf16[128,1024]{1,0:T(8,128)(2,1)}) fusion(bf16[2,256,1024]{2,1,0:T(8,128)(2,1)} %param.7), kind=kLoop, calls=%fused_computation.67 | loop fusion | bytes 1048576 | tf_op jit(solution)/shard_map/slice | solution.py:53
  2.6 3.0 %collective-permute-start.2 = (bf16[128,1024]{1,0:T(8,128)(2,1)}, bf16[128,1024]{1,0:T(8,128)(2,1)S(1)}, u32[]{:S(2)}, u32[]{:S(2)}) collective-permute-start(bf16[128,1024]{1,0:T(8,128)(2,1)} %get-tuple-element.41), channel_id=1, source_target_pairs={{0,4},{1,5},{2,6},{3,7},{4,0},{5,1},{6,2},{7,3},{8,12},{9,13},{10,... | collective-permute-start | bytes 786440 | tf_op jit(solution)/shard_map/ppermute | solution.py:24
  5.5 1.6 %collective-permute-start = (bf16[128,1024]{1,0:T(8,128)(2,1)}, bf16[128,1024]{1,0:T(8,128)(2,1)S(1)}, u32[]{:S(2)}, u32[]{:S(2)}) collective-permute-start(bf16[128,1024]{1,0:T(8,128)(2,1)} %bitcast.64), channel_id=1, source_target_pairs={{0,8},{8,0},{16,24},{24,16},{1,9},{9,1},{17,25},{25,17},{2,10},{10... | collective-permute-start | bytes 786440 | tf_op jit(solution)/shard_map/ppermute | solution.py:24
  7.1 1.5 %collective-permute-start.1 = (bf16[128,1024]{1,0:T(8,128)(2,1)}, bf16[128,1024]{1,0:T(8,128)(2,1)S(1)}, u32[]{:S(2)}, u32[]{:S(2)}) collective-permute-start(bf16[128,1024]{1,0:T(8,128)(2,1)} %get-tuple-element.42), channel_id=1, source_target_pairs={{0,2},{1,3},{2,0},{3,1},{4,6},{5,7},{6,4},{7,5},{8,10},{9,11},{10,... | collective-permute-start | bytes 786440 | tf_op jit(solution)/shard_map/ppermute | solution.py:24
  8.6 0.7 and_compare_fusion.1
  9.4 0.1 broadcast_in_dim.34
  9.4 2.6 %collective-permute-done.2.refs_4_ = bf16[128,1024]{1,0:T(8,128)(2,1)S(1)} collective-permute-done((bf16[128,1024]{1,0:T(8,128)(2,1)}, bf16[128,1024]{1,0:T(8,128)(2,1)S(1)}, u32[]{:S(2)}, u32[]{:S(2)}) %collective-permute-start.2) | collective-permute-done | bytes 262176 | tf_op jit(solution)/shard_map/ppermute | solution.py:24
  12.1 1.7 %collective-permute-start.5 = (bf16[128,1024]{1,0:T(8,128)(2,1)}, bf16[128,1024]{1,0:T(8,128)(2,1)S(1)}, u32[]{:S(2)}, u32[]{:S(2)}) collective-permute-start(bf16[128,1024]{1,0:T(8,128)(2,1)} %get-tuple-element.42), channel_id=1, source_target_pairs={{0,4},{1,5},{2,6},{3,7},{4,0},{5,1},{6,2},{7,3},{8,12},{9,13},{10,... | collective-permute-start | bytes 786440 | tf_op jit(solution)/shard_map/ppermute | solution.py:24
  13.8 1.0 broadcast_select_fusion
  14.9 2.7 %collective-permute-start.3 = (bf16[128,1024]{1,0:T(8,128)(2,1)S(1)}, bf16[128,1024]{1,0:T(8,128)(2,1)}, u32[]{:S(2)}, u32[]{:S(2)}) collective-permute-start(bf16[128,1024]{1,0:T(8,128)(2,1)S(1)} %broadcast_select_fusion), channel_id=1, source_target_pairs={{0,16},{8,24},{16,0},{24,8},{1,17},{9,25},{17,1},{25,9},{2,18},{10... | collective-permute-start | bytes 786440 | tf_op jit(solution)/shard_map/ppermute | solution.py:24
  17.5 1.5 %collective-permute-start.4 = (bf16[128,1024]{1,0:T(8,128)(2,1)}, bf16[128,1024]{1,0:T(8,128)(2,1)S(1)}, u32[]{:S(2)}, u32[]{:S(2)}) collective-permute-start(bf16[128,1024]{1,0:T(8,128)(2,1)} %get-tuple-element.41), channel_id=1, source_target_pairs={{0,2},{1,3},{2,0},{3,1},{4,6},{5,7},{6,4},{7,5},{8,10},{9,11},{10,... | collective-permute-start | bytes 786440 | tf_op jit(solution)/shard_map/ppermute | solution.py:24
  19.0 0.5 collective-permute-start.7
  19.6 0.5 collective-permute-start.6
  20.2 9.8 %collective-permute-done.7.refs_1_ = bf16[128,1024]{1,0:T(8,128)(2,1)S(1)} collective-permute-done((bf16[128,1024]{1,0:T(8,128)(2,1)S(1)}, bf16[128,1024]{1,0:T(8,128)(2,1)S(1)}, u32[]{:S(2)}, u32[]{:S(2)}) %collective-permute-start.7) | collective-permute-done | bytes 262176 | tf_op jit(solution)/shard_map/ppermute | solution.py:24
  30.0 0.5 collective-permute-start.12
  30.6 0.4 collective-permute-start.13
  31.2 0.1 broadcast_in_dim.31
  31.3 1.1 broadcast_select_fusion.1
  32.4 1.5 %collective-permute-start.10 = (bf16[128,1024]{1,0:T(8,128)(2,1)S(1)}, bf16[128,1024]{1,0:T(8,128)(2,1)S(1)}, u32[]{:S(2)}, u32[]{:S(2)}) collective-permute-start(bf16[128,1024]{1,0:T(8,128)(2,1)S(1)} %broadcast_select_fusion.1), channel_id=1, source_target_pairs={{0,6},{1,7},{2,4},{3,5},{4,2},{5,3},{6,0},{7,1},{8,14},{9,15},{10,... | collective-permute-start | bytes 786440 | tf_op jit(solution)/shard_map/ppermute | solution.py:24
  33.9 1.5 %collective-permute-start.9 = (bf16[128,1024]{1,0:T(8,128)(2,1)S(1)}, bf16[128,1024]{1,0:T(8,128)(2,1)S(1)}, u32[]{:S(2)}, u32[]{:S(2)}) collective-permute-start(bf16[128,1024]{1,0:T(8,128)(2,1)S(1)} %broadcast_select_fusion.1), channel_id=1, source_target_pairs={{0,4},{1,5},{2,6},{3,7},{4,0},{5,1},{6,2},{7,3},{8,12},{9,13},{10,... | collective-permute-start | bytes 786440 | tf_op jit(solution)/shard_map/ppermute | solution.py:24
  35.5 0.5 collective-permute-start.8
  36.0 2.2 %copy-done = bf16[2048,1024]{1,0:T(8,128)(2,1)S(1)} copy-done((bf16[2048,1024]{1,0:T(8,128)(2,1)S(1)}, bf16[2048,1024]{1,0:T(8,128)(2,1)}, u32[]{:S(2)}) %copy-start) | copy-done | bytes 4194328
  38.2 5.8 %shard_map.85.refs_5_ = f32[1024,1024]{1,0:T(8,128)S(1)} custom-call(s32[2]{0:T(128)S(1)} %pad_add_fusion.here, bf16[256,1024]{1,0:T(8,128)(2,1)S(1)} %slice_bitcast_fusion.refs_0_, bf16[128,1024]{1,0:T(8,128)(2,1)S(1)} %collective-permute-done.1.refs_1_, bf16[128,1024]{1,0:T(8,128)(2,1)S(1)} %collective-permute-done.4.refs_2_, ...), custom_call_target="tpu_custom_call" | custom-call | flops 3221225472 | bytes 10485760 | tf_op jit(solution)/shard_map/pallas_call | solution.py:209
  44.0 3.3 %collective-permute-done.9 = bf16[128,1024]{1,0:T(8,128)(2,1)S(1)} collective-permute-done((bf16[128,1024]{1,0:T(8,128)(2,1)S(1)}, bf16[128,1024]{1,0:T(8,128)(2,1)S(1)}, u32[]{:S(2)}, u32[]{:S(2)}) %collective-permute-start.9) | collective-permute-done | bytes 262176 | tf_op jit(solution)/shard_map/ppermute | solution.py:24
  47.5 0.5 collective-permute-start.18
  48.0 2.1 %collective-permute-done.16.other = bf16[512,1024]{1,0:T(8,128)(2,1)S(1)} collective-permute-done((bf16[512,1024]{1,0:T(8,128)(2,1)S(1)}, bf16[512,1024]{1,0:T(8,128)(2,1)S(1)}, u32[]{:S(2)}, u32[]{:S(2)}) %collective-permute-start.16) | collective-permute-done | bytes 1048608 | tf_op jit(solution)/shard_map/ppermute | solution.py:24
  50.1 0.8 shard_map.86
  50.9 0.5 fusion.2.refs_0_
  51.4 1.6 %collective-permute-start.26 = (bf16[256,512]{1,0:T(8,128)(2,1)S(1)}, bf16[256,512]{1,0:T(8,128)(2,1)S(1)}, u32[]{:S(2)}, u32[]{:S(2)}) collective-permute-start(bf16[256,512]{1,0:T(8,128)(2,1)S(1)} %fusion.2.refs_0_), channel_id=1, source_target_pairs={{0,6},{1,7},{2,4},{3,5},{4,2},{5,3},{6,0},{7,1},{8,14},{9,15},{10,... | collective-permute-start | bytes 786440 | tf_op jit(solution)/shard_map/ppermute | solution.py:24
  53.0 0.7 collective-permute-start.25
  53.7 1.2 collective-permute-start.24
  55.0 2.4 %shard_map.87 = (bf16[1024,1024]{1,0:T(8,128)(2,1)S(1)}, bf16[128,1024]{1,0:T(8,128)(2,1)S(1)}, bf16[128,1024]{1,0:T(8,128)(2,1)S(1)}) custom-call(s32[2]{0:T(128)S(1)} %pad_add_fusion.here, bf16[128,1024]{1,0:T(8,128)(2,1)S(1)} %collective-permute-done.6.refs_0_, bf16[128,1024]{1,0:T(8,128)(2,1)S(1)} %collective-permute-done.7.refs_1_, ...), custom_call_target="tpu_custom_call" | custom-call | flops 1610612736 | bytes 13107200 | tf_op jit(solution)/shard_map/pallas_call | solution.py:131
  57.4 1.7 %collective-permute-start.20 = (bf16[128,1024]{1,0:T(8,128)(2,1)S(1)}, bf16[128,1024]{1,0:T(8,128)(2,1)S(1)}, u32[]{:S(2)}, u32[]{:S(2)}) collective-permute-start(bf16[128,1024]{1,0:T(8,128)(2,1)S(1)} %get-tuple-element.62), channel_id=1, source_target_pairs={{0,8},{8,0},{16,24},{24,16},{1,9},{9,1},{17,25},{25,17},{2,10},{10... | collective-permute-start | bytes 786440 | tf_op jit(solution)/shard_map/ppermute | solution.py:24
  59.0 1.2 shard_map.88
  60.3 1.3 collective-permute-done.26.refs_3_
  61.6 1.6 %collective-permute-start.19 = (bf16[128,1024]{1,0:T(8,128)(2,1)S(1)}, bf16[128,1024]{1,0:T(8,128)(2,1)S(1)}, u32[]{:S(2)}, u32[]{:S(2)}) collective-permute-start(bf16[128,1024]{1,0:T(8,128)(2,1)S(1)} %get-tuple-element.60), channel_id=1, source_target_pairs={{0,8},{8,0},{16,24},{24,16},{1,9},{9,1},{17,25},{25,17},{2,10},{10... | collective-permute-start | bytes 786440 | tf_op jit(solution)/shard_map/ppermute | solution.py:24
  63.1 3.2 %collective-permute-done.25.refs_2_ = bf16[256,512]{1,0:T(8,128)(2,1)S(1)} collective-permute-done((bf16[256,512]{1,0:T(8,128)(2,1)S(1)}, bf16[256,512]{1,0:T(8,128)(2,1)S(1)}, u32[]{:S(2)}, u32[]{:S(2)}) %collective-permute-start.25) | collective-permute-done | bytes 262176 | tf_op jit(solution)/shard_map/ppermute | solution.py:24
  66.3 0.5 collective-permute-start.29
  67.0 0.4 collective-permute-start.21
  67.4 0.4 collective-permute-done.30.refs_7_
  67.8 0.4 collective-permute-done.29.refs_6_
  68.2 0.4 collective-permute-done.28.refs_5_
  68.6 1.8 %shard_map.90 = (bf16[128,1024]{1,0:T(8,128)(2,1)S(1)}, bf16[128,1024]{1,0:T(8,128)(2,1)S(1)}) custom-call(s32[2]{0:T(128)S(1)} %pad_add_fusion.here, bf16[256,512]{1,0:T(8,128)(2,1)S(1)} %fusion.2.refs_0_, bf16[256,512]{1,0:T(8,128)(2,1)S(1)} %collective-permute-done.24.refs_1_, bf16[256,512]{1,0:T(8,128)(2,1)S(1)} %collective-permute-done.25.refs_2_, ...), custom_call_target="tpu_custom_call" | custom-call | flops 1073741824 | bytes 6815744 | tf_op jit(solution)/shard_map/pallas_call | solution.py:131
  70.4 1.6 %collective-permute-start.31 = (bf16[128,1024]{1,0:T(8,128)(2,1)S(1)}, bf16[128,1024]{1,0:T(8,128)(2,1)S(1)}, u32[]{:S(2)}, u32[]{:S(2)}) collective-permute-start(bf16[128,1024]{1,0:T(8,128)(2,1)S(1)} %get-tuple-element.66), channel_id=1, source_target_pairs={{0,8},{8,0},{16,24},{24,16},{1,9},{9,1},{17,25},{25,17},{2,10},{10... | collective-permute-start | bytes 786440 | tf_op jit(solution)/shard_map/ppermute | solution.py:24
  72.1 10.3 %collective-permute-done.21 = bf16[128,1024]{1,0:T(8,128)(2,1)S(1)} collective-permute-done((bf16[128,1024]{1,0:T(8,128)(2,1)S(1)}, bf16[128,1024]{1,0:T(8,128)(2,1)S(1)}, u32[]{:S(2)}, u32[]{:S(2)}) %collective-permute-start.21) | collective-permute-done | bytes 262176 | tf_op jit(solution)/shard_map/ppermute | solution.py:24
  82.3 1.1 fusion.38
  83.5 2.2 %collective-permute-start.22 = (bf16[128,1024]{1,0:T(8,128)(2,1)}, bf16[128,1024]{1,0:T(8,128)(2,1)}, u32[]{:S(2)}, u32[]{:S(2)}) collective-permute-start(bf16[128,1024]{1,0:T(8,128)(2,1)} %get-tuple-element.63), channel_id=1, source_target_pairs={{0,16},{8,24},{16,0},{24,8},{1,17},{9,25},{17,1},{25,9},{2,18},{10... | collective-permute-start | bytes 786440 | tf_op jit(solution)/shard_map/ppermute | solution.py:24
  85.6 1.8 %shard_map.89 = (f32[128,1024]{1,0:T(8,128)S(1)}, f32[128,1024]{1,0:T(8,128)S(1)}) custom-call(s32[2]{0:T(128)S(1)} %pad_add_fusion.here, bf16[256,512]{1,0:T(8,128)(2,1)S(1)} %fusion.2.refs_0_, bf16[256,512]{1,0:T(8,128)(2,1)S(1)} %collective-permute-done.24.refs_1_, bf16[256,512]{1,0:T(8,128)(2,1)S(1)} %collective-permute-done.25.refs_2_, ...), custom_call_target="tpu_custom_call" | custom-call | flops 1073741824 | bytes 7340032 | tf_op jit(solution)/shard_map/pallas_call | solution.py:131
  87.5 0.8 add_convert_fusion
  88.2 0.7 collective-permute-start.32
  89.0 2.0 %collective-permute-start.34 = (bf16[128,1024]{1,0:T(8,128)(2,1)S(1)}, bf16[128,1024]{1,0:T(8,128)(2,1)}, u32[]{:S(2)}, u32[]{:S(2)}) collective-permute-start(bf16[128,1024]{1,0:T(8,128)(2,1)S(1)} %get-tuple-element.70), channel_id=1, source_target_pairs={{0,8},{8,0},{16,24},{24,16},{1,9},{9,1},{17,25},{25,17},{2,10},{10... | collective-permute-start | bytes 786440 | tf_op jit(solution)/shard_map/ppermute | solution.py:24
  91.0 14.2 %collective-permute-done.22 = bf16[128,1024]{1,0:T(8,128)(2,1)} collective-permute-done((bf16[128,1024]{1,0:T(8,128)(2,1)}, bf16[128,1024]{1,0:T(8,128)(2,1)}, u32[]{:S(2)}, u32[]{:S(2)}) %collective-permute-start.22) | collective-permute-done | bytes 262176 | tf_op jit(solution)/shard_map/ppermute | solution.py:24
  105.3 4.2 %collective-permute-done.32 = bf16[128,1024]{1,0:T(8,128)(2,1)} collective-permute-done((bf16[128,1024]{1,0:T(8,128)(2,1)}, bf16[128,1024]{1,0:T(8,128)(2,1)}, u32[]{:S(2)}, u32[]{:S(2)}) %collective-permute-start.32) | collective-permute-done | bytes 262176 | tf_op jit(solution)/shard_map/ppermute | solution.py:24
  109.5 1.6 %fusion.37 = (bf16[128,1024]{1,0:T(8,128)(2,1)S(1)}, f32[128,1024]{1,0:T(8,128)S(1)}) fusion(bf16[128,1024]{1,0:T(8,128)(2,1)} %collective-permute-done.32, f32[2,128,1024]{2,1,0:T(8,128)S(1)} %copy-done.3, f32[2,128,1024]{2,1,0:T(8,128)} %param.10, f32[128,1024]{1,0:T(8,128)S(1)} %get-tuple-element.69, bf16[128,1024]{1,0:T(8,128)(2,1)} %collective-permute-done.34), kind=kLoop, calls=%fused_computation.63 | loop fusion | flops 2097152 | bytes 2883584 | tf_op jit(solution)/shard_map/convert_element_type | solution.py:368
  111.1 0.4 collective-permute-start.37
  111.5 2.0 %collective-permute-start.35 = (bf16[128,1024]{1,0:T(8,128)(2,1)S(1)}, bf16[128,1024]{1,0:T(8,128)(2,1)S(1)}, u32[]{:S(2)}, u32[]{:S(2)}) collective-permute-start(bf16[128,1024]{1,0:T(8,128)(2,1)S(1)} %get-tuple-element.72), channel_id=1, source_target_pairs={{0,16},{8,24},{16,0},{24,8},{1,17},{9,25},{17,1},{25,9},{2,18},{10... | collective-permute-start | bytes 786440 | tf_op jit(solution)/shard_map/ppermute | solution.py:24
  113.5 1.4 %fusion.35 = (f32[1,128,1024]{2,1,0:T(8,128)S(1)}, f32[1,128,1024]{2,1,0:T(8,128)S(1)}, f32[1,128,1024]{2,1,0:T(8,128)S(1)}, f32[1,128,1024]{2,1,0:T(8,128)S(1)}) fusion(f32[2,128,1024]{2,1,0:T(8,128)S(1)} %copy-done.3, f32[128,1024]{1,0:T(8,128)S(1)} %get-tuple-element.73, bf16[128,1024]{1,0:T(8,128)(2,1)S(1)} %copy-done.9, ...), kind=kLoop, calls=%fused_computation.50 | loop fusion | flops 2359296 | bytes 5767168 | tf_op jit(solution)/shard_map/stack | solution.py:386
  115.0 8.1 %collective-permute-done.35 = bf16[128,1024]{1,0:T(8,128)(2,1)S(1)} collective-permute-done((bf16[128,1024]{1,0:T(8,128)(2,1)S(1)}, bf16[128,1024]{1,0:T(8,128)(2,1)S(1)}, u32[]{:S(2)}, u32[]{:S(2)}) %collective-permute-start.35) | collective-permute-done | bytes 262176 | tf_op jit(solution)/shard_map/ppermute | solution.py:24
  123.0 2.8 %collective-permute-start.36 = (bf16[128,1024]{1,0:T(8,128)(2,1)S(1)}, bf16[128,1024]{1,0:T(8,128)(2,1)S(1)}, u32[]{:S(2)}, u32[]{:S(2)}) collective-permute-start(bf16[128,1024]{1,0:T(8,128)(2,1)S(1)} %collective-permute-done.35), channel_id=1, source_target_pairs={{0,8},{8,0},{16,24},{24,16},{1,9},{9,1},{17,25},{25,17},{2,10},{10... | collective-permute-start | bytes 786440 | tf_op jit(solution)/shard_map/ppermute | solution.py:24
  125.9 1.6 %fusion = bf16[1,256,1024]{2,1,0:T(8,128)(2,1)S(1)} fusion(bf16[128,1024]{1,0:T(8,128)(2,1)} %get-tuple-element.63, bf16[128,1024]{1,0:T(8,128)(2,1)} %collective-permute-done.22, bf16[128,1024]{1,0:T(8,128)(2,1)} %collective-permute-done.33, bf16[128,1024]{1,0:T(8,128)(2,1)S(1)} %collective-permute-done.23, ...), kind=kOutput, calls=%fused_computation.2 | convolution fusion | flops 272891904 | bytes 1835012 | tf_op jit(solution)/shard_map/dot_general | solution.py:379
  127.5 1.5 %pad_maximum_fusion.2 = (f32[2,128,1024]{2,1,0:T(8,128)}, f32[2,128,1024]{2,1,0:T(8,128)}) fusion(f32[1,128,1024]{2,1,0:T(8,128)S(1)} %get-tuple-element.84, f32[1,128,1024]{2,1,0:T(8,128)S(1)} %get-tuple-element.83, f32[1,128,1024]{2,1,0:T(8,128)S(1)} %get-tuple-element.85, f32[1,128,1024]{2,1,0:T(8,128)S(1)} %get-tuple-element.86), kind=kLoop, calls=%fused_computation.22 | loop fusion | flops 524288 | bytes 4194304 | tf_op jit(solution)/shard_map/stack | solution.py:386
  128.9 2.6 %collective-permute-done.36 = bf16[128,1024]{1,0:T(8,128)(2,1)S(1)} collective-permute-done((bf16[128,1024]{1,0:T(8,128)(2,1)S(1)}, bf16[128,1024]{1,0:T(8,128)(2,1)S(1)}, u32[]{:S(2)}, u32[]{:S(2)}) %collective-permute-start.36) | collective-permute-done | bytes 262176 | tf_op jit(solution)/shard_map/ppermute | solution.py:24
  131.6 1.4 %fusion.1 = bf16[1,256,1024]{2,1,0:T(8,128)(2,1)S(1)} fusion(bf16[128,1024]{1,0:T(8,128)(2,1)S(1)} %get-tuple-element.72, bf16[128,1024]{1,0:T(8,128)(2,1)S(1)} %collective-permute-done.35, bf16[128,1024]{1,0:T(8,128)(2,1)S(1)} %collective-permute-done.37, bf16[128,1024]{1,0:T(8,128)(2,1)S(1)} %collective-permute-done.36, bf16[512,1024]{1,0:T(8,128)(2,1)} %copy-done.2, ...), kind=kOutput, calls=%fused_computation.3 | convolution fusion | flops 272891904 | bytes 1835012 | tf_op jit(solution)/shard_map/dot_general | solution.py:379
  133.0 1.1 pad_maximum_fusion.1
  (68 shorter events, 0.9 us)
Async XLA Ops:
  0.6 19.5 %copy-start.6 = (bf16[2,256,1024]{2,1,0:T(8,128)(2,1)S(1)}, bf16[2,256,1024]{2,1,0:T(8,128)(2,1)}, u32[]{:S(2)}) copy-start(bf16[2,256,1024]{2,1,0:T(8,128)(2,1)} %param.7) | copy-start | bytes 3145732
  2.6 9.5 %collective-permute-start.2 = (bf16[128,1024]{1,0:T(8,128)(2,1)}, bf16[128,1024]{1,0:T(8,128)(2,1)S(1)}, u32[]{:S(2)}, u32[]{:S(2)}) collective-permute-start(bf16[128,1024]{1,0:T(8,128)(2,1)} %get-tuple-element.41), channel_id=1, source_target_pairs={{0,4},{1,5},{2,6},{3,7},{4,0},{5,1},{6,2},{7,3},{8,12},{9,13},{10,... | collective-permute-start | bytes 786440 | tf_op jit(solution)/shard_map/ppermute | solution.py:24
  5.5 8.3 %collective-permute-start = (bf16[128,1024]{1,0:T(8,128)(2,1)}, bf16[128,1024]{1,0:T(8,128)(2,1)S(1)}, u32[]{:S(2)}, u32[]{:S(2)}) collective-permute-start(bf16[128,1024]{1,0:T(8,128)(2,1)} %bitcast.64), channel_id=1, source_target_pairs={{0,8},{8,0},{16,24},{24,16},{1,9},{9,1},{17,25},{25,17},{2,10},{10... | collective-permute-start | bytes 786440 | tf_op jit(solution)/shard_map/ppermute | solution.py:24
  7.1 7.7 %collective-permute-start.1 = (bf16[128,1024]{1,0:T(8,128)(2,1)}, bf16[128,1024]{1,0:T(8,128)(2,1)S(1)}, u32[]{:S(2)}, u32[]{:S(2)}) collective-permute-start(bf16[128,1024]{1,0:T(8,128)(2,1)} %get-tuple-element.42), channel_id=1, source_target_pairs={{0,2},{1,3},{2,0},{3,1},{4,6},{5,7},{6,4},{7,5},{8,10},{9,11},{10,... | collective-permute-start | bytes 786440 | tf_op jit(solution)/shard_map/ppermute | solution.py:24
  12.1 8.1 %collective-permute-start.5 = (bf16[128,1024]{1,0:T(8,128)(2,1)}, bf16[128,1024]{1,0:T(8,128)(2,1)S(1)}, u32[]{:S(2)}, u32[]{:S(2)}) collective-permute-start(bf16[128,1024]{1,0:T(8,128)(2,1)} %get-tuple-element.42), channel_id=1, source_target_pairs={{0,4},{1,5},{2,6},{3,7},{4,0},{5,1},{6,2},{7,3},{8,12},{9,13},{10,... | collective-permute-start | bytes 786440 | tf_op jit(solution)/shard_map/ppermute | solution.py:24
  14.9 15.6 %copy-start.10 = (bf16[128,1024]{1,0:T(8,128)(2,1)}, bf16[128,1024]{1,0:T(8,128)(2,1)S(1)}, u32[]{:S(2)}) copy-start(bf16[128,1024]{1,0:T(8,128)(2,1)S(1)} %broadcast_select_fusion) | copy-start | bytes 786436
  14.9 15.1 %collective-permute-start.3 = (bf16[128,1024]{1,0:T(8,128)(2,1)S(1)}, bf16[128,1024]{1,0:T(8,128)(2,1)}, u32[]{:S(2)}, u32[]{:S(2)}) collective-permute-start(bf16[128,1024]{1,0:T(8,128)(2,1)S(1)} %broadcast_select_fusion), channel_id=1, source_target_pairs={{0,16},{8,24},{16,0},{24,8},{1,17},{9,25},{17,1},{25,9},{2,18},{10... | collective-permute-start | bytes 786440 | tf_op jit(solution)/shard_map/ppermute | solution.py:24
  17.5 13.0 %collective-permute-start.4 = (bf16[128,1024]{1,0:T(8,128)(2,1)}, bf16[128,1024]{1,0:T(8,128)(2,1)S(1)}, u32[]{:S(2)}, u32[]{:S(2)}) collective-permute-start(bf16[128,1024]{1,0:T(8,128)(2,1)} %get-tuple-element.41), channel_id=1, source_target_pairs={{0,2},{1,3},{2,0},{3,1},{4,6},{5,7},{6,4},{7,5},{8,10},{9,11},{10,... | collective-permute-start | bytes 786440 | tf_op jit(solution)/shard_map/ppermute | solution.py:24
  19.0 11.0 %collective-permute-start.7 = (bf16[128,1024]{1,0:T(8,128)(2,1)S(1)}, bf16[128,1024]{1,0:T(8,128)(2,1)S(1)}, u32[]{:S(2)}, u32[]{:S(2)}) collective-permute-start(bf16[128,1024]{1,0:T(8,128)(2,1)S(1)} %collective-permute-done.2.refs_4_), channel_id=1, source_target_pairs={{0,2},{1,3},{2,0},{3,1},{4,6},{5,7},{6,4},{7,5},{8,10},{9,11},{10,... | collective-permute-start | bytes 786440 | tf_op jit(solution)/shard_map/ppermute | solution.py:24
  19.6 11.0 %collective-permute-start.6 = (bf16[128,1024]{1,0:T(8,128)(2,1)S(1)}, bf16[128,1024]{1,0:T(8,128)(2,1)S(1)}, u32[]{:S(2)}, u32[]{:S(2)}) collective-permute-start(bf16[128,1024]{1,0:T(8,128)(2,1)S(1)} %collective-permute-done.1.refs_1_), channel_id=1, source_target_pairs={{0,4},{1,5},{2,6},{3,7},{4,0},{5,1},{6,2},{7,3},{8,12},{9,13},{10,... | collective-permute-start | bytes 786440 | tf_op jit(solution)/shard_map/ppermute | solution.py:24
  20.1 15.9 %collective-permute-start.11 = (bf16[256,1024]{1,0:T(8,128)(2,1)S(1)}, bf16[256,1024]{1,0:T(8,128)(2,1)S(1)}, u32[]{:S(2)}, u32[]{:S(2)}) collective-permute-start(bf16[256,1024]{1,0:T(8,128)(2,1)S(1)} %slice_bitcast_fusion.refs_0_), channel_id=1, source_target_pairs={{0,1},{1,0},{2,3},{3,2},{4,5},{5,4},{6,7},{7,6},{8,9},{9,8},{10,11... | collective-permute-start | bytes 1572872 | tf_op jit(solution)/shard_map/ppermute | solution.py:24
  30.0 2.4 %collective-permute-start.15 = (bf16[128,1024]{1,0:T(8,128)(2,1)S(1)}, bf16[128,1024]{1,0:T(8,128)(2,1)S(1)}, u32[]{:S(2)}, u32[]{:S(2)}) collective-permute-start(bf16[128,1024]{1,0:T(8,128)(2,1)S(1)} %collective-permute-done.2.refs_4_), channel_id=1, source_target_pairs={{0,1},{1,0},{2,3},{3,2},{4,5},{5,4},{6,7},{7,6},{8,9},{9,8},{10,11... | collective-permute-start | bytes 786440 | tf_op jit(solution)/shard_map/ppermute | solution.py:24
  30.0 3.9 %collective-permute-start.12 = (bf16[128,1024]{1,0:T(8,128)(2,1)S(1)}, bf16[128,1024]{1,0:T(8,128)(2,1)S(1)}, u32[]{:S(2)}, u32[]{:S(2)}) collective-permute-start(bf16[128,1024]{1,0:T(8,128)(2,1)S(1)} %collective-permute-done.1.refs_1_), channel_id=1, source_target_pairs={{0,1},{1,0},{2,3},{3,2},{4,5},{5,4},{6,7},{7,6},{8,9},{9,8},{10,11... | collective-permute-start | bytes 786440 | tf_op jit(solution)/shard_map/ppermute | solution.py:24
  30.5 4.9 %collective-permute-start.14 = (bf16[128,1024]{1,0:T(8,128)(2,1)S(1)}, bf16[128,1024]{1,0:T(8,128)(2,1)S(1)}, u32[]{:S(2)}, u32[]{:S(2)}) collective-permute-start(bf16[128,1024]{1,0:T(8,128)(2,1)S(1)} %collective-permute-done.5.refs_3_), channel_id=1, source_target_pairs={{0,1},{1,0},{2,3},{3,2},{4,5},{5,4},{6,7},{7,6},{8,9},{9,8},{10,11... | collective-permute-start | bytes 786440 | tf_op jit(solution)/shard_map/ppermute | solution.py:24
  30.6 5.4 %collective-permute-start.13 = (bf16[128,1024]{1,0:T(8,128)(2,1)S(1)}, bf16[128,1024]{1,0:T(8,128)(2,1)}, u32[]{:S(2)}, u32[]{:S(2)}) collective-permute-start(bf16[128,1024]{1,0:T(8,128)(2,1)S(1)} %collective-permute-done.4.refs_2_), channel_id=1, source_target_pairs={{0,1},{1,0},{2,3},{3,2},{4,5},{5,4},{6,7},{7,6},{8,9},{9,8},{10,11... | collective-permute-start | bytes 786440 | tf_op jit(solution)/shard_map/ppermute | solution.py:24
  32.4 11.6 %collective-permute-start.10 = (bf16[128,1024]{1,0:T(8,128)(2,1)S(1)}, bf16[128,1024]{1,0:T(8,128)(2,1)S(1)}, u32[]{:S(2)}, u32[]{:S(2)}) collective-permute-start(bf16[128,1024]{1,0:T(8,128)(2,1)S(1)} %broadcast_select_fusion.1), channel_id=1, source_target_pairs={{0,6},{1,7},{2,4},{3,5},{4,2},{5,3},{6,0},{7,1},{8,14},{9,15},{10,... | collective-permute-start | bytes 786440 | tf_op jit(solution)/shard_map/ppermute | solution.py:24
  33.9 13.4 %collective-permute-start.9 = (bf16[128,1024]{1,0:T(8,128)(2,1)S(1)}, bf16[128,1024]{1,0:T(8,128)(2,1)S(1)}, u32[]{:S(2)}, u32[]{:S(2)}) collective-permute-start(bf16[128,1024]{1,0:T(8,128)(2,1)S(1)} %broadcast_select_fusion.1), channel_id=1, source_target_pairs={{0,4},{1,5},{2,6},{3,7},{4,0},{5,1},{6,2},{7,3},{8,12},{9,13},{10,... | collective-permute-start | bytes 786440 | tf_op jit(solution)/shard_map/ppermute | solution.py:24
  35.5 11.8 %collective-permute-start.8 = (bf16[128,1024]{1,0:T(8,128)(2,1)S(1)}, bf16[128,1024]{1,0:T(8,128)(2,1)S(1)}, u32[]{:S(2)}, u32[]{:S(2)}) collective-permute-start(bf16[128,1024]{1,0:T(8,128)(2,1)S(1)} %broadcast_select_fusion.1), channel_id=1, source_target_pairs={{0,2},{1,3},{2,0},{3,1},{4,6},{5,7},{6,4},{7,5},{8,10},{9,11},{10,... | collective-permute-start | bytes 786440 | tf_op jit(solution)/shard_map/ppermute | solution.py:24
  36.0 2.2 %copy-start = (bf16[2048,1024]{1,0:T(8,128)(2,1)S(1)}, bf16[2048,1024]{1,0:T(8,128)(2,1)}, u32[]{:S(2)}) copy-start(bf16[2048,1024]{1,0:T(8,128)(2,1)} %refs_8_.3) | copy-start | bytes 12582916
  44.0 6.9 %copy-start.7 = (bf16[2,256,1024]{2,1,0:T(8,128)(2,1)S(1)}, bf16[2,256,1024]{2,1,0:T(8,128)(2,1)}, u32[]{:S(2)}) copy-start(bf16[2,256,1024]{2,1,0:T(8,128)(2,1)} %param.7) | copy-start | bytes 3145732
  47.4 7.6 %copy-start.1 = (bf16[2048,1024]{1,0:T(8,128)(2,1)S(1)}, bf16[2048,1024]{1,0:T(8,128)(2,1)}, u32[]{:S(2)}) copy-start(bf16[2048,1024]{1,0:T(8,128)(2,1)} %refs_8_.3) | copy-start | bytes 12582916
  47.4 2.7 %collective-permute-start.16 = (bf16[512,1024]{1,0:T(8,128)(2,1)S(1)}, bf16[512,1024]{1,0:T(8,128)(2,1)S(1)}, u32[]{:S(2)}, u32[]{:S(2)}) collective-permute-start(bf16[512,1024]{1,0:T(8,128)(2,1)S(1)} %pad_maximum_fusion.same), channel_id=1, source_target_pairs={{0,1},{1,0},{2,3},{3,2},{4,5},{5,4},{6,7},{7,6},{8,9},{9,8},{10,11... | collective-permute-start | bytes 3145736 | tf_op jit(solution)/shard_map/ppermute | solution.py:24
  47.5 7.5 %collective-permute-start.18 = (bf16[128,1024]{1,0:T(8,128)(2,1)S(1)}, bf16[128,1024]{1,0:T(8,128)(2,1)S(1)}, u32[]{:S(2)}, u32[]{:S(2)}) collective-permute-start(bf16[128,1024]{1,0:T(8,128)(2,1)S(1)} %collective-permute-done.7.refs_1_), channel_id=1, source_target_pairs={{0,1},{1,0},{2,3},{3,2},{4,5},{5,4},{6,7},{7,6},{8,9},{9,8},{10,11... | collective-permute-start | bytes 786440 | tf_op jit(solution)/shard_map/ppermute | solution.py:24
  48.0 7.0 %collective-permute-start.17 = (bf16[128,1024]{1,0:T(8,128)(2,1)S(1)}, bf16[128,1024]{1,0:T(8,128)(2,1)S(1)}, u32[]{:S(2)}, u32[]{:S(2)}) collective-permute-start(bf16[128,1024]{1,0:T(8,128)(2,1)S(1)} %collective-permute-done.6.refs_0_), channel_id=1, source_target_pairs={{0,1},{1,0},{2,3},{3,2},{4,5},{5,4},{6,7},{7,6},{8,9},{9,8},{10,11... | collective-permute-start | bytes 786440 | tf_op jit(solution)/shard_map/ppermute | solution.py:24
  50.9 6.5 %copy-start.2 = (bf16[512,1024]{1,0:T(8,128)(2,1)}, bf16[512,1024]{1,0:T(8,128)(2,1)S(1)}, u32[]{:S(2)}) copy-start(bf16[512,1024]{1,0:T(8,128)(2,1)S(1)} %get-tuple-element.64) | copy-start | bytes 3145732
  51.4 10.2 %collective-permute-start.26 = (bf16[256,512]{1,0:T(8,128)(2,1)S(1)}, bf16[256,512]{1,0:T(8,128)(2,1)S(1)}, u32[]{:S(2)}, u32[]{:S(2)}) collective-permute-start(bf16[256,512]{1,0:T(8,128)(2,1)S(1)} %fusion.2.refs_0_), channel_id=1, source_target_pairs={{0,6},{1,7},{2,4},{3,5},{4,2},{5,3},{6,0},{7,1},{8,14},{9,15},{10,... | collective-permute-start | bytes 786440 | tf_op jit(solution)/shard_map/ppermute | solution.py:24
  53.0 13.3 %collective-permute-start.25 = (bf16[256,512]{1,0:T(8,128)(2,1)S(1)}, bf16[256,512]{1,0:T(8,128)(2,1)S(1)}, u32[]{:S(2)}, u32[]{:S(2)}) collective-permute-start(bf16[256,512]{1,0:T(8,128)(2,1)S(1)} %fusion.2.refs_0_), channel_id=1, source_target_pairs={{0,4},{1,5},{2,6},{3,7},{4,0},{5,1},{6,2},{7,3},{8,12},{9,13},{10,... | collective-permute-start | bytes 786440 | tf_op jit(solution)/shard_map/ppermute | solution.py:24
  53.7 12.6 %collective-permute-start.24 = (bf16[256,512]{1,0:T(8,128)(2,1)S(1)}, bf16[256,512]{1,0:T(8,128)(2,1)S(1)}, u32[]{:S(2)}, u32[]{:S(2)}) collective-permute-start(bf16[256,512]{1,0:T(8,128)(2,1)S(1)} %fusion.2.refs_0_), channel_id=1, source_target_pairs={{0,2},{1,3},{2,0},{3,1},{4,6},{5,7},{6,4},{7,5},{8,10},{9,11},{10,... | collective-permute-start | bytes 786440 | tf_op jit(solution)/shard_map/ppermute | solution.py:24
  57.4 9.4 %collective-permute-start.20 = (bf16[128,1024]{1,0:T(8,128)(2,1)S(1)}, bf16[128,1024]{1,0:T(8,128)(2,1)S(1)}, u32[]{:S(2)}, u32[]{:S(2)}) collective-permute-start(bf16[128,1024]{1,0:T(8,128)(2,1)S(1)} %get-tuple-element.62), channel_id=1, source_target_pairs={{0,8},{8,0},{16,24},{24,16},{1,9},{9,1},{17,25},{25,17},{2,10},{10... | collective-permute-start | bytes 786440 | tf_op jit(solution)/shard_map/ppermute | solution.py:24
  59.0 7.9 %collective-permute-start.27 = (bf16[256,512]{1,0:T(8,128)(2,1)S(1)}, bf16[256,512]{1,0:T(8,128)(2,1)S(1)}, u32[]{:S(2)}, u32[]{:S(2)}) collective-permute-start(bf16[256,512]{1,0:T(8,128)(2,1)S(1)} %fusion.2.refs_0_), channel_id=1, source_target_pairs={{0,1},{1,0},{2,3},{3,2},{4,5},{5,4},{6,7},{7,6},{8,9},{9,8},{10,11... | collective-permute-start | bytes 786440 | tf_op jit(solution)/shard_map/ppermute | solution.py:24
  61.6 10.5 %collective-permute-start.19 = (bf16[128,1024]{1,0:T(8,128)(2,1)S(1)}, bf16[128,1024]{1,0:T(8,128)(2,1)S(1)}, u32[]{:S(2)}, u32[]{:S(2)}) collective-permute-start(bf16[128,1024]{1,0:T(8,128)(2,1)S(1)} %get-tuple-element.60), channel_id=1, source_target_pairs={{0,8},{8,0},{16,24},{24,16},{1,9},{9,1},{17,25},{25,17},{2,10},{10... | collective-permute-start | bytes 786440 | tf_op jit(solution)/shard_map/ppermute | solution.py:24
  66.3 1.5 %collective-permute-start.30 = (bf16[256,512]{1,0:T(8,128)(2,1)S(1)}, bf16[256,512]{1,0:T(8,128)(2,1)S(1)}, u32[]{:S(2)}, u32[]{:S(2)}) collective-permute-start(bf16[256,512]{1,0:T(8,128)(2,1)S(1)} %collective-permute-done.26.refs_3_), channel_id=1, source_target_pairs={{0,1},{1,0},{2,3},{3,2},{4,5},{5,4},{6,7},{7,6},{8,9},{9,8},{10,11... | collective-permute-start | bytes 786440 | tf_op jit(solution)/shard_map/ppermute | solution.py:24
  66.3 1.9 %collective-permute-start.29 = (bf16[256,512]{1,0:T(8,128)(2,1)S(1)}, bf16[256,512]{1,0:T(8,128)(2,1)S(1)}, u32[]{:S(2)}, u32[]{:S(2)}) collective-permute-start(bf16[256,512]{1,0:T(8,128)(2,1)S(1)} %collective-permute-done.25.refs_2_), channel_id=1, source_target_pairs={{0,1},{1,0},{2,3},{3,2},{4,5},{5,4},{6,7},{7,6},{8,9},{9,8},{10,11... | collective-permute-start | bytes 786440 | tf_op jit(solution)/shard_map/ppermute | solution.py:24
  66.8 1.8 %collective-permute-start.28 = (bf16[256,512]{1,0:T(8,128)(2,1)S(1)}, bf16[256,512]{1,0:T(8,128)(2,1)S(1)}, u32[]{:S(2)}, u32[]{:S(2)}) collective-permute-start(bf16[256,512]{1,0:T(8,128)(2,1)S(1)} %collective-permute-done.24.refs_1_), channel_id=1, source_target_pairs={{0,1},{1,0},{2,3},{3,2},{4,5},{5,4},{6,7},{7,6},{8,9},{9,8},{10,11... | collective-permute-start | bytes 786440 | tf_op jit(solution)/shard_map/ppermute | solution.py:24
  67.0 15.4 %copy-start.3 = (f32[2,128,1024]{2,1,0:T(8,128)S(1)}, f32[2,128,1024]{2,1,0:T(8,128)}, u32[]{:S(2)}) copy-start(f32[2,128,1024]{2,1,0:T(8,128)} %param.9) | copy-start | bytes 3145732
  67.0 15.4 %copy-start.4 = (f32[2,128,1024]{2,1,0:T(8,128)S(1)}, f32[2,128,1024]{2,1,0:T(8,128)}, u32[]{:S(2)}) copy-start(f32[2,128,1024]{2,1,0:T(8,128)} %param.10) | copy-start | bytes 3145732
  67.0 15.3 %collective-permute-start.21 = (bf16[128,1024]{1,0:T(8,128)(2,1)S(1)}, bf16[128,1024]{1,0:T(8,128)(2,1)S(1)}, u32[]{:S(2)}, u32[]{:S(2)}) collective-permute-start(bf16[128,1024]{1,0:T(8,128)(2,1)S(1)} %add_convert_fusion.1), channel_id=1, source_target_pairs={{0,16},{8,24},{16,0},{24,8},{1,17},{9,25},{17,1},{25,9},{2,18},{10... | collective-permute-start | bytes 786440 | tf_op jit(solution)/shard_map/ppermute | solution.py:24
  70.4 17.1 %collective-permute-start.31 = (bf16[128,1024]{1,0:T(8,128)(2,1)S(1)}, bf16[128,1024]{1,0:T(8,128)(2,1)S(1)}, u32[]{:S(2)}, u32[]{:S(2)}) collective-permute-start(bf16[128,1024]{1,0:T(8,128)(2,1)S(1)} %get-tuple-element.66), channel_id=1, source_target_pairs={{0,8},{8,0},{16,24},{24,16},{1,9},{9,1},{17,25},{25,17},{2,10},{10... | collective-permute-start | bytes 786440 | tf_op jit(solution)/shard_map/ppermute | solution.py:24
  82.3 1.1 copy-start.8
  83.5 21.8 %collective-permute-start.33 = (bf16[128,1024]{1,0:T(8,128)(2,1)}, bf16[128,1024]{1,0:T(8,128)(2,1)}, u32[]{:S(2)}, u32[]{:S(2)}) collective-permute-start(bf16[128,1024]{1,0:T(8,128)(2,1)} %get-tuple-element.63), channel_id=1, source_target_pairs={{0,8},{8,0},{16,24},{24,16},{1,9},{9,1},{17,25},{25,17},{2,10},{10... | collective-permute-start | bytes 786440 | tf_op jit(solution)/shard_map/ppermute | solution.py:24
  83.5 21.8 %collective-permute-start.22 = (bf16[128,1024]{1,0:T(8,128)(2,1)}, bf16[128,1024]{1,0:T(8,128)(2,1)}, u32[]{:S(2)}, u32[]{:S(2)}) collective-permute-start(bf16[128,1024]{1,0:T(8,128)(2,1)} %get-tuple-element.63), channel_id=1, source_target_pairs={{0,16},{8,24},{16,0},{24,8},{1,17},{9,25},{17,1},{25,9},{2,18},{10... | collective-permute-start | bytes 786440 | tf_op jit(solution)/shard_map/ppermute | solution.py:24
  88.2 21.3 %collective-permute-start.32 = (bf16[128,1024]{1,0:T(8,128)(2,1)}, bf16[128,1024]{1,0:T(8,128)(2,1)}, u32[]{:S(2)}, u32[]{:S(2)}) collective-permute-start(bf16[128,1024]{1,0:T(8,128)(2,1)} %add_convert_fusion), channel_id=1, source_target_pairs={{0,16},{8,24},{16,0},{24,8},{1,17},{9,25},{17,1},{25,9},{2,18},{10... | collective-permute-start | bytes 786440 | tf_op jit(solution)/shard_map/ppermute | solution.py:24
  89.0 20.5 %collective-permute-start.34 = (bf16[128,1024]{1,0:T(8,128)(2,1)S(1)}, bf16[128,1024]{1,0:T(8,128)(2,1)}, u32[]{:S(2)}, u32[]{:S(2)}) collective-permute-start(bf16[128,1024]{1,0:T(8,128)(2,1)S(1)} %get-tuple-element.70), channel_id=1, source_target_pairs={{0,8},{8,0},{16,24},{24,16},{1,9},{9,1},{17,25},{25,17},{2,10},{10... | collective-permute-start | bytes 786440 | tf_op jit(solution)/shard_map/ppermute | solution.py:24
  91.0 22.5 %copy-start.5 = (f32[2,128,1024]{2,1,0:T(8,128)S(1)}, f32[2,128,1024]{2,1,0:T(8,128)}, u32[]{:S(2)}) copy-start(f32[2,128,1024]{2,1,0:T(8,128)} %param.10) | copy-start | bytes 3145732
  91.0 22.6 %copy-start.9 = (bf16[128,1024]{1,0:T(8,128)(2,1)S(1)}, bf16[128,1024]{1,0:T(8,128)(2,1)}, u32[]{:S(2)}) copy-start(bf16[128,1024]{1,0:T(8,128)(2,1)} %copy-done.8) | copy-start | bytes 786436
  105.2 20.6 %collective-permute-start.23 = (bf16[128,1024]{1,0:T(8,128)(2,1)}, bf16[128,1024]{1,0:T(8,128)(2,1)S(1)}, u32[]{:S(2)}, u32[]{:S(2)}) collective-permute-start(bf16[128,1024]{1,0:T(8,128)(2,1)} %collective-permute-done.22), channel_id=1, source_target_pairs={{0,8},{8,0},{16,24},{24,16},{1,9},{9,1},{17,25},{25,17},{2,10},{10... | collective-permute-start | bytes 786440 | tf_op jit(solution)/shard_map/ppermute | solution.py:24
  111.1 17.8 %collective-permute-start.37 = (bf16[128,1024]{1,0:T(8,128)(2,1)S(1)}, bf16[128,1024]{1,0:T(8,128)(2,1)S(1)}, u32[]{:S(2)}, u32[]{:S(2)}) collective-permute-start(bf16[128,1024]{1,0:T(8,128)(2,1)S(1)} %get-tuple-element.72), channel_id=1, source_target_pairs={{0,8},{8,0},{16,24},{24,16},{1,9},{9,1},{17,25},{25,17},{2,10},{10... | collective-permute-start | bytes 786440 | tf_op jit(solution)/shard_map/ppermute | solution.py:24
  111.5 11.5 %collective-permute-start.35 = (bf16[128,1024]{1,0:T(8,128)(2,1)S(1)}, bf16[128,1024]{1,0:T(8,128)(2,1)S(1)}, u32[]{:S(2)}, u32[]{:S(2)}) collective-permute-start(bf16[128,1024]{1,0:T(8,128)(2,1)S(1)} %get-tuple-element.72), channel_id=1, source_target_pairs={{0,16},{8,24},{16,0},{24,8},{1,17},{9,25},{17,1},{25,9},{2,18},{10... | collective-permute-start | bytes 786440 | tf_op jit(solution)/shard_map/ppermute | solution.py:24
  123.0 8.5 %collective-permute-start.36 = (bf16[128,1024]{1,0:T(8,128)(2,1)S(1)}, bf16[128,1024]{1,0:T(8,128)(2,1)S(1)}, u32[]{:S(2)}, u32[]{:S(2)}) collective-permute-start(bf16[128,1024]{1,0:T(8,128)(2,1)S(1)} %collective-permute-done.35), channel_id=1, source_target_pairs={{0,8},{8,0},{16,24},{24,16},{1,9},{9,1},{17,25},{25,17},{2,10},{10... | collective-permute-start | bytes 786440 | tf_op jit(solution)/shard_map/ppermute | solution.py:24

commit v15 on v14

--- a/solution.py
+++ b/solution.py
@@ -314,9 +314,7 @@
         near[0] = [after(cotangent, arrived, tokens)[0]]
     both = jnp.swapaxes(candidates[:, 0], 1, 2).reshape(-1, candidates.shape[2])
     both = owned(both, arrived, tokens)
-    later = [piece for mask in far_bits for piece in near.get(mask, ())]
-    later = [piece for piece in later if all(piece is not other for other in arrived)]
-    blocks = spread(after(both, later + flat(far), tokens), far_bits)
+    blocks = spread(after(both, flat(far), tokens), far_bits)
     same = jnp.concatenate([blocks[mask] for mask in sorted(blocks)], axis=0)
     near_all = with_partner(near)
     partial = add_products(near_all, here, layer_input)

time: 134 us -> 132 us (0.985)
  waiting for transfers between devices: 62.9 us -> 61.1 us
    ppermute x38, waiting for transfers between devices: 62.9 us -> 61.1 us  [swap(): return lax.ppermute(value, axis, [(i, i ^ mask) for i in range(size)])]
  transfers between devices with their start and end apart: 38 -> 38, of which waited for: 14 -> 14; matrix products, arithmetic and copies ran while one was open for 9% -> 10% of each run, Pallas kernels for 10% -> 10%
where the time goes in v15:
time: 132 us
  waiting for transfers between devices  61.1 us (46%)
  starting transfers between devices  38.2 us (29%)
  Pallas kernels  13.8 us (10%)
  other arithmetic  10.7 us (8%)
  local copies, waits for them, and re-layouts  4.71 us (4%)
  matrix products  2.55 us (2%)
    ppermute x38, waiting for transfers between devices, swap(): return lax.ppermute(value, axis, [(i, i ^ mask) for i in range(size)])  61.1 us
    ppermute x38, starting transfers between devices, swap(): return lax.ppermute(value, axis, [(i, i ^ mask) for i in range(size)])  38.2 us
    pallas_call x4, Pallas kernels, call_in_vmem(): pl.pallas_call(body, grid_spec=pltpu.PrefetchScalarGridSpec(num_scalar_pr...  7.24 us
    pallas_call x1, Pallas kernels, add_products(): pl.pallas_call(functools.partial(product_body, shape), grid_spec=pltpu.Pr...  5.8 us
    another operation x2, other arithmetic, on_device(): return (update, jnp.stack(firsts), jnp.stack(seconds))  2.95 us
    convert_element_type x2, other arithmetic, on_device(): direction = (first / (1.0 - beta_first ** STEP) / (jnp.sqrt(second / (1.0...  2.87 us
  transfers between devices with their start and end apart: 38, of which 14 were waited for; matrix products, arithmetic and copies ran while one was open for 10% of the time, Pallas kernels for 10%

profile of v15, /device:TPU:0, one launch (start us, length us, event | category | flops | bytes accessed | tf_op | source)
XLA Modules:
  0.0 131.9 jit_solution(2887409091759890045)
XLA Ops:
  0.6 1.1 slice_bitcast_fusion.1
  1.7 3.0 %collective-permute-start.2 = (bf16[128,1024]{1,0:T(8,128)(2,1)S(1)}, bf16[128,1024]{1,0:T(8,128)(2,1)S(1)}, u32[]{:S(2)}, u32[]{:S(2)}) collective-permute-start(bf16[128,1024]{1,0:T(8,128)(2,1)S(1)} %get-tuple-element.41), channel_id=1, source_target_pairs={{0,4},{1,5},{2,6},{3,7},{4,0},{5,1},{6,2},{7,3},{8,12},{9,13},{10,... | collective-permute-start | bytes 786440 | tf_op jit(solution)/shard_map/ppermute | solution.py:24
  4.7 1.6 %collective-permute-start = (bf16[128,1024]{1,0:T(8,128)(2,1)}, bf16[128,1024]{1,0:T(8,128)(2,1)S(1)}, u32[]{:S(2)}, u32[]{:S(2)}) collective-permute-start(bf16[128,1024]{1,0:T(8,128)(2,1)} %bitcast.64), channel_id=1, source_target_pairs={{0,8},{8,0},{16,24},{24,16},{1,9},{9,1},{17,25},{25,17},{2,10},{10... | collective-permute-start | bytes 786440 | tf_op jit(solution)/shard_map/ppermute | solution.py:24
  6.3 1.5 %collective-permute-start.1 = (bf16[128,1024]{1,0:T(8,128)(2,1)S(1)}, bf16[128,1024]{1,0:T(8,128)(2,1)S(1)}, u32[]{:S(2)}, u32[]{:S(2)}) collective-permute-start(bf16[128,1024]{1,0:T(8,128)(2,1)S(1)} %get-tuple-element.42), channel_id=1, source_target_pairs={{0,2},{1,3},{2,0},{3,1},{4,6},{5,7},{6,4},{7,5},{8,10},{9,11},{10,... | collective-permute-start | bytes 786440 | tf_op jit(solution)/shard_map/ppermute | solution.py:24
  7.8 0.7 and_compare_fusion.1
  8.6 2.4 %collective-permute-done.2.refs_4_ = bf16[128,1024]{1,0:T(8,128)(2,1)S(1)} collective-permute-done((bf16[128,1024]{1,0:T(8,128)(2,1)S(1)}, bf16[128,1024]{1,0:T(8,128)(2,1)S(1)}, u32[]{:S(2)}, u32[]{:S(2)}) %collective-permute-start.2) | collective-permute-done | bytes 262176 | tf_op jit(solution)/shard_map/ppermute | solution.py:24
  11.0 1.7 %collective-permute-start.10 = (bf16[128,1024]{1,0:T(8,128)(2,1)S(1)}, bf16[128,1024]{1,0:T(8,128)(2,1)S(1)}, u32[]{:S(2)}, u32[]{:S(2)}) collective-permute-start(bf16[128,1024]{1,0:T(8,128)(2,1)S(1)} %get-tuple-element.42), channel_id=1, source_target_pairs={{0,4},{1,5},{2,6},{3,7},{4,0},{5,1},{6,2},{7,3},{8,12},{9,13},{10,... | collective-permute-start | bytes 786440 | tf_op jit(solution)/shard_map/ppermute | solution.py:24
  12.8 1.0 broadcast_select_fusion
  13.9 2.7 %collective-permute-start.3 = (bf16[128,1024]{1,0:T(8,128)(2,1)S(1)}, bf16[128,1024]{1,0:T(8,128)(2,1)}, u32[]{:S(2)}, u32[]{:S(2)}) collective-permute-start(bf16[128,1024]{1,0:T(8,128)(2,1)S(1)} %broadcast_select_fusion), channel_id=1, source_target_pairs={{0,16},{8,24},{16,0},{24,8},{1,17},{9,25},{17,1},{25,9},{2,18},{10... | collective-permute-start | bytes 786440 | tf_op jit(solution)/shard_map/ppermute | solution.py:24
  16.5 1.5 %collective-permute-start.9 = (bf16[128,1024]{1,0:T(8,128)(2,1)S(1)}, bf16[128,1024]{1,0:T(8,128)(2,1)S(1)}, u32[]{:S(2)}, u32[]{:S(2)}) collective-permute-start(bf16[128,1024]{1,0:T(8,128)(2,1)S(1)} %get-tuple-element.41), channel_id=1, source_target_pairs={{0,2},{1,3},{2,0},{3,1},{4,6},{5,7},{6,4},{7,5},{8,10},{9,11},{10,... | collective-permute-start | bytes 786440 | tf_op jit(solution)/shard_map/ppermute | solution.py:24
  18.0 0.5 collective-permute-start.5
  18.5 0.5 collective-permute-start.4
  19.1 1.1 slice_bitcast_fusion.refs_0_
  20.2 8.5 %collective-permute-done.5.refs_1_ = bf16[128,1024]{1,0:T(8,128)(2,1)S(1)} collective-permute-done((bf16[128,1024]{1,0:T(8,128)(2,1)S(1)}, bf16[128,1024]{1,0:T(8,128)(2,1)S(1)}, u32[]{:S(2)}, u32[]{:S(2)}) %collective-permute-start.5) | collective-permute-done | bytes 262176 | tf_op jit(solution)/shard_map/ppermute | solution.py:24
  28.8 0.5 collective-permute-start.12
  29.4 0.4 collective-permute-start.13
  29.9 0.1 broadcast_in_dim.31
  30.0 1.1 broadcast_select_fusion.1
  31.2 1.5 %collective-permute-start.8 = (bf16[128,1024]{1,0:T(8,128)(2,1)S(1)}, bf16[128,1024]{1,0:T(8,128)(2,1)S(1)}, u32[]{:S(2)}, u32[]{:S(2)}) collective-permute-start(bf16[128,1024]{1,0:T(8,128)(2,1)S(1)} %broadcast_select_fusion.1), channel_id=1, source_target_pairs={{0,6},{1,7},{2,4},{3,5},{4,2},{5,3},{6,0},{7,1},{8,14},{9,15},{10,... | collective-permute-start | bytes 786440 | tf_op jit(solution)/shard_map/ppermute | solution.py:24
  32.7 1.5 %collective-permute-start.7 = (bf16[128,1024]{1,0:T(8,128)(2,1)S(1)}, bf16[128,1024]{1,0:T(8,128)(2,1)S(1)}, u32[]{:S(2)}, u32[]{:S(2)}) collective-permute-start(bf16[128,1024]{1,0:T(8,128)(2,1)S(1)} %broadcast_select_fusion.1), channel_id=1, source_target_pairs={{0,4},{1,5},{2,6},{3,7},{4,0},{5,1},{6,2},{7,3},{8,12},{9,13},{10,... | collective-permute-start | bytes 786440 | tf_op jit(solution)/shard_map/ppermute | solution.py:24
  34.2 0.5 collective-permute-start.6
  34.7 2.2 %copy-done = bf16[2048,1024]{1,0:T(8,128)(2,1)S(1)} copy-done((bf16[2048,1024]{1,0:T(8,128)(2,1)S(1)}, bf16[2048,1024]{1,0:T(8,128)(2,1)}, u32[]{:S(2)}) %copy-start) | copy-done | bytes 4194328
  36.9 5.8 %shard_map.85.refs_5_ = f32[1024,1024]{1,0:T(8,128)S(1)} custom-call(s32[2]{0:T(128)S(1)} %pad_add_fusion.here, bf16[256,1024]{1,0:T(8,128)(2,1)S(1)} %slice_bitcast_fusion.refs_0_, bf16[128,1024]{1,0:T(8,128)(2,1)S(1)} %collective-permute-done.1.refs_1_, bf16[128,1024]{1,0:T(8,128)(2,1)S(1)} %collective-permute-done.9.refs_2_, ...), custom_call_target="tpu_custom_call" | custom-call | flops 3221225472 | bytes 10485760 | tf_op jit(solution)/shard_map/pallas_call | solution.py:209
  42.8 3.3 %collective-permute-done.7 = bf16[128,1024]{1,0:T(8,128)(2,1)S(1)} collective-permute-done((bf16[128,1024]{1,0:T(8,128)(2,1)S(1)}, bf16[128,1024]{1,0:T(8,128)(2,1)S(1)}, u32[]{:S(2)}, u32[]{:S(2)}) %collective-permute-start.7) | collective-permute-done | bytes 262176 | tf_op jit(solution)/shard_map/ppermute | solution.py:24
  46.2 0.5 collective-permute-start.18
  46.8 2.1 %collective-permute-done.16.other = bf16[512,1024]{1,0:T(8,128)(2,1)S(1)} collective-permute-done((bf16[512,1024]{1,0:T(8,128)(2,1)S(1)}, bf16[512,1024]{1,0:T(8,128)(2,1)S(1)}, u32[]{:S(2)}, u32[]{:S(2)}) %collective-permute-start.16) | collective-permute-done | bytes 1048608 | tf_op jit(solution)/shard_map/ppermute | solution.py:24
  48.9 0.8 shard_map.86
  49.6 0.5 fusion.2.refs_0_
  50.1 1.6 %collective-permute-start.26 = (bf16[256,512]{1,0:T(8,128)(2,1)S(1)}, bf16[256,512]{1,0:T(8,128)(2,1)S(1)}, u32[]{:S(2)}, u32[]{:S(2)}) collective-permute-start(bf16[256,512]{1,0:T(8,128)(2,1)S(1)} %fusion.2.refs_0_), channel_id=1, source_target_pairs={{0,6},{1,7},{2,4},{3,5},{4,2},{5,3},{6,0},{7,1},{8,14},{9,15},{10,... | collective-permute-start | bytes 786440 | tf_op jit(solution)/shard_map/ppermute | solution.py:24
  51.7 0.7 collective-permute-start.25
  52.4 1.2 collective-permute-start.24
  53.7 2.4 %shard_map.87 = (bf16[1024,1024]{1,0:T(8,128)(2,1)S(1)}, bf16[128,1024]{1,0:T(8,128)(2,1)S(1)}, bf16[128,1024]{1,0:T(8,128)(2,1)S(1)}) custom-call(s32[2]{0:T(128)S(1)} %pad_add_fusion.here, bf16[128,1024]{1,0:T(8,128)(2,1)S(1)} %collective-permute-done.4.refs_0_, bf16[128,1024]{1,0:T(8,128)(2,1)S(1)} %collective-permute-done.5.refs_1_, ...), custom_call_target="tpu_custom_call" | custom-call | flops 1610612736 | bytes 13107200 | tf_op jit(solution)/shard_map/pallas_call | solution.py:131
  56.1 1.6 %collective-permute-start.20 = (bf16[128,1024]{1,0:T(8,128)(2,1)S(1)}, bf16[128,1024]{1,0:T(8,128)(2,1)S(1)}, u32[]{:S(2)}, u32[]{:S(2)}) collective-permute-start(bf16[128,1024]{1,0:T(8,128)(2,1)S(1)} %get-tuple-element.58), channel_id=1, source_target_pairs={{0,8},{8,0},{16,24},{24,16},{1,9},{9,1},{17,25},{25,17},{2,10},{10... | collective-permute-start | bytes 786440 | tf_op jit(solution)/shard_map/ppermute | solution.py:24
  57.7 1.2 shard_map.88
  59.0 1.3 collective-permute-done.26.refs_3_
  60.3 1.6 %collective-permute-start.19 = (bf16[128,1024]{1,0:T(8,128)(2,1)S(1)}, bf16[128,1024]{1,0:T(8,128)(2,1)S(1)}, u32[]{:S(2)}, u32[]{:S(2)}) collective-permute-start(bf16[128,1024]{1,0:T(8,128)(2,1)S(1)} %get-tuple-element.56), channel_id=1, source_target_pairs={{0,8},{8,0},{16,24},{24,16},{1,9},{9,1},{17,25},{25,17},{2,10},{10... | collective-permute-start | bytes 786440 | tf_op jit(solution)/shard_map/ppermute | solution.py:24
  61.9 3.2 %collective-permute-done.25.refs_2_ = bf16[256,512]{1,0:T(8,128)(2,1)S(1)} collective-permute-done((bf16[256,512]{1,0:T(8,128)(2,1)S(1)}, bf16[256,512]{1,0:T(8,128)(2,1)S(1)}, u32[]{:S(2)}, u32[]{:S(2)}) %collective-permute-start.25) | collective-permute-done | bytes 262176 | tf_op jit(solution)/shard_map/ppermute | solution.py:24
  65.1 0.5 collective-permute-start.29
  65.7 0.4 collective-permute-start.21
  66.2 0.4 collective-permute-done.30.refs_7_
  66.6 0.4 collective-permute-done.29.refs_6_
  67.0 0.4 collective-permute-done.28.refs_5_
  67.3 1.8 %shard_map.90 = (bf16[128,1024]{1,0:T(8,128)(2,1)S(1)}, bf16[128,1024]{1,0:T(8,128)(2,1)S(1)}) custom-call(s32[2]{0:T(128)S(1)} %pad_add_fusion.here, bf16[256,512]{1,0:T(8,128)(2,1)S(1)} %fusion.2.refs_0_, bf16[256,512]{1,0:T(8,128)(2,1)S(1)} %collective-permute-done.24.refs_1_, bf16[256,512]{1,0:T(8,128)(2,1)S(1)} %collective-permute-done.25.refs_2_, ...), custom_call_target="tpu_custom_call" | custom-call | flops 1073741824 | bytes 6815744 | tf_op jit(solution)/shard_map/pallas_call | solution.py:131
  69.1 1.6 %collective-permute-start.31 = (bf16[128,1024]{1,0:T(8,128)(2,1)S(1)}, bf16[128,1024]{1,0:T(8,128)(2,1)S(1)}, u32[]{:S(2)}, u32[]{:S(2)}) collective-permute-start(bf16[128,1024]{1,0:T(8,128)(2,1)S(1)} %get-tuple-element.62), channel_id=1, source_target_pairs={{0,8},{8,0},{16,24},{24,16},{1,9},{9,1},{17,25},{25,17},{2,10},{10... | collective-permute-start | bytes 786440 | tf_op jit(solution)/shard_map/ppermute | solution.py:24
  70.8 10.3 %collective-permute-done.21 = bf16[128,1024]{1,0:T(8,128)(2,1)S(1)} collective-permute-done((bf16[128,1024]{1,0:T(8,128)(2,1)S(1)}, bf16[128,1024]{1,0:T(8,128)(2,1)S(1)}, u32[]{:S(2)}, u32[]{:S(2)}) %collective-permute-start.21) | collective-permute-done | bytes 262176 | tf_op jit(solution)/shard_map/ppermute | solution.py:24
  81.1 1.1 fusion.38
  82.2 2.3 %collective-permute-start.22 = (bf16[128,1024]{1,0:T(8,128)(2,1)}, bf16[128,1024]{1,0:T(8,128)(2,1)}, u32[]{:S(2)}, u32[]{:S(2)}) collective-permute-start(bf16[128,1024]{1,0:T(8,128)(2,1)} %get-tuple-element.59), channel_id=1, source_target_pairs={{0,16},{8,24},{16,0},{24,8},{1,17},{9,25},{17,1},{25,9},{2,18},{10... | collective-permute-start | bytes 786440 | tf_op jit(solution)/shard_map/ppermute | solution.py:24
  84.5 1.8 %shard_map.89 = (f32[128,1024]{1,0:T(8,128)S(1)}, f32[128,1024]{1,0:T(8,128)S(1)}) custom-call(s32[2]{0:T(128)S(1)} %pad_add_fusion.here, bf16[256,512]{1,0:T(8,128)(2,1)S(1)} %fusion.2.refs_0_, bf16[256,512]{1,0:T(8,128)(2,1)S(1)} %collective-permute-done.24.refs_1_, bf16[256,512]{1,0:T(8,128)(2,1)S(1)} %collective-permute-done.25.refs_2_, ...), custom_call_target="tpu_custom_call" | custom-call | flops 1073741824 | bytes 7340032 | tf_op jit(solution)/shard_map/pallas_call | solution.py:131
  86.3 0.8 add_convert_fusion
  87.1 0.7 collective-permute-start.32
  87.7 2.0 %collective-permute-start.34 = (bf16[128,1024]{1,0:T(8,128)(2,1)S(1)}, bf16[128,1024]{1,0:T(8,128)(2,1)}, u32[]{:S(2)}, u32[]{:S(2)}) collective-permute-start(bf16[128,1024]{1,0:T(8,128)(2,1)S(1)} %get-tuple-element.66), channel_id=1, source_target_pairs={{0,8},{8,0},{16,24},{24,16},{1,9},{9,1},{17,25},{25,17},{2,10},{10... | collective-permute-start | bytes 786440 | tf_op jit(solution)/shard_map/ppermute | solution.py:24
  89.7 14.2 %collective-permute-done.22 = bf16[128,1024]{1,0:T(8,128)(2,1)} collective-permute-done((bf16[128,1024]{1,0:T(8,128)(2,1)}, bf16[128,1024]{1,0:T(8,128)(2,1)}, u32[]{:S(2)}, u32[]{:S(2)}) %collective-permute-start.22) | collective-permute-done | bytes 262176 | tf_op jit(solution)/shard_map/ppermute | solution.py:24
  104.0 4.2 %collective-permute-done.32 = bf16[128,1024]{1,0:T(8,128)(2,1)} collective-permute-done((bf16[128,1024]{1,0:T(8,128)(2,1)}, bf16[128,1024]{1,0:T(8,128)(2,1)}, u32[]{:S(2)}, u32[]{:S(2)}) %collective-permute-start.32) | collective-permute-done | bytes 262176 | tf_op jit(solution)/shard_map/ppermute | solution.py:24
  108.2 1.8 %fusion.37 = (bf16[128,1024]{1,0:T(8,128)(2,1)S(1)}, f32[128,1024]{1,0:T(8,128)S(1)}) fusion(bf16[128,1024]{1,0:T(8,128)(2,1)} %collective-permute-done.32, f32[2,128,1024]{2,1,0:T(8,128)} %param.9, f32[2,128,1024]{2,1,0:T(8,128)} %param.10, f32[128,1024]{1,0:T(8,128)S(1)} %get-tuple-element.65, bf16[128,1024]{1,0:T(8,128)(2,1)} %collective-permute-done.34), kind=kLoop, calls=%fused_computation.63 | loop fusion | flops 2097152 | bytes 2883584 | tf_op jit(solution)/shard_map/convert_element_type | solution.py:366
  110.0 0.4 collective-permute-start.37
  110.4 2.1 %collective-permute-start.35 = (bf16[128,1024]{1,0:T(8,128)(2,1)S(1)}, bf16[128,1024]{1,0:T(8,128)(2,1)S(1)}, u32[]{:S(2)}, u32[]{:S(2)}) collective-permute-start(bf16[128,1024]{1,0:T(8,128)(2,1)S(1)} %get-tuple-element.68), channel_id=1, source_target_pairs={{0,16},{8,24},{16,0},{24,8},{1,17},{9,25},{17,1},{25,9},{2,18},{10... | collective-permute-start | bytes 786440 | tf_op jit(solution)/shard_map/ppermute | solution.py:24
  112.5 1.5 %fusion.35 = (f32[1,128,1024]{2,1,0:T(8,128)S(1)}, f32[1,128,1024]{2,1,0:T(8,128)S(1)}, f32[1,128,1024]{2,1,0:T(8,128)S(1)}, f32[1,128,1024]{2,1,0:T(8,128)S(1)}) fusion(f32[2,128,1024]{2,1,0:T(8,128)S(1)} %copy-done.3, f32[128,1024]{1,0:T(8,128)S(1)} %get-tuple-element.69, bf16[128,1024]{1,0:T(8,128)(2,1)S(1)} %copy-done.8, ...), kind=kLoop, calls=%fused_computation.50 | loop fusion | flops 2359296 | bytes 5767168 | tf_op jit(solution)/shard_map/stack | solution.py:384
  114.0 7.7 %collective-permute-done.35 = bf16[128,1024]{1,0:T(8,128)(2,1)S(1)} collective-permute-done((bf16[128,1024]{1,0:T(8,128)(2,1)S(1)}, bf16[128,1024]{1,0:T(8,128)(2,1)S(1)}, u32[]{:S(2)}, u32[]{:S(2)}) %collective-permute-start.35) | collective-permute-done | bytes 262176 | tf_op jit(solution)/shard_map/ppermute | solution.py:24
  121.8 2.9 %collective-permute-start.36 = (bf16[128,1024]{1,0:T(8,128)(2,1)S(1)}, bf16[128,1024]{1,0:T(8,128)(2,1)S(1)}, u32[]{:S(2)}, u32[]{:S(2)}) collective-permute-start(bf16[128,1024]{1,0:T(8,128)(2,1)S(1)} %collective-permute-done.35), channel_id=1, source_target_pairs={{0,8},{8,0},{16,24},{24,16},{1,9},{9,1},{17,25},{25,17},{2,10},{10... | collective-permute-start | bytes 786440 | tf_op jit(solution)/shard_map/ppermute | solution.py:24
  124.7 1.6 %fusion = bf16[1,256,1024]{2,1,0:T(8,128)(2,1)S(1)} fusion(bf16[128,1024]{1,0:T(8,128)(2,1)} %get-tuple-element.59, bf16[128,1024]{1,0:T(8,128)(2,1)} %collective-permute-done.22, bf16[128,1024]{1,0:T(8,128)(2,1)} %collective-permute-done.33, bf16[128,1024]{1,0:T(8,128)(2,1)S(1)} %collective-permute-done.23, ...), kind=kOutput, calls=%fused_computation.2 | convolution fusion | flops 272891904 | bytes 1835012 | tf_op jit(solution)/shard_map/dot_general | solution.py:377
  126.3 1.5 %pad_maximum_fusion.2 = (f32[2,128,1024]{2,1,0:T(8,128)}, f32[2,128,1024]{2,1,0:T(8,128)}) fusion(f32[1,128,1024]{2,1,0:T(8,128)S(1)} %get-tuple-element.80, f32[1,128,1024]{2,1,0:T(8,128)S(1)} %get-tuple-element.79, f32[1,128,1024]{2,1,0:T(8,128)S(1)} %get-tuple-element.81, f32[1,128,1024]{2,1,0:T(8,128)S(1)} %get-tuple-element.82), kind=kLoop, calls=%fused_computation.22 | loop fusion | flops 524288 | bytes 4194304 | tf_op jit(solution)/shard_map/stack | solution.py:384
  127.7 2.6 %collective-permute-done.36 = bf16[128,1024]{1,0:T(8,128)(2,1)S(1)} collective-permute-done((bf16[128,1024]{1,0:T(8,128)(2,1)S(1)}, bf16[128,1024]{1,0:T(8,128)(2,1)S(1)}, u32[]{:S(2)}, u32[]{:S(2)}) %collective-permute-start.36) | collective-permute-done | bytes 262176 | tf_op jit(solution)/shard_map/ppermute | solution.py:24
  130.4 0.5 fusion.1
  130.9 1.1 pad_maximum_fusion.1
  (64 shorter events, 1.0 us)
Async XLA Ops:
  1.7 9.3 %collective-permute-start.2 = (bf16[128,1024]{1,0:T(8,128)(2,1)S(1)}, bf16[128,1024]{1,0:T(8,128)(2,1)S(1)}, u32[]{:S(2)}, u32[]{:S(2)}) collective-permute-start(bf16[128,1024]{1,0:T(8,128)(2,1)S(1)} %get-tuple-element.41), channel_id=1, source_target_pairs={{0,4},{1,5},{2,6},{3,7},{4,0},{5,1},{6,2},{7,3},{8,12},{9,13},{10,... | collective-permute-start | bytes 786440 | tf_op jit(solution)/shard_map/ppermute | solution.py:24
  4.7 8.1 %collective-permute-start = (bf16[128,1024]{1,0:T(8,128)(2,1)}, bf16[128,1024]{1,0:T(8,128)(2,1)S(1)}, u32[]{:S(2)}, u32[]{:S(2)}) collective-permute-start(bf16[128,1024]{1,0:T(8,128)(2,1)} %bitcast.64), channel_id=1, source_target_pairs={{0,8},{8,0},{16,24},{24,16},{1,9},{9,1},{17,25},{25,17},{2,10},{10... | collective-permute-start | bytes 786440 | tf_op jit(solution)/shard_map/ppermute | solution.py:24
  6.3 7.5 %collective-permute-start.1 = (bf16[128,1024]{1,0:T(8,128)(2,1)S(1)}, bf16[128,1024]{1,0:T(8,128)(2,1)S(1)}, u32[]{:S(2)}, u32[]{:S(2)}) collective-permute-start(bf16[128,1024]{1,0:T(8,128)(2,1)S(1)} %get-tuple-element.42), channel_id=1, source_target_pairs={{0,2},{1,3},{2,0},{3,1},{4,6},{5,7},{6,4},{7,5},{8,10},{9,11},{10,... | collective-permute-start | bytes 786440 | tf_op jit(solution)/shard_map/ppermute | solution.py:24
  11.0 9.1 %collective-permute-start.10 = (bf16[128,1024]{1,0:T(8,128)(2,1)S(1)}, bf16[128,1024]{1,0:T(8,128)(2,1)S(1)}, u32[]{:S(2)}, u32[]{:S(2)}) collective-permute-start(bf16[128,1024]{1,0:T(8,128)(2,1)S(1)} %get-tuple-element.42), channel_id=1, source_target_pairs={{0,4},{1,5},{2,6},{3,7},{4,0},{5,1},{6,2},{7,3},{8,12},{9,13},{10,... | collective-permute-start | bytes 786440 | tf_op jit(solution)/shard_map/ppermute | solution.py:24
  13.8 14.9 %copy-start.9 = (bf16[128,1024]{1,0:T(8,128)(2,1)}, bf16[128,1024]{1,0:T(8,128)(2,1)S(1)}, u32[]{:S(2)}) copy-start(bf16[128,1024]{1,0:T(8,128)(2,1)S(1)} %broadcast_select_fusion) | copy-start | bytes 786436
  13.9 14.9 %collective-permute-start.3 = (bf16[128,1024]{1,0:T(8,128)(2,1)S(1)}, bf16[128,1024]{1,0:T(8,128)(2,1)}, u32[]{:S(2)}, u32[]{:S(2)}) collective-permute-start(bf16[128,1024]{1,0:T(8,128)(2,1)S(1)} %broadcast_select_fusion), channel_id=1, source_target_pairs={{0,16},{8,24},{16,0},{24,8},{1,17},{9,25},{17,1},{25,9},{2,18},{10... | collective-permute-start | bytes 786440 | tf_op jit(solution)/shard_map/ppermute | solution.py:24
  16.5 12.8 %collective-permute-start.9 = (bf16[128,1024]{1,0:T(8,128)(2,1)S(1)}, bf16[128,1024]{1,0:T(8,128)(2,1)S(1)}, u32[]{:S(2)}, u32[]{:S(2)}) collective-permute-start(bf16[128,1024]{1,0:T(8,128)(2,1)S(1)} %get-tuple-element.41), channel_id=1, source_target_pairs={{0,2},{1,3},{2,0},{3,1},{4,6},{5,7},{6,4},{7,5},{8,10},{9,11},{10,... | collective-permute-start | bytes 786440 | tf_op jit(solution)/shard_map/ppermute | solution.py:24
  18.0 10.7 %collective-permute-start.5 = (bf16[128,1024]{1,0:T(8,128)(2,1)S(1)}, bf16[128,1024]{1,0:T(8,128)(2,1)S(1)}, u32[]{:S(2)}, u32[]{:S(2)}) collective-permute-start(bf16[128,1024]{1,0:T(8,128)(2,1)S(1)} %collective-permute-done.2.refs_4_), channel_id=1, source_target_pairs={{0,2},{1,3},{2,0},{3,1},{4,6},{5,7},{6,4},{7,5},{8,10},{9,11},{10,... | collective-permute-start | bytes 786440 | tf_op jit(solution)/shard_map/ppermute | solution.py:24
  18.5 10.8 %collective-permute-start.4 = (bf16[128,1024]{1,0:T(8,128)(2,1)S(1)}, bf16[128,1024]{1,0:T(8,128)(2,1)S(1)}, u32[]{:S(2)}, u32[]{:S(2)}) collective-permute-start(bf16[128,1024]{1,0:T(8,128)(2,1)S(1)} %collective-permute-done.1.refs_1_), channel_id=1, source_target_pairs={{0,4},{1,5},{2,6},{3,7},{4,0},{5,1},{6,2},{7,3},{8,12},{9,13},{10,... | collective-permute-start | bytes 786440 | tf_op jit(solution)/shard_map/ppermute | solution.py:24
  20.1 14.6 %collective-permute-start.11 = (bf16[256,1024]{1,0:T(8,128)(2,1)S(1)}, bf16[256,1024]{1,0:T(8,128)(2,1)S(1)}, u32[]{:S(2)}, u32[]{:S(2)}) collective-permute-start(bf16[256,1024]{1,0:T(8,128)(2,1)S(1)} %slice_bitcast_fusion.refs_0_), channel_id=1, source_target_pairs={{0,1},{1,0},{2,3},{3,2},{4,5},{5,4},{6,7},{7,6},{8,9},{9,8},{10,11... | collective-permute-start | bytes 1572872 | tf_op jit(solution)/shard_map/ppermute | solution.py:24
  28.8 2.4 %collective-permute-start.15 = (bf16[128,1024]{1,0:T(8,128)(2,1)S(1)}, bf16[128,1024]{1,0:T(8,128)(2,1)S(1)}, u32[]{:S(2)}, u32[]{:S(2)}) collective-permute-start(bf16[128,1024]{1,0:T(8,128)(2,1)S(1)} %collective-permute-done.2.refs_4_), channel_id=1, source_target_pairs={{0,1},{1,0},{2,3},{3,2},{4,5},{5,4},{6,7},{7,6},{8,9},{9,8},{10,11... | collective-permute-start | bytes 786440 | tf_op jit(solution)/shard_map/ppermute | solution.py:24
  28.8 3.9 %collective-permute-start.12 = (bf16[128,1024]{1,0:T(8,128)(2,1)S(1)}, bf16[128,1024]{1,0:T(8,128)(2,1)S(1)}, u32[]{:S(2)}, u32[]{:S(2)}) collective-permute-start(bf16[128,1024]{1,0:T(8,128)(2,1)S(1)} %collective-permute-done.1.refs_1_), channel_id=1, source_target_pairs={{0,1},{1,0},{2,3},{3,2},{4,5},{5,4},{6,7},{7,6},{8,9},{9,8},{10,11... | collective-permute-start | bytes 786440 | tf_op jit(solution)/shard_map/ppermute | solution.py:24
  29.3 4.9 %collective-permute-start.14 = (bf16[128,1024]{1,0:T(8,128)(2,1)S(1)}, bf16[128,1024]{1,0:T(8,128)(2,1)S(1)}, u32[]{:S(2)}, u32[]{:S(2)}) collective-permute-start(bf16[128,1024]{1,0:T(8,128)(2,1)S(1)} %collective-permute-done.10.refs_3_), channel_id=1, source_target_pairs={{0,1},{1,0},{2,3},{3,2},{4,5},{5,4},{6,7},{7,6},{8,9},{9,8},{10,11... | collective-permute-start | bytes 786440 | tf_op jit(solution)/shard_map/ppermute | solution.py:24
  29.4 5.4 %collective-permute-start.13 = (bf16[128,1024]{1,0:T(8,128)(2,1)S(1)}, bf16[128,1024]{1,0:T(8,128)(2,1)}, u32[]{:S(2)}, u32[]{:S(2)}) collective-permute-start(bf16[128,1024]{1,0:T(8,128)(2,1)S(1)} %collective-permute-done.9.refs_2_), channel_id=1, source_target_pairs={{0,1},{1,0},{2,3},{3,2},{4,5},{5,4},{6,7},{7,6},{8,9},{9,8},{10,11... | collective-permute-start | bytes 786440 | tf_op jit(solution)/shard_map/ppermute | solution.py:24
  31.2 11.6 %collective-permute-start.8 = (bf16[128,1024]{1,0:T(8,128)(2,1)S(1)}, bf16[128,1024]{1,0:T(8,128)(2,1)S(1)}, u32[]{:S(2)}, u32[]{:S(2)}) collective-permute-start(bf16[128,1024]{1,0:T(8,128)(2,1)S(1)} %broadcast_select_fusion.1), channel_id=1, source_target_pairs={{0,6},{1,7},{2,4},{3,5},{4,2},{5,3},{6,0},{7,1},{8,14},{9,15},{10,... | collective-permute-start | bytes 786440 | tf_op jit(solution)/shard_map/ppermute | solution.py:24
  32.7 13.4 %collective-permute-start.7 = (bf16[128,1024]{1,0:T(8,128)(2,1)S(1)}, bf16[128,1024]{1,0:T(8,128)(2,1)S(1)}, u32[]{:S(2)}, u32[]{:S(2)}) collective-permute-start(bf16[128,1024]{1,0:T(8,128)(2,1)S(1)} %broadcast_select_fusion.1), channel_id=1, source_target_pairs={{0,4},{1,5},{2,6},{3,7},{4,0},{5,1},{6,2},{7,3},{8,12},{9,13},{10,... | collective-permute-start | bytes 786440 | tf_op jit(solution)/shard_map/ppermute | solution.py:24
  34.2 11.8 %collective-permute-start.6 = (bf16[128,1024]{1,0:T(8,128)(2,1)S(1)}, bf16[128,1024]{1,0:T(8,128)(2,1)S(1)}, u32[]{:S(2)}, u32[]{:S(2)}) collective-permute-start(bf16[128,1024]{1,0:T(8,128)(2,1)S(1)} %broadcast_select_fusion.1), channel_id=1, source_target_pairs={{0,2},{1,3},{2,0},{3,1},{4,6},{5,7},{6,4},{7,5},{8,10},{9,11},{10,... | collective-permute-start | bytes 786440 | tf_op jit(solution)/shard_map/ppermute | solution.py:24
  34.7 2.2 %copy-start = (bf16[2048,1024]{1,0:T(8,128)(2,1)S(1)}, bf16[2048,1024]{1,0:T(8,128)(2,1)}, u32[]{:S(2)}) copy-start(bf16[2048,1024]{1,0:T(8,128)(2,1)} %refs_8_.3) | copy-start | bytes 12582916
  42.7 6.9 %copy-start.6 = (bf16[2,256,1024]{2,1,0:T(8,128)(2,1)S(1)}, bf16[2,256,1024]{2,1,0:T(8,128)(2,1)}, u32[]{:S(2)}) copy-start(bf16[2,256,1024]{2,1,0:T(8,128)(2,1)} %param.7) | copy-start | bytes 3145732
  46.1 7.6 %copy-start.1 = (bf16[2048,1024]{1,0:T(8,128)(2,1)S(1)}, bf16[2048,1024]{1,0:T(8,128)(2,1)}, u32[]{:S(2)}) copy-start(bf16[2048,1024]{1,0:T(8,128)(2,1)} %refs_8_.3) | copy-start | bytes 12582916
  46.1 2.7 %collective-permute-start.16 = (bf16[512,1024]{1,0:T(8,128)(2,1)S(1)}, bf16[512,1024]{1,0:T(8,128)(2,1)S(1)}, u32[]{:S(2)}, u32[]{:S(2)}) collective-permute-start(bf16[512,1024]{1,0:T(8,128)(2,1)S(1)} %pad_maximum_fusion.same), channel_id=1, source_target_pairs={{0,1},{1,0},{2,3},{3,2},{4,5},{5,4},{6,7},{7,6},{8,9},{9,8},{10,11... | collective-permute-start | bytes 3145736 | tf_op jit(solution)/shard_map/ppermute | solution.py:24
  46.2 7.5 %collective-permute-start.18 = (bf16[128,1024]{1,0:T(8,128)(2,1)S(1)}, bf16[128,1024]{1,0:T(8,128)(2,1)S(1)}, u32[]{:S(2)}, u32[]{:S(2)}) collective-permute-start(bf16[128,1024]{1,0:T(8,128)(2,1)S(1)} %collective-permute-done.5.refs_1_), channel_id=1, source_target_pairs={{0,1},{1,0},{2,3},{3,2},{4,5},{5,4},{6,7},{7,6},{8,9},{9,8},{10,11... | collective-permute-start | bytes 786440 | tf_op jit(solution)/shard_map/ppermute | solution.py:24
  46.7 7.0 %collective-permute-start.17 = (bf16[128,1024]{1,0:T(8,128)(2,1)S(1)}, bf16[128,1024]{1,0:T(8,128)(2,1)S(1)}, u32[]{:S(2)}, u32[]{:S(2)}) collective-permute-start(bf16[128,1024]{1,0:T(8,128)(2,1)S(1)} %collective-permute-done.4.refs_0_), channel_id=1, source_target_pairs={{0,1},{1,0},{2,3},{3,2},{4,5},{5,4},{6,7},{7,6},{8,9},{9,8},{10,11... | collective-permute-start | bytes 786440 | tf_op jit(solution)/shard_map/ppermute | solution.py:24
  50.1 10.2 %collective-permute-start.26 = (bf16[256,512]{1,0:T(8,128)(2,1)S(1)}, bf16[256,512]{1,0:T(8,128)(2,1)S(1)}, u32[]{:S(2)}, u32[]{:S(2)}) collective-permute-start(bf16[256,512]{1,0:T(8,128)(2,1)S(1)} %fusion.2.refs_0_), channel_id=1, source_target_pairs={{0,6},{1,7},{2,4},{3,5},{4,2},{5,3},{6,0},{7,1},{8,14},{9,15},{10,... | collective-permute-start | bytes 786440 | tf_op jit(solution)/shard_map/ppermute | solution.py:24
  51.7 13.3 %collective-permute-start.25 = (bf16[256,512]{1,0:T(8,128)(2,1)S(1)}, bf16[256,512]{1,0:T(8,128)(2,1)S(1)}, u32[]{:S(2)}, u32[]{:S(2)}) collective-permute-start(bf16[256,512]{1,0:T(8,128)(2,1)S(1)} %fusion.2.refs_0_), channel_id=1, source_target_pairs={{0,4},{1,5},{2,6},{3,7},{4,0},{5,1},{6,2},{7,3},{8,12},{9,13},{10,... | collective-permute-start | bytes 786440 | tf_op jit(solution)/shard_map/ppermute | solution.py:24
  52.4 12.6 %collective-permute-start.24 = (bf16[256,512]{1,0:T(8,128)(2,1)S(1)}, bf16[256,512]{1,0:T(8,128)(2,1)S(1)}, u32[]{:S(2)}, u32[]{:S(2)}) collective-permute-start(bf16[256,512]{1,0:T(8,128)(2,1)S(1)} %fusion.2.refs_0_), channel_id=1, source_target_pairs={{0,2},{1,3},{2,0},{3,1},{4,6},{5,7},{6,4},{7,5},{8,10},{9,11},{10,... | collective-permute-start | bytes 786440 | tf_op jit(solution)/shard_map/ppermute | solution.py:24
  56.1 9.5 %collective-permute-start.20 = (bf16[128,1024]{1,0:T(8,128)(2,1)S(1)}, bf16[128,1024]{1,0:T(8,128)(2,1)S(1)}, u32[]{:S(2)}, u32[]{:S(2)}) collective-permute-start(bf16[128,1024]{1,0:T(8,128)(2,1)S(1)} %get-tuple-element.58), channel_id=1, source_target_pairs={{0,8},{8,0},{16,24},{24,16},{1,9},{9,1},{17,25},{25,17},{2,10},{10... | collective-permute-start | bytes 786440 | tf_op jit(solution)/shard_map/ppermute | solution.py:24
  57.7 8.0 %collective-permute-start.27 = (bf16[256,512]{1,0:T(8,128)(2,1)S(1)}, bf16[256,512]{1,0:T(8,128)(2,1)S(1)}, u32[]{:S(2)}, u32[]{:S(2)}) collective-permute-start(bf16[256,512]{1,0:T(8,128)(2,1)S(1)} %fusion.2.refs_0_), channel_id=1, source_target_pairs={{0,1},{1,0},{2,3},{3,2},{4,5},{5,4},{6,7},{7,6},{8,9},{9,8},{10,11... | collective-permute-start | bytes 786440 | tf_op jit(solution)/shard_map/ppermute | solution.py:24
  60.3 10.5 %collective-permute-start.19 = (bf16[128,1024]{1,0:T(8,128)(2,1)S(1)}, bf16[128,1024]{1,0:T(8,128)(2,1)S(1)}, u32[]{:S(2)}, u32[]{:S(2)}) collective-permute-start(bf16[128,1024]{1,0:T(8,128)(2,1)S(1)} %get-tuple-element.56), channel_id=1, source_target_pairs={{0,8},{8,0},{16,24},{24,16},{1,9},{9,1},{17,25},{25,17},{2,10},{10... | collective-permute-start | bytes 786440 | tf_op jit(solution)/shard_map/ppermute | solution.py:24
  65.1 1.5 %collective-permute-start.30 = (bf16[256,512]{1,0:T(8,128)(2,1)S(1)}, bf16[256,512]{1,0:T(8,128)(2,1)S(1)}, u32[]{:S(2)}, u32[]{:S(2)}) collective-permute-start(bf16[256,512]{1,0:T(8,128)(2,1)S(1)} %collective-permute-done.26.refs_3_), channel_id=1, source_target_pairs={{0,1},{1,0},{2,3},{3,2},{4,5},{5,4},{6,7},{7,6},{8,9},{9,8},{10,11... | collective-permute-start | bytes 786440 | tf_op jit(solution)/shard_map/ppermute | solution.py:24
  65.1 1.9 %collective-permute-start.29 = (bf16[256,512]{1,0:T(8,128)(2,1)S(1)}, bf16[256,512]{1,0:T(8,128)(2,1)S(1)}, u32[]{:S(2)}, u32[]{:S(2)}) collective-permute-start(bf16[256,512]{1,0:T(8,128)(2,1)S(1)} %collective-permute-done.25.refs_2_), channel_id=1, source_target_pairs={{0,1},{1,0},{2,3},{3,2},{4,5},{5,4},{6,7},{7,6},{8,9},{9,8},{10,11... | collective-permute-start | bytes 786440 | tf_op jit(solution)/shard_map/ppermute | solution.py:24
  65.6 1.8 %collective-permute-start.28 = (bf16[256,512]{1,0:T(8,128)(2,1)S(1)}, bf16[256,512]{1,0:T(8,128)(2,1)S(1)}, u32[]{:S(2)}, u32[]{:S(2)}) collective-permute-start(bf16[256,512]{1,0:T(8,128)(2,1)S(1)} %collective-permute-done.24.refs_1_), channel_id=1, source_target_pairs={{0,1},{1,0},{2,3},{3,2},{4,5},{5,4},{6,7},{7,6},{8,9},{9,8},{10,11... | collective-permute-start | bytes 786440 | tf_op jit(solution)/shard_map/ppermute | solution.py:24
  65.7 15.4 %copy-start.2 = (f32[2,128,1024]{2,1,0:T(8,128)S(1)}, f32[2,128,1024]{2,1,0:T(8,128)}, u32[]{:S(2)}) copy-start(f32[2,128,1024]{2,1,0:T(8,128)} %param.9) | copy-start | bytes 3145732
  65.7 15.4 %copy-start.4 = (f32[2,128,1024]{2,1,0:T(8,128)S(1)}, f32[2,128,1024]{2,1,0:T(8,128)}, u32[]{:S(2)}) copy-start(f32[2,128,1024]{2,1,0:T(8,128)} %param.10) | copy-start | bytes 3145732
  65.7 15.3 %collective-permute-start.21 = (bf16[128,1024]{1,0:T(8,128)(2,1)S(1)}, bf16[128,1024]{1,0:T(8,128)(2,1)S(1)}, u32[]{:S(2)}, u32[]{:S(2)}) collective-permute-start(bf16[128,1024]{1,0:T(8,128)(2,1)S(1)} %add_convert_fusion.1), channel_id=1, source_target_pairs={{0,16},{8,24},{16,0},{24,8},{1,17},{9,25},{17,1},{25,9},{2,18},{10... | collective-permute-start | bytes 786440 | tf_op jit(solution)/shard_map/ppermute | solution.py:24
  69.1 17.1 %collective-permute-start.31 = (bf16[128,1024]{1,0:T(8,128)(2,1)S(1)}, bf16[128,1024]{1,0:T(8,128)(2,1)S(1)}, u32[]{:S(2)}, u32[]{:S(2)}) collective-permute-start(bf16[128,1024]{1,0:T(8,128)(2,1)S(1)} %get-tuple-element.62), channel_id=1, source_target_pairs={{0,8},{8,0},{16,24},{24,16},{1,9},{9,1},{17,25},{25,17},{2,10},{10... | collective-permute-start | bytes 786440 | tf_op jit(solution)/shard_map/ppermute | solution.py:24
  81.1 5.2 %copy-start.7 = (bf16[128,1024]{1,0:T(8,128)(2,1)}, bf16[128,1024]{1,0:T(8,128)(2,1)S(1)}, u32[]{:S(2)}) copy-start(bf16[128,1024]{1,0:T(8,128)(2,1)S(1)} %collective-permute-done.21) | copy-start | bytes 786436
  82.2 21.8 %collective-permute-start.33 = (bf16[128,1024]{1,0:T(8,128)(2,1)}, bf16[128,1024]{1,0:T(8,128)(2,1)}, u32[]{:S(2)}, u32[]{:S(2)}) collective-permute-start(bf16[128,1024]{1,0:T(8,128)(2,1)} %get-tuple-element.59), channel_id=1, source_target_pairs={{0,8},{8,0},{16,24},{24,16},{1,9},{9,1},{17,25},{25,17},{2,10},{10... | collective-permute-start | bytes 786440 | tf_op jit(solution)/shard_map/ppermute | solution.py:24
  82.2 21.8 %collective-permute-start.22 = (bf16[128,1024]{1,0:T(8,128)(2,1)}, bf16[128,1024]{1,0:T(8,128)(2,1)}, u32[]{:S(2)}, u32[]{:S(2)}) collective-permute-start(bf16[128,1024]{1,0:T(8,128)(2,1)} %get-tuple-element.59), channel_id=1, source_target_pairs={{0,16},{8,24},{16,0},{24,8},{1,17},{9,25},{17,1},{25,9},{2,18},{10... | collective-permute-start | bytes 786440 | tf_op jit(solution)/shard_map/ppermute | solution.py:24
  87.1 21.2 %collective-permute-start.32 = (bf16[128,1024]{1,0:T(8,128)(2,1)}, bf16[128,1024]{1,0:T(8,128)(2,1)}, u32[]{:S(2)}, u32[]{:S(2)}) collective-permute-start(bf16[128,1024]{1,0:T(8,128)(2,1)} %add_convert_fusion), channel_id=1, source_target_pairs={{0,16},{8,24},{16,0},{24,8},{1,17},{9,25},{17,1},{25,9},{2,18},{10... | collective-permute-start | bytes 786440 | tf_op jit(solution)/shard_map/ppermute | solution.py:24
  87.7 20.5 %collective-permute-start.34 = (bf16[128,1024]{1,0:T(8,128)(2,1)S(1)}, bf16[128,1024]{1,0:T(8,128)(2,1)}, u32[]{:S(2)}, u32[]{:S(2)}) collective-permute-start(bf16[128,1024]{1,0:T(8,128)(2,1)S(1)} %get-tuple-element.66), channel_id=1, source_target_pairs={{0,8},{8,0},{16,24},{24,16},{1,9},{9,1},{17,25},{25,17},{2,10},{10... | collective-permute-start | bytes 786440 | tf_op jit(solution)/shard_map/ppermute | solution.py:24
  89.7 22.8 %copy-start.3 = (f32[2,128,1024]{2,1,0:T(8,128)S(1)}, f32[2,128,1024]{2,1,0:T(8,128)}, u32[]{:S(2)}) copy-start(f32[2,128,1024]{2,1,0:T(8,128)} %param.9) | copy-start | bytes 3145732
  89.7 22.8 %copy-start.5 = (f32[2,128,1024]{2,1,0:T(8,128)S(1)}, f32[2,128,1024]{2,1,0:T(8,128)}, u32[]{:S(2)}) copy-start(f32[2,128,1024]{2,1,0:T(8,128)} %param.10) | copy-start | bytes 3145732
  89.7 22.8 %copy-start.8 = (bf16[128,1024]{1,0:T(8,128)(2,1)S(1)}, bf16[128,1024]{1,0:T(8,128)(2,1)}, u32[]{:S(2)}) copy-start(bf16[128,1024]{1,0:T(8,128)(2,1)} %copy-done.7) | copy-start | bytes 786436
  104.0 20.7 %collective-permute-start.23 = (bf16[128,1024]{1,0:T(8,128)(2,1)}, bf16[128,1024]{1,0:T(8,128)(2,1)S(1)}, u32[]{:S(2)}, u32[]{:S(2)}) collective-permute-start(bf16[128,1024]{1,0:T(8,128)(2,1)} %collective-permute-done.22), channel_id=1, source_target_pairs={{0,8},{8,0},{16,24},{24,16},{1,9},{9,1},{17,25},{25,17},{2,10},{10... | collective-permute-start | bytes 786440 | tf_op jit(solution)/shard_map/ppermute | solution.py:24
  110.0 17.8 %collective-permute-start.37 = (bf16[128,1024]{1,0:T(8,128)(2,1)S(1)}, bf16[128,1024]{1,0:T(8,128)(2,1)S(1)}, u32[]{:S(2)}, u32[]{:S(2)}) collective-permute-start(bf16[128,1024]{1,0:T(8,128)(2,1)S(1)} %get-tuple-element.68), channel_id=1, source_target_pairs={{0,8},{8,0},{16,24},{24,16},{1,9},{9,1},{17,25},{25,17},{2,10},{10... | collective-permute-start | bytes 786440 | tf_op jit(solution)/shard_map/ppermute | solution.py:24
  110.4 11.3 %collective-permute-start.35 = (bf16[128,1024]{1,0:T(8,128)(2,1)S(1)}, bf16[128,1024]{1,0:T(8,128)(2,1)S(1)}, u32[]{:S(2)}, u32[]{:S(2)}) collective-permute-start(bf16[128,1024]{1,0:T(8,128)(2,1)S(1)} %get-tuple-element.68), channel_id=1, source_target_pairs={{0,16},{8,24},{16,0},{24,8},{1,17},{9,25},{17,1},{25,9},{2,18},{10... | collective-permute-start | bytes 786440 | tf_op jit(solution)/shard_map/ppermute | solution.py:24
  121.8 8.6 %collective-permute-start.36 = (bf16[128,1024]{1,0:T(8,128)(2,1)S(1)}, bf16[128,1024]{1,0:T(8,128)(2,1)S(1)}, u32[]{:S(2)}, u32[]{:S(2)}) collective-permute-start(bf16[128,1024]{1,0:T(8,128)(2,1)S(1)} %collective-permute-done.35), channel_id=1, source_target_pairs={{0,8},{8,0},{16,24},{24,16},{1,9},{9,1},{17,25},{25,17},{2,10},{10... | collective-permute-start | bytes 786440 | tf_op jit(solution)/shard_map/ppermute | solution.py:24
